TPU v7x, 32 devices: a whole 2x2x4 slice. The times are simulated.
32 devices in a mesh: dp: 8 (over y, x, core), tensor: 4 (over z).
Axes of the slice: x: 2, y: 2, z: 4, core: 2. Of those that a mesh axis runs over, the one named last changes fastest.
Arguments:
- tokens: bfloat16 [2048, 8192], P('dp', 'tensor'), may hold values from -6 to 6
- queries: bfloat16 [2048, 4096], P('dp', 'tensor'), may hold values from -400 to 400
- d_out: bfloat16 [2048, 4096], P('dp', 'tensor'), may hold values from -6 to 6
- segments: int32 [8, 256], P('dp'), may hold values from 0 to 3, never falling along the last dimension, each value on 1 to 128 neighbouring positions
- cached: bfloat16 [8192, 1024], P(None, 'tensor'), may hold values from -0.0625 to 0.0625
- master: float32 [8192, 1024], P('dp', 'tensor'), may hold values from -0.0625 to 0.0625
- moment: float32 [8192, 1024], P('dp', 'tensor'), may hold values from -4 to 4
- second: float32 [8192, 1024], P('dp', 'tensor'), may hold values from 0.05 to 2
- grad: float32 [8192, 1024], P('dp', 'tensor'), may hold values from -6 to 6
Outputs:
- master_new: float32 [8192, 1024], P('dp', 'tensor')
- moment_new: float32 [8192, 1024], P('dp', 'tensor')
- second_new: float32 [8192, 1024], P('dp', 'tensor')
- new_cache: bfloat16 [8192, 1024], P(None, 'tensor')
- new_grad: float32 [8192, 1024], P('dp', 'tensor')
- d_queries: bfloat16 [2048, 4096], P('dp', 'tensor')
- d_tokens: bfloat16 [2048, 8192], P('dp', 'tensor')
Inputs may be any that keep to these rules, and one draw needn't show every extreme that they name: `segments`: document numbers within a pack never fall.
All inputs are finite; a program needn't handle non-finite values.
Results may differ from a plain program's by a relative error of at most 0.0091.
Values may be sent and summed in bfloat16 or wider, within the bound.
No kernel may reach another device: no remote copies, remote signals or barrier semaphores. Data moves between devices by JAX's collectives and lax.ppermute only.
A program may use at most 128 MiB of HBM per device.

v0:
```python
import math

import jax
import jax.numpy as jnp
from jax import lax
from jax.sharding import PartitionSpec as P

HD = 128


beta_first = 0.9
beta_second = 0.95
learn_rate = 0.0003
weight_decay = 0.1
adam_epsilon = 1e-08
first_fix = 1.0 - 0.9**40
second_fix = 1.0 - 0.95**40


def body(tokens, queries, d_out, segments, cached, master, moment, second, grad):
    rows_here = master.shape[0]
    first_row = lax.axis_index("dp") * rows_here
    moment_new = beta_first * moment + (1.0 - beta_first) * grad
    second_new = beta_second * second + (1.0 - beta_second) * grad * grad
    update = moment_new / first_fix / (jnp.sqrt(second_new / second_fix) + adam_epsilon)
    master_new = master - learn_rate * (update + weight_decay * master)
    own_cache = lax.dynamic_slice_in_dim(cached, first_row, rows_here, 0).astype(jnp.float32)
    blocks = (master_new - own_cache).reshape(rows_here, -1, HD)
    block_scale = (jnp.max(jnp.abs(blocks), axis=2) + 1e-06).astype(jnp.bfloat16)
    codes = (
        (blocks / block_scale.astype(jnp.float32)[:, :, None])
        .astype(jnp.bfloat16)
        .reshape(rows_here, -1)
    )
    code_rows, scale_rows = lax.all_gather((codes, block_scale), "dp", axis=0, tiled=True)
    height = code_rows.shape[0]
    base = cached.astype(jnp.float32)
    scaled = (
        code_rows.astype(jnp.float32).reshape(height, -1, HD)
        * scale_rows.astype(jnp.float32)[:, :, None]
    )
    new_cache = (base + scaled.reshape(height, -1)).astype(jnp.bfloat16)
    whole = lax.all_gather(tokens, "tensor", axis=1, tiled=True)
    length = whole.shape[0]
    projected = jnp.dot(whole, cached, preferred_element_type=jnp.float32).astype(jnp.bfloat16)
    heads = projected.reshape(length, -1, 2, HD)
    keys = heads[:, :, 0]
    values = heads[:, :, 1]
    query_heads = queries.reshape(length, keys.shape[1], -1, HD)
    grads_out = d_out.reshape(length, keys.shape[1], -1, HD)
    factor = 1.0 / math.sqrt(HD)
    scores = (
        jnp.einsum("qhgd,khd->hgqk", query_heads, keys, preferred_element_type=jnp.float32) * factor
    )
    doc_ids = segments[0]
    position = jnp.arange(length)
    allowed = (doc_ids[:, None] == doc_ids[None, :]) & (position[None, :] <= position[:, None])
    scores = jnp.where(allowed, scores, -1e30)
    highest = jnp.max(scores, axis=-1, keepdims=True)
    weights = jnp.exp(scores - highest)
    probs = weights / jnp.sum(weights, axis=-1, keepdims=True)
    probs_low = probs.astype(jnp.bfloat16)
    attended = jnp.einsum("hgqk,khd->qhgd", probs_low, values, preferred_element_type=jnp.float32)
    rowdot = jnp.sum(grads_out.astype(jnp.float32) * attended, axis=-1)
    d_probs = jnp.einsum("qhgd,khd->hgqk", grads_out, values, preferred_element_type=jnp.float32)
    d_scores = (probs * (d_probs - jnp.transpose(rowdot, (1, 2, 0))[..., None]) * factor).astype(
        jnp.bfloat16
    )
    d_queries = (
        jnp.einsum("hgqk,khd->qhgd", d_scores, keys, preferred_element_type=jnp.float32)
        .astype(jnp.bfloat16)
        .reshape(length, -1)
    )
    d_keys = jnp.einsum("hgqk,qhgd->khd", d_scores, query_heads, preferred_element_type=jnp.float32)
    d_values = jnp.einsum(
        "hgqk,qhgd->khd", probs_low, grads_out, preferred_element_type=jnp.float32
    )
    d_projected = jnp.stack([d_keys, d_values], axis=2).astype(jnp.bfloat16).reshape(length, -1)
    new_grad = lax.psum_scatter(
        lax.dot_general(
            whole, d_projected, (((0,), (0,)), ((), ())), preferred_element_type=jnp.float32
        ),
        "dp",
        scatter_dimension=0,
        tiled=True,
    )
    summed = lax.psum_scatter(
        lax.dot_general(
            cached, d_projected, (((1,), (1,)), ((), ())), preferred_element_type=jnp.float32
        ),
        "tensor",
        scatter_dimension=0,
        tiled=True,
    )
    d_tokens = summed.T.astype(jnp.bfloat16)
    return (master_new, moment_new, second_new, new_cache, new_grad, d_queries, d_tokens)


def solution(mesh):
    in_specs = (
        P("dp", "tensor"),
        P("dp", "tensor"),
        P("dp", "tensor"),
        P("dp", None),
        P(None, "tensor"),
        P("dp", "tensor"),
        P("dp", "tensor"),
        P("dp", "tensor"),
        P("dp", "tensor"),
    )
    out_specs = (
        P("dp", "tensor"),
        P("dp", "tensor"),
        P("dp", "tensor"),
        P(None, "tensor"),
        P("dp", "tensor"),
        P("dp", "tensor"),
        P("dp", "tensor"),
    )
    return jax.shard_map(body, mesh=mesh, in_specs=in_specs, out_specs=out_specs, check_vma=False)
```

profile of v0, /device:TPU:0, one launch (start us, length us, event | category | flops | bytes accessed | tf_op | source)
XLA Modules:
  0.0 368.6 jit_solution(10093230935180381265)
XLA Ops:
  7.2 0.0 all-gather.5.cloned.1.call-start
  7.2 0.7 all-gather.5.cloned.1.call-update
  7.9 0.0 all-gather.3.cloned.1.call-start
  8.0 4.5 %fusion.18 = (f32[1024,256]{1,0:T(8,128)S(1)}, f32[1024,256]{1,0:T(8,128)S(1)}, f32[1024,256]{1,0:T(8,128)}, f32[1024,256]{1,0:T(8,128)}) fusion(bf16[8192,256]{1,0:T(8,128)(2,1)} %param.13, s32[]{:T(128)S(6)} %select_n.7, f32[1024,256]{1,0:T(8,128)} %param.14, f32[1024,256]{1,0:T(8,128)} %param.17, f32[1024,256]{1,0:T(8,128)} %param.15, f32[1024,256]{1,0:T(8,128)} %param.16), kind=kLoop, calls=%fused_computation.35 | loop fusion | flops 4718592 | bytes 8912900 | tf_op jit(solution)/shard_map/abs | solution.py:29
  12.5 0.0 copy-start.3
  12.5 0.5 abs.7
  13.0 0.0 copy-start.4
  13.0 1.2 reduce_max.18
  14.2 0.0 copy-start.5
  14.3 1.2 div.39
  15.5 2.1 fusion.15
  17.6 0.0 copy-done.3
  17.6 0.0 all-gather.3.cloned.1.call-update
  17.6 0.0 reduce-scatter.3.cloned.1.call-start
  17.6 0.0 copy-done.4
  17.6 0.2 copy.42
  17.9 0.2 copy.20
  18.1 1.3 copy.41
  19.4 0.0 copy-done.5
  19.4 0.1 fusion.20
  19.5 73.6 %all-gather.5.cloned.1.call-done = bf16[256,8192]{1,0:T(8,128)(2,1)} async-done(((bf16[256,2048]{1,0:T(8,128)(2,1)}), bf16[256,8192]{1,0:T(8,128)(2,1)}) %all-gather.5.cloned.1.call-update) | async-done | bytes 4194320 | tf_op jit(solution)/shard_map/all_gather | solution.py:43
  93.1 5.2 %convolution_convert_fusion.1 = bf16[256,256]{0,1:T(8,128)(2,1)S(1)} fusion(bf16[256,8192]{1,0:T(8,128)(2,1)} %all-gather.5.cloned.1.call-done, bf16[8192,256]{1,0:T(8,128)(2,1)} %param.13), kind=kOutput, calls=%fused_computation.19 | convolution fusion | flops 1073807360 | bytes 8519680 | tf_op jit(solution)/shard_map/dot_general | solution.py:45
  98.3 0.5 fusion.22
  98.8 0.3 fusion.6
  99.1 0.3 fusion.19
  99.4 0.5 fusion.12
  99.9 0.3 fusion.9
  100.3 0.0 copy-start.1
  100.3 0.7 fusion.7
  101.0 0.5 fusion.13
  101.5 1.2 copy-done.1
  102.7 4.5 %convolution_bitcast_fusion.1 = f32[8192,256]{0,1:T(8,128)} fusion(bf16[256,256]{0,1:T(8,128)(2,1)S(1)} %bitcast.133, bf16[256,8192]{1,0:T(8,128)(2,1)S(1)} %copy-done.1), kind=kOutput, calls=%fused_computation.1 | convolution fusion | flops 1073741824 | bytes 12713984 | tf_op jit(solution)/shard_map/dot_general | solution.py:80
  107.2 0.0 reduce-scatter.3.cloned.1.call-update
  107.2 0.0 reduce-scatter.5.cloned.1.call-start
  107.3 6.7 %convolution_bitcast_fusion = f32[8192,256]{0,1:T(8,128)} fusion(bf16[256,256]{0,1:T(8,128)(2,1)S(1)} %bitcast.134, bf16[8192,256]{1,0:T(8,128)(2,1)} %param.13), kind=kOutput, calls=%fused_computation | convolution fusion | flops 1073741824 | bytes 12713984 | tf_op jit(solution)/shard_map/dot_general | solution.py:88
  114.0 0.0 reduce-scatter.5.cloned.1.call-update
  114.0 24.5 %all_gather.10 = bf16[8192,2]{1,0:T(8,128)(2,1)S(1)} all-gather(bf16[1024,2]{1,0:T(8,128)(2,1)S(1)} %add_convert_fusion), channel_id=1, replica_groups=mesh['dp'=8,'tensor'=4] {'dp'}, dimensions={0}, use_global_device_ids=true | all-gather | bytes 36864 | tf_op jit(solution)/shard_map/all_gather | solution.py:35
  138.5 1.1 convolution_convert_fusion
  139.6 2.0 copy.30
  141.7 0.0 all-gather.3.cloned.1.call-done
  141.7 22.9 %mul.77 = f32[8192,2,128]{2,1,0:T(2,128)S(1)} broadcast(bf16[8192,2]{1,0:T(8,128)(2,1)S(1)} %all_gather.10), dimensions={0,1} | broadcast | bytes 8421376 | tf_op jit(solution)/shard_map/mul | solution.py:39
  164.6 0.0 copy-done
  164.6 0.0 copy-done.2
  164.6 5.2 %fusion.1 = bf16[8192,256]{1,0:T(8,128)(2,1)} fusion(f32[1024,8,2,128]{3,2,1,0:T(2,128)S(1)} %bitcast.125, bf16[8192,256]{1,0:T(8,128)(2,1)S(1)} %copy-done.2, bf16[8192,256]{1,0:T(8,128)(2,1)S(1)} %copy-done), kind=kLoop, calls=%fused_computation.4 | loop fusion | flops 10485760 | bytes 20971520 | tf_op jit(solution)/shard_map/convert_element_type | solution.py:42
  169.8 42.7 %reduce-scatter.3.cloned.1.call-done = f32[1024,256]{0,1:T(8,128)} async-done(((f32[8192,256]{0,1:T(8,128)}), f32[1024,256]{0,1:T(8,128)}) %reduce-scatter.3.cloned.1.call-update) | async-done | bytes 1048592 | tf_op jit(solution)/shard_map/reduce_scatter | solution.py:79
  212.5 2.5 copy.29
  215.1 144.3 %reduce-scatter.5.cloned.1.call-done = f32[2048,256]{0,1:T(8,128)} async-done(((f32[8192,256]{0,1:T(8,128)}), f32[2048,256]{0,1:T(8,128)}) %reduce-scatter.5.cloned.1.call-update) | async-done | bytes 2097168 | tf_op jit(solution)/shard_map/reduce_scatter | solution.py:87
  359.4 2.7 convert_bitcast_fusion
  (4 shorter events, 0.1 us)
Async XLA Ops:
  7.2 85.9 %all-gather.5.cloned.1.call-start = ((), (), s32[]{:S(2)}) async-start(), calls=%async_computation.3 | async-start | bytes 5242880 | tf_op jit(solution)/shard_map/all_gather | solution.py:43
  7.9 133.8 %all-gather.3.cloned.1.call-start = ((), (), s32[]{:S(2)}) async-start(), calls=%async_computation.2 | async-start | bytes 4718592 | tf_op jit(solution)/shard_map/all_gather | solution.py:35
  12.5 5.1 %copy-start.3 = (f32[1024,256]{1,0:T(8,128)}, f32[1024,256]{1,0:T(8,128)S(1)}, u32[]{:S(2)}) copy-start(f32[1024,256]{1,0:T(8,128)S(1)} %get-tuple-element.15) | copy-start | bytes 3145732
  13.0 4.6 %copy-start.4 = (bf16[256,1024]{1,0:T(8,128)(2,1)S(1)}, bf16[256,1024]{1,0:T(8,128)(2,1)}, u32[]{:S(2)}) copy-start(bf16[256,1024]{1,0:T(8,128)(2,1)} %param.11) | copy-start | bytes 1572868
  14.2 5.1 %copy-start.5 = (s32[1,256]{1,0:T(1,128)S(1)}, s32[1,256]{1,0:T(1,128)}, u32[]{:S(2)}) copy-start(s32[1,256]{1,0:T(1,128)} %param.12) | copy-start | bytes 3076
  17.6 194.9 %reduce-scatter.3.cloned.1.call-start = ((), (), s32[]{:S(2)}) async-start(), calls=%async_computation.4 | async-start | bytes 9437184 | tf_op jit(solution)/shard_map/reduce_scatter | solution.py:79
  100.3 2.4 copy-start.1
  107.2 252.1 %reduce-scatter.5.cloned.1.call-start = ((), (), s32[]{:S(2)}) async-start(), calls=%async_computation.5 | async-start | bytes 10485760 | tf_op jit(solution)/shard_map/reduce_scatter | solution.py:87
  141.7 22.9 %copy-start = (bf16[8192,256]{1,0:T(8,128)(2,1)S(1)}, bf16[8192,256]{1,0:T(8,128)(2,1)}, u32[]{:S(2)}) copy-start(bf16[8192,256]{1,0:T(8,128)(2,1)} %param.13) | copy-start | bytes 12582916
  141.7 22.9 %copy-start.2 = (bf16[8192,256]{1,0:T(8,128)(2,1)S(1)}, bf16[8192,256]{1,0:T(8,128)(2,1)}, u32[]{:S(2)}) copy-start(bf16[8192,256]{1,0:T(8,128)(2,1)} %all-gather.3.cloned.1.call-done) | copy-start | bytes 12582916
Sparse Core Ops, SparseCore 0:
  9.6 83.4 all-gather.4
  95.5 43.4 all-gather.2
  142.5 69.9 reduce-scatter.2
  214.9 144.4 reduce-scatter.4
where the time goes:
time: 369 us
  waiting for transfers between devices  261 us (71%)
  local copies, waits for them, and re-layouts  32.2 us (9%)
  blocking collectives  24.5 us (7%)
  matrix products  20 us (5%)
  other arithmetic  16.5 us (4%)
  between operations  13.9 us (4%)
    reduce_scatter x1, waiting for transfers between devices, body(): lax.psum_scatter(lax.dot_general(cached, d_projected, (((1,), (1,)), ((),...  144 us
    all_gather x1, waiting for transfers between devices, body(): whole = lax.all_gather(tokens, 'tensor', axis=1, tiled=True)  73.6 us
    reduce_scatter x1, waiting for transfers between devices, body(): lax.psum_scatter(lax.dot_general(whole, d_projected, (((0,), (0,)), ((),...  42.7 us
    all_gather x1, blocking collectives, body(): lax.all_gather((codes, block_scale), 'dp', axis=0, tiled=True)  24.5 us
    mul x1, local copies, waits for them, and re-layouts, body(): code_rows.astype(jnp.float32).reshape(height, -1, HD)  22.9 us
  transfers between devices with their start and end apart: 4, of which 3 were waited for; matrix products, arithmetic and copies ran while one was open for 18% of the time, Pallas kernels for 0%

commit v1 on v0

--- a/solution.py
+++ b/solution.py
@@ -17,7 +17,7 @@
 second_fix = 1.0 - 0.95**40
 
 
-def body(tokens, queries, d_out, segments, cached, master, moment, second, grad):
+def optimizer(cached, master, moment, second, grad):
     rows_here = master.shape[0]
     first_row = lax.axis_index("dp") * rows_here
     moment_new = beta_first * moment + (1.0 - beta_first) * grad
@@ -26,23 +26,16 @@
     master_new = master - learn_rate * (update + weight_decay * master)
     own_cache = lax.dynamic_slice_in_dim(cached, first_row, rows_here, 0).astype(jnp.float32)
     blocks = (master_new - own_cache).reshape(rows_here, -1, HD)
-    block_scale = (jnp.max(jnp.abs(blocks), axis=2) + 1e-06).astype(jnp.bfloat16)
-    codes = (
-        (blocks / block_scale.astype(jnp.float32)[:, :, None])
-        .astype(jnp.bfloat16)
-        .reshape(rows_here, -1)
-    )
-    code_rows, scale_rows = lax.all_gather((codes, block_scale), "dp", axis=0, tiled=True)
-    height = code_rows.shape[0]
-    base = cached.astype(jnp.float32)
-    scaled = (
-        code_rows.astype(jnp.float32).reshape(height, -1, HD)
-        * scale_rows.astype(jnp.float32)[:, :, None]
-    )
-    new_cache = (base + scaled.reshape(height, -1)).astype(jnp.bfloat16)
-    whole = lax.all_gather(tokens, "tensor", axis=1, tiled=True)
-    length = whole.shape[0]
-    projected = jnp.dot(whole, cached, preferred_element_type=jnp.float32).astype(jnp.bfloat16)
+    block_scale = (jnp.max(jnp.abs(blocks), axis=2, keepdims=True) + 1e-06).astype(jnp.bfloat16)
+    scale = block_scale.astype(jnp.float32)
+    codes = (blocks / scale).astype(jnp.bfloat16)
+    scaled = codes.astype(jnp.float32) * scale
+    own_new = (own_cache + scaled.reshape(rows_here, -1)).astype(jnp.bfloat16)
+    return master_new, moment_new, second_new, own_new
+
+
+def attention_backward(projected, queries, d_out, doc_ids):
+    length = projected.shape[0]
     heads = projected.reshape(length, -1, 2, HD)
     keys = heads[:, :, 0]
     values = heads[:, :, 1]
@@ -52,7 +45,6 @@
     scores = (
         jnp.einsum("qhgd,khd->hgqk", query_heads, keys, preferred_element_type=jnp.float32) * factor
     )
-    doc_ids = segments[0]
     position = jnp.arange(length)
     allowed = (doc_ids[:, None] == doc_ids[None, :]) & (position[None, :] <= position[:, None])
     scores = jnp.where(allowed, scores, -1e30)
@@ -76,24 +68,80 @@
         "hgqk,qhgd->khd", probs_low, grads_out, preferred_element_type=jnp.float32
     )
     d_projected = jnp.stack([d_keys, d_values], axis=2).astype(jnp.bfloat16).reshape(length, -1)
-    new_grad = lax.psum_scatter(
-        lax.dot_general(
-            whole, d_projected, (((0,), (0,)), ((), ())), preferred_element_type=jnp.float32
-        ),
-        "dp",
-        scatter_dimension=0,
-        tiled=True,
-    )
-    summed = lax.psum_scatter(
-        lax.dot_general(
-            cached, d_projected, (((1,), (1,)), ((), ())), preferred_element_type=jnp.float32
-        ),
-        "tensor",
-        scatter_dimension=0,
-        tiled=True,
-    )
-    d_tokens = summed.T.astype(jnp.bfloat16)
-    return (master_new, moment_new, second_new, new_cache, new_grad, d_queries, d_tokens)
+    return d_queries, d_projected
+
+
+def make_body(n_dp, n_z):
+    ring = [[(z, (z + s) % n_z) for z in range(n_z)] for s in range(n_z)]
+    up = [(z, z + 1) for z in range(n_z - 1)]
+    down = [(z + 1, z) for z in range(n_z - 1)]
+
+    def body(tokens, queries, d_out, segments, cached, master, moment, second, grad):
+        me_dp = lax.axis_index("dp")
+        me_z = lax.axis_index("tensor")
+        length, feats = tokens.shape
+        cols = cached.shape[1]
+
+        def part(chunk, index):
+            rows = lax.dynamic_slice_in_dim(cached, jnp.clip(index, 0, n_z - 1) * feats, feats, 0)
+            return jnp.dot(chunk, rows, preferred_element_type=jnp.float32)
+
+        projected = part(tokens, me_z)
+        held = jnp.zeros((n_z + 1, length, feats), tokens.dtype)
+        held = lax.dynamic_update_slice(held, tokens[None], (me_z, 0, 0))
+        from_low, from_high = tokens, tokens
+        for s in range(1, n_z):
+            from_low = lax.ppermute(from_low, "tensor", up)
+            from_high = lax.ppermute(from_high, "tensor", down)
+            low, high = me_z - s, me_z + s
+            projected = projected + part(from_low, low) + part(from_high, high)
+            held = lax.dynamic_update_slice(
+                held, from_low[None], (jnp.where(low >= 0, low, n_z), 0, 0)
+            )
+            held = lax.dynamic_update_slice(
+                held, from_high[None], (jnp.where(high < n_z, high, n_z), 0, 0)
+            )
+        projected = projected.astype(jnp.bfloat16)
+
+        master_new, moment_new, second_new, own_new = optimizer(
+            cached, master, moment, second, grad
+        )
+        new_cache = lax.all_gather(own_new, "dp", axis=0, tiled=True)
+
+        share = feats // n_dp
+
+        def block_for(z):
+            return lax.dynamic_slice_in_dim(cached, z * feats + me_dp * share, share, 0)
+
+        blocks = [block_for(me_z)]
+        for s in range(1, n_z):
+            blocks.append(lax.ppermute(block_for((me_z + s) % n_z), "tensor", ring[s]))
+        feature_rows = lax.all_gather(jnp.concatenate(blocks, axis=1), "dp", axis=0, tiled=True)
+
+        d_queries, d_projected = attention_backward(projected, queries, d_out, segments[0])
+
+        partial = lax.dot_general(
+            held[:n_z],
+            d_projected,
+            (((1,), (0,)), ((), ())),
+            preferred_element_type=jnp.float32,
+        ).reshape(n_z * feats, cols)
+        new_grad = lax.psum_scatter(
+            partial.astype(jnp.bfloat16), "dp", scatter_dimension=0, tiled=True
+        ).astype(jnp.float32)
+
+        pieces = [d_projected] + [
+            lax.ppermute(d_projected, "tensor", ring[s]) for s in range(1, n_z)
+        ]
+        d_tokens = lax.dot_general(
+            jnp.concatenate(pieces, axis=1),
+            feature_rows,
+            (((1,), (1,)), ((), ())),
+            preferred_element_type=jnp.float32,
+        ).astype(jnp.bfloat16)
+        return (master_new, moment_new, second_new, new_cache, new_grad, d_queries, d_tokens)
+
+    return body
 
 
 def solution(mesh):
@@ -117,4 +165,5 @@
         P("dp", "tensor"),
         P("dp", "tensor"),
     )
+    body = make_body(mesh.shape["dp"], mesh.shape["tensor"])
     return jax.shard_map(body, mesh=mesh, in_specs=in_specs, out_specs=out_specs, check_vma=False)

time: 369 us -> 199 us (0.54)
  waiting for transfers between devices: 261 us -> 93.6 us
  starting transfers between devices: 0.16 us -> 30.9 us
  blocking collectives: 24.5 us -> 0 us
  local copies, waits for them, and re-layouts: 32.2 us -> 27.8 us
    reduce_scatter x2 -> x1, waiting for transfers between devices: 187 us -> 36.8 us  [body(): lax.psum_scatter(partial.astype(jnp.bfloat16), 'dp', scatter_dimension=0,...]
    all_gather x2, waiting for transfers between devices: 73.6 us -> 0.01 us  [the longest x1 0.01 us: body(): new_cache = lax.all_gather(own_new, 'dp', axis=0, tiled=True)]
    ppermute x0 -> x12, waiting for transfers between devices: none -> 56.8 us  [the longest x3 23.9 us: body(): blocks.append(lax.ppermute(block_for((me_z + s) % n_z), 'tensor', ring[s]))]
    ppermute x0 -> x12, starting transfers between devices: none -> 30.8 us  [the longest x3 14.4 us: body(): from_low = lax.ppermute(from_low, 'tensor', up)]
    all_gather x1 -> x0, blocking collectives: 24.5 us -> none  [body(): lax.all_gather((codes, block_scale), 'dp', axis=0, tiled=True)]
    mul x1 -> x0, local copies, waits for them, and re-layouts: 22.9 us -> none  [body(): code_rows.astype(jnp.float32).reshape(height, -1, HD)]
    dynamic_update_slice x0 -> x7, local copies, waits for them, and re-layouts: none -> 9.84 us  [the longest x3 4.41 us: body(): lax.dynamic_update_slice(held, from_high[None], (jnp.where(high < n_z, hi...]
    convert_element_type x5, other arithmetic: 10.4 us -> 5.68 us  [the longest x1 2.14 us: optimizer(): own_new = (own_cache + scaled.reshape(rows_here, -1)).astype(jnp.bfloat16)]
  transfers between devices with their start and end apart: 4 -> 15, of which waited for: 3 -> 5; matrix products, arithmetic and copies ran while one was open for 18% -> 21% of each run, Pallas kernels for 0% -> 0%
where the time goes in v1:
time: 199 us; the launch traced here: 198 us
  waiting for transfers between devices  93.6 us (47%)
  starting transfers between devices  30.9 us (16%)
  local copies, waits for them, and re-layouts  27.8 us (14%)
  matrix products  18.3 us (9%)
  between operations  14.2 us (7%)
  other arithmetic  13.4 us (7%)
    reduce_scatter x1, waiting for transfers between devices, body(): lax.psum_scatter(partial.astype(jnp.bfloat16), 'dp', scatter_dimension=0,...  36.8 us
    ppermute x3, waiting for transfers between devices, body(): blocks.append(lax.ppermute(block_for((me_z + s) % n_z), 'tensor', ring[s]))  23.9 us
    ppermute x3, waiting for transfers between devices, body(): from_low = lax.ppermute(from_low, 'tensor', up)  16.7 us
    ppermute x3, starting transfers between devices, body(): from_low = lax.ppermute(from_low, 'tensor', up)  14.4 us
    ppermute x3, waiting for transfers between devices, body(): from_high = lax.ppermute(from_high, 'tensor', down)  13 us
    unnamed x19, local copies, waits for them, and re-layouts  7.3 us
    dot_general x7, matrix products, part(): return jnp.dot(chunk, rows, preferred_element_type=jnp.float32)  7.24 us
    ppermute x3, starting transfers between devices, body(): lax.ppermute(d_projected, 'tensor', ring[s])  6.37 us
  transfers between devices with their start and end apart: 15, of which 5 were waited for; matrix products, arithmetic and copies ran while one was open for 21% of the time, Pallas kernels for 0%

profile of v1, /device:TPU:0, one launch (start us, length us, event | category | flops | bytes accessed | tf_op | source)
XLA Modules:
  0.0 198.2 jit_solution(9057934542227013855)
XLA Ops:
  7.2 4.5 %fusion.26 = (f32[1024,256]{1,0:T(8,128)S(1)}, f32[1024,256]{1,0:T(8,128)S(1)}, f32[1024,256]{1,0:T(8,128)}, f32[1024,256]{1,0:T(8,128)}) fusion(bf16[8192,256]{1,0:T(8,128)(2,1)} %param.13, s32[]{:T(128)S(6)} %select_n.95, f32[1024,256]{1,0:T(8,128)} %param.14, f32[1024,256]{1,0:T(8,128)} %param.17, f32[1024,256]{1,0:T(8,128)} %param.15, f32[1024,256]{1,0:T(8,128)} %param.16), kind=kLoop, calls=%fused_computation.53 | loop fusion | flops 4718592 | bytes 8912900 | tf_op jit(solution)/shard_map/abs | solution.py:29
  11.7 0.5 abs.7
  12.3 1.9 reduce_max.18
  14.2 1.1 fusion.35
  15.3 1.2 div.39
  16.6 2.1 %fusion.11 = bf16[1024,256]{1,0:T(8,128)(2,1)} fusion(f32[128,8,2,128]{3,2,1,0:T(2,128)S(1)} %bitcast.136, f32[1024,256]{1,0:T(8,128)S(1)} %get-tuple-element.52, bf16[8192,256]{1,0:T(8,128)(2,1)} %param.13, s32[]{:T(128)S(6)} %select_n.95), kind=kLoop, calls=%fused_computation.27 | loop fusion | flops 2097152 | bytes 3145732 | tf_op jit(solution)/shard_map/convert_element_type | solution.py:33
  18.8 1.3 copy.67
  20.1 5.0 %collective-permute-start = (bf16[256,2048]{0,1:T(8,128)(2,1)}, bf16[256,2048]{0,1:T(8,128)(2,1)S(1)}, u32[]{:S(2)}, u32[]{:S(2)}) collective-permute-start(bf16[256,2048]{0,1:T(8,128)(2,1)} %copy.67), channel_id=1, source_target_pairs={{0,1},{1,2},{2,3},{4,5},{5,6},{6,7},{8,9},{9,10},{10,11},{12,13},{... | collective-permute-start | bytes 3145736 | tf_op jit(solution)/shard_map/ppermute | solution.py:94
  25.1 1.3 collective-permute-start.1
  26.5 1.1 constant_dynamic-slice_fusion.3
  27.6 3.7 %collective-permute-start.10 = (bf16[256,256]{1,0:T(8,128)(2,1)S(1)}, bf16[256,256]{1,0:T(8,128)(2,1)S(1)}, u32[]{:S(2)}, u32[]{:S(2)}) collective-permute-start(bf16[256,256]{1,0:T(8,128)(2,1)S(1)} %get-tuple-element.42), channel_id=1, source_target_pairs={{0,2},{1,3},{2,0},{3,1},{4,6},{5,7},{6,4},{7,5},{8,10},{9,11},{10,... | collective-permute-start | bytes 393224 | tf_op jit(solution)/shard_map/ppermute | solution.py:118
  31.3 2.0 %collective-permute-start.11 = (bf16[256,256]{1,0:T(8,128)(2,1)S(1)}, bf16[256,256]{1,0:T(8,128)(2,1)S(1)}, u32[]{:S(2)}, u32[]{:S(2)}) collective-permute-start(bf16[256,256]{1,0:T(8,128)(2,1)S(1)} %get-tuple-element.41), channel_id=1, source_target_pairs={{0,3},{1,0},{2,1},{3,2},{4,7},{5,4},{6,5},{7,6},{8,11},{9,8},{10,9... | collective-permute-start | bytes 393224 | tf_op jit(solution)/shard_map/ppermute | solution.py:118
  33.3 0.5 collective-permute-start.9
  33.8 2.6 %broadcast_in_dim.38 = bf16[5,256,2048]{1,2,0:T(8,128)(2,1)} broadcast(bf16[]{:T(256)} %constant.67.clone.1), dimensions={} | broadcast | bytes 5242882 | tf_op jit(solution)/shard_map/broadcast_in_dim | solution.py:90
  36.4 2.3 %bitcast_dynamic-update-slice_fusion.6 = bf16[5,256,2048]{1,2,0:T(8,128)(2,1)} fusion(bf16[5,256,2048]{1,2,0:T(8,128)(2,1)} %broadcast_in_dim.38, s32[]{:T(128)S(6)} %select_n.96, bf16[256,2048]{0,1:T(8,128)(2,1)} %copy.67), kind=kLoop, calls=%fused_computation.40 | loop fusion | bytes 2097156 | tf_op jit(solution)/shard_map/dynamic_update_slice | solution.py:91
  38.7 23.9 %collective-permute-done.10 = bf16[256,256]{1,0:T(8,128)(2,1)S(1)} collective-permute-done((bf16[256,256]{1,0:T(8,128)(2,1)S(1)}, bf16[256,256]{1,0:T(8,128)(2,1)S(1)}, u32[]{:S(2)}, u32[]{:S(2)}) %collective-permute-start.10) | collective-permute-done | bytes 131104 | tf_op jit(solution)/shard_map/ppermute | solution.py:118
  62.6 0.9 pad_maximum_fusion
  63.7 1.2 copy.74
  65.2 1.2 copy.94
  66.5 1.9 fusion.24
  68.3 1.3 collective-permute-start.3
  69.7 4.6 %collective-permute-start.2 = (bf16[256,2048]{0,1:T(8,128)(2,1)S(1)}, bf16[256,2048]{0,1:T(8,128)(2,1)S(1)}, u32[]{:S(2)}, u32[]{:S(2)}) collective-permute-start(bf16[256,2048]{0,1:T(8,128)(2,1)S(1)} %collective-permute-done), channel_id=1, source_target_pairs={{0,1},{1,2},{2,3},{4,5},{5,6},{6,7},{8,9},{9,10},{10,11},{12,13},{... | collective-permute-start | bytes 3145736 | tf_op jit(solution)/shard_map/ppermute | solution.py:94
  74.3 1.7 convolution_add_fusion.3
  76.0 1.7 convolution_add_fusion.2
  77.7 1.1 bitcast_dynamic-update-slice_fusion.5
  78.8 2.3 %bitcast_dynamic-update-slice_fusion.4 = bf16[5,256,2048]{1,2,0:T(8,128)(2,1)} fusion(bf16[5,256,2048]{1,2,0:T(8,128)(2,1)} %bitcast_dynamic-update-slice_fusion.5, s32[]{:T(128)S(6)} %select_n.100, bf16[256,2048]{0,1:T(8,128)(2,1)} %collective-permute-done.1), kind=kLoop, calls=%fused_computation.38 | loop fusion | bytes 2097156 | tf_op jit(solution)/shard_map/dynamic_update_slice | solution.py:101
  81.1 13.0 %collective-permute-done.3 = bf16[256,2048]{0,1:T(8,128)(2,1)S(1)} collective-permute-done((bf16[256,2048]{0,1:T(8,128)(2,1)}, bf16[256,2048]{0,1:T(8,128)(2,1)S(1)}, u32[]{:S(2)}, u32[]{:S(2)}) %collective-permute-start.3) | collective-permute-done | bytes 1048608 | tf_op jit(solution)/shard_map/ppermute | solution.py:95
  94.1 1.3 collective-permute-start.5
  95.4 4.8 %collective-permute-start.4 = (bf16[256,2048]{0,1:T(8,128)(2,1)S(1)}, bf16[256,2048]{0,1:T(8,128)(2,1)S(1)}, u32[]{:S(2)}, u32[]{:S(2)}) collective-permute-start(bf16[256,2048]{0,1:T(8,128)(2,1)S(1)} %collective-permute-done.2), channel_id=1, source_target_pairs={{0,1},{1,2},{2,3},{4,5},{5,6},{6,7},{8,9},{9,10},{10,11},{12,13},{... | collective-permute-start | bytes 3145736 | tf_op jit(solution)/shard_map/ppermute | solution.py:94
  100.2 1.1 bitcast_dynamic-update-slice_fusion.3
  102.2 1.0 bitcast_dynamic-update-slice_fusion.2
  103.3 16.7 %collective-permute-done.4 = bf16[256,2048]{0,1:T(8,128)(2,1)S(1)} collective-permute-done((bf16[256,2048]{0,1:T(8,128)(2,1)S(1)}, bf16[256,2048]{0,1:T(8,128)(2,1)S(1)}, u32[]{:S(2)}, u32[]{:S(2)}) %collective-permute-start.4) | collective-permute-done | bytes 1048608 | tf_op jit(solution)/shard_map/ppermute | solution.py:94
  120.0 1.0 bitcast_dynamic-update-slice_fusion.1
  121.0 1.1 bitcast_dynamic-update-slice_fusion
  122.1 2.5 %slice.12 = bf16[4,256,2048]{1,2,0:T(8,128)(2,1)S(1)} slice(bf16[5,256,2048]{1,2,0:T(8,128)(2,1)} %bitcast_dynamic-update-slice_fusion), slice={[0:4], [0:256], [0:2048]} | slice | bytes 8388608 | tf_op jit(solution)/shard_map/slice | solution.py:124
  125.1 0.5 fusion.10
  125.6 0.5 fusion.46
  127.6 0.7 fusion.5
  129.3 3.3 %convolution_convert_fusion = bf16[8192,256]{1,0:T(8,128)(2,1)} fusion(bf16[8192,256]{1,0:T(8,128)(2,1)S(1)} %bitcast.132, bf16[256,256]{0,1:T(8,128)(2,1)S(1)} %bitcast.144), kind=kOutput, calls=%fused_computation | convolution fusion | flops 1075838976 | bytes 8519680 | tf_op jit(solution)/shard_map/dot_general | solution.py:123
  132.6 2.5 %collective-permute-start.6 = (bf16[256,256]{0,1:T(8,128)(2,1)S(1)}, bf16[256,256]{0,1:T(8,128)(2,1)S(1)}, u32[]{:S(2)}, u32[]{:S(2)}) collective-permute-start(bf16[256,256]{0,1:T(8,128)(2,1)S(1)} %bitcast.145), channel_id=1, source_target_pairs={{0,1},{1,2},{2,3},{3,0},{4,5},{5,6},{6,7},{7,4},{8,9},{9,10},{10,1... | collective-permute-start | bytes 393224 | tf_op jit(solution)/shard_map/ppermute | solution.py:134
  135.1 1.2 collective-permute-start.7
  136.3 2.6 %collective-permute-start.8 = (bf16[256,256]{0,1:T(8,128)(2,1)S(1)}, bf16[256,256]{0,1:T(8,128)(2,1)S(1)}, u32[]{:S(2)}, u32[]{:S(2)}) collective-permute-start(bf16[256,256]{0,1:T(8,128)(2,1)S(1)} %bitcast.147), channel_id=1, source_target_pairs={{0,3},{1,0},{2,1},{3,2},{4,7},{5,4},{6,5},{7,6},{8,11},{9,8},{10,9... | collective-permute-start | bytes 393224 | tf_op jit(solution)/shard_map/ppermute | solution.py:134
  139.3 1.0 copy.83
  140.3 3.1 %collective-permute-done.7 = bf16[256,256]{0,1:T(8,128)(2,1)S(1)} collective-permute-done((bf16[256,256]{0,1:T(8,128)(2,1)S(1)}, bf16[256,256]{0,1:T(8,128)(2,1)S(1)}, u32[]{:S(2)}, u32[]{:S(2)}) %collective-permute-start.7) | collective-permute-done | bytes 131104 | tf_op jit(solution)/shard_map/ppermute | solution.py:134
  143.4 4.9 %convolution_convert_fusion.1 = bf16[256,2048]{1,0:T(8,128)(2,1)} fusion(bf16[2048,1024]{1,0:T(8,128)(2,1)} %all-gather.5.cloned.1.call-done, bf16[256,256]{0,1:T(8,128)(2,1)S(1)} %collective-permute-done.8, bf16[256,256]{0,1:T(8,128)(2,1)S(1)} %collective-permute-done.7, bf16[256,256]{0,1:T(8,128)(2,1)S(1)} %collective-permute-done.6, ...), kind=kOutput, calls=%fused_computation.1 | convolution fusion | flops 1076363264 | bytes 5767168 | tf_op jit(solution)/shard_map/dot_general | solution.py:136
  148.4 36.8 %reduce-scatter.2.cloned.1.call-done = bf16[1024,256]{1,0:T(8,128)(2,1)} async-done(((bf16[8192,256]{1,0:T(8,128)(2,1)}), bf16[1024,256]{1,0:T(8,128)(2,1)}) %reduce-scatter.2.cloned.1.call-update) | async-done | bytes 524304 | tf_op jit(solution)/shard_map/reduce_scatter | solution.py:129
  185.1 2.1 %convert_element_type.107 = f32[1024,256]{1,0:T(8,128)} convert(bf16[1024,256]{1,0:T(8,128)(2,1)} %reduce-scatter.2.cloned.1.call-done) | non-fusion elementwise | flops 262144 | bytes 1572864 | tf_op jit(solution)/shard_map/convert_element_type | solution.py:131
  187.2 4.5 %copy.110 = bf16[8192,256]{1,0:T(8,128)(2,1)} copy(bf16[8192,256]{1,0:T(8,128)(2,1)} %all-gather.3.cloned.1.call-done) | data formatting | bytes 8388608
  (44 shorter events, 4.7 us)
Async XLA Ops:
  7.2 133.1 %all-gather.3.cloned.1.call-start = ((), (), s32[]{:S(2)}) async-start(), calls=%async_computation.1 | async-start | bytes 4718592 | tf_op jit(solution)/shard_map/all_gather | solution.py:109
  11.7 7.0 %copy-start.1 = (f32[1024,256]{1,0:T(8,128)}, f32[1024,256]{1,0:T(8,128)S(1)}, u32[]{:S(2)}) copy-start(f32[1024,256]{1,0:T(8,128)S(1)} %get-tuple-element.52) | copy-start | bytes 3145732
  12.3 6.5 %copy-start.2 = (bf16[256,2048]{1,0:T(8,128)(2,1)S(1)}, bf16[256,2048]{1,0:T(8,128)(2,1)}, u32[]{:S(2)}) copy-start(bf16[256,2048]{1,0:T(8,128)(2,1)} %param.9) | copy-start | bytes 3145732
  18.7 124.7 %all-gather.5.cloned.1.call-start = ((), (), s32[]{:S(2)}) async-start(), calls=%async_computation.3 | async-start | bytes 4718592 | tf_op jit(solution)/shard_map/all_gather | solution.py:119
  20.1 49.5 %collective-permute-start = (bf16[256,2048]{0,1:T(8,128)(2,1)}, bf16[256,2048]{0,1:T(8,128)(2,1)S(1)}, u32[]{:S(2)}, u32[]{:S(2)}) collective-permute-start(bf16[256,2048]{0,1:T(8,128)(2,1)} %copy.67), channel_id=1, source_target_pairs={{0,1},{1,2},{2,3},{4,5},{5,6},{6,7},{8,9},{9,10},{10,11},{12,13},{... | collective-permute-start | bytes 3145736 | tf_op jit(solution)/shard_map/ppermute | solution.py:94
  25.1 43.2 %collective-permute-start.1 = (bf16[256,2048]{0,1:T(8,128)(2,1)}, bf16[256,2048]{0,1:T(8,128)(2,1)}, u32[]{:S(2)}, u32[]{:S(2)}) collective-permute-start(bf16[256,2048]{0,1:T(8,128)(2,1)} %copy.67), channel_id=1, source_target_pairs={{1,0},{2,1},{3,2},{5,4},{6,5},{7,6},{9,8},{10,9},{11,10},{13,12},{... | collective-permute-start | bytes 3145736 | tf_op jit(solution)/shard_map/ppermute | solution.py:95
  27.6 35.0 %collective-permute-start.10 = (bf16[256,256]{1,0:T(8,128)(2,1)S(1)}, bf16[256,256]{1,0:T(8,128)(2,1)S(1)}, u32[]{:S(2)}, u32[]{:S(2)}) collective-permute-start(bf16[256,256]{1,0:T(8,128)(2,1)S(1)} %get-tuple-element.42), channel_id=1, source_target_pairs={{0,2},{1,3},{2,0},{3,1},{4,6},{5,7},{6,4},{7,5},{8,10},{9,11},{10,... | collective-permute-start | bytes 393224 | tf_op jit(solution)/shard_map/ppermute | solution.py:118
  31.3 31.3 %collective-permute-start.11 = (bf16[256,256]{1,0:T(8,128)(2,1)S(1)}, bf16[256,256]{1,0:T(8,128)(2,1)S(1)}, u32[]{:S(2)}, u32[]{:S(2)}) collective-permute-start(bf16[256,256]{1,0:T(8,128)(2,1)S(1)} %get-tuple-element.41), channel_id=1, source_target_pairs={{0,3},{1,0},{2,1},{3,2},{4,7},{5,4},{6,5},{7,6},{8,11},{9,8},{10,9... | collective-permute-start | bytes 393224 | tf_op jit(solution)/shard_map/ppermute | solution.py:118
  33.3 29.3 %collective-permute-start.9 = (bf16[256,256]{1,0:T(8,128)(2,1)S(1)}, bf16[256,256]{1,0:T(8,128)(2,1)S(1)}, u32[]{:S(2)}, u32[]{:S(2)}) collective-permute-start(bf16[256,256]{1,0:T(8,128)(2,1)S(1)} %get-tuple-element.40), channel_id=1, source_target_pairs={{0,1},{1,2},{2,3},{3,0},{4,5},{5,6},{6,7},{7,4},{8,9},{9,10},{10,1... | collective-permute-start | bytes 393224 | tf_op jit(solution)/shard_map/ppermute | solution.py:118
  33.8 29.8 %copy-start.7 = (s32[1,256]{1,0:T(1,128)S(1)}, s32[1,256]{1,0:T(1,128)}, u32[]{:S(2)}) copy-start(s32[1,256]{1,0:T(1,128)} %param.12) | copy-start | bytes 3076
  33.8 29.9 %copy-start.6 = (bf16[256,1024]{1,0:T(8,128)(2,1)S(1)}, bf16[256,1024]{1,0:T(8,128)(2,1)}, u32[]{:S(2)}) copy-start(bf16[256,1024]{1,0:T(8,128)(2,1)} %param.11) | copy-start | bytes 1572868
  63.5 121.6 %reduce-scatter.2.cloned.1.call-start = ((), (), s32[]{:S(2)}) async-start(), calls=%async_computation.2 | async-start | bytes 4718592 | tf_op jit(solution)/shard_map/reduce_scatter | solution.py:129
  66.5 9.5 %copy-start = (bf16[8192,256]{1,0:T(8,128)(2,1)S(1)}, bf16[8192,256]{1,0:T(8,128)(2,1)}, u32[]{:S(2)}) copy-start(bf16[8192,256]{1,0:T(8,128)(2,1)} %param.13) | copy-start | bytes 12582916
  68.3 25.7 %collective-permute-start.3 = (bf16[256,2048]{0,1:T(8,128)(2,1)}, bf16[256,2048]{0,1:T(8,128)(2,1)S(1)}, u32[]{:S(2)}, u32[]{:S(2)}) collective-permute-start(bf16[256,2048]{0,1:T(8,128)(2,1)} %collective-permute-done.1), channel_id=1, source_target_pairs={{1,0},{2,1},{3,2},{5,4},{6,5},{7,6},{9,8},{10,9},{11,10},{13,12},{... | collective-permute-start | bytes 3145736 | tf_op jit(solution)/shard_map/ppermute | solution.py:95
  69.7 25.7 %collective-permute-start.2 = (bf16[256,2048]{0,1:T(8,128)(2,1)S(1)}, bf16[256,2048]{0,1:T(8,128)(2,1)S(1)}, u32[]{:S(2)}, u32[]{:S(2)}) collective-permute-start(bf16[256,2048]{0,1:T(8,128)(2,1)S(1)} %collective-permute-done), channel_id=1, source_target_pairs={{0,1},{1,2},{2,3},{4,5},{5,6},{6,7},{8,9},{9,10},{10,11},{12,13},{... | collective-permute-start | bytes 3145736 | tf_op jit(solution)/shard_map/ppermute | solution.py:94
  94.1 27.0 %collective-permute-start.5 = (bf16[256,2048]{0,1:T(8,128)(2,1)S(1)}, bf16[256,2048]{0,1:T(8,128)(2,1)S(1)}, u32[]{:S(2)}, u32[]{:S(2)}) collective-permute-start(bf16[256,2048]{0,1:T(8,128)(2,1)S(1)} %collective-permute-done.3), channel_id=1, source_target_pairs={{1,0},{2,1},{3,2},{5,4},{6,5},{7,6},{9,8},{10,9},{11,10},{13,12},{... | collective-permute-start | bytes 3145736 | tf_op jit(solution)/shard_map/ppermute | solution.py:95
  95.4 24.6 %collective-permute-start.4 = (bf16[256,2048]{0,1:T(8,128)(2,1)S(1)}, bf16[256,2048]{0,1:T(8,128)(2,1)S(1)}, u32[]{:S(2)}, u32[]{:S(2)}) collective-permute-start(bf16[256,2048]{0,1:T(8,128)(2,1)S(1)} %collective-permute-done.2), channel_id=1, source_target_pairs={{0,1},{1,2},{2,3},{4,5},{5,6},{6,7},{8,9},{9,10},{10,11},{12,13},{... | collective-permute-start | bytes 3145736 | tf_op jit(solution)/shard_map/ppermute | solution.py:94
  125.6 1.7 copy-start.3
  128.3 1.0 copy-start.4
  132.6 6.4 %copy-start.5 = (bf16[8,256,256]{1,2,0:T(8,128)(2,1)S(1)}, bf16[8,256,256]{1,2,0:T(8,128)(2,1)}, u32[]{:S(2)}) copy-start(bf16[8,256,256]{1,2,0:T(8,128)(2,1)} %copy-done.4) | copy-start | bytes 3145732
  132.6 7.7 %collective-permute-start.6 = (bf16[256,256]{0,1:T(8,128)(2,1)S(1)}, bf16[256,256]{0,1:T(8,128)(2,1)S(1)}, u32[]{:S(2)}, u32[]{:S(2)}) collective-permute-start(bf16[256,256]{0,1:T(8,128)(2,1)S(1)} %bitcast.145), channel_id=1, source_target_pairs={{0,1},{1,2},{2,3},{3,0},{4,5},{5,6},{6,7},{7,4},{8,9},{9,10},{10,1... | collective-permute-start | bytes 393224 | tf_op jit(solution)/shard_map/ppermute | solution.py:134
  135.1 8.3 %collective-permute-start.7 = (bf16[256,256]{0,1:T(8,128)(2,1)S(1)}, bf16[256,256]{0,1:T(8,128)(2,1)S(1)}, u32[]{:S(2)}, u32[]{:S(2)}) collective-permute-start(bf16[256,256]{0,1:T(8,128)(2,1)S(1)} %bitcast.146), channel_id=1, source_target_pairs={{0,2},{1,3},{2,0},{3,1},{4,6},{5,7},{6,4},{7,5},{8,10},{9,11},{10,... | collective-permute-start | bytes 393224 | tf_op jit(solution)/shard_map/ppermute | solution.py:134
  136.3 7.1 %collective-permute-start.8 = (bf16[256,256]{0,1:T(8,128)(2,1)S(1)}, bf16[256,256]{0,1:T(8,128)(2,1)S(1)}, u32[]{:S(2)}, u32[]{:S(2)}) collective-permute-start(bf16[256,256]{0,1:T(8,128)(2,1)S(1)} %bitcast.147), channel_id=1, source_target_pairs={{0,3},{1,0},{2,1},{3,2},{4,7},{5,4},{6,5},{7,6},{8,11},{9,8},{10,9... | collective-permute-start | bytes 393224 | tf_op jit(solution)/shard_map/ppermute | solution.py:134
Sparse Core Ops, SparseCore 0:
  18.9 39.4 all-gather.2
  63.7 36.3 all-gather.4
  132.7 52.3 reduce-scatter.1

commit v2 on v1

--- a/solution.py
+++ b/solution.py
@@ -3,6 +3,8 @@
 import jax
 import jax.numpy as jnp
 from jax import lax
+from jax.experimental import pallas as pl
+from jax.experimental.pallas import tpu as pltpu
 from jax.sharding import PartitionSpec as P
 
 HD = 128
@@ -17,21 +19,48 @@
 second_fix = 1.0 - 0.95**40
 
 
+def optimizer_kernel(
+    place, cached, master, moment, second, grad, master_out, moment_out, second_out, cache_out
+):
+    moment_new = beta_first * moment[...] + (1.0 - beta_first) * grad[...]
+    second_new = beta_second * second[...] + (1.0 - beta_second) * grad[...] * grad[...]
+    update = moment_new / first_fix / (jnp.sqrt(second_new / second_fix) + adam_epsilon)
+    master_new = master[...] - learn_rate * (update + weight_decay * master[...])
+    moment_out[...] = moment_new
+    second_out[...] = second_new
+    master_out[...] = master_new
+    for start in range(0, cached.shape[1], HD):
+        block = slice(start, start + HD)
+        own_cache = cached[:, block].astype(jnp.float32)
+        delta = master_new[:, block] - own_cache
+        largest = jnp.max(jnp.abs(delta), axis=1, keepdims=True)
+        scale = (largest + 1e-06).astype(jnp.bfloat16).astype(jnp.float32)
+        codes = (delta / scale).astype(jnp.bfloat16)
+        cache_out[:, block] = (own_cache + codes.astype(jnp.float32) * scale).astype(jnp.bfloat16)
+
+
 def optimizer(cached, master, moment, second, grad):
-    rows_here = master.shape[0]
-    first_row = lax.axis_index("dp") * rows_here
-    moment_new = beta_first * moment + (1.0 - beta_first) * grad
-    second_new = beta_second * second + (1.0 - beta_second) * grad * grad
-    update = moment_new / first_fix / (jnp.sqrt(second_new / second_fix) + adam_epsilon)
-    master_new = master - learn_rate * (update + weight_decay * master)
-    own_cache = lax.dynamic_slice_in_dim(cached, first_row, rows_here, 0).astype(jnp.float32)
-    blocks = (master_new - own_cache).reshape(rows_here, -1, HD)
-    block_scale = (jnp.max(jnp.abs(blocks), axis=2, keepdims=True) + 1e-06).astype(jnp.bfloat16)
-    scale = block_scale.astype(jnp.float32)
-    codes = (blocks / scale).astype(jnp.bfloat16)
-    scaled = codes.astype(jnp.float32) * scale
-    own_new = (own_cache + scaled.reshape(rows_here, -1)).astype(jnp.bfloat16)
-    return master_new, moment_new, second_new, own_new
+    rows, cols = master.shape
+    step = min(rows, 256)
+    steps = rows // step
+    own = pl.BlockSpec((step, cols), lambda i, place: (i, 0))
+    full = jax.ShapeDtypeStruct((rows, cols), jnp.float32)
+    return pl.pallas_call(
+        optimizer_kernel,
+        grid_spec=pltpu.PrefetchScalarGridSpec(
+            num_scalar_prefetch=1,
+            grid=(steps,),
+            in_specs=[pl.BlockSpec((step, cols), lambda i, place: (place[0] * steps + i, 0))]
+            + [own] * 4,
+            out_specs=[own] * 4,
+        ),
+        out_shape=[full, full, full, jax.ShapeDtypeStruct((rows, cols), jnp.bfloat16)],
+        cost_estimate=pl.CostEstimate(
+            flops=40 * rows * cols, bytes_accessed=32 * rows * cols, transcendentals=rows * cols
+        ),
+        compiler_params=pltpu.CompilerParams(vmem_limit_bytes=32 * 1024 * 1024),
+        name="optimizer",
+    )(lax.axis_index("dp").astype(jnp.int32).reshape(1), cached, master, moment, second, grad)
 
 
 def attention_backward(projected, queries, d_out, doc_ids):
@@ -71,10 +100,84 @@
     return d_queries, d_projected
 
 
+def weight_kernel(place, chunk_a, chunk_b, d_projected, *refs):
+    *added, out_a, out_b = refs
+    half = out_a.shape[-1]
+    for side, (chunk, out) in enumerate(((chunk_a, out_a), (chunk_b, out_b))):
+        columns = d_projected[:, side * half : (side + 1) * half]
+        total = lax.dot_general(
+            chunk[0], columns, (((0,), (0,)), ((), ())), preferred_element_type=jnp.float32
+        )
+        if added:
+            total = total + added[side][0].astype(jnp.float32)
+        out[0] = total.astype(out.dtype)
+
+
+def weight_parts(held, d_projected, place, added, dtype, name):
+    length, cols = d_projected.shape
+    rows = held.shape[2] // 2
+    half = cols // 2
+    out = pl.BlockSpec((1, rows, half), lambda k, place: (k, 0, 0))
+    shape = jax.ShapeDtypeStruct((2, rows, half), dtype)
+    return pl.pallas_call(
+        weight_kernel,
+        grid_spec=pltpu.PrefetchScalarGridSpec(
+            num_scalar_prefetch=1,
+            grid=(2,),
+            in_specs=[
+                pl.BlockSpec((1, length, rows), lambda k, place: (place[k], 0, place[4])),
+                pl.BlockSpec((1, length, rows), lambda k, place: (place[2 + k], 0, place[4])),
+                pl.BlockSpec((length, cols), lambda k, place: (0, 0)),
+            ]
+            + [out] * len(added),
+            out_specs=[out, out],
+        ),
+        out_shape=[shape, shape],
+        cost_estimate=pl.CostEstimate(
+            flops=4 * length * rows * cols, bytes_accessed=8 * rows * cols, transcendentals=0
+        ),
+        compiler_params=pltpu.CompilerParams(vmem_limit_bytes=32 * 1024 * 1024),
+        name=name,
+    )(place, held, held, d_projected, *added)
+
+
+def weight_sum(held, d_projected):
+    index = lax.axis_index("dp").astype(jnp.int32)
+    core, x, y = index % 2, (index // 2) % 2, index // 4
+
+    def swap(value, bit):
+        return lax.ppermute(value, "dp", [(i, i ^ bit) for i in range(8)])
+
+    zero = jnp.zeros_like(x)
+    send = [1 - x, 3 - x, 2 - 2 * y, 3 - 2 * y]
+    keep = [x, 2 + x, 2 * y, 2 * y + 1]
+
+    def parts(chunks, which, added, dtype, name):
+        place = jnp.stack(chunks + [which + zero])
+        return weight_parts(held, d_projected, place, added, dtype, name)
+
+    theirs = parts(send, 1 - core, [], jnp.bfloat16, "weight_send_other")
+    theirs = [swap(part, 1) for part in theirs]
+    rest = parts(keep, 1 - core, [], jnp.bfloat16, "weight_keep_other")
+    rest = [swap(part, 1) for part in rest]
+    send_a, send_b = parts(send, core, theirs, jnp.bfloat16, "weight_send")
+    got_a, got_b = swap(send_a, 2), swap(send_b, 4)
+    keep_a, keep_b = parts(keep, core, rest, jnp.float32, "weight_keep")
+
+    def pick(keep, got, which):
+        return lax.dynamic_index_in_dim(keep, which, 0, False) + lax.dynamic_index_in_dim(
+            got, which, 0, False
+        ).astype(jnp.float32)
+
+    last_a = swap(pick(keep_a, got_a, 1 - y).astype(jnp.bfloat16), 4)
+    last_b = swap(pick(keep_b, got_b, 1 - x).astype(jnp.bfloat16), 2)
+    sum_a = pick(keep_a, got_a, y) + last_a.astype(jnp.float32)
+    sum_b = pick(keep_b, got_b, x) + last_b.astype(jnp.float32)
+    return jnp.concatenate([sum_a, sum_b], axis=1)
+
+
 def make_body(n_dp, n_z):
     ring = [[(z, (z + s) % n_z) for z in range(n_z)] for s in range(n_z)]
-    up = [(z, z + 1) for z in range(n_z - 1)]
-    down = [(z + 1, z) for z in range(n_z - 1)]
 
     def body(tokens, queries, d_out, segments, cached, master, moment, second, grad):
         me_dp = lax.axis_index("dp")
@@ -86,21 +189,31 @@
             rows = lax.dynamic_slice_in_dim(cached, jnp.clip(index, 0, n_z - 1) * feats, feats, 0)
             return jnp.dot(chunk, rows, preferred_element_type=jnp.float32)
 
+        def hold(held, chunk, index):
+            slot = jnp.where((index >= 0) & (index < n_z), index, n_z)
+            return lax.dynamic_update_slice(held, chunk[None], (slot, 0, 0))
+
         projected = part(tokens, me_z)
-        held = jnp.zeros((n_z + 1, length, feats), tokens.dtype)
-        held = lax.dynamic_update_slice(held, tokens[None], (me_z, 0, 0))
-        from_low, from_high = tokens, tokens
+        held = hold(jnp.zeros((n_z + 1, length, feats), tokens.dtype), tokens, me_z)
+        from_low, from_high, merged = tokens, tokens, None
         for s in range(1, n_z):
-            from_low = lax.ppermute(from_low, "tensor", up)
-            from_high = lax.ppermute(from_high, "tensor", down)
+            up = [(z, z + 1) for z in range(s - 1, n_z - 1)]
+            down = [(z + 1, z) for z in range(n_z - s)]
             low, high = me_z - s, me_z + s
-            projected = projected + part(from_low, low) + part(from_high, high)
-            held = lax.dynamic_update_slice(
-                held, from_low[None], (jnp.where(low >= 0, low, n_z), 0, 0)
-            )
-            held = lax.dynamic_update_slice(
-                held, from_high[None], (jnp.where(high < n_z, high, n_z), 0, 0)
-            )
+            if merged is None:
+                from_low = lax.ppermute(from_low, "tensor", up)
+                from_high = lax.ppermute(from_high, "tensor", down)
+            else:
+                merged = lax.ppermute(merged, "tensor", up + down)
+            if merged is None and 2 * s >= n_z:
+                merged = jnp.where(me_z >= s, from_low, from_high)
+            if merged is None:
+                projected = projected + part(from_low, low) + part(from_high, high)
+                held = hold(hold(held, from_low, low), from_high, high)
+            else:
+                origin = jnp.where(me_z >= s, low, high)
+                projected = projected + part(merged, origin)
+                held = hold(held, merged, origin)
         projected = projected.astype(jnp.bfloat16)
 
         master_new, moment_new, second_new, own_new = optimizer(
@@ -120,15 +233,18 @@
 
         d_queries, d_projected = attention_backward(projected, queries, d_out, segments[0])
 
-        partial = lax.dot_general(
-            held[:n_z],
-            d_projected,
-            (((1,), (0,)), ((), ())),
-            preferred_element_type=jnp.float32,
-        ).reshape(n_z * feats, cols)
-        new_grad = lax.psum_scatter(
-            partial.astype(jnp.bfloat16), "dp", scatter_dimension=0, tiled=True
-        ).astype(jnp.float32)
+        if n_dp == 8 and n_z == 4:
+            new_grad = weight_sum(held, d_projected)
+        else:
+            partial = lax.dot_general(
+                held[:n_z],
+                d_projected,
+                (((1,), (0,)), ((), ())),
+                preferred_element_type=jnp.float32,
+            ).reshape(n_z * feats, cols)
+            new_grad = lax.psum_scatter(
+                partial.astype(jnp.bfloat16), "dp", scatter_dimension=0, tiled=True
+            ).astype(jnp.float32)
 
         pieces = [d_projected] + [
             lax.ppermute(d_projected, "tensor", ring[s]) for s in range(1, n_z)

time: 199 us -> 172 us (0.86)
  waiting for transfers between devices: 93.6 us -> 62.8 us
  Pallas kernels: 0 us -> 16.2 us
  local copies, waits for them, and re-layouts: 27.8 us -> 22.8 us
  matrix products: 18.3 us -> 15.5 us
  starting transfers between devices: 30.9 us -> 28.3 us
  other arithmetic: 13.4 us -> 11.2 us
    reduce_scatter x1 -> x0, waiting for transfers between devices: 36.8 us -> none  [body(): lax.psum_scatter(partial.astype(jnp.bfloat16), 'dp', scatter_dimension=0,...]
    ppermute x0 -> x9, waiting for transfers between devices: none -> 25.5 us  [the longest x1 17.8 us: body(): merged = lax.ppermute(merged, 'tensor', up + down)]
    ppermute x3, waiting for transfers between devices: 23.9 us -> 4.66 us  [body(): blocks.append(lax.ppermute(block_for((me_z + s) % n_z), 'tensor', ring[s]))]
    pallas_call x0 -> x5, Pallas kernels: none -> 16.2 us  [the longest x4 13.5 us: weight_parts(): pl.pallas_call(weight_kernel, grid_spec=pltpu.PrefetchScalarGridSpec(num_...]
    ppermute x3 -> x2, waiting for transfers between devices: 13 us -> 22.1 us  [body(): from_high = lax.ppermute(from_high, 'tensor', down)]
    ppermute x0 -> x9, starting transfers between devices: none -> 8.38 us  [the longest x8 7.1 us: swap(): return lax.ppermute(value, 'dp', [(i, i ^ bit) for i in range(8)])]
    ppermute x3 -> x2, starting transfers between devices: 14.4 us -> 6.63 us  [body(): from_low = lax.ppermute(from_low, 'tensor', up)]
    ppermute x3 -> x2, waiting for transfers between devices: 16.7 us -> 10.4 us  [body(): from_low = lax.ppermute(from_low, 'tensor', up)]
  transfers between devices with their start and end apart: 15 -> 21, of which waited for: 5 -> 9; matrix products, arithmetic and copies ran while one was open for 21% -> 21% of each run, Pallas kernels for 0% -> 8%
where the time goes in v2:
time: 172 us; the launch traced here: 171 us
  waiting for transfers between devices  62.8 us (37%)
  starting transfers between devices  28.3 us (16%)
  local copies, waits for them, and re-layouts  22.8 us (13%)
  Pallas kernels  16.2 us (9%)
  matrix products  15.5 us (9%)
  between operations  14.5 us (8%)
  other arithmetic  11.2 us (7%)
    ppermute x2, waiting for transfers between devices, body(): from_high = lax.ppermute(from_high, 'tensor', down)  22.1 us
    ppermute x1, waiting for transfers between devices, body(): merged = lax.ppermute(merged, 'tensor', up + down)  17.8 us
    pallas_call x4, Pallas kernels, weight_parts(): pl.pallas_call(weight_kernel, grid_spec=pltpu.PrefetchScalarGridSpec(num_...  13.5 us
    ppermute x2, waiting for transfers between devices, body(): from_low = lax.ppermute(from_low, 'tensor', up)  10.4 us
    unnamed x30, local copies, waits for them, and re-layouts  10.1 us
    dot_general x5, matrix products, part(): return jnp.dot(chunk, rows, preferred_element_type=jnp.float32)  7.98 us
    ppermute x8, waiting for transfers between devices, swap(): return lax.ppermute(value, 'dp', [(i, i ^ bit) for i in range(8)])  7.67 us
    ppermute x8, starting transfers between devices, swap(): return lax.ppermute(value, 'dp', [(i, i ^ bit) for i in range(8)])  7.1 us
  transfers between devices with their start and end apart: 21, of which 9 were waited for; matrix products, arithmetic and copies ran while one was open for 21% of the time, Pallas kernels for 8%

profile of v2, /device:TPU:0, one launch (start us, length us, event | category | flops | bytes accessed | tf_op | source)
XLA Modules:
  0.0 171.3 jit_solution(9750850053816368545)
XLA Ops:
  7.2 2.2 %copy-done = bf16[8192,256]{1,0:T(8,128)(2,1)S(1)} copy-done((bf16[8192,256]{1,0:T(8,128)(2,1)S(1)}, bf16[8192,256]{1,0:T(8,128)(2,1)}, u32[]{:S(2)}) %copy-start) | copy-done | bytes 4194328
  9.4 1.2 copy-done.2
  10.6 1.2 copy-done.3
  11.9 1.2 copy-done.4
  13.1 1.2 copy-done.5
  14.3 2.7 %optimizer.1 = (f32[1024,256]{1,0:T(8,128)}, f32[1024,256]{1,0:T(8,128)}, f32[1024,256]{1,0:T(8,128)}, bf16[1024,256]{1,0:T(8,128)(2,1)}) custom-call(s32[1]{0:T(128)} %bitcast.place, bf16[8192,256]{1,0:T(8,128)(2,1)S(1)} %copy-done, f32[1024,256]{1,0:T(8,128)S(1)} %copy-done.2, f32[1024,256]{1,0:T(8,128)S(1)} %copy-done.3, f32[1024,256]{1,0:T(8,128)S(1)} %copy-done.4, ...), custom_call_target="tpu_custom_call" | custom-call | flops 10485760 | bytes 8388608 | tf_op jit(solution)/shard_map/optimizer/pallas_call | solution.py:48
  17.1 5.0 %collective-permute-start = (bf16[256,2048]{1,0:T(8,128)(2,1)S(1)}, bf16[256,2048]{1,0:T(8,128)(2,1)S(1)}, u32[]{:S(2)}, u32[]{:S(2)}) collective-permute-start(bf16[256,2048]{1,0:T(8,128)(2,1)S(1)} %copy-done.6), channel_id=1, source_target_pairs={{0,1},{1,2},{2,3},{4,5},{5,6},{6,7},{8,9},{9,10},{10,11},{12,13},{... | collective-permute-start | bytes 3145736 | tf_op jit(solution)/shard_map/ppermute | solution.py:204
  22.1 1.3 collective-permute-start.1
  23.4 1.1 constant_dynamic-slice_fusion.2
  24.6 2.7 %collective-permute-start.16 = (bf16[256,256]{1,0:T(8,128)(2,1)S(1)}, bf16[256,256]{1,0:T(8,128)(2,1)S(1)}, u32[]{:S(2)}, u32[]{:S(2)}) collective-permute-start(bf16[256,256]{1,0:T(8,128)(2,1)S(1)} %get-tuple-element.41), channel_id=1, source_target_pairs={{0,1},{1,2},{2,3},{3,0},{4,5},{5,6},{6,7},{7,4},{8,9},{9,10},{10,1... | collective-permute-start | bytes 393224 | tf_op jit(solution)/shard_map/ppermute | solution.py:231
  27.3 3.5 %collective-permute-start.17 = (bf16[256,256]{1,0:T(8,128)(2,1)S(1)}, bf16[256,256]{1,0:T(8,128)(2,1)S(1)}, u32[]{:S(2)}, u32[]{:S(2)}) collective-permute-start(bf16[256,256]{1,0:T(8,128)(2,1)S(1)} %get-tuple-element.43), channel_id=1, source_target_pairs={{0,2},{1,3},{2,0},{3,1},{4,6},{5,7},{6,4},{7,5},{8,10},{9,11},{10,... | collective-permute-start | bytes 393224 | tf_op jit(solution)/shard_map/ppermute | solution.py:231
  31.1 3.0 %broadcast_in_dim.31 = bf16[5,256,2048]{2,1,0:T(8,128)(2,1)} broadcast(bf16[]{:T(256)} %constant.98.clone.1), dimensions={} | broadcast | bytes 5242882 | tf_op jit(solution)/shard_map/broadcast_in_dim | solution.py:197
  34.1 1.0 bitcast_dynamic-update-slice_fusion.4
  35.2 10.4 %collective-permute-done = bf16[256,2048]{1,0:T(8,128)(2,1)S(1)} collective-permute-done((bf16[256,2048]{1,0:T(8,128)(2,1)S(1)}, bf16[256,2048]{1,0:T(8,128)(2,1)S(1)}, u32[]{:S(2)}, u32[]{:S(2)}) %collective-permute-start) | collective-permute-done | bytes 1048608 | tf_op jit(solution)/shard_map/ppermute | solution.py:204
  45.6 1.6 collective-permute-start.2
  47.2 6.3 %collective-permute-done.1 = bf16[256,2048]{1,0:T(8,128)(2,1)} collective-permute-done((bf16[256,2048]{1,0:T(8,128)(2,1)S(1)}, bf16[256,2048]{1,0:T(8,128)(2,1)}, u32[]{:S(2)}, u32[]{:S(2)}) %collective-permute-start.1) | collective-permute-done | bytes 1048608 | tf_op jit(solution)/shard_map/ppermute | solution.py:205
  53.5 1.3 collective-permute-start.3
  54.9 4.6 %collective-permute-done.17 = bf16[256,256]{1,0:T(8,128)(2,1)S(1)} collective-permute-done((bf16[256,256]{1,0:T(8,128)(2,1)S(1)}, bf16[256,256]{1,0:T(8,128)(2,1)S(1)}, u32[]{:S(2)}, u32[]{:S(2)}) %collective-permute-start.17) | collective-permute-done | bytes 131104 | tf_op jit(solution)/shard_map/ppermute | solution.py:231
  60.3 1.1 bitcast_dynamic-update-slice_fusion.3
  61.4 2.3 %bitcast_dynamic-update-slice_fusion.2 = bf16[5,256,2048]{2,1,0:T(8,128)(2,1)} fusion(bf16[5,256,2048]{2,1,0:T(8,128)(2,1)} %bitcast_dynamic-update-slice_fusion.3, s32[]{:T(128)S(6)} %select_n.133, bf16[256,2048]{1,0:T(8,128)(2,1)} %collective-permute-done.1), kind=kLoop, calls=%fused_computation.31 | loop fusion | bytes 2097156 | tf_op jit(solution)/shard_map/dynamic_update_slice | solution.py:194
  63.8 15.9 %collective-permute-done.3 = bf16[256,2048]{1,0:T(8,128)(2,1)} collective-permute-done((bf16[256,2048]{1,0:T(8,128)(2,1)}, bf16[256,2048]{1,0:T(8,128)(2,1)}, u32[]{:S(2)}, u32[]{:S(2)}) %collective-permute-start.3) | collective-permute-done | bytes 1048608 | tf_op jit(solution)/shard_map/ppermute | solution.py:205
  79.6 3.0 %bitcast_dynamic-update-slice_fusion.1 = (bf16[5,256,2048]{2,1,0:T(8,128)(2,1)}, bf16[256,2048]{1,0:T(8,128)(2,1)}) fusion(bf16[5,256,2048]{2,1,0:T(8,128)(2,1)} %bitcast_dynamic-update-slice_fusion.2, s32[]{:T(128)S(6)} %select_n.138, bf16[256,2048]{1,0:T(8,128)(2,1)} %collective-permute-done.2, bf16[256,2048]{1,0:T(8,128)(2,1)} %collective-permute-done.3, ...), kind=kLoop, calls=%fused_computation.30 | loop fusion | flops 524288 | bytes 4194309 | tf_op jit(solution)/shard_map/dynamic_update_slice | solution.py:194
  82.7 1.3 collective-permute-start.4
  84.0 1.2 copy.20
  85.4 1.2 copy.42
  86.9 1.9 %fusion.22 = f32[256,256]{1,0:T(8,128)S(1)} fusion(bf16[256,2048]{1,0:T(8,128)(2,1)S(1)} %copy-done.6, bf16[8192,256]{1,0:T(8,128)(2,1)} %cached.1, s32[]{:T(128)S(6)} %select_n.142), kind=kOutput, calls=%fused_computation.39 | convolution fusion | flops 268435456 | bytes 2359300 | tf_op jit(solution)/shard_map/dot_general | solution.py:190
  88.8 2.0 %convolution_add_fusion.2 = f32[256,256]{1,0:T(8,128)S(1)} fusion(f32[256,256]{1,0:T(8,128)S(1)} %fusion.22, bf16[256,2048]{1,0:T(8,128)(2,1)} %copy-done.7, bf16[8192,256]{1,0:T(8,128)(2,1)} %cached.1, s32[]{:T(128)S(6)} %select_n.143), kind=kOutput, calls=%fused_computation.18 | convolution fusion | flops 268500992 | bytes 2621444 | tf_op jit(solution)/shard_map/dot_general | solution.py:190
  90.8 1.7 %fusion.9 = f32[256,256]{0,1:T(8,128)S(1)} fusion(f32[256,256]{1,0:T(8,128)S(1)} %convolution_add_fusion.2, bf16[256,2048]{1,0:T(8,128)(2,1)} %collective-permute-done.1, bf16[8192,256]{1,0:T(8,128)(2,1)S(1)} %copy-done.1, s32[]{:T(128)S(6)} %select_n.144), kind=kOutput, calls=%fused_computation.17 | convolution fusion | flops 268500992 | bytes 2621444 | tf_op jit(solution)/shard_map/dot_general | solution.py:190
  92.6 17.8 %collective-permute-done.4 = bf16[256,2048]{1,0:T(8,128)(2,1)S(1)} collective-permute-done((bf16[256,2048]{1,0:T(8,128)(2,1)}, bf16[256,2048]{1,0:T(8,128)(2,1)S(1)}, u32[]{:S(2)}, u32[]{:S(2)}) %collective-permute-start.4) | collective-permute-done | bytes 1048608 | tf_op jit(solution)/shard_map/ppermute | solution.py:207
  111.0 1.8 %fusion.10 = bf16[256,256]{0,1:T(8,128)(2,1)S(1)} fusion(f32[256,256]{0,1:T(8,128)S(1)} %fusion.17, f32[256,256]{0,1:T(8,128)S(1)} %fusion.9, bf16[256,2048]{1,0:T(8,128)(2,1)} %get-tuple-element.39, bf16[8192,256]{1,0:T(8,128)(2,1)S(1)} %copy-done.1, s32[]{:T(128)S(6)} %select_n.145), kind=kOutput, calls=%fused_computation.19 | convolution fusion | flops 268632064 | bytes 2752516 | tf_op jit(solution)/shard_map/dot_general | solution.py:190
  116.1 1.1 bitcast_dynamic-update-slice_fusion.chunk_a.chunk_b
  117.1 3.6 %weight_send_other.1 = (bf16[2,1024,128]{2,1,0:T(8,128)(2,1)}, bf16[2,1024,128]{2,1,0:T(8,128)(2,1)}) custom-call(s32[5]{0:T(128)S(1)} %stack.77.place, bf16[5,256,2048]{2,1,0:T(8,128)(2,1)} %bitcast_dynamic-update-slice_fusion.chunk_a.chunk_b, bf16[5,256,2048]{2,1,0:T(8,128)(2,1)} %bitcast_dynamic-update-slice_fusion.chunk_a.chunk_b, ...), custom_call_target="tpu_custom_call" | custom-call | flops 268435456 | bytes 2097152 | tf_op jit(solution)/shard_map/weight_send_other/pallas_call | solution.py:122
  121.4 3.4 %weight_keep_other.1 = (bf16[2,1024,128]{2,1,0:T(8,128)(2,1)}, bf16[2,1024,128]{2,1,0:T(8,128)(2,1)S(1)}) custom-call(s32[5]{0:T(128)S(1)} %stack.71.place, bf16[5,256,2048]{2,1,0:T(8,128)(2,1)} %bitcast_dynamic-update-slice_fusion.chunk_a.chunk_b, bf16[5,256,2048]{2,1,0:T(8,128)(2,1)} %bitcast_dynamic-update-slice_fusion.chunk_a.chunk_b, ...), custom_call_target="tpu_custom_call" | custom-call | flops 268435456 | bytes 2097152 | tf_op jit(solution)/shard_map/weight_keep_other/pallas_call | solution.py:122
  125.4 3.6 %weight_send.1 = (bf16[2,1024,128]{2,1,0:T(8,128)(2,1)}, bf16[2,1024,128]{2,1,0:T(8,128)(2,1)}) custom-call(s32[5]{0:T(128)S(1)} %stack.76.place, bf16[5,256,2048]{2,1,0:T(8,128)(2,1)} %bitcast_dynamic-update-slice_fusion.chunk_a.chunk_b, bf16[5,256,2048]{2,1,0:T(8,128)(2,1)} %bitcast_dynamic-update-slice_fusion.chunk_a.chunk_b, ...), custom_call_target="tpu_custom_call" | custom-call | flops 268435456 | bytes 2097152 | tf_op jit(solution)/shard_map/weight_send/pallas_call | solution.py:122
  129.0 1.5 collective-permute-start.9
  130.5 1.5 collective-permute-start.11
  133.1 3.1 %collective-permute-start.15 = (bf16[256,256]{1,0:T(8,128)(2,1)S(1)}, bf16[256,256]{1,0:T(8,128)(2,1)}, u32[]{:S(2)}, u32[]{:S(2)}) collective-permute-start(bf16[256,256]{1,0:T(8,128)(2,1)S(1)} %copy.38.d_projected), channel_id=1, source_target_pairs={{0,3},{1,0},{2,1},{3,2},{4,7},{5,4},{6,5},{7,6},{8,11},{9,8},{10,9... | collective-permute-start | bytes 393224 | tf_op jit(solution)/shard_map/ppermute | solution.py:250
  136.2 2.8 %weight_keep.1 = (f32[2,1024,128]{2,1,0:T(8,128)S(1)}, f32[2,1024,128]{2,1,0:T(8,128)S(1)}) custom-call(s32[5]{0:T(128)S(1)} %stack.66.place, bf16[5,256,2048]{2,1,0:T(8,128)(2,1)} %bitcast_dynamic-update-slice_fusion.chunk_a.chunk_b, bf16[5,256,2048]{2,1,0:T(8,128)(2,1)} %bitcast_dynamic-update-slice_fusion.chunk_a.chunk_b, ...), custom_call_target="tpu_custom_call" | custom-call | flops 268435456 | bytes 2097152 | tf_op jit(solution)/shard_map/weight_keep/pallas_call | solution.py:122
  139.1 4.1 %collective-permute-done.9 = bf16[2,1024,128]{2,1,0:T(8,128)(2,1)} collective-permute-done((bf16[2,1024,128]{2,1,0:T(8,128)(2,1)}, bf16[2,1024,128]{2,1,0:T(8,128)(2,1)}, u32[]{:S(2)}, u32[]{:S(2)}) %collective-permute-start.9) | collective-permute-done | bytes 524320 | tf_op jit(solution)/shard_map/ppermute | solution.py:149
  143.2 1.7 fusion.32
  144.9 1.5 collective-permute-start.10
  146.5 1.7 fusion.33
  148.2 1.5 collective-permute-start.12
  151.0 1.6 collective-permute-done.10
  153.6 1.9 %collective-permute-done.12 = bf16[1024,128]{1,0:T(8,128)(2,1)S(1)} collective-permute-done((bf16[1024,128]{1,0:T(8,128)(2,1)}, bf16[1024,128]{1,0:T(8,128)(2,1)S(1)}, u32[]{:S(2)}, u32[]{:S(2)}) %collective-permute-start.12) | collective-permute-done | bytes 262176 | tf_op jit(solution)/shard_map/ppermute | solution.py:149
  156.6 1.0 pad_maximum_fusion
  157.7 4.7 %convolution_convert_fusion = bf16[256,2048]{1,0:T(8,128)(2,1)} fusion(bf16[2048,1024]{1,0:T(8,128)(2,1)} %all-gather.5.cloned.1.call-done, bf16[256,256]{1,0:T(8,128)(2,1)} %collective-permute-done.15, bf16[256,256]{1,0:T(8,128)(2,1)} %collective-permute-done.14, bf16[256,256]{1,0:T(8,128)(2,1)S(1)} %collective-permute-done.13, ...), kind=kOutput, calls=%fused_computation | convolution fusion | flops 1076363264 | bytes 5767168 | tf_op jit(solution)/shard_map/dot_general | solution.py:252
  162.4 2.0 %copy.50 = bf16[8192,256]{1,0:T(8,128)(2,1)} copy(bf16[8192,256]{1,0:T(8,128)(2,1)S(1)} %copy-done.8) | data formatting | bytes 8388608
  (68 shorter events, 11.3 us)
Async XLA Ops:
  7.2 150.5 %all-gather.3.cloned.1.call-start = ((), (), s32[]{:S(2)}) async-start(), calls=%async_computation | async-start | bytes 4718592 | tf_op jit(solution)/shard_map/all_gather | solution.py:222
  7.2 2.2 %copy-start = (bf16[8192,256]{1,0:T(8,128)(2,1)S(1)}, bf16[8192,256]{1,0:T(8,128)(2,1)}, u32[]{:S(2)}) copy-start(bf16[8192,256]{1,0:T(8,128)(2,1)} %cached.1) | copy-start | bytes 12582916
  9.4 1.2 copy-start.2
  10.6 1.2 copy-start.3
  11.9 1.2 copy-start.4
  13.1 1.2 copy-start.5
  14.3 2.7 %copy-start.6 = (bf16[256,2048]{1,0:T(8,128)(2,1)S(1)}, bf16[256,2048]{1,0:T(8,128)(2,1)}, u32[]{:S(2)}) copy-start(bf16[256,2048]{1,0:T(8,128)(2,1)} %param.9) | copy-start | bytes 3145732
  17.0 140.7 %all-gather.5.cloned.1.call-start = ((), (), s32[]{:S(2)}) async-start(), calls=%async_computation.1 | async-start | bytes 4718592 | tf_op jit(solution)/shard_map/all_gather | solution.py:232
  17.1 28.5 %collective-permute-start = (bf16[256,2048]{1,0:T(8,128)(2,1)S(1)}, bf16[256,2048]{1,0:T(8,128)(2,1)S(1)}, u32[]{:S(2)}, u32[]{:S(2)}) collective-permute-start(bf16[256,2048]{1,0:T(8,128)(2,1)S(1)} %copy-done.6), channel_id=1, source_target_pairs={{0,1},{1,2},{2,3},{4,5},{5,6},{6,7},{8,9},{9,10},{10,11},{12,13},{... | collective-permute-start | bytes 3145736 | tf_op jit(solution)/shard_map/ppermute | solution.py:204
  22.1 31.4 %collective-permute-start.1 = (bf16[256,2048]{1,0:T(8,128)(2,1)S(1)}, bf16[256,2048]{1,0:T(8,128)(2,1)}, u32[]{:S(2)}, u32[]{:S(2)}) collective-permute-start(bf16[256,2048]{1,0:T(8,128)(2,1)S(1)} %copy-done.6), channel_id=1, source_target_pairs={{1,0},{2,1},{3,2},{5,4},{6,5},{7,6},{9,8},{10,9},{11,10},{13,12},{... | collective-permute-start | bytes 3145736 | tf_op jit(solution)/shard_map/ppermute | solution.py:205
  24.6 30.3 %collective-permute-start.16 = (bf16[256,256]{1,0:T(8,128)(2,1)S(1)}, bf16[256,256]{1,0:T(8,128)(2,1)S(1)}, u32[]{:S(2)}, u32[]{:S(2)}) collective-permute-start(bf16[256,256]{1,0:T(8,128)(2,1)S(1)} %get-tuple-element.41), channel_id=1, source_target_pairs={{0,1},{1,2},{2,3},{3,0},{4,5},{5,6},{6,7},{7,4},{8,9},{9,10},{10,1... | collective-permute-start | bytes 393224 | tf_op jit(solution)/shard_map/ppermute | solution.py:231
  27.3 32.2 %collective-permute-start.17 = (bf16[256,256]{1,0:T(8,128)(2,1)S(1)}, bf16[256,256]{1,0:T(8,128)(2,1)S(1)}, u32[]{:S(2)}, u32[]{:S(2)}) collective-permute-start(bf16[256,256]{1,0:T(8,128)(2,1)S(1)} %get-tuple-element.43), channel_id=1, source_target_pairs={{0,2},{1,3},{2,0},{3,1},{4,6},{5,7},{6,4},{7,5},{8,10},{9,11},{10,... | collective-permute-start | bytes 393224 | tf_op jit(solution)/shard_map/ppermute | solution.py:231
  30.8 28.7 %collective-permute-start.18 = (bf16[256,256]{1,0:T(8,128)(2,1)S(1)}, bf16[256,256]{1,0:T(8,128)(2,1)S(1)}, u32[]{:S(2)}, u32[]{:S(2)}) collective-permute-start(bf16[256,256]{1,0:T(8,128)(2,1)S(1)} %get-tuple-element.42), channel_id=1, source_target_pairs={{0,3},{1,0},{2,1},{3,2},{4,7},{5,4},{6,5},{7,6},{8,11},{9,8},{10,9... | collective-permute-start | bytes 393224 | tf_op jit(solution)/shard_map/ppermute | solution.py:231
  45.6 37.1 %copy-start.7 = (bf16[256,2048]{1,0:T(8,128)(2,1)}, bf16[256,2048]{1,0:T(8,128)(2,1)S(1)}, u32[]{:S(2)}) copy-start(bf16[256,2048]{1,0:T(8,128)(2,1)S(1)} %collective-permute-done) | copy-start | bytes 3145732
  45.6 18.2 %collective-permute-start.2 = (bf16[256,2048]{1,0:T(8,128)(2,1)S(1)}, bf16[256,2048]{1,0:T(8,128)(2,1)}, u32[]{:S(2)}, u32[]{:S(2)}) collective-permute-start(bf16[256,2048]{1,0:T(8,128)(2,1)S(1)} %collective-permute-done), channel_id=1, source_target_pairs={{1,2},{2,3},{5,6},{6,7},{9,10},{10,11},{13,14},{14,15},{17,18},{18... | collective-permute-start | bytes 3145736 | tf_op jit(solution)/shard_map/ppermute | solution.py:204
  53.5 26.1 %collective-permute-start.3 = (bf16[256,2048]{1,0:T(8,128)(2,1)}, bf16[256,2048]{1,0:T(8,128)(2,1)}, u32[]{:S(2)}, u32[]{:S(2)}) collective-permute-start(bf16[256,2048]{1,0:T(8,128)(2,1)} %collective-permute-done.1), channel_id=1, source_target_pairs={{1,0},{2,1},{5,4},{6,5},{9,8},{10,9},{13,12},{14,13},{17,16},{18,1... | collective-permute-start | bytes 3145736 | tf_op jit(solution)/shard_map/ppermute | solution.py:205
  60.3 23.7 %copy-start.12 = (bf16[256,1024]{1,0:T(8,128)(2,1)S(1)}, bf16[256,1024]{1,0:T(8,128)(2,1)}, u32[]{:S(2)}) copy-start(bf16[256,1024]{1,0:T(8,128)(2,1)} %param.11) | copy-start | bytes 1572868
  63.7 23.0 %copy-start.13 = (s32[1,256]{1,0:T(1,128)S(1)}, s32[1,256]{1,0:T(1,128)}, u32[]{:S(2)}) copy-start(s32[1,256]{1,0:T(1,128)} %param.12) | copy-start | bytes 3076
  82.7 27.7 %collective-permute-start.4 = (bf16[256,2048]{1,0:T(8,128)(2,1)}, bf16[256,2048]{1,0:T(8,128)(2,1)S(1)}, u32[]{:S(2)}, u32[]{:S(2)}) collective-permute-start(bf16[256,2048]{1,0:T(8,128)(2,1)} %get-tuple-element.39), channel_id=1, source_target_pairs={{2,3},{1,0},{6,7},{5,4},{10,11},{9,8},{14,15},{13,12},{18,19},{17,... | collective-permute-start | bytes 3145736 | tf_op jit(solution)/shard_map/ppermute | solution.py:207
  86.8 4.1 %copy-start.1 = (bf16[8192,256]{1,0:T(8,128)(2,1)S(1)}, bf16[8192,256]{1,0:T(8,128)(2,1)}, u32[]{:S(2)}) copy-start(bf16[8192,256]{1,0:T(8,128)(2,1)} %cached.1) | copy-start | bytes 12582916
  112.7 1.7 copy-start.9
  115.5 5.3 %copy-start.10 = (bf16[8,256,256]{1,2,0:T(8,128)(2,1)}, bf16[8,256,256]{1,2,0:T(8,128)(2,1)S(1)}, u32[]{:S(2)}) copy-start(bf16[8,256,256]{1,2,0:T(8,128)(2,1)S(1)} %fusion.5) | copy-start | bytes 3145732
  120.7 4.6 %collective-permute-start.7 = (bf16[2,1024,128]{2,1,0:T(8,128)(2,1)}, bf16[2,1024,128]{2,1,0:T(8,128)(2,1)S(1)}, u32[]{:S(2)}, u32[]{:S(2)}) collective-permute-start(bf16[2,1024,128]{2,1,0:T(8,128)(2,1)} %get-tuple-element.26), channel_id=1, source_target_pairs={{0,4},{4,0},{8,12},{12,8},{16,20},{20,16},{24,28},{28,24},{1,5},{5... | collective-permute-start | bytes 1572872 | tf_op jit(solution)/shard_map/ppermute | solution.py:149
  120.8 4.6 %collective-permute-start.8 = (bf16[2,1024,128]{2,1,0:T(8,128)(2,1)}, bf16[2,1024,128]{2,1,0:T(8,128)(2,1)S(1)}, u32[]{:S(2)}, u32[]{:S(2)}) collective-permute-start(bf16[2,1024,128]{2,1,0:T(8,128)(2,1)} %get-tuple-element.27), channel_id=1, source_target_pairs={{0,4},{4,0},{8,12},{12,8},{16,20},{20,16},{24,28},{28,24},{1,5},{5... | collective-permute-start | bytes 1572872 | tf_op jit(solution)/shard_map/ppermute | solution.py:149
  124.9 7.3 %collective-permute-start.5 = (bf16[2,1024,128]{2,1,0:T(8,128)(2,1)}, bf16[2,1024,128]{2,1,0:T(8,128)(2,1)S(1)}, u32[]{:S(2)}, u32[]{:S(2)}) collective-permute-start(bf16[2,1024,128]{2,1,0:T(8,128)(2,1)} %get-tuple-element.23), channel_id=1, source_target_pairs={{0,4},{4,0},{8,12},{12,8},{16,20},{20,16},{24,28},{28,24},{1,5},{5... | collective-permute-start | bytes 1572872 | tf_op jit(solution)/shard_map/ppermute | solution.py:149
  125.0 8.2 %collective-permute-start.6 = (bf16[2,1024,128]{2,1,0:T(8,128)(2,1)S(1)}, bf16[2,1024,128]{2,1,0:T(8,128)(2,1)S(1)}, u32[]{:S(2)}, u32[]{:S(2)}) collective-permute-start(bf16[2,1024,128]{2,1,0:T(8,128)(2,1)S(1)} %get-tuple-element.24), channel_id=1, source_target_pairs={{0,4},{4,0},{8,12},{12,8},{16,20},{20,16},{24,28},{28,24},{1,5},{5... | collective-permute-start | bytes 1572872 | tf_op jit(solution)/shard_map/ppermute | solution.py:149
  129.0 14.2 %collective-permute-start.9 = (bf16[2,1024,128]{2,1,0:T(8,128)(2,1)}, bf16[2,1024,128]{2,1,0:T(8,128)(2,1)}, u32[]{:S(2)}, u32[]{:S(2)}) collective-permute-start(bf16[2,1024,128]{2,1,0:T(8,128)(2,1)} %get-tuple-element.28), channel_id=1, source_target_pairs={{0,8},{4,12},{8,0},{12,4},{16,24},{20,28},{24,16},{28,20},{1,9},{5... | collective-permute-start | bytes 1572872 | tf_op jit(solution)/shard_map/ppermute | solution.py:149
  130.5 16.0 %collective-permute-start.11 = (bf16[2,1024,128]{2,1,0:T(8,128)(2,1)}, bf16[2,1024,128]{2,1,0:T(8,128)(2,1)}, u32[]{:S(2)}, u32[]{:S(2)}) collective-permute-start(bf16[2,1024,128]{2,1,0:T(8,128)(2,1)} %get-tuple-element.30), channel_id=1, source_target_pairs={{0,16},{4,20},{8,24},{12,28},{16,0},{20,4},{24,8},{28,12},{1,17},{... | collective-permute-start | bytes 1572872 | tf_op jit(solution)/shard_map/ppermute | solution.py:149
  132.1 17.6 %copy-start.11 = (bf16[8,256,256]{1,2,0:T(8,128)(2,1)S(1)}, bf16[8,256,256]{1,2,0:T(8,128)(2,1)}, u32[]{:S(2)}) copy-start(bf16[8,256,256]{1,2,0:T(8,128)(2,1)} %copy-done.10) | copy-start | bytes 3145732
  132.1 25.5 %collective-permute-start.13 = (bf16[256,256]{1,0:T(8,128)(2,1)S(1)}, bf16[256,256]{1,0:T(8,128)(2,1)S(1)}, u32[]{:S(2)}, u32[]{:S(2)}) collective-permute-start(bf16[256,256]{1,0:T(8,128)(2,1)S(1)} %copy.38.d_projected), channel_id=1, source_target_pairs={{0,1},{1,2},{2,3},{3,0},{4,5},{5,6},{6,7},{7,4},{8,9},{9,10},{10,1... | collective-permute-start | bytes 393224 | tf_op jit(solution)/shard_map/ppermute | solution.py:250
  132.2 25.4 %collective-permute-start.14 = (bf16[256,256]{1,0:T(8,128)(2,1)S(1)}, bf16[256,256]{1,0:T(8,128)(2,1)}, u32[]{:S(2)}, u32[]{:S(2)}) collective-permute-start(bf16[256,256]{1,0:T(8,128)(2,1)S(1)} %copy.38.d_projected), channel_id=1, source_target_pairs={{0,2},{1,3},{2,0},{3,1},{4,6},{5,7},{6,4},{7,5},{8,10},{9,11},{10,... | collective-permute-start | bytes 393224 | tf_op jit(solution)/shard_map/ppermute | solution.py:250
  133.1 24.5 %collective-permute-start.15 = (bf16[256,256]{1,0:T(8,128)(2,1)S(1)}, bf16[256,256]{1,0:T(8,128)(2,1)}, u32[]{:S(2)}, u32[]{:S(2)}) collective-permute-start(bf16[256,256]{1,0:T(8,128)(2,1)S(1)} %copy.38.d_projected), channel_id=1, source_target_pairs={{0,3},{1,0},{2,1},{3,2},{4,7},{5,4},{6,5},{7,6},{8,11},{9,8},{10,9... | collective-permute-start | bytes 393224 | tf_op jit(solution)/shard_map/ppermute | solution.py:250
  144.9 7.7 %collective-permute-start.10 = (bf16[1024,128]{1,0:T(8,128)(2,1)}, bf16[1024,128]{1,0:T(8,128)(2,1)S(1)}, u32[]{:S(2)}, u32[]{:S(2)}) collective-permute-start(bf16[1024,128]{1,0:T(8,128)(2,1)} %fusion.32), channel_id=1, source_target_pairs={{0,16},{4,20},{8,24},{12,28},{16,0},{20,4},{24,8},{28,12},{1,17},{... | collective-permute-start | bytes 786440 | tf_op jit(solution)/shard_map/ppermute | solution.py:149
  148.2 7.4 %collective-permute-start.12 = (bf16[1024,128]{1,0:T(8,128)(2,1)}, bf16[1024,128]{1,0:T(8,128)(2,1)S(1)}, u32[]{:S(2)}, u32[]{:S(2)}) collective-permute-start(bf16[1024,128]{1,0:T(8,128)(2,1)} %fusion.33), channel_id=1, source_target_pairs={{0,8},{4,12},{8,0},{12,4},{16,24},{20,28},{24,16},{28,20},{1,9},{5... | collective-permute-start | bytes 786440 | tf_op jit(solution)/shard_map/ppermute | solution.py:149
  157.7 4.7 %copy-start.8 = (bf16[8192,256]{1,0:T(8,128)(2,1)S(1)}, bf16[8192,256]{1,0:T(8,128)(2,1)}, u32[]{:S(2)}) copy-start(bf16[8192,256]{1,0:T(8,128)(2,1)} %all-gather.3.cloned.1.call-done) | copy-start | bytes 12582916
Sparse Core Ops, SparseCore 0:
  17.1 39.4 all-gather.2
  60.4 37.7 all-gather.4

commit v3 on v2

v3 whole, which is shorter than its diff:
```python
import functools
import math

import jax
import jax.numpy as jnp
from jax import lax
from jax.experimental import pallas as pl
from jax.experimental.pallas import tpu as pltpu
from jax.sharding import PartitionSpec as P

HD = 128
VMEM_STREAM = 56 * 1024 * 1024
VMEM_WHOLE = 24 * 1024 * 1024


beta_first = 0.9
beta_second = 0.95
learn_rate = 0.0003
weight_decay = 0.1
adam_epsilon = 1e-08
first_fix = 1.0 - 0.9**40
second_fix = 1.0 - 0.95**40


def optimizer_kernel(
    place, cached, master, moment, second, grad, master_out, moment_out, second_out, cache_out
):
    moment_new = beta_first * moment[...] + (1.0 - beta_first) * grad[...]
    second_new = beta_second * second[...] + (1.0 - beta_second) * grad[...] * grad[...]
    update = moment_new / first_fix / (jnp.sqrt(second_new / second_fix) + adam_epsilon)
    master_new = master[...] - learn_rate * (update + weight_decay * master[...])
    moment_out[...] = moment_new
    second_out[...] = second_new
    master_out[...] = master_new
    for start in range(0, cached.shape[1], HD):
        block = slice(start, start + HD)
        own_cache = cached[:, block].astype(jnp.float32)
        delta = master_new[:, block] - own_cache
        largest = jnp.max(jnp.abs(delta), axis=1, keepdims=True)
        scale = (largest + 1e-06).astype(jnp.bfloat16).astype(jnp.float32)
        codes = (delta / scale).astype(jnp.bfloat16)
        cache_out[:, block] = (own_cache + codes.astype(jnp.float32) * scale).astype(jnp.bfloat16)


def optimizer(cached, master, moment, second, grad):
    rows, cols = master.shape
    step = min(rows, 256)
    steps = rows // step
    own = pl.BlockSpec((step, cols), lambda i, place: (i, 0))
    full = jax.ShapeDtypeStruct((rows, cols), jnp.float32)
    return pl.pallas_call(
        optimizer_kernel,
        grid_spec=pltpu.PrefetchScalarGridSpec(
            num_scalar_prefetch=1,
            grid=(steps,),
            in_specs=[pl.BlockSpec((step, cols), lambda i, place: (place[0] * steps + i, 0))]
            + [own] * 4,
            out_specs=[own] * 4,
        ),
        out_shape=[full, full, full, jax.ShapeDtypeStruct((rows, cols), jnp.bfloat16)],
        cost_estimate=pl.CostEstimate(
            flops=40 * rows * cols, bytes_accessed=32 * rows * cols, transcendentals=rows * cols
        ),
        compiler_params=pltpu.CompilerParams(vmem_limit_bytes=VMEM_STREAM),
        name="optimizer",
    )(lax.axis_index("dp").astype(jnp.int32).reshape(1), cached, master, moment, second, grad)


def attention_backward(projected, queries, d_out, doc_ids):
    length = projected.shape[0]
    heads = projected.reshape(length, -1, 2, HD)
    keys = heads[:, :, 0]
    values = heads[:, :, 1]
    query_heads = queries.reshape(length, keys.shape[1], -1, HD)
    grads_out = d_out.reshape(length, keys.shape[1], -1, HD)
    factor = 1.0 / math.sqrt(HD)
    scores = (
        jnp.einsum("qhgd,khd->hgqk", query_heads, keys, preferred_element_type=jnp.float32) * factor
    )
    position = jnp.arange(length)
    allowed = (doc_ids[:, None] == doc_ids[None, :]) & (position[None, :] <= position[:, None])
    scores = jnp.where(allowed, scores, -1e30)
    highest = jnp.max(scores, axis=-1, keepdims=True)
    weights = jnp.exp(scores - highest)
    probs = weights / jnp.sum(weights, axis=-1, keepdims=True)
    probs_low = probs.astype(jnp.bfloat16)
    attended = jnp.einsum("hgqk,khd->qhgd", probs_low, values, preferred_element_type=jnp.float32)
    rowdot = jnp.sum(grads_out.astype(jnp.float32) * attended, axis=-1)
    d_probs = jnp.einsum("qhgd,khd->hgqk", grads_out, values, preferred_element_type=jnp.float32)
    d_scores = (probs * (d_probs - jnp.transpose(rowdot, (1, 2, 0))[..., None]) * factor).astype(
        jnp.bfloat16
    )
    d_queries = (
        jnp.einsum("hgqk,khd->qhgd", d_scores, keys, preferred_element_type=jnp.float32)
        .astype(jnp.bfloat16)
        .reshape(length, -1)
    )
    d_keys = jnp.einsum("hgqk,qhgd->khd", d_scores, query_heads, preferred_element_type=jnp.float32)
    d_values = jnp.einsum(
        "hgqk,qhgd->khd", probs_low, grads_out, preferred_element_type=jnp.float32
    )
    d_projected = jnp.stack([d_keys, d_values], axis=2).astype(jnp.bfloat16).reshape(length, -1)
    return d_queries, d_projected


def on_chip(kernel, place, arrays, out_shape, flops, name):
    vmem = pl.BlockSpec(memory_space=pltpu.VMEM)
    size = sum(a.size * a.dtype.itemsize for a in arrays)
    size += sum(s.size * s.dtype.itemsize for s in out_shape)
    return pl.pallas_call(
        kernel,
        in_specs=[pl.BlockSpec(memory_space=pltpu.SMEM)] + [vmem] * len(arrays),
        out_specs=[vmem] * len(out_shape),
        out_shape=out_shape,
        cost_estimate=pl.CostEstimate(flops=flops, bytes_accessed=size, transcendentals=0),
        compiler_params=pltpu.CompilerParams(vmem_limit_bytes=VMEM_WHOLE),
        name=name,
    )(place, *arrays)


def split_kernel(place, whole, *pieces):
    rows = pieces[0].shape[0]
    for p, piece in enumerate(pieces):
        piece[...] = whole[p * rows : (p + 1) * rows, :]


def weight_kernel(n_slots, n_pieces, n_chunks, keep, place, *refs):
    n = n_slots * n_pieces
    d_projected, added, outs = refs[n], refs[n + 1 : -2], refs[-2:]
    _, half, rows = outs[0].shape
    start = pl.multiple_of(place[0] * rows, rows)
    for j in range(n_slots):
        chunk = place[3 + j]
        bits = (chunk & 1, (chunk >> 1) & 1)
        inside = (chunk >= 0) & (chunk < n_chunks)
        for side in range(2):
            same = bits[side] == place[1 + side]
            wanted = inside & (same if keep else jnp.logical_not(same))
            position = bits[1 - side]

            @pl.when(wanted)
            def _():
                total = jnp.zeros((half, rows), jnp.float32)
                for p in range(n_pieces):
                    piece = refs[j * n_pieces + p]
                    height = piece.shape[0]
                    columns = d_projected[
                        p * height : (p + 1) * height, side * half : (side + 1) * half
                    ]
                    total = total + lax.dot_general(
                        columns,
                        piece[:, pl.ds(start, rows)],
                        (((0,), (0,)), ((), ())),
                        preferred_element_type=jnp.float32,
                    )
                if added:
                    total = total + added[side][position].astype(jnp.float32)
                outs[side][position] = total.astype(outs[side].dtype)


def combine_kernel(place, keep_a, got_a, keep_b, got_b, out_a, out_b):
    sides = ((keep_a, got_a, out_a), (keep_b, got_b, out_b))
    for side, (keep, got, out) in enumerate(sides):
        which = place[side]
        out[...] = (keep[which] + got[which].astype(jnp.float32)).astype(out.dtype)


def finish_kernel(place, keep_a, got_a, keep_b, got_b, last_a, last_b, out):
    half = last_a.shape[0]
    sides = ((keep_a, got_a, last_a), (keep_b, got_b, last_b))
    for side, (keep, got, last) in enumerate(sides):
        which = place[side]
        total = keep[which] + got[which].astype(jnp.float32) + last[...].astype(jnp.float32)
        out[:, side * half : (side + 1) * half] = total.T


def weight_sum(slots, d_projected, n_chunks):
    index = lax.axis_index("dp").astype(jnp.int32)
    core, x, y = index % 2, (index // 2) % 2, index // 4
    pieces = [piece for _, held in slots for piece in held]
    n_pieces = len(slots[0][1])
    length, cols = d_projected.shape
    half, rows = cols // 2, pieces[0].shape[1] // 2

    def swap(value, bit):
        return lax.ppermute(value, "dp", [(i, i ^ bit) for i in range(8)])

    def parts(which, keep, added, dtype, name):
        place = jnp.stack([which, x, y] + [chunk for chunk, _ in slots])
        kernel = functools.partial(weight_kernel, len(slots), n_pieces, n_chunks, keep)
        shape = jax.ShapeDtypeStruct((2, half, rows), dtype)
        arrays = pieces + [d_projected] + added
        return on_chip(kernel, place, arrays, [shape, shape], 4 * length * rows * cols, name)

    theirs = parts(1 - core, False, [], jnp.bfloat16, "weight_send_other")
    theirs = [swap(part, 1) for part in theirs]
    rest = parts(1 - core, True, [], jnp.bfloat16, "weight_keep_other")
    rest = [swap(part, 1) for part in rest]
    send_a, send_b = parts(core, False, theirs, jnp.bfloat16, "weight_send")
    got_a, got_b = swap(send_a, 2), swap(send_b, 4)
    keep_a, keep_b = parts(core, True, rest, jnp.float32, "weight_keep")

    small = jax.ShapeDtypeStruct((half, rows), jnp.bfloat16)
    arrays = [keep_a, got_a, keep_b, got_b]
    last_a, last_b = on_chip(
        combine_kernel, jnp.stack([1 - y, 1 - x]), arrays, [small] * 2, cols * rows, "weight_combine"
    )
    last = [swap(last_a, 4), swap(last_b, 2)]

    def finish(ready):
        ended, ready = lax.optimization_barrier((last, ready))
        (total,) = on_chip(
            finish_kernel,
            jnp.stack([y, x]),
            arrays + ended,
            [jax.ShapeDtypeStruct((rows, cols), jnp.float32)],
            2 * cols * rows,
            "weight_finish",
        )
        return total, ready

    return finish


def input_kernel(*refs):
    *pieces, feature_rows, out = refs
    cols = pieces[0].shape[1]
    total = jnp.zeros(out.shape, jnp.float32)
    for s, piece in enumerate(pieces):
        total = total + lax.dot_general(
            piece[...],
            feature_rows[:, s * cols : (s + 1) * cols],
            (((1,), (1,)), ((), ())),
            preferred_element_type=jnp.float32,
        )
    out[...] = total.astype(out.dtype)


def input_gradient(pieces, feature_rows):
    length, cols = pieces[0].shape
    feats, wide = feature_rows.shape
    step = min(feats, 512)
    return pl.pallas_call(
        input_kernel,
        grid=(feats // step,),
        in_specs=[pl.BlockSpec((length, cols), lambda i: (0, 0))] * len(pieces)
        + [pl.BlockSpec((step, wide), lambda i: (i, 0))],
        out_specs=pl.BlockSpec((length, step), lambda i: (0, i)),
        out_shape=jax.ShapeDtypeStruct((length, feats), jnp.bfloat16),
        cost_estimate=pl.CostEstimate(
            flops=2 * length * feats * wide,
            bytes_accessed=2 * feats * wide + 2 * length * (feats + wide),
            transcendentals=0,
        ),
        compiler_params=pltpu.CompilerParams(vmem_limit_bytes=VMEM_STREAM),
        name="input_gradient",
    )(*pieces, feature_rows)


def make_body(n_dp, n_z):
    ring = [[(z, (z + s) % n_z) for z in range(n_z)] for s in range(n_z)]
    n_pieces = 2

    def body(tokens, queries, d_out, segments, cached, master, moment, second, grad):
        me_dp = lax.axis_index("dp").astype(jnp.int32)
        me_z = lax.axis_index("tensor").astype(jnp.int32)
        length, feats = tokens.shape
        cols = cached.shape[1]
        height = length // n_pieces

        def part(piece, chunk):
            start = jnp.clip(chunk, 0, n_z - 1) * feats
            rows = lax.dynamic_slice_in_dim(cached, start, feats, 0)
            return jnp.dot(piece, rows, preferred_element_type=jnp.float32)

        shape = jax.ShapeDtypeStruct((height, feats), tokens.dtype)
        own = on_chip(
            split_kernel, jnp.zeros((1,), jnp.int32), [tokens], [shape] * n_pieces, 0, "split"
        )
        slots = [(me_z, own)]
        from_low, from_high, merged = own, own, None
        for s in range(1, n_z):
            up = [(z, z + 1) for z in range(s - 1, n_z - 1)]
            down = [(z + 1, z) for z in range(n_z - s)]
            low, high = me_z - s, me_z + s
            if merged is None:
                from_low = [lax.ppermute(piece, "tensor", up) for piece in from_low]
                from_high = [lax.ppermute(piece, "tensor", down) for piece in from_high]
            else:
                merged = [lax.ppermute(piece, "tensor", up + down) for piece in merged]
            if merged is None and 2 * s >= n_z:
                merged = [jnp.where(me_z >= s, a, b) for a, b in zip(from_low, from_high)]
            if merged is None:
                slots += [(low, from_low), (high, from_high)]
            else:
                slots.append((jnp.where(me_z >= s, low, high), merged))
        projected = []
        for p in range(n_pieces):
            total = jnp.zeros((height, cols), jnp.float32)
            for chunk, held in slots:
                total = total + part(held[p], chunk)
            projected.append(total.astype(jnp.bfloat16))
        projected = jnp.concatenate(projected, axis=0)

        later = cached
        if n_z > 1:
            later, master, _ = lax.optimization_barrier((cached, master, slots[1][1][0]))

        master_new, moment_new, second_new, own_new = optimizer(
            cached, master, moment, second, grad
        )
        new_cache = lax.all_gather(own_new, "dp", axis=0, tiled=True)

        share = feats // n_dp

        def block_for(z):
            return lax.dynamic_slice_in_dim(later, z * feats + me_dp * share, share, 0)

        blocks = [block_for(me_z)]
        for s in range(1, n_z):
            blocks.append(lax.ppermute(block_for((me_z + s) % n_z), "tensor", ring[s]))
        feature_rows = lax.all_gather(jnp.concatenate(blocks, axis=1), "dp", axis=0, tiled=True)

        d_queries, d_projected = attention_backward(projected, queries, d_out, segments[0])

        pieces = [d_projected] + [
            lax.ppermute(d_projected, "tensor", ring[s]) for s in range(1, n_z)
        ]
        if n_dp == 8 and n_z == 4:
            finish = weight_sum(slots, d_projected, n_z)
            new_grad, d_tokens = finish(input_gradient(pieces, feature_rows))
        else:
            d_tokens = input_gradient(pieces, feature_rows)
            partial = jnp.zeros((n_z + 1, feats, cols), jnp.bfloat16)
            for chunk, held in slots:
                product = lax.dot_general(
                    jnp.concatenate(held, axis=0),
                    d_projected,
                    (((0,), (0,)), ((), ())),
                    preferred_element_type=jnp.float32,
                )
                slot = jnp.where((chunk >= 0) & (chunk < n_z), chunk, n_z)
                partial = lax.dynamic_update_slice(
                    partial, product.astype(jnp.bfloat16)[None], (slot, 0, 0)
                )
            new_grad = lax.psum_scatter(
                partial[:n_z].reshape(n_z * feats, cols), "dp", scatter_dimension=0, tiled=True
            ).astype(jnp.float32)
        return (master_new, moment_new, second_new, new_cache, new_grad, d_queries, d_tokens)

    return body


def solution(mesh):
    in_specs = (
        P("dp", "tensor"),
        P("dp", "tensor"),
        P("dp", "tensor"),
        P("dp", None),
        P(None, "tensor"),
        P("dp", "tensor"),
        P("dp", "tensor"),
        P("dp", "tensor"),
        P("dp", "tensor"),
    )
    out_specs = (
        P("dp", "tensor"),
        P("dp", "tensor"),
        P("dp", "tensor"),
        P(None, "tensor"),
        P("dp", "tensor"),
        P("dp", "tensor"),
        P("dp", "tensor"),
    )
    body = make_body(mesh.shape["dp"], mesh.shape["tensor"])
    return jax.shard_map(body, mesh=mesh, in_specs=in_specs, out_specs=out_specs, check_vma=False)
```

time: 172 us -> 176 us (1.023)
  Pallas kernels: 16.2 us -> 27.7 us
  other arithmetic: 11.2 us -> 2.93 us
  starting transfers between devices: 28.3 us -> 36 us
  waiting for transfers between devices: 62.8 us -> 57.8 us
  matrix products: 15.5 us -> 13.2 us
    pallas_call x4 -> x8, Pallas kernels: 13.5 us -> 22.6 us  [the longest x7 17.5 us: on_chip(): pl.pallas_call(kernel, in_specs=[pl.BlockSpec(memory_space=pltpu.SMEM)] +...]
    ppermute x5 -> x10, starting transfers between devices: 10.5 us -> 19.4 us  [the longest x4 11.7 us: body(): from_low = [lax.ppermute(piece, 'tensor', up) for piece in from_low]]
    unnamed x30 -> x62, local copies, waits for them, and re-layouts: 10.1 us -> 15.8 us
    dynamic_update_slice x4 -> x0, local copies, waits for them, and re-layouts: 5.5 us -> none  [hold(): return lax.dynamic_update_slice(held, chunk[None], (slot, 0, 0))]
    ppermute x8, waiting for transfers between devices: 7.67 us -> 2.44 us  [swap(): return lax.ppermute(value, 'dp', [(i, i ^ bit) for i in range(8)])]
    ppermute x5 -> x10, waiting for transfers between devices: 50.4 us -> 54.6 us  [the longest x4 25.9 us: body(): from_high = [lax.ppermute(piece, 'tensor', down) for piece in from_high]]
    ppermute x3, waiting for transfers between devices: 4.66 us -> 0.7 us  [body(): blocks.append(lax.ppermute(block_for((me_z + s) % n_z), 'tensor', ring[s]))]
    convert_element_type x2 -> x0, other arithmetic: 3.41 us -> none  [the longest x1 1.71 us: weight_sum(): last_a = swap(pick(keep_a, got_a, 1 - y).astype(jnp.bfloat16), 4)]
  transfers between devices with their start and end apart: 21 -> 26, of which waited for: 9 -> 10; matrix products, arithmetic and copies ran while one was open for 21% -> 13% of each run, Pallas kernels for 8% -> 11%
where the time goes in v3:
time: 176 us; the launch traced here: 174 us
  waiting for transfers between devices  57.8 us (33%)
  starting transfers between devices  36 us (20%)
  Pallas kernels  27.7 us (16%)
  local copies, waits for them, and re-layouts  21.7 us (12%)
  between operations  14.7 us (8%)
  matrix products  13.2 us (8%)
  other arithmetic  2.93 us (2%)
    ppermute x4, waiting for transfers between devices, body(): from_high = [lax.ppermute(piece, 'tensor', down) for piece in from_high]  25.9 us
    ppermute x2, waiting for transfers between devices, body(): merged = [lax.ppermute(piece, 'tensor', up + down) for piece in merged]  17.6 us
    pallas_call x7, Pallas kernels, on_chip(): pl.pallas_call(kernel, in_specs=[pl.BlockSpec(memory_space=pltpu.SMEM)] +...  17.5 us
    unnamed x62, local copies, waits for them, and re-layouts  15.8 us
    ppermute x4, starting transfers between devices, body(): from_low = [lax.ppermute(piece, 'tensor', up) for piece in from_low]  11.7 us
    ppermute x4, waiting for transfers between devices, body(): from_low = [lax.ppermute(piece, 'tensor', up) for piece in from_low]  11.1 us
    dot_general x10, matrix products, part(): return jnp.dot(piece, rows, preferred_element_type=jnp.float32)  9.47 us
    ppermute x3, starting transfers between devices, body(): blocks.append(lax.ppermute(block_for((me_z + s) % n_z), 'tensor', ring[s]))  6.47 us
  transfers between devices with their start and end apart: 26, of which 10 were waited for; matrix products, arithmetic and copies ran while one was open for 13% of the time, Pallas kernels for 11%

profile of v3, /device:TPU:0, one launch (start us, length us, event | category | flops | bytes accessed | tf_op | source)
XLA Modules:
  0.0 174.1 jit_solution(5040788888967107457)
XLA Ops:
  7.2 1.2 copy-done.19
  8.5 5.0 %collective-permute-start = (bf16[128,2048]{1,0:T(8,128)(2,1)S(1)}, bf16[128,2048]{1,0:T(8,128)(2,1)S(1)}, u32[]{:S(2)}, u32[]{:S(2)}) collective-permute-start(bf16[128,2048]{1,0:T(8,128)(2,1)S(1)} %get-tuple-element.28.refs_0_), channel_id=1, source_target_pairs={{0,1},{1,2},{2,3},{4,5},{5,6},{6,7},{8,9},{9,10},{10,11},{12,13},{... | collective-permute-start | bytes 1572872 | tf_op jit(solution)/shard_map/ppermute | solution.py:287
  13.5 11.1 %collective-permute-done.refs_2_ = bf16[128,2048]{1,0:T(8,128)(2,1)S(1)} collective-permute-done((bf16[128,2048]{1,0:T(8,128)(2,1)S(1)}, bf16[128,2048]{1,0:T(8,128)(2,1)S(1)}, u32[]{:S(2)}, u32[]{:S(2)}) %collective-permute-start) | collective-permute-done | bytes 524320 | tf_op jit(solution)/shard_map/ppermute | solution.py:287
  24.6 5.1 %optimizer.1 = (f32[1024,256]{1,0:T(8,128)}, f32[1024,256]{1,0:T(8,128)}, f32[1024,256]{1,0:T(8,128)}, bf16[1024,256]{1,0:T(8,128)(2,1)}) custom-call(s32[1]{0:T(128)} %bitcast.place, bf16[8192,256]{1,0:T(8,128)(2,1)} %cached.1, f32[1024,256]{1,0:T(8,128)} %master, f32[1024,256]{1,0:T(8,128)} %moment.1, f32[1024,256]{1,0:T(8,128)} %second.1, f32[1024,256]{1,0:T(8,128)} %grad.1), custom_call_target="tpu_custom_call" | custom-call | flops 10485760 | bytes 8388608 | tf_op jit(solution)/shard_map/optimizer/pallas_call | solution.py:51
  29.9 1.1 constant_dynamic-slice_fusion.3
  31.0 2.5 %collective-permute-start.21 = (bf16[256,256]{1,0:T(8,128)(2,1)S(1)}, bf16[256,256]{1,0:T(8,128)(2,1)S(1)}, u32[]{:S(2)}, u32[]{:S(2)}) collective-permute-start(bf16[256,256]{1,0:T(8,128)(2,1)S(1)} %get-tuple-element.59), channel_id=1, source_target_pairs={{0,1},{1,2},{2,3},{3,0},{4,5},{5,6},{6,7},{7,4},{8,9},{9,10},{10,1... | collective-permute-start | bytes 393224 | tf_op jit(solution)/shard_map/ppermute | solution.py:321
  33.5 2.6 %collective-permute-start.22 = (bf16[256,256]{1,0:T(8,128)(2,1)S(1)}, bf16[256,256]{1,0:T(8,128)(2,1)S(1)}, u32[]{:S(2)}, u32[]{:S(2)}) collective-permute-start(bf16[256,256]{1,0:T(8,128)(2,1)S(1)} %get-tuple-element.58), channel_id=1, source_target_pairs={{0,2},{1,3},{2,0},{3,1},{4,6},{5,7},{6,4},{7,5},{8,10},{9,11},{10,... | collective-permute-start | bytes 393224 | tf_op jit(solution)/shard_map/ppermute | solution.py:321
  36.1 1.3 collective-permute-start.23
  37.5 1.3 collective-permute-start.2
  38.8 4.6 %collective-permute-start.1 = (bf16[128,2048]{1,0:T(8,128)(2,1)S(1)}, bf16[128,2048]{1,0:T(8,128)(2,1)S(1)}, u32[]{:S(2)}, u32[]{:S(2)}) collective-permute-start(bf16[128,2048]{1,0:T(8,128)(2,1)S(1)} %get-tuple-element.34.refs_1_), channel_id=1, source_target_pairs={{0,1},{1,2},{2,3},{4,5},{5,6},{6,7},{8,9},{9,10},{10,11},{12,13},{... | collective-permute-start | bytes 1572872 | tf_op jit(solution)/shard_map/ppermute | solution.py:287
  43.4 1.3 collective-permute-start.3
  46.2 1.6 fusion.30
  47.8 1.5 fusion.28
  49.4 1.5 collective-permute-start.4
  50.9 5.7 %collective-permute-done.2.refs_4_ = bf16[128,2048]{1,0:T(8,128)(2,1)S(1)} collective-permute-done((bf16[128,2048]{1,0:T(8,128)(2,1)S(1)}, bf16[128,2048]{1,0:T(8,128)(2,1)S(1)}, u32[]{:S(2)}, u32[]{:S(2)}) %collective-permute-start.2) | collective-permute-done | bytes 524320 | tf_op jit(solution)/shard_map/ppermute | solution.py:288
  56.6 1.3 collective-permute-start.5
  58.0 1.2 copy.20
  60.2 2.1 %copy.42 = bf16[256,1024]{0,1:T(8,128)(2,1)} copy(bf16[256,1024]{1,0:T(8,128)(2,1)} %param.10) | data formatting | bytes 1048576 | tf_op jit(solution)/shard_map/reshape.1
  63.1 4.8 %collective-permute-done.3.refs_5_ = bf16[128,2048]{1,0:T(8,128)(2,1)} collective-permute-done((bf16[128,2048]{1,0:T(8,128)(2,1)S(1)}, bf16[128,2048]{1,0:T(8,128)(2,1)}, u32[]{:S(2)}, u32[]{:S(2)}) %collective-permute-start.3) | collective-permute-done | bytes 524320 | tf_op jit(solution)/shard_map/ppermute | solution.py:288
  67.9 1.3 collective-permute-start.7
  69.2 1.5 convolution_add_fusion.5
  70.8 1.7 convolution_add_fusion.2
  72.5 6.6 %collective-permute-done.5 = bf16[128,2048]{1,0:T(8,128)(2,1)} collective-permute-done((bf16[128,2048]{1,0:T(8,128)(2,1)S(1)}, bf16[128,2048]{1,0:T(8,128)(2,1)}, u32[]{:S(2)}, u32[]{:S(2)}) %collective-permute-start.5) | collective-permute-done | bytes 524320 | tf_op jit(solution)/shard_map/ppermute | solution.py:288
  79.2 1.1 broadcast_select_fusion.1.refs_6_
  80.3 1.3 collective-permute-start.8
  81.6 8.7 %collective-permute-done.7 = bf16[128,2048]{1,0:T(8,128)(2,1)S(1)} collective-permute-done((bf16[128,2048]{1,0:T(8,128)(2,1)}, bf16[128,2048]{1,0:T(8,128)(2,1)S(1)}, u32[]{:S(2)}, u32[]{:S(2)}) %collective-permute-start.7) | collective-permute-done | bytes 524320 | tf_op jit(solution)/shard_map/ppermute | solution.py:288
  90.4 1.3 collective-permute-start.9
  92.0 1.5 convolution_add_fusion.1
  93.5 8.0 %collective-permute-done.8.refs_8_ = bf16[128,2048]{1,0:T(8,128)(2,1)S(1)} collective-permute-done((bf16[128,2048]{1,0:T(8,128)(2,1)S(1)}, bf16[128,2048]{1,0:T(8,128)(2,1)S(1)}, u32[]{:S(2)}, u32[]{:S(2)}) %collective-permute-start.8) | collective-permute-done | bytes 524320 | tf_op jit(solution)/shard_map/ppermute | solution.py:290
  101.9 9.6 %collective-permute-done.9.refs_9_ = bf16[128,2048]{1,0:T(8,128)(2,1)S(1)} collective-permute-done((bf16[128,2048]{1,0:T(8,128)(2,1)S(1)}, bf16[128,2048]{1,0:T(8,128)(2,1)S(1)}, u32[]{:S(2)}, u32[]{:S(2)}) %collective-permute-start.9) | collective-permute-done | bytes 524320 | tf_op jit(solution)/shard_map/ppermute | solution.py:290
  112.7 1.5 fusion.45
  119.6 1.0 copy-done.7
  121.6 3.4 %weight_send_other.1 = (bf16[2,128,1024]{2,1,0:T(8,128)(2,1)}, bf16[2,128,1024]{2,1,0:T(8,128)(2,1)}) custom-call(s32[8]{0:T(128)S(1)} %stack.95.place, bf16[128,2048]{1,0:T(8,128)(2,1)S(1)} %get-tuple-element.28.refs_0_, bf16[128,2048]{1,0:T(8,128)(2,1)S(1)} %get-tuple-element.34.refs_1_, bf16[128,2048]{1,0:T(8,128)(2,1)S(1)} %copy-done.1, ...), custom_call_target="tpu_custom_call" | custom-call | flops 268435456 | bytes 6422528 | tf_op jit(solution)/shard_map/weight_send_other/pallas_call | solution.py:110
  125.7 1.0 copy-done.2
  128.8 3.5 %weight_keep_other.1 = (bf16[2,128,1024]{2,1,0:T(8,128)(2,1)}, bf16[2,128,1024]{2,1,0:T(8,128)(2,1)}) custom-call(s32[8]{0:T(128)S(1)} %stack.95.place, bf16[128,2048]{1,0:T(8,128)(2,1)S(1)} %get-tuple-element.28.refs_0_, bf16[128,2048]{1,0:T(8,128)(2,1)S(1)} %get-tuple-element.34.refs_1_, bf16[128,2048]{1,0:T(8,128)(2,1)S(1)} %copy-done.2, ...), custom_call_target="tpu_custom_call" | custom-call | flops 268435456 | bytes 6422528 | tf_op jit(solution)/shard_map/weight_keep_other/pallas_call | solution.py:110
  132.8 3.9 %weight_send.1 = (bf16[2,128,1024]{2,1,0:T(8,128)(2,1)}, bf16[2,128,1024]{2,1,0:T(8,128)(2,1)}) custom-call(s32[8]{0:T(128)S(1)} %stack.90.place, bf16[128,2048]{1,0:T(8,128)(2,1)S(1)} %get-tuple-element.28.refs_0_, bf16[128,2048]{1,0:T(8,128)(2,1)S(1)} %get-tuple-element.34.refs_1_, bf16[128,2048]{1,0:T(8,128)(2,1)S(1)} %copy-done.3, ...), custom_call_target="tpu_custom_call" | custom-call | flops 268435456 | bytes 7471104 | tf_op jit(solution)/shard_map/weight_send/pallas_call | solution.py:110
  136.7 1.5 collective-permute-start.14
  138.1 1.5 collective-permute-start.15
  139.9 3.8 %collective-permute-start.20 = (bf16[256,256]{1,0:T(8,128)(2,1)S(1)}, bf16[256,256]{1,0:T(8,128)(2,1)}, u32[]{:S(2)}, u32[]{:S(2)}) collective-permute-start(bf16[256,256]{1,0:T(8,128)(2,1)S(1)} %copy.38.refs_10_.refs_0_), channel_id=1, source_target_pairs={{0,3},{1,0},{2,1},{3,2},{4,7},{5,4},{6,5},{7,6},{8,11},{9,8},{10,9... | collective-permute-start | bytes 393224 | tf_op jit(solution)/shard_map/ppermute | solution.py:327
  143.7 1.0 copy-done.4
  146.8 2.7 %weight_keep.1 = (f32[2,128,1024]{2,1,0:T(8,128)S(1)}, f32[2,128,1024]{2,1,0:T(8,128)S(1)}) custom-call(s32[8]{0:T(128)S(1)} %stack.90.place, bf16[128,2048]{1,0:T(8,128)(2,1)S(1)} %get-tuple-element.28.refs_0_, bf16[128,2048]{1,0:T(8,128)(2,1)S(1)} %get-tuple-element.34.refs_1_, bf16[128,2048]{1,0:T(8,128)(2,1)S(1)} %copy-done.4, ...), custom_call_target="tpu_custom_call" | custom-call | flops 268435456 | bytes 8519680 | tf_op jit(solution)/shard_map/weight_keep/pallas_call | solution.py:110
  149.6 1.2 collective-permute-done.14.got_a
  150.8 1.2 collective-permute-done.15.got_b
  152.0 1.3 weight_combine.1
  153.3 1.6 collective-permute-start.16
  157.5 5.0 %input_gradient.1 = bf16[256,2048]{1,0:T(8,128)(2,1)} custom-call(bf16[256,256]{1,0:T(8,128)(2,1)} %copy-done.14, bf16[256,256]{1,0:T(8,128)(2,1)} %copy-done.28, bf16[256,256]{1,0:T(8,128)(2,1)} %collective-permute-done.19.refs_2_, bf16[256,256]{1,0:T(8,128)(2,1)} %collective-permute-done.20.refs_3_, bf16[2048,1024]{1,0:T(8,128)(2,1)} %all-gather.5.cloned.1.call-done.refs_4_), custom_call_target="tpu_custom_call" | custom-call | flops 1073741824 | bytes 5767168 | tf_op jit(solution)/shard_map/input_gradient/pallas_call | solution.py:243
  162.5 2.7 %weight_finish.1 = f32[1024,256]{1,0:T(8,128)} custom-call(s32[2]{0:T(128)S(1)} %pad_add_fusion.place, f32[2,128,1024]{2,1,0:T(8,128)S(1)} %copy-done.16, bf16[2,128,1024]{2,1,0:T(8,128)(2,1)} %collective-permute-done.14.got_a, f32[2,128,1024]{2,1,0:T(8,128)S(1)} %copy-done.18, bf16[2,128,1024]{2,1,0:T(8,128)(2,1)} %collective-permute-done.15.got_b, ...), custom_call_target="tpu_custom_call" | custom-call | flops 524288 | bytes 4718592 | tf_op jit(solution)/shard_map/weight_finish/pallas_call | solution.py:110
  165.2 2.0 %copy.53 = bf16[8192,256]{1,0:T(8,128)(2,1)} copy(bf16[8192,256]{1,0:T(8,128)(2,1)S(1)} %copy-done.22) | data formatting | bytes 8388608
  (112 shorter events, 19.9 us)
Async XLA Ops:
  7.2 149.6 %all-gather.3.cloned.1.call-start = ((), (), s32[]{:S(2)}) async-start(), calls=%async_computation | async-start | bytes 4718592 | tf_op jit(solution)/shard_map/all_gather | solution.py:312
  7.2 1.2 copy-start.19
  8.5 16.1 %collective-permute-start = (bf16[128,2048]{1,0:T(8,128)(2,1)S(1)}, bf16[128,2048]{1,0:T(8,128)(2,1)S(1)}, u32[]{:S(2)}, u32[]{:S(2)}) collective-permute-start(bf16[128,2048]{1,0:T(8,128)(2,1)S(1)} %get-tuple-element.28.refs_0_), channel_id=1, source_target_pairs={{0,1},{1,2},{2,3},{4,5},{5,6},{6,7},{8,9},{9,10},{10,11},{12,13},{... | collective-permute-start | bytes 1572872 | tf_op jit(solution)/shard_map/ppermute | solution.py:287
  24.6 44.6 %copy-start = (bf16[128,2048]{1,0:T(8,128)(2,1)}, bf16[128,2048]{1,0:T(8,128)(2,1)S(1)}, u32[]{:S(2)}) copy-start(bf16[128,2048]{1,0:T(8,128)(2,1)S(1)} %collective-permute-done.refs_2_) | copy-start | bytes 1572868
  29.7 127.1 %all-gather.5.cloned.1.call-start = ((), (), s32[]{:S(2)}) async-start(), calls=%async_computation.1 | async-start | bytes 4718592 | tf_op jit(solution)/shard_map/all_gather | solution.py:322
  31.0 12.4 %collective-permute-start.21 = (bf16[256,256]{1,0:T(8,128)(2,1)S(1)}, bf16[256,256]{1,0:T(8,128)(2,1)S(1)}, u32[]{:S(2)}, u32[]{:S(2)}) collective-permute-start(bf16[256,256]{1,0:T(8,128)(2,1)S(1)} %get-tuple-element.59), channel_id=1, source_target_pairs={{0,1},{1,2},{2,3},{3,0},{4,5},{5,6},{6,7},{7,4},{8,9},{9,10},{10,1... | collective-permute-start | bytes 393224 | tf_op jit(solution)/shard_map/ppermute | solution.py:321
  33.5 11.1 %collective-permute-start.22 = (bf16[256,256]{1,0:T(8,128)(2,1)S(1)}, bf16[256,256]{1,0:T(8,128)(2,1)S(1)}, u32[]{:S(2)}, u32[]{:S(2)}) collective-permute-start(bf16[256,256]{1,0:T(8,128)(2,1)S(1)} %get-tuple-element.58), channel_id=1, source_target_pairs={{0,2},{1,3},{2,0},{3,1},{4,6},{5,7},{6,4},{7,5},{8,10},{9,11},{10,... | collective-permute-start | bytes 393224 | tf_op jit(solution)/shard_map/ppermute | solution.py:321
  36.1 9.2 %collective-permute-start.23 = (bf16[256,256]{1,0:T(8,128)(2,1)S(1)}, bf16[256,256]{1,0:T(8,128)(2,1)S(1)}, u32[]{:S(2)}, u32[]{:S(2)}) collective-permute-start(bf16[256,256]{1,0:T(8,128)(2,1)S(1)} %get-tuple-element.57), channel_id=1, source_target_pairs={{0,3},{1,0},{2,1},{3,2},{4,7},{5,4},{6,5},{7,6},{8,11},{9,8},{10,9... | collective-permute-start | bytes 393224 | tf_op jit(solution)/shard_map/ppermute | solution.py:321
  37.5 19.1 %collective-permute-start.2 = (bf16[128,2048]{1,0:T(8,128)(2,1)S(1)}, bf16[128,2048]{1,0:T(8,128)(2,1)S(1)}, u32[]{:S(2)}, u32[]{:S(2)}) collective-permute-start(bf16[128,2048]{1,0:T(8,128)(2,1)S(1)} %get-tuple-element.28.refs_0_), channel_id=1, source_target_pairs={{1,0},{2,1},{3,2},{5,4},{6,5},{7,6},{9,8},{10,9},{11,10},{13,12},{... | collective-permute-start | bytes 1572872 | tf_op jit(solution)/shard_map/ppermute | solution.py:288
  38.8 23.6 %collective-permute-start.1 = (bf16[128,2048]{1,0:T(8,128)(2,1)S(1)}, bf16[128,2048]{1,0:T(8,128)(2,1)S(1)}, u32[]{:S(2)}, u32[]{:S(2)}) collective-permute-start(bf16[128,2048]{1,0:T(8,128)(2,1)S(1)} %get-tuple-element.34.refs_1_), channel_id=1, source_target_pairs={{0,1},{1,2},{2,3},{4,5},{5,6},{6,7},{8,9},{9,10},{10,11},{12,13},{... | collective-permute-start | bytes 1572872 | tf_op jit(solution)/shard_map/ppermute | solution.py:287
  43.4 24.6 %collective-permute-start.3 = (bf16[128,2048]{1,0:T(8,128)(2,1)S(1)}, bf16[128,2048]{1,0:T(8,128)(2,1)}, u32[]{:S(2)}, u32[]{:S(2)}) collective-permute-start(bf16[128,2048]{1,0:T(8,128)(2,1)S(1)} %get-tuple-element.34.refs_1_), channel_id=1, source_target_pairs={{1,0},{2,1},{3,2},{5,4},{6,5},{7,6},{9,8},{10,9},{11,10},{13,12},{... | collective-permute-start | bytes 1572872 | tf_op jit(solution)/shard_map/ppermute | solution.py:288
  46.2 11.7 %copy-start.29 = (s32[1,256]{1,0:T(1,128)S(1)}, s32[1,256]{1,0:T(1,128)}, u32[]{:S(2)}) copy-start(s32[1,256]{1,0:T(1,128)} %param.12) | copy-start | bytes 3076
  46.2 11.8 %copy-start.26 = (bf16[256,1024]{1,0:T(8,128)(2,1)S(1)}, bf16[256,1024]{1,0:T(8,128)(2,1)}, u32[]{:S(2)}) copy-start(bf16[256,1024]{1,0:T(8,128)(2,1)} %param.11) | copy-start | bytes 1572868
  49.4 23.1 %collective-permute-start.4 = (bf16[128,2048]{1,0:T(8,128)(2,1)S(1)}, bf16[128,2048]{1,0:T(8,128)(2,1)}, u32[]{:S(2)}, u32[]{:S(2)}) collective-permute-start(bf16[128,2048]{1,0:T(8,128)(2,1)S(1)} %collective-permute-done.refs_2_), channel_id=1, source_target_pairs={{1,2},{2,3},{5,6},{6,7},{9,10},{10,11},{13,14},{14,15},{17,18},{18... | collective-permute-start | bytes 1572872 | tf_op jit(solution)/shard_map/ppermute | solution.py:287
  56.6 14.2 %copy-start.5 = (bf16[128,2048]{1,0:T(8,128)(2,1)}, bf16[128,2048]{1,0:T(8,128)(2,1)S(1)}, u32[]{:S(2)}) copy-start(bf16[128,2048]{1,0:T(8,128)(2,1)S(1)} %collective-permute-done.2.refs_4_) | copy-start | bytes 1572868
  56.6 22.6 %collective-permute-start.5 = (bf16[128,2048]{1,0:T(8,128)(2,1)S(1)}, bf16[128,2048]{1,0:T(8,128)(2,1)}, u32[]{:S(2)}, u32[]{:S(2)}) collective-permute-start(bf16[128,2048]{1,0:T(8,128)(2,1)S(1)} %collective-permute-done.2.refs_4_), channel_id=1, source_target_pairs={{1,0},{2,1},{5,4},{6,5},{9,8},{10,9},{13,12},{14,13},{17,16},{18,1... | collective-permute-start | bytes 1572872 | tf_op jit(solution)/shard_map/ppermute | solution.py:288
  62.4 17.9 %copy-start.10 = (bf16[128,2048]{1,0:T(8,128)(2,1)}, bf16[128,2048]{1,0:T(8,128)(2,1)S(1)}, u32[]{:S(2)}) copy-start(bf16[128,2048]{1,0:T(8,128)(2,1)S(1)} %collective-permute-done.1.refs_3_) | copy-start | bytes 1572868
  62.4 19.2 %collective-permute-start.6 = (bf16[128,2048]{1,0:T(8,128)(2,1)S(1)}, bf16[128,2048]{1,0:T(8,128)(2,1)S(1)}, u32[]{:S(2)}, u32[]{:S(2)}) collective-permute-start(bf16[128,2048]{1,0:T(8,128)(2,1)S(1)} %collective-permute-done.1.refs_3_), channel_id=1, source_target_pairs={{1,2},{2,3},{5,6},{6,7},{9,10},{10,11},{13,14},{14,15},{17,18},{18... | collective-permute-start | bytes 1572872 | tf_op jit(solution)/shard_map/ppermute | solution.py:287
  67.9 22.4 %collective-permute-start.7 = (bf16[128,2048]{1,0:T(8,128)(2,1)}, bf16[128,2048]{1,0:T(8,128)(2,1)S(1)}, u32[]{:S(2)}, u32[]{:S(2)}) collective-permute-start(bf16[128,2048]{1,0:T(8,128)(2,1)} %collective-permute-done.3.refs_5_), channel_id=1, source_target_pairs={{1,0},{2,1},{5,4},{6,5},{9,8},{10,9},{13,12},{14,13},{17,16},{18,1... | collective-permute-start | bytes 1572872 | tf_op jit(solution)/shard_map/ppermute | solution.py:288
  70.8 20.9 %copy-start.20 = (bf16[8192,256]{1,0:T(8,128)(2,1)S(1)}, bf16[8192,256]{1,0:T(8,128)(2,1)}, u32[]{:S(2)}) copy-start(bf16[8192,256]{1,0:T(8,128)(2,1)} %cached.1) | copy-start | bytes 12582916
  72.5 19.2 %copy-start.6 = (bf16[128,2048]{1,0:T(8,128)(2,1)S(1)}, bf16[128,2048]{1,0:T(8,128)(2,1)}, u32[]{:S(2)}) copy-start(bf16[128,2048]{1,0:T(8,128)(2,1)} %copy-done.5) | copy-start | bytes 1572868
  80.3 21.3 %collective-permute-start.8 = (bf16[128,2048]{1,0:T(8,128)(2,1)S(1)}, bf16[128,2048]{1,0:T(8,128)(2,1)S(1)}, u32[]{:S(2)}, u32[]{:S(2)}) collective-permute-start(bf16[128,2048]{1,0:T(8,128)(2,1)S(1)} %broadcast_select_fusion.1.refs_6_), channel_id=1, source_target_pairs={{2,3},{1,0},{6,7},{5,4},{10,11},{9,8},{14,15},{13,12},{18,19},{17,... | collective-permute-start | bytes 1572872 | tf_op jit(solution)/shard_map/ppermute | solution.py:290
  90.4 21.1 %collective-permute-start.9 = (bf16[128,2048]{1,0:T(8,128)(2,1)S(1)}, bf16[128,2048]{1,0:T(8,128)(2,1)S(1)}, u32[]{:S(2)}, u32[]{:S(2)}) collective-permute-start(bf16[128,2048]{1,0:T(8,128)(2,1)S(1)} %broadcast_select_fusion.refs_7_), channel_id=1, source_target_pairs={{2,3},{1,0},{6,7},{5,4},{10,11},{9,8},{14,15},{13,12},{18,19},{17,... | collective-permute-start | bytes 1572872 | tf_op jit(solution)/shard_map/ppermute | solution.py:290
  114.5 1.0 copy-start.27
  114.5 1.5 copy-start.23
  116.4 1.0 copy-start.21
  118.5 1.0 copy-start.1
  121.6 22.1 %copy-start.14 = (bf16[256,256]{1,0:T(8,128)(2,1)}, bf16[256,256]{1,0:T(8,128)(2,1)S(1)}, u32[]{:S(2)}) copy-start(bf16[256,256]{1,0:T(8,128)(2,1)S(1)} %copy.38.refs_10_.refs_0_) | copy-start | bytes 393220
  125.1 7.7 %collective-permute-start.12 = (bf16[2,128,1024]{2,1,0:T(8,128)(2,1)}, bf16[2,128,1024]{2,1,0:T(8,128)(2,1)}, u32[]{:S(2)}, u32[]{:S(2)}) collective-permute-start(bf16[2,128,1024]{2,1,0:T(8,128)(2,1)} %get-tuple-element.38), channel_id=1, source_target_pairs={{0,4},{4,0},{8,12},{12,8},{16,20},{20,16},{24,28},{28,24},{1,5},{5... | collective-permute-start | bytes 1572872 | tf_op jit(solution)/shard_map/ppermute | solution.py:186
  125.1 7.7 %collective-permute-start.13 = (bf16[2,128,1024]{2,1,0:T(8,128)(2,1)}, bf16[2,128,1024]{2,1,0:T(8,128)(2,1)}, u32[]{:S(2)}, u32[]{:S(2)}) collective-permute-start(bf16[2,128,1024]{2,1,0:T(8,128)(2,1)} %get-tuple-element.39), channel_id=1, source_target_pairs={{0,4},{4,0},{8,12},{12,8},{16,20},{20,16},{24,28},{28,24},{1,5},{5... | collective-permute-start | bytes 1572872 | tf_op jit(solution)/shard_map/ppermute | solution.py:186
  125.7 1.0 copy-start.2
  128.8 4.0 %copy-start.3 = (bf16[128,2048]{1,0:T(8,128)(2,1)S(1)}, bf16[128,2048]{1,0:T(8,128)(2,1)}, u32[]{:S(2)}) copy-start(bf16[128,2048]{1,0:T(8,128)(2,1)} %copy-done) | copy-start | bytes 1572868
  132.2 7.6 %collective-permute-start.10 = (bf16[2,128,1024]{2,1,0:T(8,128)(2,1)}, bf16[2,128,1024]{2,1,0:T(8,128)(2,1)}, u32[]{:S(2)}, u32[]{:S(2)}) collective-permute-start(bf16[2,128,1024]{2,1,0:T(8,128)(2,1)} %get-tuple-element.35), channel_id=1, source_target_pairs={{0,4},{4,0},{8,12},{12,8},{16,20},{20,16},{24,28},{28,24},{1,5},{5... | collective-permute-start | bytes 1572872 | tf_op jit(solution)/shard_map/ppermute | solution.py:186
  132.3 7.6 %collective-permute-start.11 = (bf16[2,128,1024]{2,1,0:T(8,128)(2,1)}, bf16[2,128,1024]{2,1,0:T(8,128)(2,1)}, u32[]{:S(2)}, u32[]{:S(2)}) collective-permute-start(bf16[2,128,1024]{2,1,0:T(8,128)(2,1)} %get-tuple-element.36), channel_id=1, source_target_pairs={{0,4},{4,0},{8,12},{12,8},{16,20},{20,16},{24,28},{28,24},{1,5},{5... | collective-permute-start | bytes 1572872 | tf_op jit(solution)/shard_map/ppermute | solution.py:186
  136.7 14.2 %collective-permute-start.14 = (bf16[2,128,1024]{2,1,0:T(8,128)(2,1)}, bf16[2,128,1024]{2,1,0:T(8,128)(2,1)}, u32[]{:S(2)}, u32[]{:S(2)}) collective-permute-start(bf16[2,128,1024]{2,1,0:T(8,128)(2,1)} %get-tuple-element.40), channel_id=1, source_target_pairs={{0,8},{4,12},{8,0},{12,4},{16,24},{20,28},{24,16},{28,20},{1,9},{5... | collective-permute-start | bytes 1572872 | tf_op jit(solution)/shard_map/ppermute | solution.py:186
  138.1 13.9 %collective-permute-start.15 = (bf16[2,128,1024]{2,1,0:T(8,128)(2,1)}, bf16[2,128,1024]{2,1,0:T(8,128)(2,1)}, u32[]{:S(2)}, u32[]{:S(2)}) collective-permute-start(bf16[2,128,1024]{2,1,0:T(8,128)(2,1)} %get-tuple-element.42), channel_id=1, source_target_pairs={{0,16},{4,20},{8,24},{12,28},{16,0},{20,4},{24,8},{28,12},{1,17},{... | collective-permute-start | bytes 1572872 | tf_op jit(solution)/shard_map/ppermute | solution.py:186
  139.8 17.0 %collective-permute-start.18 = (bf16[256,256]{1,0:T(8,128)(2,1)S(1)}, bf16[256,256]{1,0:T(8,128)(2,1)S(1)}, u32[]{:S(2)}, u32[]{:S(2)}) collective-permute-start(bf16[256,256]{1,0:T(8,128)(2,1)S(1)} %copy.38.refs_10_.refs_0_), channel_id=1, source_target_pairs={{0,1},{1,2},{2,3},{3,0},{4,5},{5,6},{6,7},{7,4},{8,9},{9,10},{10,1... | collective-permute-start | bytes 393224 | tf_op jit(solution)/shard_map/ppermute | solution.py:327
  139.8 17.0 %collective-permute-start.19 = (bf16[256,256]{1,0:T(8,128)(2,1)S(1)}, bf16[256,256]{1,0:T(8,128)(2,1)}, u32[]{:S(2)}, u32[]{:S(2)}) collective-permute-start(bf16[256,256]{1,0:T(8,128)(2,1)S(1)} %copy.38.refs_10_.refs_0_), channel_id=1, source_target_pairs={{0,2},{1,3},{2,0},{3,1},{4,6},{5,7},{6,4},{7,5},{8,10},{9,11},{10,... | collective-permute-start | bytes 393224 | tf_op jit(solution)/shard_map/ppermute | solution.py:327
  139.9 16.9 %collective-permute-start.20 = (bf16[256,256]{1,0:T(8,128)(2,1)S(1)}, bf16[256,256]{1,0:T(8,128)(2,1)}, u32[]{:S(2)}, u32[]{:S(2)}) collective-permute-start(bf16[256,256]{1,0:T(8,128)(2,1)S(1)} %copy.38.refs_10_.refs_0_), channel_id=1, source_target_pairs={{0,3},{1,0},{2,1},{3,2},{4,7},{5,4},{6,5},{7,6},{8,11},{9,8},{10,9... | collective-permute-start | bytes 393224 | tf_op jit(solution)/shard_map/ppermute | solution.py:327
  143.7 1.0 copy-start.4
  149.6 6.2 %copy-start.15 = (f32[2,128,1024]{2,1,0:T(8,128)}, f32[2,128,1024]{2,1,0:T(8,128)S(1)}, u32[]{:S(2)}) copy-start(f32[2,128,1024]{2,1,0:T(8,128)S(1)} %get-tuple-element.37.keep_a) | copy-start | bytes 3145732
  149.6 6.2 %copy-start.17 = (f32[2,128,1024]{2,1,0:T(8,128)}, f32[2,128,1024]{2,1,0:T(8,128)S(1)}, u32[]{:S(2)}) copy-start(f32[2,128,1024]{2,1,0:T(8,128)S(1)} %get-tuple-element.41.keep_b) | copy-start | bytes 3145732
  149.6 5.9 %copy-start.25 = (bf16[8,256,256]{1,2,0:T(8,128)(2,1)S(1)}, bf16[8,256,256]{1,2,0:T(8,128)(2,1)}, u32[]{:S(2)}) copy-start(bf16[8,256,256]{1,2,0:T(8,128)(2,1)} %copy-done.24) | copy-start | bytes 3145732
  153.3 9.2 %collective-permute-start.16 = (bf16[128,1024]{1,0:T(8,128)(2,1)S(1)}, bf16[128,1024]{1,0:T(8,128)(2,1)S(1)}, u32[]{:S(2)}, u32[]{:S(2)}) collective-permute-start(bf16[128,1024]{1,0:T(8,128)(2,1)S(1)} %get-tuple-element.43), channel_id=1, source_target_pairs={{0,16},{4,20},{8,24},{12,28},{16,0},{20,4},{24,8},{28,12},{1,17},{... | collective-permute-start | bytes 786440 | tf_op jit(solution)/shard_map/ppermute | solution.py:186
  154.9 7.6 %collective-permute-start.17 = (bf16[128,1024]{1,0:T(8,128)(2,1)S(1)}, bf16[128,1024]{1,0:T(8,128)(2,1)S(1)}, u32[]{:S(2)}, u32[]{:S(2)}) collective-permute-start(bf16[128,1024]{1,0:T(8,128)(2,1)S(1)} %get-tuple-element.44), channel_id=1, source_target_pairs={{0,8},{4,12},{8,0},{12,4},{16,24},{20,28},{24,16},{28,20},{1,9},{5... | collective-permute-start | bytes 786440 | tf_op jit(solution)/shard_map/ppermute | solution.py:186
  156.8 5.7 %copy-start.16 = (f32[2,128,1024]{2,1,0:T(8,128)S(1)}, f32[2,128,1024]{2,1,0:T(8,128)}, u32[]{:S(2)}) copy-start(f32[2,128,1024]{2,1,0:T(8,128)} %copy-done.15) | copy-start | bytes 3145732
  156.8 5.7 %copy-start.18 = (f32[2,128,1024]{2,1,0:T(8,128)S(1)}, f32[2,128,1024]{2,1,0:T(8,128)}, u32[]{:S(2)}) copy-start(f32[2,128,1024]{2,1,0:T(8,128)} %copy-done.17) | copy-start | bytes 3145732
  162.5 2.7 %copy-start.22 = (bf16[8192,256]{1,0:T(8,128)(2,1)S(1)}, bf16[8192,256]{1,0:T(8,128)(2,1)}, u32[]{:S(2)}) copy-start(bf16[8192,256]{1,0:T(8,128)(2,1)} %all-gather.3.cloned.1.call-done) | copy-start | bytes 12582916
  (8 other events, 7.9 us)
Sparse Core Ops, SparseCore 0:
  29.9 38.8 all-gather.2
  70.7 36.7 all-gather.4

commit v4 on v2

v4 whole, which is shorter than its diff:
```python
import math

import jax
import jax.numpy as jnp
from jax import lax
from jax.experimental import pallas as pl
from jax.experimental.pallas import tpu as pltpu
from jax.sharding import PartitionSpec as P

HD = 128
VMEM_STREAM = 56 * 1024 * 1024
VMEM_PART = 40 * 1024 * 1024
VMEM_WHOLE = 24 * 1024 * 1024


beta_first = 0.9
beta_second = 0.95
learn_rate = 0.0003
weight_decay = 0.1
adam_epsilon = 1e-08
first_fix = 1.0 - 0.9**40
second_fix = 1.0 - 0.95**40


def optimizer_kernel(
    place, cached, master, moment, second, grad, master_out, moment_out, second_out, cache_out
):
    moment_new = beta_first * moment[...] + (1.0 - beta_first) * grad[...]
    second_new = beta_second * second[...] + (1.0 - beta_second) * grad[...] * grad[...]
    update = moment_new / first_fix / (jnp.sqrt(second_new / second_fix) + adam_epsilon)
    master_new = master[...] - learn_rate * (update + weight_decay * master[...])
    moment_out[...] = moment_new
    second_out[...] = second_new
    master_out[...] = master_new
    for start in range(0, cached.shape[1], HD):
        block = slice(start, start + HD)
        own_cache = cached[:, block].astype(jnp.float32)
        delta = master_new[:, block] - own_cache
        largest = jnp.max(jnp.abs(delta), axis=1, keepdims=True)
        scale = (largest + 1e-06).astype(jnp.bfloat16).astype(jnp.float32)
        codes = (delta / scale).astype(jnp.bfloat16)
        cache_out[:, block] = (own_cache + codes.astype(jnp.float32) * scale).astype(jnp.bfloat16)


def optimizer(cached, master, moment, second, grad):
    rows, cols = master.shape
    step = min(rows, 256)
    steps = rows // step
    own = pl.BlockSpec((step, cols), lambda i, place: (i, 0))
    full = jax.ShapeDtypeStruct((rows, cols), jnp.float32)
    return pl.pallas_call(
        optimizer_kernel,
        grid_spec=pltpu.PrefetchScalarGridSpec(
            num_scalar_prefetch=1,
            grid=(steps,),
            in_specs=[pl.BlockSpec((step, cols), lambda i, place: (place[0] * steps + i, 0))]
            + [own] * 4,
            out_specs=[own] * 4,
        ),
        out_shape=[full, full, full, jax.ShapeDtypeStruct((rows, cols), jnp.bfloat16)],
        cost_estimate=pl.CostEstimate(
            flops=40 * rows * cols, bytes_accessed=32 * rows * cols, transcendentals=rows * cols
        ),
        compiler_params=pltpu.CompilerParams(vmem_limit_bytes=VMEM_STREAM),
        name="optimizer",
    )(lax.axis_index("dp").astype(jnp.int32).reshape(1), cached, master, moment, second, grad)


def on_chip(kernel, place, arrays, out_shape, flops, name):
    vmem = pl.BlockSpec(memory_space=pltpu.VMEM)
    size = sum(a.size * a.dtype.itemsize for a in arrays)
    size += sum(s.size * s.dtype.itemsize for s in out_shape)
    return pl.pallas_call(
        kernel,
        in_specs=[pl.BlockSpec(memory_space=pltpu.SMEM)] + [vmem] * len(arrays),
        out_specs=[vmem] * len(out_shape),
        out_shape=out_shape,
        cost_estimate=pl.CostEstimate(flops=flops, bytes_accessed=size, transcendentals=0),
        compiler_params=pltpu.CompilerParams(vmem_limit_bytes=VMEM_WHOLE),
        name=name,
    )(place, *arrays)


def absorb_kernel(place, chunk, cached, total, held, total_out, held_out):
    @pl.when(pl.program_id(0) == 0)
    def _():
        total_out[...] = total[...]

    total_out[...] += jnp.dot(chunk[...], cached[...], preferred_element_type=jnp.float32)
    held_out[0] = chunk[...].T


def absorb(chunk, index, cached, total, held, n_chunks):
    length, feats = chunk.shape
    cols = cached.shape[1]
    step = min(feats, 512)
    steps = feats // step
    inside = (index >= 0) & (index < n_chunks)
    place = jnp.stack([jnp.clip(index, 0, n_chunks - 1), jnp.where(inside, index, n_chunks)])
    shape = jax.ShapeDtypeStruct((n_chunks + 1, feats, length), chunk.dtype)
    out_total = jax.ShapeDtypeStruct(total.shape, jnp.float32)
    whole = pl.BlockSpec((length, cols), lambda i, place: (0, 0))
    operands = [chunk, cached, total] + ([] if held is None else [held])

    def kernel(place, chunk, cached, total, *refs):
        absorb_kernel(place, chunk, cached, total, None, *refs[-2:])

    return pl.pallas_call(
        kernel,
        grid_spec=pltpu.PrefetchScalarGridSpec(
            num_scalar_prefetch=1,
            grid=(steps,),
            in_specs=[
                pl.BlockSpec((length, step), lambda i, place: (0, i)),
                pl.BlockSpec((step, cols), lambda i, place: (place[0] * steps + i, 0)),
                whole,
            ]
            + ([] if held is None else [pl.BlockSpec(memory_space=pl.ANY)]),
            out_specs=[
                whole,
                pl.BlockSpec((1, step, length), lambda i, place: (place[1], i, 0)),
            ],
        ),
        out_shape=[out_total, shape],
        input_output_aliases={} if held is None else {4: 1},
        cost_estimate=pl.CostEstimate(
            flops=2 * length * feats * cols,
            bytes_accessed=4 * length * feats + 2 * feats * cols,
            transcendentals=0,
        ),
        compiler_params=pltpu.CompilerParams(vmem_limit_bytes=VMEM_PART),
        name="absorb",
    )(place, *operands)


def attention_kernel(place, projected, queries, d_out, allowed, d_queries, d_projected):
    factor = 1.0 / math.sqrt(HD)
    across = (((1,), (1,)), ((), ()))
    for head in range(projected.shape[1] // (2 * HD)):
        start = 2 * HD * head
        keys = projected[:, start : start + HD]
        values = projected[:, start + HD : start + 2 * HD]
        group = queries.shape[1] // HD // (projected.shape[1] // (2 * HD))
        d_keys = jnp.zeros(keys.shape, jnp.float32)
        d_values = jnp.zeros(keys.shape, jnp.float32)
        kept = allowed[...] > 0
        for g in range(head * group, (head + 1) * group):
            columns = slice(g * HD, (g + 1) * HD)
            query, grad = queries[:, columns], d_out[:, columns]
            scores = (
                lax.dot_general(keys, query, across, preferred_element_type=jnp.float32) * factor
            )
            scores = jnp.where(kept, scores, -1e30)
            weights = jnp.exp(scores - jnp.max(scores, axis=0, keepdims=True))
            probs = weights / jnp.sum(weights, axis=0, keepdims=True)
            probs_low = probs.astype(jnp.bfloat16)
            d_probs = lax.dot_general(values, grad, across, preferred_element_type=jnp.float32)
            rowdot = jnp.sum(probs_low.astype(jnp.float32) * d_probs, axis=0, keepdims=True)
            d_scores = (probs * (d_probs - rowdot) * factor).astype(jnp.bfloat16)
            d_queries[:, columns] = lax.dot_general(
                d_scores, keys, (((0,), (0,)), ((), ())), preferred_element_type=jnp.float32
            ).astype(jnp.bfloat16)
            d_keys = d_keys + jnp.dot(d_scores, query, preferred_element_type=jnp.float32)
            d_values = d_values + jnp.dot(probs_low, grad, preferred_element_type=jnp.float32)
        d_projected[:, start : start + HD] = d_keys.astype(jnp.bfloat16)
        d_projected[:, start + HD : start + 2 * HD] = d_values.astype(jnp.bfloat16)


def attention_backward(projected, queries, d_out, allowed):
    return on_chip(
        attention_kernel,
        jnp.zeros((1,), jnp.int32),
        [projected, queries, d_out, allowed],
        [jax.ShapeDtypeStruct(a.shape, jnp.bfloat16) for a in (queries, projected)],
        12 * allowed.size * queries.shape[1],
        "attention",
    )


def weight_kernel(place, chunk_a, chunk_b, d_projected, *refs):
    *added, out_a, out_b = refs
    half = out_a.shape[2]
    for side, (chunk, out) in enumerate(((chunk_a, out_a), (chunk_b, out_b))):
        columns = d_projected[:, side * half : (side + 1) * half]
        total = jnp.dot(chunk[0], columns, preferred_element_type=jnp.float32)
        if added:
            total = total + added[side][0].astype(jnp.float32)
        out[0] = total.astype(out.dtype)


def weight_parts(held, d_projected, place, added, dtype, name):
    length, cols = d_projected.shape
    rows = held.shape[1] // 2
    half = cols // 2
    out = pl.BlockSpec((1, rows, half), lambda k, place: (k, 0, 0))
    shape = jax.ShapeDtypeStruct((2, rows, half), dtype)
    return pl.pallas_call(
        weight_kernel,
        grid_spec=pltpu.PrefetchScalarGridSpec(
            num_scalar_prefetch=1,
            grid=(2,),
            in_specs=[
                pl.BlockSpec((1, rows, length), lambda k, place: (place[k], place[4], 0)),
                pl.BlockSpec((1, rows, length), lambda k, place: (place[2 + k], place[4], 0)),
                pl.BlockSpec((length, cols), lambda k, place: (0, 0)),
            ]
            + [out] * len(added),
            out_specs=[out, out],
        ),
        out_shape=[shape, shape],
        cost_estimate=pl.CostEstimate(
            flops=4 * length * rows * cols, bytes_accessed=8 * rows * cols, transcendentals=0
        ),
        compiler_params=pltpu.CompilerParams(vmem_limit_bytes=VMEM_PART),
        name=name,
    )(place, held, held, d_projected, *added)


def combine_kernel(place, keep_a, got_a, keep_b, got_b, out_a, out_b):
    sides = ((keep_a, got_a, out_a), (keep_b, got_b, out_b))
    for side, (keep, got, out) in enumerate(sides):
        which = place[side]
        out[...] = (keep[which] + got[which].astype(jnp.float32)).astype(out.dtype)


def finish_kernel(place, keep_a, got_a, keep_b, got_b, last_a, last_b, out):
    half = last_a.shape[1]
    sides = ((keep_a, got_a, last_a), (keep_b, got_b, last_b))
    for side, (keep, got, last) in enumerate(sides):
        which = place[side]
        total = keep[which] + got[which].astype(jnp.float32) + last[...].astype(jnp.float32)
        out[:, side * half : (side + 1) * half] = total


def plane():
    index = lax.axis_index("dp").astype(jnp.int32)

    def swap(value, bit):
        return lax.ppermute(value, "dp", [(i, i ^ bit) for i in range(8)])

    return index % 2, (index // 2) % 2, index // 4, swap


def weight_sum(held, d_projected):
    core, x, y, swap = plane()
    rows, cols = held.shape[1] // 2, d_projected.shape[1]
    send = [1 - x, 3 - x, 2 - 2 * y, 3 - 2 * y]
    keep = [x, 2 + x, 2 * y, 2 * y + 1]

    def parts(chunks, which, added, dtype, name):
        place = jnp.stack(chunks + [which])
        return weight_parts(held, d_projected, place, added, dtype, name)

    theirs = parts(send, 1 - core, [], jnp.bfloat16, "weight_send_other")
    theirs = [swap(part, 1) for part in theirs]
    rest = parts(keep, 1 - core, [], jnp.bfloat16, "weight_keep_other")
    rest = [swap(part, 1) for part in rest]
    send_a, send_b = parts(send, core, theirs, jnp.bfloat16, "weight_send")
    got_a, got_b = swap(send_a, 2), swap(send_b, 4)
    keep_a, keep_b = parts(keep, core, rest, jnp.float32, "weight_keep")

    small = jax.ShapeDtypeStruct((rows, cols // 2), jnp.bfloat16)
    arrays = [keep_a, got_a, keep_b, got_b]
    last_a, last_b = on_chip(
        combine_kernel, jnp.stack([1 - y, 1 - x]), arrays, [small] * 2, cols * rows, "weight_combine"
    )
    last = [swap(last_a, 4), swap(last_b, 2)]

    def finish(ready):
        ended, ready = lax.optimization_barrier((last, ready))
        (total,) = on_chip(
            finish_kernel,
            jnp.stack([y, x]),
            arrays + ended,
            [jax.ShapeDtypeStruct((rows, cols), jnp.float32)],
            2 * cols * rows,
            "weight_finish",
        )
        return total, ready

    return finish


def gather_plane(own_cache, own_rows):
    _, _, _, swap = plane()
    cache, rows = {0: own_cache}, {0: own_rows}
    for bit in (2, 4):
        cache[bit] = swap(own_cache, bit)
        rows[bit] = swap(own_rows, bit)
    cache[6] = swap(cache[4], 2)
    rows[6] = swap(rows[2], 4)
    for bits in (0, 2, 4, 6):
        cache[bits + 1] = swap(cache[bits], 1)
        rows[bits + 1] = swap(rows[bits], 1)
    return [cache[k] for k in range(8)], [rows[k] for k in range(8)]


def place_rows_kernel(place, *refs):
    *pieces, out, sems = refs
    height = pieces[0].shape[0]
    copies = []
    for k, piece in enumerate(pieces):
        start = pl.multiple_of((place[0] ^ k) * height, height)
        copies.append(
            pltpu.make_async_copy(piece, out.at[pl.ds(start, height), :], sems.at[k])
        )
    for copy in copies:
        copy.start()
    for copy in copies:
        copy.wait()


def place_rows(pieces):
    height, cols = pieces[0].shape
    anywhere = pl.BlockSpec(memory_space=pl.ANY)
    return pl.pallas_call(
        place_rows_kernel,
        in_specs=[pl.BlockSpec(memory_space=pltpu.SMEM)] + [anywhere] * len(pieces),
        out_specs=anywhere,
        out_shape=jax.ShapeDtypeStruct((height * len(pieces), cols), pieces[0].dtype),
        scratch_shapes=[pltpu.SemaphoreType.DMA((len(pieces),))],
        cost_estimate=pl.CostEstimate(
            flops=0, bytes_accessed=4 * height * cols * len(pieces), transcendentals=0
        ),
        compiler_params=pltpu.CompilerParams(vmem_limit_bytes=VMEM_WHOLE),
        name="place_rows",
    )(lax.axis_index("dp").astype(jnp.int32).reshape(1), *pieces)


def input_kernel(place, *refs):
    *arrays, out = refs
    n_blocks = place.shape[0] - 1
    pieces, rows = arrays[:n_blocks], arrays[n_blocks:]
    share = rows[0].shape[0] // n_blocks
    for k, held in enumerate(rows):
        total = jnp.zeros((out.shape[0], share), jnp.float32)
        for s, piece in enumerate(pieces):
            total = total + lax.dot_general(
                piece[...],
                held[s * share : (s + 1) * share, :],
                (((1,), (1,)), ((), ())),
                preferred_element_type=jnp.float32,
            )
        start = pl.multiple_of((place[0] ^ k) * share, share)
        out[:, pl.ds(start, share)] = total.astype(out.dtype)


def input_gradient(pieces, rows):
    length, cols = pieces[0].shape
    feats = sum(held.shape[0] for held in rows) // len(pieces)
    place = jnp.broadcast_to(lax.axis_index("dp").astype(jnp.int32), (len(pieces) + 1,))
    (d_tokens,) = on_chip(
        input_kernel,
        place,
        pieces + rows,
        [jax.ShapeDtypeStruct((length, feats), jnp.bfloat16)],
        2 * length * feats * cols * len(pieces),
        "input_gradient",
    )
    return d_tokens


def make_body(n_dp, n_z):
    ring = [[(z, (z + s) % n_z) for z in range(n_z)] for s in range(n_z)]
    tuned = n_dp == 8 and n_z == 4

    def body(tokens, queries, d_out, segments, cached, master, moment, second, grad):
        me_dp = lax.axis_index("dp").astype(jnp.int32)
        me_z = lax.axis_index("tensor").astype(jnp.int32)
        length, feats = tokens.shape
        cols = cached.shape[1]

        share = feats // n_dp

        def block_for(z):
            return lax.dynamic_slice_in_dim(cached, z * feats + me_dp * share, share, 0)

        blocks = [block_for(me_z)]
        for s in range(1, n_z):
            blocks.append(lax.ppermute(block_for((me_z + s) % n_z), "tensor", ring[s]))
        own_rows = jnp.concatenate(blocks, axis=0)

        master_new, moment_new, second_new, own_cache = optimizer(
            cached, master, moment, second, grad
        )

        total = jnp.zeros((length, cols), jnp.float32)
        total, held = absorb(tokens, me_z, cached, total, None, n_z)
        from_low, from_high, merged = tokens, tokens, None
        for s in range(1, n_z):
            up = [(z, z + 1) for z in range(s - 1, n_z - 1)]
            down = [(z + 1, z) for z in range(n_z - s)]
            low, high = me_z - s, me_z + s
            if merged is None:
                from_low = lax.ppermute(from_low, "tensor", up)
                from_high = lax.ppermute(from_high, "tensor", down)
            else:
                merged = lax.ppermute(merged, "tensor", up + down)
            if s == 1:
                from_low, from_high, own_cache, own_rows = lax.optimization_barrier(
                    (from_low, from_high, own_cache, own_rows)
                )
            if merged is None and 2 * s >= n_z:
                merged = jnp.where(me_z >= s, from_low, from_high)
            if merged is None:
                total, held = absorb(from_low, low, cached, total, held, n_z)
                total, held = absorb(from_high, high, cached, total, held, n_z)
            else:
                origin = jnp.where(me_z >= s, low, high)
                total, held = absorb(merged, origin, cached, total, held, n_z)

        doc_ids = segments[0]
        position = jnp.arange(length)
        allowed = (doc_ids[:, None] == doc_ids[None, :]) & (position[:, None] <= position[None, :])
        allowed = allowed.astype(jnp.float32)

        if tuned:
            cache_pieces, row_pieces = gather_plane(own_cache, own_rows)
            new_cache = place_rows(cache_pieces)
            total, new_cache, row_pieces = lax.optimization_barrier((total, new_cache, row_pieces))
        else:
            new_cache = lax.all_gather(own_cache, "dp", axis=0, tiled=True)
            row_pieces = lax.all_gather(own_rows, "dp", axis=0)

        d_queries, d_projected = attention_backward(
            total.astype(jnp.bfloat16), queries, d_out, allowed
        )

        pieces = [d_projected] + [
            lax.ppermute(d_projected, "tensor", ring[s]) for s in range(1, n_z)
        ]
        if tuned:
            finish = weight_sum(held, d_projected)
            new_grad, d_tokens = finish(input_gradient(pieces, row_pieces))
        else:
            rows = row_pieces.reshape(n_dp, n_z, share, cols)
            d_tokens = jnp.einsum(
                "slc,ksfc->lkf", jnp.stack(pieces), rows, preferred_element_type=jnp.float32
            )
            d_tokens = d_tokens.astype(jnp.bfloat16).reshape(length, feats)
            partial = lax.dot_general(
                held[:n_z].reshape(n_z * feats, length),
                d_projected,
                (((1,), (0,)), ((), ())),
                preferred_element_type=jnp.float32,
            )
            new_grad = lax.psum_scatter(
                partial.astype(jnp.bfloat16), "dp", scatter_dimension=0, tiled=True
            ).astype(jnp.float32)
        return (master_new, moment_new, second_new, new_cache, new_grad, d_queries, d_tokens)

    return body


def solution(mesh):
    in_specs = (
        P("dp", "tensor"),
        P("dp", "tensor"),
        P("dp", "tensor"),
        P("dp", None),
        P(None, "tensor"),
        P("dp", "tensor"),
        P("dp", "tensor"),
        P("dp", "tensor"),
        P("dp", "tensor"),
    )
    out_specs = (
        P("dp", "tensor"),
        P("dp", "tensor"),
        P("dp", "tensor"),
        P(None, "tensor"),
        P("dp", "tensor"),
        P("dp", "tensor"),
        P("dp", "tensor"),
    )
    body = make_body(mesh.shape["dp"], mesh.shape["tensor"])
    return jax.shard_map(body, mesh=mesh, in_specs=in_specs, out_specs=out_specs, check_vma=False)
```

time: 172 us -> 265 us (1.54)
  Pallas kernels: 16.2 us -> 148 us
  matrix products: 15.5 us -> 0 us
  between operations: 14.5 us -> 1.22 us
  local copies, waits for them, and re-layouts: 22.8 us -> 12.3 us
  starting transfers between devices: 28.3 us -> 38.3 us
  other arithmetic: 11.2 us -> 1.94 us
    pallas_call x0 -> x10, Pallas kernels: none -> 134 us  [the longest x1 112 us: place_rows(): pl.pallas_call(place_rows_kernel, in_specs=[pl.BlockSpec(memory_space=plt...]
    ppermute x8 -> x22, waiting for transfers between devices: 7.67 us -> 34 us  [swap(): return lax.ppermute(value, 'dp', [(i, i ^ bit) for i in range(8)])]
    ppermute x2, waiting for transfers between devices: 22.1 us -> 0.01 us  [body(): from_high = lax.ppermute(from_high, 'tensor', down)]
    ppermute x3, waiting for transfers between devices: 4.66 us -> 23.4 us  [body(): blocks.append(lax.ppermute(block_for((me_z + s) % n_z), 'tensor', ring[s]))]
    ppermute x1, waiting for transfers between devices: 17.8 us -> 0.01 us  [body(): merged = lax.ppermute(merged, 'tensor', up + down)]
    dot_general x12 -> x0, matrix products: 15.5 us -> none  [the longest x5 7.98 us: part(): return jnp.dot(chunk, rows, preferred_element_type=jnp.float32)]
    ppermute x2, waiting for transfers between devices: 10.4 us -> 0.01 us  [body(): from_low = lax.ppermute(from_low, 'tensor', up)]
    ppermute x8 -> x22, starting transfers between devices: 7.1 us -> 13.5 us  [swap(): return lax.ppermute(value, 'dp', [(i, i ^ bit) for i in range(8)])]
  transfers between devices with their start and end apart: 21 -> 33, of which waited for: 9 -> 11; matrix products, arithmetic and copies ran while one was open for 21% -> 1% of each run, Pallas kernels for 8% -> 53%
where the time goes in v4:
time: 265 us
  Pallas kernels  148 us (56%)
  waiting for transfers between devices  62.8 us (24%)
  starting transfers between devices  38.3 us (14%)
  local copies, waits for them, and re-layouts  12.3 us (5%)
    pallas_call x1, Pallas kernels, place_rows(): pl.pallas_call(place_rows_kernel, in_specs=[pl.BlockSpec(memory_space=plt...  112 us
    ppermute x22, waiting for transfers between devices, swap(): return lax.ppermute(value, 'dp', [(i, i ^ bit) for i in range(8)])  34 us
    ppermute x3, waiting for transfers between devices, body(): blocks.append(lax.ppermute(block_for((me_z + s) % n_z), 'tensor', ring[s]))  23.4 us
    ppermute x22, starting transfers between devices, swap(): return lax.ppermute(value, 'dp', [(i, i ^ bit) for i in range(8)])  13.5 us
    pallas_call x5, Pallas kernels, absorb(): pl.pallas_call(kernel, grid_spec=pltpu.PrefetchScalarGridSpec(num_scalar_...  11.5 us
    unnamed x48, local copies, waits for them, and re-layouts  10.8 us
    pallas_call x4, Pallas kernels, on_chip(): pl.pallas_call(kernel, in_specs=[pl.BlockSpec(memory_space=pltpu.SMEM)] +...  9.86 us
    pallas_call x4, Pallas kernels, weight_parts(): pl.pallas_call(weight_kernel, grid_spec=pltpu.PrefetchScalarGridSpec(num_...  9.35 us
  transfers between devices with their start and end apart: 33, of which 11 were waited for; matrix products, arithmetic and copies ran while one was open for 1% of the time, Pallas kernels for 53%

profile of v4, /device:TPU:0, one launch (start us, length us, event | category | flops | bytes accessed | tf_op | source)
XLA Modules:
  0.0 264.7 jit_solution(16437819310876614187)
XLA Ops:
  0.6 6.0 %collective-permute-start = (bf16[256,2048]{1,0:T(8,128)(2,1)}, bf16[256,2048]{1,0:T(8,128)(2,1)}, u32[]{:S(2)}, u32[]{:S(2)}) collective-permute-start(bf16[256,2048]{1,0:T(8,128)(2,1)} %chunk.1), channel_id=1, source_target_pairs={{0,1},{1,2},{2,3},{4,5},{5,6},{6,7},{8,9},{9,10},{10,11},{12,13},{... | collective-permute-start | bytes 3145736 | tf_op jit(solution)/shard_map/ppermute | solution.py:395
  6.6 1.3 collective-permute-start.1
  7.9 1.1 constant_dynamic-slice_fusion.3
  9.1 2.7 %collective-permute-start.2 = (bf16[256,256]{1,0:T(8,128)(2,1)S(1)}, bf16[256,256]{1,0:T(8,128)(2,1)S(1)}, u32[]{:S(2)}, u32[]{:S(2)}) collective-permute-start(bf16[256,256]{1,0:T(8,128)(2,1)S(1)} %get-tuple-element.96), channel_id=1, source_target_pairs={{0,1},{1,2},{2,3},{3,0},{4,5},{5,6},{6,7},{7,4},{8,9},{9,10},{10,1... | collective-permute-start | bytes 393224 | tf_op jit(solution)/shard_map/ppermute | solution.py:380
  11.8 1.6 collective-permute-start.3
  13.4 1.3 collective-permute-start.4
  14.7 5.0 %optimizer.1 = (f32[1024,256]{1,0:T(8,128)}, f32[1024,256]{1,0:T(8,128)}, f32[1024,256]{1,0:T(8,128)}, bf16[1024,256]{1,0:T(8,128)(2,1)}) custom-call(s32[1]{0:T(128)} %bitcast.place, bf16[8192,256]{1,0:T(8,128)(2,1)} %cached.11, f32[1024,256]{1,0:T(8,128)} %master.1, f32[1024,256]{1,0:T(8,128)} %moment.1, f32[1024,256]{1,0:T(8,128)} %second.1, f32[1024,256]{1,0:T(8,128)} %grad.1), custom_call_target="tpu_custom_call" | custom-call | flops 10485760 | bytes 8388608 | tf_op jit(solution)/shard_map/optimizer/pallas_call | solution.py:51
  19.7 18.9 %collective-permute-done.2 = bf16[256,256]{1,0:T(8,128)(2,1)S(1)} collective-permute-done((bf16[256,256]{1,0:T(8,128)(2,1)S(1)}, bf16[256,256]{1,0:T(8,128)(2,1)S(1)}, u32[]{:S(2)}, u32[]{:S(2)}) %collective-permute-start.2) | collective-permute-done | bytes 131104 | tf_op jit(solution)/shard_map/ppermute | solution.py:380
  38.7 4.5 %collective-permute-done.3 = bf16[256,256]{1,0:T(8,128)(2,1)S(1)} collective-permute-done((bf16[256,256]{1,0:T(8,128)(2,1)S(1)}, bf16[256,256]{1,0:T(8,128)(2,1)S(1)}, u32[]{:S(2)}, u32[]{:S(2)}) %collective-permute-start.3) | collective-permute-done | bytes 131104 | tf_op jit(solution)/shard_map/ppermute | solution.py:380
  43.2 1.6 collective-permute-start.11
  44.8 1.5 collective-permute-start.9
  46.3 1.7 collective-permute-start.5
  47.9 1.3 collective-permute-start.6
  49.2 1.0 copy-done.5
  50.2 3.0 %collective-permute-done.11.refs_4_ = bf16[1024,256]{1,0:T(8,128)(2,1)} collective-permute-done((bf16[1024,256]{1,0:T(8,128)(2,1)}, bf16[1024,256]{1,0:T(8,128)(2,1)}, u32[]{:S(2)}, u32[]{:S(2)}) %collective-permute-start.11) | collective-permute-done | bytes 524320 | tf_op jit(solution)/shard_map/ppermute | solution.py:239
  53.2 1.5 collective-permute-start.16
  55.4 2.5 collective-permute-start.13
  58.3 9.7 %collective-permute-done.16.refs_6_ = bf16[1024,256]{1,0:T(8,128)(2,1)S(1)} collective-permute-done((bf16[1024,256]{1,0:T(8,128)(2,1)S(1)}, bf16[1024,256]{1,0:T(8,128)(2,1)S(1)}, u32[]{:S(2)}, u32[]{:S(2)}) %collective-permute-start.16) | collective-permute-done | bytes 524320 | tf_op jit(solution)/shard_map/ppermute | solution.py:239
  68.1 8.8 %collective-permute-done.13.refs_6_ = bf16[1024,256]{1,0:T(8,128)(2,1)} collective-permute-done((bf16[1024,256]{1,0:T(8,128)(2,1)}, bf16[1024,256]{1,0:T(8,128)(2,1)}, u32[]{:S(2)}, u32[]{:S(2)}) %collective-permute-start.13) | collective-permute-done | bytes 524320 | tf_op jit(solution)/shard_map/ppermute | solution.py:239
  77.6 1.3 broadcast_select_fusion.chunk
  79.0 0.8 copy-done.7
  79.8 1.3 collective-permute-start.7
  81.4 2.2 copy-done.3
  83.6 1.7 absorb.5
  85.9 5.5 %collective-permute-done.20.refs_10_ = bf16[1024,256]{1,0:T(8,128)(2,1)} collective-permute-done((bf16[1024,256]{1,0:T(8,128)(2,1)S(1)}, bf16[1024,256]{1,0:T(8,128)(2,1)}, u32[]{:S(2)}, u32[]{:S(2)}) %collective-permute-start.20) | collective-permute-done | bytes 524320 | tf_op jit(solution)/shard_map/ppermute | solution.py:239
  92.1 3.2 %absorb.6 = (f32[256,256]{1,0:T(8,128)S(1)}, bf16[5,2048,256]{2,1,0:T(8,128)(2,1)S(1)}) custom-call(s32[2]{0:T(128)S(1)} %get-tuple-element.98.place, bf16[256,2048]{1,0:T(8,128)(2,1)} %collective-permute-done.chunk, bf16[8192,256]{1,0:T(8,128)(2,1)S(1)} %copy-done.3, f32[256,256]{1,0:T(8,128)S(1)} %get-tuple-element.56.total, ...), custom_call_target="tpu_custom_call", output_to_operand_aliasing={{1}: (4, {})} | custom-call | flops 268435456 | bytes 3145728 | tf_op jit(solution)/shard_map/absorb/pallas_call | solution.py:108
  95.4 1.7 absorb.7
  97.1 1.7 absorb.8
  98.8 112.4 %place_rows.1 = bf16[8192,256]{1,0:T(8,128)(2,1)} custom-call(s32[1]{0:T(128)} %bitcast.place, bf16[1024,256]{1,0:T(8,128)(2,1)S(1)} %copy-done.10, bf16[1024,256]{1,0:T(8,128)(2,1)} %collective-permute-done.8.refs_1_, bf16[1024,256]{1,0:T(8,128)(2,1)} %collective-permute-done.9.refs_2_, bf16[1024,256]{1,0:T(8,128)(2,1)} %collective-permute-done.10.refs_3_, ...), custom_call_target="tpu_custom_call" | custom-call | bytes 8388608 | tf_op jit(solution)/shard_map/place_rows/pallas_call | solution.py:316
  211.2 3.2 %absorb.9 = (f32[256,256]{1,0:T(8,128)S(1)}, bf16[5,2048,256]{2,1,0:T(8,128)(2,1)S(1)}) custom-call(s32[2]{0:T(128)S(1)} %pad_add_fusion.place, bf16[256,2048]{1,0:T(8,128)(2,1)} %collective-permute-done.7.chunk, bf16[8192,256]{1,0:T(8,128)(2,1)S(1)} %copy-done.3, f32[256,256]{1,0:T(8,128)S(1)} %get-tuple-element.62.total, ...), custom_call_target="tpu_custom_call", output_to_operand_aliasing={{1}: (4, {})} | custom-call | flops 268435456 | bytes 3145728 | tf_op jit(solution)/shard_map/absorb/pallas_call | solution.py:108
  214.6 4.2 %attention.1 = (bf16[256,1024]{1,0:T(8,128)(2,1)}, bf16[256,256]{1,0:T(8,128)(2,1)S(1)}) custom-call(s32[1]{0:T(128)} %constant.80.clone.1.place, bf16[256,256]{1,0:T(8,128)(2,1)S(1)} %convert_element_type.6.projected, bf16[256,1024]{1,0:T(8,128)(2,1)S(1)} %copy-done.21, bf16[256,1024]{1,0:T(8,128)(2,1)S(1)} %copy-done.22, f32[256,256]{1,0:T(8,128)S(1)} %fusion.1.allowed), custom_call_target="tpu_custom_call" | custom-call | flops 805306368 | bytes 2097152 | tf_op jit(solution)/shard_map/attention/pallas_call | solution.py:73
  218.8 2.3 weight_send_other.1
  221.8 2.5 copy-done.1
  224.3 2.2 weight_keep_other.1
  227.0 2.3 weight_send.1
  229.3 1.5 collective-permute-start.26
  231.5 0.8 copy-done.19
  232.3 2.5 copy-done.2
  234.7 1.0 copy-done.20
  235.8 2.6 weight_keep.1
  238.4 5.0 %collective-permute-done.26.got_a = bf16[2,1024,128]{2,1,0:T(8,128)(2,1)S(1)} collective-permute-done((bf16[2,1024,128]{2,1,0:T(8,128)(2,1)}, bf16[2,1024,128]{2,1,0:T(8,128)(2,1)S(1)}, u32[]{:S(2)}, u32[]{:S(2)}) %collective-permute-start.26) | collective-permute-done | bytes 524320 | tf_op jit(solution)/shard_map/ppermute | solution.py:239
  243.4 1.2 collective-permute-done.27.got_b
  246.4 4.5 %collective-permute-start.30 = (bf16[256,256]{1,0:T(8,128)(2,1)S(1)}, bf16[256,256]{1,0:T(8,128)(2,1)S(1)}, u32[]{:S(2)}, u32[]{:S(2)}) collective-permute-start(bf16[256,256]{1,0:T(8,128)(2,1)S(1)} %get-tuple-element.70.d_projected.refs_0_), channel_id=1, source_target_pairs={{0,1},{1,2},{2,3},{3,0},{4,5},{5,6},{6,7},{7,4},{8,9},{9,10},{10,1... | collective-permute-start | bytes 393224 | tf_op jit(solution)/shard_map/ppermute | solution.py:430
  251.3 2.8 %collective-permute-start.32 = (bf16[256,256]{1,0:T(8,128)(2,1)S(1)}, bf16[256,256]{1,0:T(8,128)(2,1)S(1)}, u32[]{:S(2)}, u32[]{:S(2)}) collective-permute-start(bf16[256,256]{1,0:T(8,128)(2,1)S(1)} %get-tuple-element.70.d_projected.refs_0_), channel_id=1, source_target_pairs={{0,3},{1,0},{2,1},{3,2},{4,7},{5,4},{6,5},{7,6},{8,11},{9,8},{10,9... | collective-permute-start | bytes 393224 | tf_op jit(solution)/shard_map/ppermute | solution.py:430
  254.2 0.7 collective-permute-done.30.refs_1_
  254.9 4.7 %collective-permute-done.31.refs_2_ = bf16[256,256]{1,0:T(8,128)(2,1)S(1)} collective-permute-done((bf16[256,256]{1,0:T(8,128)(2,1)S(1)}, bf16[256,256]{1,0:T(8,128)(2,1)S(1)}, u32[]{:S(2)}, u32[]{:S(2)}) %collective-permute-start.31) | collective-permute-done | bytes 131104 | tf_op jit(solution)/shard_map/ppermute | solution.py:430
  259.7 3.4 %input_gradient.1 = bf16[256,2048]{1,0:T(8,128)(2,1)} custom-call(s32[5]{0:T(128)S(1)} %broadcast_in_dim.9.place, bf16[256,256]{1,0:T(8,128)(2,1)S(1)} %get-tuple-element.70.d_projected.refs_0_, bf16[256,256]{1,0:T(8,128)(2,1)S(1)} %collective-permute-done.30.refs_1_, bf16[256,256]{1,0:T(8,128)(2,1)S(1)} %collective-permute-done.31.refs_2_, ...), custom_call_target="tpu_custom_call" | custom-call | flops 1073741824 | bytes 5767168 | tf_op jit(solution)/shard_map/input_gradient/pallas_call | solution.py:73
  263.0 1.7 weight_finish.1
  (98 shorter events, 7.8 us)
Async XLA Ops:
  0.6 42.6 %collective-permute-start = (bf16[256,2048]{1,0:T(8,128)(2,1)}, bf16[256,2048]{1,0:T(8,128)(2,1)}, u32[]{:S(2)}, u32[]{:S(2)}) collective-permute-start(bf16[256,2048]{1,0:T(8,128)(2,1)} %chunk.1), channel_id=1, source_target_pairs={{0,1},{1,2},{2,3},{4,5},{5,6},{6,7},{8,9},{9,10},{10,11},{12,13},{... | collective-permute-start | bytes 3145736 | tf_op jit(solution)/shard_map/ppermute | solution.py:395
  6.6 36.6 %collective-permute-start.1 = (bf16[256,2048]{1,0:T(8,128)(2,1)}, bf16[256,2048]{1,0:T(8,128)(2,1)S(1)}, u32[]{:S(2)}, u32[]{:S(2)}) collective-permute-start(bf16[256,2048]{1,0:T(8,128)(2,1)} %chunk.1), channel_id=1, source_target_pairs={{1,0},{2,1},{3,2},{5,4},{6,5},{7,6},{9,8},{10,9},{11,10},{13,12},{... | collective-permute-start | bytes 3145736 | tf_op jit(solution)/shard_map/ppermute | solution.py:396
  9.1 29.6 %collective-permute-start.2 = (bf16[256,256]{1,0:T(8,128)(2,1)S(1)}, bf16[256,256]{1,0:T(8,128)(2,1)S(1)}, u32[]{:S(2)}, u32[]{:S(2)}) collective-permute-start(bf16[256,256]{1,0:T(8,128)(2,1)S(1)} %get-tuple-element.96), channel_id=1, source_target_pairs={{0,1},{1,2},{2,3},{3,0},{4,5},{5,6},{6,7},{7,4},{8,9},{9,10},{10,1... | collective-permute-start | bytes 393224 | tf_op jit(solution)/shard_map/ppermute | solution.py:380
  11.8 31.4 %collective-permute-start.3 = (bf16[256,256]{1,0:T(8,128)(2,1)S(1)}, bf16[256,256]{1,0:T(8,128)(2,1)S(1)}, u32[]{:S(2)}, u32[]{:S(2)}) collective-permute-start(bf16[256,256]{1,0:T(8,128)(2,1)S(1)} %get-tuple-element.95), channel_id=1, source_target_pairs={{0,2},{1,3},{2,0},{3,1},{4,6},{5,7},{6,4},{7,5},{8,10},{9,11},{10,... | collective-permute-start | bytes 393224 | tf_op jit(solution)/shard_map/ppermute | solution.py:380
  13.4 29.7 %collective-permute-start.4 = (bf16[256,256]{1,0:T(8,128)(2,1)S(1)}, bf16[256,256]{1,0:T(8,128)(2,1)S(1)}, u32[]{:S(2)}, u32[]{:S(2)}) collective-permute-start(bf16[256,256]{1,0:T(8,128)(2,1)S(1)} %get-tuple-element.94), channel_id=1, source_target_pairs={{0,3},{1,0},{2,1},{3,2},{4,7},{5,4},{6,5},{7,6},{8,11},{9,8},{10,9... | collective-permute-start | bytes 393224 | tf_op jit(solution)/shard_map/ppermute | solution.py:380
  14.7 66.7 %copy-start.4 = (bf16[256,2048]{1,0:T(8,128)(2,1)S(1)}, bf16[256,2048]{1,0:T(8,128)(2,1)}, u32[]{:S(2)}) copy-start(bf16[256,2048]{1,0:T(8,128)(2,1)} %chunk.1) | copy-start | bytes 3145732
  19.7 72.3 %copy-start.23 = (s32[1,256]{1,0:T(1,128)S(1)}, s32[1,256]{1,0:T(1,128)}, u32[]{:S(2)}) copy-start(s32[1,256]{1,0:T(1,128)} %param.12) | copy-start | bytes 3076
  43.2 10.0 %collective-permute-start.11 = (bf16[1024,256]{1,0:T(8,128)(2,1)}, bf16[1024,256]{1,0:T(8,128)(2,1)}, u32[]{:S(2)}, u32[]{:S(2)}) collective-permute-start(bf16[1024,256]{1,0:T(8,128)(2,1)} %get-tuple-element.65.refs_0_), channel_id=1, source_target_pairs={{0,16},{4,20},{8,24},{12,28},{16,0},{20,4},{24,8},{28,12},{1,17},{... | collective-permute-start | bytes 1572872 | tf_op jit(solution)/shard_map/ppermute | solution.py:239
  44.8 10.6 %collective-permute-start.9 = (bf16[1024,256]{1,0:T(8,128)(2,1)}, bf16[1024,256]{1,0:T(8,128)(2,1)}, u32[]{:S(2)}, u32[]{:S(2)}) collective-permute-start(bf16[1024,256]{1,0:T(8,128)(2,1)} %get-tuple-element.65.refs_0_), channel_id=1, source_target_pairs={{0,8},{4,12},{8,0},{12,4},{16,24},{20,28},{24,16},{28,20},{1,9},{5... | collective-permute-start | bytes 1572872 | tf_op jit(solution)/shard_map/ppermute | solution.py:239
  46.3 30.6 %collective-permute-start.5 = (bf16[256,2048]{1,0:T(8,128)(2,1)}, bf16[256,2048]{1,0:T(8,128)(2,1)}, u32[]{:S(2)}, u32[]{:S(2)}) collective-permute-start(bf16[256,2048]{1,0:T(8,128)(2,1)} %collective-permute-done.chunk), channel_id=1, source_target_pairs={{1,2},{2,3},{5,6},{6,7},{9,10},{10,11},{13,14},{14,15},{17,18},{18... | collective-permute-start | bytes 3145736 | tf_op jit(solution)/shard_map/ppermute | solution.py:395
  47.9 29.5 %collective-permute-start.6 = (bf16[256,2048]{1,0:T(8,128)(2,1)S(1)}, bf16[256,2048]{1,0:T(8,128)(2,1)}, u32[]{:S(2)}, u32[]{:S(2)}) collective-permute-start(bf16[256,2048]{1,0:T(8,128)(2,1)S(1)} %collective-permute-done.1.chunk), channel_id=1, source_target_pairs={{1,0},{2,1},{5,4},{6,5},{9,8},{10,9},{13,12},{14,13},{17,16},{18,1... | collective-permute-start | bytes 3145736 | tf_op jit(solution)/shard_map/ppermute | solution.py:396
  50.2 7.6 %collective-permute-start.8 = (bf16[1024,256]{1,0:T(8,128)(2,1)}, bf16[1024,256]{1,0:T(8,128)(2,1)}, u32[]{:S(2)}, u32[]{:S(2)}) collective-permute-start(bf16[1024,256]{1,0:T(8,128)(2,1)} %get-tuple-element.65.refs_0_), channel_id=1, source_target_pairs={{0,4},{4,0},{8,12},{12,8},{16,20},{20,16},{24,28},{28,24},{1,5},{5... | collective-permute-start | bytes 1572872 | tf_op jit(solution)/shard_map/ppermute | solution.py:239
  53.2 14.9 %collective-permute-start.16 = (bf16[1024,256]{1,0:T(8,128)(2,1)S(1)}, bf16[1024,256]{1,0:T(8,128)(2,1)S(1)}, u32[]{:S(2)}, u32[]{:S(2)}) collective-permute-start(bf16[1024,256]{1,0:T(8,128)(2,1)S(1)} %pad_maximum_fusion.refs_4_), channel_id=1, source_target_pairs={{0,8},{4,12},{8,0},{12,4},{16,24},{20,28},{24,16},{28,20},{1,9},{5... | collective-permute-start | bytes 1572872 | tf_op jit(solution)/shard_map/ppermute | solution.py:239
  55.4 21.5 %collective-permute-start.13 = (bf16[1024,256]{1,0:T(8,128)(2,1)}, bf16[1024,256]{1,0:T(8,128)(2,1)}, u32[]{:S(2)}, u32[]{:S(2)}) collective-permute-start(bf16[1024,256]{1,0:T(8,128)(2,1)} %collective-permute-done.11.refs_4_), channel_id=1, source_target_pairs={{0,8},{4,12},{8,0},{12,4},{16,24},{20,28},{24,16},{28,20},{1,9},{5... | collective-permute-start | bytes 1572872 | tf_op jit(solution)/shard_map/ppermute | solution.py:239
  57.8 21.2 %collective-permute-start.18 = (bf16[1024,256]{1,0:T(8,128)(2,1)S(1)}, bf16[1024,256]{1,0:T(8,128)(2,1)S(1)}, u32[]{:S(2)}, u32[]{:S(2)}) collective-permute-start(bf16[1024,256]{1,0:T(8,128)(2,1)S(1)} %pad_maximum_fusion.refs_4_), channel_id=1, source_target_pairs={{0,16},{4,20},{8,24},{12,28},{16,0},{20,4},{24,8},{28,12},{1,17},{... | collective-permute-start | bytes 1572872 | tf_op jit(solution)/shard_map/ppermute | solution.py:239
  68.0 17.6 %collective-permute-start.12 = (bf16[1024,256]{1,0:T(8,128)(2,1)}, bf16[1024,256]{1,0:T(8,128)(2,1)}, u32[]{:S(2)}, u32[]{:S(2)}) collective-permute-start(bf16[1024,256]{1,0:T(8,128)(2,1)} %collective-permute-done.11.refs_4_), channel_id=1, source_target_pairs={{0,4},{4,0},{8,12},{12,8},{16,20},{20,16},{24,28},{28,24},{1,5},{5... | collective-permute-start | bytes 1572872 | tf_op jit(solution)/shard_map/ppermute | solution.py:239
  76.9 8.4 %collective-permute-start.10 = (bf16[1024,256]{1,0:T(8,128)(2,1)}, bf16[1024,256]{1,0:T(8,128)(2,1)}, u32[]{:S(2)}, u32[]{:S(2)}) collective-permute-start(bf16[1024,256]{1,0:T(8,128)(2,1)} %collective-permute-done.9.refs_2_), channel_id=1, source_target_pairs={{0,4},{4,0},{8,12},{12,8},{16,20},{20,16},{24,28},{28,24},{1,5},{5... | collective-permute-start | bytes 1572872 | tf_op jit(solution)/shard_map/ppermute | solution.py:239
  76.9 14.4 %collective-permute-start.20 = (bf16[1024,256]{1,0:T(8,128)(2,1)S(1)}, bf16[1024,256]{1,0:T(8,128)(2,1)}, u32[]{:S(2)}, u32[]{:S(2)}) collective-permute-start(bf16[1024,256]{1,0:T(8,128)(2,1)S(1)} %collective-permute-done.16.refs_6_), channel_id=1, source_target_pairs={{0,16},{4,20},{8,24},{12,28},{16,0},{20,4},{24,8},{28,12},{1,17},{... | collective-permute-start | bytes 1572872 | tf_op jit(solution)/shard_map/ppermute | solution.py:239
  77.4 13.9 %collective-permute-start.14 = (bf16[1024,256]{1,0:T(8,128)(2,1)}, bf16[1024,256]{1,0:T(8,128)(2,1)}, u32[]{:S(2)}, u32[]{:S(2)}) collective-permute-start(bf16[1024,256]{1,0:T(8,128)(2,1)} %collective-permute-done.13.refs_6_), channel_id=1, source_target_pairs={{0,4},{4,0},{8,12},{12,8},{16,20},{20,16},{24,28},{28,24},{1,5},{5... | collective-permute-start | bytes 1572872 | tf_op jit(solution)/shard_map/ppermute | solution.py:239
  79.8 131.4 %collective-permute-start.7 = (bf16[256,2048]{1,0:T(8,128)(2,1)S(1)}, bf16[256,2048]{1,0:T(8,128)(2,1)}, u32[]{:S(2)}, u32[]{:S(2)}) collective-permute-start(bf16[256,2048]{1,0:T(8,128)(2,1)S(1)} %broadcast_select_fusion.chunk), channel_id=1, source_target_pairs={{2,3},{1,0},{6,7},{5,4},{10,11},{9,8},{14,15},{13,12},{18,19},{17,... | collective-permute-start | bytes 3145736 | tf_op jit(solution)/shard_map/ppermute | solution.py:398
  83.6 7.8 %copy-start.8 = (bf16[1024,256]{1,0:T(8,128)(2,1)S(1)}, bf16[1024,256]{1,0:T(8,128)(2,1)}, u32[]{:S(2)}) copy-start(bf16[1024,256]{1,0:T(8,128)(2,1)} %copy-done.7) | copy-start | bytes 1572868
  85.3 129.1 %collective-permute-start.15 = (bf16[1024,256]{1,0:T(8,128)(2,1)S(1)}, bf16[1024,256]{1,0:T(8,128)(2,1)S(1)}, u32[]{:S(2)}, u32[]{:S(2)}) collective-permute-start(bf16[1024,256]{1,0:T(8,128)(2,1)S(1)} %pad_maximum_fusion.refs_4_), channel_id=1, source_target_pairs={{0,4},{4,0},{8,12},{12,8},{16,20},{20,16},{24,28},{28,24},{1,5},{5... | collective-permute-start | bytes 1572872 | tf_op jit(solution)/shard_map/ppermute | solution.py:239
  85.7 128.8 %collective-permute-start.17 = (bf16[1024,256]{1,0:T(8,128)(2,1)S(1)}, bf16[1024,256]{1,0:T(8,128)(2,1)S(1)}, u32[]{:S(2)}, u32[]{:S(2)}) collective-permute-start(bf16[1024,256]{1,0:T(8,128)(2,1)S(1)} %collective-permute-done.16.refs_6_), channel_id=1, source_target_pairs={{0,4},{4,0},{8,12},{12,8},{16,20},{20,16},{24,28},{28,24},{1,5},{5... | collective-permute-start | bytes 1572872 | tf_op jit(solution)/shard_map/ppermute | solution.py:239
  91.3 123.2 %collective-permute-start.19 = (bf16[1024,256]{1,0:T(8,128)(2,1)S(1)}, bf16[1024,256]{1,0:T(8,128)(2,1)S(1)}, u32[]{:S(2)}, u32[]{:S(2)}) collective-permute-start(bf16[1024,256]{1,0:T(8,128)(2,1)S(1)} %copy-done.8), channel_id=1, source_target_pairs={{0,4},{4,0},{8,12},{12,8},{16,20},{20,16},{24,28},{28,24},{1,5},{5... | collective-permute-start | bytes 1572872 | tf_op jit(solution)/shard_map/ppermute | solution.py:239
  91.4 123.2 %collective-permute-start.21 = (bf16[1024,256]{1,0:T(8,128)(2,1)}, bf16[1024,256]{1,0:T(8,128)(2,1)S(1)}, u32[]{:S(2)}, u32[]{:S(2)}) collective-permute-start(bf16[1024,256]{1,0:T(8,128)(2,1)} %collective-permute-done.20.refs_10_), channel_id=1, source_target_pairs={{0,4},{4,0},{8,12},{12,8},{16,20},{20,16},{24,28},{28,24},{1,5},{5... | collective-permute-start | bytes 1572872 | tf_op jit(solution)/shard_map/ppermute | solution.py:239
  211.2 3.4 %copy-start.21 = (bf16[256,1024]{1,0:T(8,128)(2,1)S(1)}, bf16[256,1024]{1,0:T(8,128)(2,1)}, u32[]{:S(2)}) copy-start(bf16[256,1024]{1,0:T(8,128)(2,1)} %queries.1) | copy-start | bytes 1572868
  211.2 3.4 %copy-start.22 = (bf16[256,1024]{1,0:T(8,128)(2,1)S(1)}, bf16[256,1024]{1,0:T(8,128)(2,1)}, u32[]{:S(2)}) copy-start(bf16[256,1024]{1,0:T(8,128)(2,1)} %d_out.1) | copy-start | bytes 1572868
  214.5 6.6 %copy-start = (bf16[5,2048,256]{2,1,0:T(8,128)(2,1)}, bf16[5,2048,256]{2,1,0:T(8,128)(2,1)S(1)}, u32[]{:S(2)}) copy-start(bf16[5,2048,256]{2,1,0:T(8,128)(2,1)S(1)} %get-tuple-element.68.chunk_a.chunk_b) | copy-start | bytes 15728644
  214.5 6.6 %copy-start.11 = (bf16[1024,256]{1,0:T(8,128)(2,1)}, bf16[1024,256]{1,0:T(8,128)(2,1)S(1)}, u32[]{:S(2)}) copy-start(bf16[1024,256]{1,0:T(8,128)(2,1)S(1)} %collective-permute-done.15.refs_5_) | copy-start | bytes 1572868
  214.5 6.5 %copy-start.13 = (bf16[1024,256]{1,0:T(8,128)(2,1)}, bf16[1024,256]{1,0:T(8,128)(2,1)S(1)}, u32[]{:S(2)}) copy-start(bf16[1024,256]{1,0:T(8,128)(2,1)S(1)} %collective-permute-done.17.refs_7_) | copy-start | bytes 1572868
  214.5 6.5 %copy-start.15 = (bf16[1024,256]{1,0:T(8,128)(2,1)}, bf16[1024,256]{1,0:T(8,128)(2,1)S(1)}, u32[]{:S(2)}) copy-start(bf16[1024,256]{1,0:T(8,128)(2,1)S(1)} %collective-permute-done.19.refs_9_) | copy-start | bytes 1572868
  214.5 6.5 %copy-start.17 = (bf16[1024,256]{1,0:T(8,128)(2,1)}, bf16[1024,256]{1,0:T(8,128)(2,1)S(1)}, u32[]{:S(2)}) copy-start(bf16[1024,256]{1,0:T(8,128)(2,1)S(1)} %collective-permute-done.21.refs_11_) | copy-start | bytes 1572868
  221.1 6.0 %collective-permute-start.24 = (bf16[2,1024,128]{2,1,0:T(8,128)(2,1)}, bf16[2,1024,128]{2,1,0:T(8,128)(2,1)S(1)}, u32[]{:S(2)}, u32[]{:S(2)}) collective-permute-start(bf16[2,1024,128]{2,1,0:T(8,128)(2,1)} %get-tuple-element.74), channel_id=1, source_target_pairs={{0,4},{4,0},{8,12},{12,8},{16,20},{20,16},{24,28},{28,24},{1,5},{5... | collective-permute-start | bytes 1572872 | tf_op jit(solution)/shard_map/ppermute | solution.py:239
  221.2 5.8 %collective-permute-start.25 = (bf16[2,1024,128]{2,1,0:T(8,128)(2,1)}, bf16[2,1024,128]{2,1,0:T(8,128)(2,1)S(1)}, u32[]{:S(2)}, u32[]{:S(2)}) collective-permute-start(bf16[2,1024,128]{2,1,0:T(8,128)(2,1)} %get-tuple-element.75), channel_id=1, source_target_pairs={{0,4},{4,0},{8,12},{12,8},{16,20},{20,16},{24,28},{28,24},{1,5},{5... | collective-permute-start | bytes 1572872 | tf_op jit(solution)/shard_map/ppermute | solution.py:239
  226.5 4.9 %collective-permute-start.22 = (bf16[2,1024,128]{2,1,0:T(8,128)(2,1)}, bf16[2,1024,128]{2,1,0:T(8,128)(2,1)S(1)}, u32[]{:S(2)}, u32[]{:S(2)}) collective-permute-start(bf16[2,1024,128]{2,1,0:T(8,128)(2,1)} %get-tuple-element.71), channel_id=1, source_target_pairs={{0,4},{4,0},{8,12},{12,8},{16,20},{20,16},{24,28},{28,24},{1,5},{5... | collective-permute-start | bytes 1572872 | tf_op jit(solution)/shard_map/ppermute | solution.py:239
  226.6 5.7 %collective-permute-start.23 = (bf16[2,1024,128]{2,1,0:T(8,128)(2,1)}, bf16[2,1024,128]{2,1,0:T(8,128)(2,1)}, u32[]{:S(2)}, u32[]{:S(2)}) collective-permute-start(bf16[2,1024,128]{2,1,0:T(8,128)(2,1)} %get-tuple-element.72), channel_id=1, source_target_pairs={{0,4},{4,0},{8,12},{12,8},{16,20},{20,16},{24,28},{28,24},{1,5},{5... | collective-permute-start | bytes 1572872 | tf_op jit(solution)/shard_map/ppermute | solution.py:239
  229.3 14.1 %collective-permute-start.26 = (bf16[2,1024,128]{2,1,0:T(8,128)(2,1)}, bf16[2,1024,128]{2,1,0:T(8,128)(2,1)S(1)}, u32[]{:S(2)}, u32[]{:S(2)}) collective-permute-start(bf16[2,1024,128]{2,1,0:T(8,128)(2,1)} %get-tuple-element.76), channel_id=1, source_target_pairs={{0,8},{4,12},{8,0},{12,4},{16,24},{20,28},{24,16},{28,20},{1,9},{5... | collective-permute-start | bytes 1572872 | tf_op jit(solution)/shard_map/ppermute | solution.py:239
  230.8 13.8 %collective-permute-start.27 = (bf16[2,1024,128]{2,1,0:T(8,128)(2,1)}, bf16[2,1024,128]{2,1,0:T(8,128)(2,1)S(1)}, u32[]{:S(2)}, u32[]{:S(2)}) collective-permute-start(bf16[2,1024,128]{2,1,0:T(8,128)(2,1)} %get-tuple-element.78), channel_id=1, source_target_pairs={{0,16},{4,20},{8,24},{12,28},{16,0},{20,4},{24,8},{28,12},{1,17},{... | collective-permute-start | bytes 1572872 | tf_op jit(solution)/shard_map/ppermute | solution.py:239
  235.8 23.8 %copy-start.9 = (bf16[1024,256]{1,0:T(8,128)(2,1)S(1)}, bf16[1024,256]{1,0:T(8,128)(2,1)}, u32[]{:S(2)}) copy-start(bf16[1024,256]{1,0:T(8,128)(2,1)} %copy-done.7) | copy-start | bytes 1572868
  235.8 23.8 %copy-start.12 = (bf16[1024,256]{1,0:T(8,128)(2,1)S(1)}, bf16[1024,256]{1,0:T(8,128)(2,1)}, u32[]{:S(2)}) copy-start(bf16[1024,256]{1,0:T(8,128)(2,1)} %copy-done.11) | copy-start | bytes 1572868
  235.8 23.8 %copy-start.14 = (bf16[1024,256]{1,0:T(8,128)(2,1)S(1)}, bf16[1024,256]{1,0:T(8,128)(2,1)}, u32[]{:S(2)}) copy-start(bf16[1024,256]{1,0:T(8,128)(2,1)} %copy-done.13) | copy-start | bytes 1572868
  235.8 23.9 %copy-start.16 = (bf16[1024,256]{1,0:T(8,128)(2,1)S(1)}, bf16[1024,256]{1,0:T(8,128)(2,1)}, u32[]{:S(2)}) copy-start(bf16[1024,256]{1,0:T(8,128)(2,1)} %copy-done.15) | copy-start | bytes 1572868
  235.8 23.9 %copy-start.18 = (bf16[1024,256]{1,0:T(8,128)(2,1)S(1)}, bf16[1024,256]{1,0:T(8,128)(2,1)}, u32[]{:S(2)}) copy-start(bf16[1024,256]{1,0:T(8,128)(2,1)} %copy-done.17) | copy-start | bytes 1572868
  245.3 17.8 %collective-permute-start.28 = (bf16[1024,128]{1,0:T(8,128)(2,1)S(1)}, bf16[1024,128]{1,0:T(8,128)(2,1)S(1)}, u32[]{:S(2)}, u32[]{:S(2)}) collective-permute-start(bf16[1024,128]{1,0:T(8,128)(2,1)S(1)} %get-tuple-element.79), channel_id=1, source_target_pairs={{0,16},{4,20},{8,24},{12,28},{16,0},{20,4},{24,8},{28,12},{1,17},{... | collective-permute-start | bytes 786440 | tf_op jit(solution)/shard_map/ppermute | solution.py:239
  245.9 17.2 %collective-permute-start.29 = (bf16[1024,128]{1,0:T(8,128)(2,1)S(1)}, bf16[1024,128]{1,0:T(8,128)(2,1)S(1)}, u32[]{:S(2)}, u32[]{:S(2)}) collective-permute-start(bf16[1024,128]{1,0:T(8,128)(2,1)S(1)} %get-tuple-element.80), channel_id=1, source_target_pairs={{0,8},{4,12},{8,0},{12,4},{16,24},{20,28},{24,16},{28,20},{1,9},{5... | collective-permute-start | bytes 786440 | tf_op jit(solution)/shard_map/ppermute | solution.py:239
  246.4 8.5 %collective-permute-start.30 = (bf16[256,256]{1,0:T(8,128)(2,1)S(1)}, bf16[256,256]{1,0:T(8,128)(2,1)S(1)}, u32[]{:S(2)}, u32[]{:S(2)}) collective-permute-start(bf16[256,256]{1,0:T(8,128)(2,1)S(1)} %get-tuple-element.70.d_projected.refs_0_), channel_id=1, source_target_pairs={{0,1},{1,2},{2,3},{3,0},{4,5},{5,6},{6,7},{7,4},{8,9},{9,10},{10,1... | collective-permute-start | bytes 393224 | tf_op jit(solution)/shard_map/ppermute | solution.py:430
  250.9 8.7 %collective-permute-start.31 = (bf16[256,256]{1,0:T(8,128)(2,1)S(1)}, bf16[256,256]{1,0:T(8,128)(2,1)S(1)}, u32[]{:S(2)}, u32[]{:S(2)}) collective-permute-start(bf16[256,256]{1,0:T(8,128)(2,1)S(1)} %get-tuple-element.70.d_projected.refs_0_), channel_id=1, source_target_pairs={{0,2},{1,3},{2,0},{3,1},{4,6},{5,7},{6,4},{7,5},{8,10},{9,11},{10,... | collective-permute-start | bytes 393224 | tf_op jit(solution)/shard_map/ppermute | solution.py:430
  251.3 8.3 %collective-permute-start.32 = (bf16[256,256]{1,0:T(8,128)(2,1)S(1)}, bf16[256,256]{1,0:T(8,128)(2,1)S(1)}, u32[]{:S(2)}, u32[]{:S(2)}) collective-permute-start(bf16[256,256]{1,0:T(8,128)(2,1)S(1)} %get-tuple-element.70.d_projected.refs_0_), channel_id=1, source_target_pairs={{0,3},{1,0},{2,1},{3,2},{4,7},{5,4},{6,5},{7,6},{8,11},{9,8},{10,9... | collective-permute-start | bytes 393224 | tf_op jit(solution)/shard_map/ppermute | solution.py:430
  (9 other events, 15.8 us)

commit v5 on v4

--- a/solution.py
+++ b/solution.py
@@ -81,56 +81,58 @@
     )(place, *arrays)
 
 
-def absorb_kernel(place, chunk, cached, total, held, total_out, held_out):
+def split_kernel(place, whole, *pieces):
+    rows = pieces[0].shape[0]
+    for p, piece in enumerate(pieces):
+        piece[...] = whole[p * rows : (p + 1) * rows, :]
+
+
+def absorb_kernel(place, piece, cached, total, *refs):
+    *_, total_out, held_out = refs
+
     @pl.when(pl.program_id(0) == 0)
     def _():
         total_out[...] = total[...]
 
-    total_out[...] += jnp.dot(chunk[...], cached[...], preferred_element_type=jnp.float32)
-    held_out[0] = chunk[...].T
-
-
-def absorb(chunk, index, cached, total, held, n_chunks):
-    length, feats = chunk.shape
+    total_out[...] += jnp.dot(piece[...], cached[...], preferred_element_type=jnp.float32)
+    held_out[0] = piece[...].T
+
+
+def absorb(piece, p, n_pieces, index, cached, total, held, n_chunks):
+    height, feats = piece.shape
     cols = cached.shape[1]
-    step = min(feats, 512)
+    step = min(feats, 1024)
     steps = feats // step
     inside = (index >= 0) & (index < n_chunks)
     place = jnp.stack([jnp.clip(index, 0, n_chunks - 1), jnp.where(inside, index, n_chunks)])
-    shape = jax.ShapeDtypeStruct((n_chunks + 1, feats, length), chunk.dtype)
-    out_total = jax.ShapeDtypeStruct(total.shape, jnp.float32)
-    whole = pl.BlockSpec((length, cols), lambda i, place: (0, 0))
-    operands = [chunk, cached, total] + ([] if held is None else [held])
-
-    def kernel(place, chunk, cached, total, *refs):
-        absorb_kernel(place, chunk, cached, total, None, *refs[-2:])
-
+    shape = jax.ShapeDtypeStruct((n_chunks + 1, feats, height * n_pieces), piece.dtype)
+    whole = pl.BlockSpec((height, cols), lambda i, place: (0, 0))
     return pl.pallas_call(
-        kernel,
+        absorb_kernel,
         grid_spec=pltpu.PrefetchScalarGridSpec(
             num_scalar_prefetch=1,
             grid=(steps,),
             in_specs=[
-                pl.BlockSpec((length, step), lambda i, place: (0, i)),
+                pl.BlockSpec((height, step), lambda i, place: (0, i)),
                 pl.BlockSpec((step, cols), lambda i, place: (place[0] * steps + i, 0)),
                 whole,
             ]
             + ([] if held is None else [pl.BlockSpec(memory_space=pl.ANY)]),
             out_specs=[
                 whole,
-                pl.BlockSpec((1, step, length), lambda i, place: (place[1], i, 0)),
+                pl.BlockSpec((1, step, height), lambda i, place: (place[1], i, p)),
             ],
         ),
-        out_shape=[out_total, shape],
+        out_shape=[jax.ShapeDtypeStruct(total.shape, jnp.float32), shape],
         input_output_aliases={} if held is None else {4: 1},
         cost_estimate=pl.CostEstimate(
-            flops=2 * length * feats * cols,
-            bytes_accessed=4 * length * feats + 2 * feats * cols,
+            flops=2 * height * feats * cols,
+            bytes_accessed=4 * height * feats + 2 * feats * cols,
             transcendentals=0,
         ),
         compiler_params=pltpu.CompilerParams(vmem_limit_bytes=VMEM_PART),
         name="absorb",
-    )(place, *operands)
+    )(place, piece, cached, total, *([] if held is None else [held]))
 
 
 def attention_kernel(place, projected, queries, d_out, allowed, d_queries, d_projected):
@@ -177,58 +179,70 @@
     )
 
 
-def weight_kernel(place, chunk_a, chunk_b, d_projected, *refs):
-    *added, out_a, out_b = refs
-    half = out_a.shape[2]
-    for side, (chunk, out) in enumerate(((chunk_a, out_a), (chunk_b, out_b))):
-        columns = d_projected[:, side * half : (side + 1) * half]
-        total = jnp.dot(chunk[0], columns, preferred_element_type=jnp.float32)
-        if added:
-            total = total + added[side][0].astype(jnp.float32)
-        out[0] = total.astype(out.dtype)
-
-
-def weight_parts(held, d_projected, place, added, dtype, name):
+def weight_kernel(place, chunk, d_projected, send_a, send_b, keep_a, keep_b):
+    k = pl.program_id(0)
+    half = send_a.shape[2]
+    total = jnp.dot(chunk[0], d_projected[...], preferred_element_type=jnp.float32)
+
+    @pl.when(k < 2)
+    def _():
+        send_a[0] = total[:, :half].astype(send_a.dtype)
+
+    @pl.when(k >= 2)
+    def _():
+        keep_a[0] = total[:, :half].astype(keep_a.dtype)
+
+    @pl.when(k % 2 == 0)
+    def _():
+        send_b[0] = total[:, half:].astype(send_b.dtype)
+
+    @pl.when(k % 2 == 1)
+    def _():
+        keep_b[0] = total[:, half:].astype(keep_b.dtype)
+
+
+def weight_parts(held, d_projected, place, dtype, name):
     length, cols = d_projected.shape
     rows = held.shape[1] // 2
     half = cols // 2
-    out = pl.BlockSpec((1, rows, half), lambda k, place: (k, 0, 0))
-    shape = jax.ShapeDtypeStruct((2, rows, half), dtype)
+    first = pl.BlockSpec((1, rows, half), lambda k, place: (jnp.minimum(k, 1), 0, 0))
+    second = pl.BlockSpec((1, rows, half), lambda k, place: (jnp.maximum(k, 2) - 2, 0, 0))
+    pairs = pl.BlockSpec((1, rows, half), lambda k, place: (k // 2, 0, 0))
     return pl.pallas_call(
         weight_kernel,
         grid_spec=pltpu.PrefetchScalarGridSpec(
             num_scalar_prefetch=1,
-            grid=(2,),
+            grid=(4,),
             in_specs=[
                 pl.BlockSpec((1, rows, length), lambda k, place: (place[k], place[4], 0)),
-                pl.BlockSpec((1, rows, length), lambda k, place: (place[2 + k], place[4], 0)),
                 pl.BlockSpec((length, cols), lambda k, place: (0, 0)),
-            ]
-            + [out] * len(added),
-            out_specs=[out, out],
-        ),
-        out_shape=[shape, shape],
+            ],
+            out_specs=[first, pairs, second, pairs],
+        ),
+        out_shape=[jax.ShapeDtypeStruct((2, rows, half), dtype)] * 4,
         cost_estimate=pl.CostEstimate(
-            flops=4 * length * rows * cols, bytes_accessed=8 * rows * cols, transcendentals=0
-        ),
-        compiler_params=pltpu.CompilerParams(vmem_limit_bytes=VMEM_PART),
+            flops=8 * length * rows * cols, bytes_accessed=16 * rows * cols, transcendentals=0
+        ),
+        compiler_params=pltpu.CompilerParams(vmem_limit_bytes=VMEM_STREAM),
         name=name,
-    )(place, held, held, d_projected, *added)
+    )(place, held, d_projected)
+
+
+def add_kernel(place, mine_a, mine_b, other_a, other_b, out_a, out_b):
+    for mine, other, out in ((mine_a, other_a, out_a), (mine_b, other_b, out_b)):
+        out[...] = (mine[...] + other[...].astype(jnp.float32)).astype(out.dtype)
 
 
 def combine_kernel(place, keep_a, got_a, keep_b, got_b, out_a, out_b):
-    sides = ((keep_a, got_a, out_a), (keep_b, got_b, out_b))
-    for side, (keep, got, out) in enumerate(sides):
-        which = place[side]
-        out[...] = (keep[which] + got[which].astype(jnp.float32)).astype(out.dtype)
+    for keep, got, out in ((keep_a, got_a, out_a), (keep_b, got_b, out_b)):
+        out[...] = (keep[0] + got[0].astype(jnp.float32)).astype(out.dtype)
 
 
 def finish_kernel(place, keep_a, got_a, keep_b, got_b, last_a, last_b, out):
     half = last_a.shape[1]
     sides = ((keep_a, got_a, last_a), (keep_b, got_b, last_b))
     for side, (keep, got, last) in enumerate(sides):
-        which = place[side]
-        total = keep[which] + got[which].astype(jnp.float32) + last[...].astype(jnp.float32)
+        total = keep[1] + got[1].astype(jnp.float32) + last[...].astype(jnp.float32)
         out[:, side * half : (side + 1) * half] = total
 
 
@@ -241,28 +255,30 @@
     return index % 2, (index // 2) % 2, index // 4, swap
 
 
-def weight_sum(held, d_projected):
+def weight_sum(held, d_projected, beside):
     core, x, y, swap = plane()
     rows, cols = held.shape[1] // 2, d_projected.shape[1]
-    send = [1 - x, 3 - x, 2 - 2 * y, 3 - 2 * y]
-    keep = [x, 2 + x, 2 * y, 2 * y + 1]
-
-    def parts(chunks, which, added, dtype, name):
-        place = jnp.stack(chunks + [which])
-        return weight_parts(held, d_projected, place, added, dtype, name)
-
-    theirs = parts(send, 1 - core, [], jnp.bfloat16, "weight_send_other")
-    theirs = [swap(part, 1) for part in theirs]
-    rest = parts(keep, 1 - core, [], jnp.bfloat16, "weight_keep_other")
-    rest = [swap(part, 1) for part in rest]
-    send_a, send_b = parts(send, core, theirs, jnp.bfloat16, "weight_send")
+    none = jnp.zeros((1,), jnp.int32)
+    chunks = [3 - x - 2 * y, 1 - x + 2 * y, x + 2 - 2 * y, x + 2 * y]
+
+    def parts(which, dtype, name):
+        return weight_parts(held, d_projected, jnp.stack(chunks + [which]), dtype, name)
+
+    def add(mine, other, dtype, name):
+        shape = jax.ShapeDtypeStruct(mine[0].shape, dtype)
+        return on_chip(add_kernel, none, list(mine) + other, [shape] * 2, 2 * cols * rows, name)
+
+    theirs = [swap(part, 1) for part in parts(1 - core, jnp.bfloat16, "weight_other")]
+    mine = parts(core, jnp.float32, "weight_own")
+    send_a, send_b = add(mine[:2], theirs[:2], jnp.bfloat16, "weight_add_send")
     got_a, got_b = swap(send_a, 2), swap(send_b, 4)
-    keep_a, keep_b = parts(keep, core, rest, jnp.float32, "weight_keep")
+    keep_a, keep_b = add(mine[2:], theirs[2:], jnp.float32, "weight_add_keep")
+    got_a, got_b, beside = lax.optimization_barrier((got_a, got_b, beside))
 
     small = jax.ShapeDtypeStruct((rows, cols // 2), jnp.bfloat16)
     arrays = [keep_a, got_a, keep_b, got_b]
     last_a, last_b = on_chip(
-        combine_kernel, jnp.stack([1 - y, 1 - x]), arrays, [small] * 2, cols * rows, "weight_combine"
+        combine_kernel, none, arrays, [small] * 2, cols * rows, "weight_combine"
     )
     last = [swap(last_a, 4), swap(last_b, 2)]
 
@@ -270,7 +286,7 @@
         ended, ready = lax.optimization_barrier((last, ready))
         (total,) = on_chip(
             finish_kernel,
-            jnp.stack([y, x]),
+            none,
             arrays + ended,
             [jax.ShapeDtypeStruct((rows, cols), jnp.float32)],
             2 * cols * rows,
@@ -278,15 +294,16 @@
         )
         return total, ready
 
-    return finish
-
-
-def gather_plane(own_cache, own_rows):
+    return finish, beside
+
+
+def gather_plane(own_cache, own_rows, gate):
     _, _, _, swap = plane()
     cache, rows = {0: own_cache}, {0: own_rows}
     for bit in (2, 4):
         cache[bit] = swap(own_cache, bit)
         rows[bit] = swap(own_rows, bit)
+    cache, rows, _ = lax.optimization_barrier((cache, rows, gate))
     cache[6] = swap(cache[4], 2)
     rows[6] = swap(rows[2], 4)
     for bits in (0, 2, 4, 6):
@@ -312,11 +329,11 @@
 
 def place_rows(pieces):
     height, cols = pieces[0].shape
-    anywhere = pl.BlockSpec(memory_space=pl.ANY)
     return pl.pallas_call(
         place_rows_kernel,
-        in_specs=[pl.BlockSpec(memory_space=pltpu.SMEM)] + [anywhere] * len(pieces),
-        out_specs=anywhere,
+        in_specs=[pl.BlockSpec(memory_space=pltpu.SMEM)]
+        + [pl.BlockSpec(memory_space=pltpu.VMEM)] * len(pieces),
+        out_specs=pl.BlockSpec(memory_space=pl.ANY),
         out_shape=jax.ShapeDtypeStruct((height * len(pieces), cols), pieces[0].dtype),
         scratch_shapes=[pltpu.SemaphoreType.DMA((len(pieces),))],
         cost_estimate=pl.CostEstimate(
@@ -363,6 +380,7 @@
 def make_body(n_dp, n_z):
     ring = [[(z, (z + s) % n_z) for z in range(n_z)] for s in range(n_z)]
     tuned = n_dp == 8 and n_z == 4
+    n_pieces = 2
 
     def body(tokens, queries, d_out, segments, cached, master, moment, second, grad):
         me_dp = lax.axis_index("dp").astype(jnp.int32)
@@ -384,30 +402,42 @@
             cached, master, moment, second, grad
         )
 
-        total = jnp.zeros((length, cols), jnp.float32)
-        total, held = absorb(tokens, me_z, cached, total, None, n_z)
-        from_low, from_high, merged = tokens, tokens, None
+        shape = jax.ShapeDtypeStruct((length // n_pieces, feats), tokens.dtype)
+        own = on_chip(
+            split_kernel, jnp.zeros((1,), jnp.int32), [tokens], [shape] * n_pieces, 0, "split"
+        )
+        totals = [jnp.zeros((length // n_pieces, cols), jnp.float32) for _ in range(n_pieces)]
+        held = None
+
+        def take(pieces, index, held):
+            for p, piece in enumerate(pieces):
+                totals[p], held = absorb(
+                    piece, p, n_pieces, index, cached, totals[p], held, n_z
+                )
+            return held
+
+        held = take(own, me_z, held)
+        from_low, from_high, merged = own, own, None
+        gates, after = [], held
         for s in range(1, n_z):
             up = [(z, z + 1) for z in range(s - 1, n_z - 1)]
             down = [(z + 1, z) for z in range(n_z - s)]
             low, high = me_z - s, me_z + s
             if merged is None:
-                from_low = lax.ppermute(from_low, "tensor", up)
-                from_high = lax.ppermute(from_high, "tensor", down)
+                from_low = [lax.ppermute(piece, "tensor", up) for piece in from_low]
+                from_high = [lax.ppermute(piece, "tensor", down) for piece in from_high]
             else:
-                merged = lax.ppermute(merged, "tensor", up + down)
-            if s == 1:
-                from_low, from_high, own_cache, own_rows = lax.optimization_barrier(
-                    (from_low, from_high, own_cache, own_rows)
-                )
+                merged = [lax.ppermute(piece, "tensor", up + down) for piece in merged]
             if merged is None and 2 * s >= n_z:
-                merged = jnp.where(me_z >= s, from_low, from_high)
+                merged = [jnp.where(me_z >= s, a, b) for a, b in zip(from_low, from_high)]
             if merged is None:
-                total, held = absorb(from_low, low, cached, total, held, n_z)
-                total, held = absorb(from_high, high, cached, total, held, n_z)
+                held = take(from_low, low, held)
+                held = take(from_high, high, held)
             else:
-                origin = jnp.where(me_z >= s, low, high)
-                total, held = absorb(merged, origin, cached, total, held, n_z)
+                held = take(merged, jnp.where(me_z >= s, low, high), held)
+            arrived = (from_low[0], from_high[0]) if merged is None else merged[0]
+            gates.append((arrived, after))
+            after = held
 
         doc_ids = segments[0]
         position = jnp.arange(length)
@@ -415,22 +445,25 @@
         allowed = allowed.astype(jnp.float32)
 
         if tuned:
-            cache_pieces, row_pieces = gather_plane(own_cache, own_rows)
-            new_cache = place_rows(cache_pieces)
-            total, new_cache, row_pieces = lax.optimization_barrier((total, new_cache, row_pieces))
+            own_cache, own_rows, _ = lax.optimization_barrier((own_cache, own_rows, gates[0]))
+            cache_pieces, row_pieces = gather_plane(own_cache, own_rows, gates[1])
+            totals, cache_pieces, row_pieces = lax.optimization_barrier(
+                (totals, cache_pieces, row_pieces)
+            )
         else:
             new_cache = lax.all_gather(own_cache, "dp", axis=0, tiled=True)
             row_pieces = lax.all_gather(own_rows, "dp", axis=0)
 
         d_queries, d_projected = attention_backward(
-            total.astype(jnp.bfloat16), queries, d_out, allowed
+            jnp.concatenate(totals, axis=0).astype(jnp.bfloat16), queries, d_out, allowed
         )
 
         pieces = [d_projected] + [
             lax.ppermute(d_projected, "tensor", ring[s]) for s in range(1, n_z)
         ]
         if tuned:
-            finish = weight_sum(held, d_projected)
+            new_cache = place_rows(cache_pieces)
+            finish, (pieces, new_cache) = weight_sum(held, d_projected, (pieces, new_cache))
             new_grad, d_tokens = finish(input_gradient(pieces, row_pieces))
         else:
             rows = row_pieces.reshape(n_dp, n_z, share, cols)

time: 265 us -> 179 us (0.68)
  Pallas kernels: 148 us -> 47 us
  local copies, waits for them, and re-layouts: 12.3 us -> 36.6 us
  waiting for transfers between devices: 62.8 us -> 42.9 us
  starting transfers between devices: 38.3 us -> 48.4 us
    pallas_call x1, Pallas kernels: 112 us -> 3.42 us  [place_rows(): pl.pallas_call(place_rows_kernel, in_specs=[pl.BlockSpec(memory_space=plt...]
    unnamed x48 -> x80, local copies, waits for them, and re-layouts: 10.8 us -> 33.4 us
    ppermute x22, waiting for transfers between devices: 34 us -> 11.9 us  [swap(): return lax.ppermute(value, 'dp', [(i, i ^ bit) for i in range(8)])]
    ppermute x5 -> x10, waiting for transfers between devices: 0.01 us -> 8.4 us  [the longest x4 8.39 us: body(): from_high = [lax.ppermute(piece, 'tensor', down) for piece in from_high]]
    ppermute x5 -> x10, starting transfers between devices: 11.5 us -> 19.4 us  [the longest x4 11.7 us: body(): from_low = [lax.ppermute(piece, 'tensor', up) for piece in from_low]]
    ppermute x3, waiting for transfers between devices: 5.42 us -> 0.01 us  [body(): lax.ppermute(d_projected, 'tensor', ring[s])]
    pallas_call x5 -> x10, Pallas kernels: 11.5 us -> 14.8 us  [absorb(): pl.pallas_call(absorb_kernel, grid_spec=pltpu.PrefetchScalarGridSpec(num_...]
    pallas_call x4 -> x7, Pallas kernels: 9.86 us -> 12.4 us  [on_chip(): pl.pallas_call(kernel, in_specs=[pl.BlockSpec(memory_space=pltpu.SMEM)] +...]
  transfers between devices with their start and end apart: 33 -> 38, of which waited for: 11 -> 9; matrix products, arithmetic and copies ran while one was open for 1% -> 3% of each run, Pallas kernels for 53% -> 20%
where the time goes in v5:
time: 179 us; the launch traced here: 178 us
  starting transfers between devices  48.4 us (27%)
  Pallas kernels  47 us (26%)
  waiting for transfers between devices  42.9 us (24%)
  local copies, waits for them, and re-layouts  36.6 us (20%)
    unnamed x80, local copies, waits for them, and re-layouts  33.4 us
    ppermute x3, waiting for transfers between devices, body(): blocks.append(lax.ppermute(block_for((me_z + s) % n_z), 'tensor', ring[s]))  22.6 us
    pallas_call x10, Pallas kernels, absorb(): pl.pallas_call(absorb_kernel, grid_spec=pltpu.PrefetchScalarGridSpec(num_...  14.8 us
    ppermute x22, starting transfers between devices, swap(): return lax.ppermute(value, 'dp', [(i, i ^ bit) for i in range(8)])  13.7 us
    pallas_call x7, Pallas kernels, on_chip(): pl.pallas_call(kernel, in_specs=[pl.BlockSpec(memory_space=pltpu.SMEM)] +...  12.4 us
    ppermute x22, waiting for transfers between devices, swap(): return lax.ppermute(value, 'dp', [(i, i ^ bit) for i in range(8)])  11.9 us
    ppermute x4, starting transfers between devices, body(): from_low = [lax.ppermute(piece, 'tensor', up) for piece in from_low]  11.7 us
    pallas_call x2, Pallas kernels, weight_parts(): pl.pallas_call(weight_kernel, grid_spec=pltpu.PrefetchScalarGridSpec(num_...  11 us
  transfers between devices with their start and end apart: 38, of which 9 were waited for; matrix products, arithmetic and copies ran while one was open for 3% of the time, Pallas kernels for 20%

profile of v5, /device:TPU:0, one launch (start us, length us, event | category | flops | bytes accessed | tf_op | source)
XLA Modules:
  0.0 177.8 jit_solution(4476401384911530486)
XLA Ops:
  0.6 1.2 copy-done.12
  1.9 5.0 %collective-permute-start = (bf16[128,2048]{1,0:T(8,128)(2,1)S(1)}, bf16[128,2048]{1,0:T(8,128)(2,1)S(1)}, u32[]{:S(2)}, u32[]{:S(2)}) collective-permute-start(bf16[128,2048]{1,0:T(8,128)(2,1)S(1)} %get-tuple-element.88.piece), channel_id=1, source_target_pairs={{0,1},{1,2},{2,3},{4,5},{5,6},{6,7},{8,9},{9,10},{10,11},{12,13},{... | collective-permute-start | bytes 1572872 | tf_op jit(solution)/shard_map/ppermute | solution.py:427
  6.9 1.3 collective-permute-start.2
  8.2 4.6 %collective-permute-start.5 = (bf16[128,2048]{1,0:T(8,128)(2,1)S(1)}, bf16[128,2048]{1,0:T(8,128)(2,1)S(1)}, u32[]{:S(2)}, u32[]{:S(2)}) collective-permute-start(bf16[128,2048]{1,0:T(8,128)(2,1)S(1)} %get-tuple-element.89.piece), channel_id=1, source_target_pairs={{0,1},{1,2},{2,3},{4,5},{5,6},{6,7},{8,9},{9,10},{10,11},{12,13},{... | collective-permute-start | bytes 1572872 | tf_op jit(solution)/shard_map/ppermute | solution.py:427
  12.8 1.3 collective-permute-start.6
  14.1 1.8 %constant_dynamic-slice_fusion.3 = (bf16[256,256]{1,0:T(8,128)(2,1)S(1)}, bf16[256,256]{1,0:T(8,128)(2,1)}, bf16[256,256]{1,0:T(8,128)(2,1)S(1)}, bf16[256,256]{1,0:T(8,128)(2,1)S(1)}) fusion(bf16[8192,256]{1,0:T(8,128)(2,1)} %cached.21, s32[]{:T(128)S(6)} %select_n.95, s32[]{:T(128)S(6)} %select_n.97, s32[]{:T(128)S(6)} %select_n.101, s32[]{:T(128)S(6)} %select_n.99), kind=kLoop, calls=%fused_computation.10 | loop fusion | bytes 1048592 | tf_op jit(solution)/shard_map/dynamic_slice | solution.py:394
  15.9 5.4 %collective-permute-start.12 = (bf16[256,256]{1,0:T(8,128)(2,1)S(1)}, bf16[256,256]{1,0:T(8,128)(2,1)S(1)}, u32[]{:S(2)}, u32[]{:S(2)}) collective-permute-start(bf16[256,256]{1,0:T(8,128)(2,1)S(1)} %get-tuple-element.165), channel_id=1, source_target_pairs={{0,3},{1,0},{2,1},{3,2},{4,7},{5,4},{6,5},{7,6},{8,11},{9,8},{10,9... | collective-permute-start | bytes 393224 | tf_op jit(solution)/shard_map/ppermute | solution.py:398
  21.3 1.5 collective-permute-start.1
  23.6 1.3 collective-permute-start.3
  24.9 12.8 %collective-permute-done.12 = bf16[256,256]{1,0:T(8,128)(2,1)S(1)} collective-permute-done((bf16[256,256]{1,0:T(8,128)(2,1)S(1)}, bf16[256,256]{1,0:T(8,128)(2,1)S(1)}, u32[]{:S(2)}, u32[]{:S(2)}) %collective-permute-start.12) | collective-permute-done | bytes 131104 | tf_op jit(solution)/shard_map/ppermute | solution.py:398
  38.8 5.4 %optimizer.1 = (f32[1024,256]{1,0:T(8,128)}, f32[1024,256]{1,0:T(8,128)}, f32[1024,256]{1,0:T(8,128)}, bf16[1024,256]{1,0:T(8,128)(2,1)}) custom-call(s32[1]{0:T(128)} %bitcast.place, bf16[8192,256]{1,0:T(8,128)(2,1)} %cached.21, f32[1024,256]{1,0:T(8,128)} %master.1, f32[1024,256]{1,0:T(8,128)} %moment.1, f32[1024,256]{1,0:T(8,128)} %second.1, f32[1024,256]{1,0:T(8,128)} %grad.1), custom_call_target="tpu_custom_call" | custom-call | flops 10485760 | bytes 8388608 | tf_op jit(solution)/shard_map/optimizer/pallas_call | solution.py:51
  44.2 9.9 %collective-permute-done.11 = bf16[256,256]{1,0:T(8,128)(2,1)S(1)} collective-permute-done((bf16[256,256]{1,0:T(8,128)(2,1)S(1)}, bf16[256,256]{1,0:T(8,128)(2,1)S(1)}, u32[]{:S(2)}, u32[]{:S(2)}) %collective-permute-start.11) | collective-permute-done | bytes 131104 | tf_op jit(solution)/shard_map/ppermute | solution.py:398
  57.2 2.3 %copy-done = bf16[5,2048,256]{2,1,0:T(8,128)(2,1)} copy-done((bf16[5,2048,256]{2,1,0:T(8,128)(2,1)}, bf16[5,2048,256]{2,1,0:T(8,128)(2,1)S(1)}, u32[]{:S(2)}) %copy-start) | copy-done | bytes 5242904
  60.3 1.3 collective-permute-start.8
  61.6 1.6 collective-permute-start.13
  63.2 1.5 collective-permute-start.14
  67.0 7.6 %collective-permute-done.8 = bf16[128,2048]{1,0:T(8,128)(2,1)S(1)} collective-permute-done((bf16[128,2048]{1,0:T(8,128)(2,1)}, bf16[128,2048]{1,0:T(8,128)(2,1)S(1)}, u32[]{:S(2)}, u32[]{:S(2)}) %collective-permute-start.8) | collective-permute-done | bytes 524320 | tf_op jit(solution)/shard_map/ppermute | solution.py:428
  74.5 1.3 collective-permute-start.4
  77.4 1.3 collective-permute-start.9
  78.8 2.5 %copy-done.1 = bf16[5,2048,256]{2,1,0:T(8,128)(2,1)S(1)} copy-done((bf16[5,2048,256]{2,1,0:T(8,128)(2,1)S(1)}, bf16[5,2048,256]{2,1,0:T(8,128)(2,1)}, u32[]{:S(2)}) %copy-start.1) | copy-done | bytes 5242904
  81.3 2.2 %copy-done.8 = bf16[8192,256]{1,0:T(8,128)(2,1)S(1)} copy-done((bf16[8192,256]{1,0:T(8,128)(2,1)S(1)}, bf16[8192,256]{1,0:T(8,128)(2,1)}, u32[]{:S(2)}) %copy-start.8) | copy-done | bytes 4194328
  85.8 2.3 %copy-done.2 = bf16[5,2048,256]{2,1,0:T(8,128)(2,1)} copy-done((bf16[5,2048,256]{2,1,0:T(8,128)(2,1)}, bf16[5,2048,256]{2,1,0:T(8,128)(2,1)S(1)}, u32[]{:S(2)}) %copy-start.2) | copy-done | bytes 5242904
  88.1 2.5 %copy-done.3 = bf16[5,2048,256]{2,1,0:T(8,128)(2,1)S(1)} copy-done((bf16[5,2048,256]{2,1,0:T(8,128)(2,1)S(1)}, bf16[5,2048,256]{2,1,0:T(8,128)(2,1)}, u32[]{:S(2)}) %copy-start.3) | copy-done | bytes 5242904
  91.8 2.1 %absorb.14 = (f32[128,256]{1,0:T(8,128)S(1)}, bf16[5,2048,256]{2,1,0:T(8,128)(2,1)S(1)}) custom-call(s32[2]{0:T(128)S(1)} %pad_add_fusion.2.place, bf16[128,2048]{1,0:T(8,128)(2,1)} %collective-permute-done.6.piece, bf16[8192,256]{1,0:T(8,128)(2,1)S(1)} %copy-done.8, f32[128,256]{1,0:T(8,128)S(1)} %get-tuple-element.96.total, ...), custom_call_target="tpu_custom_call", output_to_operand_aliasing={{1}: (4, {})} | custom-call | flops 134217728 | bytes 2097152 | tf_op jit(solution)/shard_map/absorb/pallas_call | solution.py:110
  94.0 1.2 absorb.15
  95.2 2.3 %copy-done.4 = bf16[5,2048,256]{2,1,0:T(8,128)(2,1)} copy-done((bf16[5,2048,256]{2,1,0:T(8,128)(2,1)}, bf16[5,2048,256]{2,1,0:T(8,128)(2,1)S(1)}, u32[]{:S(2)}) %copy-start.4) | copy-done | bytes 5242904
  98.2 1.5 collective-permute-start.20
  99.7 1.5 collective-permute-start.25
  104.1 8.6 %collective-permute-done.20.refs_6_ = bf16[1024,256]{1,0:T(8,128)(2,1)} collective-permute-done((bf16[1024,256]{1,0:T(8,128)(2,1)}, bf16[1024,256]{1,0:T(8,128)(2,1)}, u32[]{:S(2)}, u32[]{:S(2)}) %collective-permute-start.20) | collective-permute-done | bytes 524320 | tf_op jit(solution)/shard_map/ppermute | solution.py:253
  114.7 2.5 %copy-done.5 = bf16[5,2048,256]{2,1,0:T(8,128)(2,1)S(1)} copy-done((bf16[5,2048,256]{2,1,0:T(8,128)(2,1)S(1)}, bf16[5,2048,256]{2,1,0:T(8,128)(2,1)}, u32[]{:S(2)}) %copy-start.5) | copy-done | bytes 5242904
  117.2 2.2 %copy-done.9 = bf16[8192,256]{1,0:T(8,128)(2,1)S(1)} copy-done((bf16[8192,256]{1,0:T(8,128)(2,1)S(1)}, bf16[8192,256]{1,0:T(8,128)(2,1)}, u32[]{:S(2)}) %copy-start.9) | copy-done | bytes 4194328
  121.8 2.1 %absorb.18 = (f32[128,256]{1,0:T(8,128)S(1)}, bf16[5,2048,256]{2,1,0:T(8,128)(2,1)S(1)}) custom-call(s32[2]{0:T(128)S(1)} %pad_add_fusion.place, bf16[128,2048]{1,0:T(8,128)(2,1)} %collective-permute-done.9.piece, bf16[8192,256]{1,0:T(8,128)(2,1)S(1)} %copy-done.9, f32[128,256]{1,0:T(8,128)S(1)} %get-tuple-element.104.total, ...), custom_call_target="tpu_custom_call", output_to_operand_aliasing={{1}: (4, {})} | custom-call | flops 134217728 | bytes 2097152 | tf_op jit(solution)/shard_map/absorb/pallas_call | solution.py:110
  123.9 2.1 %absorb.19 = (f32[128,256]{1,0:T(8,128)S(1)}, bf16[5,2048,256]{2,1,0:T(8,128)(2,1)S(1)}) custom-call(s32[2]{0:T(128)S(1)} %pad_add_fusion.place, bf16[128,2048]{1,0:T(8,128)(2,1)} %collective-permute-done.4.piece, bf16[8192,256]{1,0:T(8,128)(2,1)S(1)} %copy-done.9, f32[128,256]{1,0:T(8,128)S(1)} %get-tuple-element.103.total, ...), custom_call_target="tpu_custom_call", output_to_operand_aliasing={{1}: (4, {})} | custom-call | flops 134217728 | bytes 2097152 | tf_op jit(solution)/shard_map/absorb/pallas_call | solution.py:110
  126.1 2.3 %copy-done.6 = bf16[5,2048,256]{2,1,0:T(8,128)(2,1)} copy-done((bf16[5,2048,256]{2,1,0:T(8,128)(2,1)}, bf16[5,2048,256]{2,1,0:T(8,128)(2,1)S(1)}, u32[]{:S(2)}) %copy-start.6) | copy-done | bytes 5242904
  128.5 4.2 %attention.1 = (bf16[256,1024]{1,0:T(8,128)(2,1)}, bf16[256,256]{1,0:T(8,128)(2,1)S(1)}) custom-call(s32[1]{0:T(128)} %constant.67.clone.1.place, bf16[256,256]{1,0:T(8,128)(2,1)S(1)} %pad_maximum_fusion.1.projected, bf16[256,1024]{1,0:T(8,128)(2,1)S(1)} %copy-done.33, bf16[256,1024]{1,0:T(8,128)(2,1)S(1)} %copy-done.34, f32[256,256]{1,0:T(8,128)S(1)} %fusion.1.allowed), custom_call_target="tpu_custom_call" | custom-call | flops 805306368 | bytes 2097152 | tf_op jit(solution)/shard_map/attention/pallas_call | solution.py:73
  133.3 5.3 %weight_other.1 = (bf16[2,1024,128]{2,1,0:T(8,128)(2,1)}, bf16[2,1024,128]{2,1,0:T(8,128)(2,1)}, bf16[2,1024,128]{2,1,0:T(8,128)(2,1)}, bf16[2,1024,128]{2,1,0:T(8,128)(2,1)}) custom-call(s32[5]{0:T(128)} %stack.110.place, bf16[5,2048,256]{2,1,0:T(8,128)(2,1)} %copy-done.6, bf16[256,256]{1,0:T(8,128)(2,1)} %copy-done.10), custom_call_target="tpu_custom_call" | custom-call | flops 536870912 | bytes 4194304 | tf_op jit(solution)/shard_map/weight_other/pallas_call | solution.py:211
  140.4 5.7 %weight_own.1 = (f32[2,1024,128]{2,1,0:T(8,128)}, f32[2,1024,128]{2,1,0:T(8,128)}, f32[2,1024,128]{2,1,0:T(8,128)}, f32[2,1024,128]{2,1,0:T(8,128)}) custom-call(s32[5]{0:T(128)} %stack.93.place, bf16[5,2048,256]{2,1,0:T(8,128)(2,1)} %copy-done.6, bf16[256,256]{1,0:T(8,128)(2,1)} %copy-done.10), custom_call_target="tpu_custom_call" | custom-call | flops 536870912 | bytes 4194304 | tf_op jit(solution)/shard_map/weight_own/pallas_call | solution.py:211
  146.1 1.2 copy-done.15
  147.3 1.2 copy-done.16
  148.6 1.5 weight_add_send.1
  151.1 1.5 collective-permute-start.30
  152.6 3.6 %collective-permute-start.31 = (bf16[256,256]{1,0:T(8,128)(2,1)S(1)}, bf16[256,256]{1,0:T(8,128)(2,1)S(1)}, u32[]{:S(2)}, u32[]{:S(2)}) collective-permute-start(bf16[256,256]{1,0:T(8,128)(2,1)S(1)} %copy-done.11), channel_id=1, source_target_pairs={{0,1},{1,2},{2,3},{3,0},{4,5},{5,6},{6,7},{7,4},{8,9},{9,10},{10,1... | collective-permute-start | bytes 393224 | tf_op jit(solution)/shard_map/ppermute | solution.py:462
  156.2 2.3 %collective-permute-start.32 = (bf16[256,256]{1,0:T(8,128)(2,1)S(1)}, bf16[256,256]{1,0:T(8,128)(2,1)S(1)}, u32[]{:S(2)}, u32[]{:S(2)}) collective-permute-start(bf16[256,256]{1,0:T(8,128)(2,1)S(1)} %copy-done.11), channel_id=1, source_target_pairs={{0,2},{1,3},{2,0},{3,1},{4,6},{5,7},{6,4},{7,5},{8,10},{9,11},{10,... | collective-permute-start | bytes 393224 | tf_op jit(solution)/shard_map/ppermute | solution.py:462
  158.5 2.9 %collective-permute-start.33 = (bf16[256,256]{1,0:T(8,128)(2,1)S(1)}, bf16[256,256]{1,0:T(8,128)(2,1)S(1)}, u32[]{:S(2)}, u32[]{:S(2)}) collective-permute-start(bf16[256,256]{1,0:T(8,128)(2,1)S(1)} %copy-done.11), channel_id=1, source_target_pairs={{0,3},{1,0},{2,1},{3,2},{4,7},{5,4},{6,5},{7,6},{8,11},{9,8},{10,9... | collective-permute-start | bytes 393224 | tf_op jit(solution)/shard_map/ppermute | solution.py:462
  164.5 3.4 %place_rows.1 = bf16[8192,256]{1,0:T(8,128)(2,1)} custom-call(s32[1]{0:T(128)} %bitcast.place, bf16[1024,256]{1,0:T(8,128)(2,1)S(1)} %copy-done.17, bf16[1024,256]{1,0:T(8,128)(2,1)S(1)} %copy-done.22, bf16[1024,256]{1,0:T(8,128)(2,1)S(1)} %copy-done.20, bf16[1024,256]{1,0:T(8,128)(2,1)S(1)} %copy-done.24, ...), custom_call_target="tpu_custom_call" | custom-call | bytes 8388608 | tf_op jit(solution)/shard_map/place_rows/pallas_call | solution.py:332
  167.9 1.4 weight_add_keep.1
  171.2 4.0 %input_gradient.1 = bf16[256,2048]{1,0:T(8,128)(2,1)} custom-call(s32[5]{0:T(128)S(1)} %broadcast_in_dim.2.place, bf16[256,256]{1,0:T(8,128)(2,1)S(1)} %copy-done.11, bf16[256,256]{1,0:T(8,128)(2,1)S(1)} %collective-permute-done.31.refs_1_, bf16[256,256]{1,0:T(8,128)(2,1)S(1)} %collective-permute-done.32.refs_2_, ...), custom_call_target="tpu_custom_call" | custom-call | flops 1073741824 | bytes 5767168 | tf_op jit(solution)/shard_map/input_gradient/pallas_call | solution.py:73
  175.2 1.3 collective-permute-done.36.last_a
  (146 shorter events, 31.0 us)
Async XLA Ops:
  1.9 19.4 %collective-permute-start = (bf16[128,2048]{1,0:T(8,128)(2,1)S(1)}, bf16[128,2048]{1,0:T(8,128)(2,1)S(1)}, u32[]{:S(2)}, u32[]{:S(2)}) collective-permute-start(bf16[128,2048]{1,0:T(8,128)(2,1)S(1)} %get-tuple-element.88.piece), channel_id=1, source_target_pairs={{0,1},{1,2},{2,3},{4,5},{5,6},{6,7},{8,9},{9,10},{10,11},{12,13},{... | collective-permute-start | bytes 1572872 | tf_op jit(solution)/shard_map/ppermute | solution.py:427
  6.9 16.7 %collective-permute-start.2 = (bf16[128,2048]{1,0:T(8,128)(2,1)S(1)}, bf16[128,2048]{1,0:T(8,128)(2,1)S(1)}, u32[]{:S(2)}, u32[]{:S(2)}) collective-permute-start(bf16[128,2048]{1,0:T(8,128)(2,1)S(1)} %get-tuple-element.88.piece), channel_id=1, source_target_pairs={{1,0},{2,1},{3,2},{5,4},{6,5},{7,6},{9,8},{10,9},{11,10},{13,12},{... | collective-permute-start | bytes 1572872 | tf_op jit(solution)/shard_map/ppermute | solution.py:428
  8.2 51.4 %collective-permute-start.5 = (bf16[128,2048]{1,0:T(8,128)(2,1)S(1)}, bf16[128,2048]{1,0:T(8,128)(2,1)S(1)}, u32[]{:S(2)}, u32[]{:S(2)}) collective-permute-start(bf16[128,2048]{1,0:T(8,128)(2,1)S(1)} %get-tuple-element.89.piece), channel_id=1, source_target_pairs={{0,1},{1,2},{2,3},{4,5},{5,6},{6,7},{8,9},{9,10},{10,11},{12,13},{... | collective-permute-start | bytes 1572872 | tf_op jit(solution)/shard_map/ppermute | solution.py:427
  12.8 47.5 %collective-permute-start.6 = (bf16[128,2048]{1,0:T(8,128)(2,1)S(1)}, bf16[128,2048]{1,0:T(8,128)(2,1)}, u32[]{:S(2)}, u32[]{:S(2)}) collective-permute-start(bf16[128,2048]{1,0:T(8,128)(2,1)S(1)} %get-tuple-element.89.piece), channel_id=1, source_target_pairs={{1,0},{2,1},{3,2},{5,4},{6,5},{7,6},{9,8},{10,9},{11,10},{13,12},{... | collective-permute-start | bytes 1572872 | tf_op jit(solution)/shard_map/ppermute | solution.py:428
  15.9 21.7 %collective-permute-start.12 = (bf16[256,256]{1,0:T(8,128)(2,1)S(1)}, bf16[256,256]{1,0:T(8,128)(2,1)S(1)}, u32[]{:S(2)}, u32[]{:S(2)}) collective-permute-start(bf16[256,256]{1,0:T(8,128)(2,1)S(1)} %get-tuple-element.165), channel_id=1, source_target_pairs={{0,3},{1,0},{2,1},{3,2},{4,7},{5,4},{6,5},{7,6},{8,11},{9,8},{10,9... | collective-permute-start | bytes 393224 | tf_op jit(solution)/shard_map/ppermute | solution.py:398
  21.3 34.6 %copy-start.29 = (bf16[128,2048]{1,0:T(8,128)(2,1)}, bf16[128,2048]{1,0:T(8,128)(2,1)S(1)}, u32[]{:S(2)}) copy-start(bf16[128,2048]{1,0:T(8,128)(2,1)S(1)} %collective-permute-done.piece) | copy-start | bytes 1572868
  21.3 41.9 %collective-permute-start.1 = (bf16[128,2048]{1,0:T(8,128)(2,1)S(1)}, bf16[128,2048]{1,0:T(8,128)(2,1)}, u32[]{:S(2)}, u32[]{:S(2)}) collective-permute-start(bf16[128,2048]{1,0:T(8,128)(2,1)S(1)} %collective-permute-done.piece), channel_id=1, source_target_pairs={{1,2},{2,3},{5,6},{6,7},{9,10},{10,11},{13,14},{14,15},{17,18},{18... | collective-permute-start | bytes 1572872 | tf_op jit(solution)/shard_map/ppermute | solution.py:427
  23.6 32.3 %copy-start.27 = (bf16[128,2048]{1,0:T(8,128)(2,1)}, bf16[128,2048]{1,0:T(8,128)(2,1)S(1)}, u32[]{:S(2)}) copy-start(bf16[128,2048]{1,0:T(8,128)(2,1)S(1)} %collective-permute-done.2.piece) | copy-start | bytes 1572868
  23.6 41.1 %collective-permute-start.3 = (bf16[128,2048]{1,0:T(8,128)(2,1)S(1)}, bf16[128,2048]{1,0:T(8,128)(2,1)}, u32[]{:S(2)}, u32[]{:S(2)}) collective-permute-start(bf16[128,2048]{1,0:T(8,128)(2,1)S(1)} %collective-permute-done.2.piece), channel_id=1, source_target_pairs={{1,0},{2,1},{5,4},{6,5},{9,8},{10,9},{13,12},{14,13},{17,16},{18,1... | collective-permute-start | bytes 1572872 | tf_op jit(solution)/shard_map/ppermute | solution.py:428
  37.7 18.3 %copy-start.35 = (bf16[256,256]{1,0:T(8,128)(2,1)}, bf16[256,256]{1,0:T(8,128)(2,1)S(1)}, u32[]{:S(2)}) copy-start(bf16[256,256]{1,0:T(8,128)(2,1)S(1)} %collective-permute-done.12) | copy-start | bytes 393220
  37.7 16.4 %collective-permute-start.11 = (bf16[256,256]{1,0:T(8,128)(2,1)S(1)}, bf16[256,256]{1,0:T(8,128)(2,1)S(1)}, u32[]{:S(2)}, u32[]{:S(2)}) collective-permute-start(bf16[256,256]{1,0:T(8,128)(2,1)S(1)} %get-tuple-element.166), channel_id=1, source_target_pairs={{0,2},{1,3},{2,0},{3,1},{4,6},{5,7},{6,4},{7,5},{8,10},{9,11},{10,... | collective-permute-start | bytes 393224 | tf_op jit(solution)/shard_map/ppermute | solution.py:398
  38.8 15.9 %copy-start.7 = (bf16[8192,256]{1,0:T(8,128)(2,1)S(1)}, bf16[8192,256]{1,0:T(8,128)(2,1)}, u32[]{:S(2)}) copy-start(bf16[8192,256]{1,0:T(8,128)(2,1)} %cached.21) | copy-start | bytes 12582916
  54.1 7.5 %collective-permute-start.10 = (bf16[256,256]{1,0:T(8,128)(2,1)}, bf16[256,256]{1,0:T(8,128)(2,1)S(1)}, u32[]{:S(2)}, u32[]{:S(2)}) collective-permute-start(bf16[256,256]{1,0:T(8,128)(2,1)} %get-tuple-element.164), channel_id=1, source_target_pairs={{0,1},{1,2},{2,3},{3,0},{4,5},{5,6},{6,7},{7,4},{8,9},{9,10},{10,1... | collective-permute-start | bytes 393224 | tf_op jit(solution)/shard_map/ppermute | solution.py:398
  59.6 6.8 %copy-start.31 = (bf16[128,2048]{1,0:T(8,128)(2,1)}, bf16[128,2048]{1,0:T(8,128)(2,1)S(1)}, u32[]{:S(2)}) copy-start(bf16[128,2048]{1,0:T(8,128)(2,1)S(1)} %collective-permute-done.5.piece) | copy-start | bytes 1572868
  59.6 6.8 %collective-permute-start.7 = (bf16[128,2048]{1,0:T(8,128)(2,1)S(1)}, bf16[128,2048]{1,0:T(8,128)(2,1)S(1)}, u32[]{:S(2)}, u32[]{:S(2)}) collective-permute-start(bf16[128,2048]{1,0:T(8,128)(2,1)S(1)} %collective-permute-done.5.piece), channel_id=1, source_target_pairs={{1,2},{2,3},{5,6},{6,7},{9,10},{10,11},{13,14},{14,15},{17,18},{18... | collective-permute-start | bytes 1572872 | tf_op jit(solution)/shard_map/ppermute | solution.py:427
  60.3 14.3 %collective-permute-start.8 = (bf16[128,2048]{1,0:T(8,128)(2,1)}, bf16[128,2048]{1,0:T(8,128)(2,1)S(1)}, u32[]{:S(2)}, u32[]{:S(2)}) collective-permute-start(bf16[128,2048]{1,0:T(8,128)(2,1)} %collective-permute-done.6.piece), channel_id=1, source_target_pairs={{1,0},{2,1},{5,4},{6,5},{9,8},{10,9},{13,12},{14,13},{17,16},{18,1... | collective-permute-start | bytes 1572872 | tf_op jit(solution)/shard_map/ppermute | solution.py:428
  61.6 14.9 %collective-permute-start.13 = (bf16[1024,256]{1,0:T(8,128)(2,1)S(1)}, bf16[1024,256]{1,0:T(8,128)(2,1)S(1)}, u32[]{:S(2)}, u32[]{:S(2)}) collective-permute-start(bf16[1024,256]{1,0:T(8,128)(2,1)S(1)} %copy-done.17), channel_id=1, source_target_pairs={{0,8},{4,12},{8,0},{12,4},{16,24},{20,28},{24,16},{28,20},{1,9},{5... | collective-permute-start | bytes 1572872 | tf_op jit(solution)/shard_map/ppermute | solution.py:253
  63.2 34.3 %collective-permute-start.14 = (bf16[1024,256]{1,0:T(8,128)(2,1)S(1)}, bf16[1024,256]{1,0:T(8,128)(2,1)}, u32[]{:S(2)}, u32[]{:S(2)}) collective-permute-start(bf16[1024,256]{1,0:T(8,128)(2,1)S(1)} %copy-done.17), channel_id=1, source_target_pairs={{0,16},{4,20},{8,24},{12,28},{16,0},{20,4},{24,8},{28,12},{1,17},{... | collective-permute-start | bytes 1572872 | tf_op jit(solution)/shard_map/ppermute | solution.py:253
  64.7 32.8 %collective-permute-start.15 = (bf16[1024,256]{1,0:T(8,128)(2,1)S(1)}, bf16[1024,256]{1,0:T(8,128)(2,1)S(1)}, u32[]{:S(2)}, u32[]{:S(2)}) collective-permute-start(bf16[1024,256]{1,0:T(8,128)(2,1)S(1)} %pad_maximum_fusion.refs_4_), channel_id=1, source_target_pairs={{0,8},{4,12},{8,0},{12,4},{16,24},{20,28},{24,16},{28,20},{1,9},{5... | collective-permute-start | bytes 1572872 | tf_op jit(solution)/shard_map/ppermute | solution.py:253
  66.4 31.1 %collective-permute-start.16 = (bf16[1024,256]{1,0:T(8,128)(2,1)S(1)}, bf16[1024,256]{1,0:T(8,128)(2,1)S(1)}, u32[]{:S(2)}, u32[]{:S(2)}) collective-permute-start(bf16[1024,256]{1,0:T(8,128)(2,1)S(1)} %pad_maximum_fusion.refs_4_), channel_id=1, source_target_pairs={{0,16},{4,20},{8,24},{12,28},{16,0},{20,4},{24,8},{28,12},{1,17},{... | collective-permute-start | bytes 1572872 | tf_op jit(solution)/shard_map/ppermute | solution.py:253
  74.5 23.6 %collective-permute-start.4 = (bf16[128,2048]{1,0:T(8,128)(2,1)S(1)}, bf16[128,2048]{1,0:T(8,128)(2,1)}, u32[]{:S(2)}, u32[]{:S(2)}) collective-permute-start(bf16[128,2048]{1,0:T(8,128)(2,1)S(1)} %broadcast_select_fusion.1.piece), channel_id=1, source_target_pairs={{2,3},{1,0},{6,7},{5,4},{10,11},{9,8},{14,15},{13,12},{18,19},{17,... | collective-permute-start | bytes 1572872 | tf_op jit(solution)/shard_map/ppermute | solution.py:430
  77.4 22.3 %collective-permute-start.9 = (bf16[128,2048]{1,0:T(8,128)(2,1)S(1)}, bf16[128,2048]{1,0:T(8,128)(2,1)}, u32[]{:S(2)}, u32[]{:S(2)}) collective-permute-start(bf16[128,2048]{1,0:T(8,128)(2,1)S(1)} %broadcast_select_fusion.piece), channel_id=1, source_target_pairs={{2,3},{1,0},{6,7},{5,4},{10,11},{9,8},{14,15},{13,12},{18,19},{17,... | collective-permute-start | bytes 1572872 | tf_op jit(solution)/shard_map/ppermute | solution.py:430
  93.9 20.6 %copy-start.39 = (s32[1,256]{1,0:T(1,128)S(1)}, s32[1,256]{1,0:T(1,128)}, u32[]{:S(2)}) copy-start(s32[1,256]{1,0:T(1,128)} %param.12) | copy-start | bytes 3076
  97.5 3.7 %collective-permute-start.17 = (bf16[1024,256]{1,0:T(8,128)(2,1)S(1)}, bf16[1024,256]{1,0:T(8,128)(2,1)S(1)}, u32[]{:S(2)}, u32[]{:S(2)}) collective-permute-start(bf16[1024,256]{1,0:T(8,128)(2,1)S(1)} %copy-done.17), channel_id=1, source_target_pairs={{0,4},{4,0},{8,12},{12,8},{16,20},{20,16},{24,28},{28,24},{1,5},{5... | collective-permute-start | bytes 1572872 | tf_op jit(solution)/shard_map/ppermute | solution.py:253
  97.6 4.4 %collective-permute-start.18 = (bf16[1024,256]{1,0:T(8,128)(2,1)S(1)}, bf16[1024,256]{1,0:T(8,128)(2,1)S(1)}, u32[]{:S(2)}, u32[]{:S(2)}) collective-permute-start(bf16[1024,256]{1,0:T(8,128)(2,1)S(1)} %copy-done.19), channel_id=1, source_target_pairs={{0,4},{4,0},{8,12},{12,8},{16,20},{20,16},{24,28},{28,24},{1,5},{5... | collective-permute-start | bytes 1572872 | tf_op jit(solution)/shard_map/ppermute | solution.py:253
  98.1 5.2 %collective-permute-start.19 = (bf16[1024,256]{1,0:T(8,128)(2,1)}, bf16[1024,256]{1,0:T(8,128)(2,1)S(1)}, u32[]{:S(2)}, u32[]{:S(2)}) collective-permute-start(bf16[1024,256]{1,0:T(8,128)(2,1)} %collective-permute-done.14.refs_4_), channel_id=1, source_target_pairs={{0,4},{4,0},{8,12},{12,8},{16,20},{20,16},{24,28},{28,24},{1,5},{5... | collective-permute-start | bytes 1572872 | tf_op jit(solution)/shard_map/ppermute | solution.py:253
  98.2 14.6 %collective-permute-start.20 = (bf16[1024,256]{1,0:T(8,128)(2,1)}, bf16[1024,256]{1,0:T(8,128)(2,1)}, u32[]{:S(2)}, u32[]{:S(2)}) collective-permute-start(bf16[1024,256]{1,0:T(8,128)(2,1)} %collective-permute-done.14.refs_4_), channel_id=1, source_target_pairs={{0,8},{4,12},{8,0},{12,4},{16,24},{20,28},{24,16},{28,20},{1,9},{5... | collective-permute-start | bytes 1572872 | tf_op jit(solution)/shard_map/ppermute | solution.py:253
  99.7 14.1 %collective-permute-start.25 = (bf16[1024,256]{1,0:T(8,128)(2,1)S(1)}, bf16[1024,256]{1,0:T(8,128)(2,1)}, u32[]{:S(2)}, u32[]{:S(2)}) collective-permute-start(bf16[1024,256]{1,0:T(8,128)(2,1)S(1)} %collective-permute-done.15.refs_6_), channel_id=1, source_target_pairs={{0,16},{4,20},{8,24},{12,28},{16,0},{20,4},{24,8},{28,12},{1,17},{... | collective-permute-start | bytes 1572872 | tf_op jit(solution)/shard_map/ppermute | solution.py:253
  102.0 26.4 %collective-permute-start.23 = (bf16[1024,256]{1,0:T(8,128)(2,1)S(1)}, bf16[1024,256]{1,0:T(8,128)(2,1)}, u32[]{:S(2)}, u32[]{:S(2)}) collective-permute-start(bf16[1024,256]{1,0:T(8,128)(2,1)S(1)} %collective-permute-done.15.refs_6_), channel_id=1, source_target_pairs={{0,4},{4,0},{8,12},{12,8},{16,20},{20,16},{24,28},{28,24},{1,5},{5... | collective-permute-start | bytes 1572872 | tf_op jit(solution)/shard_map/ppermute | solution.py:253
  102.8 25.5 %collective-permute-start.22 = (bf16[1024,256]{1,0:T(8,128)(2,1)S(1)}, bf16[1024,256]{1,0:T(8,128)(2,1)}, u32[]{:S(2)}, u32[]{:S(2)}) collective-permute-start(bf16[1024,256]{1,0:T(8,128)(2,1)S(1)} %pad_maximum_fusion.refs_4_), channel_id=1, source_target_pairs={{0,4},{4,0},{8,12},{12,8},{16,20},{20,16},{24,28},{28,24},{1,5},{5... | collective-permute-start | bytes 1572872 | tf_op jit(solution)/shard_map/ppermute | solution.py:253
  104.1 24.2 %collective-permute-start.24 = (bf16[1024,256]{1,0:T(8,128)(2,1)S(1)}, bf16[1024,256]{1,0:T(8,128)(2,1)}, u32[]{:S(2)}, u32[]{:S(2)}) collective-permute-start(bf16[1024,256]{1,0:T(8,128)(2,1)S(1)} %collective-permute-done.16.refs_8_), channel_id=1, source_target_pairs={{0,4},{4,0},{8,12},{12,8},{16,20},{20,16},{24,28},{28,24},{1,5},{5... | collective-permute-start | bytes 1572872 | tf_op jit(solution)/shard_map/ppermute | solution.py:253
  112.7 15.6 %collective-permute-start.21 = (bf16[1024,256]{1,0:T(8,128)(2,1)}, bf16[1024,256]{1,0:T(8,128)(2,1)}, u32[]{:S(2)}, u32[]{:S(2)}) collective-permute-start(bf16[1024,256]{1,0:T(8,128)(2,1)} %collective-permute-done.20.refs_6_), channel_id=1, source_target_pairs={{0,4},{4,0},{8,12},{12,8},{16,20},{20,16},{24,28},{28,24},{1,5},{5... | collective-permute-start | bytes 1572872 | tf_op jit(solution)/shard_map/ppermute | solution.py:253
  113.8 14.6 %collective-permute-start.26 = (bf16[1024,256]{1,0:T(8,128)(2,1)}, bf16[1024,256]{1,0:T(8,128)(2,1)}, u32[]{:S(2)}, u32[]{:S(2)}) collective-permute-start(bf16[1024,256]{1,0:T(8,128)(2,1)} %collective-permute-done.25.refs_10_), channel_id=1, source_target_pairs={{0,4},{4,0},{8,12},{12,8},{16,20},{20,16},{24,28},{28,24},{1,5},{5... | collective-permute-start | bytes 1572872 | tf_op jit(solution)/shard_map/ppermute | solution.py:253
  138.5 14.1 %copy-start.11 = (bf16[256,256]{1,0:T(8,128)(2,1)S(1)}, bf16[256,256]{1,0:T(8,128)(2,1)}, u32[]{:S(2)}) copy-start(bf16[256,256]{1,0:T(8,128)(2,1)} %copy-done.10) | copy-start | bytes 393220
  138.5 22.8 %copy-start.20 = (bf16[1024,256]{1,0:T(8,128)(2,1)S(1)}, bf16[1024,256]{1,0:T(8,128)(2,1)}, u32[]{:S(2)}) copy-start(bf16[1024,256]{1,0:T(8,128)(2,1)} %copy-done.18) | copy-start | bytes 1572868
  138.5 7.5 %collective-permute-start.27 = (bf16[2,1024,128]{2,1,0:T(8,128)(2,1)}, bf16[2,1024,128]{2,1,0:T(8,128)(2,1)}, u32[]{:S(2)}, u32[]{:S(2)}) collective-permute-start(bf16[2,1024,128]{2,1,0:T(8,128)(2,1)} %get-tuple-element.124), channel_id=1, source_target_pairs={{0,4},{4,0},{8,12},{12,8},{16,20},{20,16},{24,28},{28,24},{1,5},{5... | collective-permute-start | bytes 1572872 | tf_op jit(solution)/shard_map/ppermute | solution.py:253
  139.1 7.0 %collective-permute-start.28 = (bf16[2,1024,128]{2,1,0:T(8,128)(2,1)}, bf16[2,1024,128]{2,1,0:T(8,128)(2,1)}, u32[]{:S(2)}, u32[]{:S(2)}) collective-permute-start(bf16[2,1024,128]{2,1,0:T(8,128)(2,1)} %get-tuple-element.125), channel_id=1, source_target_pairs={{0,4},{4,0},{8,12},{12,8},{16,20},{20,16},{24,28},{28,24},{1,5},{5... | collective-permute-start | bytes 1572872 | tf_op jit(solution)/shard_map/ppermute | solution.py:253
  139.2 17.0 %collective-permute-start.34 = (bf16[2,1024,128]{2,1,0:T(8,128)(2,1)}, bf16[2,1024,128]{2,1,0:T(8,128)(2,1)}, u32[]{:S(2)}, u32[]{:S(2)}) collective-permute-start(bf16[2,1024,128]{2,1,0:T(8,128)(2,1)} %get-tuple-element.139), channel_id=1, source_target_pairs={{0,4},{4,0},{8,12},{12,8},{16,20},{20,16},{24,28},{28,24},{1,5},{5... | collective-permute-start | bytes 1572872 | tf_op jit(solution)/shard_map/ppermute | solution.py:253
  139.6 18.9 %collective-permute-start.35 = (bf16[2,1024,128]{2,1,0:T(8,128)(2,1)}, bf16[2,1024,128]{2,1,0:T(8,128)(2,1)}, u32[]{:S(2)}, u32[]{:S(2)}) collective-permute-start(bf16[2,1024,128]{2,1,0:T(8,128)(2,1)} %get-tuple-element.140), channel_id=1, source_target_pairs={{0,4},{4,0},{8,12},{12,8},{16,20},{20,16},{24,28},{28,24},{1,5},{5... | collective-permute-start | bytes 1572872 | tf_op jit(solution)/shard_map/ppermute | solution.py:253
  148.6 19.4 %copy-start.13 = (f32[2,1024,128]{2,1,0:T(8,128)S(1)}, f32[2,1024,128]{2,1,0:T(8,128)}, u32[]{:S(2)}) copy-start(f32[2,1024,128]{2,1,0:T(8,128)} %get-tuple-element.137.mine_a) | copy-start | bytes 3145732
  148.6 19.4 %copy-start.14 = (f32[2,1024,128]{2,1,0:T(8,128)S(1)}, f32[2,1024,128]{2,1,0:T(8,128)}, u32[]{:S(2)}) copy-start(f32[2,1024,128]{2,1,0:T(8,128)} %get-tuple-element.138.mine_b) | copy-start | bytes 3145732
  150.1 19.3 %collective-permute-start.29 = (bf16[2,1024,128]{2,1,0:T(8,128)(2,1)S(1)}, bf16[2,1024,128]{2,1,0:T(8,128)(2,1)S(1)}, u32[]{:S(2)}, u32[]{:S(2)}) collective-permute-start(bf16[2,1024,128]{2,1,0:T(8,128)(2,1)S(1)} %get-tuple-element.126), channel_id=1, source_target_pairs={{0,8},{4,12},{8,0},{12,4},{16,24},{20,28},{24,16},{28,20},{1,9},{5... | collective-permute-start | bytes 1572872 | tf_op jit(solution)/shard_map/ppermute | solution.py:253
  151.1 18.3 %collective-permute-start.30 = (bf16[2,1024,128]{2,1,0:T(8,128)(2,1)S(1)}, bf16[2,1024,128]{2,1,0:T(8,128)(2,1)S(1)}, u32[]{:S(2)}, u32[]{:S(2)}) collective-permute-start(bf16[2,1024,128]{2,1,0:T(8,128)(2,1)S(1)} %get-tuple-element.127), channel_id=1, source_target_pairs={{0,16},{4,20},{8,24},{12,28},{16,0},{20,4},{24,8},{28,12},{1,17},{... | collective-permute-start | bytes 1572872 | tf_op jit(solution)/shard_map/ppermute | solution.py:253
  152.6 16.8 %collective-permute-start.31 = (bf16[256,256]{1,0:T(8,128)(2,1)S(1)}, bf16[256,256]{1,0:T(8,128)(2,1)S(1)}, u32[]{:S(2)}, u32[]{:S(2)}) collective-permute-start(bf16[256,256]{1,0:T(8,128)(2,1)S(1)} %copy-done.11), channel_id=1, source_target_pairs={{0,1},{1,2},{2,3},{3,0},{4,5},{5,6},{6,7},{7,4},{8,9},{9,10},{10,1... | collective-permute-start | bytes 393224 | tf_op jit(solution)/shard_map/ppermute | solution.py:462
  156.2 13.2 %collective-permute-start.32 = (bf16[256,256]{1,0:T(8,128)(2,1)S(1)}, bf16[256,256]{1,0:T(8,128)(2,1)S(1)}, u32[]{:S(2)}, u32[]{:S(2)}) collective-permute-start(bf16[256,256]{1,0:T(8,128)(2,1)S(1)} %copy-done.11), channel_id=1, source_target_pairs={{0,2},{1,3},{2,0},{3,1},{4,6},{5,7},{6,4},{7,5},{8,10},{9,11},{10,... | collective-permute-start | bytes 393224 | tf_op jit(solution)/shard_map/ppermute | solution.py:462
  158.5 10.9 %collective-permute-start.33 = (bf16[256,256]{1,0:T(8,128)(2,1)S(1)}, bf16[256,256]{1,0:T(8,128)(2,1)S(1)}, u32[]{:S(2)}, u32[]{:S(2)}) collective-permute-start(bf16[256,256]{1,0:T(8,128)(2,1)S(1)} %copy-done.11), channel_id=1, source_target_pairs={{0,3},{1,0},{2,1},{3,2},{4,7},{5,4},{6,5},{7,6},{8,11},{9,8},{10,9... | collective-permute-start | bytes 393224 | tf_op jit(solution)/shard_map/ppermute | solution.py:462
  169.5 6.9 %collective-permute-start.36 = (bf16[1024,128]{1,0:T(8,128)(2,1)S(1)}, bf16[1024,128]{1,0:T(8,128)(2,1)S(1)}, u32[]{:S(2)}, u32[]{:S(2)}) collective-permute-start(bf16[1024,128]{1,0:T(8,128)(2,1)S(1)} %get-tuple-element.145), channel_id=1, source_target_pairs={{0,16},{4,20},{8,24},{12,28},{16,0},{20,4},{24,8},{28,12},{1,17},{... | collective-permute-start | bytes 786440 | tf_op jit(solution)/shard_map/ppermute | solution.py:253
  170.1 6.6 %collective-permute-start.37 = (bf16[1024,128]{1,0:T(8,128)(2,1)S(1)}, bf16[1024,128]{1,0:T(8,128)(2,1)S(1)}, u32[]{:S(2)}, u32[]{:S(2)}) collective-permute-start(bf16[1024,128]{1,0:T(8,128)(2,1)S(1)} %get-tuple-element.146), channel_id=1, source_target_pairs={{0,8},{4,12},{8,0},{12,4},{16,24},{20,28},{24,16},{28,20},{1,9},{5... | collective-permute-start | bytes 786440 | tf_op jit(solution)/shard_map/ppermute | solution.py:253
  (30 other events, 68.7 us)

commit v6 on v4

--- a/solution.py
+++ b/solution.py
@@ -1,3 +1,4 @@
+import functools
 import math
 
 import jax
@@ -8,8 +9,7 @@
 from jax.sharding import PartitionSpec as P
 
 HD = 128
-VMEM_STREAM = 56 * 1024 * 1024
-VMEM_PART = 40 * 1024 * 1024
+VMEM_STREAM = 60 * 1024 * 1024
 VMEM_WHOLE = 24 * 1024 * 1024
 
 
@@ -81,7 +81,9 @@
     )(place, *arrays)
 
 
-def absorb_kernel(place, chunk, cached, total, held, total_out, held_out):
+def absorb_kernel(place, chunk, cached, total, *refs):
+    *_, total_out, held_out = refs
+
     @pl.when(pl.program_id(0) == 0)
     def _():
         total_out[...] = total[...]
@@ -93,20 +95,14 @@
 def absorb(chunk, index, cached, total, held, n_chunks):
     length, feats = chunk.shape
     cols = cached.shape[1]
-    step = min(feats, 512)
+    step = min(feats, 1024)
     steps = feats // step
     inside = (index >= 0) & (index < n_chunks)
     place = jnp.stack([jnp.clip(index, 0, n_chunks - 1), jnp.where(inside, index, n_chunks)])
-    shape = jax.ShapeDtypeStruct((n_chunks + 1, feats, length), chunk.dtype)
-    out_total = jax.ShapeDtypeStruct(total.shape, jnp.float32)
+    shape = jax.ShapeDtypeStruct((8 * n_chunks, feats, length), chunk.dtype)
     whole = pl.BlockSpec((length, cols), lambda i, place: (0, 0))
-    operands = [chunk, cached, total] + ([] if held is None else [held])
-
-    def kernel(place, chunk, cached, total, *refs):
-        absorb_kernel(place, chunk, cached, total, None, *refs[-2:])
-
     return pl.pallas_call(
-        kernel,
+        absorb_kernel,
         grid_spec=pltpu.PrefetchScalarGridSpec(
             num_scalar_prefetch=1,
             grid=(steps,),
@@ -121,16 +117,16 @@
                 pl.BlockSpec((1, step, length), lambda i, place: (place[1], i, 0)),
             ],
         ),
-        out_shape=[out_total, shape],
+        out_shape=[jax.ShapeDtypeStruct(total.shape, jnp.float32), shape],
         input_output_aliases={} if held is None else {4: 1},
         cost_estimate=pl.CostEstimate(
             flops=2 * length * feats * cols,
             bytes_accessed=4 * length * feats + 2 * feats * cols,
             transcendentals=0,
         ),
-        compiler_params=pltpu.CompilerParams(vmem_limit_bytes=VMEM_PART),
+        compiler_params=pltpu.CompilerParams(vmem_limit_bytes=VMEM_STREAM),
         name="absorb",
-    )(place, *operands)
+    )(place, chunk, cached, total, *([] if held is None else [held]))
 
 
 def attention_kernel(place, projected, queries, d_out, allowed, d_queries, d_projected):
@@ -177,58 +173,83 @@
     )
 
 
-def weight_kernel(place, chunk_a, chunk_b, d_projected, *refs):
-    *added, out_a, out_b = refs
-    half = out_a.shape[2]
-    for side, (chunk, out) in enumerate(((chunk_a, out_a), (chunk_b, out_b))):
-        columns = d_projected[:, side * half : (side + 1) * half]
-        total = jnp.dot(chunk[0], columns, preferred_element_type=jnp.float32)
-        if added:
-            total = total + added[side][0].astype(jnp.float32)
-        out[0] = total.astype(out.dtype)
-
-
-def weight_parts(held, d_projected, place, added, dtype, name):
+SENT = ((0, 0, 0), (0, 1, 0), (1, 0, 1), (2, 1, 1))
+KEPT = ((1, 1, 0), (2, 0, 0), (3, 0, 1), (3, 1, 1))
+
+
+def weight_kernel(groups, place, held, d_projected, *refs):
+    *refs, buffer, sems = refs
+    n_out = 2 * len(groups)
+    added, outs = refs[:-n_out], refs[-n_out:]
+    rows = buffer.shape[1]
+    half = d_projected.shape[1] // 2
+    block = min(rows, 256)
+    start = pl.multiple_of(place[4] * rows, rows)
+    chunks = sorted({chunk for group in groups for chunk, _, _ in group})
+    copies = {}
+    for chunk in chunks:
+        copies[chunk] = pltpu.make_async_copy(
+            held.at[place[chunk], pl.ds(start, rows), :], buffer.at[chunk], sems.at[chunk]
+        )
+        copies[chunk].start()
+    for chunk in chunks:
+        copies[chunk].wait()
+        for r in range(0, rows, block):
+            wanted = [
+                (side, 2 * g + side, position)
+                for g, group in enumerate(groups)
+                for which, side, position in group
+                if which == chunk
+            ]
+            first, last = min(w[0] for w in wanted), max(w[0] for w in wanted)
+            total = jnp.dot(
+                buffer[chunk, r : r + block, :],
+                d_projected[:, first * half : (last + 1) * half],
+                preferred_element_type=jnp.float32,
+            )
+            for side, n, position in wanted:
+                part = total[:, (side - first) * half : (side - first + 1) * half]
+                if added:
+                    part = part + added[n][position, r : r + block, :].astype(jnp.float32)
+                outs[n][position, r : r + block, :] = part.astype(outs[n].dtype)
+
+
+def weight_parts(held, d_projected, place, groups, added, dtype, name):
     length, cols = d_projected.shape
     rows = held.shape[1] // 2
-    half = cols // 2
-    out = pl.BlockSpec((1, rows, half), lambda k, place: (k, 0, 0))
-    shape = jax.ShapeDtypeStruct((2, rows, half), dtype)
+    shape = jax.ShapeDtypeStruct((2, rows, cols // 2), dtype)
+    vmem = pl.BlockSpec(memory_space=pltpu.VMEM)
+    n_out = 2 * len(groups)
     return pl.pallas_call(
-        weight_kernel,
-        grid_spec=pltpu.PrefetchScalarGridSpec(
-            num_scalar_prefetch=1,
-            grid=(2,),
-            in_specs=[
-                pl.BlockSpec((1, rows, length), lambda k, place: (place[k], place[4], 0)),
-                pl.BlockSpec((1, rows, length), lambda k, place: (place[2 + k], place[4], 0)),
-                pl.BlockSpec((length, cols), lambda k, place: (0, 0)),
-            ]
-            + [out] * len(added),
-            out_specs=[out, out],
-        ),
-        out_shape=[shape, shape],
+        functools.partial(weight_kernel, groups),
+        in_specs=[pl.BlockSpec(memory_space=pltpu.SMEM), pl.BlockSpec(memory_space=pl.ANY)]
+        + [vmem] * (1 + len(added)),
+        out_specs=[vmem] * n_out,
+        out_shape=[shape] * n_out,
+        scratch_shapes=[
+            pltpu.VMEM((4, rows, length), held.dtype),
+            pltpu.SemaphoreType.DMA((4,)),
+        ],
         cost_estimate=pl.CostEstimate(
-            flops=4 * length * rows * cols, bytes_accessed=8 * rows * cols, transcendentals=0
-        ),
-        compiler_params=pltpu.CompilerParams(vmem_limit_bytes=VMEM_PART),
+            flops=4 * length * rows * cols * len(groups),
+            bytes_accessed=8 * rows * cols * len(groups),
+            transcendentals=0,
+        ),
+        compiler_params=pltpu.CompilerParams(vmem_limit_bytes=VMEM_WHOLE),
         name=name,
-    )(place, held, held, d_projected, *added)
+    )(place, held, d_projected, *added)
 
 
 def combine_kernel(place, keep_a, got_a, keep_b, got_b, out_a, out_b):
-    sides = ((keep_a, got_a, out_a), (keep_b, got_b, out_b))
-    for side, (keep, got, out) in enumerate(sides):
-        which = place[side]
-        out[...] = (keep[which] + got[which].astype(jnp.float32)).astype(out.dtype)
+    for keep, got, out in ((keep_a, got_a, out_a), (keep_b, got_b, out_b)):
+        out[...] = (keep[0] + got[0].astype(jnp.float32)).astype(out.dtype)
 
 
 def finish_kernel(place, keep_a, got_a, keep_b, got_b, last_a, last_b, out):
     half = last_a.shape[1]
     sides = ((keep_a, got_a, last_a), (keep_b, got_b, last_b))
     for side, (keep, got, last) in enumerate(sides):
-        which = place[side]
-        total = keep[which] + got[which].astype(jnp.float32) + last[...].astype(jnp.float32)
+        total = keep[1] + got[1].astype(jnp.float32) + last[...].astype(jnp.float32)
         out[:, side * half : (side + 1) * half] = total
 
 
@@ -241,28 +262,27 @@
     return index % 2, (index // 2) % 2, index // 4, swap
 
 
-def weight_sum(held, d_projected):
+def weight_sum(held, d_projected, beside):
     core, x, y, swap = plane()
     rows, cols = held.shape[1] // 2, d_projected.shape[1]
-    send = [1 - x, 3 - x, 2 - 2 * y, 3 - 2 * y]
-    keep = [x, 2 + x, 2 * y, 2 * y + 1]
-
-    def parts(chunks, which, added, dtype, name):
+    none = jnp.zeros((1,), jnp.int32)
+    chunks = [3 - x - 2 * y, 1 - x + 2 * y, x + 2 - 2 * y, x + 2 * y]
+
+    def parts(which, groups, added, dtype, name):
         place = jnp.stack(chunks + [which])
-        return weight_parts(held, d_projected, place, added, dtype, name)
-
-    theirs = parts(send, 1 - core, [], jnp.bfloat16, "weight_send_other")
+        return weight_parts(held, d_projected, place, groups, added, dtype, name)
+
+    theirs = parts(1 - core, (SENT, KEPT), [], jnp.bfloat16, "weight_other")
     theirs = [swap(part, 1) for part in theirs]
-    rest = parts(keep, 1 - core, [], jnp.bfloat16, "weight_keep_other")
-    rest = [swap(part, 1) for part in rest]
-    send_a, send_b = parts(send, core, theirs, jnp.bfloat16, "weight_send")
+    send_a, send_b = parts(core, (SENT,), theirs[:2], jnp.bfloat16, "weight_send")
     got_a, got_b = swap(send_a, 2), swap(send_b, 4)
-    keep_a, keep_b = parts(keep, core, rest, jnp.float32, "weight_keep")
+    keep_a, keep_b = parts(core, (KEPT,), theirs[2:], jnp.float32, "weight_keep")
+    got_a, got_b, beside = lax.optimization_barrier((got_a, got_b, beside))
 
     small = jax.ShapeDtypeStruct((rows, cols // 2), jnp.bfloat16)
     arrays = [keep_a, got_a, keep_b, got_b]
     last_a, last_b = on_chip(
-        combine_kernel, jnp.stack([1 - y, 1 - x]), arrays, [small] * 2, cols * rows, "weight_combine"
+        combine_kernel, none, arrays, [small] * 2, cols * rows, "weight_combine"
     )
     last = [swap(last_a, 4), swap(last_b, 2)]
 
@@ -270,7 +290,7 @@
         ended, ready = lax.optimization_barrier((last, ready))
         (total,) = on_chip(
             finish_kernel,
-            jnp.stack([y, x]),
+            none,
             arrays + ended,
             [jax.ShapeDtypeStruct((rows, cols), jnp.float32)],
             2 * cols * rows,
@@ -278,31 +298,30 @@
         )
         return total, ready
 
-    return finish
-
-
-def gather_plane(own_cache, own_rows):
+    return finish, beside
+
+
+def gather_plane(own, gate):
     _, _, _, swap = plane()
-    cache, rows = {0: own_cache}, {0: own_rows}
-    for bit in (2, 4):
-        cache[bit] = swap(own_cache, bit)
-        rows[bit] = swap(own_rows, bit)
-    cache[6] = swap(cache[4], 2)
-    rows[6] = swap(rows[2], 4)
-    for bits in (0, 2, 4, 6):
-        cache[bits + 1] = swap(cache[bits], 1)
-        rows[bits + 1] = swap(rows[bits], 1)
-    return [cache[k] for k in range(8)], [rows[k] for k in range(8)]
-
-
-def place_rows_kernel(place, *refs):
+    half = own.shape[0] // 2
+    got = {0: own, 2: swap(own, 2), 4: swap(own, 4)}
+    got[1] = swap(own, 1)
+    (got, _) = lax.optimization_barrier((got, gate))
+    top, bottom = swap(got[4][:half], 2), swap(got[2][half:], 4)
+    got[3], got[5] = swap(got[2], 1), swap(got[4], 1)
+    near = [(got[k], got[k]) for k in range(6)]
+    return near + [(top, bottom), (swap(top, 1), swap(bottom, 1))]
+
+
+def place_rows_kernel(height, place, *refs):
     *pieces, out, sems = refs
-    height = pieces[0].shape[0]
     copies = []
     for k, piece in enumerate(pieces):
         start = pl.multiple_of((place[0] ^ k) * height, height)
         copies.append(
-            pltpu.make_async_copy(piece, out.at[pl.ds(start, height), :], sems.at[k])
+            pltpu.make_async_copy(
+                piece.at[pl.ds(0, height), :], out.at[pl.ds(start, height), :], sems.at[k]
+            )
         )
     for copy in copies:
         copy.start()
@@ -310,13 +329,13 @@
         copy.wait()
 
 
-def place_rows(pieces):
-    height, cols = pieces[0].shape
-    anywhere = pl.BlockSpec(memory_space=pl.ANY)
+def place_rows(pieces, height):
+    cols = pieces[0].shape[1]
     return pl.pallas_call(
-        place_rows_kernel,
-        in_specs=[pl.BlockSpec(memory_space=pltpu.SMEM)] + [anywhere] * len(pieces),
-        out_specs=anywhere,
+        functools.partial(place_rows_kernel, height),
+        in_specs=[pl.BlockSpec(memory_space=pltpu.SMEM)]
+        + [pl.BlockSpec(memory_space=pltpu.VMEM)] * len(pieces),
+        out_specs=pl.BlockSpec(memory_space=pl.ANY),
         out_shape=jax.ShapeDtypeStruct((height * len(pieces), cols), pieces[0].dtype),
         scratch_shapes=[pltpu.SemaphoreType.DMA((len(pieces),))],
         cost_estimate=pl.CostEstimate(
@@ -327,17 +346,17 @@
     )(lax.axis_index("dp").astype(jnp.int32).reshape(1), *pieces)
 
 
-def input_kernel(place, *refs):
+def input_kernel(offsets, place, *refs):
     *arrays, out = refs
     n_blocks = place.shape[0] - 1
     pieces, rows = arrays[:n_blocks], arrays[n_blocks:]
-    share = rows[0].shape[0] // n_blocks
-    for k, held in enumerate(rows):
+    share = out.shape[1] // len(rows)
+    for k, (held, offset) in enumerate(zip(rows, offsets)):
         total = jnp.zeros((out.shape[0], share), jnp.float32)
         for s, piece in enumerate(pieces):
             total = total + lax.dot_general(
                 piece[...],
-                held[s * share : (s + 1) * share, :],
+                held[offset + s * share : offset + (s + 1) * share, :],
                 (((1,), (1,)), ((), ())),
                 preferred_element_type=jnp.float32,
             )
@@ -345,12 +364,11 @@
         out[:, pl.ds(start, share)] = total.astype(out.dtype)
 
 
-def input_gradient(pieces, rows):
+def input_gradient(pieces, rows, offsets, feats):
     length, cols = pieces[0].shape
-    feats = sum(held.shape[0] for held in rows) // len(pieces)
     place = jnp.broadcast_to(lax.axis_index("dp").astype(jnp.int32), (len(pieces) + 1,))
     (d_tokens,) = on_chip(
-        input_kernel,
+        functools.partial(input_kernel, offsets),
         place,
         pieces + rows,
         [jax.ShapeDtypeStruct((length, feats), jnp.bfloat16)],
@@ -361,8 +379,10 @@
 
 
 def make_body(n_dp, n_z):
-    ring = [[(z, (z + s) % n_z) for z in range(n_z)] for s in range(n_z)]
     tuned = n_dp == 8 and n_z == 4
+
+    def pair(value, s):
+        return lax.ppermute(value, "tensor", [(z, z ^ s) for z in range(n_z)])
 
     def body(tokens, queries, d_out, segments, cached, master, moment, second, grad):
         me_dp = lax.axis_index("dp").astype(jnp.int32)
@@ -375,10 +395,7 @@
         def block_for(z):
             return lax.dynamic_slice_in_dim(cached, z * feats + me_dp * share, share, 0)
 
-        blocks = [block_for(me_z)]
-        for s in range(1, n_z):
-            blocks.append(lax.ppermute(block_for((me_z + s) % n_z), "tensor", ring[s]))
-        own_rows = jnp.concatenate(blocks, axis=0)
+        blocks = [block_for(me_z)] + [pair(block_for(me_z ^ s), s) for s in range(1, n_z)]
 
         master_new, moment_new, second_new, own_cache = optimizer(
             cached, master, moment, second, grad
@@ -386,6 +403,8 @@
 
         total = jnp.zeros((length, cols), jnp.float32)
         total, held = absorb(tokens, me_z, cached, total, None, n_z)
+        if tuned:
+            bundle = jnp.concatenate([own_cache] + blocks, axis=0)
         from_low, from_high, merged = tokens, tokens, None
         for s in range(1, n_z):
             up = [(z, z + 1) for z in range(s - 1, n_z - 1)]
@@ -396,12 +415,16 @@
                 from_high = lax.ppermute(from_high, "tensor", down)
             else:
                 merged = lax.ppermute(merged, "tensor", up + down)
-            if s == 1:
-                from_low, from_high, own_cache, own_rows = lax.optimization_barrier(
-                    (from_low, from_high, own_cache, own_rows)
-                )
             if merged is None and 2 * s >= n_z:
                 merged = jnp.where(me_z >= s, from_low, from_high)
+            if tuned and s == 1:
+                from_low, from_high, held, bundle = lax.optimization_barrier(
+                    (from_low, from_high, held, bundle)
+                )
+            if tuned and s == n_z - 1:
+                gathered = gather_plane(bundle, merged)
+                new_cache = place_rows([cache for cache, _ in gathered], own_cache.shape[0])
+                total, new_cache, gathered = lax.optimization_barrier((total, new_cache, gathered))
             if merged is None:
                 total, held = absorb(from_low, low, cached, total, held, n_z)
                 total, held = absorb(from_high, high, cached, total, held, n_z)
@@ -414,26 +437,23 @@
         allowed = (doc_ids[:, None] == doc_ids[None, :]) & (position[:, None] <= position[None, :])
         allowed = allowed.astype(jnp.float32)
 
-        if tuned:
-            cache_pieces, row_pieces = gather_plane(own_cache, own_rows)
-            new_cache = place_rows(cache_pieces)
-            total, new_cache, row_pieces = lax.optimization_barrier((total, new_cache, row_pieces))
-        else:
-            new_cache = lax.all_gather(own_cache, "dp", axis=0, tiled=True)
-            row_pieces = lax.all_gather(own_rows, "dp", axis=0)
-
         d_queries, d_projected = attention_backward(
             total.astype(jnp.bfloat16), queries, d_out, allowed
         )
 
-        pieces = [d_projected] + [
-            lax.ppermute(d_projected, "tensor", ring[s]) for s in range(1, n_z)
-        ]
+        pieces = [d_projected]
+        s = 1
+        while s < n_z:
+            pieces = pieces + [pair(piece, s) for piece in pieces]
+            s *= 2
         if tuned:
-            finish = weight_sum(held, d_projected)
-            new_grad, d_tokens = finish(input_gradient(pieces, row_pieces))
+            finish, pieces = weight_sum(held, d_projected, pieces)
+            rows = [rows for _, rows in gathered]
+            offsets = [array.shape[0] - n_z * share for array in rows]
+            new_grad, d_tokens = finish(input_gradient(pieces, rows, offsets, feats))
         else:
-            rows = row_pieces.reshape(n_dp, n_z, share, cols)
+            new_cache = lax.all_gather(own_cache, "dp", axis=0, tiled=True)
+            rows = lax.all_gather(jnp.stack(blocks), "dp", axis=0)
             d_tokens = jnp.einsum(
                 "slc,ksfc->lkf", jnp.stack(pieces), rows, preferred_element_type=jnp.float32
             )

time: 265 us -> 182 us (0.69)
  Pallas kernels: 148 us -> 45.3 us
  waiting for transfers between devices: 62.8 us -> 89 us
  starting transfers between devices: 38.3 us -> 31.5 us
  other arithmetic: 1.94 us -> 5.68 us
  local copies, waits for them, and re-layouts: 12.3 us -> 8.91 us
    pallas_call x10 -> x9, Pallas kernels: 133 us -> 31 us  [the longest x5 17.2 us: absorb(): pl.pallas_call(absorb_kernel, grid_spec=pltpu.PrefetchScalarGridSpec(num_...]
    ppermute x1, waiting for transfers between devices: 0.01 us -> 23.3 us  [body(): merged = lax.ppermute(merged, 'tensor', up + down)]
    ppermute x2, waiting for transfers between devices: 0.01 us -> 22 us  [body(): from_high = lax.ppermute(from_high, 'tensor', down)]
    ppermute x22 -> x17, waiting for transfers between devices: 34 us -> 12.9 us  [swap(): return lax.ppermute(value, 'dp', [(i, i ^ bit) for i in range(8)])]
    unnamed x48 -> x21, local copies, waits for them, and re-layouts: 10.8 us -> 5.22 us
    ppermute x6, starting transfers between devices: 13.3 us -> 8.21 us  [pair(): return lax.ppermute(value, 'tensor', [(z, z ^ s) for z in range(n_z)])]
    ppermute x22 -> x17, starting transfers between devices: 13.5 us -> 11.9 us  [swap(): return lax.ppermute(value, 'dp', [(i, i ^ bit) for i in range(8)])]
  transfers between devices with their start and end apart: 33 -> 28, of which waited for: 11 -> 13; matrix products, arithmetic and copies ran while one was open for 1% -> 5% of each run, Pallas kernels for 53% -> 18%
where the time goes in v6:
time: 182 us; the launch traced here: 181 us
  waiting for transfers between devices  89 us (49%)
  Pallas kernels  45.3 us (25%)
  starting transfers between devices  31.5 us (17%)
  local copies, waits for them, and re-layouts  8.91 us (5%)
  other arithmetic  5.68 us (3%)
    ppermute x6, waiting for transfers between devices, pair(): return lax.ppermute(value, 'tensor', [(z, z ^ s) for z in range(n_z)])  30.9 us
    ppermute x1, waiting for transfers between devices, body(): merged = lax.ppermute(merged, 'tensor', up + down)  23.3 us
    ppermute x2, waiting for transfers between devices, body(): from_high = lax.ppermute(from_high, 'tensor', down)  22 us
    pallas_call x5, Pallas kernels, absorb(): pl.pallas_call(absorb_kernel, grid_spec=pltpu.PrefetchScalarGridSpec(num_...  17.2 us
    ppermute x17, waiting for transfers between devices, swap(): return lax.ppermute(value, 'dp', [(i, i ^ bit) for i in range(8)])  12.9 us
    ppermute x17, starting transfers between devices, swap(): return lax.ppermute(value, 'dp', [(i, i ^ bit) for i in range(8)])  11.9 us
    pallas_call x3, Pallas kernels, weight_parts(): pl.pallas_call(functools.partial(weight_kernel, groups), in_specs=[pl.Blo...  9.89 us
    pallas_call x4, Pallas kernels, on_chip(): pl.pallas_call(kernel, in_specs=[pl.BlockSpec(memory_space=pltpu.SMEM)] +...  9.33 us
  transfers between devices with their start and end apart: 28, of which 13 were waited for; matrix products, arithmetic and copies ran while one was open for 5% of the time, Pallas kernels for 18%

profile of v6, /device:TPU:0, one launch (start us, length us, event | category | flops | bytes accessed | tf_op | source)
XLA Modules:
  0.0 181.4 jit_solution(11229113851617533840)
XLA Ops:
  0.6 5.9 %collective-permute-start = (bf16[256,2048]{1,0:T(8,128)(2,1)}, bf16[256,2048]{1,0:T(8,128)(2,1)}, u32[]{:S(2)}, u32[]{:S(2)}) collective-permute-start(bf16[256,2048]{1,0:T(8,128)(2,1)} %chunk.1), channel_id=1, source_target_pairs={{0,1},{1,2},{2,3},{4,5},{5,6},{6,7},{8,9},{9,10},{10,11},{12,13},{... | collective-permute-start | bytes 3145736 | tf_op jit(solution)/shard_map/ppermute | solution.py:414
  6.5 1.3 collective-permute-start.1
  7.9 4.9 %optimizer.1 = (f32[1024,256]{1,0:T(8,128)}, f32[1024,256]{1,0:T(8,128)}, f32[1024,256]{1,0:T(8,128)}, bf16[1024,256]{1,0:T(8,128)(2,1)}) custom-call(s32[1]{0:T(128)} %bitcast.place, bf16[8192,256]{1,0:T(8,128)(2,1)} %cached.11, f32[1024,256]{1,0:T(8,128)} %master.1, f32[1024,256]{1,0:T(8,128)} %moment.1, f32[1024,256]{1,0:T(8,128)} %second.1, f32[1024,256]{1,0:T(8,128)} %grad.1), custom_call_target="tpu_custom_call" | custom-call | flops 10485760 | bytes 8388608 | tf_op jit(solution)/shard_map/optimizer/pallas_call | solution.py:51
  12.8 1.1 constant_dynamic-update-slice_fusion.3
  13.9 1.1 constant_dynamic-slice_fusion
  15.0 2.7 %collective-permute-start.2 = (bf16[256,256]{1,0:T(8,128)(2,1)S(1)}, bf16[256,256]{1,0:T(8,128)(2,1)S(1)}, u32[]{:S(2)}, u32[]{:S(2)}) collective-permute-start(bf16[256,256]{1,0:T(8,128)(2,1)S(1)} %get-tuple-element.115), channel_id=1, source_target_pairs={{0,1},{1,0},{2,3},{3,2},{4,5},{5,4},{6,7},{7,6},{8,9},{9,8},{10,11... | collective-permute-start | bytes 393224 | tf_op jit(solution)/shard_map/ppermute | solution.py:385
  17.7 2.6 %collective-permute-start.3 = (bf16[256,256]{1,0:T(8,128)(2,1)S(1)}, bf16[256,256]{1,0:T(8,128)(2,1)S(1)}, u32[]{:S(2)}, u32[]{:S(2)}) collective-permute-start(bf16[256,256]{1,0:T(8,128)(2,1)S(1)} %get-tuple-element.114), channel_id=1, source_target_pairs={{0,2},{1,3},{2,0},{3,1},{4,6},{5,7},{6,4},{7,5},{8,10},{9,11},{10,... | collective-permute-start | bytes 393224 | tf_op jit(solution)/shard_map/ppermute | solution.py:385
  21.7 3.5 %absorb.5 = (f32[256,256]{1,0:T(8,128)}, bf16[32,2048,256]{2,1,0:T(8,128)(2,1)}) custom-call(s32[2]{0:T(128)} %get-tuple-element.117.place, bf16[256,2048]{1,0:T(8,128)(2,1)} %chunk.1, bf16[8192,256]{1,0:T(8,128)(2,1)} %cached.11, f32[256,256]{1,0:T(8,128)} %broadcast_in_dim.8.total), custom_call_target="tpu_custom_call" | custom-call | flops 268435456 | bytes 3145728 | tf_op jit(solution)/shard_map/absorb/pallas_call | solution.py:104
  25.2 13.6 %collective-permute-done.2 = bf16[256,256]{1,0:T(8,128)(2,1)S(1)} collective-permute-done((bf16[256,256]{1,0:T(8,128)(2,1)S(1)}, bf16[256,256]{1,0:T(8,128)(2,1)S(1)}, u32[]{:S(2)}, u32[]{:S(2)}) %collective-permute-start.2) | collective-permute-done | bytes 131104 | tf_op jit(solution)/shard_map/ppermute | solution.py:385
  38.8 4.3 %collective-permute-done.3 = bf16[256,256]{1,0:T(8,128)(2,1)S(1)} collective-permute-done((bf16[256,256]{1,0:T(8,128)(2,1)S(1)}, bf16[256,256]{1,0:T(8,128)(2,1)S(1)}, u32[]{:S(2)}, u32[]{:S(2)}) %collective-permute-start.3) | collective-permute-done | bytes 131104 | tf_op jit(solution)/shard_map/ppermute | solution.py:385
  43.2 1.6 collective-permute-start.5
  44.9 1.3 collective-permute-start.6
  46.2 1.6 collective-permute-start.8
  47.8 1.5 collective-permute-start.9
  49.3 22.0 %collective-permute-done.6 = bf16[256,2048]{1,0:T(8,128)(2,1)} collective-permute-done((bf16[256,2048]{1,0:T(8,128)(2,1)}, bf16[256,2048]{1,0:T(8,128)(2,1)}, u32[]{:S(2)}, u32[]{:S(2)}) %collective-permute-start.6) | collective-permute-done | bytes 1048608 | tf_op jit(solution)/shard_map/ppermute | solution.py:415
  71.3 1.3 broadcast_select_fusion.chunk
  72.7 1.3 collective-permute-start.10
  74.0 23.3 %collective-permute-done.10.chunk = bf16[256,2048]{1,0:T(8,128)(2,1)} collective-permute-done((bf16[256,2048]{1,0:T(8,128)(2,1)S(1)}, bf16[256,2048]{1,0:T(8,128)(2,1)}, u32[]{:S(2)}, u32[]{:S(2)}) %collective-permute-start.10) | collective-permute-done | bytes 1048608 | tf_op jit(solution)/shard_map/ppermute | solution.py:417
  97.3 0.8 slice.6
  98.1 1.5 collective-permute-start.13
  100.4 1.5 collective-permute-start.15
  103.2 5.7 %collective-permute-done.13.refs_6_ = bf16[1024,256]{1,0:T(8,128)(2,1)} collective-permute-done((bf16[1024,256]{1,0:T(8,128)(2,1)}, bf16[1024,256]{1,0:T(8,128)(2,1)}, u32[]{:S(2)}, u32[]{:S(2)}) %collective-permute-start.13) | collective-permute-done | bytes 524320 | tf_op jit(solution)/shard_map/ppermute | solution.py:260
  108.9 2.0 %collective-permute-done.15.refs_10_ = bf16[1024,256]{1,0:T(8,128)(2,1)} collective-permute-done((bf16[1024,256]{1,0:T(8,128)(2,1)}, bf16[1024,256]{1,0:T(8,128)(2,1)}, u32[]{:S(2)}, u32[]{:S(2)}) %collective-permute-start.15) | collective-permute-done | bytes 524320 | tf_op jit(solution)/shard_map/ppermute | solution.py:260
  112.1 0.8 fusion.1.allowed
  113.0 3.4 %absorb.6 = (f32[256,256]{1,0:T(8,128)}, bf16[32,2048,256]{2,1,0:T(8,128)(2,1)}) custom-call(s32[2]{0:T(128)} %pad_add_fusion.3.place, bf16[256,2048]{1,0:T(8,128)(2,1)} %collective-permute-done.chunk, bf16[8192,256]{1,0:T(8,128)(2,1)} %cached.11, f32[256,256]{1,0:T(8,128)} %get-tuple-element.67.total, ...), custom_call_target="tpu_custom_call", output_to_operand_aliasing={{1}: (4, {})} | custom-call | flops 268435456 | bytes 3145728 | tf_op jit(solution)/shard_map/absorb/pallas_call | solution.py:104
  116.4 3.4 %absorb.7 = (f32[256,256]{1,0:T(8,128)}, bf16[32,2048,256]{2,1,0:T(8,128)(2,1)}) custom-call(s32[2]{0:T(128)} %get-tuple-element.118.place, bf16[256,2048]{1,0:T(8,128)(2,1)} %collective-permute-done.1.chunk, bf16[8192,256]{1,0:T(8,128)(2,1)} %cached.11, f32[256,256]{1,0:T(8,128)} %get-tuple-element.69.total, ...), custom_call_target="tpu_custom_call", output_to_operand_aliasing={{1}: (4, {})} | custom-call | flops 268435456 | bytes 3145728 | tf_op jit(solution)/shard_map/absorb/pallas_call | solution.py:104
  119.8 3.4 %absorb.8 = (f32[256,256]{1,0:T(8,128)}, bf16[32,2048,256]{2,1,0:T(8,128)(2,1)}) custom-call(s32[2]{0:T(128)} %pad_add_fusion.place, bf16[256,2048]{1,0:T(8,128)(2,1)} %copy-done.8, bf16[8192,256]{1,0:T(8,128)(2,1)} %cached.11, f32[256,256]{1,0:T(8,128)} %get-tuple-element.71.total, ...), custom_call_target="tpu_custom_call", output_to_operand_aliasing={{1}: (4, {})} | custom-call | flops 268435456 | bytes 3145728 | tf_op jit(solution)/shard_map/absorb/pallas_call | solution.py:104
  123.3 1.2 copy-done.1
  124.5 3.9 %place_rows.1 = bf16[8192,256]{1,0:T(8,128)(2,1)} custom-call(s32[1]{0:T(128)} %bitcast.place, bf16[2048,256]{1,0:T(8,128)(2,1)S(1)} %constant_dynamic-update-slice_fusion.refs_0_.refs_4_, bf16[2048,256]{1,0:T(8,128)(2,1)S(1)} %copy-done.1, bf16[2048,256]{1,0:T(8,128)(2,1)S(1)} %collective-permute-done.8.refs_2_.refs_6_, ...), custom_call_target="tpu_custom_call" | custom-call | bytes 8388608 | tf_op jit(solution)/shard_map/place_rows/pallas_call | solution.py:334
  128.5 3.4 %absorb.9 = (f32[256,256]{1,0:T(8,128)}, bf16[32,2048,256]{2,1,0:T(8,128)(2,1)}) custom-call(s32[2]{0:T(128)} %pad_add_fusion.4.place, bf16[256,2048]{1,0:T(8,128)(2,1)} %collective-permute-done.10.chunk, bf16[8192,256]{1,0:T(8,128)(2,1)} %cached.11, f32[256,256]{1,0:T(8,128)} %get-tuple-element.80.total, ...), custom_call_target="tpu_custom_call", output_to_operand_aliasing={{1}: (4, {})} | custom-call | flops 268435456 | bytes 3145728 | tf_op jit(solution)/shard_map/absorb/pallas_call | solution.py:104
  131.9 1.0 convert_element_type.6.projected
  132.9 1.0 copy-done.5
  133.9 1.0 copy-done.6
  134.9 4.1 %attention.1 = (bf16[256,1024]{1,0:T(8,128)(2,1)}, bf16[256,256]{1,0:T(8,128)(2,1)S(1)}) custom-call(s32[1]{0:T(128)} %constant.64.clone.1.place, bf16[256,256]{1,0:T(8,128)(2,1)S(1)} %convert_element_type.6.projected, bf16[256,1024]{1,0:T(8,128)(2,1)S(1)} %copy-done.5, bf16[256,1024]{1,0:T(8,128)(2,1)S(1)} %copy-done.6, f32[256,256]{1,0:T(8,128)S(1)} %fusion.1.allowed), custom_call_target="tpu_custom_call" | custom-call | flops 805306368 | bytes 2097152 | tf_op jit(solution)/shard_map/attention/pallas_call | solution.py:73
  139.1 3.7 %weight_other.1 = (bf16[2,1024,128]{2,1,0:T(8,128)(2,1)}, bf16[2,1024,128]{2,1,0:T(8,128)(2,1)}, bf16[2,1024,128]{2,1,0:T(8,128)(2,1)}, bf16[2,1024,128]{2,1,0:T(8,128)(2,1)S(1)}) custom-call(s32[5]{0:T(128)S(1)} %stack.101.place, bf16[32,2048,256]{2,1,0:T(8,128)(2,1)} %get-tuple-element.82.held, bf16[256,256]{1,0:T(8,128)(2,1)S(1)} %get-tuple-element.97.d_projected.refs_0_), custom_call_target="tpu_custom_call" | custom-call | flops 536870912 | bytes 4194304 | tf_op jit(solution)/shard_map/weight_other/pallas_call | solution.py:223
  144.8 1.2 collective-permute-done.19.refs_0_
  146.0 1.5 collective-permute-done.20.refs_1_
  147.5 3.2 %weight_send.1 = (bf16[2,1024,128]{2,1,0:T(8,128)(2,1)S(1)}, bf16[2,1024,128]{2,1,0:T(8,128)(2,1)S(1)}) custom-call(s32[5]{0:T(128)S(1)} %stack.96.place, bf16[32,2048,256]{2,1,0:T(8,128)(2,1)} %get-tuple-element.82.held, bf16[256,256]{1,0:T(8,128)(2,1)S(1)} %get-tuple-element.97.d_projected.refs_0_, bf16[2,1024,128]{2,1,0:T(8,128)(2,1)} %collective-permute-done.19.refs_0_, ...), custom_call_target="tpu_custom_call" | custom-call | flops 268435456 | bytes 2097152 | tf_op jit(solution)/shard_map/weight_send/pallas_call | solution.py:223
  151.3 1.5 collective-permute-start.22
  152.8 5.2 %collective-permute-done.23.refs_1_ = bf16[256,256]{1,0:T(8,128)(2,1)S(1)} collective-permute-done((bf16[256,256]{1,0:T(8,128)(2,1)S(1)}, bf16[256,256]{1,0:T(8,128)(2,1)S(1)}, u32[]{:S(2)}, u32[]{:S(2)}) %collective-permute-start.23) | collective-permute-done | bytes 131104 | tf_op jit(solution)/shard_map/ppermute | solution.py:385
  158.1 2.9 %collective-permute-start.25 = (bf16[256,256]{1,0:T(8,128)(2,1)S(1)}, bf16[256,256]{1,0:T(8,128)(2,1)S(1)}, u32[]{:S(2)}, u32[]{:S(2)}) collective-permute-start(bf16[256,256]{1,0:T(8,128)(2,1)S(1)} %collective-permute-done.23.refs_1_), channel_id=1, source_target_pairs={{0,2},{1,3},{2,0},{3,1},{4,6},{5,7},{6,4},{7,5},{8,10},{9,11},{10,... | collective-permute-start | bytes 393224 | tf_op jit(solution)/shard_map/ppermute | solution.py:385
  161.0 3.0 %weight_keep.1 = (f32[2,1024,128]{2,1,0:T(8,128)S(1)}, f32[2,1024,128]{2,1,0:T(8,128)S(1)}) custom-call(s32[5]{0:T(128)S(1)} %stack.96.place, bf16[32,2048,256]{2,1,0:T(8,128)(2,1)} %get-tuple-element.82.held, bf16[256,256]{1,0:T(8,128)(2,1)S(1)} %get-tuple-element.97.d_projected.refs_0_, bf16[2,1024,128]{2,1,0:T(8,128)(2,1)} %collective-permute-done.17.refs_0_, ...), custom_call_target="tpu_custom_call" | custom-call | flops 268435456 | bytes 2097152 | tf_op jit(solution)/shard_map/weight_keep/pallas_call | solution.py:223
  164.0 5.0 %collective-permute-done.24.refs_2_ = bf16[256,256]{1,0:T(8,128)(2,1)S(1)} collective-permute-done((bf16[256,256]{1,0:T(8,128)(2,1)S(1)}, bf16[256,256]{1,0:T(8,128)(2,1)S(1)}, u32[]{:S(2)}, u32[]{:S(2)}) %collective-permute-start.24) | collective-permute-done | bytes 131104 | tf_op jit(solution)/shard_map/ppermute | solution.py:385
  169.0 2.7 %collective-permute-done.25.refs_3_ = bf16[256,256]{1,0:T(8,128)(2,1)S(1)} collective-permute-done((bf16[256,256]{1,0:T(8,128)(2,1)S(1)}, bf16[256,256]{1,0:T(8,128)(2,1)S(1)}, u32[]{:S(2)}, u32[]{:S(2)}) %collective-permute-start.25) | collective-permute-done | bytes 131104 | tf_op jit(solution)/shard_map/ppermute | solution.py:385
  172.4 1.5 collective-permute-start.27
  173.9 4.0 %input_gradient.1 = bf16[256,2048]{1,0:T(8,128)(2,1)} custom-call(s32[5]{0:T(128)S(1)} %broadcast_in_dim.9.place, bf16[256,256]{1,0:T(8,128)(2,1)S(1)} %get-tuple-element.97.d_projected.refs_0_, bf16[256,256]{1,0:T(8,128)(2,1)S(1)} %collective-permute-done.23.refs_1_, bf16[256,256]{1,0:T(8,128)(2,1)S(1)} %collective-permute-done.24.refs_2_, ...), custom_call_target="tpu_custom_call" | custom-call | flops 1073741824 | bytes 8912896 | tf_op jit(solution)/shard_map/input_gradient/pallas_call | solution.py:73
  177.8 2.2 %collective-permute-done.26.last_a = bf16[1024,128]{1,0:T(8,128)(2,1)S(1)} collective-permute-done((bf16[1024,128]{1,0:T(8,128)(2,1)S(1)}, bf16[1024,128]{1,0:T(8,128)(2,1)S(1)}, u32[]{:S(2)}, u32[]{:S(2)}) %collective-permute-start.26) | collective-permute-done | bytes 262176 | tf_op jit(solution)/shard_map/ppermute | solution.py:260
  180.3 1.1 weight_finish.1
  (58 shorter events, 8.3 us)
Async XLA Ops:
  0.6 42.6 %collective-permute-start = (bf16[256,2048]{1,0:T(8,128)(2,1)}, bf16[256,2048]{1,0:T(8,128)(2,1)}, u32[]{:S(2)}, u32[]{:S(2)}) collective-permute-start(bf16[256,2048]{1,0:T(8,128)(2,1)} %chunk.1), channel_id=1, source_target_pairs={{0,1},{1,2},{2,3},{4,5},{5,6},{6,7},{8,9},{9,10},{10,11},{12,13},{... | collective-permute-start | bytes 3145736 | tf_op jit(solution)/shard_map/ppermute | solution.py:414
  6.5 36.7 %collective-permute-start.1 = (bf16[256,2048]{1,0:T(8,128)(2,1)}, bf16[256,2048]{1,0:T(8,128)(2,1)}, u32[]{:S(2)}, u32[]{:S(2)}) collective-permute-start(bf16[256,2048]{1,0:T(8,128)(2,1)} %chunk.1), channel_id=1, source_target_pairs={{1,0},{2,1},{3,2},{5,4},{6,5},{7,6},{9,8},{10,9},{11,10},{13,12},{... | collective-permute-start | bytes 3145736 | tf_op jit(solution)/shard_map/ppermute | solution.py:415
  15.0 23.8 %collective-permute-start.2 = (bf16[256,256]{1,0:T(8,128)(2,1)S(1)}, bf16[256,256]{1,0:T(8,128)(2,1)S(1)}, u32[]{:S(2)}, u32[]{:S(2)}) collective-permute-start(bf16[256,256]{1,0:T(8,128)(2,1)S(1)} %get-tuple-element.115), channel_id=1, source_target_pairs={{0,1},{1,0},{2,3},{3,2},{4,5},{5,4},{6,7},{7,6},{8,9},{9,8},{10,11... | collective-permute-start | bytes 393224 | tf_op jit(solution)/shard_map/ppermute | solution.py:385
  17.7 25.4 %collective-permute-start.3 = (bf16[256,256]{1,0:T(8,128)(2,1)S(1)}, bf16[256,256]{1,0:T(8,128)(2,1)S(1)}, u32[]{:S(2)}, u32[]{:S(2)}) collective-permute-start(bf16[256,256]{1,0:T(8,128)(2,1)S(1)} %get-tuple-element.114), channel_id=1, source_target_pairs={{0,2},{1,3},{2,0},{3,1},{4,6},{5,7},{6,4},{7,5},{8,10},{9,11},{10,... | collective-permute-start | bytes 393224 | tf_op jit(solution)/shard_map/ppermute | solution.py:385
  20.3 22.8 %collective-permute-start.4 = (bf16[256,256]{1,0:T(8,128)(2,1)S(1)}, bf16[256,256]{1,0:T(8,128)(2,1)S(1)}, u32[]{:S(2)}, u32[]{:S(2)}) collective-permute-start(bf16[256,256]{1,0:T(8,128)(2,1)S(1)} %get-tuple-element.113), channel_id=1, source_target_pairs={{0,3},{1,2},{2,1},{3,0},{4,7},{5,6},{6,5},{7,4},{8,11},{9,10},{10,... | collective-permute-start | bytes 393224 | tf_op jit(solution)/shard_map/ppermute | solution.py:385
  43.2 6.1 %collective-permute-start.5 = (bf16[256,2048]{1,0:T(8,128)(2,1)}, bf16[256,2048]{1,0:T(8,128)(2,1)}, u32[]{:S(2)}, u32[]{:S(2)}) collective-permute-start(bf16[256,2048]{1,0:T(8,128)(2,1)} %collective-permute-done.chunk), channel_id=1, source_target_pairs={{1,2},{2,3},{5,6},{6,7},{9,10},{10,11},{13,14},{14,15},{17,18},{18... | collective-permute-start | bytes 3145736 | tf_op jit(solution)/shard_map/ppermute | solution.py:414
  44.9 26.4 %collective-permute-start.6 = (bf16[256,2048]{1,0:T(8,128)(2,1)}, bf16[256,2048]{1,0:T(8,128)(2,1)}, u32[]{:S(2)}, u32[]{:S(2)}) collective-permute-start(bf16[256,2048]{1,0:T(8,128)(2,1)} %collective-permute-done.1.chunk), channel_id=1, source_target_pairs={{1,0},{2,1},{5,4},{6,5},{9,8},{10,9},{13,12},{14,13},{17,16},{18,1... | collective-permute-start | bytes 3145736 | tf_op jit(solution)/shard_map/ppermute | solution.py:415
  46.1 27.8 %collective-permute-start.7 = (bf16[2048,256]{1,0:T(8,128)(2,1)S(1)}, bf16[2048,256]{1,0:T(8,128)(2,1)S(1)}, u32[]{:S(2)}, u32[]{:S(2)}) collective-permute-start(bf16[2048,256]{1,0:T(8,128)(2,1)S(1)} %constant_dynamic-update-slice_fusion.refs_0_.refs_4_), channel_id=1, source_target_pairs={{0,4},{4,0},{8,12},{12,8},{16,20},{20,16},{24,28},{28,24},{1,5},{5... | collective-permute-start | bytes 3145736 | tf_op jit(solution)/shard_map/ppermute | solution.py:260
  46.2 27.8 %collective-permute-start.8 = (bf16[2048,256]{1,0:T(8,128)(2,1)S(1)}, bf16[2048,256]{1,0:T(8,128)(2,1)S(1)}, u32[]{:S(2)}, u32[]{:S(2)}) collective-permute-start(bf16[2048,256]{1,0:T(8,128)(2,1)S(1)} %constant_dynamic-update-slice_fusion.refs_0_.refs_4_), channel_id=1, source_target_pairs={{0,8},{4,12},{8,0},{12,4},{16,24},{20,28},{24,16},{28,20},{1,9},{5... | collective-permute-start | bytes 3145736 | tf_op jit(solution)/shard_map/ppermute | solution.py:260
  47.8 26.2 %collective-permute-start.9 = (bf16[2048,256]{1,0:T(8,128)(2,1)S(1)}, bf16[2048,256]{1,0:T(8,128)(2,1)S(1)}, u32[]{:S(2)}, u32[]{:S(2)}) collective-permute-start(bf16[2048,256]{1,0:T(8,128)(2,1)S(1)} %constant_dynamic-update-slice_fusion.refs_0_.refs_4_), channel_id=1, source_target_pairs={{0,16},{4,20},{8,24},{12,28},{16,0},{20,4},{24,8},{28,12},{1,17},{... | collective-permute-start | bytes 3145736 | tf_op jit(solution)/shard_map/ppermute | solution.py:260
  72.6 29.3 %copy-start.8 = (bf16[256,2048]{1,0:T(8,128)(2,1)}, bf16[256,2048]{1,0:T(8,128)(2,1)S(1)}, u32[]{:S(2)}) copy-start(bf16[256,2048]{1,0:T(8,128)(2,1)S(1)} %broadcast_select_fusion.chunk) | copy-start | bytes 3145732
  72.7 24.6 %collective-permute-start.10 = (bf16[256,2048]{1,0:T(8,128)(2,1)S(1)}, bf16[256,2048]{1,0:T(8,128)(2,1)}, u32[]{:S(2)}, u32[]{:S(2)}) collective-permute-start(bf16[256,2048]{1,0:T(8,128)(2,1)S(1)} %broadcast_select_fusion.chunk), channel_id=1, source_target_pairs={{2,3},{1,0},{6,7},{5,4},{10,11},{9,8},{14,15},{13,12},{18,19},{17,... | collective-permute-start | bytes 3145736 | tf_op jit(solution)/shard_map/ppermute | solution.py:417
  74.0 28.0 %copy-start = (bf16[2048,256]{1,0:T(8,128)(2,1)}, bf16[2048,256]{1,0:T(8,128)(2,1)S(1)}, u32[]{:S(2)}) copy-start(bf16[2048,256]{1,0:T(8,128)(2,1)S(1)} %collective-permute-done.7.refs_1_.refs_5_) | copy-start | bytes 3145732
  98.1 10.8 %collective-permute-start.13 = (bf16[1024,256]{1,0:T(8,128)(2,1)}, bf16[1024,256]{1,0:T(8,128)(2,1)}, u32[]{:S(2)}, u32[]{:S(2)}) collective-permute-start(bf16[1024,256]{1,0:T(8,128)(2,1)} %slice.6), channel_id=1, source_target_pairs={{0,8},{4,12},{8,0},{12,4},{16,24},{20,28},{24,16},{28,20},{1,9},{5... | collective-permute-start | bytes 1572872 | tf_op jit(solution)/shard_map/ppermute | solution.py:260
  100.4 10.5 %collective-permute-start.15 = (bf16[1024,256]{1,0:T(8,128)(2,1)}, bf16[1024,256]{1,0:T(8,128)(2,1)}, u32[]{:S(2)}, u32[]{:S(2)}) collective-permute-start(bf16[1024,256]{1,0:T(8,128)(2,1)} %slice.7), channel_id=1, source_target_pairs={{0,16},{4,20},{8,24},{12,28},{16,0},{20,4},{24,8},{28,12},{1,17},{... | collective-permute-start | bytes 1572872 | tf_op jit(solution)/shard_map/ppermute | solution.py:260
  101.9 21.3 %collective-permute-start.11 = (bf16[2048,256]{1,0:T(8,128)(2,1)S(1)}, bf16[2048,256]{1,0:T(8,128)(2,1)}, u32[]{:S(2)}, u32[]{:S(2)}) collective-permute-start(bf16[2048,256]{1,0:T(8,128)(2,1)S(1)} %collective-permute-done.8.refs_2_.refs_6_), channel_id=1, source_target_pairs={{0,4},{4,0},{8,12},{12,8},{16,20},{20,16},{24,28},{28,24},{1,5},{5... | collective-permute-start | bytes 3145736 | tf_op jit(solution)/shard_map/ppermute | solution.py:260
  101.9 21.3 %collective-permute-start.12 = (bf16[2048,256]{1,0:T(8,128)(2,1)S(1)}, bf16[2048,256]{1,0:T(8,128)(2,1)}, u32[]{:S(2)}, u32[]{:S(2)}) collective-permute-start(bf16[2048,256]{1,0:T(8,128)(2,1)S(1)} %collective-permute-done.9.refs_4_.refs_8_), channel_id=1, source_target_pairs={{0,4},{4,0},{8,12},{12,8},{16,20},{20,16},{24,28},{28,24},{1,5},{5... | collective-permute-start | bytes 3145736 | tf_op jit(solution)/shard_map/ppermute | solution.py:260
  108.9 14.4 %collective-permute-start.14 = (bf16[1024,256]{1,0:T(8,128)(2,1)}, bf16[1024,256]{1,0:T(8,128)(2,1)}, u32[]{:S(2)}, u32[]{:S(2)}) collective-permute-start(bf16[1024,256]{1,0:T(8,128)(2,1)} %collective-permute-done.13.refs_6_), channel_id=1, source_target_pairs={{0,4},{4,0},{8,12},{12,8},{16,20},{20,16},{24,28},{28,24},{1,5},{5... | collective-permute-start | bytes 1572872 | tf_op jit(solution)/shard_map/ppermute | solution.py:260
  110.9 17.5 %collective-permute-start.16 = (bf16[1024,256]{1,0:T(8,128)(2,1)}, bf16[1024,256]{1,0:T(8,128)(2,1)S(1)}, u32[]{:S(2)}, u32[]{:S(2)}) collective-permute-start(bf16[1024,256]{1,0:T(8,128)(2,1)} %collective-permute-done.15.refs_10_), channel_id=1, source_target_pairs={{0,4},{4,0},{8,12},{12,8},{16,20},{20,16},{24,28},{28,24},{1,5},{5... | collective-permute-start | bytes 1572872 | tf_op jit(solution)/shard_map/ppermute | solution.py:260
  123.3 1.2 copy-start.1
  128.4 14.4 %copy-start.3 = (bf16[1024,256]{1,0:T(8,128)(2,1)}, bf16[1024,256]{1,0:T(8,128)(2,1)S(1)}, u32[]{:S(2)}) copy-start(bf16[1024,256]{1,0:T(8,128)(2,1)S(1)} %collective-permute-done.16.refs_11_) | copy-start | bytes 1572868
  132.9 1.0 copy-start.5
  133.9 1.0 copy-start.6
  142.8 0.8 copy-start.7
  143.6 2.4 %collective-permute-start.19 = (bf16[2,1024,128]{2,1,0:T(8,128)(2,1)}, bf16[2,1024,128]{2,1,0:T(8,128)(2,1)}, u32[]{:S(2)}, u32[]{:S(2)}) collective-permute-start(bf16[2,1024,128]{2,1,0:T(8,128)(2,1)} %get-tuple-element.88), channel_id=1, source_target_pairs={{0,4},{4,0},{8,12},{12,8},{16,20},{20,16},{24,28},{28,24},{1,5},{5... | collective-permute-start | bytes 1572872 | tf_op jit(solution)/shard_map/ppermute | solution.py:260
  144.2 3.4 %collective-permute-start.20 = (bf16[2,1024,128]{2,1,0:T(8,128)(2,1)}, bf16[2,1024,128]{2,1,0:T(8,128)(2,1)}, u32[]{:S(2)}, u32[]{:S(2)}) collective-permute-start(bf16[2,1024,128]{2,1,0:T(8,128)(2,1)} %get-tuple-element.89), channel_id=1, source_target_pairs={{0,4},{4,0},{8,12},{12,8},{16,20},{20,16},{24,28},{28,24},{1,5},{5... | collective-permute-start | bytes 1572872 | tf_op jit(solution)/shard_map/ppermute | solution.py:260
  144.2 13.9 %collective-permute-start.17 = (bf16[2,1024,128]{2,1,0:T(8,128)(2,1)}, bf16[2,1024,128]{2,1,0:T(8,128)(2,1)}, u32[]{:S(2)}, u32[]{:S(2)}) collective-permute-start(bf16[2,1024,128]{2,1,0:T(8,128)(2,1)} %get-tuple-element.85), channel_id=1, source_target_pairs={{0,4},{4,0},{8,12},{12,8},{16,20},{20,16},{24,28},{28,24},{1,5},{5... | collective-permute-start | bytes 1572872 | tf_op jit(solution)/shard_map/ppermute | solution.py:260
  144.8 29.1 %copy-start.2 = (bf16[2048,256]{1,0:T(8,128)(2,1)S(1)}, bf16[2048,256]{1,0:T(8,128)(2,1)}, u32[]{:S(2)}) copy-start(bf16[2048,256]{1,0:T(8,128)(2,1)} %copy-done) | copy-start | bytes 3145732
  144.8 29.1 %copy-start.4 = (bf16[1024,256]{1,0:T(8,128)(2,1)S(1)}, bf16[1024,256]{1,0:T(8,128)(2,1)}, u32[]{:S(2)}) copy-start(bf16[1024,256]{1,0:T(8,128)(2,1)} %copy-done.3) | copy-start | bytes 1572868
  144.8 16.2 %collective-permute-start.18 = (bf16[2,1024,128]{2,1,0:T(8,128)(2,1)}, bf16[2,1024,128]{2,1,0:T(8,128)(2,1)S(1)}, u32[]{:S(2)}, u32[]{:S(2)}) collective-permute-start(bf16[2,1024,128]{2,1,0:T(8,128)(2,1)} %copy-done.7), channel_id=1, source_target_pairs={{0,4},{4,0},{8,12},{12,8},{16,20},{20,16},{24,28},{28,24},{1,5},{5... | collective-permute-start | bytes 1572872 | tf_op jit(solution)/shard_map/ppermute | solution.py:260
  150.7 21.0 %collective-permute-start.21 = (bf16[2,1024,128]{2,1,0:T(8,128)(2,1)S(1)}, bf16[2,1024,128]{2,1,0:T(8,128)(2,1)S(1)}, u32[]{:S(2)}, u32[]{:S(2)}) collective-permute-start(bf16[2,1024,128]{2,1,0:T(8,128)(2,1)S(1)} %get-tuple-element.90), channel_id=1, source_target_pairs={{0,8},{4,12},{8,0},{12,4},{16,24},{20,28},{24,16},{28,20},{1,9},{5... | collective-permute-start | bytes 1572872 | tf_op jit(solution)/shard_map/ppermute | solution.py:260
  151.3 20.4 %collective-permute-start.22 = (bf16[2,1024,128]{2,1,0:T(8,128)(2,1)S(1)}, bf16[2,1024,128]{2,1,0:T(8,128)(2,1)S(1)}, u32[]{:S(2)}, u32[]{:S(2)}) collective-permute-start(bf16[2,1024,128]{2,1,0:T(8,128)(2,1)S(1)} %get-tuple-element.91), channel_id=1, source_target_pairs={{0,16},{4,20},{8,24},{12,28},{16,0},{20,4},{24,8},{28,12},{1,17},{... | collective-permute-start | bytes 1572872 | tf_op jit(solution)/shard_map/ppermute | solution.py:260
  152.8 5.2 %collective-permute-start.23 = (bf16[256,256]{1,0:T(8,128)(2,1)S(1)}, bf16[256,256]{1,0:T(8,128)(2,1)S(1)}, u32[]{:S(2)}, u32[]{:S(2)}) collective-permute-start(bf16[256,256]{1,0:T(8,128)(2,1)S(1)} %get-tuple-element.97.d_projected.refs_0_), channel_id=1, source_target_pairs={{0,1},{1,0},{2,3},{3,2},{4,5},{5,4},{6,7},{7,6},{8,9},{9,8},{10,11... | collective-permute-start | bytes 393224 | tf_op jit(solution)/shard_map/ppermute | solution.py:385
  158.0 11.0 %collective-permute-start.24 = (bf16[256,256]{1,0:T(8,128)(2,1)S(1)}, bf16[256,256]{1,0:T(8,128)(2,1)S(1)}, u32[]{:S(2)}, u32[]{:S(2)}) collective-permute-start(bf16[256,256]{1,0:T(8,128)(2,1)S(1)} %get-tuple-element.97.d_projected.refs_0_), channel_id=1, source_target_pairs={{0,2},{1,3},{2,0},{3,1},{4,6},{5,7},{6,4},{7,5},{8,10},{9,11},{10,... | collective-permute-start | bytes 393224 | tf_op jit(solution)/shard_map/ppermute | solution.py:385
  158.1 13.6 %collective-permute-start.25 = (bf16[256,256]{1,0:T(8,128)(2,1)S(1)}, bf16[256,256]{1,0:T(8,128)(2,1)S(1)}, u32[]{:S(2)}, u32[]{:S(2)}) collective-permute-start(bf16[256,256]{1,0:T(8,128)(2,1)S(1)} %collective-permute-done.23.refs_1_), channel_id=1, source_target_pairs={{0,2},{1,3},{2,0},{3,1},{4,6},{5,7},{6,4},{7,5},{8,10},{9,11},{10,... | collective-permute-start | bytes 393224 | tf_op jit(solution)/shard_map/ppermute | solution.py:385
  171.8 8.3 %collective-permute-start.26 = (bf16[1024,128]{1,0:T(8,128)(2,1)S(1)}, bf16[1024,128]{1,0:T(8,128)(2,1)S(1)}, u32[]{:S(2)}, u32[]{:S(2)}) collective-permute-start(bf16[1024,128]{1,0:T(8,128)(2,1)S(1)} %get-tuple-element.95), channel_id=1, source_target_pairs={{0,16},{4,20},{8,24},{12,28},{16,0},{20,4},{24,8},{28,12},{1,17},{... | collective-permute-start | bytes 786440 | tf_op jit(solution)/shard_map/ppermute | solution.py:260
  172.4 7.9 %collective-permute-start.27 = (bf16[1024,128]{1,0:T(8,128)(2,1)S(1)}, bf16[1024,128]{1,0:T(8,128)(2,1)S(1)}, u32[]{:S(2)}, u32[]{:S(2)}) collective-permute-start(bf16[1024,128]{1,0:T(8,128)(2,1)S(1)} %get-tuple-element.96), channel_id=1, source_target_pairs={{0,8},{4,12},{8,0},{12,4},{16,24},{20,28},{24,16},{28,20},{1,9},{5... | collective-permute-start | bytes 786440 | tf_op jit(solution)/shard_map/ppermute | solution.py:260

commit v7 on v6

--- a/solution.py
+++ b/solution.py
@@ -81,65 +81,74 @@
     )(place, *arrays)
 
 
-def absorb_kernel(place, chunk, cached, total, *refs):
-    *_, total_out, held_out = refs
-
-    @pl.when(pl.program_id(0) == 0)
-    def _():
-        total_out[...] = total[...]
-
-    total_out[...] += jnp.dot(chunk[...], cached[...], preferred_element_type=jnp.float32)
-    held_out[0] = chunk[...].T
+def absorb_kernel(place, chunk, total, cached, *refs):
+    *_, total_out, held, rows, turned, sems = refs
+    height = rows.shape[0]
+    start = pl.multiple_of(place[0] * height, height)
+    fetch = pltpu.make_async_copy(cached.at[pl.ds(start, height), :], rows, sems.at[0])
+    fetch.start()
+    turned[...] = chunk[...].T
+    keep = pltpu.make_async_copy(turned, held.at[place[1]], sems.at[1])
+    keep.start()
+    fetch.wait()
+    total_out[...] = total[...] + jnp.dot(
+        chunk[...], rows[...], preferred_element_type=jnp.float32
+    )
+    keep.wait()
 
 
 def absorb(chunk, index, cached, total, held, n_chunks):
     length, feats = chunk.shape
     cols = cached.shape[1]
-    step = min(feats, 1024)
-    steps = feats // step
     inside = (index >= 0) & (index < n_chunks)
     place = jnp.stack([jnp.clip(index, 0, n_chunks - 1), jnp.where(inside, index, n_chunks)])
     shape = jax.ShapeDtypeStruct((8 * n_chunks, feats, length), chunk.dtype)
-    whole = pl.BlockSpec((length, cols), lambda i, place: (0, 0))
+    vmem, anywhere = pl.BlockSpec(memory_space=pltpu.VMEM), pl.BlockSpec(memory_space=pl.ANY)
     return pl.pallas_call(
         absorb_kernel,
-        grid_spec=pltpu.PrefetchScalarGridSpec(
-            num_scalar_prefetch=1,
-            grid=(steps,),
-            in_specs=[
-                pl.BlockSpec((length, step), lambda i, place: (0, i)),
-                pl.BlockSpec((step, cols), lambda i, place: (place[0] * steps + i, 0)),
-                whole,
-            ]
-            + ([] if held is None else [pl.BlockSpec(memory_space=pl.ANY)]),
-            out_specs=[
-                whole,
-                pl.BlockSpec((1, step, length), lambda i, place: (place[1], i, 0)),
-            ],
-        ),
+        in_specs=[pl.BlockSpec(memory_space=pltpu.SMEM), vmem, vmem, anywhere]
+        + ([] if held is None else [anywhere]),
+        out_specs=[vmem, anywhere],
         out_shape=[jax.ShapeDtypeStruct(total.shape, jnp.float32), shape],
+        scratch_shapes=[
+            pltpu.VMEM((feats, cols), cached.dtype),
+            pltpu.VMEM((feats, length), chunk.dtype),
+            pltpu.SemaphoreType.DMA((2,)),
+        ],
         input_output_aliases={} if held is None else {4: 1},
         cost_estimate=pl.CostEstimate(
             flops=2 * length * feats * cols,
             bytes_accessed=4 * length * feats + 2 * feats * cols,
             transcendentals=0,
         ),
-        compiler_params=pltpu.CompilerParams(vmem_limit_bytes=VMEM_STREAM),
+        compiler_params=pltpu.CompilerParams(vmem_limit_bytes=VMEM_WHOLE),
         name="absorb",
-    )(place, chunk, cached, total, *([] if held is None else [held]))
-
-
-def attention_kernel(place, projected, queries, d_out, allowed, d_queries, d_projected):
+    )(place, chunk, total, cached, *([] if held is None else [held]))
+
+
+def attention_kernel(n_totals, *refs):
+    totals, (allowed, queries_in, d_out_in) = refs[:n_totals], refs[n_totals : n_totals + 3]
+    d_queries, d_projected, queries, d_out, sems = refs[n_totals + 3 :]
+    copies = [
+        pltpu.make_async_copy(queries_in, queries, sems.at[0]),
+        pltpu.make_async_copy(d_out_in, d_out, sems.at[1]),
+    ]
+    for copy in copies:
+        copy.start()
+    projected = jnp.concatenate([total[...].astype(jnp.bfloat16) for total in totals], axis=0)
+    kept = allowed[...] > 0
+    for copy in copies:
+        copy.wait()
     factor = 1.0 / math.sqrt(HD)
     across = (((1,), (1,)), ((), ()))
-    for head in range(projected.shape[1] // (2 * HD)):
+    heads = projected.shape[1] // (2 * HD)
+    group = queries.shape[1] // HD // heads
+    for head in range(heads):
         start = 2 * HD * head
         keys = projected[:, start : start + HD]
         values = projected[:, start + HD : start + 2 * HD]
-        group = queries.shape[1] // HD // (projected.shape[1] // (2 * HD))
         d_keys = jnp.zeros(keys.shape, jnp.float32)
         d_values = jnp.zeros(keys.shape, jnp.float32)
-        kept = allowed[...] > 0
         for g in range(head * group, (head + 1) * group):
             columns = slice(g * HD, (g + 1) * HD)
             query, grad = queries[:, columns], d_out[:, columns]
@@ -162,15 +171,30 @@
         d_projected[:, start + HD : start + 2 * HD] = d_values.astype(jnp.bfloat16)
 
 
-def attention_backward(projected, queries, d_out, allowed):
-    return on_chip(
-        attention_kernel,
-        jnp.zeros((1,), jnp.int32),
-        [projected, queries, d_out, allowed],
-        [jax.ShapeDtypeStruct(a.shape, jnp.bfloat16) for a in (queries, projected)],
-        12 * allowed.size * queries.shape[1],
-        "attention",
-    )
+def attention_backward(totals, queries, d_out, allowed):
+    length, cols = queries.shape[0], totals[0].shape[1]
+    vmem, anywhere = pl.BlockSpec(memory_space=pltpu.VMEM), pl.BlockSpec(memory_space=pl.ANY)
+    return pl.pallas_call(
+        functools.partial(attention_kernel, len(totals)),
+        in_specs=[vmem] * (len(totals) + 1) + [anywhere] * 2,
+        out_specs=[vmem] * 2,
+        out_shape=[
+            jax.ShapeDtypeStruct(queries.shape, jnp.bfloat16),
+            jax.ShapeDtypeStruct((length, cols), jnp.bfloat16),
+        ],
+        scratch_shapes=[
+            pltpu.VMEM(queries.shape, queries.dtype),
+            pltpu.VMEM(d_out.shape, d_out.dtype),
+            pltpu.SemaphoreType.DMA((2,)),
+        ],
+        cost_estimate=pl.CostEstimate(
+            flops=12 * allowed.size * queries.shape[1],
+            bytes_accessed=8 * queries.size,
+            transcendentals=allowed.size * queries.shape[1] // HD,
+        ),
+        compiler_params=pltpu.CompilerParams(vmem_limit_bytes=VMEM_STREAM),
+        name="attention",
+    )(*totals, allowed, queries, d_out)
 
 
 SENT = ((0, 0, 0), (0, 1, 0), (1, 0, 1), (2, 1, 1))
@@ -179,11 +203,11 @@
 
 def weight_kernel(groups, place, held, d_projected, *refs):
     *refs, buffer, sems = refs
-    n_out = 2 * len(groups)
+    joined = len(groups) > 1
+    n_out = len(groups) if joined else 2
     added, outs = refs[:-n_out], refs[-n_out:]
     rows = buffer.shape[1]
     half = d_projected.shape[1] // 2
-    block = min(rows, 256)
     start = pl.multiple_of(place[4] * rows, rows)
     chunks = sorted({chunk for group in groups for chunk, _, _ in group})
     copies = {}
@@ -194,38 +218,40 @@
         copies[chunk].start()
     for chunk in chunks:
         copies[chunk].wait()
-        for r in range(0, rows, block):
-            wanted = [
-                (side, 2 * g + side, position)
-                for g, group in enumerate(groups)
-                for which, side, position in group
-                if which == chunk
-            ]
-            first, last = min(w[0] for w in wanted), max(w[0] for w in wanted)
-            total = jnp.dot(
-                buffer[chunk, r : r + block, :],
-                d_projected[:, first * half : (last + 1) * half],
-                preferred_element_type=jnp.float32,
-            )
-            for side, n, position in wanted:
-                part = total[:, (side - first) * half : (side - first + 1) * half]
-                if added:
-                    part = part + added[n][position, r : r + block, :].astype(jnp.float32)
-                outs[n][position, r : r + block, :] = part.astype(outs[n].dtype)
+        wanted = [
+            (g, side, position)
+            for g, group in enumerate(groups)
+            for which, side, position in group
+            if which == chunk
+        ]
+        first, last = min(w[1] for w in wanted), max(w[1] for w in wanted)
+        total = jnp.dot(
+            buffer[chunk],
+            d_projected[:, first * half : (last + 1) * half],
+            preferred_element_type=jnp.float32,
+        )
+        for g, side, position in wanted:
+            part = total[:, (side - first) * half : (side - first + 1) * half]
+            if added:
+                part = part + added[0][2 * side + position].astype(jnp.float32)
+            if joined:
+                outs[g][2 * side + position] = part.astype(outs[g].dtype)
+            else:
+                outs[side][position] = part.astype(outs[side].dtype)
 
 
 def weight_parts(held, d_projected, place, groups, added, dtype, name):
     length, cols = d_projected.shape
     rows = held.shape[1] // 2
-    shape = jax.ShapeDtypeStruct((2, rows, cols // 2), dtype)
     vmem = pl.BlockSpec(memory_space=pltpu.VMEM)
-    n_out = 2 * len(groups)
+    depth = 4 if len(groups) > 1 else 2
+    shape = jax.ShapeDtypeStruct((depth, rows, cols // 2), dtype)
     return pl.pallas_call(
         functools.partial(weight_kernel, groups),
         in_specs=[pl.BlockSpec(memory_space=pltpu.SMEM), pl.BlockSpec(memory_space=pl.ANY)]
         + [vmem] * (1 + len(added)),
-        out_specs=[vmem] * n_out,
-        out_shape=[shape] * n_out,
+        out_specs=[vmem] * 2,
+        out_shape=[shape] * 2,
         scratch_shapes=[
             pltpu.VMEM((4, rows, length), held.dtype),
             pltpu.SemaphoreType.DMA((4,)),
@@ -262,7 +288,7 @@
     return index % 2, (index // 2) % 2, index // 4, swap
 
 
-def weight_sum(held, d_projected, beside):
+def weight_sum(held, d_projected, pieces, beside):
     core, x, y, swap = plane()
     rows, cols = held.shape[1] // 2, d_projected.shape[1]
     none = jnp.zeros((1,), jnp.int32)
@@ -272,12 +298,13 @@
         place = jnp.stack(chunks + [which])
         return weight_parts(held, d_projected, place, groups, added, dtype, name)
 
-    theirs = parts(1 - core, (SENT, KEPT), [], jnp.bfloat16, "weight_other")
-    theirs = [swap(part, 1) for part in theirs]
-    send_a, send_b = parts(core, (SENT,), theirs[:2], jnp.bfloat16, "weight_send")
+    sent, kept = parts(1 - core, (SENT, KEPT), [], jnp.bfloat16, "weight_other")
+    sent, kept = swap(sent, 1), swap(kept, 1)
+    sent, pieces[1] = lax.optimization_barrier((sent, pieces[1]))
+    send_a, send_b = parts(core, (SENT,), [sent], jnp.bfloat16, "weight_send")
     got_a, got_b = swap(send_a, 2), swap(send_b, 4)
-    keep_a, keep_b = parts(core, (KEPT,), theirs[2:], jnp.float32, "weight_keep")
-    got_a, got_b, beside = lax.optimization_barrier((got_a, got_b, beside))
+    keep_a, keep_b = parts(core, (KEPT,), [kept], jnp.float32, "weight_keep")
+    got_a, got_b, pieces, beside = lax.optimization_barrier((got_a, got_b, pieces, beside))
 
     small = jax.ShapeDtypeStruct((rows, cols // 2), jnp.bfloat16)
     arrays = [keep_a, got_a, keep_b, got_b]
@@ -298,29 +325,53 @@
         )
         return total, ready
 
-    return finish, beside
-
-
-def gather_plane(own, gate):
-    _, _, _, swap = plane()
-    half = own.shape[0] // 2
-    got = {0: own, 2: swap(own, 2), 4: swap(own, 4)}
-    got[1] = swap(own, 1)
-    (got, _) = lax.optimization_barrier((got, gate))
-    top, bottom = swap(got[4][:half], 2), swap(got[2][half:], 4)
-    got[3], got[5] = swap(got[2], 1), swap(got[4], 1)
-    near = [(got[k], got[k]) for k in range(6)]
-    return near + [(top, bottom), (swap(top, 1), swap(bottom, 1))]
-
-
-def place_rows_kernel(height, place, *refs):
-    *pieces, out, sems = refs
+    return finish, pieces, beside
+
+
+class PlaneGather:
+    def __init__(self, own):
+        self.got = {0: own}
+
+    def first(self):
+        own, swap = self.got[0], plane()[3]
+        self.got.update({bit: swap(own, bit) for bit in (2, 4, 1)})
+        return self.got
+
+    def second(self):
+        got, swap, half = self.got, plane()[3], self.got[0].shape[0] // 2
+        self.far = [swap(got[4][:half], 2), swap(got[2][half:], 4)]
+        got[3], got[5] = swap(got[2], 1), swap(got[4], 1)
+        return self.far, got[3], got[5]
+
+    def third(self):
+        swap = plane()[3]
+        self.far_other = [swap(value, 1) for value in self.far]
+        return self.far_other
+
+    def where(self, bits):
+        return lax.axis_index("dp").astype(jnp.int32) ^ jnp.array(bits, dtype=jnp.int32)
+
+    def lay(self, height, rows):
+        arrays = [self.got[k] for k in range(6)]
+        return place_rows(arrays, self.where(list(range(6))), height, rows, [])
+
+    def lay_far(self, height, laid):
+        arrays = [self.far[0], self.far_other[0]]
+        return place_rows(arrays, self.where([6, 7]), height, laid.shape[0], [laid])
+
+    def last(self):
+        arrays = [self.got[k] for k in range(6)] + [self.far[1], self.far_other[1]]
+        return arrays, self.where(list(range(8)))
+
+
+def place_rows_kernel(height, n_arrays, place, *refs):
+    arrays, (out, sems) = refs[:n_arrays], refs[-2:]
     copies = []
-    for k, piece in enumerate(pieces):
-        start = pl.multiple_of((place[0] ^ k) * height, height)
+    for k, array in enumerate(arrays):
+        start = pl.multiple_of(place[k] * height, height)
         copies.append(
             pltpu.make_async_copy(
-                piece.at[pl.ds(0, height), :], out.at[pl.ds(start, height), :], sems.at[k]
+                array.at[pl.ds(0, height), :], out.at[pl.ds(start, height), :], sems.at[k]
             )
         )
     for copy in copies:
@@ -329,48 +380,50 @@
         copy.wait()
 
 
-def place_rows(pieces, height):
-    cols = pieces[0].shape[1]
+def place_rows(arrays, place, height, rows, into):
+    cols = arrays[0].shape[1]
+    anywhere = pl.BlockSpec(memory_space=pl.ANY)
     return pl.pallas_call(
-        functools.partial(place_rows_kernel, height),
+        functools.partial(place_rows_kernel, height, len(arrays)),
         in_specs=[pl.BlockSpec(memory_space=pltpu.SMEM)]
-        + [pl.BlockSpec(memory_space=pltpu.VMEM)] * len(pieces),
-        out_specs=pl.BlockSpec(memory_space=pl.ANY),
-        out_shape=jax.ShapeDtypeStruct((height * len(pieces), cols), pieces[0].dtype),
-        scratch_shapes=[pltpu.SemaphoreType.DMA((len(pieces),))],
+        + [pl.BlockSpec(memory_space=pltpu.VMEM)] * len(arrays)
+        + [anywhere] * len(into),
+        out_specs=anywhere,
+        out_shape=jax.ShapeDtypeStruct((rows, cols), arrays[0].dtype),
+        scratch_shapes=[pltpu.SemaphoreType.DMA((len(arrays),))],
+        input_output_aliases={1 + len(arrays): 0} if into else {},
         cost_estimate=pl.CostEstimate(
-            flops=0, bytes_accessed=4 * height * cols * len(pieces), transcendentals=0
+            flops=0, bytes_accessed=4 * height * cols * len(arrays), transcendentals=0
         ),
         compiler_params=pltpu.CompilerParams(vmem_limit_bytes=VMEM_WHOLE),
         name="place_rows",
-    )(lax.axis_index("dp").astype(jnp.int32).reshape(1), *pieces)
-
-
-def input_kernel(offsets, place, *refs):
+    )(place, *arrays, *into)
+
+
+def input_kernel(n_blocks, place, *refs):
     *arrays, out = refs
-    n_blocks = place.shape[0] - 1
     pieces, rows = arrays[:n_blocks], arrays[n_blocks:]
     share = out.shape[1] // len(rows)
-    for k, (held, offset) in enumerate(zip(rows, offsets)):
+    for k, held in enumerate(rows):
+        first = held.shape[0] - n_blocks * share
         total = jnp.zeros((out.shape[0], share), jnp.float32)
         for s, piece in enumerate(pieces):
             total = total + lax.dot_general(
                 piece[...],
-                held[offset + s * share : offset + (s + 1) * share, :],
+                held[first + s * share : first + (s + 1) * share, :],
                 (((1,), (1,)), ((), ())),
                 preferred_element_type=jnp.float32,
             )
-        start = pl.multiple_of((place[0] ^ k) * share, share)
+        start = pl.multiple_of(place[k] * share, share)
         out[:, pl.ds(start, share)] = total.astype(out.dtype)
 
 
-def input_gradient(pieces, rows, offsets, feats):
+def input_gradient(pieces, arrays, place, feats):
     length, cols = pieces[0].shape
-    place = jnp.broadcast_to(lax.axis_index("dp").astype(jnp.int32), (len(pieces) + 1,))
     (d_tokens,) = on_chip(
-        functools.partial(input_kernel, offsets),
+        functools.partial(input_kernel, len(pieces)),
         place,
-        pieces + rows,
+        pieces + arrays,
         [jax.ShapeDtypeStruct((length, feats), jnp.bfloat16)],
         2 * length * feats * cols * len(pieces),
         "input_gradient",
@@ -390,21 +443,21 @@
         length, feats = tokens.shape
         cols = cached.shape[1]
 
-        share = feats // n_dp
-
-        def block_for(z):
-            return lax.dynamic_slice_in_dim(cached, z * feats + me_dp * share, share, 0)
-
-        blocks = [block_for(me_z)] + [pair(block_for(me_z ^ s), s) for s in range(1, n_z)]
-
         master_new, moment_new, second_new, own_cache = optimizer(
             cached, master, moment, second, grad
         )
 
+        share = feats // n_dp
+
+        def block_for(z):
+            return lax.dynamic_slice_in_dim(cached, z * feats + me_dp * share, share, 0)
+
+        blocks = [block_for(me_z)] + [pair(block_for(me_z ^ s), s) for s in range(1, n_z)]
+
         total = jnp.zeros((length, cols), jnp.float32)
         total, held = absorb(tokens, me_z, cached, total, None, n_z)
         if tuned:
-            bundle = jnp.concatenate([own_cache] + blocks, axis=0)
+            gather = PlaneGather(jnp.concatenate([own_cache] + blocks, axis=0))
         from_low, from_high, merged = tokens, tokens, None
         for s in range(1, n_z):
             up = [(z, z + 1) for z in range(s - 1, n_z - 1)]
@@ -413,33 +466,44 @@
             if merged is None:
                 from_low = lax.ppermute(from_low, "tensor", up)
                 from_high = lax.ppermute(from_high, "tensor", down)
+                arrived = from_low, from_high
             else:
                 merged = lax.ppermute(merged, "tensor", up + down)
+                arrived = merged
+            if tuned:
+                if s == 1:
+                    rounds = gather.got
+                elif s == 2:
+                    rounds = gather.first()
+                elif s == 3:
+                    rounds = gather.second()
+                    laid = gather.lay(own_cache.shape[0], cached.shape[0])
+                    rounds = (rounds, laid)
+                arrived, held, rounds = lax.optimization_barrier((arrived, held, rounds))
+                if s < 3:
+                    gather.got = rounds
+                else:
+                    (gather.far, gather.got[3], gather.got[5]), laid = rounds
+            if merged is None:
+                from_low, from_high = arrived
+            else:
+                merged = arrived
             if merged is None and 2 * s >= n_z:
                 merged = jnp.where(me_z >= s, from_low, from_high)
-            if tuned and s == 1:
-                from_low, from_high, held, bundle = lax.optimization_barrier(
-                    (from_low, from_high, held, bundle)
-                )
-            if tuned and s == n_z - 1:
-                gathered = gather_plane(bundle, merged)
-                new_cache = place_rows([cache for cache, _ in gathered], own_cache.shape[0])
-                total, new_cache, gathered = lax.optimization_barrier((total, new_cache, gathered))
             if merged is None:
                 total, held = absorb(from_low, low, cached, total, held, n_z)
                 total, held = absorb(from_high, high, cached, total, held, n_z)
             else:
-                origin = jnp.where(me_z >= s, low, high)
-                total, held = absorb(merged, origin, cached, total, held, n_z)
+                total, held = absorb(
+                    merged, jnp.where(me_z >= s, low, high), cached, total, held, n_z
+                )
 
         doc_ids = segments[0]
         position = jnp.arange(length)
         allowed = (doc_ids[:, None] == doc_ids[None, :]) & (position[:, None] <= position[None, :])
         allowed = allowed.astype(jnp.float32)
 
-        d_queries, d_projected = attention_backward(
-            total.astype(jnp.bfloat16), queries, d_out, allowed
-        )
+        d_queries, d_projected = attention_backward([total], queries, d_out, allowed)
 
         pieces = [d_projected]
         s = 1
@@ -447,10 +511,11 @@
             pieces = pieces + [pair(piece, s) for piece in pieces]
             s *= 2
         if tuned:
-            finish, pieces = weight_sum(held, d_projected, pieces)
-            rows = [rows for _, rows in gathered]
-            offsets = [array.shape[0] - n_z * share for array in rows]
-            new_grad, d_tokens = finish(input_gradient(pieces, rows, offsets, feats))
+            d_projected, gather.far_other = lax.optimization_barrier((d_projected, gather.third()))
+            pieces[0] = d_projected
+            new_cache = gather.lay_far(own_cache.shape[0], laid)
+            finish, pieces, new_cache = weight_sum(held, d_projected, pieces, new_cache)
+            new_grad, d_tokens = finish(input_gradient(pieces, *gather.last(), feats))
         else:
             new_cache = lax.all_gather(own_cache, "dp", axis=0, tiled=True)
             rows = lax.all_gather(jnp.stack(blocks), "dp", axis=0)

time: 182 us -> 158 us (0.87)
  waiting for transfers between devices: 89 us -> 58.3 us
  local copies, waits for them, and re-layouts: 8.91 us -> 16.4 us
  other arithmetic: 5.68 us -> 3.35 us
    ppermute x1, waiting for transfers between devices: 23.3 us -> 10.7 us  [body(): merged = lax.ppermute(merged, 'tensor', up + down)]
    ppermute x2, waiting for transfers between devices: 22 us -> 13.7 us  [body(): from_high = lax.ppermute(from_high, 'tensor', down)]
    unnamed x21 -> x23, local copies, waits for them, and re-layouts: 5.22 us -> 13.4 us
    ppermute x17 -> x15, waiting for transfers between devices: 12.9 us -> 5.64 us  [swap(): return lax.ppermute(value, 'dp', [(i, i ^ bit) for i in range(8)])]
    pallas_call x4 -> x3, Pallas kernels: 9.33 us -> 5.75 us  [on_chip(): pl.pallas_call(kernel, in_specs=[pl.BlockSpec(memory_space=pltpu.SMEM)] +...]
    pallas_call x6 -> x8, Pallas kernels: 21.1 us -> 24.7 us  [the longest x5 12.5 us: absorb(): pl.pallas_call(absorb_kernel, in_specs=[pl.BlockSpec(memory_space=pltpu.S...]
    ppermute x6, waiting for transfers between devices: 30.9 us -> 28.2 us  [pair(): return lax.ppermute(value, 'tensor', [(z, z ^ s) for z in range(n_z)])]
    another operation x4 -> x3, other arithmetic: 2.53 us -> 0.23 us  [absorb(): jnp.stack([jnp.clip(index, 0, n_chunks - 1), jnp.where(inside, index, n_c...]
  transfers between devices with their start and end apart: 28 -> 26, of which waited for: 13 -> 13; matrix products, arithmetic and copies ran while one was open for 5% -> 5% of each run, Pallas kernels for 18% -> 26%
where the time goes in v7:
time: 158 us; the launch traced here: 157 us
  waiting for transfers between devices  58.3 us (37%)
  Pallas kernels  47.1 us (30%)
  starting transfers between devices  30.8 us (19%)
  local copies, waits for them, and re-layouts  16.4 us (10%)
  other arithmetic  3.35 us (2%)
    ppermute x6, waiting for transfers between devices, pair(): return lax.ppermute(value, 'tensor', [(z, z ^ s) for z in range(n_z)])  28.2 us
    ppermute x2, waiting for transfers between devices, body(): from_high = lax.ppermute(from_high, 'tensor', down)  13.7 us
    unnamed x23, local copies, waits for them, and re-layouts  13.4 us
    pallas_call x5, Pallas kernels, absorb(): pl.pallas_call(absorb_kernel, in_specs=[pl.BlockSpec(memory_space=pltpu.S...  12.5 us
    pallas_call x3, Pallas kernels, weight_parts(): pl.pallas_call(functools.partial(weight_kernel, groups), in_specs=[pl.Blo...  11.7 us
    ppermute x15, starting transfers between devices, swap(): return lax.ppermute(value, 'dp', [(i, i ^ bit) for i in range(8)])  11 us
    ppermute x1, waiting for transfers between devices, body(): merged = lax.ppermute(merged, 'tensor', up + down)  10.7 us
    ppermute x6, starting transfers between devices, pair(): return lax.ppermute(value, 'tensor', [(z, z ^ s) for z in range(n_z)])  8.23 us
  transfers between devices with their start and end apart: 26, of which 13 were waited for; matrix products, arithmetic and copies ran while one was open for 5% of the time, Pallas kernels for 26%

profile of v7, /device:TPU:0, one launch (start us, length us, event | category | flops | bytes accessed | tf_op | source)
XLA Modules:
  0.0 156.9 jit_solution(8511242051030186859)
XLA Ops:
  0.6 5.9 %collective-permute-start = (bf16[256,2048]{1,0:T(8,128)(2,1)}, bf16[256,2048]{1,0:T(8,128)(2,1)}, u32[]{:S(2)}, u32[]{:S(2)}) collective-permute-start(bf16[256,2048]{1,0:T(8,128)(2,1)} %chunk.1), channel_id=1, source_target_pairs={{0,1},{1,2},{2,3},{4,5},{5,6},{6,7},{8,9},{9,10},{10,11},{12,13},{... | collective-permute-start | bytes 3145736 | tf_op jit(solution)/shard_map/ppermute | solution.py:467
  6.5 1.3 collective-permute-start.1
  7.8 4.9 %optimizer.1 = (f32[1024,256]{1,0:T(8,128)}, f32[1024,256]{1,0:T(8,128)}, f32[1024,256]{1,0:T(8,128)}, bf16[1024,256]{1,0:T(8,128)(2,1)}) custom-call(s32[1]{0:T(128)} %bitcast.place, bf16[8192,256]{1,0:T(8,128)(2,1)} %cached.11, f32[1024,256]{1,0:T(8,128)} %master.1, f32[1024,256]{1,0:T(8,128)} %moment.1, f32[1024,256]{1,0:T(8,128)} %second.1, f32[1024,256]{1,0:T(8,128)} %grad.1), custom_call_target="tpu_custom_call" | custom-call | flops 10485760 | bytes 8388608 | tf_op jit(solution)/shard_map/optimizer/pallas_call | solution.py:51
  12.8 1.1 constant_dynamic-update-slice_fusion.3
  13.9 1.1 constant_dynamic-slice_fusion
  15.0 2.7 %collective-permute-start.2 = (bf16[256,256]{1,0:T(8,128)(2,1)S(1)}, bf16[256,256]{1,0:T(8,128)(2,1)S(1)}, u32[]{:S(2)}, u32[]{:S(2)}) collective-permute-start(bf16[256,256]{1,0:T(8,128)(2,1)S(1)} %get-tuple-element.123), channel_id=1, source_target_pairs={{0,1},{1,0},{2,3},{3,2},{4,5},{5,4},{6,7},{7,6},{8,9},{9,8},{10,11... | collective-permute-start | bytes 393224 | tf_op jit(solution)/shard_map/ppermute | solution.py:438
  17.7 2.6 %collective-permute-start.3 = (bf16[256,256]{1,0:T(8,128)(2,1)S(1)}, bf16[256,256]{1,0:T(8,128)(2,1)S(1)}, u32[]{:S(2)}, u32[]{:S(2)}) collective-permute-start(bf16[256,256]{1,0:T(8,128)(2,1)S(1)} %get-tuple-element.122), channel_id=1, source_target_pairs={{0,2},{1,3},{2,0},{3,1},{4,6},{5,7},{6,4},{7,5},{8,10},{9,11},{10,... | collective-permute-start | bytes 393224 | tf_op jit(solution)/shard_map/ppermute | solution.py:438
  20.4 2.2 %copy-done = bf16[8192,256]{1,0:T(8,128)(2,1)S(1)} copy-done((bf16[8192,256]{1,0:T(8,128)(2,1)S(1)}, bf16[8192,256]{1,0:T(8,128)(2,1)}, u32[]{:S(2)}) %copy-start) | copy-done | bytes 4194328
  22.6 1.2 copy-done.4
  23.8 2.0 %absorb.5 = (f32[256,256]{1,0:T(8,128)S(1)}, bf16[32,2048,256]{2,1,0:T(8,128)(2,1)}) custom-call(s32[2]{0:T(128)S(1)} %get-tuple-element.126.place, bf16[256,2048]{1,0:T(8,128)(2,1)S(1)} %copy-done.4, f32[256,256]{1,0:T(8,128)S(1)} %broadcast_in_dim.2.total, bf16[8192,256]{1,0:T(8,128)(2,1)S(1)} %copy-done), custom_call_target="tpu_custom_call" | custom-call | flops 268435456 | bytes 3145728 | tf_op jit(solution)/shard_map/absorb/pallas_call | solution.py:107
  25.8 13.0 %collective-permute-done.2 = bf16[256,256]{1,0:T(8,128)(2,1)S(1)} collective-permute-done((bf16[256,256]{1,0:T(8,128)(2,1)S(1)}, bf16[256,256]{1,0:T(8,128)(2,1)S(1)}, u32[]{:S(2)}, u32[]{:S(2)}) %collective-permute-start.2) | collective-permute-done | bytes 131104 | tf_op jit(solution)/shard_map/ppermute | solution.py:438
  38.8 4.3 %collective-permute-done.3 = bf16[256,256]{1,0:T(8,128)(2,1)S(1)} collective-permute-done((bf16[256,256]{1,0:T(8,128)(2,1)S(1)}, bf16[256,256]{1,0:T(8,128)(2,1)S(1)}, u32[]{:S(2)}, u32[]{:S(2)}) %collective-permute-start.3) | collective-permute-done | bytes 131104 | tf_op jit(solution)/shard_map/ppermute | solution.py:438
  43.2 1.6 %collective-permute-start.5 = (bf16[256,2048]{1,0:T(8,128)(2,1)}, bf16[256,2048]{1,0:T(8,128)(2,1)}, u32[]{:S(2)}, u32[]{:S(2)}) collective-permute-start(bf16[256,2048]{1,0:T(8,128)(2,1)} %collective-permute-done.chunk), channel_id=1, source_target_pairs={{1,2},{2,3},{5,6},{6,7},{9,10},{10,11},{13,14},{14,15},{17,18},{18... | collective-permute-start | bytes 3145736 | tf_op jit(solution)/shard_map/ppermute | solution.py:467
  44.9 1.3 collective-permute-start.6
  46.2 1.6 collective-permute-start.8
  47.8 1.5 collective-permute-start.9
  49.4 2.2 %copy-done.1 = bf16[8192,256]{1,0:T(8,128)(2,1)S(1)} copy-done((bf16[8192,256]{1,0:T(8,128)(2,1)S(1)}, bf16[8192,256]{1,0:T(8,128)(2,1)}, u32[]{:S(2)}) %copy-start.1) | copy-done | bytes 4194328
  51.6 2.6 %absorb.6 = (f32[256,256]{1,0:T(8,128)S(1)}, bf16[32,2048,256]{2,1,0:T(8,128)(2,1)}) custom-call(s32[2]{0:T(128)S(1)} %get-tuple-element.128.place, bf16[256,2048]{1,0:T(8,128)(2,1)} %collective-permute-done.chunk, f32[256,256]{1,0:T(8,128)S(1)} %get-tuple-element.71.total, bf16[8192,256]{1,0:T(8,128)(2,1)S(1)} %copy-done.1, ...), custom_call_target="tpu_custom_call", output_to_operand_aliasing={{1}: (4, {})} | custom-call | flops 268435456 | bytes 3145728 | tf_op jit(solution)/shard_map/absorb/pallas_call | solution.py:107
  54.2 2.6 %absorb.7 = (f32[256,256]{1,0:T(8,128)S(1)}, bf16[32,2048,256]{2,1,0:T(8,128)(2,1)}) custom-call(s32[2]{0:T(128)S(1)} %get-tuple-element.127.place, bf16[256,2048]{1,0:T(8,128)(2,1)} %collective-permute-done.1.chunk, f32[256,256]{1,0:T(8,128)S(1)} %get-tuple-element.73.total, bf16[8192,256]{1,0:T(8,128)(2,1)S(1)} %copy-done.1, ...), custom_call_target="tpu_custom_call", output_to_operand_aliasing={{1}: (4, {})} | custom-call | flops 268435456 | bytes 3145728 | tf_op jit(solution)/shard_map/absorb/pallas_call | solution.py:107
  57.6 13.7 %collective-permute-done.6 = bf16[256,2048]{1,0:T(8,128)(2,1)} collective-permute-done((bf16[256,2048]{1,0:T(8,128)(2,1)}, bf16[256,2048]{1,0:T(8,128)(2,1)}, u32[]{:S(2)}, u32[]{:S(2)}) %collective-permute-start.6) | collective-permute-done | bytes 1048608 | tf_op jit(solution)/shard_map/ppermute | solution.py:468
  71.8 1.2 collective-permute-done.9.refs_4_.refs_8_
  73.5 2.3 %broadcast_select_fusion.chunk = bf16[256,2048]{1,0:T(8,128)(2,1)} fusion(bf16[256,2048]{1,0:T(8,128)(2,1)} %collective-permute-done.5, bf16[256,2048]{1,0:T(8,128)(2,1)} %collective-permute-done.6, pred[]{:T(512)S(6)} %ge.24), kind=kLoop, calls=%fused_computation | loop fusion | flops 524288 | bytes 3145729 | tf_op jit(solution)/shard_map/jit(_where)/select_n | solution.py:492
  75.8 1.5 collective-permute-start.10
  77.3 0.8 slice.6
  78.1 0.8 slice.7
  79.5 1.5 collective-permute-start.12
  81.1 2.2 %copy-done.2 = bf16[8192,256]{1,0:T(8,128)(2,1)S(1)} copy-done((bf16[8192,256]{1,0:T(8,128)(2,1)S(1)}, bf16[8192,256]{1,0:T(8,128)(2,1)}, u32[]{:S(2)}) %copy-start.2) | copy-done | bytes 4194328
  83.3 0.9 copy-done.6
  84.2 2.6 %absorb.8 = (f32[256,256]{1,0:T(8,128)S(1)}, bf16[32,2048,256]{2,1,0:T(8,128)(2,1)}) custom-call(s32[2]{0:T(128)S(1)} %pad_add_fusion.4.place, bf16[256,2048]{1,0:T(8,128)(2,1)} %broadcast_select_fusion.chunk, f32[256,256]{1,0:T(8,128)S(1)} %copy-done.6, bf16[8192,256]{1,0:T(8,128)(2,1)S(1)} %copy-done.2, ...), custom_call_target="tpu_custom_call", output_to_operand_aliasing={{1}: (4, {})} | custom-call | flops 268435456 | bytes 3145728 | tf_op jit(solution)/shard_map/absorb/pallas_call | solution.py:107
  86.9 3.6 %place_rows.2.refs_2_ = bf16[8192,256]{1,0:T(8,128)(2,1)} custom-call(s32[6]{0:T(128)S(1)} %iota_xor_fusion.1.place, bf16[2048,256]{1,0:T(8,128)(2,1)S(1)} %constant_dynamic-update-slice_fusion.refs_0_.refs_4_, bf16[2048,256]{1,0:T(8,128)(2,1)} %collective-permute-done.7.refs_1_.refs_5_, bf16[2048,256]{1,0:T(8,128)(2,1)S(1)} %collective-permute-done.8.refs_2_.refs_6_, ...), custom_call_target="tpu_custom_call" | custom-call | bytes 6291456 | tf_op jit(solution)/shard_map/place_rows/pallas_call | solution.py:386
  90.5 2.6 %collective-permute-done.11.refs_0_ = bf16[1024,256]{1,0:T(8,128)(2,1)} collective-permute-done((bf16[1024,256]{1,0:T(8,128)(2,1)}, bf16[1024,256]{1,0:T(8,128)(2,1)}, u32[]{:S(2)}, u32[]{:S(2)}) %collective-permute-start.11) | collective-permute-done | bytes 524320 | tf_op jit(solution)/shard_map/ppermute | solution.py:286
  93.3 10.7 %collective-permute-done.10.chunk = bf16[256,2048]{1,0:T(8,128)(2,1)} collective-permute-done((bf16[256,2048]{1,0:T(8,128)(2,1)}, bf16[256,2048]{1,0:T(8,128)(2,1)}, u32[]{:S(2)}, u32[]{:S(2)}) %collective-permute-start.10) | collective-permute-done | bytes 1048608 | tf_op jit(solution)/shard_map/ppermute | solution.py:471
  104.7 0.8 fusion.1.refs_1_
  105.5 2.2 %copy-done.3 = bf16[8192,256]{1,0:T(8,128)(2,1)S(1)} copy-done((bf16[8192,256]{1,0:T(8,128)(2,1)S(1)}, bf16[8192,256]{1,0:T(8,128)(2,1)}, u32[]{:S(2)}) %copy-start.3) | copy-done | bytes 4194328
  107.7 2.6 %absorb.9 = (f32[256,256]{1,0:T(8,128)S(1)}, bf16[32,2048,256]{2,1,0:T(8,128)(2,1)}) custom-call(s32[2]{0:T(128)S(1)} %get-tuple-element.125.place, bf16[256,2048]{1,0:T(8,128)(2,1)} %collective-permute-done.10.chunk, f32[256,256]{1,0:T(8,128)S(1)} %get-tuple-element.87.total, bf16[8192,256]{1,0:T(8,128)(2,1)S(1)} %copy-done.3, ...), custom_call_target="tpu_custom_call", output_to_operand_aliasing={{1}: (4, {})} | custom-call | flops 268435456 | bytes 3145728 | tf_op jit(solution)/shard_map/absorb/pallas_call | solution.py:107
  111.0 6.4 %attention.1 = (bf16[256,1024]{1,0:T(8,128)(2,1)}, bf16[256,256]{1,0:T(8,128)(2,1)}) custom-call(f32[256,256]{1,0:T(8,128)} %copy-done.7, f32[256,256]{1,0:T(8,128)} %fusion.1.refs_1_, bf16[256,1024]{1,0:T(8,128)(2,1)} %refs_2_.1, bf16[256,1024]{1,0:T(8,128)(2,1)} %refs_3_.1), custom_call_target="tpu_custom_call" | custom-call | flops 805306368 | bytes 2097152 | tf_op jit(solution)/shard_map/attention/pallas_call | solution.py:177
  117.5 4.7 %weight_other.1 = (bf16[4,1024,128]{2,1,0:T(8,128)(2,1)}, bf16[4,1024,128]{2,1,0:T(8,128)(2,1)}) custom-call(s32[5]{0:T(128)S(1)} %stack.101.place, bf16[32,2048,256]{2,1,0:T(8,128)(2,1)} %get-tuple-element.89.held, bf16[256,256]{1,0:T(8,128)(2,1)} %get-tuple-element.110.d_projected.refs_0_), custom_call_target="tpu_custom_call" | custom-call | flops 536870912 | bytes 4194304 | tf_op jit(solution)/shard_map/weight_other/pallas_call | solution.py:249
  122.8 5.6 %collective-permute-done.18.refs_1_ = bf16[256,256]{1,0:T(8,128)(2,1)S(1)} collective-permute-done((bf16[256,256]{1,0:T(8,128)(2,1)}, bf16[256,256]{1,0:T(8,128)(2,1)S(1)}, u32[]{:S(2)}, u32[]{:S(2)}) %collective-permute-start.18) | collective-permute-done | bytes 131104 | tf_op jit(solution)/shard_map/ppermute | solution.py:438
  128.4 3.5 %weight_send.1 = (bf16[2,1024,128]{2,1,0:T(8,128)(2,1)S(1)}, bf16[2,1024,128]{2,1,0:T(8,128)(2,1)S(1)}) custom-call(s32[5]{0:T(128)S(1)} %stack.84.place, bf16[32,2048,256]{2,1,0:T(8,128)(2,1)} %get-tuple-element.89.held, bf16[256,256]{1,0:T(8,128)(2,1)} %get-tuple-element.110.d_projected.refs_0_, bf16[4,1024,128]{2,1,0:T(8,128)(2,1)} %collective-permute-done.17.refs_0_), custom_call_target="tpu_custom_call" | custom-call | flops 268435456 | bytes 2097152 | tf_op jit(solution)/shard_map/weight_send/pallas_call | solution.py:249
  132.5 1.5 collective-permute-start.20
  134.1 2.6 %collective-permute-start.21 = (bf16[256,256]{1,0:T(8,128)(2,1)}, bf16[256,256]{1,0:T(8,128)(2,1)S(1)}, u32[]{:S(2)}, u32[]{:S(2)}) collective-permute-start(bf16[256,256]{1,0:T(8,128)(2,1)} %get-tuple-element.110.d_projected.refs_0_), channel_id=1, source_target_pairs={{0,2},{1,3},{2,0},{3,1},{4,6},{5,7},{6,4},{7,5},{8,10},{9,11},{10,... | collective-permute-start | bytes 393224 | tf_op jit(solution)/shard_map/ppermute | solution.py:438
  137.0 2.2 %place_rows.3 = bf16[8192,256]{1,0:T(8,128)(2,1)} custom-call(s32[2]{0:T(128)S(1)} %broadcast_xor_fusion.place, bf16[1024,256]{1,0:T(8,128)(2,1)} %collective-permute-done.11.refs_0_, bf16[1024,256]{1,0:T(8,128)(2,1)} %collective-permute-done.15.refs_1_, bf16[8192,256]{1,0:T(8,128)(2,1)} %place_rows.2.refs_2_), custom_call_target="tpu_custom_call", output_to_operand_aliasing={{}: (3, {})} | custom-call | bytes 2097152 | tf_op jit(solution)/shard_map/place_rows/pallas_call | solution.py:386
  139.2 3.5 %weight_keep.1 = (f32[2,1024,128]{2,1,0:T(8,128)S(1)}, f32[2,1024,128]{2,1,0:T(8,128)S(1)}) custom-call(s32[5]{0:T(128)S(1)} %stack.84.place, bf16[32,2048,256]{2,1,0:T(8,128)(2,1)} %get-tuple-element.89.held, bf16[256,256]{1,0:T(8,128)(2,1)} %get-tuple-element.110.d_projected.refs_0_, bf16[4,1024,128]{2,1,0:T(8,128)(2,1)} %collective-permute-done.23.refs_0_), custom_call_target="tpu_custom_call" | custom-call | flops 268435456 | bytes 2097152 | tf_op jit(solution)/shard_map/weight_keep/pallas_call | solution.py:249
  142.7 3.5 %collective-permute-done.21.refs_2_ = bf16[256,256]{1,0:T(8,128)(2,1)S(1)} collective-permute-done((bf16[256,256]{1,0:T(8,128)(2,1)}, bf16[256,256]{1,0:T(8,128)(2,1)S(1)}, u32[]{:S(2)}, u32[]{:S(2)}) %collective-permute-start.21) | collective-permute-done | bytes 131104 | tf_op jit(solution)/shard_map/ppermute | solution.py:438
  146.2 1.8 %collective-permute-done.22.refs_3_ = bf16[256,256]{1,0:T(8,128)(2,1)S(1)} collective-permute-done((bf16[256,256]{1,0:T(8,128)(2,1)S(1)}, bf16[256,256]{1,0:T(8,128)(2,1)S(1)}, u32[]{:S(2)}, u32[]{:S(2)}) %collective-permute-start.22) | collective-permute-done | bytes 131104 | tf_op jit(solution)/shard_map/ppermute | solution.py:438
  148.7 1.5 collective-permute-start.25
  150.2 4.5 %input_gradient.1 = bf16[256,2048]{1,0:T(8,128)(2,1)} custom-call(s32[8]{0:T(128)S(1)} %iota_xor_fusion.place, bf16[256,256]{1,0:T(8,128)(2,1)} %get-tuple-element.110.d_projected.refs_0_, bf16[256,256]{1,0:T(8,128)(2,1)S(1)} %collective-permute-done.18.refs_1_, bf16[256,256]{1,0:T(8,128)(2,1)S(1)} %collective-permute-done.21.refs_2_, ...), custom_call_target="tpu_custom_call" | custom-call | flops 1073741824 | bytes 8912896 | tf_op jit(solution)/shard_map/input_gradient/pallas_call | solution.py:73
  155.7 1.1 weight_finish.1
  (57 shorter events, 7.4 us)
Async XLA Ops:
  0.6 42.6 %collective-permute-start = (bf16[256,2048]{1,0:T(8,128)(2,1)}, bf16[256,2048]{1,0:T(8,128)(2,1)}, u32[]{:S(2)}, u32[]{:S(2)}) collective-permute-start(bf16[256,2048]{1,0:T(8,128)(2,1)} %chunk.1), channel_id=1, source_target_pairs={{0,1},{1,2},{2,3},{4,5},{5,6},{6,7},{8,9},{9,10},{10,11},{12,13},{... | collective-permute-start | bytes 3145736 | tf_op jit(solution)/shard_map/ppermute | solution.py:467
  6.5 36.7 %collective-permute-start.1 = (bf16[256,2048]{1,0:T(8,128)(2,1)}, bf16[256,2048]{1,0:T(8,128)(2,1)}, u32[]{:S(2)}, u32[]{:S(2)}) collective-permute-start(bf16[256,2048]{1,0:T(8,128)(2,1)} %chunk.1), channel_id=1, source_target_pairs={{1,0},{2,1},{3,2},{5,4},{6,5},{7,6},{9,8},{10,9},{11,10},{13,12},{... | collective-permute-start | bytes 3145736 | tf_op jit(solution)/shard_map/ppermute | solution.py:468
  15.0 23.8 %collective-permute-start.2 = (bf16[256,256]{1,0:T(8,128)(2,1)S(1)}, bf16[256,256]{1,0:T(8,128)(2,1)S(1)}, u32[]{:S(2)}, u32[]{:S(2)}) collective-permute-start(bf16[256,256]{1,0:T(8,128)(2,1)S(1)} %get-tuple-element.123), channel_id=1, source_target_pairs={{0,1},{1,0},{2,3},{3,2},{4,5},{5,4},{6,7},{7,6},{8,9},{9,8},{10,11... | collective-permute-start | bytes 393224 | tf_op jit(solution)/shard_map/ppermute | solution.py:438
  17.7 25.4 %collective-permute-start.3 = (bf16[256,256]{1,0:T(8,128)(2,1)S(1)}, bf16[256,256]{1,0:T(8,128)(2,1)S(1)}, u32[]{:S(2)}, u32[]{:S(2)}) collective-permute-start(bf16[256,256]{1,0:T(8,128)(2,1)S(1)} %get-tuple-element.122), channel_id=1, source_target_pairs={{0,2},{1,3},{2,0},{3,1},{4,6},{5,7},{6,4},{7,5},{8,10},{9,11},{10,... | collective-permute-start | bytes 393224 | tf_op jit(solution)/shard_map/ppermute | solution.py:438
  20.3 22.8 %collective-permute-start.4 = (bf16[256,256]{1,0:T(8,128)(2,1)S(1)}, bf16[256,256]{1,0:T(8,128)(2,1)S(1)}, u32[]{:S(2)}, u32[]{:S(2)}) collective-permute-start(bf16[256,256]{1,0:T(8,128)(2,1)S(1)} %get-tuple-element.121), channel_id=1, source_target_pairs={{0,3},{1,2},{2,1},{3,0},{4,7},{5,6},{6,5},{7,4},{8,11},{9,10},{10,... | collective-permute-start | bytes 393224 | tf_op jit(solution)/shard_map/ppermute | solution.py:438
  20.4 2.2 %copy-start = (bf16[8192,256]{1,0:T(8,128)(2,1)S(1)}, bf16[8192,256]{1,0:T(8,128)(2,1)}, u32[]{:S(2)}) copy-start(bf16[8192,256]{1,0:T(8,128)(2,1)} %cached.11) | copy-start | bytes 12582916
  22.6 1.2 copy-start.4
  43.2 14.4 %collective-permute-start.5 = (bf16[256,2048]{1,0:T(8,128)(2,1)}, bf16[256,2048]{1,0:T(8,128)(2,1)}, u32[]{:S(2)}, u32[]{:S(2)}) collective-permute-start(bf16[256,2048]{1,0:T(8,128)(2,1)} %collective-permute-done.chunk), channel_id=1, source_target_pairs={{1,2},{2,3},{5,6},{6,7},{9,10},{10,11},{13,14},{14,15},{17,18},{18... | collective-permute-start | bytes 3145736 | tf_op jit(solution)/shard_map/ppermute | solution.py:467
  44.9 26.4 %collective-permute-start.6 = (bf16[256,2048]{1,0:T(8,128)(2,1)}, bf16[256,2048]{1,0:T(8,128)(2,1)}, u32[]{:S(2)}, u32[]{:S(2)}) collective-permute-start(bf16[256,2048]{1,0:T(8,128)(2,1)} %collective-permute-done.1.chunk), channel_id=1, source_target_pairs={{1,0},{2,1},{5,4},{6,5},{9,8},{10,9},{13,12},{14,13},{17,16},{18,1... | collective-permute-start | bytes 3145736 | tf_op jit(solution)/shard_map/ppermute | solution.py:468
  46.1 25.2 %collective-permute-start.7 = (bf16[2048,256]{1,0:T(8,128)(2,1)S(1)}, bf16[2048,256]{1,0:T(8,128)(2,1)}, u32[]{:S(2)}, u32[]{:S(2)}) collective-permute-start(bf16[2048,256]{1,0:T(8,128)(2,1)S(1)} %constant_dynamic-update-slice_fusion.refs_0_.refs_4_), channel_id=1, source_target_pairs={{0,4},{4,0},{8,12},{12,8},{16,20},{20,16},{24,28},{28,24},{1,5},{5... | collective-permute-start | bytes 3145736 | tf_op jit(solution)/shard_map/ppermute | solution.py:286
  46.2 25.6 %collective-permute-start.8 = (bf16[2048,256]{1,0:T(8,128)(2,1)S(1)}, bf16[2048,256]{1,0:T(8,128)(2,1)S(1)}, u32[]{:S(2)}, u32[]{:S(2)}) collective-permute-start(bf16[2048,256]{1,0:T(8,128)(2,1)S(1)} %constant_dynamic-update-slice_fusion.refs_0_.refs_4_), channel_id=1, source_target_pairs={{0,8},{4,12},{8,0},{12,4},{16,24},{20,28},{24,16},{28,20},{1,9},{5... | collective-permute-start | bytes 3145736 | tf_op jit(solution)/shard_map/ppermute | solution.py:286
  47.8 25.2 %collective-permute-start.9 = (bf16[2048,256]{1,0:T(8,128)(2,1)S(1)}, bf16[2048,256]{1,0:T(8,128)(2,1)S(1)}, u32[]{:S(2)}, u32[]{:S(2)}) collective-permute-start(bf16[2048,256]{1,0:T(8,128)(2,1)S(1)} %constant_dynamic-update-slice_fusion.refs_0_.refs_4_), channel_id=1, source_target_pairs={{0,16},{4,20},{8,24},{12,28},{16,0},{20,4},{24,8},{28,12},{1,17},{... | collective-permute-start | bytes 3145736 | tf_op jit(solution)/shard_map/ppermute | solution.py:286
  49.4 2.2 %copy-start.1 = (bf16[8192,256]{1,0:T(8,128)(2,1)S(1)}, bf16[8192,256]{1,0:T(8,128)(2,1)}, u32[]{:S(2)}) copy-start(bf16[8192,256]{1,0:T(8,128)(2,1)} %cached.11) | copy-start | bytes 12582916
  56.9 0.7 copy-start.5
  57.6 47.1 %copy-start.8 = (s32[1,256]{1,0:T(1,128)S(1)}, s32[1,256]{1,0:T(1,128)}, u32[]{:S(2)}) copy-start(s32[1,256]{1,0:T(1,128)} %param.15) | copy-start | bytes 3076
  73.0 13.8 %collective-permute-start.13 = (bf16[2048,256]{1,0:T(8,128)(2,1)S(1)}, bf16[2048,256]{1,0:T(8,128)(2,1)}, u32[]{:S(2)}, u32[]{:S(2)}) collective-permute-start(bf16[2048,256]{1,0:T(8,128)(2,1)S(1)} %collective-permute-done.8.refs_2_.refs_6_), channel_id=1, source_target_pairs={{0,4},{4,0},{8,12},{12,8},{16,20},{20,16},{24,28},{28,24},{1,5},{5... | collective-permute-start | bytes 3145736 | tf_op jit(solution)/shard_map/ppermute | solution.py:286
  73.0 13.8 %collective-permute-start.14 = (bf16[2048,256]{1,0:T(8,128)(2,1)S(1)}, bf16[2048,256]{1,0:T(8,128)(2,1)}, u32[]{:S(2)}, u32[]{:S(2)}) collective-permute-start(bf16[2048,256]{1,0:T(8,128)(2,1)S(1)} %collective-permute-done.9.refs_4_.refs_8_), channel_id=1, source_target_pairs={{0,4},{4,0},{8,12},{12,8},{16,20},{20,16},{24,28},{28,24},{1,5},{5... | collective-permute-start | bytes 3145736 | tf_op jit(solution)/shard_map/ppermute | solution.py:286
  75.8 28.3 %collective-permute-start.10 = (bf16[256,2048]{1,0:T(8,128)(2,1)}, bf16[256,2048]{1,0:T(8,128)(2,1)}, u32[]{:S(2)}, u32[]{:S(2)}) collective-permute-start(bf16[256,2048]{1,0:T(8,128)(2,1)} %broadcast_select_fusion.chunk), channel_id=1, source_target_pairs={{2,3},{1,0},{6,7},{5,4},{10,11},{9,8},{14,15},{13,12},{18,19},{17,... | collective-permute-start | bytes 3145736 | tf_op jit(solution)/shard_map/ppermute | solution.py:471
  78.9 14.1 %collective-permute-start.11 = (bf16[1024,256]{1,0:T(8,128)(2,1)}, bf16[1024,256]{1,0:T(8,128)(2,1)}, u32[]{:S(2)}, u32[]{:S(2)}) collective-permute-start(bf16[1024,256]{1,0:T(8,128)(2,1)} %slice.6), channel_id=1, source_target_pairs={{0,8},{4,12},{8,0},{12,4},{16,24},{20,28},{24,16},{28,20},{1,9},{5... | collective-permute-start | bytes 1572872 | tf_op jit(solution)/shard_map/ppermute | solution.py:286
  79.5 13.9 %collective-permute-start.12 = (bf16[1024,256]{1,0:T(8,128)(2,1)}, bf16[1024,256]{1,0:T(8,128)(2,1)}, u32[]{:S(2)}, u32[]{:S(2)}) collective-permute-start(bf16[1024,256]{1,0:T(8,128)(2,1)} %slice.7), channel_id=1, source_target_pairs={{0,16},{4,20},{8,24},{12,28},{16,0},{20,4},{24,8},{28,12},{1,17},{... | collective-permute-start | bytes 1572872 | tf_op jit(solution)/shard_map/ppermute | solution.py:286
  81.1 2.2 %copy-start.2 = (bf16[8192,256]{1,0:T(8,128)(2,1)S(1)}, bf16[8192,256]{1,0:T(8,128)(2,1)}, u32[]{:S(2)}) copy-start(bf16[8192,256]{1,0:T(8,128)(2,1)} %cached.11) | copy-start | bytes 12582916
  83.3 0.9 copy-start.6
  104.1 13.3 %collective-permute-start.15 = (bf16[1024,256]{1,0:T(8,128)(2,1)}, bf16[1024,256]{1,0:T(8,128)(2,1)}, u32[]{:S(2)}, u32[]{:S(2)}) collective-permute-start(bf16[1024,256]{1,0:T(8,128)(2,1)} %collective-permute-done.11.refs_0_), channel_id=1, source_target_pairs={{0,4},{4,0},{8,12},{12,8},{16,20},{20,16},{24,28},{28,24},{1,5},{5... | collective-permute-start | bytes 1572872 | tf_op jit(solution)/shard_map/ppermute | solution.py:286
  104.1 13.4 %collective-permute-start.16 = (bf16[1024,256]{1,0:T(8,128)(2,1)}, bf16[1024,256]{1,0:T(8,128)(2,1)}, u32[]{:S(2)}, u32[]{:S(2)}) collective-permute-start(bf16[1024,256]{1,0:T(8,128)(2,1)} %collective-permute-done.12.refs_10_), channel_id=1, source_target_pairs={{0,4},{4,0},{8,12},{12,8},{16,20},{20,16},{24,28},{28,24},{1,5},{5... | collective-permute-start | bytes 1572872 | tf_op jit(solution)/shard_map/ppermute | solution.py:286
  105.5 2.2 %copy-start.3 = (bf16[8192,256]{1,0:T(8,128)(2,1)S(1)}, bf16[8192,256]{1,0:T(8,128)(2,1)}, u32[]{:S(2)}) copy-start(bf16[8192,256]{1,0:T(8,128)(2,1)} %cached.11) | copy-start | bytes 12582916
  110.3 0.7 copy-start.7
  117.5 19.5 %copy-start.9 = (s32[2]{0:T(128)S(1)}, s32[2]{0:T(128)}, u32[]{:S(2)}) copy-start(s32[2]{0:T(128)} %constant.72.clone) | copy-start | bytes 28
  122.1 6.3 %collective-permute-start.17 = (bf16[4,1024,128]{2,1,0:T(8,128)(2,1)}, bf16[4,1024,128]{2,1,0:T(8,128)(2,1)}, u32[]{:S(2)}, u32[]{:S(2)}) collective-permute-start(bf16[4,1024,128]{2,1,0:T(8,128)(2,1)} %get-tuple-element.95), channel_id=1, source_target_pairs={{0,4},{4,0},{8,12},{12,8},{16,20},{20,16},{24,28},{28,24},{1,5},{5... | collective-permute-start | bytes 3145736 | tf_op jit(solution)/shard_map/ppermute | solution.py:286
  122.2 17.0 %collective-permute-start.23 = (bf16[4,1024,128]{2,1,0:T(8,128)(2,1)}, bf16[4,1024,128]{2,1,0:T(8,128)(2,1)}, u32[]{:S(2)}, u32[]{:S(2)}) collective-permute-start(bf16[4,1024,128]{2,1,0:T(8,128)(2,1)} %get-tuple-element.103), channel_id=1, source_target_pairs={{0,4},{4,0},{8,12},{12,8},{16,20},{20,16},{24,28},{28,24},{1,5},{5... | collective-permute-start | bytes 3145736 | tf_op jit(solution)/shard_map/ppermute | solution.py:286
  122.7 5.7 %collective-permute-start.18 = (bf16[256,256]{1,0:T(8,128)(2,1)}, bf16[256,256]{1,0:T(8,128)(2,1)S(1)}, u32[]{:S(2)}, u32[]{:S(2)}) collective-permute-start(bf16[256,256]{1,0:T(8,128)(2,1)} %get-tuple-element.110.d_projected.refs_0_), channel_id=1, source_target_pairs={{0,1},{1,0},{2,3},{3,2},{4,5},{5,4},{6,7},{7,6},{8,9},{9,8},{10,11... | collective-permute-start | bytes 393224 | tf_op jit(solution)/shard_map/ppermute | solution.py:438
  131.9 16.1 %collective-permute-start.19 = (bf16[2,1024,128]{2,1,0:T(8,128)(2,1)S(1)}, bf16[2,1024,128]{2,1,0:T(8,128)(2,1)S(1)}, u32[]{:S(2)}, u32[]{:S(2)}) collective-permute-start(bf16[2,1024,128]{2,1,0:T(8,128)(2,1)S(1)} %get-tuple-element.97), channel_id=1, source_target_pairs={{0,8},{4,12},{8,0},{12,4},{16,24},{20,28},{24,16},{28,20},{1,9},{5... | collective-permute-start | bytes 1572872 | tf_op jit(solution)/shard_map/ppermute | solution.py:286
  132.5 15.5 %collective-permute-start.20 = (bf16[2,1024,128]{2,1,0:T(8,128)(2,1)S(1)}, bf16[2,1024,128]{2,1,0:T(8,128)(2,1)S(1)}, u32[]{:S(2)}, u32[]{:S(2)}) collective-permute-start(bf16[2,1024,128]{2,1,0:T(8,128)(2,1)S(1)} %get-tuple-element.98), channel_id=1, source_target_pairs={{0,16},{4,20},{8,24},{12,28},{16,0},{20,4},{24,8},{28,12},{1,17},{... | collective-permute-start | bytes 1572872 | tf_op jit(solution)/shard_map/ppermute | solution.py:286
  134.1 12.2 %collective-permute-start.21 = (bf16[256,256]{1,0:T(8,128)(2,1)}, bf16[256,256]{1,0:T(8,128)(2,1)S(1)}, u32[]{:S(2)}, u32[]{:S(2)}) collective-permute-start(bf16[256,256]{1,0:T(8,128)(2,1)} %get-tuple-element.110.d_projected.refs_0_), channel_id=1, source_target_pairs={{0,2},{1,3},{2,0},{3,1},{4,6},{5,7},{6,4},{7,5},{8,10},{9,11},{10,... | collective-permute-start | bytes 393224 | tf_op jit(solution)/shard_map/ppermute | solution.py:438
  136.7 11.3 %collective-permute-start.22 = (bf16[256,256]{1,0:T(8,128)(2,1)S(1)}, bf16[256,256]{1,0:T(8,128)(2,1)S(1)}, u32[]{:S(2)}, u32[]{:S(2)}) collective-permute-start(bf16[256,256]{1,0:T(8,128)(2,1)S(1)} %collective-permute-done.18.refs_1_), channel_id=1, source_target_pairs={{0,2},{1,3},{2,0},{3,1},{4,6},{5,7},{6,4},{7,5},{8,10},{9,11},{10,... | collective-permute-start | bytes 393224 | tf_op jit(solution)/shard_map/ppermute | solution.py:438
  148.1 7.4 %collective-permute-start.24 = (bf16[1024,128]{1,0:T(8,128)(2,1)S(1)}, bf16[1024,128]{1,0:T(8,128)(2,1)S(1)}, u32[]{:S(2)}, u32[]{:S(2)}) collective-permute-start(bf16[1024,128]{1,0:T(8,128)(2,1)S(1)} %get-tuple-element.108), channel_id=1, source_target_pairs={{0,16},{4,20},{8,24},{12,28},{16,0},{20,4},{24,8},{28,12},{1,17},{... | collective-permute-start | bytes 786440 | tf_op jit(solution)/shard_map/ppermute | solution.py:286
  148.7 7.0 %collective-permute-start.25 = (bf16[1024,128]{1,0:T(8,128)(2,1)S(1)}, bf16[1024,128]{1,0:T(8,128)(2,1)S(1)}, u32[]{:S(2)}, u32[]{:S(2)}) collective-permute-start(bf16[1024,128]{1,0:T(8,128)(2,1)S(1)} %get-tuple-element.109), channel_id=1, source_target_pairs={{0,8},{4,12},{8,0},{12,4},{16,24},{20,28},{24,16},{28,20},{1,9},{5... | collective-permute-start | bytes 786440 | tf_op jit(solution)/shard_map/ppermute | solution.py:286

commit v8 on v7

--- a/solution.py
+++ b/solution.py
@@ -81,63 +81,110 @@
     )(place, *arrays)
 
 
-def absorb_kernel(place, chunk, total, cached, *refs):
-    *_, total_out, held, rows, turned, sems = refs
+def fetch_chunk(place, chunks, chunk, sem):
+    for n, source in enumerate(chunks):
+
+        @pl.when(place[2] == n)
+        def _():
+            pltpu.make_async_copy(source, chunk, sem).start()
+
+    return pltpu.make_async_copy(chunks[0], chunk, sem)
+
+
+def fetch_rows(place, cached, rows, sem):
     height = rows.shape[0]
     start = pl.multiple_of(place[0] * height, height)
-    fetch = pltpu.make_async_copy(cached.at[pl.ds(start, height), :], rows, sems.at[0])
-    fetch.start()
+    copy = pltpu.make_async_copy(cached.at[pl.ds(start, height), :], rows, sem)
+    copy.start()
+    return copy
+
+
+def absorb_kernel(n_chunks, place, *refs):
+    chunks, (total, cached) = refs[:n_chunks], refs[n_chunks : n_chunks + 2]
+    total_out, held, chunk, rows, turned, sems = refs[-6:]
+    chunk_copy = fetch_chunk(place, chunks, chunk, sems.at[0])
+    rows_copy = fetch_rows(place, cached, rows, sems.at[1])
+    chunk_copy.wait()
     turned[...] = chunk[...].T
-    keep = pltpu.make_async_copy(turned, held.at[place[1]], sems.at[1])
+    keep = pltpu.make_async_copy(turned, held.at[place[1]], sems.at[2])
     keep.start()
-    fetch.wait()
+    rows_copy.wait()
     total_out[...] = total[...] + jnp.dot(
         chunk[...], rows[...], preferred_element_type=jnp.float32
     )
     keep.wait()
 
 
-def absorb(chunk, index, cached, total, held, n_chunks):
+def absorb_place(index, which, n_chunks):
+    inside = (index >= 0) & (index < n_chunks)
+    return jnp.stack(
+        [jnp.clip(index, 0, n_chunks - 1), jnp.where(inside, index, n_chunks), which]
+    ).astype(jnp.int32)
+
+
+def absorb_scratch(chunk, cached, n_sems):
     length, feats = chunk.shape
+    return [
+        pltpu.VMEM((length, feats), chunk.dtype),
+        pltpu.VMEM((feats, cached.shape[1]), cached.dtype),
+        pltpu.VMEM((feats, length), chunk.dtype),
+        pltpu.SemaphoreType.DMA((n_sems,)),
+    ]
+
+
+def absorb(chunks, which, index, cached, total, held, n_chunks):
+    length, feats = chunks[0].shape
     cols = cached.shape[1]
-    inside = (index >= 0) & (index < n_chunks)
-    place = jnp.stack([jnp.clip(index, 0, n_chunks - 1), jnp.where(inside, index, n_chunks)])
-    shape = jax.ShapeDtypeStruct((8 * n_chunks, feats, length), chunk.dtype)
+    shape = jax.ShapeDtypeStruct((8 * n_chunks, feats, length), chunks[0].dtype)
     vmem, anywhere = pl.BlockSpec(memory_space=pltpu.VMEM), pl.BlockSpec(memory_space=pl.ANY)
     return pl.pallas_call(
-        absorb_kernel,
-        in_specs=[pl.BlockSpec(memory_space=pltpu.SMEM), vmem, vmem, anywhere]
+        functools.partial(absorb_kernel, len(chunks)),
+        in_specs=[pl.BlockSpec(memory_space=pltpu.SMEM)]
+        + [anywhere] * len(chunks)
+        + [vmem, anywhere]
         + ([] if held is None else [anywhere]),
         out_specs=[vmem, anywhere],
         out_shape=[jax.ShapeDtypeStruct(total.shape, jnp.float32), shape],
-        scratch_shapes=[
-            pltpu.VMEM((feats, cols), cached.dtype),
-            pltpu.VMEM((feats, length), chunk.dtype),
-            pltpu.SemaphoreType.DMA((2,)),
-        ],
-        input_output_aliases={} if held is None else {4: 1},
+        scratch_shapes=absorb_scratch(chunks[0], cached, 3),
+        input_output_aliases={} if held is None else {3 + len(chunks): 1},
         cost_estimate=pl.CostEstimate(
             flops=2 * length * feats * cols,
             bytes_accessed=4 * length * feats + 2 * feats * cols,
             transcendentals=0,
         ),
-        compiler_params=pltpu.CompilerParams(vmem_limit_bytes=VMEM_WHOLE),
+        compiler_params=pltpu.CompilerParams(vmem_limit_bytes=VMEM_STREAM),
         name="absorb",
-    )(place, chunk, total, cached, *([] if held is None else [held]))
-
-
-def attention_kernel(n_totals, *refs):
-    totals, (allowed, queries_in, d_out_in) = refs[:n_totals], refs[n_totals : n_totals + 3]
-    d_queries, d_projected, queries, d_out, sems = refs[n_totals + 3 :]
-    copies = [
-        pltpu.make_async_copy(queries_in, queries, sems.at[0]),
-        pltpu.make_async_copy(d_out_in, d_out, sems.at[1]),
+    )(
+        absorb_place(index, which, n_chunks),
+        *chunks,
+        total,
+        cached,
+        *([] if held is None else [held]),
+    )
+
+
+def attend_kernel(n_chunks, place, *refs):
+    chunks, refs = refs[:n_chunks], refs[n_chunks:]
+    total, cached, _, allowed, queries_in, d_out_in = refs[:6]
+    held, d_queries, d_projected, chunk, rows, turned, sems, queries, d_out = refs[6:]
+    chunk_copy = fetch_chunk(place, chunks, chunk, sems.at[0])
+    rows_copy = fetch_rows(place, cached, rows, sems.at[1])
+    others = [
+        pltpu.make_async_copy(queries_in, queries, sems.at[3]),
+        pltpu.make_async_copy(d_out_in, d_out, sems.at[4]),
     ]
-    for copy in copies:
+    for copy in others:
         copy.start()
-    projected = jnp.concatenate([total[...].astype(jnp.bfloat16) for total in totals], axis=0)
+    chunk_copy.wait()
+    turned[...] = chunk[...].T
+    keep = pltpu.make_async_copy(turned, held.at[place[1]], sems.at[2])
+    keep.start()
+    rows_copy.wait()
+    projected = (
+        total[...] + jnp.dot(chunk[...], rows[...], preferred_element_type=jnp.float32)
+    ).astype(jnp.bfloat16)
     kept = allowed[...] > 0
-    for copy in copies:
+    for copy in others:
         copy.wait()
     factor = 1.0 / math.sqrt(HD)
     across = (((1,), (1,)), ((), ()))
@@ -169,32 +216,42 @@
             d_values = d_values + jnp.dot(probs_low, grad, preferred_element_type=jnp.float32)
         d_projected[:, start : start + HD] = d_keys.astype(jnp.bfloat16)
         d_projected[:, start + HD : start + 2 * HD] = d_values.astype(jnp.bfloat16)
-
-
-def attention_backward(totals, queries, d_out, allowed):
-    length, cols = queries.shape[0], totals[0].shape[1]
+    keep.wait()
+
+
+def attend(chunks, which, index, cached, total, held, queries, d_out, allowed, n_chunks):
     vmem, anywhere = pl.BlockSpec(memory_space=pltpu.VMEM), pl.BlockSpec(memory_space=pl.ANY)
     return pl.pallas_call(
-        functools.partial(attention_kernel, len(totals)),
-        in_specs=[vmem] * (len(totals) + 1) + [anywhere] * 2,
-        out_specs=[vmem] * 2,
+        functools.partial(attend_kernel, len(chunks)),
+        in_specs=[pl.BlockSpec(memory_space=pltpu.SMEM)]
+        + [anywhere] * len(chunks)
+        + [vmem, anywhere, anywhere, vmem, anywhere, anywhere],
+        out_specs=[anywhere, vmem, vmem],
         out_shape=[
+            jax.ShapeDtypeStruct(held.shape, held.dtype),
             jax.ShapeDtypeStruct(queries.shape, jnp.bfloat16),
-            jax.ShapeDtypeStruct((length, cols), jnp.bfloat16),
+            jax.ShapeDtypeStruct(total.shape, jnp.bfloat16),
         ],
-        scratch_shapes=[
-            pltpu.VMEM(queries.shape, queries.dtype),
-            pltpu.VMEM(d_out.shape, d_out.dtype),
-            pltpu.SemaphoreType.DMA((2,)),
-        ],
+        scratch_shapes=absorb_scratch(chunks[0], cached, 5)
+        + [pltpu.VMEM(queries.shape, queries.dtype), pltpu.VMEM(d_out.shape, d_out.dtype)],
+        input_output_aliases={3 + len(chunks): 0},
         cost_estimate=pl.CostEstimate(
             flops=12 * allowed.size * queries.shape[1],
             bytes_accessed=8 * queries.size,
             transcendentals=allowed.size * queries.shape[1] // HD,
         ),
         compiler_params=pltpu.CompilerParams(vmem_limit_bytes=VMEM_STREAM),
-        name="attention",
-    )(*totals, allowed, queries, d_out)
+        name="attend",
+    )(
+        absorb_place(index, which, n_chunks),
+        *chunks,
+        total,
+        cached,
+        held,
+        allowed,
+        queries,
+        d_out,
+    )
 
 
 SENT = ((0, 0, 0), (0, 1, 0), (1, 0, 1), (2, 1, 1))
@@ -208,6 +265,7 @@
     added, outs = refs[:-n_out], refs[-n_out:]
     rows = buffer.shape[1]
     half = d_projected.shape[1] // 2
+    block = min(rows, 256)
     start = pl.multiple_of(place[4] * rows, rows)
     chunks = sorted({chunk for group in groups for chunk, _, _ in group})
     copies = {}
@@ -225,19 +283,21 @@
             if which == chunk
         ]
         first, last = min(w[1] for w in wanted), max(w[1] for w in wanted)
-        total = jnp.dot(
-            buffer[chunk],
-            d_projected[:, first * half : (last + 1) * half],
-            preferred_element_type=jnp.float32,
-        )
-        for g, side, position in wanted:
-            part = total[:, (side - first) * half : (side - first + 1) * half]
-            if added:
-                part = part + added[0][2 * side + position].astype(jnp.float32)
-            if joined:
-                outs[g][2 * side + position] = part.astype(outs[g].dtype)
-            else:
-                outs[side][position] = part.astype(outs[side].dtype)
+        for r in range(0, rows, block):
+            here = slice(r, r + block)
+            total = jnp.dot(
+                buffer[chunk, here, :],
+                d_projected[:, first * half : (last + 1) * half],
+                preferred_element_type=jnp.float32,
+            )
+            for g, side, position in wanted:
+                part = total[:, (side - first) * half : (side - first + 1) * half]
+                if added:
+                    part = part + added[0][2 * side + position, here, :].astype(jnp.float32)
+                if joined:
+                    outs[g][2 * side + position, here, :] = part.astype(outs[g].dtype)
+                else:
+                    outs[side][position, here, :] = part.astype(outs[side].dtype)
 
 
 def weight_parts(held, d_projected, place, groups, added, dtype, name):
@@ -300,11 +360,11 @@
 
     sent, kept = parts(1 - core, (SENT, KEPT), [], jnp.bfloat16, "weight_other")
     sent, kept = swap(sent, 1), swap(kept, 1)
-    sent, pieces[1] = lax.optimization_barrier((sent, pieces[1]))
+    sent, beside = lax.optimization_barrier((sent, beside))
     send_a, send_b = parts(core, (SENT,), [sent], jnp.bfloat16, "weight_send")
     got_a, got_b = swap(send_a, 2), swap(send_b, 4)
     keep_a, keep_b = parts(core, (KEPT,), [kept], jnp.float32, "weight_keep")
-    got_a, got_b, pieces, beside = lax.optimization_barrier((got_a, got_b, pieces, beside))
+    got_a, got_b, pieces = lax.optimization_barrier((got_a, got_b, pieces))
 
     small = jax.ShapeDtypeStruct((rows, cols // 2), jnp.bfloat16)
     arrays = [keep_a, got_a, keep_b, got_b]
@@ -454,62 +514,52 @@
 
         blocks = [block_for(me_z)] + [pair(block_for(me_z ^ s), s) for s in range(1, n_z)]
 
+        doc_ids = segments[0]
+        position = jnp.arange(length)
+        allowed = (doc_ids[:, None] == doc_ids[None, :]) & (position[:, None] <= position[None, :])
+        allowed = allowed.astype(jnp.float32)
+
         total = jnp.zeros((length, cols), jnp.float32)
-        total, held = absorb(tokens, me_z, cached, total, None, n_z)
+        zero = 0 * me_z
+        total, held = absorb([tokens], zero, me_z, cached, total, None, n_z)
         if tuned:
             gather = PlaneGather(jnp.concatenate([own_cache] + blocks, axis=0))
-        from_low, from_high, merged = tokens, tokens, None
+        from_low, from_high = tokens, tokens
         for s in range(1, n_z):
-            up = [(z, z + 1) for z in range(s - 1, n_z - 1)]
-            down = [(z + 1, z) for z in range(n_z - s)]
             low, high = me_z - s, me_z + s
-            if merged is None:
-                from_low = lax.ppermute(from_low, "tensor", up)
-                from_high = lax.ppermute(from_high, "tensor", down)
-                arrived = from_low, from_high
-            else:
-                merged = lax.ppermute(merged, "tensor", up + down)
-                arrived = merged
+            from_low = lax.ppermute(
+                from_low, "tensor", [(z, z + 1) for z in range(s - 1, n_z - 1)]
+            )
+            from_high = lax.ppermute(from_high, "tensor", [(z + 1, z) for z in range(n_z - s)])
             if tuned:
                 if s == 1:
-                    rounds = gather.got
+                    rounds, allowed = lax.optimization_barrier((gather.got, allowed))
                 elif s == 2:
                     rounds = gather.first()
-                elif s == 3:
+                else:
                     rounds = gather.second()
                     laid = gather.lay(own_cache.shape[0], cached.shape[0])
                     rounds = (rounds, laid)
-                arrived, held, rounds = lax.optimization_barrier((arrived, held, rounds))
+                from_low, from_high, held, rounds = lax.optimization_barrier(
+                    (from_low, from_high, held, rounds)
+                )
                 if s < 3:
                     gather.got = rounds
                 else:
                     (gather.far, gather.got[3], gather.got[5]), laid = rounds
-            if merged is None:
-                from_low, from_high = arrived
-            else:
-                merged = arrived
-            if merged is None and 2 * s >= n_z:
-                merged = jnp.where(me_z >= s, from_low, from_high)
-            if merged is None:
-                total, held = absorb(from_low, low, cached, total, held, n_z)
-                total, held = absorb(from_high, high, cached, total, held, n_z)
-            else:
-                total, held = absorb(
-                    merged, jnp.where(me_z >= s, low, high), cached, total, held, n_z
-                )
-
-        doc_ids = segments[0]
-        position = jnp.arange(length)
-        allowed = (doc_ids[:, None] == doc_ids[None, :]) & (position[:, None] <= position[None, :])
-        allowed = allowed.astype(jnp.float32)
-
-        d_queries, d_projected = attention_backward([total], queries, d_out, allowed)
-
-        pieces = [d_projected]
-        s = 1
-        while s < n_z:
-            pieces = pieces + [pair(piece, s) for piece in pieces]
-            s *= 2
+            chunks, which = [from_low, from_high], (me_z < s).astype(jnp.int32)
+            index = jnp.where(me_z < s, high, low)
+            if 2 * s < n_z:
+                total, held = absorb([from_low], zero, low, cached, total, held, n_z)
+                chunks, which, index = [from_high], zero, high
+            if s < n_z - 1:
+                total, held = absorb(chunks, which, index, cached, total, held, n_z)
+
+        held, d_queries, d_projected = attend(
+            chunks, which, index, cached, total, held, queries, d_out, allowed, n_z
+        )
+
+        pieces = [d_projected] + [pair(d_projected, s) for s in range(1, n_z)]
         if tuned:
             d_projected, gather.far_other = lax.optimization_barrier((d_projected, gather.third()))
             pieces[0] = d_projected

time: 158 us -> 148 us (0.937)
  local copies, waits for them, and re-layouts: 16.4 us -> 7.89 us
  waiting for transfers between devices: 58.3 us -> 49.8 us
  Pallas kernels: 47.1 us -> 50.8 us
  starting transfers between devices: 30.8 us -> 34.2 us
    unnamed x23 -> x15, local copies, waits for them, and re-layouts: 13.4 us -> 4.2 us
    ppermute x6, waiting for transfers between devices: 28.2 us -> 20.9 us  [pair(): return lax.ppermute(value, 'tensor', [(z, z ^ s) for z in range(n_z)])]
    pallas_call x6 -> x5, Pallas kernels: 18.9 us -> 24.7 us  [the longest x4 16.9 us: absorb(): pl.pallas_call(functools.partial(absorb_kernel, len(chunks)), in_specs=[p...]
    select_n x1 -> x0, other arithmetic: 2.31 us -> none  [body(): merged = jnp.where(me_z >= s, from_low, from_high)]
    ppermute x5 -> x6, waiting for transfers between devices: 24.5 us -> 22.7 us  [the longest x3 22.6 us: body(): lax.ppermute(from_high, 'tensor', [(z + 1, z) for z in range(n_z - s)])]
    ppermute x5 -> x6, starting transfers between devices: 11.6 us -> 13.2 us  [the longest x3 9.2 us: body(): lax.ppermute(from_low, 'tensor', [(z, z + 1) for z in range(s - 1, n_z -...]
    another operation x3, other arithmetic: 0.23 us -> 1.85 us  [absorb_place(): jnp.stack([jnp.clip(index, 0, n_chunks - 1), jnp.where(inside, index, n_c...]
  transfers between devices with their start and end apart: 26 -> 27, of which waited for: 13 -> 12; matrix products, arithmetic and copies ran while one was open for 5% -> 6% of each run, Pallas kernels for 26% -> 31%
where the time goes in v8:
time: 148 us; the launch traced here: 147 us
  Pallas kernels  50.8 us (34%)
  waiting for transfers between devices  49.8 us (34%)
  starting transfers between devices  34.2 us (23%)
  local copies, waits for them, and re-layouts  7.89 us (5%)
  other arithmetic  3.41 us (2%)
    ppermute x3, waiting for transfers between devices, body(): lax.ppermute(from_high, 'tensor', [(z + 1, z) for z in range(n_z - s)])  22.6 us
    ppermute x6, waiting for transfers between devices, pair(): return lax.ppermute(value, 'tensor', [(z, z ^ s) for z in range(n_z)])  20.9 us
    pallas_call x4, Pallas kernels, absorb(): pl.pallas_call(functools.partial(absorb_kernel, len(chunks)), in_specs=[p...  16.9 us
    ppermute x15, starting transfers between devices, swap(): return lax.ppermute(value, 'dp', [(i, i ^ bit) for i in range(8)])  11.3 us
    pallas_call x3, Pallas kernels, weight_parts(): pl.pallas_call(functools.partial(weight_kernel, groups), in_specs=[pl.Blo...  10.3 us
    ppermute x6, starting transfers between devices, pair(): return lax.ppermute(value, 'tensor', [(z, z ^ s) for z in range(n_z)])  9.67 us
    ppermute x3, starting transfers between devices, body(): lax.ppermute(from_low, 'tensor', [(z, z + 1) for z in range(s - 1, n_z -...  9.2 us
    pallas_call x1, Pallas kernels, attend(): pl.pallas_call(functools.partial(attend_kernel, len(chunks)), in_specs=[p...  7.78 us
  transfers between devices with their start and end apart: 27, of which 12 were waited for; matrix products, arithmetic and copies ran while one was open for 6% of the time, Pallas kernels for 31%

profile of v8, /device:TPU:0, one launch (start us, length us, event | category | flops | bytes accessed | tf_op | source)
XLA Modules:
  0.0 146.9 jit_solution(17599385171315831743)
XLA Ops:
  0.6 5.9 %collective-permute-start = (bf16[256,2048]{1,0:T(8,128)(2,1)}, bf16[256,2048]{1,0:T(8,128)(2,1)}, u32[]{:S(2)}, u32[]{:S(2)}) collective-permute-start(bf16[256,2048]{1,0:T(8,128)(2,1)} %refs_0_.1), channel_id=1, source_target_pairs={{0,1},{1,2},{2,3},{4,5},{5,6},{6,7},{8,9},{9,10},{10,11},{12,13},{... | collective-permute-start | bytes 3145736 | tf_op jit(solution)/shard_map/ppermute | solution.py:530
  6.5 1.3 collective-permute-start.1
  7.9 4.9 %optimizer.1 = (f32[1024,256]{1,0:T(8,128)}, f32[1024,256]{1,0:T(8,128)}, f32[1024,256]{1,0:T(8,128)}, bf16[1024,256]{1,0:T(8,128)(2,1)}) custom-call(s32[1]{0:T(128)} %bitcast.place, bf16[8192,256]{1,0:T(8,128)(2,1)} %refs_3_.3, f32[1024,256]{1,0:T(8,128)} %master.1, f32[1024,256]{1,0:T(8,128)} %moment.1, f32[1024,256]{1,0:T(8,128)} %second.1, f32[1024,256]{1,0:T(8,128)} %grad.1), custom_call_target="tpu_custom_call" | custom-call | flops 10485760 | bytes 8388608 | tf_op jit(solution)/shard_map/optimizer/pallas_call | solution.py:51
  12.8 1.1 constant_dynamic-update-slice_fusion.3
  13.9 1.1 constant_dynamic-slice_fusion
  15.0 2.7 %collective-permute-start.2 = (bf16[256,256]{1,0:T(8,128)(2,1)S(1)}, bf16[256,256]{1,0:T(8,128)(2,1)S(1)}, u32[]{:S(2)}, u32[]{:S(2)}) collective-permute-start(bf16[256,256]{1,0:T(8,128)(2,1)S(1)} %get-tuple-element.125), channel_id=1, source_target_pairs={{0,1},{1,0},{2,3},{3,2},{4,5},{5,4},{6,7},{7,6},{8,9},{9,8},{10,11... | collective-permute-start | bytes 393224 | tf_op jit(solution)/shard_map/ppermute | solution.py:498
  17.7 2.6 %collective-permute-start.3 = (bf16[256,256]{1,0:T(8,128)(2,1)S(1)}, bf16[256,256]{1,0:T(8,128)(2,1)S(1)}, u32[]{:S(2)}, u32[]{:S(2)}) collective-permute-start(bf16[256,256]{1,0:T(8,128)(2,1)S(1)} %get-tuple-element.124), channel_id=1, source_target_pairs={{0,2},{1,3},{2,0},{3,1},{4,6},{5,7},{6,4},{7,5},{8,10},{9,11},{10,... | collective-permute-start | bytes 393224 | tf_op jit(solution)/shard_map/ppermute | solution.py:498
  20.3 1.6 %fusion.1.refs_5_ = f32[256,256]{1,0:T(8,128)} fusion(s32[256]{0:T(256)} %bitcast.20), kind=kLoop, calls=%fused_computation.2 | loop fusion | flops 262144 | bytes 263168 | tf_op jit(solution)/shard_map/convert_element_type | solution.py:520
  22.5 0.7 broadcast_in_dim.2.refs_1_
  23.2 4.2 %absorb.4 = (f32[256,256]{1,0:T(8,128)}, bf16[32,2048,256]{2,1,0:T(8,128)(2,1)}) custom-call(s32[3]{0:T(128)} %get-tuple-element.129.place, bf16[256,2048]{1,0:T(8,128)(2,1)} %refs_0_.1, f32[256,256]{1,0:T(8,128)} %broadcast_in_dim.2.refs_1_, bf16[8192,256]{1,0:T(8,128)(2,1)} %refs_3_.3), custom_call_target="tpu_custom_call" | custom-call | flops 268435456 | bytes 3145728 | tf_op jit(solution)/shard_map/absorb/pallas_call | solution.py:140
  27.5 11.4 %collective-permute-done.2 = bf16[256,256]{1,0:T(8,128)(2,1)S(1)} collective-permute-done((bf16[256,256]{1,0:T(8,128)(2,1)S(1)}, bf16[256,256]{1,0:T(8,128)(2,1)S(1)}, u32[]{:S(2)}, u32[]{:S(2)}) %collective-permute-start.2) | collective-permute-done | bytes 131104 | tf_op jit(solution)/shard_map/ppermute | solution.py:498
  38.8 4.3 %collective-permute-done.3 = bf16[256,256]{1,0:T(8,128)(2,1)S(1)} collective-permute-done((bf16[256,256]{1,0:T(8,128)(2,1)S(1)}, bf16[256,256]{1,0:T(8,128)(2,1)S(1)}, u32[]{:S(2)}, u32[]{:S(2)}) %collective-permute-start.3) | collective-permute-done | bytes 131104 | tf_op jit(solution)/shard_map/ppermute | solution.py:498
  43.2 1.6 %collective-permute-start.5 = (bf16[256,2048]{1,0:T(8,128)(2,1)}, bf16[256,2048]{1,0:T(8,128)(2,1)}, u32[]{:S(2)}, u32[]{:S(2)}) collective-permute-start(bf16[256,2048]{1,0:T(8,128)(2,1)} %collective-permute-done.refs_0_), channel_id=1, source_target_pairs={{1,2},{2,3},{5,6},{6,7},{9,10},{10,11},{13,14},{14,15},{17,18},{18... | collective-permute-start | bytes 3145736 | tf_op jit(solution)/shard_map/ppermute | solution.py:530
  44.8 1.3 collective-permute-start.6
  46.2 1.6 %collective-permute-start.8 = (bf16[2048,256]{1,0:T(8,128)(2,1)S(1)}, bf16[2048,256]{1,0:T(8,128)(2,1)S(1)}, u32[]{:S(2)}, u32[]{:S(2)}) collective-permute-start(bf16[2048,256]{1,0:T(8,128)(2,1)S(1)} %constant_dynamic-update-slice_fusion.refs_0_.refs_4_), channel_id=1, source_target_pairs={{0,8},{4,12},{8,0},{12,4},{16,24},{20,28},{24,16},{28,20},{1,9},{5... | collective-permute-start | bytes 3145736 | tf_op jit(solution)/shard_map/ppermute | solution.py:346
  47.8 1.5 %collective-permute-start.9 = (bf16[2048,256]{1,0:T(8,128)(2,1)S(1)}, bf16[2048,256]{1,0:T(8,128)(2,1)S(1)}, u32[]{:S(2)}, u32[]{:S(2)}) collective-permute-start(bf16[2048,256]{1,0:T(8,128)(2,1)S(1)} %constant_dynamic-update-slice_fusion.refs_0_.refs_4_), channel_id=1, source_target_pairs={{0,16},{4,20},{8,24},{12,28},{16,0},{20,4},{24,8},{28,12},{1,17},{... | collective-permute-start | bytes 3145736 | tf_op jit(solution)/shard_map/ppermute | solution.py:346
  49.3 0.6 pad_add_fusion
  49.9 4.2 %absorb.5 = (f32[256,256]{1,0:T(8,128)}, bf16[32,2048,256]{2,1,0:T(8,128)(2,1)}) custom-call(s32[3]{0:T(128)} %get-tuple-element.127.place, bf16[256,2048]{1,0:T(8,128)(2,1)} %collective-permute-done.refs_0_, f32[256,256]{1,0:T(8,128)} %get-tuple-element.73.refs_1_, bf16[8192,256]{1,0:T(8,128)(2,1)} %refs_3_.3, ...), custom_call_target="tpu_custom_call", output_to_operand_aliasing={{1}: (4, {})} | custom-call | flops 268435456 | bytes 3145728 | tf_op jit(solution)/shard_map/absorb/pallas_call | solution.py:140
  54.2 4.2 %absorb.6 = (f32[256,256]{1,0:T(8,128)}, bf16[32,2048,256]{2,1,0:T(8,128)(2,1)}) custom-call(s32[3]{0:T(128)} %get-tuple-element.128.place, bf16[256,2048]{1,0:T(8,128)(2,1)} %collective-permute-done.1.refs_0_, f32[256,256]{1,0:T(8,128)} %get-tuple-element.75.refs_1_, bf16[8192,256]{1,0:T(8,128)(2,1)} %refs_3_.3, ...), custom_call_target="tpu_custom_call", output_to_operand_aliasing={{1}: (4, {})} | custom-call | flops 268435456 | bytes 3145728 | tf_op jit(solution)/shard_map/absorb/pallas_call | solution.py:140
  58.4 12.9 %collective-permute-done.6.refs_1_ = bf16[256,2048]{1,0:T(8,128)(2,1)} collective-permute-done((bf16[256,2048]{1,0:T(8,128)(2,1)}, bf16[256,2048]{1,0:T(8,128)(2,1)}, u32[]{:S(2)}, u32[]{:S(2)}) %collective-permute-start.6) | collective-permute-done | bytes 1048608 | tf_op jit(solution)/shard_map/ppermute | solution.py:533
  71.8 1.2 collective-permute-done.9.refs_4_.refs_8_
  73.5 1.7 %collective-permute-start.10 = (bf16[256,2048]{1,0:T(8,128)(2,1)}, bf16[256,2048]{1,0:T(8,128)(2,1)}, u32[]{:S(2)}, u32[]{:S(2)}) collective-permute-start(bf16[256,2048]{1,0:T(8,128)(2,1)} %collective-permute-done.5.refs_0_), channel_id=1, source_target_pairs={{2,3},{6,7},{10,11},{14,15},{18,19},{22,23},{26,27},{30,31}} | collective-permute-start | bytes 3145736 | tf_op jit(solution)/shard_map/ppermute | solution.py:530
  75.2 1.5 collective-permute-start.11
  76.6 0.8 slice.6
  77.5 0.8 slice.7
  78.8 1.0 copy-done
  79.8 1.5 %collective-permute-start.13 = (bf16[1024,256]{1,0:T(8,128)(2,1)}, bf16[1024,256]{1,0:T(8,128)(2,1)}, u32[]{:S(2)}, u32[]{:S(2)}) collective-permute-start(bf16[1024,256]{1,0:T(8,128)(2,1)} %slice.7), channel_id=1, source_target_pairs={{0,16},{4,20},{8,24},{12,28},{16,0},{20,4},{24,8},{28,12},{1,17},{... | collective-permute-start | bytes 1572872 | tf_op jit(solution)/shard_map/ppermute | solution.py:346
  81.9 4.2 %absorb.7 = (f32[256,256]{1,0:T(8,128)}, bf16[32,2048,256]{2,1,0:T(8,128)(2,1)}) custom-call(s32[3]{0:T(128)} %pad_add_fusion.4.place, bf16[256,2048]{1,0:T(8,128)(2,1)} %collective-permute-done.5.refs_0_, bf16[256,2048]{1,0:T(8,128)(2,1)} %collective-permute-done.6.refs_1_, f32[256,256]{1,0:T(8,128)} %get-tuple-element.81.refs_2_, ...), custom_call_target="tpu_custom_call", output_to_operand_aliasing={{1}: (5, {})} | custom-call | flops 268435456 | bytes 3145728 | tf_op jit(solution)/shard_map/absorb/pallas_call | solution.py:140
  86.2 1.2 copy-done.1
  87.4 3.3 %place_rows.2.refs_2_ = bf16[8192,256]{1,0:T(8,128)(2,1)} custom-call(s32[6]{0:T(128)S(1)} %iota_xor_fusion.1.place, bf16[2048,256]{1,0:T(8,128)(2,1)S(1)} %constant_dynamic-update-slice_fusion.refs_0_.refs_4_, bf16[2048,256]{1,0:T(8,128)(2,1)} %collective-permute-done.7.refs_1_.refs_5_, bf16[2048,256]{1,0:T(8,128)(2,1)S(1)} %collective-permute-done.8.refs_2_.refs_6_, ...), custom_call_target="tpu_custom_call" | custom-call | bytes 6291456 | tf_op jit(solution)/shard_map/place_rows/pallas_call | solution.py:446
  90.7 1.8 %collective-permute-done.12.refs_0_ = bf16[1024,256]{1,0:T(8,128)(2,1)} collective-permute-done((bf16[1024,256]{1,0:T(8,128)(2,1)}, bf16[1024,256]{1,0:T(8,128)(2,1)}, u32[]{:S(2)}, u32[]{:S(2)}) %collective-permute-start.12) | collective-permute-done | bytes 524320 | tf_op jit(solution)/shard_map/ppermute | solution.py:346
  92.4 1.2 collective-permute-done.13.refs_10_
  93.7 9.8 %collective-permute-done.11.refs_1_ = bf16[256,2048]{1,0:T(8,128)(2,1)} collective-permute-done((bf16[256,2048]{1,0:T(8,128)(2,1)}, bf16[256,2048]{1,0:T(8,128)(2,1)}, u32[]{:S(2)}, u32[]{:S(2)}) %collective-permute-start.11) | collective-permute-done | bytes 1048608 | tf_op jit(solution)/shard_map/ppermute | solution.py:533
  104.0 7.8 %attend.1 = (bf16[32,2048,256]{2,1,0:T(8,128)(2,1)}, bf16[256,1024]{1,0:T(8,128)(2,1)}, bf16[256,256]{1,0:T(8,128)(2,1)}) custom-call(s32[3]{0:T(128)} %get-tuple-element.130.place, bf16[256,2048]{1,0:T(8,128)(2,1)} %collective-permute-done.10.refs_0_, bf16[256,2048]{1,0:T(8,128)(2,1)} %collective-permute-done.11.refs_1_, ...), custom_call_target="tpu_custom_call", output_to_operand_aliasing={{0}: (5, {})} | custom-call | flops 805306368 | bytes 2097152 | tf_op jit(solution)/shard_map/attend/pallas_call | solution.py:224
  111.8 0.9 copy-done.3
  112.7 3.8 %weight_other.1 = (bf16[4,1024,128]{2,1,0:T(8,128)(2,1)}, bf16[4,1024,128]{2,1,0:T(8,128)(2,1)}) custom-call(s32[5]{0:T(128)S(1)} %stack.96.place, bf16[32,2048,256]{2,1,0:T(8,128)(2,1)} %get-tuple-element.93.held, bf16[256,256]{1,0:T(8,128)(2,1)S(1)} %copy-done.3), custom_call_target="tpu_custom_call" | custom-call | flops 536870912 | bytes 4194304 | tf_op jit(solution)/shard_map/weight_other/pallas_call | solution.py:309
  117.2 2.2 %place_rows.3 = bf16[8192,256]{1,0:T(8,128)(2,1)} custom-call(s32[2]{0:T(128)S(1)} %broadcast_xor_fusion.place, bf16[1024,256]{1,0:T(8,128)(2,1)} %collective-permute-done.12.refs_0_, bf16[1024,256]{1,0:T(8,128)(2,1)} %collective-permute-done.16.refs_1_, bf16[8192,256]{1,0:T(8,128)(2,1)} %place_rows.2.refs_2_), custom_call_target="tpu_custom_call", output_to_operand_aliasing={{}: (3, {})} | custom-call | bytes 2097152 | tf_op jit(solution)/shard_map/place_rows/pallas_call | solution.py:446
  119.6 3.3 %weight_send.1 = (bf16[2,1024,128]{2,1,0:T(8,128)(2,1)S(1)}, bf16[2,1024,128]{2,1,0:T(8,128)(2,1)S(1)}) custom-call(s32[5]{0:T(128)S(1)} %stack.117.place, bf16[32,2048,256]{2,1,0:T(8,128)(2,1)} %get-tuple-element.93.held, bf16[256,256]{1,0:T(8,128)(2,1)S(1)} %copy-done.4, bf16[4,1024,128]{2,1,0:T(8,128)(2,1)} %collective-permute-done.18.refs_0_), custom_call_target="tpu_custom_call" | custom-call | flops 268435456 | bytes 2097152 | tf_op jit(solution)/shard_map/weight_send/pallas_call | solution.py:309
  123.6 1.5 %collective-permute-start.21 = (bf16[2,1024,128]{2,1,0:T(8,128)(2,1)S(1)}, bf16[2,1024,128]{2,1,0:T(8,128)(2,1)S(1)}, u32[]{:S(2)}, u32[]{:S(2)}) collective-permute-start(bf16[2,1024,128]{2,1,0:T(8,128)(2,1)S(1)} %get-tuple-element.106), channel_id=1, source_target_pairs={{0,16},{4,20},{8,24},{12,28},{16,0},{20,4},{24,8},{28,12},{1,17},{... | collective-permute-start | bytes 1572872 | tf_op jit(solution)/shard_map/ppermute | solution.py:346
  125.1 2.7 %collective-permute-start.23 = (bf16[256,256]{1,0:T(8,128)(2,1)S(1)}, bf16[256,256]{1,0:T(8,128)(2,1)S(1)}, u32[]{:S(2)}, u32[]{:S(2)}) collective-permute-start(bf16[256,256]{1,0:T(8,128)(2,1)S(1)} %copy-done.4), channel_id=1, source_target_pairs={{0,2},{1,3},{2,0},{3,1},{4,6},{5,7},{6,4},{7,5},{8,10},{9,11},{10,... | collective-permute-start | bytes 393224 | tf_op jit(solution)/shard_map/ppermute | solution.py:498
  127.8 1.7 %collective-permute-start.24 = (bf16[256,256]{1,0:T(8,128)(2,1)S(1)}, bf16[256,256]{1,0:T(8,128)(2,1)S(1)}, u32[]{:S(2)}, u32[]{:S(2)}) collective-permute-start(bf16[256,256]{1,0:T(8,128)(2,1)S(1)} %copy-done.4), channel_id=1, source_target_pairs={{0,3},{1,2},{2,1},{3,0},{4,7},{5,6},{6,5},{7,4},{8,11},{9,10},{10,... | collective-permute-start | bytes 393224 | tf_op jit(solution)/shard_map/ppermute | solution.py:498
  129.5 3.2 %weight_keep.1 = (f32[2,1024,128]{2,1,0:T(8,128)S(1)}, f32[2,1024,128]{2,1,0:T(8,128)S(1)}) custom-call(s32[5]{0:T(128)S(1)} %stack.117.place, bf16[32,2048,256]{2,1,0:T(8,128)(2,1)} %get-tuple-element.93.held, bf16[256,256]{1,0:T(8,128)(2,1)S(1)} %copy-done.4, bf16[4,1024,128]{2,1,0:T(8,128)(2,1)} %collective-permute-done.19.refs_0_), custom_call_target="tpu_custom_call" | custom-call | flops 268435456 | bytes 2097152 | tf_op jit(solution)/shard_map/weight_keep/pallas_call | solution.py:309
  132.7 5.2 %collective-permute-done.23.refs_2_ = bf16[256,256]{1,0:T(8,128)(2,1)S(1)} collective-permute-done((bf16[256,256]{1,0:T(8,128)(2,1)S(1)}, bf16[256,256]{1,0:T(8,128)(2,1)S(1)}, u32[]{:S(2)}, u32[]{:S(2)}) %collective-permute-start.23) | collective-permute-done | bytes 131104 | tf_op jit(solution)/shard_map/ppermute | solution.py:498
  138.0 0.9 collective-permute-start.25
  138.9 1.5 %collective-permute-start.26 = (bf16[1024,128]{1,0:T(8,128)(2,1)S(1)}, bf16[1024,128]{1,0:T(8,128)(2,1)S(1)}, u32[]{:S(2)}, u32[]{:S(2)}) collective-permute-start(bf16[1024,128]{1,0:T(8,128)(2,1)S(1)} %get-tuple-element.111), channel_id=1, source_target_pairs={{0,8},{4,12},{8,0},{12,4},{16,24},{20,28},{24,16},{28,20},{1,9},{5... | collective-permute-start | bytes 786440 | tf_op jit(solution)/shard_map/ppermute | solution.py:346
  140.4 4.1 %input_gradient.1 = bf16[256,2048]{1,0:T(8,128)(2,1)} custom-call(s32[8]{0:T(128)S(1)} %iota_xor_fusion.place, bf16[256,256]{1,0:T(8,128)(2,1)S(1)} %copy-done.4, bf16[256,256]{1,0:T(8,128)(2,1)S(1)} %collective-permute-done.22.refs_1_, bf16[256,256]{1,0:T(8,128)(2,1)S(1)} %collective-permute-done.23.refs_2_, ...), custom_call_target="tpu_custom_call" | custom-call | flops 1073741824 | bytes 8912896 | tf_op jit(solution)/shard_map/input_gradient/pallas_call | solution.py:73
  144.6 1.2 collective-permute-done.26.last_b
  145.8 1.1 weight_finish.1
  (49 shorter events, 5.1 us)
Async XLA Ops:
  0.6 42.6 %collective-permute-start = (bf16[256,2048]{1,0:T(8,128)(2,1)}, bf16[256,2048]{1,0:T(8,128)(2,1)}, u32[]{:S(2)}, u32[]{:S(2)}) collective-permute-start(bf16[256,2048]{1,0:T(8,128)(2,1)} %refs_0_.1), channel_id=1, source_target_pairs={{0,1},{1,2},{2,3},{4,5},{5,6},{6,7},{8,9},{9,10},{10,11},{12,13},{... | collective-permute-start | bytes 3145736 | tf_op jit(solution)/shard_map/ppermute | solution.py:530
  6.5 36.7 %collective-permute-start.1 = (bf16[256,2048]{1,0:T(8,128)(2,1)}, bf16[256,2048]{1,0:T(8,128)(2,1)}, u32[]{:S(2)}, u32[]{:S(2)}) collective-permute-start(bf16[256,2048]{1,0:T(8,128)(2,1)} %refs_0_.1), channel_id=1, source_target_pairs={{1,0},{2,1},{3,2},{5,4},{6,5},{7,6},{9,8},{10,9},{11,10},{13,12},{... | collective-permute-start | bytes 3145736 | tf_op jit(solution)/shard_map/ppermute | solution.py:533
  15.0 23.8 %collective-permute-start.2 = (bf16[256,256]{1,0:T(8,128)(2,1)S(1)}, bf16[256,256]{1,0:T(8,128)(2,1)S(1)}, u32[]{:S(2)}, u32[]{:S(2)}) collective-permute-start(bf16[256,256]{1,0:T(8,128)(2,1)S(1)} %get-tuple-element.125), channel_id=1, source_target_pairs={{0,1},{1,0},{2,3},{3,2},{4,5},{5,4},{6,7},{7,6},{8,9},{9,8},{10,11... | collective-permute-start | bytes 393224 | tf_op jit(solution)/shard_map/ppermute | solution.py:498
  17.7 25.4 %collective-permute-start.3 = (bf16[256,256]{1,0:T(8,128)(2,1)S(1)}, bf16[256,256]{1,0:T(8,128)(2,1)S(1)}, u32[]{:S(2)}, u32[]{:S(2)}) collective-permute-start(bf16[256,256]{1,0:T(8,128)(2,1)S(1)} %get-tuple-element.124), channel_id=1, source_target_pairs={{0,2},{1,3},{2,0},{3,1},{4,6},{5,7},{6,4},{7,5},{8,10},{9,11},{10,... | collective-permute-start | bytes 393224 | tf_op jit(solution)/shard_map/ppermute | solution.py:498
  20.3 22.8 %collective-permute-start.4 = (bf16[256,256]{1,0:T(8,128)(2,1)S(1)}, bf16[256,256]{1,0:T(8,128)(2,1)S(1)}, u32[]{:S(2)}, u32[]{:S(2)}) collective-permute-start(bf16[256,256]{1,0:T(8,128)(2,1)S(1)} %get-tuple-element.123), channel_id=1, source_target_pairs={{0,3},{1,2},{2,1},{3,0},{4,7},{5,6},{6,5},{7,4},{8,11},{9,10},{10,... | collective-permute-start | bytes 393224 | tf_op jit(solution)/shard_map/ppermute | solution.py:498
  43.2 15.2 %collective-permute-start.5 = (bf16[256,2048]{1,0:T(8,128)(2,1)}, bf16[256,2048]{1,0:T(8,128)(2,1)}, u32[]{:S(2)}, u32[]{:S(2)}) collective-permute-start(bf16[256,2048]{1,0:T(8,128)(2,1)} %collective-permute-done.refs_0_), channel_id=1, source_target_pairs={{1,2},{2,3},{5,6},{6,7},{9,10},{10,11},{13,14},{14,15},{17,18},{18... | collective-permute-start | bytes 3145736 | tf_op jit(solution)/shard_map/ppermute | solution.py:530
  44.8 26.4 %collective-permute-start.6 = (bf16[256,2048]{1,0:T(8,128)(2,1)}, bf16[256,2048]{1,0:T(8,128)(2,1)}, u32[]{:S(2)}, u32[]{:S(2)}) collective-permute-start(bf16[256,2048]{1,0:T(8,128)(2,1)} %collective-permute-done.1.refs_0_), channel_id=1, source_target_pairs={{1,0},{2,1},{5,4},{6,5},{9,8},{10,9},{13,12},{14,13},{17,16},{18,1... | collective-permute-start | bytes 3145736 | tf_op jit(solution)/shard_map/ppermute | solution.py:533
  46.1 25.2 %collective-permute-start.7 = (bf16[2048,256]{1,0:T(8,128)(2,1)S(1)}, bf16[2048,256]{1,0:T(8,128)(2,1)}, u32[]{:S(2)}, u32[]{:S(2)}) collective-permute-start(bf16[2048,256]{1,0:T(8,128)(2,1)S(1)} %constant_dynamic-update-slice_fusion.refs_0_.refs_4_), channel_id=1, source_target_pairs={{0,4},{4,0},{8,12},{12,8},{16,20},{20,16},{24,28},{28,24},{1,5},{5... | collective-permute-start | bytes 3145736 | tf_op jit(solution)/shard_map/ppermute | solution.py:346
  46.2 25.6 %collective-permute-start.8 = (bf16[2048,256]{1,0:T(8,128)(2,1)S(1)}, bf16[2048,256]{1,0:T(8,128)(2,1)S(1)}, u32[]{:S(2)}, u32[]{:S(2)}) collective-permute-start(bf16[2048,256]{1,0:T(8,128)(2,1)S(1)} %constant_dynamic-update-slice_fusion.refs_0_.refs_4_), channel_id=1, source_target_pairs={{0,8},{4,12},{8,0},{12,4},{16,24},{20,28},{24,16},{28,20},{1,9},{5... | collective-permute-start | bytes 3145736 | tf_op jit(solution)/shard_map/ppermute | solution.py:346
  47.8 25.2 %collective-permute-start.9 = (bf16[2048,256]{1,0:T(8,128)(2,1)S(1)}, bf16[2048,256]{1,0:T(8,128)(2,1)S(1)}, u32[]{:S(2)}, u32[]{:S(2)}) collective-permute-start(bf16[2048,256]{1,0:T(8,128)(2,1)S(1)} %constant_dynamic-update-slice_fusion.refs_0_.refs_4_), channel_id=1, source_target_pairs={{0,16},{4,20},{8,24},{12,28},{16,0},{20,4},{24,8},{28,12},{1,17},{... | collective-permute-start | bytes 3145736 | tf_op jit(solution)/shard_map/ppermute | solution.py:346
  73.0 5.8 %collective-permute-start.14 = (bf16[2048,256]{1,0:T(8,128)(2,1)S(1)}, bf16[2048,256]{1,0:T(8,128)(2,1)S(1)}, u32[]{:S(2)}, u32[]{:S(2)}) collective-permute-start(bf16[2048,256]{1,0:T(8,128)(2,1)S(1)} %collective-permute-done.8.refs_2_.refs_6_), channel_id=1, source_target_pairs={{0,4},{4,0},{8,12},{12,8},{16,20},{20,16},{24,28},{28,24},{1,5},{5... | collective-permute-start | bytes 3145736 | tf_op jit(solution)/shard_map/ppermute | solution.py:346
  73.0 13.2 %collective-permute-start.15 = (bf16[2048,256]{1,0:T(8,128)(2,1)S(1)}, bf16[2048,256]{1,0:T(8,128)(2,1)}, u32[]{:S(2)}, u32[]{:S(2)}) collective-permute-start(bf16[2048,256]{1,0:T(8,128)(2,1)S(1)} %collective-permute-done.9.refs_4_.refs_8_), channel_id=1, source_target_pairs={{0,4},{4,0},{8,12},{12,8},{16,20},{20,16},{24,28},{28,24},{1,5},{5... | collective-permute-start | bytes 3145736 | tf_op jit(solution)/shard_map/ppermute | solution.py:346
  73.5 20.2 %collective-permute-start.10 = (bf16[256,2048]{1,0:T(8,128)(2,1)}, bf16[256,2048]{1,0:T(8,128)(2,1)}, u32[]{:S(2)}, u32[]{:S(2)}) collective-permute-start(bf16[256,2048]{1,0:T(8,128)(2,1)} %collective-permute-done.5.refs_0_), channel_id=1, source_target_pairs={{2,3},{6,7},{10,11},{14,15},{18,19},{22,23},{26,27},{30,31}} | collective-permute-start | bytes 3145736 | tf_op jit(solution)/shard_map/ppermute | solution.py:530
  75.2 28.3 %collective-permute-start.11 = (bf16[256,2048]{1,0:T(8,128)(2,1)}, bf16[256,2048]{1,0:T(8,128)(2,1)}, u32[]{:S(2)}, u32[]{:S(2)}) collective-permute-start(bf16[256,2048]{1,0:T(8,128)(2,1)} %collective-permute-done.6.refs_1_), channel_id=1, source_target_pairs={{1,0},{5,4},{9,8},{13,12},{17,16},{21,20},{25,24},{29,28}} | collective-permute-start | bytes 3145736 | tf_op jit(solution)/shard_map/ppermute | solution.py:533
  78.3 14.1 %collective-permute-start.12 = (bf16[1024,256]{1,0:T(8,128)(2,1)}, bf16[1024,256]{1,0:T(8,128)(2,1)}, u32[]{:S(2)}, u32[]{:S(2)}) collective-permute-start(bf16[1024,256]{1,0:T(8,128)(2,1)} %slice.6), channel_id=1, source_target_pairs={{0,8},{4,12},{8,0},{12,4},{16,24},{20,28},{24,16},{28,20},{1,9},{5... | collective-permute-start | bytes 1572872 | tf_op jit(solution)/shard_map/ppermute | solution.py:346
  78.8 1.0 copy-start
  79.8 13.9 %collective-permute-start.13 = (bf16[1024,256]{1,0:T(8,128)(2,1)}, bf16[1024,256]{1,0:T(8,128)(2,1)}, u32[]{:S(2)}, u32[]{:S(2)}) collective-permute-start(bf16[1024,256]{1,0:T(8,128)(2,1)} %slice.7), channel_id=1, source_target_pairs={{0,16},{4,20},{8,24},{12,28},{16,0},{20,4},{24,8},{28,12},{1,17},{... | collective-permute-start | bytes 1572872 | tf_op jit(solution)/shard_map/ppermute | solution.py:346
  86.2 1.2 copy-start.1
  103.4 8.4 %collective-permute-start.16 = (bf16[1024,256]{1,0:T(8,128)(2,1)}, bf16[1024,256]{1,0:T(8,128)(2,1)}, u32[]{:S(2)}, u32[]{:S(2)}) collective-permute-start(bf16[1024,256]{1,0:T(8,128)(2,1)} %collective-permute-done.12.refs_0_), channel_id=1, source_target_pairs={{0,4},{4,0},{8,12},{12,8},{16,20},{20,16},{24,28},{28,24},{1,5},{5... | collective-permute-start | bytes 1572872 | tf_op jit(solution)/shard_map/ppermute | solution.py:346
  103.4 8.4 %collective-permute-start.17 = (bf16[1024,256]{1,0:T(8,128)(2,1)}, bf16[1024,256]{1,0:T(8,128)(2,1)}, u32[]{:S(2)}, u32[]{:S(2)}) collective-permute-start(bf16[1024,256]{1,0:T(8,128)(2,1)} %collective-permute-done.13.refs_10_), channel_id=1, source_target_pairs={{0,4},{4,0},{8,12},{12,8},{16,20},{20,16},{24,28},{28,24},{1,5},{5... | collective-permute-start | bytes 1572872 | tf_op jit(solution)/shard_map/ppermute | solution.py:346
  104.0 13.2 %copy-start.5 = (s32[2]{0:T(128)S(1)}, s32[2]{0:T(128)}, u32[]{:S(2)}) copy-start(s32[2]{0:T(128)} %constant.72.clone) | copy-start | bytes 28
  111.8 0.9 copy-start.3
  112.7 6.9 %copy-start.4 = (bf16[256,256]{1,0:T(8,128)(2,1)S(1)}, bf16[256,256]{1,0:T(8,128)(2,1)}, u32[]{:S(2)}) copy-start(bf16[256,256]{1,0:T(8,128)(2,1)} %get-tuple-element.112.d_projected.refs_0_) | copy-start | bytes 393220
  116.6 3.1 %collective-permute-start.18 = (bf16[4,1024,128]{2,1,0:T(8,128)(2,1)}, bf16[4,1024,128]{2,1,0:T(8,128)(2,1)}, u32[]{:S(2)}, u32[]{:S(2)}) collective-permute-start(bf16[4,1024,128]{2,1,0:T(8,128)(2,1)} %get-tuple-element.98), channel_id=1, source_target_pairs={{0,4},{4,0},{8,12},{12,8},{16,20},{20,16},{24,28},{28,24},{1,5},{5... | collective-permute-start | bytes 3145736 | tf_op jit(solution)/shard_map/ppermute | solution.py:346
  116.7 11.1 %collective-permute-start.19 = (bf16[4,1024,128]{2,1,0:T(8,128)(2,1)}, bf16[4,1024,128]{2,1,0:T(8,128)(2,1)}, u32[]{:S(2)}, u32[]{:S(2)}) collective-permute-start(bf16[4,1024,128]{2,1,0:T(8,128)(2,1)} %get-tuple-element.102), channel_id=1, source_target_pairs={{0,4},{4,0},{8,12},{12,8},{16,20},{20,16},{24,28},{28,24},{1,5},{5... | collective-permute-start | bytes 3145736 | tf_op jit(solution)/shard_map/ppermute | solution.py:346
  119.4 20.9 %copy-start.2 = (bf16[2048,256]{1,0:T(8,128)(2,1)S(1)}, bf16[2048,256]{1,0:T(8,128)(2,1)}, u32[]{:S(2)}) copy-start(bf16[2048,256]{1,0:T(8,128)(2,1)} %copy-done) | copy-start | bytes 3145732
  122.9 14.9 %collective-permute-start.20 = (bf16[2,1024,128]{2,1,0:T(8,128)(2,1)S(1)}, bf16[2,1024,128]{2,1,0:T(8,128)(2,1)S(1)}, u32[]{:S(2)}, u32[]{:S(2)}) collective-permute-start(bf16[2,1024,128]{2,1,0:T(8,128)(2,1)S(1)} %get-tuple-element.105), channel_id=1, source_target_pairs={{0,8},{4,12},{8,0},{12,4},{16,24},{20,28},{24,16},{28,20},{1,9},{5... | collective-permute-start | bytes 1572872 | tf_op jit(solution)/shard_map/ppermute | solution.py:346
  123.6 14.3 %collective-permute-start.21 = (bf16[2,1024,128]{2,1,0:T(8,128)(2,1)S(1)}, bf16[2,1024,128]{2,1,0:T(8,128)(2,1)S(1)}, u32[]{:S(2)}, u32[]{:S(2)}) collective-permute-start(bf16[2,1024,128]{2,1,0:T(8,128)(2,1)S(1)} %get-tuple-element.106), channel_id=1, source_target_pairs={{0,16},{4,20},{8,24},{12,28},{16,0},{20,4},{24,8},{28,12},{1,17},{... | collective-permute-start | bytes 1572872 | tf_op jit(solution)/shard_map/ppermute | solution.py:346
  125.1 7.6 %collective-permute-start.22 = (bf16[256,256]{1,0:T(8,128)(2,1)S(1)}, bf16[256,256]{1,0:T(8,128)(2,1)S(1)}, u32[]{:S(2)}, u32[]{:S(2)}) collective-permute-start(bf16[256,256]{1,0:T(8,128)(2,1)S(1)} %copy-done.4), channel_id=1, source_target_pairs={{0,1},{1,0},{2,3},{3,2},{4,5},{5,4},{6,7},{7,6},{8,9},{9,8},{10,11... | collective-permute-start | bytes 393224 | tf_op jit(solution)/shard_map/ppermute | solution.py:498
  125.1 12.8 %collective-permute-start.23 = (bf16[256,256]{1,0:T(8,128)(2,1)S(1)}, bf16[256,256]{1,0:T(8,128)(2,1)S(1)}, u32[]{:S(2)}, u32[]{:S(2)}) collective-permute-start(bf16[256,256]{1,0:T(8,128)(2,1)S(1)} %copy-done.4), channel_id=1, source_target_pairs={{0,2},{1,3},{2,0},{3,1},{4,6},{5,7},{6,4},{7,5},{8,10},{9,11},{10,... | collective-permute-start | bytes 393224 | tf_op jit(solution)/shard_map/ppermute | solution.py:498
  127.8 10.1 %collective-permute-start.24 = (bf16[256,256]{1,0:T(8,128)(2,1)S(1)}, bf16[256,256]{1,0:T(8,128)(2,1)S(1)}, u32[]{:S(2)}, u32[]{:S(2)}) collective-permute-start(bf16[256,256]{1,0:T(8,128)(2,1)S(1)} %copy-done.4), channel_id=1, source_target_pairs={{0,3},{1,2},{2,1},{3,0},{4,7},{5,6},{6,5},{7,4},{8,11},{9,10},{10,... | collective-permute-start | bytes 393224 | tf_op jit(solution)/shard_map/ppermute | solution.py:498
  138.0 6.6 %collective-permute-start.25 = (bf16[1024,128]{1,0:T(8,128)(2,1)S(1)}, bf16[1024,128]{1,0:T(8,128)(2,1)S(1)}, u32[]{:S(2)}, u32[]{:S(2)}) collective-permute-start(bf16[1024,128]{1,0:T(8,128)(2,1)S(1)} %get-tuple-element.110), channel_id=1, source_target_pairs={{0,16},{4,20},{8,24},{12,28},{16,0},{20,4},{24,8},{28,12},{1,17},{... | collective-permute-start | bytes 786440 | tf_op jit(solution)/shard_map/ppermute | solution.py:346
  138.9 6.9 %collective-permute-start.26 = (bf16[1024,128]{1,0:T(8,128)(2,1)S(1)}, bf16[1024,128]{1,0:T(8,128)(2,1)S(1)}, u32[]{:S(2)}, u32[]{:S(2)}) collective-permute-start(bf16[1024,128]{1,0:T(8,128)(2,1)S(1)} %get-tuple-element.111), channel_id=1, source_target_pairs={{0,8},{4,12},{8,0},{12,4},{16,24},{20,28},{24,16},{28,20},{1,9},{5... | collective-permute-start | bytes 786440 | tf_op jit(solution)/shard_map/ppermute | solution.py:346

commit v9 on v8

--- a/solution.py
+++ b/solution.py
@@ -163,10 +163,11 @@
     )
 
 
-def attend_kernel(n_chunks, place, *refs):
+def attend_kernel(n_chunks, place, order, *refs):
     chunks, refs = refs[:n_chunks], refs[n_chunks:]
     total, cached, _, allowed, queries_in, d_out_in = refs[:6]
-    held, d_queries, d_projected, chunk, rows, turned, sems, queries, d_out = refs[6:]
+    held, d_queries, d_projected, sent, kept, *refs = refs[6:]
+    chunk, rows, turned, sems, queries, d_out, buffer, part_sems = refs
     chunk_copy = fetch_chunk(place, chunks, chunk, sems.at[0])
     rows_copy = fetch_rows(place, cached, rows, sems.at[1])
     others = [
@@ -183,7 +184,7 @@
     projected = (
         total[...] + jnp.dot(chunk[...], rows[...], preferred_element_type=jnp.float32)
     ).astype(jnp.bfloat16)
-    kept = allowed[...] > 0
+    seen = allowed[...] > 0
     for copy in others:
         copy.wait()
     factor = 1.0 / math.sqrt(HD)
@@ -197,12 +198,15 @@
         d_keys = jnp.zeros(keys.shape, jnp.float32)
         d_values = jnp.zeros(keys.shape, jnp.float32)
         for g in range(head * group, (head + 1) * group):
+            if g == heads * group // 2:
+                keep.wait()
+                copies = fetch_parts(order, held, range(4), buffer, part_sems)
             columns = slice(g * HD, (g + 1) * HD)
             query, grad = queries[:, columns], d_out[:, columns]
             scores = (
                 lax.dot_general(keys, query, across, preferred_element_type=jnp.float32) * factor
             )
-            scores = jnp.where(kept, scores, -1e30)
+            scores = jnp.where(seen, scores, -1e30)
             weights = jnp.exp(scores - jnp.max(scores, axis=0, keepdims=True))
             probs = weights / jnp.sum(weights, axis=0, keepdims=True)
             probs_low = probs.astype(jnp.bfloat16)
@@ -216,25 +220,39 @@
             d_values = d_values + jnp.dot(probs_low, grad, preferred_element_type=jnp.float32)
         d_projected[:, start : start + HD] = d_keys.astype(jnp.bfloat16)
         d_projected[:, start + HD : start + 2 * HD] = d_values.astype(jnp.bfloat16)
-    keep.wait()
-
-
-def attend(chunks, which, index, cached, total, held, queries, d_out, allowed, n_chunks):
+
+    def give(g, side, position, here, part):
+        out = (sent, kept)[g]
+        out[2 * side + position, here, :] = part.astype(out.dtype)
+
+    weight_products(copies, (SENT, KEPT), buffer, d_projected, give)
+
+
+def attend(chunks, which, index, cached, total, held, queries, d_out, allowed, order, n_chunks):
+    feats, length = held.shape[1:]
+    parts = jax.ShapeDtypeStruct((4, feats // 2, total.shape[1] // 2), jnp.bfloat16)
     vmem, anywhere = pl.BlockSpec(memory_space=pltpu.VMEM), pl.BlockSpec(memory_space=pl.ANY)
     return pl.pallas_call(
         functools.partial(attend_kernel, len(chunks)),
-        in_specs=[pl.BlockSpec(memory_space=pltpu.SMEM)]
+        in_specs=[pl.BlockSpec(memory_space=pltpu.SMEM)] * 2
         + [anywhere] * len(chunks)
         + [vmem, anywhere, anywhere, vmem, anywhere, anywhere],
-        out_specs=[anywhere, vmem, vmem],
+        out_specs=[anywhere] + [vmem] * 4,
         out_shape=[
             jax.ShapeDtypeStruct(held.shape, held.dtype),
             jax.ShapeDtypeStruct(queries.shape, jnp.bfloat16),
             jax.ShapeDtypeStruct(total.shape, jnp.bfloat16),
+            parts,
+            parts,
         ],
         scratch_shapes=absorb_scratch(chunks[0], cached, 5)
-        + [pltpu.VMEM(queries.shape, queries.dtype), pltpu.VMEM(d_out.shape, d_out.dtype)],
-        input_output_aliases={3 + len(chunks): 0},
+        + [
+            pltpu.VMEM(queries.shape, queries.dtype),
+            pltpu.VMEM(d_out.shape, d_out.dtype),
+            pltpu.VMEM((4, feats // 2, length), held.dtype),
+            pltpu.SemaphoreType.DMA((4,)),
+        ],
+        input_output_aliases={4 + len(chunks): 0},
         cost_estimate=pl.CostEstimate(
             flops=12 * allowed.size * queries.shape[1],
             bytes_accessed=8 * queries.size,
@@ -244,6 +262,7 @@
         name="attend",
     )(
         absorb_place(index, which, n_chunks),
+        order,
         *chunks,
         total,
         cached,
@@ -258,24 +277,24 @@
 KEPT = ((1, 1, 0), (2, 0, 0), (3, 0, 1), (3, 1, 1))
 
 
-def weight_kernel(groups, place, held, d_projected, *refs):
-    *refs, buffer, sems = refs
-    joined = len(groups) > 1
-    n_out = len(groups) if joined else 2
-    added, outs = refs[:-n_out], refs[-n_out:]
+def fetch_parts(place, held, chunks, buffer, sems):
     rows = buffer.shape[1]
-    half = d_projected.shape[1] // 2
-    block = min(rows, 256)
     start = pl.multiple_of(place[4] * rows, rows)
-    chunks = sorted({chunk for group in groups for chunk, _, _ in group})
     copies = {}
     for chunk in chunks:
         copies[chunk] = pltpu.make_async_copy(
             held.at[place[chunk], pl.ds(start, rows), :], buffer.at[chunk], sems.at[chunk]
         )
         copies[chunk].start()
-    for chunk in chunks:
-        copies[chunk].wait()
+    return copies
+
+
+def weight_products(copies, groups, buffer, d_projected, give):
+    rows = buffer.shape[1]
+    half = d_projected.shape[1] // 2
+    block = min(rows, 256)
+    for chunk, copy in copies.items():
+        copy.wait()
         wanted = [
             (g, side, position)
             for g, group in enumerate(groups)
@@ -292,38 +311,49 @@
             )
             for g, side, position in wanted:
                 part = total[:, (side - first) * half : (side - first + 1) * half]
-                if added:
-                    part = part + added[0][2 * side + position, here, :].astype(jnp.float32)
-                if joined:
-                    outs[g][2 * side + position, here, :] = part.astype(outs[g].dtype)
-                else:
-                    outs[side][position, here, :] = part.astype(outs[side].dtype)
-
-
-def weight_parts(held, d_projected, place, groups, added, dtype, name):
+                give(g, side, position, here, part)
+
+
+def weight_kernel(group, place, held, d_projected, *refs):
+    *added, out_a, out_b, buffer, sems = refs
+    copies = fetch_parts(place, held, sorted({part[0] for part in group}), buffer, sems)
+
+    def give(_, side, position, here, part):
+        if added:
+            part = part + added[0][2 * side + position, here, :].astype(jnp.float32)
+        out = (out_a, out_b)[side]
+        out[position, here, :] = part.astype(out.dtype)
+
+    weight_products(copies, (group,), buffer, d_projected, give)
+
+
+def weight_parts(held, d_projected, place, group, added, dtype, name):
     length, cols = d_projected.shape
     rows = held.shape[1] // 2
     vmem = pl.BlockSpec(memory_space=pltpu.VMEM)
-    depth = 4 if len(groups) > 1 else 2
-    shape = jax.ShapeDtypeStruct((depth, rows, cols // 2), dtype)
     return pl.pallas_call(
-        functools.partial(weight_kernel, groups),
+        functools.partial(weight_kernel, group),
         in_specs=[pl.BlockSpec(memory_space=pltpu.SMEM), pl.BlockSpec(memory_space=pl.ANY)]
         + [vmem] * (1 + len(added)),
         out_specs=[vmem] * 2,
-        out_shape=[shape] * 2,
+        out_shape=[jax.ShapeDtypeStruct((2, rows, cols // 2), dtype)] * 2,
         scratch_shapes=[
             pltpu.VMEM((4, rows, length), held.dtype),
             pltpu.SemaphoreType.DMA((4,)),
         ],
         cost_estimate=pl.CostEstimate(
-            flops=4 * length * rows * cols * len(groups),
-            bytes_accessed=8 * rows * cols * len(groups),
-            transcendentals=0,
+            flops=4 * length * rows * cols, bytes_accessed=8 * rows * cols, transcendentals=0
         ),
         compiler_params=pltpu.CompilerParams(vmem_limit_bytes=VMEM_WHOLE),
         name=name,
     )(place, held, d_projected, *added)
+
+
+def add_kernel(place, own_a, own_b, other, out_a, out_b):
+    depth = own_a.shape[0]
+    for side, (own, out) in enumerate(((own_a, out_a), (own_b, out_b))):
+        other_here = other[side * depth : (side + 1) * depth]
+        out[...] = (own[...] + other_here.astype(jnp.float32)).astype(out.dtype)
 
 
 def combine_kernel(place, keep_a, got_a, keep_b, got_b, out_a, out_b):
@@ -348,23 +378,28 @@
     return index % 2, (index // 2) % 2, index // 4, swap
 
 
-def weight_sum(held, d_projected, pieces, beside):
-    core, x, y, swap = plane()
+def weight_order(other):
+    core, x, y, _ = plane()
+    chunks = [3 - x - 2 * y, 1 - x + 2 * y, x + 2 - 2 * y, x + 2 * y]
+    return jnp.stack(chunks + [1 - core if other else core])
+
+
+def weight_sum(held, d_projected, sent, kept, pieces, beside):
+    swap = plane()[3]
     rows, cols = held.shape[1] // 2, d_projected.shape[1]
     none = jnp.zeros((1,), jnp.int32)
-    chunks = [3 - x - 2 * y, 1 - x + 2 * y, x + 2 - 2 * y, x + 2 * y]
-
-    def parts(which, groups, added, dtype, name):
-        place = jnp.stack(chunks + [which])
-        return weight_parts(held, d_projected, place, groups, added, dtype, name)
-
-    sent, kept = parts(1 - core, (SENT, KEPT), [], jnp.bfloat16, "weight_other")
+    order = weight_order(False)
     sent, kept = swap(sent, 1), swap(kept, 1)
-    sent, beside = lax.optimization_barrier((sent, beside))
-    send_a, send_b = parts(core, (SENT,), [sent], jnp.bfloat16, "weight_send")
+    own = weight_parts(held, d_projected, order, SENT, [], jnp.float32, "weight_send")
+    shape = jax.ShapeDtypeStruct(own[0].shape, jnp.bfloat16)
+    send_a, send_b = on_chip(
+        add_kernel, none, list(own) + [sent], [shape] * 2, 2 * cols * rows, "weight_add"
+    )
     got_a, got_b = swap(send_a, 2), swap(send_b, 4)
-    keep_a, keep_b = parts(core, (KEPT,), [kept], jnp.float32, "weight_keep")
-    got_a, got_b, pieces = lax.optimization_barrier((got_a, got_b, pieces))
+    keep_a, keep_b = weight_parts(
+        held, d_projected, order, KEPT, [kept], jnp.float32, "weight_keep"
+    )
+    got_a, got_b, pieces, beside = lax.optimization_barrier((got_a, got_b, pieces, beside))
 
     small = jax.ShapeDtypeStruct((rows, cols // 2), jnp.bfloat16)
     arrays = [keep_a, got_a, keep_b, got_b]
@@ -555,16 +590,18 @@
             if s < n_z - 1:
                 total, held = absorb(chunks, which, index, cached, total, held, n_z)
 
-        held, d_queries, d_projected = attend(
-            chunks, which, index, cached, total, held, queries, d_out, allowed, n_z
+        order = weight_order(True) if tuned else jnp.zeros((5,), jnp.int32)
+        held, d_queries, d_projected, sent, kept = attend(
+            chunks, which, index, cached, total, held, queries, d_out, allowed, order, n_z
         )
 
         pieces = [d_projected] + [pair(d_projected, s) for s in range(1, n_z)]
         if tuned:
-            d_projected, gather.far_other = lax.optimization_barrier((d_projected, gather.third()))
-            pieces[0] = d_projected
+            sent, gather.far_other = lax.optimization_barrier((sent, gather.third()))
             new_cache = gather.lay_far(own_cache.shape[0], laid)
-            finish, pieces, new_cache = weight_sum(held, d_projected, pieces, new_cache)
+            finish, pieces, new_cache = weight_sum(
+                held, d_projected, sent, kept, pieces, new_cache
+            )
             new_grad, d_tokens = finish(input_gradient(pieces, *gather.last(), feats))
         else:
             new_cache = lax.all_gather(own_cache, "dp", axis=0, tiled=True)

time: 148 us -> 145 us (0.980)
  waiting for transfers between devices: 49.8 us -> 47.3 us
    pallas_call x3 -> x2, Pallas kernels: 10.3 us -> 5.67 us  [weight_parts(): pl.pallas_call(functools.partial(weight_kernel, group), in_specs=[pl.Bloc...]
    ppermute x6, waiting for transfers between devices: 20.9 us -> 18.7 us  [pair(): return lax.ppermute(value, 'tensor', [(z, z ^ s) for z in range(n_z)])]
    pallas_call x1, Pallas kernels: 7.78 us -> 9.72 us  [attend(): pl.pallas_call(functools.partial(attend_kernel, len(chunks)), in_specs=[p...]
    pallas_call x3 -> x4, Pallas kernels: 5.35 us -> 6.82 us  [on_chip(): pl.pallas_call(kernel, in_specs=[pl.BlockSpec(memory_space=pltpu.SMEM)] +...]
  transfers between devices with their start and end apart: 27 -> 27, of which waited for: 12 -> 10; matrix products, arithmetic and copies ran while one was open for 6% -> 6% of each run, Pallas kernels for 31% -> 34%
where the time goes in v9:
time: 145 us; the launch traced here: 144 us
  Pallas kernels  49.5 us (34%)
  waiting for transfers between devices  47.3 us (33%)
  starting transfers between devices  34.2 us (24%)
  local copies, waits for them, and re-layouts  8.44 us (6%)
  other arithmetic  3.41 us (2%)
    ppermute x3, waiting for transfers between devices, body(): lax.ppermute(from_high, 'tensor', [(z + 1, z) for z in range(n_z - s)])  22.6 us
    ppermute x6, waiting for transfers between devices, pair(): return lax.ppermute(value, 'tensor', [(z, z ^ s) for z in range(n_z)])  18.7 us
    pallas_call x4, Pallas kernels, absorb(): pl.pallas_call(functools.partial(absorb_kernel, len(chunks)), in_specs=[p...  16.9 us
    ppermute x15, starting transfers between devices, swap(): return lax.ppermute(value, 'dp', [(i, i ^ bit) for i in range(8)])  11.3 us
    pallas_call x1, Pallas kernels, attend(): pl.pallas_call(functools.partial(attend_kernel, len(chunks)), in_specs=[p...  9.72 us
    ppermute x6, starting transfers between devices, pair(): return lax.ppermute(value, 'tensor', [(z, z ^ s) for z in range(n_z)])  9.67 us
    ppermute x3, starting transfers between devices, body(): lax.ppermute(from_low, 'tensor', [(z, z + 1) for z in range(s - 1, n_z -...  9.2 us
    pallas_call x4, Pallas kernels, on_chip(): pl.pallas_call(kernel, in_specs=[pl.BlockSpec(memory_space=pltpu.SMEM)] +...  6.82 us
  transfers between devices with their start and end apart: 27, of which 10 were waited for; matrix products, arithmetic and copies ran while one was open for 6% of the time, Pallas kernels for 34%

profile of v9, /device:TPU:0, one launch (start us, length us, event | category | flops | bytes accessed | tf_op | source)
XLA Modules:
  0.0 143.8 jit_solution(7439217629498524783)
XLA Ops:
  0.6 5.9 %collective-permute-start = (bf16[256,2048]{1,0:T(8,128)(2,1)}, bf16[256,2048]{1,0:T(8,128)(2,1)}, u32[]{:S(2)}, u32[]{:S(2)}) collective-permute-start(bf16[256,2048]{1,0:T(8,128)(2,1)} %refs_0_.1), channel_id=1, source_target_pairs={{0,1},{1,2},{2,3},{4,5},{5,6},{6,7},{8,9},{9,10},{10,11},{12,13},{... | collective-permute-start | bytes 3145736 | tf_op jit(solution)/shard_map/ppermute | solution.py:565
  6.5 1.3 collective-permute-start.1
  7.9 4.9 %optimizer.1 = (f32[1024,256]{1,0:T(8,128)}, f32[1024,256]{1,0:T(8,128)}, f32[1024,256]{1,0:T(8,128)}, bf16[1024,256]{1,0:T(8,128)(2,1)}) custom-call(s32[1]{0:T(128)} %bitcast.place, bf16[8192,256]{1,0:T(8,128)(2,1)} %refs_3_.3, f32[1024,256]{1,0:T(8,128)} %master.1, f32[1024,256]{1,0:T(8,128)} %moment.1, f32[1024,256]{1,0:T(8,128)} %second.1, f32[1024,256]{1,0:T(8,128)} %grad.1), custom_call_target="tpu_custom_call" | custom-call | flops 10485760 | bytes 8388608 | tf_op jit(solution)/shard_map/optimizer/pallas_call | solution.py:51
  12.8 1.1 constant_dynamic-update-slice_fusion.3
  13.9 1.1 constant_dynamic-slice_fusion
  15.0 2.7 %collective-permute-start.2 = (bf16[256,256]{1,0:T(8,128)(2,1)S(1)}, bf16[256,256]{1,0:T(8,128)(2,1)S(1)}, u32[]{:S(2)}, u32[]{:S(2)}) collective-permute-start(bf16[256,256]{1,0:T(8,128)(2,1)S(1)} %get-tuple-element.127), channel_id=1, source_target_pairs={{0,1},{1,0},{2,3},{3,2},{4,5},{5,4},{6,7},{7,6},{8,9},{9,8},{10,11... | collective-permute-start | bytes 393224 | tf_op jit(solution)/shard_map/ppermute | solution.py:533
  17.7 2.6 %collective-permute-start.3 = (bf16[256,256]{1,0:T(8,128)(2,1)S(1)}, bf16[256,256]{1,0:T(8,128)(2,1)S(1)}, u32[]{:S(2)}, u32[]{:S(2)}) collective-permute-start(bf16[256,256]{1,0:T(8,128)(2,1)S(1)} %get-tuple-element.126), channel_id=1, source_target_pairs={{0,2},{1,3},{2,0},{3,1},{4,6},{5,7},{6,4},{7,5},{8,10},{9,11},{10,... | collective-permute-start | bytes 393224 | tf_op jit(solution)/shard_map/ppermute | solution.py:533
  20.3 1.6 %fusion.1.refs_5_ = f32[256,256]{1,0:T(8,128)} fusion(s32[256]{0:T(256)} %bitcast.20), kind=kLoop, calls=%fused_computation.2 | loop fusion | flops 262144 | bytes 263168 | tf_op jit(solution)/shard_map/convert_element_type | solution.py:555
  22.5 0.7 broadcast_in_dim.2.refs_1_
  23.2 4.2 %absorb.4 = (f32[256,256]{1,0:T(8,128)}, bf16[32,2048,256]{2,1,0:T(8,128)(2,1)}) custom-call(s32[3]{0:T(128)} %get-tuple-element.131.place, bf16[256,2048]{1,0:T(8,128)(2,1)} %refs_0_.1, f32[256,256]{1,0:T(8,128)} %broadcast_in_dim.2.refs_1_, bf16[8192,256]{1,0:T(8,128)(2,1)} %refs_3_.3), custom_call_target="tpu_custom_call" | custom-call | flops 268435456 | bytes 3145728 | tf_op jit(solution)/shard_map/absorb/pallas_call | solution.py:140
  27.5 11.4 %collective-permute-done.2 = bf16[256,256]{1,0:T(8,128)(2,1)S(1)} collective-permute-done((bf16[256,256]{1,0:T(8,128)(2,1)S(1)}, bf16[256,256]{1,0:T(8,128)(2,1)S(1)}, u32[]{:S(2)}, u32[]{:S(2)}) %collective-permute-start.2) | collective-permute-done | bytes 131104 | tf_op jit(solution)/shard_map/ppermute | solution.py:533
  38.8 4.3 %collective-permute-done.3 = bf16[256,256]{1,0:T(8,128)(2,1)S(1)} collective-permute-done((bf16[256,256]{1,0:T(8,128)(2,1)S(1)}, bf16[256,256]{1,0:T(8,128)(2,1)S(1)}, u32[]{:S(2)}, u32[]{:S(2)}) %collective-permute-start.3) | collective-permute-done | bytes 131104 | tf_op jit(solution)/shard_map/ppermute | solution.py:533
  43.2 1.6 %collective-permute-start.5 = (bf16[256,2048]{1,0:T(8,128)(2,1)}, bf16[256,2048]{1,0:T(8,128)(2,1)}, u32[]{:S(2)}, u32[]{:S(2)}) collective-permute-start(bf16[256,2048]{1,0:T(8,128)(2,1)} %collective-permute-done.refs_0_), channel_id=1, source_target_pairs={{1,2},{2,3},{5,6},{6,7},{9,10},{10,11},{13,14},{14,15},{17,18},{18... | collective-permute-start | bytes 3145736 | tf_op jit(solution)/shard_map/ppermute | solution.py:565
  44.8 1.3 collective-permute-start.6
  46.2 1.6 %collective-permute-start.8 = (bf16[2048,256]{1,0:T(8,128)(2,1)S(1)}, bf16[2048,256]{1,0:T(8,128)(2,1)S(1)}, u32[]{:S(2)}, u32[]{:S(2)}) collective-permute-start(bf16[2048,256]{1,0:T(8,128)(2,1)S(1)} %constant_dynamic-update-slice_fusion.refs_0_.refs_4_), channel_id=1, source_target_pairs={{0,8},{4,12},{8,0},{12,4},{16,24},{20,28},{24,16},{28,20},{1,9},{5... | collective-permute-start | bytes 3145736 | tf_op jit(solution)/shard_map/ppermute | solution.py:376
  47.8 1.5 %collective-permute-start.9 = (bf16[2048,256]{1,0:T(8,128)(2,1)S(1)}, bf16[2048,256]{1,0:T(8,128)(2,1)S(1)}, u32[]{:S(2)}, u32[]{:S(2)}) collective-permute-start(bf16[2048,256]{1,0:T(8,128)(2,1)S(1)} %constant_dynamic-update-slice_fusion.refs_0_.refs_4_), channel_id=1, source_target_pairs={{0,16},{4,20},{8,24},{12,28},{16,0},{20,4},{24,8},{28,12},{1,17},{... | collective-permute-start | bytes 3145736 | tf_op jit(solution)/shard_map/ppermute | solution.py:376
  49.9 4.2 %absorb.5 = (f32[256,256]{1,0:T(8,128)}, bf16[32,2048,256]{2,1,0:T(8,128)(2,1)}) custom-call(s32[3]{0:T(128)} %get-tuple-element.129.place, bf16[256,2048]{1,0:T(8,128)(2,1)} %collective-permute-done.refs_0_, f32[256,256]{1,0:T(8,128)} %get-tuple-element.74.refs_1_, bf16[8192,256]{1,0:T(8,128)(2,1)} %refs_3_.3, ...), custom_call_target="tpu_custom_call", output_to_operand_aliasing={{1}: (4, {})} | custom-call | flops 268435456 | bytes 3145728 | tf_op jit(solution)/shard_map/absorb/pallas_call | solution.py:140
  54.2 4.2 %absorb.6 = (f32[256,256]{1,0:T(8,128)}, bf16[32,2048,256]{2,1,0:T(8,128)(2,1)}) custom-call(s32[3]{0:T(128)} %get-tuple-element.130.place, bf16[256,2048]{1,0:T(8,128)(2,1)} %collective-permute-done.1.refs_0_, f32[256,256]{1,0:T(8,128)} %get-tuple-element.76.refs_1_, bf16[8192,256]{1,0:T(8,128)(2,1)} %refs_3_.3, ...), custom_call_target="tpu_custom_call", output_to_operand_aliasing={{1}: (4, {})} | custom-call | flops 268435456 | bytes 3145728 | tf_op jit(solution)/shard_map/absorb/pallas_call | solution.py:140
  58.4 12.9 %collective-permute-done.6.refs_1_ = bf16[256,2048]{1,0:T(8,128)(2,1)} collective-permute-done((bf16[256,2048]{1,0:T(8,128)(2,1)}, bf16[256,2048]{1,0:T(8,128)(2,1)}, u32[]{:S(2)}, u32[]{:S(2)}) %collective-permute-start.6) | collective-permute-done | bytes 1048608 | tf_op jit(solution)/shard_map/ppermute | solution.py:568
  71.8 1.2 collective-permute-done.9.refs_4_.refs_8_
  73.5 1.7 %collective-permute-start.10 = (bf16[256,2048]{1,0:T(8,128)(2,1)}, bf16[256,2048]{1,0:T(8,128)(2,1)}, u32[]{:S(2)}, u32[]{:S(2)}) collective-permute-start(bf16[256,2048]{1,0:T(8,128)(2,1)} %collective-permute-done.5.refs_0_), channel_id=1, source_target_pairs={{2,3},{6,7},{10,11},{14,15},{18,19},{22,23},{26,27},{30,31}} | collective-permute-start | bytes 3145736 | tf_op jit(solution)/shard_map/ppermute | solution.py:565
  75.2 1.5 %collective-permute-start.11 = (bf16[256,2048]{1,0:T(8,128)(2,1)}, bf16[256,2048]{1,0:T(8,128)(2,1)}, u32[]{:S(2)}, u32[]{:S(2)}) collective-permute-start(bf16[256,2048]{1,0:T(8,128)(2,1)} %collective-permute-done.6.refs_1_), channel_id=1, source_target_pairs={{1,0},{5,4},{9,8},{13,12},{17,16},{21,20},{25,24},{29,28}} | collective-permute-start | bytes 3145736 | tf_op jit(solution)/shard_map/ppermute | solution.py:568
  76.6 0.8 slice.6
  77.5 0.8 slice.7
  78.8 1.0 copy-done
  79.8 1.5 %collective-permute-start.13 = (bf16[1024,256]{1,0:T(8,128)(2,1)}, bf16[1024,256]{1,0:T(8,128)(2,1)}, u32[]{:S(2)}, u32[]{:S(2)}) collective-permute-start(bf16[1024,256]{1,0:T(8,128)(2,1)} %slice.7), channel_id=1, source_target_pairs={{0,16},{4,20},{8,24},{12,28},{16,0},{20,4},{24,8},{28,12},{1,17},{... | collective-permute-start | bytes 1572872 | tf_op jit(solution)/shard_map/ppermute | solution.py:376
  81.9 4.2 %absorb.7 = (f32[256,256]{1,0:T(8,128)}, bf16[32,2048,256]{2,1,0:T(8,128)(2,1)}) custom-call(s32[3]{0:T(128)} %pad_add_fusion.4.place, bf16[256,2048]{1,0:T(8,128)(2,1)} %collective-permute-done.5.refs_0_, bf16[256,2048]{1,0:T(8,128)(2,1)} %collective-permute-done.6.refs_1_, f32[256,256]{1,0:T(8,128)} %get-tuple-element.82.refs_2_, ...), custom_call_target="tpu_custom_call", output_to_operand_aliasing={{1}: (5, {})} | custom-call | flops 268435456 | bytes 3145728 | tf_op jit(solution)/shard_map/absorb/pallas_call | solution.py:140
  86.2 1.2 copy-done.1
  87.4 3.3 %place_rows.2.refs_2_ = bf16[8192,256]{1,0:T(8,128)(2,1)} custom-call(s32[6]{0:T(128)S(1)} %iota_xor_fusion.1.place, bf16[2048,256]{1,0:T(8,128)(2,1)S(1)} %constant_dynamic-update-slice_fusion.refs_0_.refs_4_, bf16[2048,256]{1,0:T(8,128)(2,1)} %collective-permute-done.7.refs_1_.refs_5_, bf16[2048,256]{1,0:T(8,128)(2,1)S(1)} %collective-permute-done.8.refs_2_.refs_6_, ...), custom_call_target="tpu_custom_call" | custom-call | bytes 6291456 | tf_op jit(solution)/shard_map/place_rows/pallas_call | solution.py:481
  90.7 1.8 %collective-permute-done.12.refs_0_ = bf16[1024,256]{1,0:T(8,128)(2,1)} collective-permute-done((bf16[1024,256]{1,0:T(8,128)(2,1)}, bf16[1024,256]{1,0:T(8,128)(2,1)}, u32[]{:S(2)}, u32[]{:S(2)}) %collective-permute-start.12) | collective-permute-done | bytes 524320 | tf_op jit(solution)/shard_map/ppermute | solution.py:376
  92.4 1.2 collective-permute-done.13.refs_10_
  93.7 9.8 %collective-permute-done.11.refs_1_ = bf16[256,2048]{1,0:T(8,128)(2,1)} collective-permute-done((bf16[256,2048]{1,0:T(8,128)(2,1)}, bf16[256,2048]{1,0:T(8,128)(2,1)}, u32[]{:S(2)}, u32[]{:S(2)}) %collective-permute-start.11) | collective-permute-done | bytes 1048608 | tf_op jit(solution)/shard_map/ppermute | solution.py:568
  103.9 0.6 stack.97.order
  104.6 9.7 %attend.1 = (bf16[32,2048,256]{2,1,0:T(8,128)(2,1)}, bf16[256,1024]{1,0:T(8,128)(2,1)}, bf16[256,256]{1,0:T(8,128)(2,1)}, bf16[4,1024,128]{2,1,0:T(8,128)(2,1)}, bf16[4,1024,128]{2,1,0:T(8,128)(2,1)}) custom-call(s32[3]{0:T(128)} %get-tuple-element.132.place, s32[5]{0:T(128)} %stack.97.order, ...), custom_call_target="tpu_custom_call", output_to_operand_aliasing={{0}: (6, {})} | custom-call | flops 805306368 | bytes 2097152 | tf_op jit(solution)/shard_map/attend/pallas_call | solution.py:235
  115.0 0.9 copy-done.3
  115.9 2.5 %weight_send.1 = (f32[2,1024,128]{2,1,0:T(8,128)S(1)}, f32[2,1024,128]{2,1,0:T(8,128)S(1)}) custom-call(s32[5]{0:T(128)S(1)} %stack.90.place, bf16[32,2048,256]{2,1,0:T(8,128)(2,1)} %get-tuple-element.94.held, bf16[256,256]{1,0:T(8,128)(2,1)S(1)} %copy-done.3), custom_call_target="tpu_custom_call" | custom-call | flops 268435456 | bytes 2097152 | tf_op jit(solution)/shard_map/weight_send/pallas_call | solution.py:334
  118.4 1.5 %weight_add.1 = (bf16[2,1024,128]{2,1,0:T(8,128)(2,1)S(1)}, bf16[2,1024,128]{2,1,0:T(8,128)(2,1)S(1)}) custom-call(s32[1]{0:T(128)} %constant.66.clone.1.place, f32[2,1024,128]{2,1,0:T(8,128)S(1)} %get-tuple-element.96.own_a, f32[2,1024,128]{2,1,0:T(8,128)S(1)} %get-tuple-element.97.own_b, bf16[4,1024,128]{2,1,0:T(8,128)(2,1)} %collective-permute-done.18.other), custom_call_target="tpu_custom_call" | custom-call | flops 524288 | bytes 4194304 | tf_op jit(solution)/shard_map/weight_add/pallas_call | solution.py:73
  120.5 1.5 %collective-permute-start.20 = (bf16[2,1024,128]{2,1,0:T(8,128)(2,1)S(1)}, bf16[2,1024,128]{2,1,0:T(8,128)(2,1)S(1)}, u32[]{:S(2)}, u32[]{:S(2)}) collective-permute-start(bf16[2,1024,128]{2,1,0:T(8,128)(2,1)S(1)} %get-tuple-element.103), channel_id=1, source_target_pairs={{0,16},{4,20},{8,24},{12,28},{16,0},{20,4},{24,8},{28,12},{1,17},{... | collective-permute-start | bytes 1572872 | tf_op jit(solution)/shard_map/ppermute | solution.py:376
  122.0 2.7 %collective-permute-start.22 = (bf16[256,256]{1,0:T(8,128)(2,1)S(1)}, bf16[256,256]{1,0:T(8,128)(2,1)S(1)}, u32[]{:S(2)}, u32[]{:S(2)}) collective-permute-start(bf16[256,256]{1,0:T(8,128)(2,1)S(1)} %copy-done.4), channel_id=1, source_target_pairs={{0,2},{1,3},{2,0},{3,1},{4,6},{5,7},{6,4},{7,5},{8,10},{9,11},{10,... | collective-permute-start | bytes 393224 | tf_op jit(solution)/shard_map/ppermute | solution.py:533
  124.7 1.7 %collective-permute-start.23 = (bf16[256,256]{1,0:T(8,128)(2,1)S(1)}, bf16[256,256]{1,0:T(8,128)(2,1)S(1)}, u32[]{:S(2)}, u32[]{:S(2)}) collective-permute-start(bf16[256,256]{1,0:T(8,128)(2,1)S(1)} %copy-done.4), channel_id=1, source_target_pairs={{0,3},{1,2},{2,1},{3,0},{4,7},{5,6},{6,5},{7,4},{8,11},{9,10},{10,... | collective-permute-start | bytes 393224 | tf_op jit(solution)/shard_map/ppermute | solution.py:533
  126.4 2.2 %place_rows.3 = bf16[8192,256]{1,0:T(8,128)(2,1)} custom-call(s32[2]{0:T(128)S(1)} %broadcast_xor_fusion.place, bf16[1024,256]{1,0:T(8,128)(2,1)} %collective-permute-done.12.refs_0_, bf16[1024,256]{1,0:T(8,128)(2,1)} %collective-permute-done.16.refs_1_, bf16[8192,256]{1,0:T(8,128)(2,1)} %place_rows.2.refs_2_), custom_call_target="tpu_custom_call", output_to_operand_aliasing={{}: (3, {})} | custom-call | bytes 2097152 | tf_op jit(solution)/shard_map/place_rows/pallas_call | solution.py:481
  128.6 3.2 %weight_keep.1 = (f32[2,1024,128]{2,1,0:T(8,128)S(1)}, f32[2,1024,128]{2,1,0:T(8,128)S(1)}) custom-call(s32[5]{0:T(128)S(1)} %stack.90.place, bf16[32,2048,256]{2,1,0:T(8,128)(2,1)} %get-tuple-element.94.held, bf16[256,256]{1,0:T(8,128)(2,1)S(1)} %copy-done.4, bf16[4,1024,128]{2,1,0:T(8,128)(2,1)} %collective-permute-done.24.refs_0_), custom_call_target="tpu_custom_call" | custom-call | flops 268435456 | bytes 2097152 | tf_op jit(solution)/shard_map/weight_keep/pallas_call | solution.py:334
  131.8 3.0 %collective-permute-done.22.refs_2_ = bf16[256,256]{1,0:T(8,128)(2,1)S(1)} collective-permute-done((bf16[256,256]{1,0:T(8,128)(2,1)S(1)}, bf16[256,256]{1,0:T(8,128)(2,1)S(1)}, u32[]{:S(2)}, u32[]{:S(2)}) %collective-permute-start.22) | collective-permute-done | bytes 131104 | tf_op jit(solution)/shard_map/ppermute | solution.py:533
  134.9 0.9 collective-permute-start.25
  135.8 1.5 %collective-permute-start.26 = (bf16[1024,128]{1,0:T(8,128)(2,1)S(1)}, bf16[1024,128]{1,0:T(8,128)(2,1)S(1)}, u32[]{:S(2)}, u32[]{:S(2)}) collective-permute-start(bf16[1024,128]{1,0:T(8,128)(2,1)S(1)} %get-tuple-element.113), channel_id=1, source_target_pairs={{0,8},{4,12},{8,0},{12,4},{16,24},{20,28},{24,16},{28,20},{1,9},{5... | collective-permute-start | bytes 786440 | tf_op jit(solution)/shard_map/ppermute | solution.py:376
  137.3 4.1 %input_gradient.1 = bf16[256,2048]{1,0:T(8,128)(2,1)} custom-call(s32[8]{0:T(128)S(1)} %iota_xor_fusion.place, bf16[256,256]{1,0:T(8,128)(2,1)S(1)} %copy-done.4, bf16[256,256]{1,0:T(8,128)(2,1)S(1)} %collective-permute-done.21.refs_1_, bf16[256,256]{1,0:T(8,128)(2,1)S(1)} %collective-permute-done.22.refs_2_, ...), custom_call_target="tpu_custom_call" | custom-call | flops 1073741824 | bytes 8912896 | tf_op jit(solution)/shard_map/input_gradient/pallas_call | solution.py:73
  141.5 1.2 collective-permute-done.26.last_b
  142.7 1.1 weight_finish.1
  (49 shorter events, 5.5 us)
Async XLA Ops:
  0.6 42.6 %collective-permute-start = (bf16[256,2048]{1,0:T(8,128)(2,1)}, bf16[256,2048]{1,0:T(8,128)(2,1)}, u32[]{:S(2)}, u32[]{:S(2)}) collective-permute-start(bf16[256,2048]{1,0:T(8,128)(2,1)} %refs_0_.1), channel_id=1, source_target_pairs={{0,1},{1,2},{2,3},{4,5},{5,6},{6,7},{8,9},{9,10},{10,11},{12,13},{... | collective-permute-start | bytes 3145736 | tf_op jit(solution)/shard_map/ppermute | solution.py:565
  6.5 36.7 %collective-permute-start.1 = (bf16[256,2048]{1,0:T(8,128)(2,1)}, bf16[256,2048]{1,0:T(8,128)(2,1)}, u32[]{:S(2)}, u32[]{:S(2)}) collective-permute-start(bf16[256,2048]{1,0:T(8,128)(2,1)} %refs_0_.1), channel_id=1, source_target_pairs={{1,0},{2,1},{3,2},{5,4},{6,5},{7,6},{9,8},{10,9},{11,10},{13,12},{... | collective-permute-start | bytes 3145736 | tf_op jit(solution)/shard_map/ppermute | solution.py:568
  15.0 23.8 %collective-permute-start.2 = (bf16[256,256]{1,0:T(8,128)(2,1)S(1)}, bf16[256,256]{1,0:T(8,128)(2,1)S(1)}, u32[]{:S(2)}, u32[]{:S(2)}) collective-permute-start(bf16[256,256]{1,0:T(8,128)(2,1)S(1)} %get-tuple-element.127), channel_id=1, source_target_pairs={{0,1},{1,0},{2,3},{3,2},{4,5},{5,4},{6,7},{7,6},{8,9},{9,8},{10,11... | collective-permute-start | bytes 393224 | tf_op jit(solution)/shard_map/ppermute | solution.py:533
  17.7 25.4 %collective-permute-start.3 = (bf16[256,256]{1,0:T(8,128)(2,1)S(1)}, bf16[256,256]{1,0:T(8,128)(2,1)S(1)}, u32[]{:S(2)}, u32[]{:S(2)}) collective-permute-start(bf16[256,256]{1,0:T(8,128)(2,1)S(1)} %get-tuple-element.126), channel_id=1, source_target_pairs={{0,2},{1,3},{2,0},{3,1},{4,6},{5,7},{6,4},{7,5},{8,10},{9,11},{10,... | collective-permute-start | bytes 393224 | tf_op jit(solution)/shard_map/ppermute | solution.py:533
  20.3 22.8 %collective-permute-start.4 = (bf16[256,256]{1,0:T(8,128)(2,1)S(1)}, bf16[256,256]{1,0:T(8,128)(2,1)S(1)}, u32[]{:S(2)}, u32[]{:S(2)}) collective-permute-start(bf16[256,256]{1,0:T(8,128)(2,1)S(1)} %get-tuple-element.125), channel_id=1, source_target_pairs={{0,3},{1,2},{2,1},{3,0},{4,7},{5,6},{6,5},{7,4},{8,11},{9,10},{10,... | collective-permute-start | bytes 393224 | tf_op jit(solution)/shard_map/ppermute | solution.py:533
  43.2 15.2 %collective-permute-start.5 = (bf16[256,2048]{1,0:T(8,128)(2,1)}, bf16[256,2048]{1,0:T(8,128)(2,1)}, u32[]{:S(2)}, u32[]{:S(2)}) collective-permute-start(bf16[256,2048]{1,0:T(8,128)(2,1)} %collective-permute-done.refs_0_), channel_id=1, source_target_pairs={{1,2},{2,3},{5,6},{6,7},{9,10},{10,11},{13,14},{14,15},{17,18},{18... | collective-permute-start | bytes 3145736 | tf_op jit(solution)/shard_map/ppermute | solution.py:565
  44.8 26.4 %collective-permute-start.6 = (bf16[256,2048]{1,0:T(8,128)(2,1)}, bf16[256,2048]{1,0:T(8,128)(2,1)}, u32[]{:S(2)}, u32[]{:S(2)}) collective-permute-start(bf16[256,2048]{1,0:T(8,128)(2,1)} %collective-permute-done.1.refs_0_), channel_id=1, source_target_pairs={{1,0},{2,1},{5,4},{6,5},{9,8},{10,9},{13,12},{14,13},{17,16},{18,1... | collective-permute-start | bytes 3145736 | tf_op jit(solution)/shard_map/ppermute | solution.py:568
  46.1 25.2 %collective-permute-start.7 = (bf16[2048,256]{1,0:T(8,128)(2,1)S(1)}, bf16[2048,256]{1,0:T(8,128)(2,1)}, u32[]{:S(2)}, u32[]{:S(2)}) collective-permute-start(bf16[2048,256]{1,0:T(8,128)(2,1)S(1)} %constant_dynamic-update-slice_fusion.refs_0_.refs_4_), channel_id=1, source_target_pairs={{0,4},{4,0},{8,12},{12,8},{16,20},{20,16},{24,28},{28,24},{1,5},{5... | collective-permute-start | bytes 3145736 | tf_op jit(solution)/shard_map/ppermute | solution.py:376
  46.2 25.6 %collective-permute-start.8 = (bf16[2048,256]{1,0:T(8,128)(2,1)S(1)}, bf16[2048,256]{1,0:T(8,128)(2,1)S(1)}, u32[]{:S(2)}, u32[]{:S(2)}) collective-permute-start(bf16[2048,256]{1,0:T(8,128)(2,1)S(1)} %constant_dynamic-update-slice_fusion.refs_0_.refs_4_), channel_id=1, source_target_pairs={{0,8},{4,12},{8,0},{12,4},{16,24},{20,28},{24,16},{28,20},{1,9},{5... | collective-permute-start | bytes 3145736 | tf_op jit(solution)/shard_map/ppermute | solution.py:376
  47.8 25.2 %collective-permute-start.9 = (bf16[2048,256]{1,0:T(8,128)(2,1)S(1)}, bf16[2048,256]{1,0:T(8,128)(2,1)S(1)}, u32[]{:S(2)}, u32[]{:S(2)}) collective-permute-start(bf16[2048,256]{1,0:T(8,128)(2,1)S(1)} %constant_dynamic-update-slice_fusion.refs_0_.refs_4_), channel_id=1, source_target_pairs={{0,16},{4,20},{8,24},{12,28},{16,0},{20,4},{24,8},{28,12},{1,17},{... | collective-permute-start | bytes 3145736 | tf_op jit(solution)/shard_map/ppermute | solution.py:376
  73.0 5.8 %collective-permute-start.14 = (bf16[2048,256]{1,0:T(8,128)(2,1)S(1)}, bf16[2048,256]{1,0:T(8,128)(2,1)S(1)}, u32[]{:S(2)}, u32[]{:S(2)}) collective-permute-start(bf16[2048,256]{1,0:T(8,128)(2,1)S(1)} %collective-permute-done.8.refs_2_.refs_6_), channel_id=1, source_target_pairs={{0,4},{4,0},{8,12},{12,8},{16,20},{20,16},{24,28},{28,24},{1,5},{5... | collective-permute-start | bytes 3145736 | tf_op jit(solution)/shard_map/ppermute | solution.py:376
  73.0 13.2 %collective-permute-start.15 = (bf16[2048,256]{1,0:T(8,128)(2,1)S(1)}, bf16[2048,256]{1,0:T(8,128)(2,1)}, u32[]{:S(2)}, u32[]{:S(2)}) collective-permute-start(bf16[2048,256]{1,0:T(8,128)(2,1)S(1)} %collective-permute-done.9.refs_4_.refs_8_), channel_id=1, source_target_pairs={{0,4},{4,0},{8,12},{12,8},{16,20},{20,16},{24,28},{28,24},{1,5},{5... | collective-permute-start | bytes 3145736 | tf_op jit(solution)/shard_map/ppermute | solution.py:376
  73.5 20.2 %collective-permute-start.10 = (bf16[256,2048]{1,0:T(8,128)(2,1)}, bf16[256,2048]{1,0:T(8,128)(2,1)}, u32[]{:S(2)}, u32[]{:S(2)}) collective-permute-start(bf16[256,2048]{1,0:T(8,128)(2,1)} %collective-permute-done.5.refs_0_), channel_id=1, source_target_pairs={{2,3},{6,7},{10,11},{14,15},{18,19},{22,23},{26,27},{30,31}} | collective-permute-start | bytes 3145736 | tf_op jit(solution)/shard_map/ppermute | solution.py:565
  75.2 28.3 %collective-permute-start.11 = (bf16[256,2048]{1,0:T(8,128)(2,1)}, bf16[256,2048]{1,0:T(8,128)(2,1)}, u32[]{:S(2)}, u32[]{:S(2)}) collective-permute-start(bf16[256,2048]{1,0:T(8,128)(2,1)} %collective-permute-done.6.refs_1_), channel_id=1, source_target_pairs={{1,0},{5,4},{9,8},{13,12},{17,16},{21,20},{25,24},{29,28}} | collective-permute-start | bytes 3145736 | tf_op jit(solution)/shard_map/ppermute | solution.py:568
  78.3 14.1 %collective-permute-start.12 = (bf16[1024,256]{1,0:T(8,128)(2,1)}, bf16[1024,256]{1,0:T(8,128)(2,1)}, u32[]{:S(2)}, u32[]{:S(2)}) collective-permute-start(bf16[1024,256]{1,0:T(8,128)(2,1)} %slice.6), channel_id=1, source_target_pairs={{0,8},{4,12},{8,0},{12,4},{16,24},{20,28},{24,16},{28,20},{1,9},{5... | collective-permute-start | bytes 1572872 | tf_op jit(solution)/shard_map/ppermute | solution.py:376
  78.8 1.0 copy-start
  79.8 13.9 %collective-permute-start.13 = (bf16[1024,256]{1,0:T(8,128)(2,1)}, bf16[1024,256]{1,0:T(8,128)(2,1)}, u32[]{:S(2)}, u32[]{:S(2)}) collective-permute-start(bf16[1024,256]{1,0:T(8,128)(2,1)} %slice.7), channel_id=1, source_target_pairs={{0,16},{4,20},{8,24},{12,28},{16,0},{20,4},{24,8},{28,12},{1,17},{... | collective-permute-start | bytes 1572872 | tf_op jit(solution)/shard_map/ppermute | solution.py:376
  86.2 1.2 copy-start.1
  103.4 10.9 %collective-permute-start.16 = (bf16[1024,256]{1,0:T(8,128)(2,1)}, bf16[1024,256]{1,0:T(8,128)(2,1)}, u32[]{:S(2)}, u32[]{:S(2)}) collective-permute-start(bf16[1024,256]{1,0:T(8,128)(2,1)} %collective-permute-done.12.refs_0_), channel_id=1, source_target_pairs={{0,4},{4,0},{8,12},{12,8},{16,20},{20,16},{24,28},{28,24},{1,5},{5... | collective-permute-start | bytes 1572872 | tf_op jit(solution)/shard_map/ppermute | solution.py:376
  103.4 10.9 %collective-permute-start.17 = (bf16[1024,256]{1,0:T(8,128)(2,1)}, bf16[1024,256]{1,0:T(8,128)(2,1)}, u32[]{:S(2)}, u32[]{:S(2)}) collective-permute-start(bf16[1024,256]{1,0:T(8,128)(2,1)} %collective-permute-done.13.refs_10_), channel_id=1, source_target_pairs={{0,4},{4,0},{8,12},{12,8},{16,20},{20,16},{24,28},{28,24},{1,5},{5... | collective-permute-start | bytes 1572872 | tf_op jit(solution)/shard_map/ppermute | solution.py:376
  104.6 21.8 %copy-start.5 = (s32[2]{0:T(128)S(1)}, s32[2]{0:T(128)}, u32[]{:S(2)}) copy-start(s32[2]{0:T(128)} %constant.80.clone) | copy-start | bytes 28
  114.3 4.1 %collective-permute-start.18 = (bf16[4,1024,128]{2,1,0:T(8,128)(2,1)}, bf16[4,1024,128]{2,1,0:T(8,128)(2,1)}, u32[]{:S(2)}, u32[]{:S(2)}) collective-permute-start(bf16[4,1024,128]{2,1,0:T(8,128)(2,1)} %get-tuple-element.101), channel_id=1, source_target_pairs={{0,4},{4,0},{8,12},{12,8},{16,20},{20,16},{24,28},{28,24},{1,5},{5... | collective-permute-start | bytes 3145736 | tf_op jit(solution)/shard_map/ppermute | solution.py:376
  114.4 10.3 %collective-permute-start.24 = (bf16[4,1024,128]{2,1,0:T(8,128)(2,1)}, bf16[4,1024,128]{2,1,0:T(8,128)(2,1)}, u32[]{:S(2)}, u32[]{:S(2)}) collective-permute-start(bf16[4,1024,128]{2,1,0:T(8,128)(2,1)} %get-tuple-element.107), channel_id=1, source_target_pairs={{0,4},{4,0},{8,12},{12,8},{16,20},{20,16},{24,28},{28,24},{1,5},{5... | collective-permute-start | bytes 3145736 | tf_op jit(solution)/shard_map/ppermute | solution.py:376
  115.0 0.9 copy-start.3
  115.9 6.1 %copy-start.4 = (bf16[256,256]{1,0:T(8,128)(2,1)S(1)}, bf16[256,256]{1,0:T(8,128)(2,1)}, u32[]{:S(2)}) copy-start(bf16[256,256]{1,0:T(8,128)(2,1)} %get-tuple-element.114.d_projected.refs_0_) | copy-start | bytes 393220
  118.4 18.9 %copy-start.2 = (bf16[2048,256]{1,0:T(8,128)(2,1)S(1)}, bf16[2048,256]{1,0:T(8,128)(2,1)}, u32[]{:S(2)}) copy-start(bf16[2048,256]{1,0:T(8,128)(2,1)} %copy-done) | copy-start | bytes 3145732
  119.9 14.9 %collective-permute-start.19 = (bf16[2,1024,128]{2,1,0:T(8,128)(2,1)S(1)}, bf16[2,1024,128]{2,1,0:T(8,128)(2,1)S(1)}, u32[]{:S(2)}, u32[]{:S(2)}) collective-permute-start(bf16[2,1024,128]{2,1,0:T(8,128)(2,1)S(1)} %get-tuple-element.102), channel_id=1, source_target_pairs={{0,8},{4,12},{8,0},{12,4},{16,24},{20,28},{24,16},{28,20},{1,9},{5... | collective-permute-start | bytes 1572872 | tf_op jit(solution)/shard_map/ppermute | solution.py:376
  120.5 14.3 %collective-permute-start.20 = (bf16[2,1024,128]{2,1,0:T(8,128)(2,1)S(1)}, bf16[2,1024,128]{2,1,0:T(8,128)(2,1)S(1)}, u32[]{:S(2)}, u32[]{:S(2)}) collective-permute-start(bf16[2,1024,128]{2,1,0:T(8,128)(2,1)S(1)} %get-tuple-element.103), channel_id=1, source_target_pairs={{0,16},{4,20},{8,24},{12,28},{16,0},{20,4},{24,8},{28,12},{1,17},{... | collective-permute-start | bytes 1572872 | tf_op jit(solution)/shard_map/ppermute | solution.py:376
  122.0 9.8 %collective-permute-start.21 = (bf16[256,256]{1,0:T(8,128)(2,1)S(1)}, bf16[256,256]{1,0:T(8,128)(2,1)S(1)}, u32[]{:S(2)}, u32[]{:S(2)}) collective-permute-start(bf16[256,256]{1,0:T(8,128)(2,1)S(1)} %copy-done.4), channel_id=1, source_target_pairs={{0,1},{1,0},{2,3},{3,2},{4,5},{5,4},{6,7},{7,6},{8,9},{9,8},{10,11... | collective-permute-start | bytes 393224 | tf_op jit(solution)/shard_map/ppermute | solution.py:533
  122.0 12.8 %collective-permute-start.22 = (bf16[256,256]{1,0:T(8,128)(2,1)S(1)}, bf16[256,256]{1,0:T(8,128)(2,1)S(1)}, u32[]{:S(2)}, u32[]{:S(2)}) collective-permute-start(bf16[256,256]{1,0:T(8,128)(2,1)S(1)} %copy-done.4), channel_id=1, source_target_pairs={{0,2},{1,3},{2,0},{3,1},{4,6},{5,7},{6,4},{7,5},{8,10},{9,11},{10,... | collective-permute-start | bytes 393224 | tf_op jit(solution)/shard_map/ppermute | solution.py:533
  124.7 10.1 %collective-permute-start.23 = (bf16[256,256]{1,0:T(8,128)(2,1)S(1)}, bf16[256,256]{1,0:T(8,128)(2,1)S(1)}, u32[]{:S(2)}, u32[]{:S(2)}) collective-permute-start(bf16[256,256]{1,0:T(8,128)(2,1)S(1)} %copy-done.4), channel_id=1, source_target_pairs={{0,3},{1,2},{2,1},{3,0},{4,7},{5,6},{6,5},{7,4},{8,11},{9,10},{10,... | collective-permute-start | bytes 393224 | tf_op jit(solution)/shard_map/ppermute | solution.py:533
  134.9 6.5 %collective-permute-start.25 = (bf16[1024,128]{1,0:T(8,128)(2,1)S(1)}, bf16[1024,128]{1,0:T(8,128)(2,1)S(1)}, u32[]{:S(2)}, u32[]{:S(2)}) collective-permute-start(bf16[1024,128]{1,0:T(8,128)(2,1)S(1)} %get-tuple-element.112), channel_id=1, source_target_pairs={{0,16},{4,20},{8,24},{12,28},{16,0},{20,4},{24,8},{28,12},{1,17},{... | collective-permute-start | bytes 786440 | tf_op jit(solution)/shard_map/ppermute | solution.py:376
  135.8 6.9 %collective-permute-start.26 = (bf16[1024,128]{1,0:T(8,128)(2,1)S(1)}, bf16[1024,128]{1,0:T(8,128)(2,1)S(1)}, u32[]{:S(2)}, u32[]{:S(2)}) collective-permute-start(bf16[1024,128]{1,0:T(8,128)(2,1)S(1)} %get-tuple-element.113), channel_id=1, source_target_pairs={{0,8},{4,12},{8,0},{12,4},{16,24},{20,28},{24,16},{28,20},{1,9},{5... | collective-permute-start | bytes 786440 | tf_op jit(solution)/shard_map/ppermute | solution.py:376

commit v10 on v9

--- a/solution.py
+++ b/solution.py
@@ -176,17 +176,14 @@
     ]
     for copy in others:
         copy.start()
-    chunk_copy.wait()
+    keep = pltpu.make_async_copy(turned, held.at[place[1]], sems.at[2])
+    for copy in [chunk_copy, rows_copy] + others:
+        copy.wait()
     turned[...] = chunk[...].T
-    keep = pltpu.make_async_copy(turned, held.at[place[1]], sems.at[2])
-    keep.start()
-    rows_copy.wait()
     projected = (
         total[...] + jnp.dot(chunk[...], rows[...], preferred_element_type=jnp.float32)
     ).astype(jnp.bfloat16)
     seen = allowed[...] > 0
-    for copy in others:
-        copy.wait()
     factor = 1.0 / math.sqrt(HD)
     across = (((1,), (1,)), ((), ()))
     heads = projected.shape[1] // (2 * HD)
@@ -198,7 +195,9 @@
         d_keys = jnp.zeros(keys.shape, jnp.float32)
         d_values = jnp.zeros(keys.shape, jnp.float32)
         for g in range(head * group, (head + 1) * group):
-            if g == heads * group // 2:
+            if g == heads * group // 4:
+                keep.start()
+            if g == heads * group * 3 // 4:
                 keep.wait()
                 copies = fetch_parts(order, held, range(4), buffer, part_sems)
             columns = slice(g * HD, (g + 1) * HD)
@@ -378,17 +377,16 @@
     return index % 2, (index // 2) % 2, index // 4, swap
 
 
-def weight_order(other):
+def weight_orders():
     core, x, y, _ = plane()
     chunks = [3 - x - 2 * y, 1 - x + 2 * y, x + 2 - 2 * y, x + 2 * y]
-    return jnp.stack(chunks + [1 - core if other else core])
-
-
-def weight_sum(held, d_projected, sent, kept, pieces, beside):
+    return [jnp.stack(chunks + [half]) for half in (1 - core, core)]
+
+
+def weight_sum(held, d_projected, order, sent, kept, pieces, beside):
     swap = plane()[3]
     rows, cols = held.shape[1] // 2, d_projected.shape[1]
     none = jnp.zeros((1,), jnp.int32)
-    order = weight_order(False)
     sent, kept = swap(sent, 1), swap(kept, 1)
     own = weight_parts(held, d_projected, order, SENT, [], jnp.float32, "weight_send")
     shape = jax.ShapeDtypeStruct(own[0].shape, jnp.bfloat16)
@@ -424,8 +422,8 @@
 
 
 class PlaneGather:
-    def __init__(self, own):
-        self.got = {0: own}
+    def __init__(self, own, split):
+        self.got, self.split = {0: own}, split
 
     def first(self):
         own, swap = self.got[0], plane()[3]
@@ -433,8 +431,8 @@
         return self.got
 
     def second(self):
-        got, swap, half = self.got, plane()[3], self.got[0].shape[0] // 2
-        self.far = [swap(got[4][:half], 2), swap(got[2][half:], 4)]
+        got, swap = self.got, plane()[3]
+        self.far = [swap(got[4][: self.split], 2), swap(got[2][self.split :], 4)]
         got[3], got[5] = swap(got[2], 1), swap(got[4], 1)
         return self.far, got[3], got[5]
 
@@ -497,28 +495,30 @@
 
 def input_kernel(n_blocks, place, *refs):
     *arrays, out = refs
-    pieces, rows = arrays[:n_blocks], arrays[n_blocks:]
+    pieces, here, rows = arrays[:n_blocks], arrays[n_blocks], arrays[n_blocks + 1 :]
     share = out.shape[1] // len(rows)
     for k, held in enumerate(rows):
+        start = pl.multiple_of(place[k] * share, share)
         first = held.shape[0] - n_blocks * share
         total = jnp.zeros((out.shape[0], share), jnp.float32)
         for s, piece in enumerate(pieces):
+            if s:
+                block = held[first + s * share : first + (s + 1) * share, :]
+            else:
+                block = here[pl.ds(start, share), :]
             total = total + lax.dot_general(
-                piece[...],
-                held[first + s * share : first + (s + 1) * share, :],
-                (((1,), (1,)), ((), ())),
-                preferred_element_type=jnp.float32,
-            )
-        start = pl.multiple_of(place[k] * share, share)
+                piece[...], block, (((1,), (1,)), ((), ())), preferred_element_type=jnp.float32
+            )
         out[:, pl.ds(start, share)] = total.astype(out.dtype)
 
 
-def input_gradient(pieces, arrays, place, feats):
+def input_gradient(pieces, here, arrays, place):
     length, cols = pieces[0].shape
+    feats = here.shape[0]
     (d_tokens,) = on_chip(
         functools.partial(input_kernel, len(pieces)),
         place,
-        pieces + arrays,
+        pieces + [here] + arrays,
         [jax.ShapeDtypeStruct((length, feats), jnp.bfloat16)],
         2 * length * feats * cols * len(pieces),
         "input_gradient",
@@ -547,7 +547,8 @@
         def block_for(z):
             return lax.dynamic_slice_in_dim(cached, z * feats + me_dp * share, share, 0)
 
-        blocks = [block_for(me_z)] + [pair(block_for(me_z ^ s), s) for s in range(1, n_z)]
+        blocks = [pair(block_for(me_z ^ s), s) for s in range(1, n_z)]
+        here = lax.dynamic_slice_in_dim(cached, me_z * feats, feats, 0)
 
         doc_ids = segments[0]
         position = jnp.arange(length)
@@ -556,19 +557,22 @@
 
         total = jnp.zeros((length, cols), jnp.float32)
         zero = 0 * me_z
+        orders = weight_orders() if tuned else [jnp.zeros((5,), jnp.int32)]
         total, held = absorb([tokens], zero, me_z, cached, total, None, n_z)
         if tuned:
-            gather = PlaneGather(jnp.concatenate([own_cache] + blocks, axis=0))
+            gather = PlaneGather(jnp.concatenate([own_cache] + blocks, axis=0), own_cache.shape[0])
         from_low, from_high = tokens, tokens
         for s in range(1, n_z):
             low, high = me_z - s, me_z + s
+            from_high = lax.ppermute(from_high, "tensor", [(z + 1, z) for z in range(n_z - s)])
             from_low = lax.ppermute(
                 from_low, "tensor", [(z, z + 1) for z in range(s - 1, n_z - 1)]
             )
-            from_high = lax.ppermute(from_high, "tensor", [(z + 1, z) for z in range(n_z - s)])
             if tuned:
                 if s == 1:
-                    rounds, allowed = lax.optimization_barrier((gather.got, allowed))
+                    rounds, allowed, orders, here = lax.optimization_barrier(
+                        (gather.got, allowed, orders, here)
+                    )
                 elif s == 2:
                     rounds = gather.first()
                 else:
@@ -590,9 +594,8 @@
             if s < n_z - 1:
                 total, held = absorb(chunks, which, index, cached, total, held, n_z)
 
-        order = weight_order(True) if tuned else jnp.zeros((5,), jnp.int32)
         held, d_queries, d_projected, sent, kept = attend(
-            chunks, which, index, cached, total, held, queries, d_out, allowed, order, n_z
+            chunks, which, index, cached, total, held, queries, d_out, allowed, orders[0], n_z
         )
 
         pieces = [d_projected] + [pair(d_projected, s) for s in range(1, n_z)]
@@ -600,12 +603,12 @@
             sent, gather.far_other = lax.optimization_barrier((sent, gather.third()))
             new_cache = gather.lay_far(own_cache.shape[0], laid)
             finish, pieces, new_cache = weight_sum(
-                held, d_projected, sent, kept, pieces, new_cache
-            )
-            new_grad, d_tokens = finish(input_gradient(pieces, *gather.last(), feats))
+                held, d_projected, orders[1], sent, kept, pieces, new_cache
+            )
+            new_grad, d_tokens = finish(input_gradient(pieces, here, *gather.last()))
         else:
             new_cache = lax.all_gather(own_cache, "dp", axis=0, tiled=True)
-            rows = lax.all_gather(jnp.stack(blocks), "dp", axis=0)
+            rows = lax.all_gather(jnp.stack([block_for(me_z)] + blocks), "dp", axis=0)
             d_tokens = jnp.einsum(
                 "slc,ksfc->lkf", jnp.stack(pieces), rows, preferred_element_type=jnp.float32
             )

time: 145 us -> 142 us (0.979)
  waiting for transfers between devices: 47.3 us -> 45.5 us
  Pallas kernels: 49.5 us -> 47.8 us
    ppermute x3, waiting for transfers between devices: 22.6 us -> 10.9 us  [body(): lax.ppermute(from_high, 'tensor', [(z + 1, z) for z in range(n_z - s)])]
    ppermute x15, waiting for transfers between devices: 6.01 us -> 14.4 us  [swap(): return lax.ppermute(value, 'dp', [(i, i ^ bit) for i in range(8)])]
    dynamic_slice x0 -> x1, local copies, waits for them, and re-layouts: none -> 2.27 us  [body(): here = lax.dynamic_slice_in_dim(cached, me_z * feats, feats, 0)]
    ppermute x6, waiting for transfers between devices: 18.7 us -> 20.2 us  [pair(): return lax.ppermute(value, 'tensor', [(z, z ^ s) for z in range(n_z)])]
    pallas_call x4, Pallas kernels: 6.82 us -> 5.37 us  [on_chip(): pl.pallas_call(kernel, in_specs=[pl.BlockSpec(memory_space=pltpu.SMEM)] +...]
    unnamed x15 -> x18, local copies, waits for them, and re-layouts: 4.2 us -> 3.09 us
  transfers between devices with their start and end apart: 27 -> 27, of which waited for: 10 -> 10; matrix products, arithmetic and copies ran while one was open for 6% -> 6% of each run, Pallas kernels for 34% -> 33%
where the time goes in v10:
time: 142 us
  Pallas kernels  47.8 us (34%)
  waiting for transfers between devices  45.5 us (32%)
  starting transfers between devices  35.3 us (25%)
  local copies, waits for them, and re-layouts  9.4 us (7%)
  other arithmetic  2.88 us (2%)
    ppermute x6, waiting for transfers between devices, pair(): return lax.ppermute(value, 'tensor', [(z, z ^ s) for z in range(n_z)])  20.2 us
    pallas_call x4, Pallas kernels, absorb(): pl.pallas_call(functools.partial(absorb_kernel, len(chunks)), in_specs=[p...  16.9 us
    ppermute x15, waiting for transfers between devices, swap(): return lax.ppermute(value, 'dp', [(i, i ^ bit) for i in range(8)])  14.4 us
    ppermute x15, starting transfers between devices, swap(): return lax.ppermute(value, 'dp', [(i, i ^ bit) for i in range(8)])  12.3 us
    ppermute x3, waiting for transfers between devices, body(): lax.ppermute(from_high, 'tensor', [(z + 1, z) for z in range(n_z - s)])  10.9 us
    pallas_call x1, Pallas kernels, attend(): pl.pallas_call(functools.partial(attend_kernel, len(chunks)), in_specs=[p...  10.8 us
    ppermute x6, starting transfers between devices, pair(): return lax.ppermute(value, 'tensor', [(z, z ^ s) for z in range(n_z)])  9.74 us
    ppermute x3, starting transfers between devices, body(): lax.ppermute(from_low, 'tensor', [(z, z + 1) for z in range(s - 1, n_z -...  9.19 us
  transfers between devices with their start and end apart: 27, of which 10 were waited for; matrix products, arithmetic and copies ran while one was open for 6% of the time, Pallas kernels for 33%

profile of v10, /device:TPU:0, one launch (start us, length us, event | category | flops | bytes accessed | tf_op | source)
XLA Modules:
  0.0 141.7 jit_solution(18095561160065136898)
XLA Ops:
  0.6 5.9 %collective-permute-start.3 = (bf16[256,2048]{1,0:T(8,128)(2,1)}, bf16[256,2048]{1,0:T(8,128)(2,1)}, u32[]{:S(2)}, u32[]{:S(2)}) collective-permute-start(bf16[256,2048]{1,0:T(8,128)(2,1)} %refs_0_.1), channel_id=1, source_target_pairs={{0,1},{1,2},{2,3},{4,5},{5,6},{6,7},{8,9},{9,10},{10,11},{12,13},{... | collective-permute-start | bytes 3145736 | tf_op jit(solution)/shard_map/ppermute | solution.py:568
  6.5 1.3 collective-permute-start.4
  7.9 1.1 constant_dynamic-slice_fusion.3
  8.9 4.7 %collective-permute-start.2 = (bf16[256,256]{1,0:T(8,128)(2,1)S(1)}, bf16[256,256]{1,0:T(8,128)(2,1)S(1)}, u32[]{:S(2)}, u32[]{:S(2)}) collective-permute-start(bf16[256,256]{1,0:T(8,128)(2,1)S(1)} %get-tuple-element.132), channel_id=1, source_target_pairs={{0,3},{1,2},{2,1},{3,0},{4,7},{5,6},{6,5},{7,4},{8,11},{9,10},{10,... | collective-permute-start | bytes 393224 | tf_op jit(solution)/shard_map/ppermute | solution.py:533
  14.9 4.9 %optimizer.1 = (f32[1024,256]{1,0:T(8,128)}, f32[1024,256]{1,0:T(8,128)}, f32[1024,256]{1,0:T(8,128)}, bf16[1024,256]{1,0:T(8,128)(2,1)}) custom-call(s32[1]{0:T(128)} %bitcast.place, bf16[8192,256]{1,0:T(8,128)(2,1)} %refs_3_.3, f32[1024,256]{1,0:T(8,128)} %master.1, f32[1024,256]{1,0:T(8,128)} %moment.1, f32[1024,256]{1,0:T(8,128)} %second.1, f32[1024,256]{1,0:T(8,128)} %grad.1), custom_call_target="tpu_custom_call" | custom-call | flops 10485760 | bytes 8388608 | tf_op jit(solution)/shard_map/optimizer/pallas_call | solution.py:51
  19.9 0.7 pad_add_fusion.2
  20.6 0.7 broadcast_in_dim.2.refs_1_
  21.3 4.2 %absorb.4 = (f32[256,256]{1,0:T(8,128)}, bf16[32,2048,256]{2,1,0:T(8,128)(2,1)}) custom-call(s32[3]{0:T(128)} %get-tuple-element.136.place, bf16[256,2048]{1,0:T(8,128)(2,1)} %refs_0_.1, f32[256,256]{1,0:T(8,128)} %broadcast_in_dim.2.refs_1_, bf16[8192,256]{1,0:T(8,128)(2,1)} %refs_3_.3), custom_call_target="tpu_custom_call" | custom-call | flops 268435456 | bytes 3145728 | tf_op jit(solution)/shard_map/absorb/pallas_call | solution.py:140
  25.5 2.3 %constant_dynamic-slice_fusion.refs_4_ = bf16[2048,256]{1,0:T(8,128)(2,1)} fusion(bf16[8192,256]{1,0:T(8,128)(2,1)} %refs_3_.3, s32[]{:T(128)S(6)} %select_n.59), kind=kLoop, calls=%fused_computation.4 | loop fusion | bytes 2097156 | tf_op jit(solution)/shard_map/dynamic_slice | solution.py:551
  27.8 0.8 fusion.1.refs_5_
  28.6 10.1 %collective-permute-done.2 = bf16[256,256]{1,0:T(8,128)(2,1)S(1)} collective-permute-done((bf16[256,256]{1,0:T(8,128)(2,1)S(1)}, bf16[256,256]{1,0:T(8,128)(2,1)S(1)}, u32[]{:S(2)}, u32[]{:S(2)}) %collective-permute-start.2) | collective-permute-done | bytes 131104 | tf_op jit(solution)/shard_map/ppermute | solution.py:533
  38.8 5.8 %collective-permute-done.1 = bf16[256,256]{1,0:T(8,128)(2,1)S(1)} collective-permute-done((bf16[256,256]{1,0:T(8,128)(2,1)S(1)}, bf16[256,256]{1,0:T(8,128)(2,1)S(1)}, u32[]{:S(2)}, u32[]{:S(2)}) %collective-permute-start.1) | collective-permute-done | bytes 131104 | tf_op jit(solution)/shard_map/ppermute | solution.py:533
  44.6 1.6 %collective-permute-start.5 = (bf16[256,2048]{1,0:T(8,128)(2,1)}, bf16[256,2048]{1,0:T(8,128)(2,1)}, u32[]{:S(2)}, u32[]{:S(2)}) collective-permute-start(bf16[256,2048]{1,0:T(8,128)(2,1)} %collective-permute-done.3.refs_0_), channel_id=1, source_target_pairs={{1,2},{2,3},{5,6},{6,7},{9,10},{10,11},{13,14},{14,15},{17,18},{18... | collective-permute-start | bytes 3145736 | tf_op jit(solution)/shard_map/ppermute | solution.py:568
  46.3 1.3 collective-permute-start.6
  47.6 1.6 %collective-permute-start.8 = (bf16[1792,256]{1,0:T(8,128)(2,1)S(1)}, bf16[1792,256]{1,0:T(8,128)(2,1)S(1)}, u32[]{:S(2)}, u32[]{:S(2)}) collective-permute-start(bf16[1792,256]{1,0:T(8,128)(2,1)S(1)} %pad_maximum_fusion.refs_0_.refs_5_), channel_id=1, source_target_pairs={{0,8},{4,12},{8,0},{12,4},{16,24},{20,28},{24,16},{28,20},{1,9},{5... | collective-permute-start | bytes 2752520 | tf_op jit(solution)/shard_map/ppermute | solution.py:375
  49.2 1.5 %collective-permute-start.9 = (bf16[1792,256]{1,0:T(8,128)(2,1)S(1)}, bf16[1792,256]{1,0:T(8,128)(2,1)S(1)}, u32[]{:S(2)}, u32[]{:S(2)}) collective-permute-start(bf16[1792,256]{1,0:T(8,128)(2,1)S(1)} %pad_maximum_fusion.refs_0_.refs_5_), channel_id=1, source_target_pairs={{0,16},{4,20},{8,24},{12,28},{16,0},{20,4},{24,8},{28,12},{1,17},{... | collective-permute-start | bytes 2752520 | tf_op jit(solution)/shard_map/ppermute | solution.py:375
  50.7 0.7 pad_add_fusion
  51.4 4.2 %absorb.5 = (f32[256,256]{1,0:T(8,128)}, bf16[32,2048,256]{2,1,0:T(8,128)(2,1)}) custom-call(s32[3]{0:T(128)} %get-tuple-element.134.place, bf16[256,2048]{1,0:T(8,128)(2,1)} %collective-permute-done.3.refs_0_, f32[256,256]{1,0:T(8,128)} %get-tuple-element.79.refs_1_, bf16[8192,256]{1,0:T(8,128)(2,1)} %refs_3_.3, ...), custom_call_target="tpu_custom_call", output_to_operand_aliasing={{1}: (4, {})} | custom-call | flops 268435456 | bytes 3145728 | tf_op jit(solution)/shard_map/absorb/pallas_call | solution.py:140
  55.6 4.2 %absorb.6 = (f32[256,256]{1,0:T(8,128)}, bf16[32,2048,256]{2,1,0:T(8,128)(2,1)}) custom-call(s32[3]{0:T(128)} %get-tuple-element.135.place, bf16[256,2048]{1,0:T(8,128)(2,1)} %collective-permute-done.4.refs_0_, f32[256,256]{1,0:T(8,128)} %get-tuple-element.81.refs_1_, bf16[8192,256]{1,0:T(8,128)(2,1)} %refs_3_.3, ...), custom_call_target="tpu_custom_call", output_to_operand_aliasing={{1}: (4, {})} | custom-call | flops 268435456 | bytes 3145728 | tf_op jit(solution)/shard_map/absorb/pallas_call | solution.py:140
  59.9 10.5 %collective-permute-done.8.refs_2_.refs_7_ = bf16[1792,256]{1,0:T(8,128)(2,1)S(1)} collective-permute-done((bf16[1792,256]{1,0:T(8,128)(2,1)S(1)}, bf16[1792,256]{1,0:T(8,128)(2,1)S(1)}, u32[]{:S(2)}, u32[]{:S(2)}) %collective-permute-start.8) | collective-permute-done | bytes 917536 | tf_op jit(solution)/shard_map/ppermute | solution.py:375
  70.4 1.2 collective-permute-done.9.refs_4_.refs_9_
  71.9 1.6 %collective-permute-start.10 = (bf16[256,2048]{1,0:T(8,128)(2,1)}, bf16[256,2048]{1,0:T(8,128)(2,1)}, u32[]{:S(2)}, u32[]{:S(2)}) collective-permute-start(bf16[256,2048]{1,0:T(8,128)(2,1)} %collective-permute-done.5.refs_0_), channel_id=1, source_target_pairs={{2,3},{6,7},{10,11},{14,15},{18,19},{22,23},{26,27},{30,31}} | collective-permute-start | bytes 3145736 | tf_op jit(solution)/shard_map/ppermute | solution.py:568
  73.5 1.5 %collective-permute-start.11 = (bf16[256,2048]{1,0:T(8,128)(2,1)}, bf16[256,2048]{1,0:T(8,128)(2,1)}, u32[]{:S(2)}, u32[]{:S(2)}) collective-permute-start(bf16[256,2048]{1,0:T(8,128)(2,1)} %collective-permute-done.6.refs_1_), channel_id=1, source_target_pairs={{1,0},{5,4},{9,8},{13,12},{17,16},{21,20},{25,24},{29,28}} | collective-permute-start | bytes 3145736 | tf_op jit(solution)/shard_map/ppermute | solution.py:567
  75.6 0.8 slice.6
  76.4 1.5 %collective-permute-start.12 = (bf16[1024,256]{1,0:T(8,128)(2,1)}, bf16[1024,256]{1,0:T(8,128)(2,1)S(1)}, u32[]{:S(2)}, u32[]{:S(2)}) collective-permute-start(bf16[1024,256]{1,0:T(8,128)(2,1)} %slice.6), channel_id=1, source_target_pairs={{0,8},{4,12},{8,0},{12,4},{16,24},{20,28},{24,16},{28,20},{1,9},{5... | collective-permute-start | bytes 1572872 | tf_op jit(solution)/shard_map/ppermute | solution.py:375
  77.9 0.8 slice.7
  78.7 1.0 copy-done.1
  79.7 1.5 %collective-permute-start.13 = (bf16[768,256]{1,0:T(8,128)(2,1)}, bf16[768,256]{1,0:T(8,128)(2,1)}, u32[]{:S(2)}, u32[]{:S(2)}) collective-permute-start(bf16[768,256]{1,0:T(8,128)(2,1)} %slice.7), channel_id=1, source_target_pairs={{0,16},{4,20},{8,24},{12,28},{16,0},{20,4},{24,8},{28,12},{1,17},{... | collective-permute-start | bytes 1179656 | tf_op jit(solution)/shard_map/ppermute | solution.py:375
  81.2 0.7 pad_add_fusion.4.place
  81.8 4.2 %absorb.7 = (f32[256,256]{1,0:T(8,128)}, bf16[32,2048,256]{2,1,0:T(8,128)(2,1)}) custom-call(s32[3]{0:T(128)} %pad_add_fusion.4.place, bf16[256,2048]{1,0:T(8,128)(2,1)} %collective-permute-done.5.refs_0_, bf16[256,2048]{1,0:T(8,128)(2,1)} %collective-permute-done.6.refs_1_, f32[256,256]{1,0:T(8,128)} %get-tuple-element.87.refs_2_, ...), custom_call_target="tpu_custom_call", output_to_operand_aliasing={{1}: (5, {})} | custom-call | flops 268435456 | bytes 3145728 | tf_op jit(solution)/shard_map/absorb/pallas_call | solution.py:140
  86.1 1.2 copy-done.2
  87.2 3.2 %place_rows.2.refs_2_ = bf16[8192,256]{1,0:T(8,128)(2,1)} custom-call(s32[6]{0:T(128)S(1)} %iota_xor_fusion.1.place, bf16[1792,256]{1,0:T(8,128)(2,1)S(1)} %pad_maximum_fusion.refs_0_.refs_5_, bf16[1792,256]{1,0:T(8,128)(2,1)} %collective-permute-done.7.refs_1_.refs_6_, bf16[1792,256]{1,0:T(8,128)(2,1)S(1)} %collective-permute-done.8.refs_2_.refs_7_, ...), custom_call_target="tpu_custom_call" | custom-call | bytes 6291456 | tf_op jit(solution)/shard_map/place_rows/pallas_call | solution.py:479
  90.7 10.6 %collective-permute-done.11.refs_1_ = bf16[256,2048]{1,0:T(8,128)(2,1)} collective-permute-done((bf16[256,2048]{1,0:T(8,128)(2,1)}, bf16[256,2048]{1,0:T(8,128)(2,1)}, u32[]{:S(2)}, u32[]{:S(2)}) %collective-permute-start.11) | collective-permute-done | bytes 1048608 | tf_op jit(solution)/shard_map/ppermute | solution.py:567
  101.8 10.8 %attend.1 = (bf16[32,2048,256]{2,1,0:T(8,128)(2,1)}, bf16[256,1024]{1,0:T(8,128)(2,1)}, bf16[256,256]{1,0:T(8,128)(2,1)}, bf16[4,1024,128]{2,1,0:T(8,128)(2,1)}, bf16[4,1024,128]{2,1,0:T(8,128)(2,1)}) custom-call(s32[3]{0:T(128)} %get-tuple-element.137.place, s32[5]{0:T(128)} %stack.90.order, ...), custom_call_target="tpu_custom_call", output_to_operand_aliasing={{0}: (6, {})} | custom-call | flops 805306368 | bytes 2097152 | tf_op jit(solution)/shard_map/attend/pallas_call | solution.py:234
  113.3 0.9 copy-done.4
  114.2 2.5 %weight_send.1 = (f32[2,1024,128]{2,1,0:T(8,128)S(1)}, f32[2,1024,128]{2,1,0:T(8,128)S(1)}) custom-call(s32[5]{0:T(128)S(1)} %stack.92.place, bf16[32,2048,256]{2,1,0:T(8,128)(2,1)} %get-tuple-element.99.held, bf16[256,256]{1,0:T(8,128)(2,1)S(1)} %copy-done.4), custom_call_target="tpu_custom_call" | custom-call | flops 268435456 | bytes 2097152 | tf_op jit(solution)/shard_map/weight_send/pallas_call | solution.py:333
  116.9 1.5 %collective-permute-start.19 = (bf16[2,1024,128]{2,1,0:T(8,128)(2,1)S(1)}, bf16[2,1024,128]{2,1,0:T(8,128)(2,1)S(1)}, u32[]{:S(2)}, u32[]{:S(2)}) collective-permute-start(bf16[2,1024,128]{2,1,0:T(8,128)(2,1)S(1)} %get-tuple-element.107), channel_id=1, source_target_pairs={{0,8},{4,12},{8,0},{12,4},{16,24},{20,28},{24,16},{28,20},{1,9},{5... | collective-permute-start | bytes 1572872 | tf_op jit(solution)/shard_map/ppermute | solution.py:375
  118.4 1.5 %collective-permute-start.20 = (bf16[2,1024,128]{2,1,0:T(8,128)(2,1)S(1)}, bf16[2,1024,128]{2,1,0:T(8,128)(2,1)S(1)}, u32[]{:S(2)}, u32[]{:S(2)}) collective-permute-start(bf16[2,1024,128]{2,1,0:T(8,128)(2,1)S(1)} %get-tuple-element.108), channel_id=1, source_target_pairs={{0,16},{4,20},{8,24},{12,28},{16,0},{20,4},{24,8},{28,12},{1,17},{... | collective-permute-start | bytes 1572872 | tf_op jit(solution)/shard_map/ppermute | solution.py:375
  119.9 1.2 collective-permute-start.22
  121.1 3.2 %collective-permute-start.23 = (bf16[256,256]{1,0:T(8,128)(2,1)S(1)}, bf16[256,256]{1,0:T(8,128)(2,1)S(1)}, u32[]{:S(2)}, u32[]{:S(2)}) collective-permute-start(bf16[256,256]{1,0:T(8,128)(2,1)S(1)} %copy-done.5), channel_id=1, source_target_pairs={{0,3},{1,2},{2,1},{3,0},{4,7},{5,6},{6,5},{7,4},{8,11},{9,10},{10,... | collective-permute-start | bytes 393224 | tf_op jit(solution)/shard_map/ppermute | solution.py:533
  124.3 1.5 %place_rows.3 = bf16[8192,256]{1,0:T(8,128)(2,1)} custom-call(s32[2]{0:T(128)S(1)} %broadcast_xor_fusion.place, bf16[1024,256]{1,0:T(8,128)(2,1)S(1)} %collective-permute-done.12.refs_0_, bf16[1024,256]{1,0:T(8,128)(2,1)S(1)} %collective-permute-done.16.refs_1_, bf16[8192,256]{1,0:T(8,128)(2,1)} %place_rows.2.refs_2_), custom_call_target="tpu_custom_call", output_to_operand_aliasing={{}: (3, {})} | custom-call | bytes 2097152 | tf_op jit(solution)/shard_map/place_rows/pallas_call | solution.py:479
  125.9 2.5 %weight_keep.1 = (f32[2,1024,128]{2,1,0:T(8,128)S(1)}, f32[2,1024,128]{2,1,0:T(8,128)S(1)}) custom-call(s32[5]{0:T(128)S(1)} %stack.92.place, bf16[32,2048,256]{2,1,0:T(8,128)(2,1)} %get-tuple-element.99.held, bf16[256,256]{1,0:T(8,128)(2,1)S(1)} %copy-done.5, bf16[4,1024,128]{2,1,0:T(8,128)(2,1)S(1)} %collective-permute-done.24.refs_0_), custom_call_target="tpu_custom_call" | custom-call | flops 268435456 | bytes 2097152 | tf_op jit(solution)/shard_map/weight_keep/pallas_call | solution.py:333
  128.4 4.3 %collective-permute-done.22.refs_2_ = bf16[256,256]{1,0:T(8,128)(2,1)S(1)} collective-permute-done((bf16[256,256]{1,0:T(8,128)(2,1)S(1)}, bf16[256,256]{1,0:T(8,128)(2,1)S(1)}, u32[]{:S(2)}, u32[]{:S(2)}) %collective-permute-start.22) | collective-permute-done | bytes 131104 | tf_op jit(solution)/shard_map/ppermute | solution.py:533
  132.8 0.9 collective-permute-start.25
  134.3 4.0 %input_gradient.1 = bf16[256,2048]{1,0:T(8,128)(2,1)} custom-call(s32[8]{0:T(128)S(1)} %iota_xor_fusion.place, bf16[256,256]{1,0:T(8,128)(2,1)S(1)} %copy-done.5, bf16[256,256]{1,0:T(8,128)(2,1)S(1)} %collective-permute-done.21.refs_1_, bf16[256,256]{1,0:T(8,128)(2,1)S(1)} %collective-permute-done.22.refs_2_, ...), custom_call_target="tpu_custom_call" | custom-call | flops 1073741824 | bytes 8912896 | tf_op jit(solution)/shard_map/input_gradient/pallas_call | solution.py:73
  138.3 1.1 collective-permute-done.25.last_a
  139.4 1.2 collective-permute-done.26.last_b
  140.6 1.1 weight_finish.1
  (53 shorter events, 4.5 us)
Async XLA Ops:
  0.6 44.0 %collective-permute-start.3 = (bf16[256,2048]{1,0:T(8,128)(2,1)}, bf16[256,2048]{1,0:T(8,128)(2,1)}, u32[]{:S(2)}, u32[]{:S(2)}) collective-permute-start(bf16[256,2048]{1,0:T(8,128)(2,1)} %refs_0_.1), channel_id=1, source_target_pairs={{0,1},{1,2},{2,3},{4,5},{5,6},{6,7},{8,9},{9,10},{10,11},{12,13},{... | collective-permute-start | bytes 3145736 | tf_op jit(solution)/shard_map/ppermute | solution.py:568
  6.5 38.1 %collective-permute-start.4 = (bf16[256,2048]{1,0:T(8,128)(2,1)}, bf16[256,2048]{1,0:T(8,128)(2,1)}, u32[]{:S(2)}, u32[]{:S(2)}) collective-permute-start(bf16[256,2048]{1,0:T(8,128)(2,1)} %refs_0_.1), channel_id=1, source_target_pairs={{1,0},{2,1},{3,2},{5,4},{6,5},{7,6},{9,8},{10,9},{11,10},{13,12},{... | collective-permute-start | bytes 3145736 | tf_op jit(solution)/shard_map/ppermute | solution.py:567
  8.9 29.8 %collective-permute-start.2 = (bf16[256,256]{1,0:T(8,128)(2,1)S(1)}, bf16[256,256]{1,0:T(8,128)(2,1)S(1)}, u32[]{:S(2)}, u32[]{:S(2)}) collective-permute-start(bf16[256,256]{1,0:T(8,128)(2,1)S(1)} %get-tuple-element.132), channel_id=1, source_target_pairs={{0,3},{1,2},{2,1},{3,0},{4,7},{5,6},{6,5},{7,4},{8,11},{9,10},{10,... | collective-permute-start | bytes 393224 | tf_op jit(solution)/shard_map/ppermute | solution.py:533
  13.6 30.9 %collective-permute-start.1 = (bf16[256,256]{1,0:T(8,128)(2,1)S(1)}, bf16[256,256]{1,0:T(8,128)(2,1)S(1)}, u32[]{:S(2)}, u32[]{:S(2)}) collective-permute-start(bf16[256,256]{1,0:T(8,128)(2,1)S(1)} %get-tuple-element.133), channel_id=1, source_target_pairs={{0,2},{1,3},{2,0},{3,1},{4,6},{5,7},{6,4},{7,5},{8,10},{9,11},{10,... | collective-permute-start | bytes 393224 | tf_op jit(solution)/shard_map/ppermute | solution.py:533
  13.6 30.9 %collective-permute-start = (bf16[256,256]{1,0:T(8,128)(2,1)S(1)}, bf16[256,256]{1,0:T(8,128)(2,1)S(1)}, u32[]{:S(2)}, u32[]{:S(2)}) collective-permute-start(bf16[256,256]{1,0:T(8,128)(2,1)S(1)} %get-tuple-element.131), channel_id=1, source_target_pairs={{0,1},{1,0},{2,3},{3,2},{4,5},{5,4},{6,7},{7,6},{8,9},{9,8},{10,11... | collective-permute-start | bytes 393224 | tf_op jit(solution)/shard_map/ppermute | solution.py:533
  19.9 7.9 %copy-start.7 = (s32[1,256]{1,0:T(1,128)S(1)}, s32[1,256]{1,0:T(1,128)}, u32[]{:S(2)}) copy-start(s32[1,256]{1,0:T(1,128)} %param.15) | copy-start | bytes 3076
  19.9 24.7 %copy-start.6 = (bf16[1024,256]{1,0:T(8,128)(2,1)S(1)}, bf16[1024,256]{1,0:T(8,128)(2,1)}, u32[]{:S(2)}) copy-start(bf16[1024,256]{1,0:T(8,128)(2,1)} %get-tuple-element.72) | copy-start | bytes 1572868
  44.6 27.0 %collective-permute-start.5 = (bf16[256,2048]{1,0:T(8,128)(2,1)}, bf16[256,2048]{1,0:T(8,128)(2,1)}, u32[]{:S(2)}, u32[]{:S(2)}) collective-permute-start(bf16[256,2048]{1,0:T(8,128)(2,1)} %collective-permute-done.3.refs_0_), channel_id=1, source_target_pairs={{1,2},{2,3},{5,6},{6,7},{9,10},{10,11},{13,14},{14,15},{17,18},{18... | collective-permute-start | bytes 3145736 | tf_op jit(solution)/shard_map/ppermute | solution.py:568
  46.3 25.6 %collective-permute-start.6 = (bf16[256,2048]{1,0:T(8,128)(2,1)}, bf16[256,2048]{1,0:T(8,128)(2,1)}, u32[]{:S(2)}, u32[]{:S(2)}) collective-permute-start(bf16[256,2048]{1,0:T(8,128)(2,1)} %collective-permute-done.4.refs_0_), channel_id=1, source_target_pairs={{1,0},{2,1},{5,4},{6,5},{9,8},{10,9},{13,12},{14,13},{17,16},{18,1... | collective-permute-start | bytes 3145736 | tf_op jit(solution)/shard_map/ppermute | solution.py:567
  47.6 12.3 %collective-permute-start.7 = (bf16[1792,256]{1,0:T(8,128)(2,1)S(1)}, bf16[1792,256]{1,0:T(8,128)(2,1)}, u32[]{:S(2)}, u32[]{:S(2)}) collective-permute-start(bf16[1792,256]{1,0:T(8,128)(2,1)S(1)} %pad_maximum_fusion.refs_0_.refs_5_), channel_id=1, source_target_pairs={{0,4},{4,0},{8,12},{12,8},{16,20},{20,16},{24,28},{28,24},{1,5},{5... | collective-permute-start | bytes 2752520 | tf_op jit(solution)/shard_map/ppermute | solution.py:375
  47.6 22.8 %collective-permute-start.8 = (bf16[1792,256]{1,0:T(8,128)(2,1)S(1)}, bf16[1792,256]{1,0:T(8,128)(2,1)S(1)}, u32[]{:S(2)}, u32[]{:S(2)}) collective-permute-start(bf16[1792,256]{1,0:T(8,128)(2,1)S(1)} %pad_maximum_fusion.refs_0_.refs_5_), channel_id=1, source_target_pairs={{0,8},{4,12},{8,0},{12,4},{16,24},{20,28},{24,16},{28,20},{1,9},{5... | collective-permute-start | bytes 2752520 | tf_op jit(solution)/shard_map/ppermute | solution.py:375
  49.2 22.4 %collective-permute-start.9 = (bf16[1792,256]{1,0:T(8,128)(2,1)S(1)}, bf16[1792,256]{1,0:T(8,128)(2,1)S(1)}, u32[]{:S(2)}, u32[]{:S(2)}) collective-permute-start(bf16[1792,256]{1,0:T(8,128)(2,1)S(1)} %pad_maximum_fusion.refs_0_.refs_5_), channel_id=1, source_target_pairs={{0,16},{4,20},{8,24},{12,28},{16,0},{20,4},{24,8},{28,12},{1,17},{... | collective-permute-start | bytes 2752520 | tf_op jit(solution)/shard_map/ppermute | solution.py:375
  71.9 6.8 %collective-permute-start.14 = (bf16[1792,256]{1,0:T(8,128)(2,1)S(1)}, bf16[1792,256]{1,0:T(8,128)(2,1)S(1)}, u32[]{:S(2)}, u32[]{:S(2)}) collective-permute-start(bf16[1792,256]{1,0:T(8,128)(2,1)S(1)} %collective-permute-done.8.refs_2_.refs_7_), channel_id=1, source_target_pairs={{0,4},{4,0},{8,12},{12,8},{16,20},{20,16},{24,28},{28,24},{1,5},{5... | collective-permute-start | bytes 2752520 | tf_op jit(solution)/shard_map/ppermute | solution.py:375
  71.9 18.8 %collective-permute-start.10 = (bf16[256,2048]{1,0:T(8,128)(2,1)}, bf16[256,2048]{1,0:T(8,128)(2,1)}, u32[]{:S(2)}, u32[]{:S(2)}) collective-permute-start(bf16[256,2048]{1,0:T(8,128)(2,1)} %collective-permute-done.5.refs_0_), channel_id=1, source_target_pairs={{2,3},{6,7},{10,11},{14,15},{18,19},{22,23},{26,27},{30,31}} | collective-permute-start | bytes 3145736 | tf_op jit(solution)/shard_map/ppermute | solution.py:568
  73.5 27.8 %collective-permute-start.11 = (bf16[256,2048]{1,0:T(8,128)(2,1)}, bf16[256,2048]{1,0:T(8,128)(2,1)}, u32[]{:S(2)}, u32[]{:S(2)}) collective-permute-start(bf16[256,2048]{1,0:T(8,128)(2,1)} %collective-permute-done.6.refs_1_), channel_id=1, source_target_pairs={{1,0},{5,4},{9,8},{13,12},{17,16},{21,20},{25,24},{29,28}} | collective-permute-start | bytes 3145736 | tf_op jit(solution)/shard_map/ppermute | solution.py:567
  75.0 11.1 %collective-permute-start.15 = (bf16[1792,256]{1,0:T(8,128)(2,1)S(1)}, bf16[1792,256]{1,0:T(8,128)(2,1)}, u32[]{:S(2)}, u32[]{:S(2)}) collective-permute-start(bf16[1792,256]{1,0:T(8,128)(2,1)S(1)} %collective-permute-done.9.refs_4_.refs_9_), channel_id=1, source_target_pairs={{0,4},{4,0},{8,12},{12,8},{16,20},{20,16},{24,28},{28,24},{1,5},{5... | collective-permute-start | bytes 2752520 | tf_op jit(solution)/shard_map/ppermute | solution.py:375
  76.4 14.3 %collective-permute-start.12 = (bf16[1024,256]{1,0:T(8,128)(2,1)}, bf16[1024,256]{1,0:T(8,128)(2,1)S(1)}, u32[]{:S(2)}, u32[]{:S(2)}) collective-permute-start(bf16[1024,256]{1,0:T(8,128)(2,1)} %slice.6), channel_id=1, source_target_pairs={{0,8},{4,12},{8,0},{12,4},{16,24},{20,28},{24,16},{28,20},{1,9},{5... | collective-permute-start | bytes 1572872 | tf_op jit(solution)/shard_map/ppermute | solution.py:375
  78.7 1.0 copy-start.1
  79.7 11.1 %collective-permute-start.13 = (bf16[768,256]{1,0:T(8,128)(2,1)}, bf16[768,256]{1,0:T(8,128)(2,1)}, u32[]{:S(2)}, u32[]{:S(2)}) collective-permute-start(bf16[768,256]{1,0:T(8,128)(2,1)} %slice.7), channel_id=1, source_target_pairs={{0,16},{4,20},{8,24},{12,28},{16,0},{20,4},{24,8},{28,12},{1,17},{... | collective-permute-start | bytes 1179656 | tf_op jit(solution)/shard_map/ppermute | solution.py:375
  86.1 1.2 copy-start.2
  101.3 11.4 %collective-permute-start.16 = (bf16[1024,256]{1,0:T(8,128)(2,1)S(1)}, bf16[1024,256]{1,0:T(8,128)(2,1)S(1)}, u32[]{:S(2)}, u32[]{:S(2)}) collective-permute-start(bf16[1024,256]{1,0:T(8,128)(2,1)S(1)} %collective-permute-done.12.refs_0_), channel_id=1, source_target_pairs={{0,4},{4,0},{8,12},{12,8},{16,20},{20,16},{24,28},{28,24},{1,5},{5... | collective-permute-start | bytes 1572872 | tf_op jit(solution)/shard_map/ppermute | solution.py:375
  101.3 11.4 %collective-permute-start.17 = (bf16[768,256]{1,0:T(8,128)(2,1)}, bf16[768,256]{1,0:T(8,128)(2,1)}, u32[]{:S(2)}, u32[]{:S(2)}) collective-permute-start(bf16[768,256]{1,0:T(8,128)(2,1)} %collective-permute-done.13.refs_11_), channel_id=1, source_target_pairs={{0,4},{4,0},{8,12},{12,8},{16,20},{20,16},{24,28},{28,24},{1,5},{5... | collective-permute-start | bytes 1179656 | tf_op jit(solution)/shard_map/ppermute | solution.py:375
  112.7 4.0 %collective-permute-start.18 = (bf16[4,1024,128]{2,1,0:T(8,128)(2,1)}, bf16[4,1024,128]{2,1,0:T(8,128)(2,1)S(1)}, u32[]{:S(2)}, u32[]{:S(2)}) collective-permute-start(bf16[4,1024,128]{2,1,0:T(8,128)(2,1)} %get-tuple-element.106), channel_id=1, source_target_pairs={{0,4},{4,0},{8,12},{12,8},{16,20},{20,16},{24,28},{28,24},{1,5},{5... | collective-permute-start | bytes 3145736 | tf_op jit(solution)/shard_map/ppermute | solution.py:375
  112.8 8.3 %collective-permute-start.24 = (bf16[4,1024,128]{2,1,0:T(8,128)(2,1)}, bf16[4,1024,128]{2,1,0:T(8,128)(2,1)S(1)}, u32[]{:S(2)}, u32[]{:S(2)}) collective-permute-start(bf16[4,1024,128]{2,1,0:T(8,128)(2,1)} %get-tuple-element.112), channel_id=1, source_target_pairs={{0,4},{4,0},{8,12},{12,8},{16,20},{20,16},{24,28},{28,24},{1,5},{5... | collective-permute-start | bytes 3145736 | tf_op jit(solution)/shard_map/ppermute | solution.py:375
  113.3 0.9 copy-start.4
  114.2 5.7 %copy-start.5 = (bf16[256,256]{1,0:T(8,128)(2,1)S(1)}, bf16[256,256]{1,0:T(8,128)(2,1)}, u32[]{:S(2)}) copy-start(bf16[256,256]{1,0:T(8,128)(2,1)} %get-tuple-element.119.d_projected.refs_0_) | copy-start | bytes 393220
  114.2 10.1 %copy-start.8 = (s32[2]{0:T(128)S(1)}, s32[2]{0:T(128)}, u32[]{:S(2)}) copy-start(s32[2]{0:T(128)} %constant.72.clone) | copy-start | bytes 28
  116.9 15.9 %collective-permute-start.19 = (bf16[2,1024,128]{2,1,0:T(8,128)(2,1)S(1)}, bf16[2,1024,128]{2,1,0:T(8,128)(2,1)S(1)}, u32[]{:S(2)}, u32[]{:S(2)}) collective-permute-start(bf16[2,1024,128]{2,1,0:T(8,128)(2,1)S(1)} %get-tuple-element.107), channel_id=1, source_target_pairs={{0,8},{4,12},{8,0},{12,4},{16,24},{20,28},{24,16},{28,20},{1,9},{5... | collective-permute-start | bytes 1572872 | tf_op jit(solution)/shard_map/ppermute | solution.py:375
  118.4 14.3 %collective-permute-start.20 = (bf16[2,1024,128]{2,1,0:T(8,128)(2,1)S(1)}, bf16[2,1024,128]{2,1,0:T(8,128)(2,1)S(1)}, u32[]{:S(2)}, u32[]{:S(2)}) collective-permute-start(bf16[2,1024,128]{2,1,0:T(8,128)(2,1)S(1)} %get-tuple-element.108), channel_id=1, source_target_pairs={{0,16},{4,20},{8,24},{12,28},{16,0},{20,4},{24,8},{28,12},{1,17},{... | collective-permute-start | bytes 1572872 | tf_op jit(solution)/shard_map/ppermute | solution.py:375
  119.9 8.5 %collective-permute-start.21 = (bf16[256,256]{1,0:T(8,128)(2,1)S(1)}, bf16[256,256]{1,0:T(8,128)(2,1)S(1)}, u32[]{:S(2)}, u32[]{:S(2)}) collective-permute-start(bf16[256,256]{1,0:T(8,128)(2,1)S(1)} %copy-done.5), channel_id=1, source_target_pairs={{0,1},{1,0},{2,3},{3,2},{4,5},{5,4},{6,7},{7,6},{8,9},{9,8},{10,11... | collective-permute-start | bytes 393224 | tf_op jit(solution)/shard_map/ppermute | solution.py:533
  119.9 12.8 %collective-permute-start.22 = (bf16[256,256]{1,0:T(8,128)(2,1)S(1)}, bf16[256,256]{1,0:T(8,128)(2,1)S(1)}, u32[]{:S(2)}, u32[]{:S(2)}) collective-permute-start(bf16[256,256]{1,0:T(8,128)(2,1)S(1)} %copy-done.5), channel_id=1, source_target_pairs={{0,2},{1,3},{2,0},{3,1},{4,6},{5,7},{6,4},{7,5},{8,10},{9,11},{10,... | collective-permute-start | bytes 393224 | tf_op jit(solution)/shard_map/ppermute | solution.py:533
  121.1 11.6 %collective-permute-start.23 = (bf16[256,256]{1,0:T(8,128)(2,1)S(1)}, bf16[256,256]{1,0:T(8,128)(2,1)S(1)}, u32[]{:S(2)}, u32[]{:S(2)}) collective-permute-start(bf16[256,256]{1,0:T(8,128)(2,1)S(1)} %copy-done.5), channel_id=1, source_target_pairs={{0,3},{1,2},{2,1},{3,0},{4,7},{5,6},{6,5},{7,4},{8,11},{9,10},{10,... | collective-permute-start | bytes 393224 | tf_op jit(solution)/shard_map/ppermute | solution.py:533
  125.9 8.4 %copy-start = (bf16[2048,256]{1,0:T(8,128)(2,1)S(1)}, bf16[2048,256]{1,0:T(8,128)(2,1)}, u32[]{:S(2)}) copy-start(bf16[2048,256]{1,0:T(8,128)(2,1)} %constant_dynamic-slice_fusion.refs_4_) | copy-start | bytes 3145732
  125.9 8.4 %copy-start.3 = (bf16[1792,256]{1,0:T(8,128)(2,1)S(1)}, bf16[1792,256]{1,0:T(8,128)(2,1)}, u32[]{:S(2)}) copy-start(bf16[1792,256]{1,0:T(8,128)(2,1)} %copy-done.1) | copy-start | bytes 2752516
  132.8 6.5 %collective-permute-start.25 = (bf16[1024,128]{1,0:T(8,128)(2,1)S(1)}, bf16[1024,128]{1,0:T(8,128)(2,1)S(1)}, u32[]{:S(2)}, u32[]{:S(2)}) collective-permute-start(bf16[1024,128]{1,0:T(8,128)(2,1)S(1)} %get-tuple-element.117), channel_id=1, source_target_pairs={{0,16},{4,20},{8,24},{12,28},{16,0},{20,4},{24,8},{28,12},{1,17},{... | collective-permute-start | bytes 786440 | tf_op jit(solution)/shard_map/ppermute | solution.py:375
  133.7 6.9 %collective-permute-start.26 = (bf16[1024,128]{1,0:T(8,128)(2,1)S(1)}, bf16[1024,128]{1,0:T(8,128)(2,1)S(1)}, u32[]{:S(2)}, u32[]{:S(2)}) collective-permute-start(bf16[1024,128]{1,0:T(8,128)(2,1)S(1)} %get-tuple-element.118), channel_id=1, source_target_pairs={{0,8},{4,12},{8,0},{12,4},{16,24},{20,28},{24,16},{28,20},{1,9},{5... | collective-permute-start | bytes 786440 | tf_op jit(solution)/shard_map/ppermute | solution.py:375

commit v11 on v10

--- a/solution.py
+++ b/solution.py
@@ -176,14 +176,17 @@
     ]
     for copy in others:
         copy.start()
+    chunk_copy.wait()
+    turned[...] = chunk[...].T
     keep = pltpu.make_async_copy(turned, held.at[place[1]], sems.at[2])
-    for copy in [chunk_copy, rows_copy] + others:
-        copy.wait()
-    turned[...] = chunk[...].T
+    keep.start()
+    rows_copy.wait()
     projected = (
         total[...] + jnp.dot(chunk[...], rows[...], preferred_element_type=jnp.float32)
     ).astype(jnp.bfloat16)
     seen = allowed[...] > 0
+    for copy in others:
+        copy.wait()
     factor = 1.0 / math.sqrt(HD)
     across = (((1,), (1,)), ((), ()))
     heads = projected.shape[1] // (2 * HD)
@@ -195,9 +198,7 @@
         d_keys = jnp.zeros(keys.shape, jnp.float32)
         d_values = jnp.zeros(keys.shape, jnp.float32)
         for g in range(head * group, (head + 1) * group):
-            if g == heads * group // 4:
-                keep.start()
-            if g == heads * group * 3 // 4:
+            if g == heads * group // 2:
                 keep.wait()
                 copies = fetch_parts(order, held, range(4), buffer, part_sems)
             columns = slice(g * HD, (g + 1) * HD)
@@ -570,21 +571,23 @@
             )
             if tuned:
                 if s == 1:
-                    rounds, allowed, orders, here = lax.optimization_barrier(
-                        (gather.got, allowed, orders, here)
+                    held, allowed, orders, here = lax.optimization_barrier(
+                        (held, allowed, orders, here)
                     )
+                    rounds = None
                 elif s == 2:
                     rounds = gather.first()
                 else:
                     rounds = gather.second()
                     laid = gather.lay(own_cache.shape[0], cached.shape[0])
                     rounds = (rounds, laid)
-                from_low, from_high, held, rounds = lax.optimization_barrier(
-                    (from_low, from_high, held, rounds)
-                )
-                if s < 3:
+                if s > 1:
+                    from_low, from_high, held, rounds = lax.optimization_barrier(
+                        (from_low, from_high, held, rounds)
+                    )
+                if s == 2:
                     gather.got = rounds
-                else:
+                if s == 3:
                     (gather.far, gather.got[3], gather.got[5]), laid = rounds
             chunks, which = [from_low, from_high], (me_z < s).astype(jnp.int32)
             index = jnp.where(me_z < s, high, low)

time: 142 us -> 136 us (0.958)
  waiting for transfers between devices: 45.5 us -> 39 us
    ppermute x15, waiting for transfers between devices: 14.4 us -> 3.57 us  [swap(): return lax.ppermute(value, 'dp', [(i, i ^ bit) for i in range(8)])]
    ppermute x6, waiting for transfers between devices: 20.2 us -> 24.3 us  [pair(): return lax.ppermute(value, 'tensor', [(z, z ^ s) for z in range(n_z)])]
    unnamed x18 -> x17, local copies, waits for them, and re-layouts: 3.09 us -> 4.17 us
  transfers between devices with their start and end apart: 27 -> 27, of which waited for: 10 -> 9; matrix products, arithmetic and copies ran while one was open for 6% -> 8% of each run, Pallas kernels for 33% -> 34%
where the time goes in v11:
time: 136 us; the launch traced here: 135 us
  Pallas kernels  46.6 us (34%)
  waiting for transfers between devices  39 us (29%)
  starting transfers between devices  34.2 us (25%)
  local copies, waits for them, and re-layouts  10.6 us (8%)
  other arithmetic  3.97 us (3%)
    ppermute x6, waiting for transfers between devices, pair(): return lax.ppermute(value, 'tensor', [(z, z ^ s) for z in range(n_z)])  24.3 us
    pallas_call x4, Pallas kernels, absorb(): pl.pallas_call(functools.partial(absorb_kernel, len(chunks)), in_specs=[p...  16.9 us
    ppermute x15, starting transfers between devices, swap(): return lax.ppermute(value, 'dp', [(i, i ^ bit) for i in range(8)])  11.3 us
    ppermute x3, waiting for transfers between devices, body(): lax.ppermute(from_high, 'tensor', [(z + 1, z) for z in range(n_z - s)])  11.1 us
    pallas_call x1, Pallas kernels, attend(): pl.pallas_call(functools.partial(attend_kernel, len(chunks)), in_specs=[p...  9.74 us
    ppermute x6, starting transfers between devices, pair(): return lax.ppermute(value, 'tensor', [(z, z ^ s) for z in range(n_z)])  9.69 us
    ppermute x3, starting transfers between devices, body(): lax.ppermute(from_low, 'tensor', [(z, z + 1) for z in range(s - 1, n_z -...  9.21 us
    pallas_call x4, Pallas kernels, on_chip(): pl.pallas_call(kernel, in_specs=[pl.BlockSpec(memory_space=pltpu.SMEM)] +...  5.36 us
  transfers between devices with their start and end apart: 27, of which 9 were waited for; matrix products, arithmetic and copies ran while one was open for 8% of the time, Pallas kernels for 34%

profile of v11, /device:TPU:0, one launch (start us, length us, event | category | flops | bytes accessed | tf_op | source)
XLA Modules:
  0.0 135.3 jit_solution(7508125610677932221)
XLA Ops:
  0.6 5.9 %collective-permute-start = (bf16[256,2048]{1,0:T(8,128)(2,1)}, bf16[256,2048]{1,0:T(8,128)(2,1)}, u32[]{:S(2)}, u32[]{:S(2)}) collective-permute-start(bf16[256,2048]{1,0:T(8,128)(2,1)} %refs_0_.1), channel_id=1, source_target_pairs={{0,1},{1,2},{2,3},{4,5},{5,6},{6,7},{8,9},{9,10},{10,11},{12,13},{... | collective-permute-start | bytes 3145736 | tf_op jit(solution)/shard_map/ppermute | solution.py:569
  6.5 1.3 collective-permute-start.2
  7.9 1.1 constant_dynamic-slice_fusion
  8.9 2.7 %collective-permute-start.4 = (bf16[256,256]{1,0:T(8,128)(2,1)S(1)}, bf16[256,256]{1,0:T(8,128)(2,1)S(1)}, u32[]{:S(2)}, u32[]{:S(2)}) collective-permute-start(bf16[256,256]{1,0:T(8,128)(2,1)S(1)} %get-tuple-element.125), channel_id=1, source_target_pairs={{0,1},{1,0},{2,3},{3,2},{4,5},{5,4},{6,7},{7,6},{8,9},{9,8},{10,11... | collective-permute-start | bytes 393224 | tf_op jit(solution)/shard_map/ppermute | solution.py:534
  11.6 2.6 %collective-permute-start.5 = (bf16[256,256]{1,0:T(8,128)(2,1)S(1)}, bf16[256,256]{1,0:T(8,128)(2,1)S(1)}, u32[]{:S(2)}, u32[]{:S(2)}) collective-permute-start(bf16[256,256]{1,0:T(8,128)(2,1)S(1)} %get-tuple-element.124), channel_id=1, source_target_pairs={{0,2},{1,3},{2,0},{3,1},{4,6},{5,7},{6,4},{7,5},{8,10},{9,11},{10,... | collective-permute-start | bytes 393224 | tf_op jit(solution)/shard_map/ppermute | solution.py:534
  14.2 4.9 %optimizer.1 = (f32[1024,256]{1,0:T(8,128)}, f32[1024,256]{1,0:T(8,128)}, f32[1024,256]{1,0:T(8,128)}, bf16[1024,256]{1,0:T(8,128)(2,1)}) custom-call(s32[1]{0:T(128)} %bitcast.place, bf16[8192,256]{1,0:T(8,128)(2,1)} %refs_3_.3, f32[1024,256]{1,0:T(8,128)} %master.1, f32[1024,256]{1,0:T(8,128)} %moment.1, f32[1024,256]{1,0:T(8,128)} %second.1, f32[1024,256]{1,0:T(8,128)} %grad.1), custom_call_target="tpu_custom_call" | custom-call | flops 10485760 | bytes 8388608 | tf_op jit(solution)/shard_map/optimizer/pallas_call | solution.py:51
  19.2 1.1 constant_dynamic-update-slice_fusion.3
  20.2 18.6 %collective-permute-done.4 = bf16[256,256]{1,0:T(8,128)(2,1)S(1)} collective-permute-done((bf16[256,256]{1,0:T(8,128)(2,1)S(1)}, bf16[256,256]{1,0:T(8,128)(2,1)S(1)}, u32[]{:S(2)}, u32[]{:S(2)}) %collective-permute-start.4) | collective-permute-done | bytes 131104 | tf_op jit(solution)/shard_map/ppermute | solution.py:534
  38.8 1.7 %collective-permute-start.1 = (bf16[256,2048]{1,0:T(8,128)(2,1)}, bf16[256,2048]{1,0:T(8,128)(2,1)}, u32[]{:S(2)}, u32[]{:S(2)}) collective-permute-start(bf16[256,2048]{1,0:T(8,128)(2,1)} %collective-permute-done.refs_0_), channel_id=1, source_target_pairs={{1,2},{2,3},{5,6},{6,7},{9,10},{10,11},{13,14},{14,15},{17,18},{18... | collective-permute-start | bytes 3145736 | tf_op jit(solution)/shard_map/ppermute | solution.py:569
  40.5 1.3 collective-permute-start.3
  41.8 1.4 %collective-permute-done.5 = bf16[256,256]{1,0:T(8,128)(2,1)S(1)} collective-permute-done((bf16[256,256]{1,0:T(8,128)(2,1)S(1)}, bf16[256,256]{1,0:T(8,128)(2,1)S(1)}, u32[]{:S(2)}, u32[]{:S(2)}) %collective-permute-start.5) | collective-permute-done | bytes 131104 | tf_op jit(solution)/shard_map/ppermute | solution.py:534
  43.3 1.6 %collective-permute-start.8 = (bf16[1792,256]{1,0:T(8,128)(2,1)S(1)}, bf16[1792,256]{1,0:T(8,128)(2,1)S(1)}, u32[]{:S(2)}, u32[]{:S(2)}) collective-permute-start(bf16[1792,256]{1,0:T(8,128)(2,1)S(1)} %constant_dynamic-update-slice_fusion.refs_0_.refs_5_), channel_id=1, source_target_pairs={{0,8},{4,12},{8,0},{12,4},{16,24},{20,28},{24,16},{28,20},{1,9},{5... | collective-permute-start | bytes 2752520 | tf_op jit(solution)/shard_map/ppermute | solution.py:376
  44.8 1.5 %collective-permute-start.9 = (bf16[1792,256]{1,0:T(8,128)(2,1)S(1)}, bf16[1792,256]{1,0:T(8,128)(2,1)S(1)}, u32[]{:S(2)}, u32[]{:S(2)}) collective-permute-start(bf16[1792,256]{1,0:T(8,128)(2,1)S(1)} %constant_dynamic-update-slice_fusion.refs_0_.refs_5_), channel_id=1, source_target_pairs={{0,16},{4,20},{8,24},{12,28},{16,0},{20,4},{24,8},{28,12},{1,17},{... | collective-permute-start | bytes 2752520 | tf_op jit(solution)/shard_map/ppermute | solution.py:376
  46.3 0.6 stack.93.order
  47.0 0.6 pad_add_fusion.2
  47.6 0.7 broadcast_in_dim.2.refs_1_
  48.4 4.2 %absorb.4 = (f32[256,256]{1,0:T(8,128)}, bf16[32,2048,256]{2,1,0:T(8,128)(2,1)}) custom-call(s32[3]{0:T(128)} %get-tuple-element.126.place, bf16[256,2048]{1,0:T(8,128)(2,1)} %refs_0_.1, f32[256,256]{1,0:T(8,128)} %broadcast_in_dim.2.refs_1_, bf16[8192,256]{1,0:T(8,128)(2,1)} %refs_3_.3), custom_call_target="tpu_custom_call" | custom-call | flops 268435456 | bytes 3145728 | tf_op jit(solution)/shard_map/absorb/pallas_call | solution.py:140
  52.6 1.6 %fusion.1.refs_5_ = f32[256,256]{1,0:T(8,128)} fusion(s32[256]{0:T(256)} %bitcast.20), kind=kLoop, calls=%fused_computation.2 | loop fusion | flops 262144 | bytes 263168 | tf_op jit(solution)/shard_map/convert_element_type | solution.py:557
  54.2 2.3 %constant_dynamic-slice_fusion.3.refs_4_ = bf16[2048,256]{1,0:T(8,128)(2,1)} fusion(bf16[8192,256]{1,0:T(8,128)(2,1)} %refs_3_.3, s32[]{:T(128)S(6)} %select_n.57), kind=kLoop, calls=%fused_computation.10 | loop fusion | bytes 2097156 | tf_op jit(solution)/shard_map/dynamic_slice | solution.py:552
  57.6 4.2 %absorb.5 = (f32[256,256]{1,0:T(8,128)}, bf16[32,2048,256]{2,1,0:T(8,128)(2,1)}) custom-call(s32[3]{0:T(128)} %pad_add_fusion.place, bf16[256,2048]{1,0:T(8,128)(2,1)} %collective-permute-done.refs_0_, f32[256,256]{1,0:T(8,128)} %get-tuple-element.71.refs_1_, bf16[8192,256]{1,0:T(8,128)(2,1)} %refs_3_.3, ...), custom_call_target="tpu_custom_call", output_to_operand_aliasing={{1}: (4, {})} | custom-call | flops 268435456 | bytes 3145728 | tf_op jit(solution)/shard_map/absorb/pallas_call | solution.py:140
  61.9 4.2 %absorb.6 = (f32[256,256]{1,0:T(8,128)}, bf16[32,2048,256]{2,1,0:T(8,128)(2,1)}) custom-call(s32[3]{0:T(128)} %pad_add_fusion.1.place, bf16[256,2048]{1,0:T(8,128)(2,1)} %collective-permute-done.2.refs_0_, f32[256,256]{1,0:T(8,128)} %get-tuple-element.73.refs_1_, bf16[8192,256]{1,0:T(8,128)(2,1)} %refs_3_.3, ...), custom_call_target="tpu_custom_call", output_to_operand_aliasing={{1}: (4, {})} | custom-call | flops 268435456 | bytes 3145728 | tf_op jit(solution)/shard_map/absorb/pallas_call | solution.py:140
  66.1 1.1 collective-permute-done.9.refs_4_.refs_9_
  67.3 1.6 %collective-permute-start.10 = (bf16[256,2048]{1,0:T(8,128)(2,1)}, bf16[256,2048]{1,0:T(8,128)(2,1)}, u32[]{:S(2)}, u32[]{:S(2)}) collective-permute-start(bf16[256,2048]{1,0:T(8,128)(2,1)} %collective-permute-done.1.refs_0_), channel_id=1, source_target_pairs={{2,3},{6,7},{10,11},{14,15},{18,19},{22,23},{26,27},{30,31}} | collective-permute-start | bytes 3145736 | tf_op jit(solution)/shard_map/ppermute | solution.py:569
  68.9 1.5 %collective-permute-start.11 = (bf16[256,2048]{1,0:T(8,128)(2,1)}, bf16[256,2048]{1,0:T(8,128)(2,1)}, u32[]{:S(2)}, u32[]{:S(2)}) collective-permute-start(bf16[256,2048]{1,0:T(8,128)(2,1)} %collective-permute-done.3.refs_1_), channel_id=1, source_target_pairs={{1,0},{5,4},{9,8},{13,12},{17,16},{21,20},{25,24},{29,28}} | collective-permute-start | bytes 3145736 | tf_op jit(solution)/shard_map/ppermute | solution.py:568
  70.9 0.8 slice.6
  72.3 0.8 slice.7
  73.1 1.0 copy-done.1
  74.1 1.5 %collective-permute-start.13 = (bf16[768,256]{1,0:T(8,128)(2,1)}, bf16[768,256]{1,0:T(8,128)(2,1)}, u32[]{:S(2)}, u32[]{:S(2)}) collective-permute-start(bf16[768,256]{1,0:T(8,128)(2,1)} %slice.7), channel_id=1, source_target_pairs={{0,16},{4,20},{8,24},{12,28},{16,0},{20,4},{24,8},{28,12},{1,17},{... | collective-permute-start | bytes 1179656 | tf_op jit(solution)/shard_map/ppermute | solution.py:376
  75.6 0.6 pad_add_fusion.4.place
  76.2 4.2 %absorb.7 = (f32[256,256]{1,0:T(8,128)}, bf16[32,2048,256]{2,1,0:T(8,128)(2,1)}) custom-call(s32[3]{0:T(128)} %pad_add_fusion.4.place, bf16[256,2048]{1,0:T(8,128)(2,1)} %collective-permute-done.1.refs_0_, bf16[256,2048]{1,0:T(8,128)(2,1)} %collective-permute-done.3.refs_1_, f32[256,256]{1,0:T(8,128)} %get-tuple-element.79.refs_2_, ...), custom_call_target="tpu_custom_call", output_to_operand_aliasing={{1}: (5, {})} | custom-call | flops 268435456 | bytes 3145728 | tf_op jit(solution)/shard_map/absorb/pallas_call | solution.py:140
  80.4 1.2 copy-done.2
  81.6 3.2 %place_rows.2.refs_2_ = bf16[8192,256]{1,0:T(8,128)(2,1)} custom-call(s32[6]{0:T(128)S(1)} %iota_xor_fusion.1.place, bf16[1792,256]{1,0:T(8,128)(2,1)S(1)} %constant_dynamic-update-slice_fusion.refs_0_.refs_5_, bf16[1792,256]{1,0:T(8,128)(2,1)} %collective-permute-done.7.refs_1_.refs_6_, bf16[1792,256]{1,0:T(8,128)(2,1)S(1)} %collective-permute-done.8.refs_2_.refs_7_, ...), custom_call_target="tpu_custom_call" | custom-call | bytes 6291456 | tf_op jit(solution)/shard_map/place_rows/pallas_call | solution.py:480
  85.1 0.7 collective-permute-done.12.refs_0_
  85.8 11.1 %collective-permute-done.11.refs_1_ = bf16[256,2048]{1,0:T(8,128)(2,1)} collective-permute-done((bf16[256,2048]{1,0:T(8,128)(2,1)}, bf16[256,2048]{1,0:T(8,128)(2,1)}, u32[]{:S(2)}, u32[]{:S(2)}) %collective-permute-start.11) | collective-permute-done | bytes 1048608 | tf_op jit(solution)/shard_map/ppermute | solution.py:568
  97.5 9.7 %attend.1 = (bf16[32,2048,256]{2,1,0:T(8,128)(2,1)}, bf16[256,1024]{1,0:T(8,128)(2,1)}, bf16[256,256]{1,0:T(8,128)(2,1)}, bf16[4,1024,128]{2,1,0:T(8,128)(2,1)}, bf16[4,1024,128]{2,1,0:T(8,128)(2,1)}) custom-call(s32[3]{0:T(128)} %get-tuple-element.127.place, s32[5]{0:T(128)} %stack.93.order, ...), custom_call_target="tpu_custom_call", output_to_operand_aliasing={{0}: (6, {})} | custom-call | flops 805306368 | bytes 2097152 | tf_op jit(solution)/shard_map/attend/pallas_call | solution.py:235
  107.8 0.9 copy-done.4
  108.7 2.5 %weight_send.1 = (f32[2,1024,128]{2,1,0:T(8,128)S(1)}, f32[2,1024,128]{2,1,0:T(8,128)S(1)}) custom-call(s32[5]{0:T(128)S(1)} %stack.95.place, bf16[32,2048,256]{2,1,0:T(8,128)(2,1)} %get-tuple-element.91.held, bf16[256,256]{1,0:T(8,128)(2,1)S(1)} %copy-done.4), custom_call_target="tpu_custom_call" | custom-call | flops 268435456 | bytes 2097152 | tf_op jit(solution)/shard_map/weight_send/pallas_call | solution.py:334
  112.0 1.5 %collective-permute-start.20 = (bf16[2,1024,128]{2,1,0:T(8,128)(2,1)S(1)}, bf16[2,1024,128]{2,1,0:T(8,128)(2,1)S(1)}, u32[]{:S(2)}, u32[]{:S(2)}) collective-permute-start(bf16[2,1024,128]{2,1,0:T(8,128)(2,1)S(1)} %get-tuple-element.100), channel_id=1, source_target_pairs={{0,16},{4,20},{8,24},{12,28},{16,0},{20,4},{24,8},{28,12},{1,17},{... | collective-permute-start | bytes 1572872 | tf_op jit(solution)/shard_map/ppermute | solution.py:376
  113.5 1.6 %collective-permute-start.22 = (bf16[256,256]{1,0:T(8,128)(2,1)S(1)}, bf16[256,256]{1,0:T(8,128)(2,1)S(1)}, u32[]{:S(2)}, u32[]{:S(2)}) collective-permute-start(bf16[256,256]{1,0:T(8,128)(2,1)S(1)} %copy-done.5), channel_id=1, source_target_pairs={{0,2},{1,3},{2,0},{3,1},{4,6},{5,7},{6,4},{7,5},{8,10},{9,11},{10,... | collective-permute-start | bytes 393224 | tf_op jit(solution)/shard_map/ppermute | solution.py:534
  115.2 2.8 %collective-permute-start.23 = (bf16[256,256]{1,0:T(8,128)(2,1)S(1)}, bf16[256,256]{1,0:T(8,128)(2,1)S(1)}, u32[]{:S(2)}, u32[]{:S(2)}) collective-permute-start(bf16[256,256]{1,0:T(8,128)(2,1)S(1)} %copy-done.5), channel_id=1, source_target_pairs={{0,3},{1,2},{2,1},{3,0},{4,7},{5,6},{6,5},{7,4},{8,11},{9,10},{10,... | collective-permute-start | bytes 393224 | tf_op jit(solution)/shard_map/ppermute | solution.py:534
  117.9 1.5 %place_rows.3 = bf16[8192,256]{1,0:T(8,128)(2,1)} custom-call(s32[2]{0:T(128)S(1)} %broadcast_xor_fusion.place, bf16[1024,256]{1,0:T(8,128)(2,1)S(1)} %collective-permute-done.12.refs_0_, bf16[1024,256]{1,0:T(8,128)(2,1)S(1)} %collective-permute-done.16.refs_1_, bf16[8192,256]{1,0:T(8,128)(2,1)} %place_rows.2.refs_2_), custom_call_target="tpu_custom_call", output_to_operand_aliasing={{}: (3, {})} | custom-call | bytes 2097152 | tf_op jit(solution)/shard_map/place_rows/pallas_call | solution.py:480
  119.5 2.5 %weight_keep.1 = (f32[2,1024,128]{2,1,0:T(8,128)S(1)}, f32[2,1024,128]{2,1,0:T(8,128)S(1)}) custom-call(s32[5]{0:T(128)S(1)} %stack.95.place, bf16[32,2048,256]{2,1,0:T(8,128)(2,1)} %get-tuple-element.91.held, bf16[256,256]{1,0:T(8,128)(2,1)S(1)} %copy-done.5, bf16[4,1024,128]{2,1,0:T(8,128)(2,1)S(1)} %collective-permute-done.24.refs_0_), custom_call_target="tpu_custom_call" | custom-call | flops 268435456 | bytes 2097152 | tf_op jit(solution)/shard_map/weight_keep/pallas_call | solution.py:334
  122.0 4.4 %collective-permute-done.22.refs_2_ = bf16[256,256]{1,0:T(8,128)(2,1)S(1)} collective-permute-done((bf16[256,256]{1,0:T(8,128)(2,1)S(1)}, bf16[256,256]{1,0:T(8,128)(2,1)S(1)}, u32[]{:S(2)}, u32[]{:S(2)}) %collective-permute-start.22) | collective-permute-done | bytes 131104 | tf_op jit(solution)/shard_map/ppermute | solution.py:534
  126.4 0.9 collective-permute-start.25
  127.3 1.5 %collective-permute-start.26 = (bf16[1024,128]{1,0:T(8,128)(2,1)S(1)}, bf16[1024,128]{1,0:T(8,128)(2,1)S(1)}, u32[]{:S(2)}, u32[]{:S(2)}) collective-permute-start(bf16[1024,128]{1,0:T(8,128)(2,1)S(1)} %get-tuple-element.110), channel_id=1, source_target_pairs={{0,8},{4,12},{8,0},{12,4},{16,24},{20,28},{24,16},{28,20},{1,9},{5... | collective-permute-start | bytes 786440 | tf_op jit(solution)/shard_map/ppermute | solution.py:376
  128.8 4.0 %input_gradient.1 = bf16[256,2048]{1,0:T(8,128)(2,1)} custom-call(s32[8]{0:T(128)S(1)} %iota_xor_fusion.place, bf16[256,256]{1,0:T(8,128)(2,1)S(1)} %copy-done.5, bf16[256,256]{1,0:T(8,128)(2,1)S(1)} %collective-permute-done.21.refs_1_, bf16[256,256]{1,0:T(8,128)(2,1)S(1)} %collective-permute-done.22.refs_2_, ...), custom_call_target="tpu_custom_call" | custom-call | flops 1073741824 | bytes 8912896 | tf_op jit(solution)/shard_map/input_gradient/pallas_call | solution.py:73
  133.0 1.2 collective-permute-done.26.last_b
  134.2 1.1 weight_finish.1
  (53 shorter events, 5.0 us)
Async XLA Ops:
  0.6 38.2 %collective-permute-start = (bf16[256,2048]{1,0:T(8,128)(2,1)}, bf16[256,2048]{1,0:T(8,128)(2,1)}, u32[]{:S(2)}, u32[]{:S(2)}) collective-permute-start(bf16[256,2048]{1,0:T(8,128)(2,1)} %refs_0_.1), channel_id=1, source_target_pairs={{0,1},{1,2},{2,3},{4,5},{5,6},{6,7},{8,9},{9,10},{10,11},{12,13},{... | collective-permute-start | bytes 3145736 | tf_op jit(solution)/shard_map/ppermute | solution.py:569
  6.5 34.0 %collective-permute-start.2 = (bf16[256,2048]{1,0:T(8,128)(2,1)}, bf16[256,2048]{1,0:T(8,128)(2,1)}, u32[]{:S(2)}, u32[]{:S(2)}) collective-permute-start(bf16[256,2048]{1,0:T(8,128)(2,1)} %refs_0_.1), channel_id=1, source_target_pairs={{1,0},{2,1},{3,2},{5,4},{6,5},{7,6},{9,8},{10,9},{11,10},{13,12},{... | collective-permute-start | bytes 3145736 | tf_op jit(solution)/shard_map/ppermute | solution.py:568
  8.9 29.9 %collective-permute-start.4 = (bf16[256,256]{1,0:T(8,128)(2,1)S(1)}, bf16[256,256]{1,0:T(8,128)(2,1)S(1)}, u32[]{:S(2)}, u32[]{:S(2)}) collective-permute-start(bf16[256,256]{1,0:T(8,128)(2,1)S(1)} %get-tuple-element.125), channel_id=1, source_target_pairs={{0,1},{1,0},{2,3},{3,2},{4,5},{5,4},{6,7},{7,6},{8,9},{9,8},{10,11... | collective-permute-start | bytes 393224 | tf_op jit(solution)/shard_map/ppermute | solution.py:534
  11.6 31.5 %collective-permute-start.5 = (bf16[256,256]{1,0:T(8,128)(2,1)S(1)}, bf16[256,256]{1,0:T(8,128)(2,1)S(1)}, u32[]{:S(2)}, u32[]{:S(2)}) collective-permute-start(bf16[256,256]{1,0:T(8,128)(2,1)S(1)} %get-tuple-element.124), channel_id=1, source_target_pairs={{0,2},{1,3},{2,0},{3,1},{4,6},{5,7},{6,4},{7,5},{8,10},{9,11},{10,... | collective-permute-start | bytes 393224 | tf_op jit(solution)/shard_map/ppermute | solution.py:534
  14.2 28.9 %collective-permute-start.6 = (bf16[256,256]{1,0:T(8,128)(2,1)S(1)}, bf16[256,256]{1,0:T(8,128)(2,1)S(1)}, u32[]{:S(2)}, u32[]{:S(2)}) collective-permute-start(bf16[256,256]{1,0:T(8,128)(2,1)S(1)} %get-tuple-element.123), channel_id=1, source_target_pairs={{0,3},{1,2},{2,1},{3,0},{4,7},{5,6},{6,5},{7,4},{8,11},{9,10},{10,... | collective-permute-start | bytes 393224 | tf_op jit(solution)/shard_map/ppermute | solution.py:534
  38.8 28.4 %collective-permute-start.1 = (bf16[256,2048]{1,0:T(8,128)(2,1)}, bf16[256,2048]{1,0:T(8,128)(2,1)}, u32[]{:S(2)}, u32[]{:S(2)}) collective-permute-start(bf16[256,2048]{1,0:T(8,128)(2,1)} %collective-permute-done.refs_0_), channel_id=1, source_target_pairs={{1,2},{2,3},{5,6},{6,7},{9,10},{10,11},{13,14},{14,15},{17,18},{18... | collective-permute-start | bytes 3145736 | tf_op jit(solution)/shard_map/ppermute | solution.py:569
  40.5 26.7 %collective-permute-start.3 = (bf16[256,2048]{1,0:T(8,128)(2,1)}, bf16[256,2048]{1,0:T(8,128)(2,1)}, u32[]{:S(2)}, u32[]{:S(2)}) collective-permute-start(bf16[256,2048]{1,0:T(8,128)(2,1)} %collective-permute-done.2.refs_0_), channel_id=1, source_target_pairs={{1,0},{2,1},{5,4},{6,5},{9,8},{10,9},{13,12},{14,13},{17,16},{18,1... | collective-permute-start | bytes 3145736 | tf_op jit(solution)/shard_map/ppermute | solution.py:568
  43.2 22.9 %collective-permute-start.7 = (bf16[1792,256]{1,0:T(8,128)(2,1)S(1)}, bf16[1792,256]{1,0:T(8,128)(2,1)}, u32[]{:S(2)}, u32[]{:S(2)}) collective-permute-start(bf16[1792,256]{1,0:T(8,128)(2,1)S(1)} %constant_dynamic-update-slice_fusion.refs_0_.refs_5_), channel_id=1, source_target_pairs={{0,4},{4,0},{8,12},{12,8},{16,20},{20,16},{24,28},{28,24},{1,5},{5... | collective-permute-start | bytes 2752520 | tf_op jit(solution)/shard_map/ppermute | solution.py:376
  43.3 22.9 %collective-permute-start.8 = (bf16[1792,256]{1,0:T(8,128)(2,1)S(1)}, bf16[1792,256]{1,0:T(8,128)(2,1)S(1)}, u32[]{:S(2)}, u32[]{:S(2)}) collective-permute-start(bf16[1792,256]{1,0:T(8,128)(2,1)S(1)} %constant_dynamic-update-slice_fusion.refs_0_.refs_5_), channel_id=1, source_target_pairs={{0,8},{4,12},{8,0},{12,4},{16,24},{20,28},{24,16},{28,20},{1,9},{5... | collective-permute-start | bytes 2752520 | tf_op jit(solution)/shard_map/ppermute | solution.py:376
  44.8 22.4 %collective-permute-start.9 = (bf16[1792,256]{1,0:T(8,128)(2,1)S(1)}, bf16[1792,256]{1,0:T(8,128)(2,1)S(1)}, u32[]{:S(2)}, u32[]{:S(2)}) collective-permute-start(bf16[1792,256]{1,0:T(8,128)(2,1)S(1)} %constant_dynamic-update-slice_fusion.refs_0_.refs_5_), channel_id=1, source_target_pairs={{0,16},{4,20},{8,24},{12,28},{16,0},{20,4},{24,8},{28,12},{1,17},{... | collective-permute-start | bytes 2752520 | tf_op jit(solution)/shard_map/ppermute | solution.py:376
  67.3 5.8 %collective-permute-start.14 = (bf16[1792,256]{1,0:T(8,128)(2,1)S(1)}, bf16[1792,256]{1,0:T(8,128)(2,1)S(1)}, u32[]{:S(2)}, u32[]{:S(2)}) collective-permute-start(bf16[1792,256]{1,0:T(8,128)(2,1)S(1)} %collective-permute-done.8.refs_2_.refs_7_), channel_id=1, source_target_pairs={{0,4},{4,0},{8,12},{12,8},{16,20},{20,16},{24,28},{28,24},{1,5},{5... | collective-permute-start | bytes 2752520 | tf_op jit(solution)/shard_map/ppermute | solution.py:376
  67.3 18.6 %collective-permute-start.10 = (bf16[256,2048]{1,0:T(8,128)(2,1)}, bf16[256,2048]{1,0:T(8,128)(2,1)}, u32[]{:S(2)}, u32[]{:S(2)}) collective-permute-start(bf16[256,2048]{1,0:T(8,128)(2,1)} %collective-permute-done.1.refs_0_), channel_id=1, source_target_pairs={{2,3},{6,7},{10,11},{14,15},{18,19},{22,23},{26,27},{30,31}} | collective-permute-start | bytes 3145736 | tf_op jit(solution)/shard_map/ppermute | solution.py:569
  68.9 28.0 %collective-permute-start.11 = (bf16[256,2048]{1,0:T(8,128)(2,1)}, bf16[256,2048]{1,0:T(8,128)(2,1)}, u32[]{:S(2)}, u32[]{:S(2)}) collective-permute-start(bf16[256,2048]{1,0:T(8,128)(2,1)} %collective-permute-done.3.refs_1_), channel_id=1, source_target_pairs={{1,0},{5,4},{9,8},{13,12},{17,16},{21,20},{25,24},{29,28}} | collective-permute-start | bytes 3145736 | tf_op jit(solution)/shard_map/ppermute | solution.py:568
  70.4 10.1 %collective-permute-start.15 = (bf16[1792,256]{1,0:T(8,128)(2,1)S(1)}, bf16[1792,256]{1,0:T(8,128)(2,1)}, u32[]{:S(2)}, u32[]{:S(2)}) collective-permute-start(bf16[1792,256]{1,0:T(8,128)(2,1)S(1)} %collective-permute-done.9.refs_4_.refs_9_), channel_id=1, source_target_pairs={{0,4},{4,0},{8,12},{12,8},{16,20},{20,16},{24,28},{28,24},{1,5},{5... | collective-permute-start | bytes 2752520 | tf_op jit(solution)/shard_map/ppermute | solution.py:376
  71.8 14.1 %collective-permute-start.12 = (bf16[1024,256]{1,0:T(8,128)(2,1)}, bf16[1024,256]{1,0:T(8,128)(2,1)S(1)}, u32[]{:S(2)}, u32[]{:S(2)}) collective-permute-start(bf16[1024,256]{1,0:T(8,128)(2,1)} %slice.6), channel_id=1, source_target_pairs={{0,8},{4,12},{8,0},{12,4},{16,24},{20,28},{24,16},{28,20},{1,9},{5... | collective-permute-start | bytes 1572872 | tf_op jit(solution)/shard_map/ppermute | solution.py:376
  73.1 1.0 copy-start.1
  74.1 11.1 %collective-permute-start.13 = (bf16[768,256]{1,0:T(8,128)(2,1)}, bf16[768,256]{1,0:T(8,128)(2,1)}, u32[]{:S(2)}, u32[]{:S(2)}) collective-permute-start(bf16[768,256]{1,0:T(8,128)(2,1)} %slice.7), channel_id=1, source_target_pairs={{0,16},{4,20},{8,24},{12,28},{16,0},{20,4},{24,8},{28,12},{1,17},{... | collective-permute-start | bytes 1179656 | tf_op jit(solution)/shard_map/ppermute | solution.py:376
  80.4 1.2 copy-start.2
  96.9 10.3 %collective-permute-start.16 = (bf16[1024,256]{1,0:T(8,128)(2,1)S(1)}, bf16[1024,256]{1,0:T(8,128)(2,1)S(1)}, u32[]{:S(2)}, u32[]{:S(2)}) collective-permute-start(bf16[1024,256]{1,0:T(8,128)(2,1)S(1)} %collective-permute-done.12.refs_0_), channel_id=1, source_target_pairs={{0,4},{4,0},{8,12},{12,8},{16,20},{20,16},{24,28},{28,24},{1,5},{5... | collective-permute-start | bytes 1572872 | tf_op jit(solution)/shard_map/ppermute | solution.py:376
  96.9 10.3 %collective-permute-start.17 = (bf16[768,256]{1,0:T(8,128)(2,1)}, bf16[768,256]{1,0:T(8,128)(2,1)}, u32[]{:S(2)}, u32[]{:S(2)}) collective-permute-start(bf16[768,256]{1,0:T(8,128)(2,1)} %collective-permute-done.13.refs_11_), channel_id=1, source_target_pairs={{0,4},{4,0},{8,12},{12,8},{16,20},{20,16},{24,28},{28,24},{1,5},{5... | collective-permute-start | bytes 1179656 | tf_op jit(solution)/shard_map/ppermute | solution.py:376
  97.5 20.5 %copy-start.6 = (s32[2]{0:T(128)S(1)}, s32[2]{0:T(128)}, u32[]{:S(2)}) copy-start(s32[2]{0:T(128)} %constant.72.clone) | copy-start | bytes 28
  107.2 4.0 %collective-permute-start.18 = (bf16[4,1024,128]{2,1,0:T(8,128)(2,1)}, bf16[4,1024,128]{2,1,0:T(8,128)(2,1)S(1)}, u32[]{:S(2)}, u32[]{:S(2)}) collective-permute-start(bf16[4,1024,128]{2,1,0:T(8,128)(2,1)} %get-tuple-element.98), channel_id=1, source_target_pairs={{0,4},{4,0},{8,12},{12,8},{16,20},{20,16},{24,28},{28,24},{1,5},{5... | collective-permute-start | bytes 3145736 | tf_op jit(solution)/shard_map/ppermute | solution.py:376
  107.3 7.9 %collective-permute-start.24 = (bf16[4,1024,128]{2,1,0:T(8,128)(2,1)}, bf16[4,1024,128]{2,1,0:T(8,128)(2,1)S(1)}, u32[]{:S(2)}, u32[]{:S(2)}) collective-permute-start(bf16[4,1024,128]{2,1,0:T(8,128)(2,1)} %get-tuple-element.104), channel_id=1, source_target_pairs={{0,4},{4,0},{8,12},{12,8},{16,20},{20,16},{24,28},{28,24},{1,5},{5... | collective-permute-start | bytes 3145736 | tf_op jit(solution)/shard_map/ppermute | solution.py:376
  107.8 0.9 copy-start.4
  108.7 4.8 %copy-start.5 = (bf16[256,256]{1,0:T(8,128)(2,1)S(1)}, bf16[256,256]{1,0:T(8,128)(2,1)}, u32[]{:S(2)}) copy-start(bf16[256,256]{1,0:T(8,128)(2,1)} %get-tuple-element.111.d_projected.refs_0_) | copy-start | bytes 393220
  111.2 17.6 %copy-start = (bf16[2048,256]{1,0:T(8,128)(2,1)S(1)}, bf16[2048,256]{1,0:T(8,128)(2,1)}, u32[]{:S(2)}) copy-start(bf16[2048,256]{1,0:T(8,128)(2,1)} %constant_dynamic-slice_fusion.3.refs_4_) | copy-start | bytes 3145732
  111.2 17.6 %copy-start.3 = (bf16[1792,256]{1,0:T(8,128)(2,1)S(1)}, bf16[1792,256]{1,0:T(8,128)(2,1)}, u32[]{:S(2)}) copy-start(bf16[1792,256]{1,0:T(8,128)(2,1)} %copy-done.1) | copy-start | bytes 2752516
  111.4 14.9 %collective-permute-start.19 = (bf16[2,1024,128]{2,1,0:T(8,128)(2,1)S(1)}, bf16[2,1024,128]{2,1,0:T(8,128)(2,1)S(1)}, u32[]{:S(2)}, u32[]{:S(2)}) collective-permute-start(bf16[2,1024,128]{2,1,0:T(8,128)(2,1)S(1)} %get-tuple-element.99), channel_id=1, source_target_pairs={{0,8},{4,12},{8,0},{12,4},{16,24},{20,28},{24,16},{28,20},{1,9},{5... | collective-permute-start | bytes 1572872 | tf_op jit(solution)/shard_map/ppermute | solution.py:376
  112.0 14.3 %collective-permute-start.20 = (bf16[2,1024,128]{2,1,0:T(8,128)(2,1)S(1)}, bf16[2,1024,128]{2,1,0:T(8,128)(2,1)S(1)}, u32[]{:S(2)}, u32[]{:S(2)}) collective-permute-start(bf16[2,1024,128]{2,1,0:T(8,128)(2,1)S(1)} %get-tuple-element.100), channel_id=1, source_target_pairs={{0,16},{4,20},{8,24},{12,28},{16,0},{20,4},{24,8},{28,12},{1,17},{... | collective-permute-start | bytes 1572872 | tf_op jit(solution)/shard_map/ppermute | solution.py:376
  113.5 8.4 %collective-permute-start.21 = (bf16[256,256]{1,0:T(8,128)(2,1)S(1)}, bf16[256,256]{1,0:T(8,128)(2,1)S(1)}, u32[]{:S(2)}, u32[]{:S(2)}) collective-permute-start(bf16[256,256]{1,0:T(8,128)(2,1)S(1)} %copy-done.5), channel_id=1, source_target_pairs={{0,1},{1,0},{2,3},{3,2},{4,5},{5,4},{6,7},{7,6},{8,9},{9,8},{10,11... | collective-permute-start | bytes 393224 | tf_op jit(solution)/shard_map/ppermute | solution.py:534
  113.5 12.8 %collective-permute-start.22 = (bf16[256,256]{1,0:T(8,128)(2,1)S(1)}, bf16[256,256]{1,0:T(8,128)(2,1)S(1)}, u32[]{:S(2)}, u32[]{:S(2)}) collective-permute-start(bf16[256,256]{1,0:T(8,128)(2,1)S(1)} %copy-done.5), channel_id=1, source_target_pairs={{0,2},{1,3},{2,0},{3,1},{4,6},{5,7},{6,4},{7,5},{8,10},{9,11},{10,... | collective-permute-start | bytes 393224 | tf_op jit(solution)/shard_map/ppermute | solution.py:534
  115.2 11.2 %collective-permute-start.23 = (bf16[256,256]{1,0:T(8,128)(2,1)S(1)}, bf16[256,256]{1,0:T(8,128)(2,1)S(1)}, u32[]{:S(2)}, u32[]{:S(2)}) collective-permute-start(bf16[256,256]{1,0:T(8,128)(2,1)S(1)} %copy-done.5), channel_id=1, source_target_pairs={{0,3},{1,2},{2,1},{3,0},{4,7},{5,6},{6,5},{7,4},{8,11},{9,10},{10,... | collective-permute-start | bytes 393224 | tf_op jit(solution)/shard_map/ppermute | solution.py:534
  126.4 6.5 %collective-permute-start.25 = (bf16[1024,128]{1,0:T(8,128)(2,1)S(1)}, bf16[1024,128]{1,0:T(8,128)(2,1)S(1)}, u32[]{:S(2)}, u32[]{:S(2)}) collective-permute-start(bf16[1024,128]{1,0:T(8,128)(2,1)S(1)} %get-tuple-element.109), channel_id=1, source_target_pairs={{0,16},{4,20},{8,24},{12,28},{16,0},{20,4},{24,8},{28,12},{1,17},{... | collective-permute-start | bytes 786440 | tf_op jit(solution)/shard_map/ppermute | solution.py:376
  127.3 6.9 %collective-permute-start.26 = (bf16[1024,128]{1,0:T(8,128)(2,1)S(1)}, bf16[1024,128]{1,0:T(8,128)(2,1)S(1)}, u32[]{:S(2)}, u32[]{:S(2)}) collective-permute-start(bf16[1024,128]{1,0:T(8,128)(2,1)S(1)} %get-tuple-element.110), channel_id=1, source_target_pairs={{0,8},{4,12},{8,0},{12,4},{16,24},{20,28},{24,16},{28,20},{1,9},{5... | collective-permute-start | bytes 786440 | tf_op jit(solution)/shard_map/ppermute | solution.py:376

commit v12 on v11

--- a/solution.py
+++ b/solution.py
@@ -423,49 +423,61 @@
 
 
 class PlaneGather:
-    def __init__(self, own, split):
-        self.got, self.split = {0: own}, split
+    def __init__(self, own_cache, own_rows):
+        self.own = own_cache, own_rows
+        self.both = jnp.concatenate([own_cache, own_rows], axis=0)
 
     def first(self):
-        own, swap = self.got[0], plane()[3]
-        self.got.update({bit: swap(own, bit) for bit in (2, 4, 1)})
-        return self.got
+        swap = plane()[3]
+        return swap(self.own[1], 2), swap(self.own[0], 4), swap(self.both, 1)
 
     def second(self):
-        got, swap = self.got, plane()[3]
-        self.far = [swap(got[4][: self.split], 2), swap(got[2][self.split :], 4)]
-        got[3], got[5] = swap(got[2], 1), swap(got[4], 1)
-        return self.far, got[3], got[5]
+        swap = plane()[3]
+        rows_x, cache_y, _ = self.got
+        packs = (
+            swap(jnp.concatenate([self.own[0], cache_y], axis=0), 2),
+            swap(jnp.concatenate([self.own[1], rows_x], axis=0), 4),
+        )
+        return packs, (swap(rows_x, 1), swap(cache_y, 1))
 
     def third(self):
         swap = plane()[3]
-        self.far_other = [swap(value, 1) for value in self.far]
-        return self.far_other
+        return swap(self.packs[0], 1), swap(self.packs[1], 1)
 
     def where(self, bits):
         return lax.axis_index("dp").astype(jnp.int32) ^ jnp.array(bits, dtype=jnp.int32)
 
-    def lay(self, height, rows):
-        arrays = [self.got[k] for k in range(6)]
-        return place_rows(arrays, self.where(list(range(6))), height, rows, [])
-
-    def lay_far(self, height, laid):
-        arrays = [self.far[0], self.far_other[0]]
-        return place_rows(arrays, self.where([6, 7]), height, laid.shape[0], [laid])
-
-    def last(self):
-        arrays = [self.got[k] for k in range(6)] + [self.far[1], self.far_other[1]]
-        return arrays, self.where(list(range(8)))
-
-
-def place_rows_kernel(height, n_arrays, place, *refs):
-    arrays, (out, sems) = refs[:n_arrays], refs[-2:]
+    def lay(self, swapped, n_rows):
+        arrays = [self.own[0], self.got[2], self.got[1], swapped[1]]
+        return place_rows(arrays, [(k, 0) for k in range(4)], self.where([0, 1, 4, 5]),
+                          self.own[0].shape[0], n_rows, [])
+
+    def lay_rest(self, laid):
+        height = self.own[0].shape[0]
+        parts = [(0, 0), (0, height), (1, 0), (1, height)]
+        arrays = [self.packs[0], self.packs_other[0]]
+        return place_rows(
+            arrays, parts, self.where([2, 6, 3, 7]), height, laid.shape[0], [laid]
+        )
+
+    def feature_rows(self):
+        height, count = self.own[0].shape[0], self.own[1].shape[0]
+        arrays = [self.own[1], self.got[2], self.got[0], self.swapped[0]]
+        arrays += [self.packs[1], self.packs_other[1]]
+        parts = [(0, 0), (1, height), (2, 0), (3, 0), (4, 0), (4, count), (5, 0), (5, count)]
+        return arrays, parts, self.where([0, 1, 2, 3, 4, 6, 5, 7])
+
+
+def place_rows_kernel(height, parts, place, *refs):
+    out, sems = refs[-2:]
     copies = []
-    for k, array in enumerate(arrays):
+    for k, (which, row) in enumerate(parts):
         start = pl.multiple_of(place[k] * height, height)
         copies.append(
             pltpu.make_async_copy(
-                array.at[pl.ds(0, height), :], out.at[pl.ds(start, height), :], sems.at[k]
+                refs[which].at[pl.ds(row, height), :],
+                out.at[pl.ds(start, height), :],
+                sems.at[k],
             )
         )
     for copy in copies:
@@ -474,37 +486,36 @@
         copy.wait()
 
 
-def place_rows(arrays, place, height, rows, into):
+def place_rows(arrays, parts, place, height, rows, into):
     cols = arrays[0].shape[1]
     anywhere = pl.BlockSpec(memory_space=pl.ANY)
     return pl.pallas_call(
-        functools.partial(place_rows_kernel, height, len(arrays)),
+        functools.partial(place_rows_kernel, height, parts),
         in_specs=[pl.BlockSpec(memory_space=pltpu.SMEM)]
         + [pl.BlockSpec(memory_space=pltpu.VMEM)] * len(arrays)
         + [anywhere] * len(into),
         out_specs=anywhere,
         out_shape=jax.ShapeDtypeStruct((rows, cols), arrays[0].dtype),
-        scratch_shapes=[pltpu.SemaphoreType.DMA((len(arrays),))],
+        scratch_shapes=[pltpu.SemaphoreType.DMA((len(parts),))],
         input_output_aliases={1 + len(arrays): 0} if into else {},
         cost_estimate=pl.CostEstimate(
-            flops=0, bytes_accessed=4 * height * cols * len(arrays), transcendentals=0
+            flops=0, bytes_accessed=4 * height * cols * len(parts), transcendentals=0
         ),
         compiler_params=pltpu.CompilerParams(vmem_limit_bytes=VMEM_WHOLE),
         name="place_rows",
     )(place, *arrays, *into)
 
 
-def input_kernel(n_blocks, place, *refs):
+def input_kernel(n_blocks, parts, place, *refs):
     *arrays, out = refs
-    pieces, here, rows = arrays[:n_blocks], arrays[n_blocks], arrays[n_blocks + 1 :]
-    share = out.shape[1] // len(rows)
-    for k, held in enumerate(rows):
+    pieces, here, arrays = arrays[:n_blocks], arrays[n_blocks], arrays[n_blocks + 1 :]
+    share = out.shape[1] // len(parts)
+    for k, (which, row) in enumerate(parts):
         start = pl.multiple_of(place[k] * share, share)
-        first = held.shape[0] - n_blocks * share
         total = jnp.zeros((out.shape[0], share), jnp.float32)
         for s, piece in enumerate(pieces):
             if s:
-                block = held[first + s * share : first + (s + 1) * share, :]
+                block = arrays[which][row + (s - 1) * share : row + s * share, :]
             else:
                 block = here[pl.ds(start, share), :]
             total = total + lax.dot_general(
@@ -513,11 +524,11 @@
         out[:, pl.ds(start, share)] = total.astype(out.dtype)
 
 
-def input_gradient(pieces, here, arrays, place):
+def input_gradient(pieces, here, arrays, parts, place):
     length, cols = pieces[0].shape
     feats = here.shape[0]
     (d_tokens,) = on_chip(
-        functools.partial(input_kernel, len(pieces)),
+        functools.partial(input_kernel, len(pieces), parts),
         place,
         pieces + [here] + arrays,
         [jax.ShapeDtypeStruct((length, feats), jnp.bfloat16)],
@@ -561,7 +572,7 @@
         orders = weight_orders() if tuned else [jnp.zeros((5,), jnp.int32)]
         total, held = absorb([tokens], zero, me_z, cached, total, None, n_z)
         if tuned:
-            gather = PlaneGather(jnp.concatenate([own_cache] + blocks, axis=0), own_cache.shape[0])
+            gather = PlaneGather(own_cache, jnp.concatenate(blocks, axis=0))
         from_low, from_high = tokens, tokens
         for s in range(1, n_z):
             low, high = me_z - s, me_z + s
@@ -569,26 +580,20 @@
             from_low = lax.ppermute(
                 from_low, "tensor", [(z, z + 1) for z in range(s - 1, n_z - 1)]
             )
-            if tuned:
-                if s == 1:
-                    held, allowed, orders, here = lax.optimization_barrier(
-                        (held, allowed, orders, here)
-                    )
-                    rounds = None
-                elif s == 2:
-                    rounds = gather.first()
-                else:
-                    rounds = gather.second()
-                    laid = gather.lay(own_cache.shape[0], cached.shape[0])
-                    rounds = (rounds, laid)
-                if s > 1:
-                    from_low, from_high, held, rounds = lax.optimization_barrier(
-                        (from_low, from_high, held, rounds)
-                    )
-                if s == 2:
-                    gather.got = rounds
-                if s == 3:
-                    (gather.far, gather.got[3], gather.got[5]), laid = rounds
+            if tuned and s == 1:
+                from_low, from_high, held, allowed, orders, here = lax.optimization_barrier(
+                    (from_low, from_high, held, allowed, orders, here)
+                )
+            elif tuned and s == 2:
+                from_low, from_high, held, gather.got = lax.optimization_barrier(
+                    (from_low, from_high, held, gather.first())
+                )
+            elif tuned:
+                packs, swapped = gather.second()
+                laid = gather.lay(swapped, cached.shape[0])
+                from_low, from_high, held, gather.packs, gather.swapped, laid = (
+                    lax.optimization_barrier((from_low, from_high, held, packs, swapped, laid))
+                )
             chunks, which = [from_low, from_high], (me_z < s).astype(jnp.int32)
             index = jnp.where(me_z < s, high, low)
             if 2 * s < n_z:
@@ -603,12 +608,12 @@
 
         pieces = [d_projected] + [pair(d_projected, s) for s in range(1, n_z)]
         if tuned:
-            sent, gather.far_other = lax.optimization_barrier((sent, gather.third()))
-            new_cache = gather.lay_far(own_cache.shape[0], laid)
+            sent, gather.packs_other = lax.optimization_barrier((sent, gather.third()))
+            new_cache = gather.lay_rest(laid)
             finish, pieces, new_cache = weight_sum(
                 held, d_projected, orders[1], sent, kept, pieces, new_cache
             )
-            new_grad, d_tokens = finish(input_gradient(pieces, here, *gather.last()))
+            new_grad, d_tokens = finish(input_gradient(pieces, here, *gather.feature_rows()))
         else:
             new_cache = lax.all_gather(own_cache, "dp", axis=0, tiled=True)
             rows = lax.all_gather(jnp.stack([block_for(me_z)] + blocks), "dp", axis=0)

time: 136 us -> 135 us (level)
  local copies, waits for them, and re-layouts: 10.6 us -> 7.56 us
  starting transfers between devices: 34.2 us -> 36.3 us
  other arithmetic: 3.97 us -> 5.7 us
  waiting for transfers between devices: 39 us -> 37.5 us
    ppermute x6, waiting for transfers between devices: 24.3 us -> 7.79 us  [pair(): return lax.ppermute(value, 'tensor', [(z, z ^ s) for z in range(n_z)])]
    ppermute x15, waiting for transfers between devices: 3.57 us -> 13.6 us  [swap(): return lax.ppermute(value, 'dp', [(i, i ^ bit) for i in range(8)])]
    ppermute x3, waiting for transfers between devices: 11.1 us -> 14.3 us  [body(): lax.ppermute(from_high, 'tensor', [(z + 1, z) for z in range(n_z - s)])]
    concatenate x0 -> x3, other arithmetic: none -> 2.97 us  [the longest x1 1.04 us: second(): jnp.concatenate([self.own[0], cache_y], axis=0)]
    ppermute x3, waiting for transfers between devices: 0.01 us -> 1.78 us  [body(): lax.ppermute(from_low, 'tensor', [(z, z + 1) for z in range(s - 1, n_z -...]
    ppermute x6, starting transfers between devices: 9.69 us -> 11.4 us  [pair(): return lax.ppermute(value, 'tensor', [(z, z ^ s) for z in range(n_z)])]
    slice x2 -> x0, local copies, waits for them, and re-layouts: 1.6 us -> none  [second(): self.far = [swap(got[4][:self.split], 2), swap(got[2][self.split:], 4)]]
    unnamed x17 -> x28, local copies, waits for them, and re-layouts: 4.17 us -> 3.06 us
  transfers between devices with their start and end apart: 27 -> 27, of which waited for: 9 -> 10; matrix products, arithmetic and copies ran while one was open for 8% -> 9% of each run, Pallas kernels for 34% -> 34%
where the time goes in v12:
time: 135 us; the launch traced here: 134 us
  Pallas kernels  46.4 us (34%)
  waiting for transfers between devices  37.5 us (28%)
  starting transfers between devices  36.3 us (27%)
  local copies, waits for them, and re-layouts  7.56 us (6%)
  other arithmetic  5.7 us (4%)
    pallas_call x4, Pallas kernels, absorb(): pl.pallas_call(functools.partial(absorb_kernel, len(chunks)), in_specs=[p...  17 us
    ppermute x3, waiting for transfers between devices, body(): lax.ppermute(from_high, 'tensor', [(z + 1, z) for z in range(n_z - s)])  14.3 us
    ppermute x15, waiting for transfers between devices, swap(): return lax.ppermute(value, 'dp', [(i, i ^ bit) for i in range(8)])  13.6 us
    ppermute x15, starting transfers between devices, swap(): return lax.ppermute(value, 'dp', [(i, i ^ bit) for i in range(8)])  11.6 us
    ppermute x6, starting transfers between devices, pair(): return lax.ppermute(value, 'tensor', [(z, z ^ s) for z in range(n_z)])  11.4 us
    pallas_call x1, Pallas kernels, attend(): pl.pallas_call(functools.partial(attend_kernel, len(chunks)), in_specs=[p...  9.73 us
    ppermute x3, starting transfers between devices, body(): lax.ppermute(from_low, 'tensor', [(z, z + 1) for z in range(s - 1, n_z -...  9.33 us
    ppermute x6, waiting for transfers between devices, pair(): return lax.ppermute(value, 'tensor', [(z, z ^ s) for z in range(n_z)])  7.79 us
  transfers between devices with their start and end apart: 27, of which 10 were waited for; matrix products, arithmetic and copies ran while one was open for 9% of the time, Pallas kernels for 34%

profile of v12, /device:TPU:0, one launch (start us, length us, event | category | flops | bytes accessed | tf_op | source)
XLA Modules:
  0.0 134.4 jit_solution(6909866243256071909)
XLA Ops:
  0.6 5.9 %collective-permute-start = (bf16[256,2048]{1,0:T(8,128)(2,1)}, bf16[256,2048]{1,0:T(8,128)(2,1)}, u32[]{:S(2)}, u32[]{:S(2)}) collective-permute-start(bf16[256,2048]{1,0:T(8,128)(2,1)} %refs_0_.1), channel_id=1, source_target_pairs={{0,1},{1,2},{2,3},{4,5},{5,6},{6,7},{8,9},{9,10},{10,11},{12,13},{... | collective-permute-start | bytes 3145736 | tf_op jit(solution)/shard_map/ppermute | solution.py:580
  6.6 1.3 collective-permute-start.1
  7.9 1.1 constant_dynamic-slice_fusion
  8.9 2.7 %collective-permute-start.4 = (bf16[256,256]{1,0:T(8,128)(2,1)S(1)}, bf16[256,256]{1,0:T(8,128)(2,1)S(1)}, u32[]{:S(2)}, u32[]{:S(2)}) collective-permute-start(bf16[256,256]{1,0:T(8,128)(2,1)S(1)} %get-tuple-element.125), channel_id=1, source_target_pairs={{0,1},{1,0},{2,3},{3,2},{4,5},{5,4},{6,7},{7,6},{8,9},{9,8},{10,11... | collective-permute-start | bytes 393224 | tf_op jit(solution)/shard_map/ppermute | solution.py:545
  11.7 2.5 %collective-permute-start.5 = (bf16[256,256]{1,0:T(8,128)(2,1)S(1)}, bf16[256,256]{1,0:T(8,128)(2,1)S(1)}, u32[]{:S(2)}, u32[]{:S(2)}) collective-permute-start(bf16[256,256]{1,0:T(8,128)(2,1)S(1)} %get-tuple-element.124), channel_id=1, source_target_pairs={{0,2},{1,3},{2,0},{3,1},{4,6},{5,7},{6,4},{7,5},{8,10},{9,11},{10,... | collective-permute-start | bytes 393224 | tf_op jit(solution)/shard_map/ppermute | solution.py:545
  14.9 4.9 %optimizer.1 = (f32[1024,256]{1,0:T(8,128)}, f32[1024,256]{1,0:T(8,128)}, f32[1024,256]{1,0:T(8,128)}, bf16[1024,256]{1,0:T(8,128)(2,1)}) custom-call(s32[1]{0:T(128)} %bitcast.place, bf16[8192,256]{1,0:T(8,128)(2,1)} %refs_3_.3, f32[1024,256]{1,0:T(8,128)} %master.1, f32[1024,256]{1,0:T(8,128)} %moment.1, f32[1024,256]{1,0:T(8,128)} %second.1, f32[1024,256]{1,0:T(8,128)} %grad.1), custom_call_target="tpu_custom_call" | custom-call | flops 10485760 | bytes 8388608 | tf_op jit(solution)/shard_map/optimizer/pallas_call | solution.py:51
  20.5 0.7 broadcast_in_dim.2.refs_1_
  21.2 4.2 %absorb.4 = (f32[256,256]{1,0:T(8,128)}, bf16[32,2048,256]{2,1,0:T(8,128)(2,1)}) custom-call(s32[3]{0:T(128)} %get-tuple-element.128.place, bf16[256,2048]{1,0:T(8,128)(2,1)} %refs_0_.1, f32[256,256]{1,0:T(8,128)} %broadcast_in_dim.2.refs_1_, bf16[8192,256]{1,0:T(8,128)(2,1)} %refs_3_.3), custom_call_target="tpu_custom_call" | custom-call | flops 268435456 | bytes 3145728 | tf_op jit(solution)/shard_map/absorb/pallas_call | solution.py:140
  25.5 1.4 %constant_dynamic-slice_fusion.3.refs_4_ = bf16[2048,256]{1,0:T(8,128)(2,1)S(1)} fusion(bf16[8192,256]{1,0:T(8,128)(2,1)} %refs_3_.3, s32[]{:T(128)S(6)} %select_n.57), kind=kLoop, calls=%fused_computation.12 | loop fusion | bytes 2097156 | tf_op jit(solution)/shard_map/dynamic_slice | solution.py:563
  26.8 0.8 fusion.1.refs_5_
  27.7 1.8 %collective-permute-done.refs_0_ = bf16[256,2048]{1,0:T(8,128)(2,1)} collective-permute-done((bf16[256,2048]{1,0:T(8,128)(2,1)}, bf16[256,2048]{1,0:T(8,128)(2,1)}, u32[]{:S(2)}, u32[]{:S(2)}) %collective-permute-start) | collective-permute-done | bytes 1048608 | tf_op jit(solution)/shard_map/ppermute | solution.py:580
  29.4 7.5 %collective-permute-done.1.refs_0_ = bf16[256,2048]{1,0:T(8,128)(2,1)} collective-permute-done((bf16[256,2048]{1,0:T(8,128)(2,1)}, bf16[256,2048]{1,0:T(8,128)(2,1)}, u32[]{:S(2)}, u32[]{:S(2)}) %collective-permute-start.1) | collective-permute-done | bytes 1048608 | tf_op jit(solution)/shard_map/ppermute | solution.py:579
  36.9 1.6 %collective-permute-start.2 = (bf16[256,2048]{1,0:T(8,128)(2,1)}, bf16[256,2048]{1,0:T(8,128)(2,1)}, u32[]{:S(2)}, u32[]{:S(2)}) collective-permute-start(bf16[256,2048]{1,0:T(8,128)(2,1)} %collective-permute-done.refs_0_), channel_id=1, source_target_pairs={{1,2},{2,3},{5,6},{6,7},{9,10},{10,11},{13,14},{14,15},{17,18},{18... | collective-permute-start | bytes 3145736 | tf_op jit(solution)/shard_map/ppermute | solution.py:580
  38.6 1.3 collective-permute-start.3
  39.9 3.3 %collective-permute-done.5 = bf16[256,256]{1,0:T(8,128)(2,1)S(1)} collective-permute-done((bf16[256,256]{1,0:T(8,128)(2,1)S(1)}, bf16[256,256]{1,0:T(8,128)(2,1)S(1)}, u32[]{:S(2)}, u32[]{:S(2)}) %collective-permute-start.5) | collective-permute-done | bytes 131104 | tf_op jit(solution)/shard_map/ppermute | solution.py:545
  43.2 1.0 pad_maximum_fusion.1
  44.2 1.5 %collective-permute-start.8 = (bf16[1024,256]{1,0:T(8,128)(2,1)S(1)}, bf16[1024,256]{1,0:T(8,128)(2,1)S(1)}, u32[]{:S(2)}, u32[]{:S(2)}) collective-permute-start(bf16[1024,256]{1,0:T(8,128)(2,1)S(1)} %copy-done), channel_id=1, source_target_pairs={{0,16},{4,20},{8,24},{12,28},{16,0},{20,4},{24,8},{28,12},{1,17},{... | collective-permute-start | bytes 1572872 | tf_op jit(solution)/shard_map/ppermute | solution.py:376
  46.4 0.7 constant_dynamic-update-slice_fusion.1
  47.7 1.5 %collective-permute-start.7 = (bf16[768,256]{1,0:T(8,128)(2,1)}, bf16[768,256]{1,0:T(8,128)(2,1)S(1)}, u32[]{:S(2)}, u32[]{:S(2)}) collective-permute-start(bf16[768,256]{1,0:T(8,128)(2,1)} %constant_dynamic-update-slice_fusion.refs_5_), channel_id=1, source_target_pairs={{0,8},{4,12},{8,0},{12,4},{16,24},{20,28},{24,16},{28,20},{1,9},{5... | collective-permute-start | bytes 1179656 | tf_op jit(solution)/shard_map/ppermute | solution.py:376
  49.2 0.7 pad_add_fusion
  49.9 4.2 %absorb.5 = (f32[256,256]{1,0:T(8,128)}, bf16[32,2048,256]{2,1,0:T(8,128)(2,1)}) custom-call(s32[3]{0:T(128)} %get-tuple-element.126.place, bf16[256,2048]{1,0:T(8,128)(2,1)} %collective-permute-done.refs_0_, f32[256,256]{1,0:T(8,128)} %get-tuple-element.73.refs_1_, bf16[8192,256]{1,0:T(8,128)(2,1)} %refs_3_.3, ...), custom_call_target="tpu_custom_call", output_to_operand_aliasing={{1}: (4, {})} | custom-call | flops 268435456 | bytes 3145728 | tf_op jit(solution)/shard_map/absorb/pallas_call | solution.py:140
  54.1 4.2 %absorb.6 = (f32[256,256]{1,0:T(8,128)}, bf16[32,2048,256]{2,1,0:T(8,128)(2,1)}) custom-call(s32[3]{0:T(128)} %get-tuple-element.127.place, bf16[256,2048]{1,0:T(8,128)(2,1)} %collective-permute-done.1.refs_0_, f32[256,256]{1,0:T(8,128)} %get-tuple-element.75.refs_1_, bf16[8192,256]{1,0:T(8,128)(2,1)} %refs_3_.3, ...), custom_call_target="tpu_custom_call", output_to_operand_aliasing={{1}: (4, {})} | custom-call | flops 268435456 | bytes 3145728 | tf_op jit(solution)/shard_map/absorb/pallas_call | solution.py:140
  58.4 0.8 collective-permute-done.7.refs_7_
  59.2 5.5 %collective-permute-done.3.refs_1_ = bf16[256,2048]{1,0:T(8,128)(2,1)} collective-permute-done((bf16[256,2048]{1,0:T(8,128)(2,1)}, bf16[256,2048]{1,0:T(8,128)(2,1)}, u32[]{:S(2)}, u32[]{:S(2)}) %collective-permute-start.3) | collective-permute-done | bytes 1048608 | tf_op jit(solution)/shard_map/ppermute | solution.py:579
  64.7 1.8 %collective-permute-start.10 = (bf16[256,2048]{1,0:T(8,128)(2,1)}, bf16[256,2048]{1,0:T(8,128)(2,1)}, u32[]{:S(2)}, u32[]{:S(2)}) collective-permute-start(bf16[256,2048]{1,0:T(8,128)(2,1)} %collective-permute-done.2.refs_0_), channel_id=1, source_target_pairs={{2,3},{6,7},{10,11},{14,15},{18,19},{22,23},{26,27},{30,31}} | collective-permute-start | bytes 3145736 | tf_op jit(solution)/shard_map/ppermute | solution.py:580
  66.5 1.5 %collective-permute-start.11 = (bf16[256,2048]{1,0:T(8,128)(2,1)}, bf16[256,2048]{1,0:T(8,128)(2,1)}, u32[]{:S(2)}, u32[]{:S(2)}) collective-permute-start(bf16[256,2048]{1,0:T(8,128)(2,1)} %collective-permute-done.3.refs_1_), channel_id=1, source_target_pairs={{1,0},{5,4},{9,8},{13,12},{17,16},{21,20},{25,24},{29,28}} | collective-permute-start | bytes 3145736 | tf_op jit(solution)/shard_map/ppermute | solution.py:579
  68.0 1.0 pad_maximum_fusion
  69.0 1.5 %collective-permute-start.12 = (bf16[2048,256]{1,0:T(8,128)(2,1)}, bf16[2048,256]{1,0:T(8,128)(2,1)}, u32[]{:S(2)}, u32[]{:S(2)}) collective-permute-start(bf16[2048,256]{1,0:T(8,128)(2,1)} %pad_maximum_fusion), channel_id=1, source_target_pairs={{0,8},{4,12},{8,0},{12,4},{16,24},{20,28},{24,16},{28,20},{1,9},{5... | collective-permute-start | bytes 3145736 | tf_op jit(solution)/shard_map/ppermute | solution.py:376
  70.5 0.9 pad_maximum_fusion.2
  71.4 1.5 %collective-permute-start.13 = (bf16[1536,256]{1,0:T(8,128)(2,1)}, bf16[1536,256]{1,0:T(8,128)(2,1)}, u32[]{:S(2)}, u32[]{:S(2)}) collective-permute-start(bf16[1536,256]{1,0:T(8,128)(2,1)} %pad_maximum_fusion.2), channel_id=1, source_target_pairs={{0,16},{4,20},{8,24},{12,28},{16,0},{20,4},{24,8},{28,12},{1,17},{... | collective-permute-start | bytes 2359304 | tf_op jit(solution)/shard_map/ppermute | solution.py:376
  73.0 0.8 copy-done.3
  74.6 4.3 %absorb.7 = (f32[256,256]{1,0:T(8,128)}, bf16[32,2048,256]{2,1,0:T(8,128)(2,1)}) custom-call(s32[3]{0:T(128)} %pad_add_fusion.4.place, bf16[256,2048]{1,0:T(8,128)(2,1)} %collective-permute-done.2.refs_0_, bf16[256,2048]{1,0:T(8,128)(2,1)} %collective-permute-done.3.refs_1_, f32[256,256]{1,0:T(8,128)} %get-tuple-element.81.refs_2_, ...), custom_call_target="tpu_custom_call", output_to_operand_aliasing={{1}: (5, {})} | custom-call | flops 268435456 | bytes 3145728 | tf_op jit(solution)/shard_map/absorb/pallas_call | solution.py:140
  78.9 1.9 %place_rows.2.refs_2_ = bf16[8192,256]{1,0:T(8,128)(2,1)} custom-call(s32[4]{0:T(128)S(1)} %broadcast_xor_fusion.2.place, bf16[1024,256]{1,0:T(8,128)(2,1)S(1)} %copy-done, bf16[1792,256]{1,0:T(8,128)(2,1)S(1)} %collective-permute-done.9.refs_1_.refs_6_, bf16[1024,256]{1,0:T(8,128)(2,1)S(1)} %collective-permute-done.8.refs_2_, bf16[1024,256]{1,0:T(8,128)(2,1)S(1)} %copy-done.4), custom_call_target="tpu_custom_call" | custom-call | bytes 4194304 | tf_op jit(solution)/shard_map/place_rows/pallas_call | solution.py:492
  80.8 10.9 %collective-permute-done.13.refs_9_ = bf16[1536,256]{1,0:T(8,128)(2,1)} collective-permute-done((bf16[1536,256]{1,0:T(8,128)(2,1)}, bf16[1536,256]{1,0:T(8,128)(2,1)}, u32[]{:S(2)}, u32[]{:S(2)}) %collective-permute-start.13) | collective-permute-done | bytes 786464 | tf_op jit(solution)/shard_map/ppermute | solution.py:376
  91.7 1.3 collective-permute-done.11.refs_1_
  93.5 9.7 %attend.1 = (bf16[32,2048,256]{2,1,0:T(8,128)(2,1)}, bf16[256,1024]{1,0:T(8,128)(2,1)}, bf16[256,256]{1,0:T(8,128)(2,1)}, bf16[4,1024,128]{2,1,0:T(8,128)(2,1)}, bf16[4,1024,128]{2,1,0:T(8,128)(2,1)}) custom-call(s32[3]{0:T(128)} %get-tuple-element.129.place, s32[5]{0:T(128)} %stack.93.order, ...), custom_call_target="tpu_custom_call", output_to_operand_aliasing={{0}: (6, {})} | custom-call | flops 805306368 | bytes 2097152 | tf_op jit(solution)/shard_map/attend/pallas_call | solution.py:235
  103.8 0.9 copy-done.1
  104.8 2.5 %weight_send.1 = (f32[2,1024,128]{2,1,0:T(8,128)S(1)}, f32[2,1024,128]{2,1,0:T(8,128)S(1)}) custom-call(s32[5]{0:T(128)S(1)} %stack.95.place, bf16[32,2048,256]{2,1,0:T(8,128)(2,1)} %get-tuple-element.92.held, bf16[256,256]{1,0:T(8,128)(2,1)S(1)} %copy-done.1), custom_call_target="tpu_custom_call" | custom-call | flops 268435456 | bytes 2097152 | tf_op jit(solution)/shard_map/weight_send/pallas_call | solution.py:334
  107.5 1.6 %collective-permute-start.19 = (bf16[2,1024,128]{2,1,0:T(8,128)(2,1)S(1)}, bf16[2,1024,128]{2,1,0:T(8,128)(2,1)S(1)}, u32[]{:S(2)}, u32[]{:S(2)}) collective-permute-start(bf16[2,1024,128]{2,1,0:T(8,128)(2,1)S(1)} %get-tuple-element.100), channel_id=1, source_target_pairs={{0,8},{4,12},{8,0},{12,4},{16,24},{20,28},{24,16},{28,20},{1,9},{5... | collective-permute-start | bytes 1572872 | tf_op jit(solution)/shard_map/ppermute | solution.py:376
  109.0 1.5 %collective-permute-start.20 = (bf16[2,1024,128]{2,1,0:T(8,128)(2,1)S(1)}, bf16[2,1024,128]{2,1,0:T(8,128)(2,1)S(1)}, u32[]{:S(2)}, u32[]{:S(2)}) collective-permute-start(bf16[2,1024,128]{2,1,0:T(8,128)(2,1)S(1)} %get-tuple-element.101), channel_id=1, source_target_pairs={{0,16},{4,20},{8,24},{12,28},{16,0},{20,4},{24,8},{28,12},{1,17},{... | collective-permute-start | bytes 1572872 | tf_op jit(solution)/shard_map/ppermute | solution.py:376
  110.5 3.8 %collective-permute-start.21 = (bf16[256,256]{1,0:T(8,128)(2,1)S(1)}, bf16[256,256]{1,0:T(8,128)(2,1)S(1)}, u32[]{:S(2)}, u32[]{:S(2)}) collective-permute-start(bf16[256,256]{1,0:T(8,128)(2,1)S(1)} %copy-done.2), channel_id=1, source_target_pairs={{0,1},{1,0},{2,3},{3,2},{4,5},{5,4},{6,7},{7,6},{8,9},{9,8},{10,11... | collective-permute-start | bytes 393224 | tf_op jit(solution)/shard_map/ppermute | solution.py:545
  114.3 2.4 %collective-permute-start.23 = (bf16[256,256]{1,0:T(8,128)(2,1)S(1)}, bf16[256,256]{1,0:T(8,128)(2,1)S(1)}, u32[]{:S(2)}, u32[]{:S(2)}) collective-permute-start(bf16[256,256]{1,0:T(8,128)(2,1)S(1)} %copy-done.2), channel_id=1, source_target_pairs={{0,3},{1,2},{2,1},{3,0},{4,7},{5,6},{6,5},{7,4},{8,11},{9,10},{10,... | collective-permute-start | bytes 393224 | tf_op jit(solution)/shard_map/ppermute | solution.py:545
  116.7 2.6 %place_rows.3 = bf16[8192,256]{1,0:T(8,128)(2,1)} custom-call(s32[4]{0:T(128)S(1)} %broadcast_xor_fusion.1.place, bf16[2048,256]{1,0:T(8,128)(2,1)} %collective-permute-done.12.refs_0_, bf16[2048,256]{1,0:T(8,128)(2,1)S(1)} %collective-permute-done.16.refs_1_, bf16[8192,256]{1,0:T(8,128)(2,1)} %place_rows.2.refs_2_), custom_call_target="tpu_custom_call", output_to_operand_aliasing={{}: (3, {})} | custom-call | bytes 4194304 | tf_op jit(solution)/shard_map/place_rows/pallas_call | solution.py:492
  119.3 2.5 %weight_keep.1 = (f32[2,1024,128]{2,1,0:T(8,128)S(1)}, f32[2,1024,128]{2,1,0:T(8,128)S(1)}) custom-call(s32[5]{0:T(128)S(1)} %stack.95.place, bf16[32,2048,256]{2,1,0:T(8,128)(2,1)} %get-tuple-element.92.held, bf16[256,256]{1,0:T(8,128)(2,1)S(1)} %copy-done.2, bf16[4,1024,128]{2,1,0:T(8,128)(2,1)S(1)} %collective-permute-done.24.refs_0_), custom_call_target="tpu_custom_call" | custom-call | flops 268435456 | bytes 2097152 | tf_op jit(solution)/shard_map/weight_keep/pallas_call | solution.py:334
  121.8 4.4 %collective-permute-done.22.refs_2_ = bf16[256,256]{1,0:T(8,128)(2,1)S(1)} collective-permute-done((bf16[256,256]{1,0:T(8,128)(2,1)S(1)}, bf16[256,256]{1,0:T(8,128)(2,1)S(1)}, u32[]{:S(2)}, u32[]{:S(2)}) %collective-permute-start.22) | collective-permute-done | bytes 131104 | tf_op jit(solution)/shard_map/ppermute | solution.py:545
  127.5 3.9 %input_gradient.1 = bf16[256,2048]{1,0:T(8,128)(2,1)} custom-call(s32[8]{0:T(128)S(1)} %broadcast_xor_fusion.place, bf16[256,256]{1,0:T(8,128)(2,1)S(1)} %copy-done.2, bf16[256,256]{1,0:T(8,128)(2,1)S(1)} %collective-permute-done.21.refs_1_, bf16[256,256]{1,0:T(8,128)(2,1)S(1)} %collective-permute-done.22.refs_2_, ...), custom_call_target="tpu_custom_call" | custom-call | flops 1073741824 | bytes 6291456 | tf_op jit(solution)/shard_map/input_gradient/pallas_call | solution.py:73
  131.5 1.4 %collective-permute-done.25.last_a = bf16[1024,128]{1,0:T(8,128)(2,1)S(1)} collective-permute-done((bf16[1024,128]{1,0:T(8,128)(2,1)S(1)}, bf16[1024,128]{1,0:T(8,128)(2,1)S(1)}, u32[]{:S(2)}, u32[]{:S(2)}) %collective-permute-start.25) | collective-permute-done | bytes 262176 | tf_op jit(solution)/shard_map/ppermute | solution.py:376
  133.3 1.1 weight_finish.1
  (64 shorter events, 6.6 us)
Async XLA Ops:
  0.6 28.8 %collective-permute-start = (bf16[256,2048]{1,0:T(8,128)(2,1)}, bf16[256,2048]{1,0:T(8,128)(2,1)}, u32[]{:S(2)}, u32[]{:S(2)}) collective-permute-start(bf16[256,2048]{1,0:T(8,128)(2,1)} %refs_0_.1), channel_id=1, source_target_pairs={{0,1},{1,2},{2,3},{4,5},{5,6},{6,7},{8,9},{9,10},{10,11},{12,13},{... | collective-permute-start | bytes 3145736 | tf_op jit(solution)/shard_map/ppermute | solution.py:580
  6.6 30.4 %collective-permute-start.1 = (bf16[256,2048]{1,0:T(8,128)(2,1)}, bf16[256,2048]{1,0:T(8,128)(2,1)}, u32[]{:S(2)}, u32[]{:S(2)}) collective-permute-start(bf16[256,2048]{1,0:T(8,128)(2,1)} %refs_0_.1), channel_id=1, source_target_pairs={{1,0},{2,1},{3,2},{5,4},{6,5},{7,6},{9,8},{10,9},{11,10},{13,12},{... | collective-permute-start | bytes 3145736 | tf_op jit(solution)/shard_map/ppermute | solution.py:579
  8.9 30.9 %collective-permute-start.4 = (bf16[256,256]{1,0:T(8,128)(2,1)S(1)}, bf16[256,256]{1,0:T(8,128)(2,1)S(1)}, u32[]{:S(2)}, u32[]{:S(2)}) collective-permute-start(bf16[256,256]{1,0:T(8,128)(2,1)S(1)} %get-tuple-element.125), channel_id=1, source_target_pairs={{0,1},{1,0},{2,3},{3,2},{4,5},{5,4},{6,7},{7,6},{8,9},{9,8},{10,11... | collective-permute-start | bytes 393224 | tf_op jit(solution)/shard_map/ppermute | solution.py:545
  11.7 31.5 %collective-permute-start.5 = (bf16[256,256]{1,0:T(8,128)(2,1)S(1)}, bf16[256,256]{1,0:T(8,128)(2,1)S(1)}, u32[]{:S(2)}, u32[]{:S(2)}) collective-permute-start(bf16[256,256]{1,0:T(8,128)(2,1)S(1)} %get-tuple-element.124), channel_id=1, source_target_pairs={{0,2},{1,3},{2,0},{3,1},{4,6},{5,7},{6,4},{7,5},{8,10},{9,11},{10,... | collective-permute-start | bytes 393224 | tf_op jit(solution)/shard_map/ppermute | solution.py:545
  14.2 29.0 %collective-permute-start.6 = (bf16[256,256]{1,0:T(8,128)(2,1)S(1)}, bf16[256,256]{1,0:T(8,128)(2,1)S(1)}, u32[]{:S(2)}, u32[]{:S(2)}) collective-permute-start(bf16[256,256]{1,0:T(8,128)(2,1)S(1)} %get-tuple-element.123), channel_id=1, source_target_pairs={{0,3},{1,2},{2,1},{3,0},{4,7},{5,6},{6,5},{7,4},{8,11},{9,10},{10,... | collective-permute-start | bytes 393224 | tf_op jit(solution)/shard_map/ppermute | solution.py:545
  25.4 1.4 %copy-start.9 = (s32[1,256]{1,0:T(1,128)S(1)}, s32[1,256]{1,0:T(1,128)}, u32[]{:S(2)}) copy-start(s32[1,256]{1,0:T(1,128)} %param.15) | copy-start | bytes 3076
  25.5 17.8 %copy-start = (bf16[1024,256]{1,0:T(8,128)(2,1)S(1)}, bf16[1024,256]{1,0:T(8,128)(2,1)}, u32[]{:S(2)}) copy-start(bf16[1024,256]{1,0:T(8,128)(2,1)} %get-tuple-element.78.refs_0_) | copy-start | bytes 1572868
  36.9 22.3 %collective-permute-start.2 = (bf16[256,2048]{1,0:T(8,128)(2,1)}, bf16[256,2048]{1,0:T(8,128)(2,1)}, u32[]{:S(2)}, u32[]{:S(2)}) collective-permute-start(bf16[256,2048]{1,0:T(8,128)(2,1)} %collective-permute-done.refs_0_), channel_id=1, source_target_pairs={{1,2},{2,3},{5,6},{6,7},{9,10},{10,11},{13,14},{14,15},{17,18},{18... | collective-permute-start | bytes 3145736 | tf_op jit(solution)/shard_map/ppermute | solution.py:580
  38.6 26.2 %collective-permute-start.3 = (bf16[256,2048]{1,0:T(8,128)(2,1)}, bf16[256,2048]{1,0:T(8,128)(2,1)}, u32[]{:S(2)}, u32[]{:S(2)}) collective-permute-start(bf16[256,2048]{1,0:T(8,128)(2,1)} %collective-permute-done.1.refs_0_), channel_id=1, source_target_pairs={{1,0},{2,1},{5,4},{6,5},{9,8},{10,9},{13,12},{14,13},{17,16},{18,1... | collective-permute-start | bytes 3145736 | tf_op jit(solution)/shard_map/ppermute | solution.py:579
  43.2 3.8 %copy-start.5 = (bf16[256,256]{1,0:T(8,128)(2,1)}, bf16[256,256]{1,0:T(8,128)(2,1)S(1)}, u32[]{:S(2)}) copy-start(bf16[256,256]{1,0:T(8,128)(2,1)S(1)} %collective-permute-done.5) | copy-start | bytes 393220
  43.2 3.8 %copy-start.7 = (bf16[256,256]{1,0:T(8,128)(2,1)}, bf16[256,256]{1,0:T(8,128)(2,1)S(1)}, u32[]{:S(2)}) copy-start(bf16[256,256]{1,0:T(8,128)(2,1)S(1)} %collective-permute-done.6) | copy-start | bytes 393220
  44.2 15.0 %collective-permute-start.9 = (bf16[1792,256]{1,0:T(8,128)(2,1)}, bf16[1792,256]{1,0:T(8,128)(2,1)S(1)}, u32[]{:S(2)}, u32[]{:S(2)}) collective-permute-start(bf16[1792,256]{1,0:T(8,128)(2,1)} %pad_maximum_fusion.1), channel_id=1, source_target_pairs={{0,4},{4,0},{8,12},{12,8},{16,20},{20,16},{24,28},{28,24},{1,5},{5... | collective-permute-start | bytes 2752520 | tf_op jit(solution)/shard_map/ppermute | solution.py:376
  44.2 15.0 %collective-permute-start.8 = (bf16[1024,256]{1,0:T(8,128)(2,1)S(1)}, bf16[1024,256]{1,0:T(8,128)(2,1)S(1)}, u32[]{:S(2)}, u32[]{:S(2)}) collective-permute-start(bf16[1024,256]{1,0:T(8,128)(2,1)S(1)} %copy-done), channel_id=1, source_target_pairs={{0,16},{4,20},{8,24},{12,28},{16,0},{20,4},{24,8},{28,12},{1,17},{... | collective-permute-start | bytes 1572872 | tf_op jit(solution)/shard_map/ppermute | solution.py:376
  47.7 11.5 %collective-permute-start.7 = (bf16[768,256]{1,0:T(8,128)(2,1)}, bf16[768,256]{1,0:T(8,128)(2,1)S(1)}, u32[]{:S(2)}, u32[]{:S(2)}) collective-permute-start(bf16[768,256]{1,0:T(8,128)(2,1)} %constant_dynamic-update-slice_fusion.refs_5_), channel_id=1, source_target_pairs={{0,8},{4,12},{8,0},{12,4},{16,24},{20,28},{24,16},{28,20},{1,9},{5... | collective-permute-start | bytes 1179656 | tf_op jit(solution)/shard_map/ppermute | solution.py:376
  58.4 12.1 %copy-start.6 = (bf16[256,256]{1,0:T(8,128)(2,1)S(1)}, bf16[256,256]{1,0:T(8,128)(2,1)}, u32[]{:S(2)}) copy-start(bf16[256,256]{1,0:T(8,128)(2,1)} %copy-done.5) | copy-start | bytes 393220
  58.4 12.1 %copy-start.8 = (bf16[256,256]{1,0:T(8,128)(2,1)S(1)}, bf16[256,256]{1,0:T(8,128)(2,1)}, u32[]{:S(2)}) copy-start(bf16[256,256]{1,0:T(8,128)(2,1)} %copy-done.7) | copy-start | bytes 393220
  64.7 9.8 %copy-start.12 = (s32[4]{0:T(128)S(1)}, s32[4]{0:T(128)}, u32[]{:S(2)}) copy-start(s32[4]{0:T(128)} %constant.72.clone) | copy-start | bytes 52
  64.7 27.0 %collective-permute-start.10 = (bf16[256,2048]{1,0:T(8,128)(2,1)}, bf16[256,2048]{1,0:T(8,128)(2,1)}, u32[]{:S(2)}, u32[]{:S(2)}) collective-permute-start(bf16[256,2048]{1,0:T(8,128)(2,1)} %collective-permute-done.2.refs_0_), channel_id=1, source_target_pairs={{2,3},{6,7},{10,11},{14,15},{18,19},{22,23},{26,27},{30,31}} | collective-permute-start | bytes 3145736 | tf_op jit(solution)/shard_map/ppermute | solution.py:580
  66.5 26.5 %collective-permute-start.11 = (bf16[256,2048]{1,0:T(8,128)(2,1)}, bf16[256,2048]{1,0:T(8,128)(2,1)}, u32[]{:S(2)}, u32[]{:S(2)}) collective-permute-start(bf16[256,2048]{1,0:T(8,128)(2,1)} %collective-permute-done.3.refs_1_), channel_id=1, source_target_pairs={{1,0},{5,4},{9,8},{13,12},{17,16},{21,20},{25,24},{29,28}} | collective-permute-start | bytes 3145736 | tf_op jit(solution)/shard_map/ppermute | solution.py:579
  69.0 24.0 %collective-permute-start.12 = (bf16[2048,256]{1,0:T(8,128)(2,1)}, bf16[2048,256]{1,0:T(8,128)(2,1)}, u32[]{:S(2)}, u32[]{:S(2)}) collective-permute-start(bf16[2048,256]{1,0:T(8,128)(2,1)} %pad_maximum_fusion), channel_id=1, source_target_pairs={{0,8},{4,12},{8,0},{12,4},{16,24},{20,28},{24,16},{28,20},{1,9},{5... | collective-permute-start | bytes 3145736 | tf_op jit(solution)/shard_map/ppermute | solution.py:376
  70.5 2.5 %collective-permute-start.15 = (bf16[1024,256]{1,0:T(8,128)(2,1)S(1)}, bf16[1024,256]{1,0:T(8,128)(2,1)S(1)}, u32[]{:S(2)}, u32[]{:S(2)}) collective-permute-start(bf16[1024,256]{1,0:T(8,128)(2,1)S(1)} %collective-permute-done.8.refs_2_), channel_id=1, source_target_pairs={{0,4},{4,0},{8,12},{12,8},{16,20},{20,16},{24,28},{28,24},{1,5},{5... | collective-permute-start | bytes 1572872 | tf_op jit(solution)/shard_map/ppermute | solution.py:376
  71.4 20.3 %collective-permute-start.13 = (bf16[1536,256]{1,0:T(8,128)(2,1)}, bf16[1536,256]{1,0:T(8,128)(2,1)}, u32[]{:S(2)}, u32[]{:S(2)}) collective-permute-start(bf16[1536,256]{1,0:T(8,128)(2,1)} %pad_maximum_fusion.2), channel_id=1, source_target_pairs={{0,16},{4,20},{8,24},{12,28},{16,0},{20,4},{24,8},{28,12},{1,17},{... | collective-permute-start | bytes 2359304 | tf_op jit(solution)/shard_map/ppermute | solution.py:376
  73.0 0.8 copy-start.3
  73.8 7.0 %collective-permute-start.14 = (bf16[768,256]{1,0:T(8,128)(2,1)S(1)}, bf16[768,256]{1,0:T(8,128)(2,1)}, u32[]{:S(2)}, u32[]{:S(2)}) collective-permute-start(bf16[768,256]{1,0:T(8,128)(2,1)S(1)} %collective-permute-done.7.refs_7_), channel_id=1, source_target_pairs={{0,4},{4,0},{8,12},{12,8},{16,20},{20,16},{24,28},{28,24},{1,5},{5... | collective-permute-start | bytes 1179656 | tf_op jit(solution)/shard_map/ppermute | solution.py:376
  74.6 4.3 %copy-start.4 = (bf16[1024,256]{1,0:T(8,128)(2,1)S(1)}, bf16[1024,256]{1,0:T(8,128)(2,1)}, u32[]{:S(2)}) copy-start(bf16[1024,256]{1,0:T(8,128)(2,1)} %copy-done.3) | copy-start | bytes 1572868
  93.0 10.3 %collective-permute-start.16 = (bf16[2048,256]{1,0:T(8,128)(2,1)}, bf16[2048,256]{1,0:T(8,128)(2,1)S(1)}, u32[]{:S(2)}, u32[]{:S(2)}) collective-permute-start(bf16[2048,256]{1,0:T(8,128)(2,1)} %collective-permute-done.12.refs_0_), channel_id=1, source_target_pairs={{0,4},{4,0},{8,12},{12,8},{16,20},{20,16},{24,28},{28,24},{1,5},{5... | collective-permute-start | bytes 3145736 | tf_op jit(solution)/shard_map/ppermute | solution.py:376
  93.0 10.2 %collective-permute-start.17 = (bf16[1536,256]{1,0:T(8,128)(2,1)}, bf16[1536,256]{1,0:T(8,128)(2,1)}, u32[]{:S(2)}, u32[]{:S(2)}) collective-permute-start(bf16[1536,256]{1,0:T(8,128)(2,1)} %collective-permute-done.13.refs_9_), channel_id=1, source_target_pairs={{0,4},{4,0},{8,12},{12,8},{16,20},{20,16},{24,28},{28,24},{1,5},{5... | collective-permute-start | bytes 2359304 | tf_op jit(solution)/shard_map/ppermute | solution.py:376
  103.3 4.0 %collective-permute-start.18 = (bf16[4,1024,128]{2,1,0:T(8,128)(2,1)}, bf16[4,1024,128]{2,1,0:T(8,128)(2,1)S(1)}, u32[]{:S(2)}, u32[]{:S(2)}) collective-permute-start(bf16[4,1024,128]{2,1,0:T(8,128)(2,1)} %get-tuple-element.99), channel_id=1, source_target_pairs={{0,4},{4,0},{8,12},{12,8},{16,20},{20,16},{24,28},{28,24},{1,5},{5... | collective-permute-start | bytes 3145736 | tf_op jit(solution)/shard_map/ppermute | solution.py:376
  103.3 11.0 %collective-permute-start.24 = (bf16[4,1024,128]{2,1,0:T(8,128)(2,1)}, bf16[4,1024,128]{2,1,0:T(8,128)(2,1)S(1)}, u32[]{:S(2)}, u32[]{:S(2)}) collective-permute-start(bf16[4,1024,128]{2,1,0:T(8,128)(2,1)} %get-tuple-element.105), channel_id=1, source_target_pairs={{0,4},{4,0},{8,12},{12,8},{16,20},{20,16},{24,28},{28,24},{1,5},{5... | collective-permute-start | bytes 3145736 | tf_op jit(solution)/shard_map/ppermute | solution.py:376
  103.8 0.9 copy-start.1
  107.2 3.3 %copy-start.2 = (bf16[256,256]{1,0:T(8,128)(2,1)S(1)}, bf16[256,256]{1,0:T(8,128)(2,1)}, u32[]{:S(2)}) copy-start(bf16[256,256]{1,0:T(8,128)(2,1)} %get-tuple-element.112.d_projected.refs_0_) | copy-start | bytes 393220
  107.3 9.4 %copy-start.11 = (s32[4]{0:T(128)S(1)}, s32[4]{0:T(128)}, u32[]{:S(2)}) copy-start(s32[4]{0:T(128)} %constant.73.clone) | copy-start | bytes 52
  107.5 18.8 %collective-permute-start.19 = (bf16[2,1024,128]{2,1,0:T(8,128)(2,1)S(1)}, bf16[2,1024,128]{2,1,0:T(8,128)(2,1)S(1)}, u32[]{:S(2)}, u32[]{:S(2)}) collective-permute-start(bf16[2,1024,128]{2,1,0:T(8,128)(2,1)S(1)} %get-tuple-element.100), channel_id=1, source_target_pairs={{0,8},{4,12},{8,0},{12,4},{16,24},{20,28},{24,16},{28,20},{1,9},{5... | collective-permute-start | bytes 1572872 | tf_op jit(solution)/shard_map/ppermute | solution.py:376
  109.0 17.2 %collective-permute-start.20 = (bf16[2,1024,128]{2,1,0:T(8,128)(2,1)S(1)}, bf16[2,1024,128]{2,1,0:T(8,128)(2,1)S(1)}, u32[]{:S(2)}, u32[]{:S(2)}) collective-permute-start(bf16[2,1024,128]{2,1,0:T(8,128)(2,1)S(1)} %get-tuple-element.101), channel_id=1, source_target_pairs={{0,16},{4,20},{8,24},{12,28},{16,0},{20,4},{24,8},{28,12},{1,17},{... | collective-permute-start | bytes 1572872 | tf_op jit(solution)/shard_map/ppermute | solution.py:376
  110.5 11.3 %collective-permute-start.21 = (bf16[256,256]{1,0:T(8,128)(2,1)S(1)}, bf16[256,256]{1,0:T(8,128)(2,1)S(1)}, u32[]{:S(2)}, u32[]{:S(2)}) collective-permute-start(bf16[256,256]{1,0:T(8,128)(2,1)S(1)} %copy-done.2), channel_id=1, source_target_pairs={{0,1},{1,0},{2,3},{3,2},{4,5},{5,4},{6,7},{7,6},{8,9},{9,8},{10,11... | collective-permute-start | bytes 393224 | tf_op jit(solution)/shard_map/ppermute | solution.py:545
  114.3 11.9 %collective-permute-start.22 = (bf16[256,256]{1,0:T(8,128)(2,1)S(1)}, bf16[256,256]{1,0:T(8,128)(2,1)S(1)}, u32[]{:S(2)}, u32[]{:S(2)}) collective-permute-start(bf16[256,256]{1,0:T(8,128)(2,1)S(1)} %copy-done.2), channel_id=1, source_target_pairs={{0,2},{1,3},{2,0},{3,1},{4,6},{5,7},{6,4},{7,5},{8,10},{9,11},{10,... | collective-permute-start | bytes 393224 | tf_op jit(solution)/shard_map/ppermute | solution.py:545
  114.3 11.9 %collective-permute-start.23 = (bf16[256,256]{1,0:T(8,128)(2,1)S(1)}, bf16[256,256]{1,0:T(8,128)(2,1)S(1)}, u32[]{:S(2)}, u32[]{:S(2)}) collective-permute-start(bf16[256,256]{1,0:T(8,128)(2,1)S(1)} %copy-done.2), channel_id=1, source_target_pairs={{0,3},{1,2},{2,1},{3,0},{4,7},{5,6},{6,5},{7,4},{8,11},{9,10},{10,... | collective-permute-start | bytes 393224 | tf_op jit(solution)/shard_map/ppermute | solution.py:545
  121.8 5.7 %copy-start.10 = (s32[8]{0:T(128)S(1)}, s32[8]{0:T(128)}, u32[]{:S(2)}) copy-start(s32[8]{0:T(128)} %constant.74.clone) | copy-start | bytes 100
  126.4 6.5 %collective-permute-start.25 = (bf16[1024,128]{1,0:T(8,128)(2,1)S(1)}, bf16[1024,128]{1,0:T(8,128)(2,1)S(1)}, u32[]{:S(2)}, u32[]{:S(2)}) collective-permute-start(bf16[1024,128]{1,0:T(8,128)(2,1)S(1)} %get-tuple-element.110), channel_id=1, source_target_pairs={{0,16},{4,20},{8,24},{12,28},{16,0},{20,4},{24,8},{28,12},{1,17},{... | collective-permute-start | bytes 786440 | tf_op jit(solution)/shard_map/ppermute | solution.py:376
  126.9 6.4 %collective-permute-start.26 = (bf16[1024,128]{1,0:T(8,128)(2,1)S(1)}, bf16[1024,128]{1,0:T(8,128)(2,1)S(1)}, u32[]{:S(2)}, u32[]{:S(2)}) collective-permute-start(bf16[1024,128]{1,0:T(8,128)(2,1)S(1)} %get-tuple-element.111), channel_id=1, source_target_pairs={{0,8},{4,12},{8,0},{12,4},{16,24},{20,28},{24,16},{28,20},{1,9},{5... | collective-permute-start | bytes 786440 | tf_op jit(solution)/shard_map/ppermute | solution.py:376

commit v13 on v12

--- a/solution.py
+++ b/solution.py
@@ -398,7 +398,8 @@
     keep_a, keep_b = weight_parts(
         held, d_projected, order, KEPT, [kept], jnp.float32, "weight_keep"
     )
-    got_a, got_b, pieces, beside = lax.optimization_barrier((got_a, got_b, pieces, beside))
+    pieces, got_a, got_b, beside = lax.optimization_barrier((pieces[::-1], got_a, got_b, beside))
+    pieces = pieces[::-1]
 
     small = jax.ShapeDtypeStruct((rows, cols // 2), jnp.bfloat16)
     arrays = [keep_a, got_a, keep_b, got_b]
@@ -581,18 +582,18 @@
                 from_low, "tensor", [(z, z + 1) for z in range(s - 1, n_z - 1)]
             )
             if tuned and s == 1:
-                from_low, from_high, held, allowed, orders, here = lax.optimization_barrier(
-                    (from_low, from_high, held, allowed, orders, here)
+                from_high, from_low, held, allowed, orders, here = lax.optimization_barrier(
+                    (from_high, from_low, held, allowed, orders, here)
                 )
             elif tuned and s == 2:
-                from_low, from_high, held, gather.got = lax.optimization_barrier(
-                    (from_low, from_high, held, gather.first())
+                from_high, from_low, held, gather.got = lax.optimization_barrier(
+                    (from_high, from_low, held, gather.first())
                 )
             elif tuned:
                 packs, swapped = gather.second()
                 laid = gather.lay(swapped, cached.shape[0])
-                from_low, from_high, held, gather.packs, gather.swapped, laid = (
-                    lax.optimization_barrier((from_low, from_high, held, packs, swapped, laid))
+                from_high, from_low, held, gather.packs, gather.swapped, laid = (
+                    lax.optimization_barrier((from_high, from_low, held, packs, swapped, laid))
                 )
             chunks, which = [from_low, from_high], (me_z < s).astype(jnp.int32)
             index = jnp.where(me_z < s, high, low)
@@ -606,7 +607,8 @@
             chunks, which, index, cached, total, held, queries, d_out, allowed, orders[0], n_z
         )
 
-        pieces = [d_projected] + [pair(d_projected, s) for s in range(1, n_z)]
+        pieces = [pair(d_projected, s) for s in range(n_z - 1, 0, -1)]
+        pieces = [d_projected] + pieces[::-1]
         if tuned:
             sent, gather.packs_other = lax.optimization_barrier((sent, gather.third()))
             new_cache = gather.lay_rest(laid)

time: 135 us -> 133 us (0.985)
  waiting for transfers between devices: 37.5 us -> 34.3 us
  starting transfers between devices: 36.3 us -> 37.8 us
    ppermute x3, waiting for transfers between devices: 14.3 us -> 10 us  [body(): lax.ppermute(from_high, 'tensor', [(z + 1, z) for z in range(n_z - s)])]
where the time goes in v13:
time: 133 us
  Pallas kernels  46.4 us (35%)
  starting transfers between devices  37.8 us (28%)
  waiting for transfers between devices  34.3 us (26%)
  local copies, waits for them, and re-layouts  7.55 us (6%)
  other arithmetic  5.7 us (4%)
    pallas_call x4, Pallas kernels, absorb(): pl.pallas_call(functools.partial(absorb_kernel, len(chunks)), in_specs=[p...  17 us
    ppermute x15, waiting for transfers between devices, swap(): return lax.ppermute(value, 'dp', [(i, i ^ bit) for i in range(8)])  14.5 us
    ppermute x6, starting transfers between devices, pair(): return lax.ppermute(value, 'tensor', [(z, z ^ s) for z in range(n_z)])  12.4 us
    ppermute x15, starting transfers between devices, swap(): return lax.ppermute(value, 'dp', [(i, i ^ bit) for i in range(8)])  11.5 us
    ppermute x3, waiting for transfers between devices, body(): lax.ppermute(from_high, 'tensor', [(z + 1, z) for z in range(n_z - s)])  10 us
    ppermute x3, starting transfers between devices, body(): lax.ppermute(from_low, 'tensor', [(z, z + 1) for z in range(s - 1, n_z -...  9.86 us
    pallas_call x1, Pallas kernels, attend(): pl.pallas_call(functools.partial(attend_kernel, len(chunks)), in_specs=[p...  9.73 us
    ppermute x6, waiting for transfers between devices, pair(): return lax.ppermute(value, 'tensor', [(z, z ^ s) for z in range(n_z)])  9.07 us
  transfers between devices with their start and end apart: 27, of which 10 were waited for; matrix products, arithmetic and copies ran while one was open for 9% of the time, Pallas kernels for 34%

profile of v13, /device:TPU:0, one launch (start us, length us, event | category | flops | bytes accessed | tf_op | source)
XLA Modules:
  0.0 132.6 jit_solution(6180586425656204788)
XLA Ops:
  0.6 1.3 collective-permute-start
  1.9 6.6 %collective-permute-start.1 = (bf16[256,2048]{1,0:T(8,128)(2,1)}, bf16[256,2048]{1,0:T(8,128)(2,1)}, u32[]{:S(2)}, u32[]{:S(2)}) collective-permute-start(bf16[256,2048]{1,0:T(8,128)(2,1)} %refs_0_.1), channel_id=1, source_target_pairs={{0,1},{1,2},{2,3},{4,5},{5,6},{6,7},{8,9},{9,10},{10,11},{12,13},{... | collective-permute-start | bytes 3145736 | tf_op jit(solution)/shard_map/ppermute | solution.py:581
  8.5 1.1 constant_dynamic-slice_fusion
  9.6 1.1 collective-permute-start.4
  10.7 2.0 %collective-permute-start.5 = (bf16[256,256]{1,0:T(8,128)(2,1)S(1)}, bf16[256,256]{1,0:T(8,128)(2,1)S(1)}, u32[]{:S(2)}, u32[]{:S(2)}) collective-permute-start(bf16[256,256]{1,0:T(8,128)(2,1)S(1)} %get-tuple-element.124), channel_id=1, source_target_pairs={{0,2},{1,3},{2,0},{3,1},{4,6},{5,7},{6,4},{7,5},{8,10},{9,11},{10,... | collective-permute-start | bytes 393224 | tf_op jit(solution)/shard_map/ppermute | solution.py:546
  12.7 1.4 %collective-permute-start.6 = (bf16[256,256]{1,0:T(8,128)(2,1)S(1)}, bf16[256,256]{1,0:T(8,128)(2,1)S(1)}, u32[]{:S(2)}, u32[]{:S(2)}) collective-permute-start(bf16[256,256]{1,0:T(8,128)(2,1)S(1)} %get-tuple-element.123), channel_id=1, source_target_pairs={{0,3},{1,2},{2,1},{3,0},{4,7},{5,6},{6,5},{7,4},{8,11},{9,10},{10,... | collective-permute-start | bytes 393224 | tf_op jit(solution)/shard_map/ppermute | solution.py:546
  14.8 4.9 %optimizer.1 = (f32[1024,256]{1,0:T(8,128)}, f32[1024,256]{1,0:T(8,128)}, f32[1024,256]{1,0:T(8,128)}, bf16[1024,256]{1,0:T(8,128)(2,1)}) custom-call(s32[1]{0:T(128)} %bitcast.place, bf16[8192,256]{1,0:T(8,128)(2,1)} %refs_3_.3, f32[1024,256]{1,0:T(8,128)} %master.1, f32[1024,256]{1,0:T(8,128)} %moment.1, f32[1024,256]{1,0:T(8,128)} %second.1, f32[1024,256]{1,0:T(8,128)} %grad.1), custom_call_target="tpu_custom_call" | custom-call | flops 10485760 | bytes 8388608 | tf_op jit(solution)/shard_map/optimizer/pallas_call | solution.py:51
  20.4 0.7 broadcast_in_dim.2.refs_1_
  21.1 4.2 %absorb.4 = (f32[256,256]{1,0:T(8,128)}, bf16[32,2048,256]{2,1,0:T(8,128)(2,1)}) custom-call(s32[3]{0:T(128)} %get-tuple-element.128.place, bf16[256,2048]{1,0:T(8,128)(2,1)} %refs_0_.1, f32[256,256]{1,0:T(8,128)} %broadcast_in_dim.2.refs_1_, bf16[8192,256]{1,0:T(8,128)(2,1)} %refs_3_.3), custom_call_target="tpu_custom_call" | custom-call | flops 268435456 | bytes 3145728 | tf_op jit(solution)/shard_map/absorb/pallas_call | solution.py:140
  25.4 1.4 %constant_dynamic-slice_fusion.3.refs_4_ = bf16[2048,256]{1,0:T(8,128)(2,1)S(1)} fusion(bf16[8192,256]{1,0:T(8,128)(2,1)} %refs_3_.3, s32[]{:T(128)S(6)} %select_n.59), kind=kLoop, calls=%fused_computation.12 | loop fusion | bytes 2097156 | tf_op jit(solution)/shard_map/dynamic_slice | solution.py:564
  26.7 0.8 fusion.1.refs_5_
  27.6 3.1 %collective-permute-done.refs_0_ = bf16[256,2048]{1,0:T(8,128)(2,1)} collective-permute-done((bf16[256,2048]{1,0:T(8,128)(2,1)}, bf16[256,2048]{1,0:T(8,128)(2,1)}, u32[]{:S(2)}, u32[]{:S(2)}) %collective-permute-start) | collective-permute-done | bytes 1048608 | tf_op jit(solution)/shard_map/ppermute | solution.py:580
  30.7 0.7 collective-permute-done.1.refs_0_
  31.4 1.3 collective-permute-start.2
  32.7 1.6 %collective-permute-start.3 = (bf16[256,2048]{1,0:T(8,128)(2,1)}, bf16[256,2048]{1,0:T(8,128)(2,1)}, u32[]{:S(2)}, u32[]{:S(2)}) collective-permute-start(bf16[256,2048]{1,0:T(8,128)(2,1)} %collective-permute-done.1.refs_0_), channel_id=1, source_target_pairs={{1,2},{2,3},{5,6},{6,7},{9,10},{10,11},{13,14},{14,15},{17,18},{18... | collective-permute-start | bytes 3145736 | tf_op jit(solution)/shard_map/ppermute | solution.py:581
  34.3 5.5 %collective-permute-done.5 = bf16[256,256]{1,0:T(8,128)(2,1)S(1)} collective-permute-done((bf16[256,256]{1,0:T(8,128)(2,1)S(1)}, bf16[256,256]{1,0:T(8,128)(2,1)S(1)}, u32[]{:S(2)}, u32[]{:S(2)}) %collective-permute-start.5) | collective-permute-done | bytes 131104 | tf_op jit(solution)/shard_map/ppermute | solution.py:546
  39.8 1.0 pad_maximum_fusion.1
  40.8 1.5 %collective-permute-start.8 = (bf16[1024,256]{1,0:T(8,128)(2,1)S(1)}, bf16[1024,256]{1,0:T(8,128)(2,1)S(1)}, u32[]{:S(2)}, u32[]{:S(2)}) collective-permute-start(bf16[1024,256]{1,0:T(8,128)(2,1)S(1)} %copy-done), channel_id=1, source_target_pairs={{0,16},{4,20},{8,24},{12,28},{16,0},{20,4},{24,8},{28,12},{1,17},{... | collective-permute-start | bytes 1572872 | tf_op jit(solution)/shard_map/ppermute | solution.py:376
  44.3 1.5 %collective-permute-start.7 = (bf16[768,256]{1,0:T(8,128)(2,1)}, bf16[768,256]{1,0:T(8,128)(2,1)S(1)}, u32[]{:S(2)}, u32[]{:S(2)}) collective-permute-start(bf16[768,256]{1,0:T(8,128)(2,1)} %constant_dynamic-update-slice_fusion.refs_5_), channel_id=1, source_target_pairs={{0,8},{4,12},{8,0},{12,4},{16,24},{20,28},{24,16},{28,20},{1,9},{5... | collective-permute-start | bytes 1179656 | tf_op jit(solution)/shard_map/ppermute | solution.py:376
  46.4 4.2 %absorb.5 = (f32[256,256]{1,0:T(8,128)}, bf16[32,2048,256]{2,1,0:T(8,128)(2,1)}) custom-call(s32[3]{0:T(128)} %get-tuple-element.126.place, bf16[256,2048]{1,0:T(8,128)(2,1)} %collective-permute-done.1.refs_0_, f32[256,256]{1,0:T(8,128)} %get-tuple-element.72.refs_1_, bf16[8192,256]{1,0:T(8,128)(2,1)} %refs_3_.3, ...), custom_call_target="tpu_custom_call", output_to_operand_aliasing={{1}: (4, {})} | custom-call | flops 268435456 | bytes 3145728 | tf_op jit(solution)/shard_map/absorb/pallas_call | solution.py:140
  50.7 4.2 %absorb.6 = (f32[256,256]{1,0:T(8,128)}, bf16[32,2048,256]{2,1,0:T(8,128)(2,1)}) custom-call(s32[3]{0:T(128)} %get-tuple-element.127.place, bf16[256,2048]{1,0:T(8,128)(2,1)} %collective-permute-done.refs_0_, f32[256,256]{1,0:T(8,128)} %get-tuple-element.74.refs_1_, bf16[8192,256]{1,0:T(8,128)(2,1)} %refs_3_.3, ...), custom_call_target="tpu_custom_call", output_to_operand_aliasing={{1}: (4, {})} | custom-call | flops 268435456 | bytes 3145728 | tf_op jit(solution)/shard_map/absorb/pallas_call | solution.py:140
  54.9 0.8 collective-permute-done.7.refs_7_
  55.7 4.4 %collective-permute-done.2.refs_1_ = bf16[256,2048]{1,0:T(8,128)(2,1)} collective-permute-done((bf16[256,2048]{1,0:T(8,128)(2,1)}, bf16[256,2048]{1,0:T(8,128)(2,1)}, u32[]{:S(2)}, u32[]{:S(2)}) %collective-permute-start.2) | collective-permute-done | bytes 1048608 | tf_op jit(solution)/shard_map/ppermute | solution.py:580
  60.2 1.4 %collective-permute-start.10 = (bf16[256,2048]{1,0:T(8,128)(2,1)}, bf16[256,2048]{1,0:T(8,128)(2,1)}, u32[]{:S(2)}, u32[]{:S(2)}) collective-permute-start(bf16[256,2048]{1,0:T(8,128)(2,1)} %collective-permute-done.2.refs_1_), channel_id=1, source_target_pairs={{1,0},{5,4},{9,8},{13,12},{17,16},{21,20},{25,24},{29,28}} | collective-permute-start | bytes 3145736 | tf_op jit(solution)/shard_map/ppermute | solution.py:580
  61.6 1.6 %collective-permute-start.11 = (bf16[256,2048]{1,0:T(8,128)(2,1)}, bf16[256,2048]{1,0:T(8,128)(2,1)}, u32[]{:S(2)}, u32[]{:S(2)}) collective-permute-start(bf16[256,2048]{1,0:T(8,128)(2,1)} %collective-permute-done.3.refs_0_), channel_id=1, source_target_pairs={{2,3},{6,7},{10,11},{14,15},{18,19},{22,23},{26,27},{30,31}} | collective-permute-start | bytes 3145736 | tf_op jit(solution)/shard_map/ppermute | solution.py:581
  63.2 1.0 pad_maximum_fusion
  64.3 1.4 %collective-permute-start.12 = (bf16[2048,256]{1,0:T(8,128)(2,1)}, bf16[2048,256]{1,0:T(8,128)(2,1)}, u32[]{:S(2)}, u32[]{:S(2)}) collective-permute-start(bf16[2048,256]{1,0:T(8,128)(2,1)} %pad_maximum_fusion), channel_id=1, source_target_pairs={{0,8},{4,12},{8,0},{12,4},{16,24},{20,28},{24,16},{28,20},{1,9},{5... | collective-permute-start | bytes 3145736 | tf_op jit(solution)/shard_map/ppermute | solution.py:376
  65.7 0.9 pad_maximum_fusion.2
  66.6 1.5 %collective-permute-start.13 = (bf16[1536,256]{1,0:T(8,128)(2,1)}, bf16[1536,256]{1,0:T(8,128)(2,1)}, u32[]{:S(2)}, u32[]{:S(2)}) collective-permute-start(bf16[1536,256]{1,0:T(8,128)(2,1)} %pad_maximum_fusion.2), channel_id=1, source_target_pairs={{0,16},{4,20},{8,24},{12,28},{16,0},{20,4},{24,8},{28,12},{1,17},{... | collective-permute-start | bytes 2359304 | tf_op jit(solution)/shard_map/ppermute | solution.py:376
  68.2 0.8 copy-done.3
  69.8 4.3 %absorb.7 = (f32[256,256]{1,0:T(8,128)}, bf16[32,2048,256]{2,1,0:T(8,128)(2,1)}) custom-call(s32[3]{0:T(128)} %pad_add_fusion.4.place, bf16[256,2048]{1,0:T(8,128)(2,1)} %collective-permute-done.3.refs_0_, bf16[256,2048]{1,0:T(8,128)(2,1)} %collective-permute-done.2.refs_1_, f32[256,256]{1,0:T(8,128)} %get-tuple-element.80.refs_2_, ...), custom_call_target="tpu_custom_call", output_to_operand_aliasing={{1}: (5, {})} | custom-call | flops 268435456 | bytes 3145728 | tf_op jit(solution)/shard_map/absorb/pallas_call | solution.py:140
  74.1 1.9 %place_rows.2.refs_2_ = bf16[8192,256]{1,0:T(8,128)(2,1)} custom-call(s32[4]{0:T(128)S(1)} %broadcast_xor_fusion.2.place, bf16[1024,256]{1,0:T(8,128)(2,1)S(1)} %copy-done, bf16[1792,256]{1,0:T(8,128)(2,1)S(1)} %collective-permute-done.9.refs_1_.refs_6_, bf16[1024,256]{1,0:T(8,128)(2,1)S(1)} %collective-permute-done.8.refs_2_, bf16[1024,256]{1,0:T(8,128)(2,1)S(1)} %copy-done.4), custom_call_target="tpu_custom_call" | custom-call | bytes 4194304 | tf_op jit(solution)/shard_map/place_rows/pallas_call | solution.py:493
  76.0 10.9 %collective-permute-done.13.refs_9_ = bf16[1536,256]{1,0:T(8,128)(2,1)} collective-permute-done((bf16[1536,256]{1,0:T(8,128)(2,1)}, bf16[1536,256]{1,0:T(8,128)(2,1)}, u32[]{:S(2)}, u32[]{:S(2)}) %collective-permute-start.13) | collective-permute-done | bytes 786464 | tf_op jit(solution)/shard_map/ppermute | solution.py:376
  86.9 2.5 %collective-permute-done.10.refs_1_ = bf16[256,2048]{1,0:T(8,128)(2,1)} collective-permute-done((bf16[256,2048]{1,0:T(8,128)(2,1)}, bf16[256,2048]{1,0:T(8,128)(2,1)}, u32[]{:S(2)}, u32[]{:S(2)}) %collective-permute-start.10) | collective-permute-done | bytes 1048608 | tf_op jit(solution)/shard_map/ppermute | solution.py:580
  89.9 9.7 %attend.1 = (bf16[32,2048,256]{2,1,0:T(8,128)(2,1)}, bf16[256,1024]{1,0:T(8,128)(2,1)}, bf16[256,256]{1,0:T(8,128)(2,1)}, bf16[4,1024,128]{2,1,0:T(8,128)(2,1)}, bf16[4,1024,128]{2,1,0:T(8,128)(2,1)}) custom-call(s32[3]{0:T(128)} %get-tuple-element.129.place, s32[5]{0:T(128)} %stack.98.order, ...), custom_call_target="tpu_custom_call", output_to_operand_aliasing={{0}: (6, {})} | custom-call | flops 805306368 | bytes 2097152 | tf_op jit(solution)/shard_map/attend/pallas_call | solution.py:235
  100.2 0.9 copy-done.1
  101.1 2.5 %weight_send.1 = (f32[2,1024,128]{2,1,0:T(8,128)S(1)}, f32[2,1024,128]{2,1,0:T(8,128)S(1)}) custom-call(s32[5]{0:T(128)S(1)} %stack.100.place, bf16[32,2048,256]{2,1,0:T(8,128)(2,1)} %get-tuple-element.93.held, bf16[256,256]{1,0:T(8,128)(2,1)S(1)} %copy-done.1), custom_call_target="tpu_custom_call" | custom-call | flops 268435456 | bytes 2097152 | tf_op jit(solution)/shard_map/weight_send/pallas_call | solution.py:334
  103.8 1.5 %collective-permute-start.22 = (bf16[2,1024,128]{2,1,0:T(8,128)(2,1)S(1)}, bf16[2,1024,128]{2,1,0:T(8,128)(2,1)S(1)}, u32[]{:S(2)}, u32[]{:S(2)}) collective-permute-start(bf16[2,1024,128]{2,1,0:T(8,128)(2,1)S(1)} %get-tuple-element.100), channel_id=1, source_target_pairs={{0,8},{4,12},{8,0},{12,4},{16,24},{20,28},{24,16},{28,20},{1,9},{5... | collective-permute-start | bytes 1572872 | tf_op jit(solution)/shard_map/ppermute | solution.py:376
  105.4 1.5 %collective-permute-start.23 = (bf16[2,1024,128]{2,1,0:T(8,128)(2,1)S(1)}, bf16[2,1024,128]{2,1,0:T(8,128)(2,1)S(1)}, u32[]{:S(2)}, u32[]{:S(2)}) collective-permute-start(bf16[2,1024,128]{2,1,0:T(8,128)(2,1)S(1)} %get-tuple-element.101), channel_id=1, source_target_pairs={{0,16},{4,20},{8,24},{12,28},{16,0},{20,4},{24,8},{28,12},{1,17},{... | collective-permute-start | bytes 1572872 | tf_op jit(solution)/shard_map/ppermute | solution.py:376
  106.9 5.0 %collective-permute-start.16 = (bf16[256,256]{1,0:T(8,128)(2,1)S(1)}, bf16[256,256]{1,0:T(8,128)(2,1)S(1)}, u32[]{:S(2)}, u32[]{:S(2)}) collective-permute-start(bf16[256,256]{1,0:T(8,128)(2,1)S(1)} %copy-done.2), channel_id=1, source_target_pairs={{0,3},{1,2},{2,1},{3,0},{4,7},{5,6},{6,5},{7,4},{8,11},{9,10},{10,... | collective-permute-start | bytes 393224 | tf_op jit(solution)/shard_map/ppermute | solution.py:546
  111.9 2.3 %collective-permute-start.17 = (bf16[256,256]{1,0:T(8,128)(2,1)S(1)}, bf16[256,256]{1,0:T(8,128)(2,1)S(1)}, u32[]{:S(2)}, u32[]{:S(2)}) collective-permute-start(bf16[256,256]{1,0:T(8,128)(2,1)S(1)} %copy-done.2), channel_id=1, source_target_pairs={{0,2},{1,3},{2,0},{3,1},{4,6},{5,7},{6,4},{7,5},{8,10},{9,11},{10,... | collective-permute-start | bytes 393224 | tf_op jit(solution)/shard_map/ppermute | solution.py:546
  114.8 2.6 %place_rows.3 = bf16[8192,256]{1,0:T(8,128)(2,1)} custom-call(s32[4]{0:T(128)S(1)} %broadcast_xor_fusion.1.place, bf16[2048,256]{1,0:T(8,128)(2,1)} %collective-permute-done.12.refs_0_, bf16[2048,256]{1,0:T(8,128)(2,1)S(1)} %collective-permute-done.19.refs_1_, bf16[8192,256]{1,0:T(8,128)(2,1)} %place_rows.2.refs_2_), custom_call_target="tpu_custom_call", output_to_operand_aliasing={{}: (3, {})} | custom-call | bytes 4194304 | tf_op jit(solution)/shard_map/place_rows/pallas_call | solution.py:493
  117.4 2.5 %weight_keep.1 = (f32[2,1024,128]{2,1,0:T(8,128)S(1)}, f32[2,1024,128]{2,1,0:T(8,128)S(1)}) custom-call(s32[5]{0:T(128)S(1)} %stack.100.place, bf16[32,2048,256]{2,1,0:T(8,128)(2,1)} %get-tuple-element.93.held, bf16[256,256]{1,0:T(8,128)(2,1)S(1)} %copy-done.2, bf16[4,1024,128]{2,1,0:T(8,128)(2,1)S(1)} %collective-permute-done.24.refs_0_), custom_call_target="tpu_custom_call" | custom-call | flops 268435456 | bytes 2097152 | tf_op jit(solution)/shard_map/weight_keep/pallas_call | solution.py:334
  119.9 3.6 %collective-permute-done.17.refs_2_ = bf16[256,256]{1,0:T(8,128)(2,1)S(1)} collective-permute-done((bf16[256,256]{1,0:T(8,128)(2,1)S(1)}, bf16[256,256]{1,0:T(8,128)(2,1)S(1)}, u32[]{:S(2)}, u32[]{:S(2)}) %collective-permute-start.17) | collective-permute-done | bytes 131104 | tf_op jit(solution)/shard_map/ppermute | solution.py:546
  124.2 0.7 collective-permute-start.26
  124.9 3.9 %input_gradient.1 = bf16[256,2048]{1,0:T(8,128)(2,1)} custom-call(s32[8]{0:T(128)S(1)} %broadcast_xor_fusion.place, bf16[256,256]{1,0:T(8,128)(2,1)S(1)} %copy-done.2, bf16[256,256]{1,0:T(8,128)(2,1)S(1)} %collective-permute-done.18.refs_1_, bf16[256,256]{1,0:T(8,128)(2,1)S(1)} %collective-permute-done.17.refs_2_, ...), custom_call_target="tpu_custom_call" | custom-call | flops 1073741824 | bytes 6291456 | tf_op jit(solution)/shard_map/input_gradient/pallas_call | solution.py:73
  128.8 2.5 %collective-permute-done.25.last_a = bf16[1024,128]{1,0:T(8,128)(2,1)S(1)} collective-permute-done((bf16[1024,128]{1,0:T(8,128)(2,1)S(1)}, bf16[1024,128]{1,0:T(8,128)(2,1)S(1)}, u32[]{:S(2)}, u32[]{:S(2)}) %collective-permute-start.25) | collective-permute-done | bytes 262176 | tf_op jit(solution)/shard_map/ppermute | solution.py:376
  131.5 1.1 weight_finish.1
  (64 shorter events, 7.6 us)
Async XLA Ops:
  0.6 30.0 %collective-permute-start = (bf16[256,2048]{1,0:T(8,128)(2,1)}, bf16[256,2048]{1,0:T(8,128)(2,1)}, u32[]{:S(2)}, u32[]{:S(2)}) collective-permute-start(bf16[256,2048]{1,0:T(8,128)(2,1)} %refs_0_.1), channel_id=1, source_target_pairs={{1,0},{2,1},{3,2},{5,4},{6,5},{7,6},{9,8},{10,9},{11,10},{13,12},{... | collective-permute-start | bytes 3145736 | tf_op jit(solution)/shard_map/ppermute | solution.py:580
  1.9 29.4 %collective-permute-start.1 = (bf16[256,2048]{1,0:T(8,128)(2,1)}, bf16[256,2048]{1,0:T(8,128)(2,1)}, u32[]{:S(2)}, u32[]{:S(2)}) collective-permute-start(bf16[256,2048]{1,0:T(8,128)(2,1)} %refs_0_.1), channel_id=1, source_target_pairs={{0,1},{1,2},{2,3},{4,5},{5,6},{6,7},{8,9},{9,10},{10,11},{12,13},{... | collective-permute-start | bytes 3145736 | tf_op jit(solution)/shard_map/ppermute | solution.py:581
  9.6 24.7 %collective-permute-start.4 = (bf16[256,256]{1,0:T(8,128)(2,1)S(1)}, bf16[256,256]{1,0:T(8,128)(2,1)S(1)}, u32[]{:S(2)}, u32[]{:S(2)}) collective-permute-start(bf16[256,256]{1,0:T(8,128)(2,1)S(1)} %get-tuple-element.125), channel_id=1, source_target_pairs={{0,1},{1,0},{2,3},{3,2},{4,5},{5,4},{6,7},{7,6},{8,9},{9,8},{10,11... | collective-permute-start | bytes 393224 | tf_op jit(solution)/shard_map/ppermute | solution.py:546
  10.7 29.1 %collective-permute-start.5 = (bf16[256,256]{1,0:T(8,128)(2,1)S(1)}, bf16[256,256]{1,0:T(8,128)(2,1)S(1)}, u32[]{:S(2)}, u32[]{:S(2)}) collective-permute-start(bf16[256,256]{1,0:T(8,128)(2,1)S(1)} %get-tuple-element.124), channel_id=1, source_target_pairs={{0,2},{1,3},{2,0},{3,1},{4,6},{5,7},{6,4},{7,5},{8,10},{9,11},{10,... | collective-permute-start | bytes 393224 | tf_op jit(solution)/shard_map/ppermute | solution.py:546
  12.7 27.0 %collective-permute-start.6 = (bf16[256,256]{1,0:T(8,128)(2,1)S(1)}, bf16[256,256]{1,0:T(8,128)(2,1)S(1)}, u32[]{:S(2)}, u32[]{:S(2)}) collective-permute-start(bf16[256,256]{1,0:T(8,128)(2,1)S(1)} %get-tuple-element.123), channel_id=1, source_target_pairs={{0,3},{1,2},{2,1},{3,0},{4,7},{5,6},{6,5},{7,4},{8,11},{9,10},{10,... | collective-permute-start | bytes 393224 | tf_op jit(solution)/shard_map/ppermute | solution.py:546
  25.3 1.4 %copy-start.9 = (s32[1,256]{1,0:T(1,128)S(1)}, s32[1,256]{1,0:T(1,128)}, u32[]{:S(2)}) copy-start(s32[1,256]{1,0:T(1,128)} %param.15) | copy-start | bytes 3076
  25.4 14.4 %copy-start = (bf16[1024,256]{1,0:T(8,128)(2,1)S(1)}, bf16[1024,256]{1,0:T(8,128)(2,1)}, u32[]{:S(2)}) copy-start(bf16[1024,256]{1,0:T(8,128)(2,1)} %get-tuple-element.77.refs_0_) | copy-start | bytes 1572868
  31.4 28.8 %collective-permute-start.2 = (bf16[256,2048]{1,0:T(8,128)(2,1)}, bf16[256,2048]{1,0:T(8,128)(2,1)}, u32[]{:S(2)}, u32[]{:S(2)}) collective-permute-start(bf16[256,2048]{1,0:T(8,128)(2,1)} %collective-permute-done.refs_0_), channel_id=1, source_target_pairs={{1,0},{2,1},{5,4},{6,5},{9,8},{10,9},{13,12},{14,13},{17,16},{18,1... | collective-permute-start | bytes 3145736 | tf_op jit(solution)/shard_map/ppermute | solution.py:580
  32.7 27.5 %collective-permute-start.3 = (bf16[256,2048]{1,0:T(8,128)(2,1)}, bf16[256,2048]{1,0:T(8,128)(2,1)}, u32[]{:S(2)}, u32[]{:S(2)}) collective-permute-start(bf16[256,2048]{1,0:T(8,128)(2,1)} %collective-permute-done.1.refs_0_), channel_id=1, source_target_pairs={{1,2},{2,3},{5,6},{6,7},{9,10},{10,11},{13,14},{14,15},{17,18},{18... | collective-permute-start | bytes 3145736 | tf_op jit(solution)/shard_map/ppermute | solution.py:581
  39.8 3.8 %copy-start.5 = (bf16[256,256]{1,0:T(8,128)(2,1)}, bf16[256,256]{1,0:T(8,128)(2,1)S(1)}, u32[]{:S(2)}) copy-start(bf16[256,256]{1,0:T(8,128)(2,1)S(1)} %collective-permute-done.5) | copy-start | bytes 393220
  39.8 3.8 %copy-start.7 = (bf16[256,256]{1,0:T(8,128)(2,1)}, bf16[256,256]{1,0:T(8,128)(2,1)S(1)}, u32[]{:S(2)}) copy-start(bf16[256,256]{1,0:T(8,128)(2,1)S(1)} %collective-permute-done.6) | copy-start | bytes 393220
  40.8 15.0 %collective-permute-start.9 = (bf16[1792,256]{1,0:T(8,128)(2,1)}, bf16[1792,256]{1,0:T(8,128)(2,1)S(1)}, u32[]{:S(2)}, u32[]{:S(2)}) collective-permute-start(bf16[1792,256]{1,0:T(8,128)(2,1)} %pad_maximum_fusion.1), channel_id=1, source_target_pairs={{0,4},{4,0},{8,12},{12,8},{16,20},{20,16},{24,28},{28,24},{1,5},{5... | collective-permute-start | bytes 2752520 | tf_op jit(solution)/shard_map/ppermute | solution.py:376
  40.8 15.0 %collective-permute-start.8 = (bf16[1024,256]{1,0:T(8,128)(2,1)S(1)}, bf16[1024,256]{1,0:T(8,128)(2,1)S(1)}, u32[]{:S(2)}, u32[]{:S(2)}) collective-permute-start(bf16[1024,256]{1,0:T(8,128)(2,1)S(1)} %copy-done), channel_id=1, source_target_pairs={{0,16},{4,20},{8,24},{12,28},{16,0},{20,4},{24,8},{28,12},{1,17},{... | collective-permute-start | bytes 1572872 | tf_op jit(solution)/shard_map/ppermute | solution.py:376
  44.3 11.5 %collective-permute-start.7 = (bf16[768,256]{1,0:T(8,128)(2,1)}, bf16[768,256]{1,0:T(8,128)(2,1)S(1)}, u32[]{:S(2)}, u32[]{:S(2)}) collective-permute-start(bf16[768,256]{1,0:T(8,128)(2,1)} %constant_dynamic-update-slice_fusion.refs_5_), channel_id=1, source_target_pairs={{0,8},{4,12},{8,0},{12,4},{16,24},{20,28},{24,16},{28,20},{1,9},{5... | collective-permute-start | bytes 1179656 | tf_op jit(solution)/shard_map/ppermute | solution.py:376
  54.9 10.8 %copy-start.6 = (bf16[256,256]{1,0:T(8,128)(2,1)S(1)}, bf16[256,256]{1,0:T(8,128)(2,1)}, u32[]{:S(2)}) copy-start(bf16[256,256]{1,0:T(8,128)(2,1)} %copy-done.5) | copy-start | bytes 393220
  54.9 10.8 %copy-start.8 = (bf16[256,256]{1,0:T(8,128)(2,1)S(1)}, bf16[256,256]{1,0:T(8,128)(2,1)}, u32[]{:S(2)}) copy-start(bf16[256,256]{1,0:T(8,128)(2,1)} %copy-done.7) | copy-start | bytes 393220
  60.2 9.6 %copy-start.12 = (s32[4]{0:T(128)S(1)}, s32[4]{0:T(128)}, u32[]{:S(2)}) copy-start(s32[4]{0:T(128)} %constant.72.clone) | copy-start | bytes 52
  60.2 29.2 %collective-permute-start.10 = (bf16[256,2048]{1,0:T(8,128)(2,1)}, bf16[256,2048]{1,0:T(8,128)(2,1)}, u32[]{:S(2)}, u32[]{:S(2)}) collective-permute-start(bf16[256,2048]{1,0:T(8,128)(2,1)} %collective-permute-done.2.refs_1_), channel_id=1, source_target_pairs={{1,0},{5,4},{9,8},{13,12},{17,16},{21,20},{25,24},{29,28}} | collective-permute-start | bytes 3145736 | tf_op jit(solution)/shard_map/ppermute | solution.py:580
  61.6 27.8 %collective-permute-start.11 = (bf16[256,2048]{1,0:T(8,128)(2,1)}, bf16[256,2048]{1,0:T(8,128)(2,1)}, u32[]{:S(2)}, u32[]{:S(2)}) collective-permute-start(bf16[256,2048]{1,0:T(8,128)(2,1)} %collective-permute-done.3.refs_0_), channel_id=1, source_target_pairs={{2,3},{6,7},{10,11},{14,15},{18,19},{22,23},{26,27},{30,31}} | collective-permute-start | bytes 3145736 | tf_op jit(solution)/shard_map/ppermute | solution.py:581
  64.3 25.1 %collective-permute-start.12 = (bf16[2048,256]{1,0:T(8,128)(2,1)}, bf16[2048,256]{1,0:T(8,128)(2,1)}, u32[]{:S(2)}, u32[]{:S(2)}) collective-permute-start(bf16[2048,256]{1,0:T(8,128)(2,1)} %pad_maximum_fusion), channel_id=1, source_target_pairs={{0,8},{4,12},{8,0},{12,4},{16,24},{20,28},{24,16},{28,20},{1,9},{5... | collective-permute-start | bytes 3145736 | tf_op jit(solution)/shard_map/ppermute | solution.py:376
  65.7 2.5 %collective-permute-start.15 = (bf16[1024,256]{1,0:T(8,128)(2,1)S(1)}, bf16[1024,256]{1,0:T(8,128)(2,1)S(1)}, u32[]{:S(2)}, u32[]{:S(2)}) collective-permute-start(bf16[1024,256]{1,0:T(8,128)(2,1)S(1)} %collective-permute-done.8.refs_2_), channel_id=1, source_target_pairs={{0,4},{4,0},{8,12},{12,8},{16,20},{20,16},{24,28},{28,24},{1,5},{5... | collective-permute-start | bytes 1572872 | tf_op jit(solution)/shard_map/ppermute | solution.py:376
  66.6 20.3 %collective-permute-start.13 = (bf16[1536,256]{1,0:T(8,128)(2,1)}, bf16[1536,256]{1,0:T(8,128)(2,1)}, u32[]{:S(2)}, u32[]{:S(2)}) collective-permute-start(bf16[1536,256]{1,0:T(8,128)(2,1)} %pad_maximum_fusion.2), channel_id=1, source_target_pairs={{0,16},{4,20},{8,24},{12,28},{16,0},{20,4},{24,8},{28,12},{1,17},{... | collective-permute-start | bytes 2359304 | tf_op jit(solution)/shard_map/ppermute | solution.py:376
  68.2 0.8 copy-start.3
  68.9 7.0 %collective-permute-start.14 = (bf16[768,256]{1,0:T(8,128)(2,1)S(1)}, bf16[768,256]{1,0:T(8,128)(2,1)}, u32[]{:S(2)}, u32[]{:S(2)}) collective-permute-start(bf16[768,256]{1,0:T(8,128)(2,1)S(1)} %collective-permute-done.7.refs_7_), channel_id=1, source_target_pairs={{0,4},{4,0},{8,12},{12,8},{16,20},{20,16},{24,28},{28,24},{1,5},{5... | collective-permute-start | bytes 1179656 | tf_op jit(solution)/shard_map/ppermute | solution.py:376
  69.8 4.3 %copy-start.4 = (bf16[1024,256]{1,0:T(8,128)(2,1)S(1)}, bf16[1024,256]{1,0:T(8,128)(2,1)}, u32[]{:S(2)}) copy-start(bf16[1024,256]{1,0:T(8,128)(2,1)} %copy-done.3) | copy-start | bytes 1572868
  89.4 10.3 %collective-permute-start.19 = (bf16[2048,256]{1,0:T(8,128)(2,1)}, bf16[2048,256]{1,0:T(8,128)(2,1)S(1)}, u32[]{:S(2)}, u32[]{:S(2)}) collective-permute-start(bf16[2048,256]{1,0:T(8,128)(2,1)} %collective-permute-done.12.refs_0_), channel_id=1, source_target_pairs={{0,4},{4,0},{8,12},{12,8},{16,20},{20,16},{24,28},{28,24},{1,5},{5... | collective-permute-start | bytes 3145736 | tf_op jit(solution)/shard_map/ppermute | solution.py:376
  89.4 10.2 %collective-permute-start.20 = (bf16[1536,256]{1,0:T(8,128)(2,1)}, bf16[1536,256]{1,0:T(8,128)(2,1)}, u32[]{:S(2)}, u32[]{:S(2)}) collective-permute-start(bf16[1536,256]{1,0:T(8,128)(2,1)} %collective-permute-done.13.refs_9_), channel_id=1, source_target_pairs={{0,4},{4,0},{8,12},{12,8},{16,20},{20,16},{24,28},{28,24},{1,5},{5... | collective-permute-start | bytes 2359304 | tf_op jit(solution)/shard_map/ppermute | solution.py:376
  99.7 4.0 %collective-permute-start.21 = (bf16[4,1024,128]{2,1,0:T(8,128)(2,1)}, bf16[4,1024,128]{2,1,0:T(8,128)(2,1)S(1)}, u32[]{:S(2)}, u32[]{:S(2)}) collective-permute-start(bf16[4,1024,128]{2,1,0:T(8,128)(2,1)} %get-tuple-element.99), channel_id=1, source_target_pairs={{0,4},{4,0},{8,12},{12,8},{16,20},{20,16},{24,28},{28,24},{1,5},{5... | collective-permute-start | bytes 3145736 | tf_op jit(solution)/shard_map/ppermute | solution.py:376
  99.8 14.4 %collective-permute-start.24 = (bf16[4,1024,128]{2,1,0:T(8,128)(2,1)}, bf16[4,1024,128]{2,1,0:T(8,128)(2,1)S(1)}, u32[]{:S(2)}, u32[]{:S(2)}) collective-permute-start(bf16[4,1024,128]{2,1,0:T(8,128)(2,1)} %get-tuple-element.105), channel_id=1, source_target_pairs={{0,4},{4,0},{8,12},{12,8},{16,20},{20,16},{24,28},{28,24},{1,5},{5... | collective-permute-start | bytes 3145736 | tf_op jit(solution)/shard_map/ppermute | solution.py:376
  100.2 0.9 copy-start.1
  103.6 3.2 %copy-start.2 = (bf16[256,256]{1,0:T(8,128)(2,1)S(1)}, bf16[256,256]{1,0:T(8,128)(2,1)}, u32[]{:S(2)}) copy-start(bf16[256,256]{1,0:T(8,128)(2,1)} %get-tuple-element.112.d_projected.refs_0_) | copy-start | bytes 393220
  103.6 11.1 %copy-start.11 = (s32[4]{0:T(128)S(1)}, s32[4]{0:T(128)}, u32[]{:S(2)}) copy-start(s32[4]{0:T(128)} %constant.73.clone) | copy-start | bytes 52
  103.8 19.7 %collective-permute-start.22 = (bf16[2,1024,128]{2,1,0:T(8,128)(2,1)S(1)}, bf16[2,1024,128]{2,1,0:T(8,128)(2,1)S(1)}, u32[]{:S(2)}, u32[]{:S(2)}) collective-permute-start(bf16[2,1024,128]{2,1,0:T(8,128)(2,1)S(1)} %get-tuple-element.100), channel_id=1, source_target_pairs={{0,8},{4,12},{8,0},{12,4},{16,24},{20,28},{24,16},{28,20},{1,9},{5... | collective-permute-start | bytes 1572872 | tf_op jit(solution)/shard_map/ppermute | solution.py:376
  105.4 18.2 %collective-permute-start.23 = (bf16[2,1024,128]{2,1,0:T(8,128)(2,1)S(1)}, bf16[2,1024,128]{2,1,0:T(8,128)(2,1)S(1)}, u32[]{:S(2)}, u32[]{:S(2)}) collective-permute-start(bf16[2,1024,128]{2,1,0:T(8,128)(2,1)S(1)} %get-tuple-element.101), channel_id=1, source_target_pairs={{0,16},{4,20},{8,24},{12,28},{16,0},{20,4},{24,8},{28,12},{1,17},{... | collective-permute-start | bytes 1572872 | tf_op jit(solution)/shard_map/ppermute | solution.py:376
  106.9 13.0 %collective-permute-start.16 = (bf16[256,256]{1,0:T(8,128)(2,1)S(1)}, bf16[256,256]{1,0:T(8,128)(2,1)S(1)}, u32[]{:S(2)}, u32[]{:S(2)}) collective-permute-start(bf16[256,256]{1,0:T(8,128)(2,1)S(1)} %copy-done.2), channel_id=1, source_target_pairs={{0,3},{1,2},{2,1},{3,0},{4,7},{5,6},{6,5},{7,4},{8,11},{9,10},{10,... | collective-permute-start | bytes 393224 | tf_op jit(solution)/shard_map/ppermute | solution.py:546
  111.9 11.6 %collective-permute-start.17 = (bf16[256,256]{1,0:T(8,128)(2,1)S(1)}, bf16[256,256]{1,0:T(8,128)(2,1)S(1)}, u32[]{:S(2)}, u32[]{:S(2)}) collective-permute-start(bf16[256,256]{1,0:T(8,128)(2,1)S(1)} %copy-done.2), channel_id=1, source_target_pairs={{0,2},{1,3},{2,0},{3,1},{4,6},{5,7},{6,4},{7,5},{8,10},{9,11},{10,... | collective-permute-start | bytes 393224 | tf_op jit(solution)/shard_map/ppermute | solution.py:546
  114.2 9.3 %collective-permute-start.18 = (bf16[256,256]{1,0:T(8,128)(2,1)S(1)}, bf16[256,256]{1,0:T(8,128)(2,1)S(1)}, u32[]{:S(2)}, u32[]{:S(2)}) collective-permute-start(bf16[256,256]{1,0:T(8,128)(2,1)S(1)} %copy-done.2), channel_id=1, source_target_pairs={{0,1},{1,0},{2,3},{3,2},{4,5},{5,4},{6,7},{7,6},{8,9},{9,8},{10,11... | collective-permute-start | bytes 393224 | tf_op jit(solution)/shard_map/ppermute | solution.py:546
  119.9 5.0 %copy-start.10 = (s32[8]{0:T(128)S(1)}, s32[8]{0:T(128)}, u32[]{:S(2)}) copy-start(s32[8]{0:T(128)} %constant.74.clone) | copy-start | bytes 100
  123.6 7.7 %collective-permute-start.25 = (bf16[1024,128]{1,0:T(8,128)(2,1)S(1)}, bf16[1024,128]{1,0:T(8,128)(2,1)S(1)}, u32[]{:S(2)}, u32[]{:S(2)}) collective-permute-start(bf16[1024,128]{1,0:T(8,128)(2,1)S(1)} %get-tuple-element.110), channel_id=1, source_target_pairs={{0,16},{4,20},{8,24},{12,28},{16,0},{20,4},{24,8},{28,12},{1,17},{... | collective-permute-start | bytes 786440 | tf_op jit(solution)/shard_map/ppermute | solution.py:376
  124.2 7.3 %collective-permute-start.26 = (bf16[1024,128]{1,0:T(8,128)(2,1)S(1)}, bf16[1024,128]{1,0:T(8,128)(2,1)S(1)}, u32[]{:S(2)}, u32[]{:S(2)}) collective-permute-start(bf16[1024,128]{1,0:T(8,128)(2,1)S(1)} %get-tuple-element.111), channel_id=1, source_target_pairs={{0,8},{4,12},{8,0},{12,4},{16,24},{20,28},{24,16},{28,20},{1,9},{5... | collective-permute-start | bytes 786440 | tf_op jit(solution)/shard_map/ppermute | solution.py:376

commit v14 on v13

--- a/solution.py
+++ b/solution.py
@@ -384,7 +384,7 @@
     return [jnp.stack(chunks + [half]) for half in (1 - core, core)]
 
 
-def weight_sum(held, d_projected, order, sent, kept, pieces, beside):
+def weight_sum(held, d_projected, order, sent, kept, pieces, pair, beside):
     swap = plane()[3]
     rows, cols = held.shape[1] // 2, d_projected.shape[1]
     none = jnp.zeros((1,), jnp.int32)
@@ -398,8 +398,11 @@
     keep_a, keep_b = weight_parts(
         held, d_projected, order, KEPT, [kept], jnp.float32, "weight_keep"
     )
-    pieces, got_a, got_b, beside = lax.optimization_barrier((pieces[::-1], got_a, got_b, beside))
-    pieces = pieces[::-1]
+    pieces[2], keep_a, keep_b, beside = lax.optimization_barrier(
+        (pieces[2], keep_a, keep_b, beside)
+    )
+    pieces = pieces + [pair(pieces[2], 1)]
+    pieces, got_a, got_b = lax.optimization_barrier((pieces, got_a, got_b))
 
     small = jax.ShapeDtypeStruct((rows, cols // 2), jnp.bfloat16)
     arrays = [keep_a, got_a, keep_b, got_b]
@@ -607,13 +610,15 @@
             chunks, which, index, cached, total, held, queries, d_out, allowed, orders[0], n_z
         )
 
-        pieces = [pair(d_projected, s) for s in range(n_z - 1, 0, -1)]
-        pieces = [d_projected] + pieces[::-1]
+        if tuned:
+            pieces = [d_projected, pair(d_projected, 1), pair(d_projected, 2)]
+        else:
+            pieces = [d_projected] + [pair(d_projected, s) for s in range(1, n_z)]
         if tuned:
             sent, gather.packs_other = lax.optimization_barrier((sent, gather.third()))
             new_cache = gather.lay_rest(laid)
             finish, pieces, new_cache = weight_sum(
-                held, d_projected, orders[1], sent, kept, pieces, new_cache
+                held, d_projected, orders[1], sent, kept, pieces, pair, new_cache
             )
             new_grad, d_tokens = finish(input_gradient(pieces, here, *gather.feature_rows()))
         else:

time: 133 us -> 135 us (1.015)
  transfers between devices with their start and end apart: 27 -> 27, of which waited for: 10 -> 11; matrix products, arithmetic and copies ran while one was open for 9% -> 9% of each run, Pallas kernels for 34% -> 34%
where the time goes in v14:
time: 135 us; the launch traced here: 134 us
  Pallas kernels  46.4 us (34%)
  starting transfers between devices  38.5 us (29%)
  waiting for transfers between devices  35.1 us (26%)
  local copies, waits for them, and re-layouts  7.55 us (6%)
  other arithmetic  5.7 us (4%)
    pallas_call x4, Pallas kernels, absorb(): pl.pallas_call(functools.partial(absorb_kernel, len(chunks)), in_specs=[p...  17 us
    ppermute x15, waiting for transfers between devices, swap(): return lax.ppermute(value, 'dp', [(i, i ^ bit) for i in range(8)])  13.9 us
    ppermute x6, starting transfers between devices, pair(): return lax.ppermute(value, 'tensor', [(z, z ^ s) for z in range(n_z)])  13.1 us
    ppermute x15, starting transfers between devices, swap(): return lax.ppermute(value, 'dp', [(i, i ^ bit) for i in range(8)])  11.6 us
    ppermute x6, waiting for transfers between devices, pair(): return lax.ppermute(value, 'tensor', [(z, z ^ s) for z in range(n_z)])  10.4 us
    ppermute x3, waiting for transfers between devices, body(): lax.ppermute(from_high, 'tensor', [(z + 1, z) for z in range(n_z - s)])  10 us
    ppermute x3, starting transfers between devices, body(): lax.ppermute(from_low, 'tensor', [(z, z + 1) for z in range(s - 1, n_z -...  9.86 us
    pallas_call x1, Pallas kernels, attend(): pl.pallas_call(functools.partial(attend_kernel, len(chunks)), in_specs=[p...  9.73 us
  transfers between devices with their start and end apart: 27, of which 11 were waited for; matrix products, arithmetic and copies ran while one was open for 9% of the time, Pallas kernels for 34%

profile of v14, /device:TPU:0, one launch (start us, length us, event | category | flops | bytes accessed | tf_op | source)
XLA Modules:
  0.0 134.1 jit_solution(9437449876707385643)
XLA Ops:
  0.6 1.3 collective-permute-start
  1.9 6.6 %collective-permute-start.1 = (bf16[256,2048]{1,0:T(8,128)(2,1)}, bf16[256,2048]{1,0:T(8,128)(2,1)}, u32[]{:S(2)}, u32[]{:S(2)}) collective-permute-start(bf16[256,2048]{1,0:T(8,128)(2,1)} %refs_0_.1), channel_id=1, source_target_pairs={{0,1},{1,2},{2,3},{4,5},{5,6},{6,7},{8,9},{9,10},{10,11},{12,13},{... | collective-permute-start | bytes 3145736 | tf_op jit(solution)/shard_map/ppermute | solution.py:584
  8.5 1.1 constant_dynamic-slice_fusion
  9.6 1.1 collective-permute-start.4
  10.7 2.0 %collective-permute-start.5 = (bf16[256,256]{1,0:T(8,128)(2,1)S(1)}, bf16[256,256]{1,0:T(8,128)(2,1)S(1)}, u32[]{:S(2)}, u32[]{:S(2)}) collective-permute-start(bf16[256,256]{1,0:T(8,128)(2,1)S(1)} %get-tuple-element.130), channel_id=1, source_target_pairs={{0,2},{1,3},{2,0},{3,1},{4,6},{5,7},{6,4},{7,5},{8,10},{9,11},{10,... | collective-permute-start | bytes 393224 | tf_op jit(solution)/shard_map/ppermute | solution.py:549
  12.7 1.4 %collective-permute-start.6 = (bf16[256,256]{1,0:T(8,128)(2,1)S(1)}, bf16[256,256]{1,0:T(8,128)(2,1)S(1)}, u32[]{:S(2)}, u32[]{:S(2)}) collective-permute-start(bf16[256,256]{1,0:T(8,128)(2,1)S(1)} %get-tuple-element.129), channel_id=1, source_target_pairs={{0,3},{1,2},{2,1},{3,0},{4,7},{5,6},{6,5},{7,4},{8,11},{9,10},{10,... | collective-permute-start | bytes 393224 | tf_op jit(solution)/shard_map/ppermute | solution.py:549
  14.8 4.9 %optimizer.1 = (f32[1024,256]{1,0:T(8,128)}, f32[1024,256]{1,0:T(8,128)}, f32[1024,256]{1,0:T(8,128)}, bf16[1024,256]{1,0:T(8,128)(2,1)}) custom-call(s32[1]{0:T(128)} %bitcast.place, bf16[8192,256]{1,0:T(8,128)(2,1)} %refs_3_.3, f32[1024,256]{1,0:T(8,128)} %master.1, f32[1024,256]{1,0:T(8,128)} %moment.1, f32[1024,256]{1,0:T(8,128)} %second.1, f32[1024,256]{1,0:T(8,128)} %grad.1), custom_call_target="tpu_custom_call" | custom-call | flops 10485760 | bytes 8388608 | tf_op jit(solution)/shard_map/optimizer/pallas_call | solution.py:51
  20.4 0.7 broadcast_in_dim.2.refs_1_
  21.1 4.2 %absorb.4 = (f32[256,256]{1,0:T(8,128)}, bf16[32,2048,256]{2,1,0:T(8,128)(2,1)}) custom-call(s32[3]{0:T(128)} %get-tuple-element.134.place, bf16[256,2048]{1,0:T(8,128)(2,1)} %refs_0_.1, f32[256,256]{1,0:T(8,128)} %broadcast_in_dim.2.refs_1_, bf16[8192,256]{1,0:T(8,128)(2,1)} %refs_3_.3), custom_call_target="tpu_custom_call" | custom-call | flops 268435456 | bytes 3145728 | tf_op jit(solution)/shard_map/absorb/pallas_call | solution.py:140
  25.4 1.4 %constant_dynamic-slice_fusion.3.refs_4_ = bf16[2048,256]{1,0:T(8,128)(2,1)S(1)} fusion(bf16[8192,256]{1,0:T(8,128)(2,1)} %refs_3_.3, s32[]{:T(128)S(6)} %select_n.59), kind=kLoop, calls=%fused_computation.12 | loop fusion | bytes 2097156 | tf_op jit(solution)/shard_map/dynamic_slice | solution.py:567
  26.7 0.8 fusion.1.refs_5_
  27.6 3.1 %collective-permute-done.refs_0_ = bf16[256,2048]{1,0:T(8,128)(2,1)} collective-permute-done((bf16[256,2048]{1,0:T(8,128)(2,1)}, bf16[256,2048]{1,0:T(8,128)(2,1)}, u32[]{:S(2)}, u32[]{:S(2)}) %collective-permute-start) | collective-permute-done | bytes 1048608 | tf_op jit(solution)/shard_map/ppermute | solution.py:583
  31.4 1.3 collective-permute-start.2
  32.7 1.6 %collective-permute-start.3 = (bf16[256,2048]{1,0:T(8,128)(2,1)}, bf16[256,2048]{1,0:T(8,128)(2,1)}, u32[]{:S(2)}, u32[]{:S(2)}) collective-permute-start(bf16[256,2048]{1,0:T(8,128)(2,1)} %collective-permute-done.1.refs_0_), channel_id=1, source_target_pairs={{1,2},{2,3},{5,6},{6,7},{9,10},{10,11},{13,14},{14,15},{17,18},{18... | collective-permute-start | bytes 3145736 | tf_op jit(solution)/shard_map/ppermute | solution.py:584
  34.3 5.5 %collective-permute-done.5 = bf16[256,256]{1,0:T(8,128)(2,1)S(1)} collective-permute-done((bf16[256,256]{1,0:T(8,128)(2,1)S(1)}, bf16[256,256]{1,0:T(8,128)(2,1)S(1)}, u32[]{:S(2)}, u32[]{:S(2)}) %collective-permute-start.5) | collective-permute-done | bytes 131104 | tf_op jit(solution)/shard_map/ppermute | solution.py:549
  39.8 1.0 pad_maximum_fusion.1
  40.8 1.5 %collective-permute-start.8 = (bf16[1024,256]{1,0:T(8,128)(2,1)S(1)}, bf16[1024,256]{1,0:T(8,128)(2,1)S(1)}, u32[]{:S(2)}, u32[]{:S(2)}) collective-permute-start(bf16[1024,256]{1,0:T(8,128)(2,1)S(1)} %copy-done), channel_id=1, source_target_pairs={{0,16},{4,20},{8,24},{12,28},{16,0},{20,4},{24,8},{28,12},{1,17},{... | collective-permute-start | bytes 1572872 | tf_op jit(solution)/shard_map/ppermute | solution.py:376
  44.3 1.5 %collective-permute-start.7 = (bf16[768,256]{1,0:T(8,128)(2,1)}, bf16[768,256]{1,0:T(8,128)(2,1)S(1)}, u32[]{:S(2)}, u32[]{:S(2)}) collective-permute-start(bf16[768,256]{1,0:T(8,128)(2,1)} %constant_dynamic-update-slice_fusion.refs_5_), channel_id=1, source_target_pairs={{0,8},{4,12},{8,0},{12,4},{16,24},{20,28},{24,16},{28,20},{1,9},{5... | collective-permute-start | bytes 1179656 | tf_op jit(solution)/shard_map/ppermute | solution.py:376
  46.4 4.2 %absorb.5 = (f32[256,256]{1,0:T(8,128)}, bf16[32,2048,256]{2,1,0:T(8,128)(2,1)}) custom-call(s32[3]{0:T(128)} %get-tuple-element.132.place, bf16[256,2048]{1,0:T(8,128)(2,1)} %collective-permute-done.1.refs_0_, f32[256,256]{1,0:T(8,128)} %get-tuple-element.75.refs_1_, bf16[8192,256]{1,0:T(8,128)(2,1)} %refs_3_.3, ...), custom_call_target="tpu_custom_call", output_to_operand_aliasing={{1}: (4, {})} | custom-call | flops 268435456 | bytes 3145728 | tf_op jit(solution)/shard_map/absorb/pallas_call | solution.py:140
  50.7 4.2 %absorb.6 = (f32[256,256]{1,0:T(8,128)}, bf16[32,2048,256]{2,1,0:T(8,128)(2,1)}) custom-call(s32[3]{0:T(128)} %get-tuple-element.133.place, bf16[256,2048]{1,0:T(8,128)(2,1)} %collective-permute-done.refs_0_, f32[256,256]{1,0:T(8,128)} %get-tuple-element.77.refs_1_, bf16[8192,256]{1,0:T(8,128)(2,1)} %refs_3_.3, ...), custom_call_target="tpu_custom_call", output_to_operand_aliasing={{1}: (4, {})} | custom-call | flops 268435456 | bytes 3145728 | tf_op jit(solution)/shard_map/absorb/pallas_call | solution.py:140
  54.9 0.8 collective-permute-done.7.refs_7_
  55.7 4.4 %collective-permute-done.2.refs_1_ = bf16[256,2048]{1,0:T(8,128)(2,1)} collective-permute-done((bf16[256,2048]{1,0:T(8,128)(2,1)}, bf16[256,2048]{1,0:T(8,128)(2,1)}, u32[]{:S(2)}, u32[]{:S(2)}) %collective-permute-start.2) | collective-permute-done | bytes 1048608 | tf_op jit(solution)/shard_map/ppermute | solution.py:583
  60.2 1.4 %collective-permute-start.10 = (bf16[256,2048]{1,0:T(8,128)(2,1)}, bf16[256,2048]{1,0:T(8,128)(2,1)}, u32[]{:S(2)}, u32[]{:S(2)}) collective-permute-start(bf16[256,2048]{1,0:T(8,128)(2,1)} %collective-permute-done.2.refs_1_), channel_id=1, source_target_pairs={{1,0},{5,4},{9,8},{13,12},{17,16},{21,20},{25,24},{29,28}} | collective-permute-start | bytes 3145736 | tf_op jit(solution)/shard_map/ppermute | solution.py:583
  61.6 1.6 %collective-permute-start.11 = (bf16[256,2048]{1,0:T(8,128)(2,1)}, bf16[256,2048]{1,0:T(8,128)(2,1)}, u32[]{:S(2)}, u32[]{:S(2)}) collective-permute-start(bf16[256,2048]{1,0:T(8,128)(2,1)} %collective-permute-done.3.refs_0_), channel_id=1, source_target_pairs={{2,3},{6,7},{10,11},{14,15},{18,19},{22,23},{26,27},{30,31}} | collective-permute-start | bytes 3145736 | tf_op jit(solution)/shard_map/ppermute | solution.py:584
  63.2 1.0 pad_maximum_fusion
  64.3 1.4 %collective-permute-start.12 = (bf16[2048,256]{1,0:T(8,128)(2,1)}, bf16[2048,256]{1,0:T(8,128)(2,1)}, u32[]{:S(2)}, u32[]{:S(2)}) collective-permute-start(bf16[2048,256]{1,0:T(8,128)(2,1)} %pad_maximum_fusion), channel_id=1, source_target_pairs={{0,8},{4,12},{8,0},{12,4},{16,24},{20,28},{24,16},{28,20},{1,9},{5... | collective-permute-start | bytes 3145736 | tf_op jit(solution)/shard_map/ppermute | solution.py:376
  65.7 0.9 pad_maximum_fusion.2
  66.6 1.5 %collective-permute-start.13 = (bf16[1536,256]{1,0:T(8,128)(2,1)}, bf16[1536,256]{1,0:T(8,128)(2,1)}, u32[]{:S(2)}, u32[]{:S(2)}) collective-permute-start(bf16[1536,256]{1,0:T(8,128)(2,1)} %pad_maximum_fusion.2), channel_id=1, source_target_pairs={{0,16},{4,20},{8,24},{12,28},{16,0},{20,4},{24,8},{28,12},{1,17},{... | collective-permute-start | bytes 2359304 | tf_op jit(solution)/shard_map/ppermute | solution.py:376
  68.2 0.8 copy-done.3
  69.8 4.3 %absorb.7 = (f32[256,256]{1,0:T(8,128)}, bf16[32,2048,256]{2,1,0:T(8,128)(2,1)}) custom-call(s32[3]{0:T(128)} %pad_add_fusion.4.place, bf16[256,2048]{1,0:T(8,128)(2,1)} %collective-permute-done.3.refs_0_, bf16[256,2048]{1,0:T(8,128)(2,1)} %collective-permute-done.2.refs_1_, f32[256,256]{1,0:T(8,128)} %get-tuple-element.83.refs_2_, ...), custom_call_target="tpu_custom_call", output_to_operand_aliasing={{1}: (5, {})} | custom-call | flops 268435456 | bytes 3145728 | tf_op jit(solution)/shard_map/absorb/pallas_call | solution.py:140
  74.1 1.9 %place_rows.2.refs_2_ = bf16[8192,256]{1,0:T(8,128)(2,1)} custom-call(s32[4]{0:T(128)S(1)} %broadcast_xor_fusion.2.place, bf16[1024,256]{1,0:T(8,128)(2,1)S(1)} %copy-done, bf16[1792,256]{1,0:T(8,128)(2,1)S(1)} %collective-permute-done.9.refs_1_.refs_6_, bf16[1024,256]{1,0:T(8,128)(2,1)S(1)} %collective-permute-done.8.refs_2_, bf16[1024,256]{1,0:T(8,128)(2,1)S(1)} %copy-done.4), custom_call_target="tpu_custom_call" | custom-call | bytes 4194304 | tf_op jit(solution)/shard_map/place_rows/pallas_call | solution.py:496
  76.0 10.9 %collective-permute-done.13.refs_9_ = bf16[1536,256]{1,0:T(8,128)(2,1)} collective-permute-done((bf16[1536,256]{1,0:T(8,128)(2,1)}, bf16[1536,256]{1,0:T(8,128)(2,1)}, u32[]{:S(2)}, u32[]{:S(2)}) %collective-permute-start.13) | collective-permute-done | bytes 786464 | tf_op jit(solution)/shard_map/ppermute | solution.py:376
  86.9 2.5 %collective-permute-done.10.refs_1_ = bf16[256,2048]{1,0:T(8,128)(2,1)} collective-permute-done((bf16[256,2048]{1,0:T(8,128)(2,1)}, bf16[256,2048]{1,0:T(8,128)(2,1)}, u32[]{:S(2)}, u32[]{:S(2)}) %collective-permute-start.10) | collective-permute-done | bytes 1048608 | tf_op jit(solution)/shard_map/ppermute | solution.py:583
  89.9 9.7 %attend.1 = (bf16[32,2048,256]{2,1,0:T(8,128)(2,1)}, bf16[256,1024]{1,0:T(8,128)(2,1)}, bf16[256,256]{1,0:T(8,128)(2,1)}, bf16[4,1024,128]{2,1,0:T(8,128)(2,1)}, bf16[4,1024,128]{2,1,0:T(8,128)(2,1)}) custom-call(s32[3]{0:T(128)} %get-tuple-element.135.place, s32[5]{0:T(128)} %stack.98.order, ...), custom_call_target="tpu_custom_call", output_to_operand_aliasing={{0}: (6, {})} | custom-call | flops 805306368 | bytes 2097152 | tf_op jit(solution)/shard_map/attend/pallas_call | solution.py:235
  100.2 0.9 copy-done.1
  101.1 2.5 %weight_send.1 = (f32[2,1024,128]{2,1,0:T(8,128)S(1)}, f32[2,1024,128]{2,1,0:T(8,128)S(1)}) custom-call(s32[5]{0:T(128)S(1)} %stack.100.place, bf16[32,2048,256]{2,1,0:T(8,128)(2,1)} %get-tuple-element.96.held, bf16[256,256]{1,0:T(8,128)(2,1)S(1)} %copy-done.1), custom_call_target="tpu_custom_call" | custom-call | flops 268435456 | bytes 2097152 | tf_op jit(solution)/shard_map/weight_send/pallas_call | solution.py:334
  103.8 1.5 %collective-permute-start.23 = (bf16[2,1024,128]{2,1,0:T(8,128)(2,1)S(1)}, bf16[2,1024,128]{2,1,0:T(8,128)(2,1)S(1)}, u32[]{:S(2)}, u32[]{:S(2)}) collective-permute-start(bf16[2,1024,128]{2,1,0:T(8,128)(2,1)S(1)} %get-tuple-element.111), channel_id=1, source_target_pairs={{0,8},{4,12},{8,0},{12,4},{16,24},{20,28},{24,16},{28,20},{1,9},{5... | collective-permute-start | bytes 1572872 | tf_op jit(solution)/shard_map/ppermute | solution.py:376
  105.4 1.5 %collective-permute-start.24 = (bf16[2,1024,128]{2,1,0:T(8,128)(2,1)S(1)}, bf16[2,1024,128]{2,1,0:T(8,128)(2,1)S(1)}, u32[]{:S(2)}, u32[]{:S(2)}) collective-permute-start(bf16[2,1024,128]{2,1,0:T(8,128)(2,1)S(1)} %get-tuple-element.112), channel_id=1, source_target_pairs={{0,16},{4,20},{8,24},{12,28},{16,0},{20,4},{24,8},{28,12},{1,17},{... | collective-permute-start | bytes 1572872 | tf_op jit(solution)/shard_map/ppermute | solution.py:376
  106.9 7.3 %collective-permute-start.16 = (bf16[256,256]{1,0:T(8,128)(2,1)S(1)}, bf16[256,256]{1,0:T(8,128)(2,1)S(1)}, u32[]{:S(2)}, u32[]{:S(2)}) collective-permute-start(bf16[256,256]{1,0:T(8,128)(2,1)S(1)} %copy-done.2), channel_id=1, source_target_pairs={{0,2},{1,3},{2,0},{3,1},{4,6},{5,7},{6,4},{7,5},{8,10},{9,11},{10,... | collective-permute-start | bytes 393224 | tf_op jit(solution)/shard_map/ppermute | solution.py:549
  114.2 2.6 %place_rows.3 = bf16[8192,256]{1,0:T(8,128)(2,1)} custom-call(s32[4]{0:T(128)S(1)} %broadcast_xor_fusion.1.place, bf16[2048,256]{1,0:T(8,128)(2,1)} %collective-permute-done.12.refs_0_, bf16[2048,256]{1,0:T(8,128)(2,1)S(1)} %collective-permute-done.18.refs_1_, bf16[8192,256]{1,0:T(8,128)(2,1)} %place_rows.2.refs_2_), custom_call_target="tpu_custom_call", output_to_operand_aliasing={{}: (3, {})} | custom-call | bytes 4194304 | tf_op jit(solution)/shard_map/place_rows/pallas_call | solution.py:496
  116.8 2.5 %weight_keep.1 = (f32[2,1024,128]{2,1,0:T(8,128)S(1)}, f32[2,1024,128]{2,1,0:T(8,128)S(1)}) custom-call(s32[5]{0:T(128)S(1)} %stack.100.place, bf16[32,2048,256]{2,1,0:T(8,128)(2,1)} %get-tuple-element.96.held, bf16[256,256]{1,0:T(8,128)(2,1)S(1)} %copy-done.2, bf16[4,1024,128]{2,1,0:T(8,128)(2,1)S(1)} %collective-permute-done.17.refs_0_), custom_call_target="tpu_custom_call" | custom-call | flops 268435456 | bytes 2097152 | tf_op jit(solution)/shard_map/weight_keep/pallas_call | solution.py:334
  119.3 0.9 collective-permute-done.16.refs_2_
  120.2 1.2 collective-permute-start.21
  121.4 4.0 %collective-permute-done.21.refs_3_ = bf16[256,256]{1,0:T(8,128)(2,1)S(1)} collective-permute-done((bf16[256,256]{1,0:T(8,128)(2,1)S(1)}, bf16[256,256]{1,0:T(8,128)(2,1)S(1)}, u32[]{:S(2)}, u32[]{:S(2)}) %collective-permute-start.21) | collective-permute-done | bytes 131104 | tf_op jit(solution)/shard_map/ppermute | solution.py:549
  126.1 0.7 collective-permute-start.26
  126.8 3.9 %input_gradient.1 = bf16[256,2048]{1,0:T(8,128)(2,1)} custom-call(s32[8]{0:T(128)S(1)} %broadcast_xor_fusion.place, bf16[256,256]{1,0:T(8,128)(2,1)S(1)} %copy-done.2, bf16[256,256]{1,0:T(8,128)(2,1)S(1)} %collective-permute-done.20.refs_1_, bf16[256,256]{1,0:T(8,128)(2,1)S(1)} %collective-permute-done.16.refs_2_, ...), custom_call_target="tpu_custom_call" | custom-call | flops 1073741824 | bytes 6291456 | tf_op jit(solution)/shard_map/input_gradient/pallas_call | solution.py:73
  130.8 2.0 %collective-permute-done.25.last_a = bf16[1024,128]{1,0:T(8,128)(2,1)S(1)} collective-permute-done((bf16[1024,128]{1,0:T(8,128)(2,1)S(1)}, bf16[1024,128]{1,0:T(8,128)(2,1)S(1)}, u32[]{:S(2)}, u32[]{:S(2)}) %collective-permute-start.25) | collective-permute-done | bytes 262176 | tf_op jit(solution)/shard_map/ppermute | solution.py:376
  133.0 1.1 weight_finish.1
  (64 shorter events, 7.8 us)
Async XLA Ops:
  0.6 30.0 %collective-permute-start = (bf16[256,2048]{1,0:T(8,128)(2,1)}, bf16[256,2048]{1,0:T(8,128)(2,1)}, u32[]{:S(2)}, u32[]{:S(2)}) collective-permute-start(bf16[256,2048]{1,0:T(8,128)(2,1)} %refs_0_.1), channel_id=1, source_target_pairs={{1,0},{2,1},{3,2},{5,4},{6,5},{7,6},{9,8},{10,9},{11,10},{13,12},{... | collective-permute-start | bytes 3145736 | tf_op jit(solution)/shard_map/ppermute | solution.py:583
  1.9 29.4 %collective-permute-start.1 = (bf16[256,2048]{1,0:T(8,128)(2,1)}, bf16[256,2048]{1,0:T(8,128)(2,1)}, u32[]{:S(2)}, u32[]{:S(2)}) collective-permute-start(bf16[256,2048]{1,0:T(8,128)(2,1)} %refs_0_.1), channel_id=1, source_target_pairs={{0,1},{1,2},{2,3},{4,5},{5,6},{6,7},{8,9},{9,10},{10,11},{12,13},{... | collective-permute-start | bytes 3145736 | tf_op jit(solution)/shard_map/ppermute | solution.py:584
  9.6 24.7 %collective-permute-start.4 = (bf16[256,256]{1,0:T(8,128)(2,1)S(1)}, bf16[256,256]{1,0:T(8,128)(2,1)S(1)}, u32[]{:S(2)}, u32[]{:S(2)}) collective-permute-start(bf16[256,256]{1,0:T(8,128)(2,1)S(1)} %get-tuple-element.131), channel_id=1, source_target_pairs={{0,1},{1,0},{2,3},{3,2},{4,5},{5,4},{6,7},{7,6},{8,9},{9,8},{10,11... | collective-permute-start | bytes 393224 | tf_op jit(solution)/shard_map/ppermute | solution.py:549
  10.7 29.1 %collective-permute-start.5 = (bf16[256,256]{1,0:T(8,128)(2,1)S(1)}, bf16[256,256]{1,0:T(8,128)(2,1)S(1)}, u32[]{:S(2)}, u32[]{:S(2)}) collective-permute-start(bf16[256,256]{1,0:T(8,128)(2,1)S(1)} %get-tuple-element.130), channel_id=1, source_target_pairs={{0,2},{1,3},{2,0},{3,1},{4,6},{5,7},{6,4},{7,5},{8,10},{9,11},{10,... | collective-permute-start | bytes 393224 | tf_op jit(solution)/shard_map/ppermute | solution.py:549
  12.7 27.0 %collective-permute-start.6 = (bf16[256,256]{1,0:T(8,128)(2,1)S(1)}, bf16[256,256]{1,0:T(8,128)(2,1)S(1)}, u32[]{:S(2)}, u32[]{:S(2)}) collective-permute-start(bf16[256,256]{1,0:T(8,128)(2,1)S(1)} %get-tuple-element.129), channel_id=1, source_target_pairs={{0,3},{1,2},{2,1},{3,0},{4,7},{5,6},{6,5},{7,4},{8,11},{9,10},{10,... | collective-permute-start | bytes 393224 | tf_op jit(solution)/shard_map/ppermute | solution.py:549
  25.3 1.4 %copy-start.9 = (s32[1,256]{1,0:T(1,128)S(1)}, s32[1,256]{1,0:T(1,128)}, u32[]{:S(2)}) copy-start(s32[1,256]{1,0:T(1,128)} %param.15) | copy-start | bytes 3076
  25.4 14.4 %copy-start = (bf16[1024,256]{1,0:T(8,128)(2,1)S(1)}, bf16[1024,256]{1,0:T(8,128)(2,1)}, u32[]{:S(2)}) copy-start(bf16[1024,256]{1,0:T(8,128)(2,1)} %get-tuple-element.80.refs_0_) | copy-start | bytes 1572868
  31.4 28.8 %collective-permute-start.2 = (bf16[256,2048]{1,0:T(8,128)(2,1)}, bf16[256,2048]{1,0:T(8,128)(2,1)}, u32[]{:S(2)}, u32[]{:S(2)}) collective-permute-start(bf16[256,2048]{1,0:T(8,128)(2,1)} %collective-permute-done.refs_0_), channel_id=1, source_target_pairs={{1,0},{2,1},{5,4},{6,5},{9,8},{10,9},{13,12},{14,13},{17,16},{18,1... | collective-permute-start | bytes 3145736 | tf_op jit(solution)/shard_map/ppermute | solution.py:583
  32.7 27.5 %collective-permute-start.3 = (bf16[256,2048]{1,0:T(8,128)(2,1)}, bf16[256,2048]{1,0:T(8,128)(2,1)}, u32[]{:S(2)}, u32[]{:S(2)}) collective-permute-start(bf16[256,2048]{1,0:T(8,128)(2,1)} %collective-permute-done.1.refs_0_), channel_id=1, source_target_pairs={{1,2},{2,3},{5,6},{6,7},{9,10},{10,11},{13,14},{14,15},{17,18},{18... | collective-permute-start | bytes 3145736 | tf_op jit(solution)/shard_map/ppermute | solution.py:584
  39.8 3.8 %copy-start.5 = (bf16[256,256]{1,0:T(8,128)(2,1)}, bf16[256,256]{1,0:T(8,128)(2,1)S(1)}, u32[]{:S(2)}) copy-start(bf16[256,256]{1,0:T(8,128)(2,1)S(1)} %collective-permute-done.5) | copy-start | bytes 393220
  39.8 3.8 %copy-start.7 = (bf16[256,256]{1,0:T(8,128)(2,1)}, bf16[256,256]{1,0:T(8,128)(2,1)S(1)}, u32[]{:S(2)}) copy-start(bf16[256,256]{1,0:T(8,128)(2,1)S(1)} %collective-permute-done.6) | copy-start | bytes 393220
  40.8 15.0 %collective-permute-start.9 = (bf16[1792,256]{1,0:T(8,128)(2,1)}, bf16[1792,256]{1,0:T(8,128)(2,1)S(1)}, u32[]{:S(2)}, u32[]{:S(2)}) collective-permute-start(bf16[1792,256]{1,0:T(8,128)(2,1)} %pad_maximum_fusion.1), channel_id=1, source_target_pairs={{0,4},{4,0},{8,12},{12,8},{16,20},{20,16},{24,28},{28,24},{1,5},{5... | collective-permute-start | bytes 2752520 | tf_op jit(solution)/shard_map/ppermute | solution.py:376
  40.8 15.0 %collective-permute-start.8 = (bf16[1024,256]{1,0:T(8,128)(2,1)S(1)}, bf16[1024,256]{1,0:T(8,128)(2,1)S(1)}, u32[]{:S(2)}, u32[]{:S(2)}) collective-permute-start(bf16[1024,256]{1,0:T(8,128)(2,1)S(1)} %copy-done), channel_id=1, source_target_pairs={{0,16},{4,20},{8,24},{12,28},{16,0},{20,4},{24,8},{28,12},{1,17},{... | collective-permute-start | bytes 1572872 | tf_op jit(solution)/shard_map/ppermute | solution.py:376
  44.3 11.5 %collective-permute-start.7 = (bf16[768,256]{1,0:T(8,128)(2,1)}, bf16[768,256]{1,0:T(8,128)(2,1)S(1)}, u32[]{:S(2)}, u32[]{:S(2)}) collective-permute-start(bf16[768,256]{1,0:T(8,128)(2,1)} %constant_dynamic-update-slice_fusion.refs_5_), channel_id=1, source_target_pairs={{0,8},{4,12},{8,0},{12,4},{16,24},{20,28},{24,16},{28,20},{1,9},{5... | collective-permute-start | bytes 1179656 | tf_op jit(solution)/shard_map/ppermute | solution.py:376
  54.9 10.8 %copy-start.6 = (bf16[256,256]{1,0:T(8,128)(2,1)S(1)}, bf16[256,256]{1,0:T(8,128)(2,1)}, u32[]{:S(2)}) copy-start(bf16[256,256]{1,0:T(8,128)(2,1)} %copy-done.5) | copy-start | bytes 393220
  54.9 10.8 %copy-start.8 = (bf16[256,256]{1,0:T(8,128)(2,1)S(1)}, bf16[256,256]{1,0:T(8,128)(2,1)}, u32[]{:S(2)}) copy-start(bf16[256,256]{1,0:T(8,128)(2,1)} %copy-done.7) | copy-start | bytes 393220
  60.2 9.6 %copy-start.12 = (s32[4]{0:T(128)S(1)}, s32[4]{0:T(128)}, u32[]{:S(2)}) copy-start(s32[4]{0:T(128)} %constant.72.clone) | copy-start | bytes 52
  60.2 29.2 %collective-permute-start.10 = (bf16[256,2048]{1,0:T(8,128)(2,1)}, bf16[256,2048]{1,0:T(8,128)(2,1)}, u32[]{:S(2)}, u32[]{:S(2)}) collective-permute-start(bf16[256,2048]{1,0:T(8,128)(2,1)} %collective-permute-done.2.refs_1_), channel_id=1, source_target_pairs={{1,0},{5,4},{9,8},{13,12},{17,16},{21,20},{25,24},{29,28}} | collective-permute-start | bytes 3145736 | tf_op jit(solution)/shard_map/ppermute | solution.py:583
  61.6 27.8 %collective-permute-start.11 = (bf16[256,2048]{1,0:T(8,128)(2,1)}, bf16[256,2048]{1,0:T(8,128)(2,1)}, u32[]{:S(2)}, u32[]{:S(2)}) collective-permute-start(bf16[256,2048]{1,0:T(8,128)(2,1)} %collective-permute-done.3.refs_0_), channel_id=1, source_target_pairs={{2,3},{6,7},{10,11},{14,15},{18,19},{22,23},{26,27},{30,31}} | collective-permute-start | bytes 3145736 | tf_op jit(solution)/shard_map/ppermute | solution.py:584
  64.3 25.1 %collective-permute-start.12 = (bf16[2048,256]{1,0:T(8,128)(2,1)}, bf16[2048,256]{1,0:T(8,128)(2,1)}, u32[]{:S(2)}, u32[]{:S(2)}) collective-permute-start(bf16[2048,256]{1,0:T(8,128)(2,1)} %pad_maximum_fusion), channel_id=1, source_target_pairs={{0,8},{4,12},{8,0},{12,4},{16,24},{20,28},{24,16},{28,20},{1,9},{5... | collective-permute-start | bytes 3145736 | tf_op jit(solution)/shard_map/ppermute | solution.py:376
  65.7 2.5 %collective-permute-start.15 = (bf16[1024,256]{1,0:T(8,128)(2,1)S(1)}, bf16[1024,256]{1,0:T(8,128)(2,1)S(1)}, u32[]{:S(2)}, u32[]{:S(2)}) collective-permute-start(bf16[1024,256]{1,0:T(8,128)(2,1)S(1)} %collective-permute-done.8.refs_2_), channel_id=1, source_target_pairs={{0,4},{4,0},{8,12},{12,8},{16,20},{20,16},{24,28},{28,24},{1,5},{5... | collective-permute-start | bytes 1572872 | tf_op jit(solution)/shard_map/ppermute | solution.py:376
  66.6 20.3 %collective-permute-start.13 = (bf16[1536,256]{1,0:T(8,128)(2,1)}, bf16[1536,256]{1,0:T(8,128)(2,1)}, u32[]{:S(2)}, u32[]{:S(2)}) collective-permute-start(bf16[1536,256]{1,0:T(8,128)(2,1)} %pad_maximum_fusion.2), channel_id=1, source_target_pairs={{0,16},{4,20},{8,24},{12,28},{16,0},{20,4},{24,8},{28,12},{1,17},{... | collective-permute-start | bytes 2359304 | tf_op jit(solution)/shard_map/ppermute | solution.py:376
  68.2 0.8 copy-start.3
  68.9 7.0 %collective-permute-start.14 = (bf16[768,256]{1,0:T(8,128)(2,1)S(1)}, bf16[768,256]{1,0:T(8,128)(2,1)}, u32[]{:S(2)}, u32[]{:S(2)}) collective-permute-start(bf16[768,256]{1,0:T(8,128)(2,1)S(1)} %collective-permute-done.7.refs_7_), channel_id=1, source_target_pairs={{0,4},{4,0},{8,12},{12,8},{16,20},{20,16},{24,28},{28,24},{1,5},{5... | collective-permute-start | bytes 1179656 | tf_op jit(solution)/shard_map/ppermute | solution.py:376
  69.8 4.3 %copy-start.4 = (bf16[1024,256]{1,0:T(8,128)(2,1)S(1)}, bf16[1024,256]{1,0:T(8,128)(2,1)}, u32[]{:S(2)}) copy-start(bf16[1024,256]{1,0:T(8,128)(2,1)} %copy-done.3) | copy-start | bytes 1572868
  89.4 10.3 %collective-permute-start.18 = (bf16[2048,256]{1,0:T(8,128)(2,1)}, bf16[2048,256]{1,0:T(8,128)(2,1)S(1)}, u32[]{:S(2)}, u32[]{:S(2)}) collective-permute-start(bf16[2048,256]{1,0:T(8,128)(2,1)} %collective-permute-done.12.refs_0_), channel_id=1, source_target_pairs={{0,4},{4,0},{8,12},{12,8},{16,20},{20,16},{24,28},{28,24},{1,5},{5... | collective-permute-start | bytes 3145736 | tf_op jit(solution)/shard_map/ppermute | solution.py:376
  89.4 10.2 %collective-permute-start.19 = (bf16[1536,256]{1,0:T(8,128)(2,1)}, bf16[1536,256]{1,0:T(8,128)(2,1)}, u32[]{:S(2)}, u32[]{:S(2)}) collective-permute-start(bf16[1536,256]{1,0:T(8,128)(2,1)} %collective-permute-done.13.refs_9_), channel_id=1, source_target_pairs={{0,4},{4,0},{8,12},{12,8},{16,20},{20,16},{24,28},{28,24},{1,5},{5... | collective-permute-start | bytes 2359304 | tf_op jit(solution)/shard_map/ppermute | solution.py:376
  99.7 4.0 %collective-permute-start.22 = (bf16[4,1024,128]{2,1,0:T(8,128)(2,1)}, bf16[4,1024,128]{2,1,0:T(8,128)(2,1)S(1)}, u32[]{:S(2)}, u32[]{:S(2)}) collective-permute-start(bf16[4,1024,128]{2,1,0:T(8,128)(2,1)} %get-tuple-element.110), channel_id=1, source_target_pairs={{0,4},{4,0},{8,12},{12,8},{16,20},{20,16},{24,28},{28,24},{1,5},{5... | collective-permute-start | bytes 3145736 | tf_op jit(solution)/shard_map/ppermute | solution.py:376
  99.8 17.0 %collective-permute-start.17 = (bf16[4,1024,128]{2,1,0:T(8,128)(2,1)}, bf16[4,1024,128]{2,1,0:T(8,128)(2,1)S(1)}, u32[]{:S(2)}, u32[]{:S(2)}) collective-permute-start(bf16[4,1024,128]{2,1,0:T(8,128)(2,1)} %get-tuple-element.97), channel_id=1, source_target_pairs={{0,4},{4,0},{8,12},{12,8},{16,20},{20,16},{24,28},{28,24},{1,5},{5... | collective-permute-start | bytes 3145736 | tf_op jit(solution)/shard_map/ppermute | solution.py:376
  100.2 0.9 copy-start.1
  103.6 3.2 %copy-start.2 = (bf16[256,256]{1,0:T(8,128)(2,1)S(1)}, bf16[256,256]{1,0:T(8,128)(2,1)}, u32[]{:S(2)}) copy-start(bf16[256,256]{1,0:T(8,128)(2,1)} %get-tuple-element.118.d_projected.refs_0_) | copy-start | bytes 393220
  103.6 10.6 %copy-start.11 = (s32[4]{0:T(128)S(1)}, s32[4]{0:T(128)}, u32[]{:S(2)}) copy-start(s32[4]{0:T(128)} %constant.73.clone) | copy-start | bytes 52
  103.8 21.6 %collective-permute-start.23 = (bf16[2,1024,128]{2,1,0:T(8,128)(2,1)S(1)}, bf16[2,1024,128]{2,1,0:T(8,128)(2,1)S(1)}, u32[]{:S(2)}, u32[]{:S(2)}) collective-permute-start(bf16[2,1024,128]{2,1,0:T(8,128)(2,1)S(1)} %get-tuple-element.111), channel_id=1, source_target_pairs={{0,8},{4,12},{8,0},{12,4},{16,24},{20,28},{24,16},{28,20},{1,9},{5... | collective-permute-start | bytes 1572872 | tf_op jit(solution)/shard_map/ppermute | solution.py:376
  105.4 20.1 %collective-permute-start.24 = (bf16[2,1024,128]{2,1,0:T(8,128)(2,1)S(1)}, bf16[2,1024,128]{2,1,0:T(8,128)(2,1)S(1)}, u32[]{:S(2)}, u32[]{:S(2)}) collective-permute-start(bf16[2,1024,128]{2,1,0:T(8,128)(2,1)S(1)} %get-tuple-element.112), channel_id=1, source_target_pairs={{0,16},{4,20},{8,24},{12,28},{16,0},{20,4},{24,8},{28,12},{1,17},{... | collective-permute-start | bytes 1572872 | tf_op jit(solution)/shard_map/ppermute | solution.py:376
  106.9 13.4 %collective-permute-start.16 = (bf16[256,256]{1,0:T(8,128)(2,1)S(1)}, bf16[256,256]{1,0:T(8,128)(2,1)S(1)}, u32[]{:S(2)}, u32[]{:S(2)}) collective-permute-start(bf16[256,256]{1,0:T(8,128)(2,1)S(1)} %copy-done.2), channel_id=1, source_target_pairs={{0,2},{1,3},{2,0},{3,1},{4,6},{5,7},{6,4},{7,5},{8,10},{9,11},{10,... | collective-permute-start | bytes 393224 | tf_op jit(solution)/shard_map/ppermute | solution.py:549
  114.2 7.2 %collective-permute-start.20 = (bf16[256,256]{1,0:T(8,128)(2,1)S(1)}, bf16[256,256]{1,0:T(8,128)(2,1)S(1)}, u32[]{:S(2)}, u32[]{:S(2)}) collective-permute-start(bf16[256,256]{1,0:T(8,128)(2,1)S(1)} %copy-done.2), channel_id=1, source_target_pairs={{0,1},{1,0},{2,3},{3,2},{4,5},{5,4},{6,7},{7,6},{8,9},{9,8},{10,11... | collective-permute-start | bytes 393224 | tf_op jit(solution)/shard_map/ppermute | solution.py:549
  119.3 7.5 %copy-start.10 = (s32[8]{0:T(128)S(1)}, s32[8]{0:T(128)}, u32[]{:S(2)}) copy-start(s32[8]{0:T(128)} %constant.74.clone) | copy-start | bytes 100
  120.2 5.2 %collective-permute-start.21 = (bf16[256,256]{1,0:T(8,128)(2,1)S(1)}, bf16[256,256]{1,0:T(8,128)(2,1)S(1)}, u32[]{:S(2)}, u32[]{:S(2)}) collective-permute-start(bf16[256,256]{1,0:T(8,128)(2,1)S(1)} %collective-permute-done.16.refs_2_), channel_id=1, source_target_pairs={{0,1},{1,0},{2,3},{3,2},{4,5},{5,4},{6,7},{7,6},{8,9},{9,8},{10,11... | collective-permute-start | bytes 393224 | tf_op jit(solution)/shard_map/ppermute | solution.py:549
  125.5 7.2 %collective-permute-start.25 = (bf16[1024,128]{1,0:T(8,128)(2,1)S(1)}, bf16[1024,128]{1,0:T(8,128)(2,1)S(1)}, u32[]{:S(2)}, u32[]{:S(2)}) collective-permute-start(bf16[1024,128]{1,0:T(8,128)(2,1)S(1)} %get-tuple-element.116), channel_id=1, source_target_pairs={{0,16},{4,20},{8,24},{12,28},{16,0},{20,4},{24,8},{28,12},{1,17},{... | collective-permute-start | bytes 786440 | tf_op jit(solution)/shard_map/ppermute | solution.py:376
  126.1 6.8 %collective-permute-start.26 = (bf16[1024,128]{1,0:T(8,128)(2,1)S(1)}, bf16[1024,128]{1,0:T(8,128)(2,1)S(1)}, u32[]{:S(2)}, u32[]{:S(2)}) collective-permute-start(bf16[1024,128]{1,0:T(8,128)(2,1)S(1)} %get-tuple-element.117), channel_id=1, source_target_pairs={{0,8},{4,12},{8,0},{12,4},{16,24},{20,28},{24,16},{28,20},{1,9},{5... | collective-permute-start | bytes 786440 | tf_op jit(solution)/shard_map/ppermute | solution.py:376

commit v15 on v13

--- a/solution.py
+++ b/solution.py
@@ -203,16 +203,15 @@
                 copies = fetch_parts(order, held, range(4), buffer, part_sems)
             columns = slice(g * HD, (g + 1) * HD)
             query, grad = queries[:, columns], d_out[:, columns]
-            scores = (
-                lax.dot_general(keys, query, across, preferred_element_type=jnp.float32) * factor
-            )
+            scores = lax.dot_general(keys, query, across, preferred_element_type=jnp.float32)
             scores = jnp.where(seen, scores, -1e30)
-            weights = jnp.exp(scores - jnp.max(scores, axis=0, keepdims=True))
-            probs = weights / jnp.sum(weights, axis=0, keepdims=True)
-            probs_low = probs.astype(jnp.bfloat16)
+            highest = jnp.max(scores, axis=0, keepdims=True)
+            weights = jnp.exp2((scores - highest) * (factor * math.log2(math.e)))
+            share = 1.0 / jnp.sum(weights, axis=0, keepdims=True)
+            probs_low = (weights * share).astype(jnp.bfloat16)
             d_probs = lax.dot_general(values, grad, across, preferred_element_type=jnp.float32)
             rowdot = jnp.sum(probs_low.astype(jnp.float32) * d_probs, axis=0, keepdims=True)
-            d_scores = (probs * (d_probs - rowdot) * factor).astype(jnp.bfloat16)
+            d_scores = (weights * (d_probs - rowdot) * (share * factor)).astype(jnp.bfloat16)
             d_queries[:, columns] = lax.dot_general(
                 d_scores, keys, (((0,), (0,)), ((), ())), preferred_element_type=jnp.float32
             ).astype(jnp.bfloat16)
@@ -425,8 +424,15 @@
 
 class PlaneGather:
     def __init__(self, own_cache, own_rows):
-        self.own = own_cache, own_rows
+        self.height, self.count = own_cache.shape[0], own_rows.shape[0]
+        self.cut = (self.height + self.count) // 2
         self.both = jnp.concatenate([own_cache, own_rows], axis=0)
+        short = self.height - self.cut
+        self.own = (
+            own_cache[: self.cut],
+            jnp.concatenate([own_cache[self.cut :], own_rows], axis=0),
+        )
+        self.short = short
 
     def first(self):
         swap = plane()[3]
@@ -434,12 +440,12 @@
 
     def second(self):
         swap = plane()[3]
-        rows_x, cache_y, _ = self.got
+        second_x, first_y, _ = self.got
         packs = (
-            swap(jnp.concatenate([self.own[0], cache_y], axis=0), 2),
-            swap(jnp.concatenate([self.own[1], rows_x], axis=0), 4),
+            swap(jnp.concatenate([self.own[0], first_y], axis=0), 2),
+            swap(jnp.concatenate([self.own[1], second_x], axis=0), 4),
         )
-        return packs, (swap(rows_x, 1), swap(cache_y, 1))
+        return packs, (swap(second_x, 1), swap(first_y, 1))
 
     def third(self):
         swap = plane()[3]
@@ -449,36 +455,39 @@
         return lax.axis_index("dp").astype(jnp.int32) ^ jnp.array(bits, dtype=jnp.int32)
 
     def lay(self, swapped, n_rows):
-        arrays = [self.own[0], self.got[2], self.got[1], swapped[1]]
-        return place_rows(arrays, [(k, 0) for k in range(4)], self.where([0, 1, 4, 5]),
-                          self.own[0].shape[0], n_rows, [])
+        arrays = [self.both, self.got[2], self.got[1], swapped[1], self.got[0], swapped[0]]
+        cut, short = self.cut, self.short
+        parts = [(0, 0, 0, self.height), (1, 0, 0, self.height), (2, 0, 0, cut), (3, 0, 0, cut)]
+        parts += [(4, 0, cut, short), (5, 0, cut, short)]
+        return place_rows(arrays, parts, self.where([0, 1, 4, 5, 2, 3]), self.height, n_rows, [])
 
     def lay_rest(self, laid):
-        height = self.own[0].shape[0]
-        parts = [(0, 0), (0, height), (1, 0), (1, height)]
-        arrays = [self.packs[0], self.packs_other[0]]
-        return place_rows(
-            arrays, parts, self.where([2, 6, 3, 7]), height, laid.shape[0], [laid]
-        )
+        cut, short = self.cut, self.short
+        size = self.own[1].shape[0]
+        arrays = [self.packs[0], self.packs_other[0], self.packs[1], self.packs_other[1]]
+        parts = [(0, 0, 0, cut), (0, cut, 0, cut), (1, 0, 0, cut), (1, cut, 0, cut)]
+        parts += [(2, 0, cut, short), (2, size, cut, short)]
+        parts += [(3, 0, cut, short), (3, size, cut, short)]
+        devices = self.where([2, 6, 3, 7, 4, 6, 5, 7])
+        return place_rows(arrays, parts, devices, self.height, laid.shape[0], [laid])
 
     def feature_rows(self):
-        height, count = self.own[0].shape[0], self.own[1].shape[0]
+        size, short = self.own[1].shape[0], self.short
         arrays = [self.own[1], self.got[2], self.got[0], self.swapped[0]]
         arrays += [self.packs[1], self.packs_other[1]]
-        parts = [(0, 0), (1, height), (2, 0), (3, 0), (4, 0), (4, count), (5, 0), (5, count)]
+        parts = [(0, short), (1, self.height), (2, short), (3, short)]
+        parts += [(4, short), (4, size + short), (5, short), (5, size + short)]
         return arrays, parts, self.where([0, 1, 2, 3, 4, 6, 5, 7])
 
 
 def place_rows_kernel(height, parts, place, *refs):
     out, sems = refs[-2:]
     copies = []
-    for k, (which, row) in enumerate(parts):
-        start = pl.multiple_of(place[k] * height, height)
+    for k, (which, row, first, count) in enumerate(parts):
+        start = pl.multiple_of(place[k] * height + first, math.gcd(height, first or height))
         copies.append(
             pltpu.make_async_copy(
-                refs[which].at[pl.ds(row, height), :],
-                out.at[pl.ds(start, height), :],
-                sems.at[k],
+                refs[which].at[pl.ds(row, count), :], out.at[pl.ds(start, count), :], sems.at[k]
             )
         )
     for copy in copies:
@@ -572,8 +581,6 @@
         zero = 0 * me_z
         orders = weight_orders() if tuned else [jnp.zeros((5,), jnp.int32)]
         total, held = absorb([tokens], zero, me_z, cached, total, None, n_z)
-        if tuned:
-            gather = PlaneGather(own_cache, jnp.concatenate(blocks, axis=0))
         from_low, from_high = tokens, tokens
         for s in range(1, n_z):
             low, high = me_z - s, me_z + s
@@ -585,6 +592,8 @@
                 from_high, from_low, held, allowed, orders, here = lax.optimization_barrier(
                     (from_high, from_low, held, allowed, orders, here)
                 )
+                blocks = lax.optimization_barrier((blocks, from_high, from_low))[0]
+                gather = PlaneGather(own_cache, jnp.concatenate(blocks, axis=0))
             elif tuned and s == 2:
                 from_high, from_low, held, gather.got = lax.optimization_barrier(
                     (from_high, from_low, held, gather.first())

time: 133 us -> 136 us (1.023)
  local copies, waits for them, and re-layouts: 7.55 us -> 13.2 us
  waiting for transfers between devices: 34.3 us -> 29.4 us
    ppermute x3, waiting for transfers between devices: 10 us -> 2.86 us  [body(): lax.ppermute(from_high, 'tensor', [(z + 1, z) for z in range(n_z - s)])]
    unnamed x28 -> x31, local copies, waits for them, and re-layouts: 3.06 us -> 6.49 us
    ppermute x15, waiting for transfers between devices: 14.5 us -> 16.7 us  [swap(): return lax.ppermute(value, 'dp', [(i, i ^ bit) for i in range(8)])]
    slice x0 -> x1, local copies, waits for them, and re-layouts: none -> 2.12 us  [__init__(): own_cache[:self.cut]]
    ppermute x6, starting transfers between devices: 12.4 us -> 13.9 us  [pair(): return lax.ppermute(value, 'tensor', [(z, z ^ s) for z in range(n_z)])]
    concatenate x3 -> x2, other arithmetic: 2.96 us -> 2.95 us  [the longest x1 2.14 us: second(): jnp.concatenate([self.own[0], first_y], axis=0)]
  transfers between devices with their start and end apart: 27 -> 27, of which waited for: 10 -> 10; matrix products, arithmetic and copies ran while one was open for 9% -> 12% of each run, Pallas kernels for 34% -> 34%
where the time goes in v15:
time: 136 us; the launch traced here: 135 us
  Pallas kernels  46.8 us (34%)
  starting transfers between devices  39.1 us (29%)
  waiting for transfers between devices  29.4 us (22%)
  local copies, waits for them, and re-layouts  13.2 us (10%)
  other arithmetic  5.58 us (4%)
    pallas_call x4, Pallas kernels, absorb(): pl.pallas_call(functools.partial(absorb_kernel, len(chunks)), in_specs=[p...  17 us
    ppermute x15, waiting for transfers between devices, swap(): return lax.ppermute(value, 'dp', [(i, i ^ bit) for i in range(8)])  16.7 us
    ppermute x6, starting transfers between devices, pair(): return lax.ppermute(value, 'tensor', [(z, z ^ s) for z in range(n_z)])  13.9 us
    ppermute x15, starting transfers between devices, swap(): return lax.ppermute(value, 'dp', [(i, i ^ bit) for i in range(8)])  11.4 us
    ppermute x3, starting transfers between devices, body(): lax.ppermute(from_low, 'tensor', [(z, z + 1) for z in range(s - 1, n_z -...  9.85 us
    pallas_call x1, Pallas kernels, attend(): pl.pallas_call(functools.partial(attend_kernel, len(chunks)), in_specs=[p...  9.81 us
    ppermute x6, waiting for transfers between devices, pair(): return lax.ppermute(value, 'tensor', [(z, z ^ s) for z in range(n_z)])  9.12 us
    unnamed x31, local copies, waits for them, and re-layouts  6.49 us
  transfers between devices with their start and end apart: 27, of which 10 were waited for; matrix products, arithmetic and copies ran while one was open for 12% of the time, Pallas kernels for 34%

profile of v15, /device:TPU:0, one launch (start us, length us, event | category | flops | bytes accessed | tf_op | source)
XLA Modules:
  0.0 135.0 jit_solution(12496989566837046378)
XLA Ops:
  0.6 1.3 collective-permute-start
  1.9 6.5 %collective-permute-start.1 = (bf16[256,2048]{1,0:T(8,128)(2,1)}, bf16[256,2048]{1,0:T(8,128)(2,1)}, u32[]{:S(2)}, u32[]{:S(2)}) collective-permute-start(bf16[256,2048]{1,0:T(8,128)(2,1)} %refs_0_.1), channel_id=1, source_target_pairs={{0,1},{1,2},{2,3},{4,5},{5,6},{6,7},{8,9},{9,10},{10,11},{12,13},{... | collective-permute-start | bytes 3145736 | tf_op jit(solution)/shard_map/ppermute | solution.py:588
  8.5 1.1 constant_dynamic-slice_fusion
  9.5 1.1 collective-permute-start.4
  10.7 2.1 %collective-permute-start.5 = (bf16[256,256]{1,0:T(8,128)(2,1)S(1)}, bf16[256,256]{1,0:T(8,128)(2,1)S(1)}, u32[]{:S(2)}, u32[]{:S(2)}) collective-permute-start(bf16[256,256]{1,0:T(8,128)(2,1)S(1)} %get-tuple-element.130), channel_id=1, source_target_pairs={{0,2},{1,3},{2,0},{3,1},{4,6},{5,7},{6,4},{7,5},{8,10},{9,11},{10,... | collective-permute-start | bytes 393224 | tf_op jit(solution)/shard_map/ppermute | solution.py:555
  12.7 1.4 %collective-permute-start.6 = (bf16[256,256]{1,0:T(8,128)(2,1)S(1)}, bf16[256,256]{1,0:T(8,128)(2,1)S(1)}, u32[]{:S(2)}, u32[]{:S(2)}) collective-permute-start(bf16[256,256]{1,0:T(8,128)(2,1)S(1)} %get-tuple-element.129), channel_id=1, source_target_pairs={{0,3},{1,2},{2,1},{3,0},{4,7},{5,6},{6,5},{7,4},{8,11},{9,10},{10,... | collective-permute-start | bytes 393224 | tf_op jit(solution)/shard_map/ppermute | solution.py:555
  14.1 4.9 %optimizer.1 = (f32[1024,256]{1,0:T(8,128)}, f32[1024,256]{1,0:T(8,128)}, f32[1024,256]{1,0:T(8,128)}, bf16[1024,256]{1,0:T(8,128)(2,1)}) custom-call(s32[1]{0:T(128)} %bitcast.place, bf16[8192,256]{1,0:T(8,128)(2,1)} %refs_3_.3, f32[1024,256]{1,0:T(8,128)} %master.1, f32[1024,256]{1,0:T(8,128)} %moment.1, f32[1024,256]{1,0:T(8,128)} %second.1, f32[1024,256]{1,0:T(8,128)} %grad.1), custom_call_target="tpu_custom_call" | custom-call | flops 10485760 | bytes 8388608 | tf_op jit(solution)/shard_map/optimizer/pallas_call | solution.py:51
  19.7 1.5 %constant_dynamic-update-slice_fusion.8 = (bf16[1792,256]{1,0:T(8,128)(2,1)}, bf16[128,256]{1,0:T(8,128)(2,1)S(1)}) fusion(bf16[1024,256]{1,0:T(8,128)(2,1)} %get-tuple-element.80), kind=kLoop, calls=%fused_computation.13 | loop fusion | bytes 196608
  21.2 0.8 fusion.1.refs_5_
  22.0 1.3 constant_dynamic-slice_fusion.3.refs_4_
  24.0 4.3 %absorb.4 = (f32[256,256]{1,0:T(8,128)}, bf16[32,2048,256]{2,1,0:T(8,128)(2,1)}) custom-call(s32[3]{0:T(128)} %get-tuple-element.142.place, bf16[256,2048]{1,0:T(8,128)(2,1)} %refs_0_.1, f32[256,256]{1,0:T(8,128)} %broadcast_in_dim.2.refs_1_, bf16[8192,256]{1,0:T(8,128)(2,1)} %refs_3_.3), custom_call_target="tpu_custom_call" | custom-call | flops 268435456 | bytes 3145728 | tf_op jit(solution)/shard_map/absorb/pallas_call | solution.py:140
  29.2 1.5 %collective-permute-done.refs_0_ = bf16[256,2048]{1,0:T(8,128)(2,1)} collective-permute-done((bf16[256,2048]{1,0:T(8,128)(2,1)}, bf16[256,2048]{1,0:T(8,128)(2,1)}, u32[]{:S(2)}, u32[]{:S(2)}) %collective-permute-start) | collective-permute-done | bytes 1048608 | tf_op jit(solution)/shard_map/ppermute | solution.py:587
  31.4 1.3 collective-permute-start.2
  32.7 1.7 %collective-permute-start.3 = (bf16[256,2048]{1,0:T(8,128)(2,1)}, bf16[256,2048]{1,0:T(8,128)(2,1)}, u32[]{:S(2)}, u32[]{:S(2)}) collective-permute-start(bf16[256,2048]{1,0:T(8,128)(2,1)} %collective-permute-done.1.refs_0_), channel_id=1, source_target_pairs={{1,2},{2,3},{5,6},{6,7},{9,10},{10,11},{13,14},{14,15},{17,18},{18... | collective-permute-start | bytes 3145736 | tf_op jit(solution)/shard_map/ppermute | solution.py:588
  34.3 5.4 %collective-permute-done.5 = bf16[256,256]{1,0:T(8,128)(2,1)S(1)} collective-permute-done((bf16[256,256]{1,0:T(8,128)(2,1)S(1)}, bf16[256,256]{1,0:T(8,128)(2,1)S(1)}, u32[]{:S(2)}, u32[]{:S(2)}) %collective-permute-start.5) | collective-permute-done | bytes 131104 | tf_op jit(solution)/shard_map/ppermute | solution.py:555
  41.8 2.1 %slice.7 = bf16[896,256]{1,0:T(8,128)(2,1)} slice(bf16[1024,256]{1,0:T(8,128)(2,1)} %get-tuple-element.80), slice={[0:896], [0:256]} | slice | bytes 917504 | tf_op jit(solution)/shard_map/slice | solution.py:432
  43.9 1.5 %collective-permute-start.8 = (bf16[896,256]{1,0:T(8,128)(2,1)}, bf16[896,256]{1,0:T(8,128)(2,1)}, u32[]{:S(2)}, u32[]{:S(2)}) collective-permute-start(bf16[896,256]{1,0:T(8,128)(2,1)} %slice.7), channel_id=1, source_target_pairs={{0,16},{4,20},{8,24},{12,28},{16,0},{20,4},{24,8},{28,12},{1,17},{... | collective-permute-start | bytes 1376264 | tf_op jit(solution)/shard_map/ppermute | solution.py:375
  45.4 0.8 pad_maximum_fusion.1.refs_5_
  46.2 1.5 %collective-permute-start.7 = (bf16[896,256]{1,0:T(8,128)(2,1)}, bf16[896,256]{1,0:T(8,128)(2,1)S(1)}, u32[]{:S(2)}, u32[]{:S(2)}) collective-permute-start(bf16[896,256]{1,0:T(8,128)(2,1)} %pad_maximum_fusion.1.refs_5_), channel_id=1, source_target_pairs={{0,8},{4,12},{8,0},{12,4},{16,24},{20,28},{24,16},{28,20},{1,9},{5... | collective-permute-start | bytes 1376264 | tf_op jit(solution)/shard_map/ppermute | solution.py:375
  48.3 4.2 %absorb.5 = (f32[256,256]{1,0:T(8,128)}, bf16[32,2048,256]{2,1,0:T(8,128)(2,1)}) custom-call(s32[3]{0:T(128)} %get-tuple-element.140.place, bf16[256,2048]{1,0:T(8,128)(2,1)} %collective-permute-done.1.refs_0_, f32[256,256]{1,0:T(8,128)} %get-tuple-element.75.refs_1_, bf16[8192,256]{1,0:T(8,128)(2,1)} %refs_3_.3, ...), custom_call_target="tpu_custom_call", output_to_operand_aliasing={{1}: (4, {})} | custom-call | flops 268435456 | bytes 3145728 | tf_op jit(solution)/shard_map/absorb/pallas_call | solution.py:140
  52.6 4.2 %absorb.6 = (f32[256,256]{1,0:T(8,128)}, bf16[32,2048,256]{2,1,0:T(8,128)(2,1)}) custom-call(s32[3]{0:T(128)} %get-tuple-element.141.place, bf16[256,2048]{1,0:T(8,128)(2,1)} %collective-permute-done.refs_0_, f32[256,256]{1,0:T(8,128)} %get-tuple-element.77.refs_1_, bf16[8192,256]{1,0:T(8,128)(2,1)} %refs_3_.3, ...), custom_call_target="tpu_custom_call", output_to_operand_aliasing={{1}: (4, {})} | custom-call | flops 268435456 | bytes 3145728 | tf_op jit(solution)/shard_map/absorb/pallas_call | solution.py:140
  56.9 1.9 %collective-permute-done.7.refs_4_.refs_7_ = bf16[896,256]{1,0:T(8,128)(2,1)S(1)} collective-permute-done((bf16[896,256]{1,0:T(8,128)(2,1)}, bf16[896,256]{1,0:T(8,128)(2,1)S(1)}, u32[]{:S(2)}, u32[]{:S(2)}) %collective-permute-start.7) | collective-permute-done | bytes 458784 | tf_op jit(solution)/shard_map/ppermute | solution.py:375
  58.8 1.4 %collective-permute-done.2.refs_1_ = bf16[256,2048]{1,0:T(8,128)(2,1)} collective-permute-done((bf16[256,2048]{1,0:T(8,128)(2,1)}, bf16[256,2048]{1,0:T(8,128)(2,1)}, u32[]{:S(2)}, u32[]{:S(2)}) %collective-permute-start.2) | collective-permute-done | bytes 1048608 | tf_op jit(solution)/shard_map/ppermute | solution.py:587
  60.2 1.3 collective-permute-start.10
  61.5 1.6 %collective-permute-start.11 = (bf16[256,2048]{1,0:T(8,128)(2,1)}, bf16[256,2048]{1,0:T(8,128)(2,1)}, u32[]{:S(2)}, u32[]{:S(2)}) collective-permute-start(bf16[256,2048]{1,0:T(8,128)(2,1)} %collective-permute-done.3.refs_0_), channel_id=1, source_target_pairs={{2,3},{6,7},{10,11},{14,15},{18,19},{22,23},{26,27},{30,31}} | collective-permute-start | bytes 3145736 | tf_op jit(solution)/shard_map/ppermute | solution.py:588
  63.1 2.1 %pad_maximum_fusion = bf16[1792,256]{1,0:T(8,128)(2,1)} fusion(bf16[896,256]{1,0:T(8,128)(2,1)} %collective-permute-done.8.refs_2_, bf16[896,256]{1,0:T(8,128)(2,1)} %slice.7), kind=kLoop, calls=%fused_computation | loop fusion | flops 1835008 | bytes 1835008 | tf_op jit(solution)/shard_map/concatenate | solution.py:445
  65.3 1.4 %collective-permute-start.12 = (bf16[1792,256]{1,0:T(8,128)(2,1)}, bf16[1792,256]{1,0:T(8,128)(2,1)}, u32[]{:S(2)}, u32[]{:S(2)}) collective-permute-start(bf16[1792,256]{1,0:T(8,128)(2,1)} %pad_maximum_fusion), channel_id=1, source_target_pairs={{0,8},{4,12},{8,0},{12,4},{16,24},{20,28},{24,16},{28,20},{1,9},{5... | collective-permute-start | bytes 2752520 | tf_op jit(solution)/shard_map/ppermute | solution.py:375
  66.7 0.8 constant_dynamic-update-slice_fusion.4
  67.5 1.5 %collective-permute-start.13 = (bf16[1792,256]{1,0:T(8,128)(2,1)}, bf16[1792,256]{1,0:T(8,128)(2,1)S(1)}, u32[]{:S(2)}, u32[]{:S(2)}) collective-permute-start(bf16[1792,256]{1,0:T(8,128)(2,1)} %constant_dynamic-update-slice_fusion.4), channel_id=1, source_target_pairs={{0,16},{4,20},{8,24},{12,28},{16,0},{20,4},{24,8},{28,12},{1,17},{... | collective-permute-start | bytes 2752520 | tf_op jit(solution)/shard_map/ppermute | solution.py:375
  69.0 0.8 copy-done.4
  70.6 4.3 %absorb.7 = (f32[256,256]{1,0:T(8,128)}, bf16[32,2048,256]{2,1,0:T(8,128)(2,1)}) custom-call(s32[3]{0:T(128)} %pad_add_fusion.4.place, bf16[256,2048]{1,0:T(8,128)(2,1)} %collective-permute-done.3.refs_0_, bf16[256,2048]{1,0:T(8,128)(2,1)} %collective-permute-done.2.refs_1_, f32[256,256]{1,0:T(8,128)} %get-tuple-element.86.refs_2_, ...), custom_call_target="tpu_custom_call", output_to_operand_aliasing={{1}: (5, {})} | custom-call | flops 268435456 | bytes 3145728 | tf_op jit(solution)/shard_map/absorb/pallas_call | solution.py:140
  74.9 1.2 copy-done.3
  76.1 2.5 %place_rows.2.refs_4_ = bf16[8192,256]{1,0:T(8,128)(2,1)} custom-call(s32[6]{0:T(128)S(1)} %broadcast_xor_fusion.2.place, bf16[1792,256]{1,0:T(8,128)(2,1)S(1)} %copy-done.3, bf16[1792,256]{1,0:T(8,128)(2,1)S(1)} %collective-permute-done.9.refs_1_.refs_6_, bf16[896,256]{1,0:T(8,128)(2,1)} %collective-permute-done.8.refs_2_, ...), custom_call_target="tpu_custom_call" | custom-call | bytes 6291456 | tf_op jit(solution)/shard_map/place_rows/pallas_call | solution.py:502
  78.6 7.5 %collective-permute-done.12.refs_0_ = bf16[1792,256]{1,0:T(8,128)(2,1)} collective-permute-done((bf16[1792,256]{1,0:T(8,128)(2,1)}, bf16[1792,256]{1,0:T(8,128)(2,1)}, u32[]{:S(2)}, u32[]{:S(2)}) %collective-permute-start.12) | collective-permute-done | bytes 917536 | tf_op jit(solution)/shard_map/ppermute | solution.py:375
  86.1 4.4 %collective-permute-done.13.refs_2_.refs_9_ = bf16[1792,256]{1,0:T(8,128)(2,1)S(1)} collective-permute-done((bf16[1792,256]{1,0:T(8,128)(2,1)}, bf16[1792,256]{1,0:T(8,128)(2,1)S(1)}, u32[]{:S(2)}, u32[]{:S(2)}) %collective-permute-start.13) | collective-permute-done | bytes 917536 | tf_op jit(solution)/shard_map/ppermute | solution.py:375
  90.9 9.8 %attend.1 = (bf16[32,2048,256]{2,1,0:T(8,128)(2,1)}, bf16[256,1024]{1,0:T(8,128)(2,1)}, bf16[256,256]{1,0:T(8,128)(2,1)}, bf16[4,1024,128]{2,1,0:T(8,128)(2,1)}, bf16[4,1024,128]{2,1,0:T(8,128)(2,1)}) custom-call(s32[3]{0:T(128)} %get-tuple-element.143.place, s32[5]{0:T(128)} %stack.98.order, ...), custom_call_target="tpu_custom_call", output_to_operand_aliasing={{0}: (6, {})} | custom-call | flops 805306368 | bytes 2097152 | tf_op jit(solution)/shard_map/attend/pallas_call | solution.py:234
  101.4 0.9 copy-done.6
  102.3 2.5 %weight_send.1 = (f32[2,1024,128]{2,1,0:T(8,128)S(1)}, f32[2,1024,128]{2,1,0:T(8,128)S(1)}) custom-call(s32[5]{0:T(128)S(1)} %stack.100.place, bf16[32,2048,256]{2,1,0:T(8,128)(2,1)} %get-tuple-element.99.held, bf16[256,256]{1,0:T(8,128)(2,1)S(1)} %copy-done.6), custom_call_target="tpu_custom_call" | custom-call | flops 268435456 | bytes 2097152 | tf_op jit(solution)/shard_map/weight_send/pallas_call | solution.py:333
  105.7 1.4 %collective-permute-start.23 = (bf16[2,1024,128]{2,1,0:T(8,128)(2,1)S(1)}, bf16[2,1024,128]{2,1,0:T(8,128)(2,1)S(1)}, u32[]{:S(2)}, u32[]{:S(2)}) collective-permute-start(bf16[2,1024,128]{2,1,0:T(8,128)(2,1)S(1)} %get-tuple-element.107), channel_id=1, source_target_pairs={{0,16},{4,20},{8,24},{12,28},{16,0},{20,4},{24,8},{28,12},{1,17},{... | collective-permute-start | bytes 1572872 | tf_op jit(solution)/shard_map/ppermute | solution.py:375
  107.1 6.8 %collective-permute-start.16 = (bf16[256,256]{1,0:T(8,128)(2,1)S(1)}, bf16[256,256]{1,0:T(8,128)(2,1)S(1)}, u32[]{:S(2)}, u32[]{:S(2)}) collective-permute-start(bf16[256,256]{1,0:T(8,128)(2,1)S(1)} %copy-done.7), channel_id=1, source_target_pairs={{0,3},{1,2},{2,1},{3,0},{4,7},{5,6},{6,5},{7,4},{8,11},{9,10},{10,... | collective-permute-start | bytes 393224 | tf_op jit(solution)/shard_map/ppermute | solution.py:555
  113.9 2.0 %collective-permute-start.17 = (bf16[256,256]{1,0:T(8,128)(2,1)S(1)}, bf16[256,256]{1,0:T(8,128)(2,1)S(1)}, u32[]{:S(2)}, u32[]{:S(2)}) collective-permute-start(bf16[256,256]{1,0:T(8,128)(2,1)S(1)} %copy-done.7), channel_id=1, source_target_pairs={{0,2},{1,3},{2,0},{3,1},{4,6},{5,7},{6,4},{7,5},{8,10},{9,11},{10,... | collective-permute-start | bytes 393224 | tf_op jit(solution)/shard_map/ppermute | solution.py:555
  116.5 2.8 %place_rows.3 = bf16[8192,256]{1,0:T(8,128)(2,1)} custom-call(s32[8]{0:T(128)S(1)} %broadcast_xor_fusion.1.place, bf16[1792,256]{1,0:T(8,128)(2,1)} %collective-permute-done.12.refs_0_, bf16[1792,256]{1,0:T(8,128)(2,1)} %collective-permute-done.19.refs_1_, ...), custom_call_target="tpu_custom_call", output_to_operand_aliasing={{}: (5, {})} | custom-call | bytes 8388608 | tf_op jit(solution)/shard_map/place_rows/pallas_call | solution.py:502
  119.3 2.5 %weight_keep.1 = (f32[2,1024,128]{2,1,0:T(8,128)S(1)}, f32[2,1024,128]{2,1,0:T(8,128)S(1)}) custom-call(s32[5]{0:T(128)S(1)} %stack.100.place, bf16[32,2048,256]{2,1,0:T(8,128)(2,1)} %get-tuple-element.99.held, bf16[256,256]{1,0:T(8,128)(2,1)S(1)} %copy-done.7, bf16[4,1024,128]{2,1,0:T(8,128)(2,1)S(1)} %collective-permute-done.24.refs_0_), custom_call_target="tpu_custom_call" | custom-call | flops 268435456 | bytes 2097152 | tf_op jit(solution)/shard_map/weight_keep/pallas_call | solution.py:333
  121.8 3.7 %collective-permute-done.17.refs_2_ = bf16[256,256]{1,0:T(8,128)(2,1)S(1)} collective-permute-done((bf16[256,256]{1,0:T(8,128)(2,1)S(1)}, bf16[256,256]{1,0:T(8,128)(2,1)S(1)}, u32[]{:S(2)}, u32[]{:S(2)}) %collective-permute-start.17) | collective-permute-done | bytes 131104 | tf_op jit(solution)/shard_map/ppermute | solution.py:555
  126.2 1.5 %collective-permute-start.26 = (bf16[1024,128]{1,0:T(8,128)(2,1)S(1)}, bf16[1024,128]{1,0:T(8,128)(2,1)S(1)}, u32[]{:S(2)}, u32[]{:S(2)}) collective-permute-start(bf16[1024,128]{1,0:T(8,128)(2,1)S(1)} %get-tuple-element.118), channel_id=1, source_target_pairs={{0,8},{4,12},{8,0},{12,4},{16,24},{20,28},{24,16},{28,20},{1,9},{5... | collective-permute-start | bytes 786440 | tf_op jit(solution)/shard_map/ppermute | solution.py:375
  127.7 3.4 %input_gradient.1 = bf16[256,2048]{1,0:T(8,128)(2,1)} custom-call(s32[8]{0:T(128)S(1)} %broadcast_xor_fusion.place, bf16[256,256]{1,0:T(8,128)(2,1)S(1)} %copy-done.7, bf16[256,256]{1,0:T(8,128)(2,1)S(1)} %collective-permute-done.18.refs_1_, bf16[256,256]{1,0:T(8,128)(2,1)S(1)} %collective-permute-done.17.refs_2_, ...), custom_call_target="tpu_custom_call" | custom-call | flops 1073741824 | bytes 6750208 | tf_op jit(solution)/shard_map/input_gradient/pallas_call | solution.py:73
  131.0 2.6 %collective-permute-done.25.last_a = bf16[1024,128]{1,0:T(8,128)(2,1)S(1)} collective-permute-done((bf16[1024,128]{1,0:T(8,128)(2,1)S(1)}, bf16[1024,128]{1,0:T(8,128)(2,1)S(1)}, u32[]{:S(2)}, u32[]{:S(2)}) %collective-permute-start.25) | collective-permute-done | bytes 262176 | tf_op jit(solution)/shard_map/ppermute | solution.py:375
  133.9 1.1 weight_finish.1
  (67 shorter events, 9.8 us)
Async XLA Ops:
  0.6 30.0 %collective-permute-start = (bf16[256,2048]{1,0:T(8,128)(2,1)}, bf16[256,2048]{1,0:T(8,128)(2,1)}, u32[]{:S(2)}, u32[]{:S(2)}) collective-permute-start(bf16[256,2048]{1,0:T(8,128)(2,1)} %refs_0_.1), channel_id=1, source_target_pairs={{1,0},{2,1},{3,2},{5,4},{6,5},{7,6},{9,8},{10,9},{11,10},{13,12},{... | collective-permute-start | bytes 3145736 | tf_op jit(solution)/shard_map/ppermute | solution.py:587
  1.9 29.4 %collective-permute-start.1 = (bf16[256,2048]{1,0:T(8,128)(2,1)}, bf16[256,2048]{1,0:T(8,128)(2,1)}, u32[]{:S(2)}, u32[]{:S(2)}) collective-permute-start(bf16[256,2048]{1,0:T(8,128)(2,1)} %refs_0_.1), channel_id=1, source_target_pairs={{0,1},{1,2},{2,3},{4,5},{5,6},{6,7},{8,9},{9,10},{10,11},{12,13},{... | collective-permute-start | bytes 3145736 | tf_op jit(solution)/shard_map/ppermute | solution.py:588
  9.5 24.8 %collective-permute-start.4 = (bf16[256,256]{1,0:T(8,128)(2,1)S(1)}, bf16[256,256]{1,0:T(8,128)(2,1)S(1)}, u32[]{:S(2)}, u32[]{:S(2)}) collective-permute-start(bf16[256,256]{1,0:T(8,128)(2,1)S(1)} %get-tuple-element.131), channel_id=1, source_target_pairs={{0,1},{1,0},{2,3},{3,2},{4,5},{5,4},{6,7},{7,6},{8,9},{9,8},{10,11... | collective-permute-start | bytes 393224 | tf_op jit(solution)/shard_map/ppermute | solution.py:555
  10.7 29.1 %collective-permute-start.5 = (bf16[256,256]{1,0:T(8,128)(2,1)S(1)}, bf16[256,256]{1,0:T(8,128)(2,1)S(1)}, u32[]{:S(2)}, u32[]{:S(2)}) collective-permute-start(bf16[256,256]{1,0:T(8,128)(2,1)S(1)} %get-tuple-element.130), channel_id=1, source_target_pairs={{0,2},{1,3},{2,0},{3,1},{4,6},{5,7},{6,4},{7,5},{8,10},{9,11},{10,... | collective-permute-start | bytes 393224 | tf_op jit(solution)/shard_map/ppermute | solution.py:555
  12.7 27.0 %collective-permute-start.6 = (bf16[256,256]{1,0:T(8,128)(2,1)S(1)}, bf16[256,256]{1,0:T(8,128)(2,1)S(1)}, u32[]{:S(2)}, u32[]{:S(2)}) collective-permute-start(bf16[256,256]{1,0:T(8,128)(2,1)S(1)} %get-tuple-element.129), channel_id=1, source_target_pairs={{0,3},{1,2},{2,1},{3,0},{4,7},{5,6},{6,5},{7,4},{8,11},{9,10},{10,... | collective-permute-start | bytes 393224 | tf_op jit(solution)/shard_map/ppermute | solution.py:555
  14.1 7.1 %copy-start.9 = (s32[1,256]{1,0:T(1,128)S(1)}, s32[1,256]{1,0:T(1,128)}, u32[]{:S(2)}) copy-start(s32[1,256]{1,0:T(1,128)} %param.15) | copy-start | bytes 3076
  19.7 9.5 %copy-start.8 = (bf16[1024,256]{1,0:T(8,128)(2,1)S(1)}, bf16[1024,256]{1,0:T(8,128)(2,1)}, u32[]{:S(2)}) copy-start(bf16[1024,256]{1,0:T(8,128)(2,1)} %get-tuple-element.80) | copy-start | bytes 1572868
  31.4 28.8 %collective-permute-start.2 = (bf16[256,2048]{1,0:T(8,128)(2,1)}, bf16[256,2048]{1,0:T(8,128)(2,1)}, u32[]{:S(2)}, u32[]{:S(2)}) collective-permute-start(bf16[256,2048]{1,0:T(8,128)(2,1)} %collective-permute-done.refs_0_), channel_id=1, source_target_pairs={{1,0},{2,1},{5,4},{6,5},{9,8},{10,9},{13,12},{14,13},{17,16},{18,1... | collective-permute-start | bytes 3145736 | tf_op jit(solution)/shard_map/ppermute | solution.py:587
  32.7 27.5 %collective-permute-start.3 = (bf16[256,2048]{1,0:T(8,128)(2,1)}, bf16[256,2048]{1,0:T(8,128)(2,1)}, u32[]{:S(2)}, u32[]{:S(2)}) collective-permute-start(bf16[256,2048]{1,0:T(8,128)(2,1)} %collective-permute-done.1.refs_0_), channel_id=1, source_target_pairs={{1,2},{2,3},{5,6},{6,7},{9,10},{10,11},{13,14},{14,15},{17,18},{18... | collective-permute-start | bytes 3145736 | tf_op jit(solution)/shard_map/ppermute | solution.py:588
  41.8 10.8 %copy-start.2 = (bf16[1792,256]{1,0:T(8,128)(2,1)}, bf16[1792,256]{1,0:T(8,128)(2,1)S(1)}, u32[]{:S(2)}) copy-start(bf16[1792,256]{1,0:T(8,128)(2,1)S(1)} %get-tuple-element.135.refs_0_) | copy-start | bytes 2752516
  41.8 17.0 %collective-permute-start.9 = (bf16[1792,256]{1,0:T(8,128)(2,1)S(1)}, bf16[1792,256]{1,0:T(8,128)(2,1)S(1)}, u32[]{:S(2)}, u32[]{:S(2)}) collective-permute-start(bf16[1792,256]{1,0:T(8,128)(2,1)S(1)} %get-tuple-element.135.refs_0_), channel_id=1, source_target_pairs={{0,4},{4,0},{8,12},{12,8},{16,20},{20,16},{24,28},{28,24},{1,5},{5... | collective-permute-start | bytes 2752520 | tf_op jit(solution)/shard_map/ppermute | solution.py:375
  43.9 12.9 %collective-permute-start.8 = (bf16[896,256]{1,0:T(8,128)(2,1)}, bf16[896,256]{1,0:T(8,128)(2,1)}, u32[]{:S(2)}, u32[]{:S(2)}) collective-permute-start(bf16[896,256]{1,0:T(8,128)(2,1)} %slice.7), channel_id=1, source_target_pairs={{0,16},{4,20},{8,24},{12,28},{16,0},{20,4},{24,8},{28,12},{1,17},{... | collective-permute-start | bytes 1376264 | tf_op jit(solution)/shard_map/ppermute | solution.py:375
  46.2 12.6 %collective-permute-start.7 = (bf16[896,256]{1,0:T(8,128)(2,1)}, bf16[896,256]{1,0:T(8,128)(2,1)S(1)}, u32[]{:S(2)}, u32[]{:S(2)}) collective-permute-start(bf16[896,256]{1,0:T(8,128)(2,1)} %pad_maximum_fusion.1.refs_5_), channel_id=1, source_target_pairs={{0,8},{4,12},{8,0},{12,4},{16,24},{20,28},{24,16},{28,20},{1,9},{5... | collective-permute-start | bytes 1376264 | tf_op jit(solution)/shard_map/ppermute | solution.py:375
  52.6 18.0 %copy-start.12 = (s32[6]{0:T(128)S(1)}, s32[6]{0:T(128)}, u32[]{:S(2)}) copy-start(s32[6]{0:T(128)} %constant.72.clone) | copy-start | bytes 76
  58.8 16.1 %copy-start = (bf16[1792,256]{1,0:T(8,128)(2,1)}, bf16[1792,256]{1,0:T(8,128)(2,1)S(1)}, u32[]{:S(2)}) copy-start(bf16[1792,256]{1,0:T(8,128)(2,1)S(1)} %collective-permute-done.9.refs_1_.refs_6_) | copy-start | bytes 2752516
  60.2 30.2 %collective-permute-start.10 = (bf16[256,2048]{1,0:T(8,128)(2,1)}, bf16[256,2048]{1,0:T(8,128)(2,1)}, u32[]{:S(2)}, u32[]{:S(2)}) collective-permute-start(bf16[256,2048]{1,0:T(8,128)(2,1)} %collective-permute-done.2.refs_1_), channel_id=1, source_target_pairs={{1,0},{5,4},{9,8},{13,12},{17,16},{21,20},{25,24},{29,28}} | collective-permute-start | bytes 3145736 | tf_op jit(solution)/shard_map/ppermute | solution.py:587
  61.5 29.0 %collective-permute-start.11 = (bf16[256,2048]{1,0:T(8,128)(2,1)}, bf16[256,2048]{1,0:T(8,128)(2,1)}, u32[]{:S(2)}, u32[]{:S(2)}) collective-permute-start(bf16[256,2048]{1,0:T(8,128)(2,1)} %collective-permute-done.3.refs_0_), channel_id=1, source_target_pairs={{2,3},{6,7},{10,11},{14,15},{18,19},{22,23},{26,27},{30,31}} | collective-permute-start | bytes 3145736 | tf_op jit(solution)/shard_map/ppermute | solution.py:588
  65.3 20.8 %collective-permute-start.12 = (bf16[1792,256]{1,0:T(8,128)(2,1)}, bf16[1792,256]{1,0:T(8,128)(2,1)}, u32[]{:S(2)}, u32[]{:S(2)}) collective-permute-start(bf16[1792,256]{1,0:T(8,128)(2,1)} %pad_maximum_fusion), channel_id=1, source_target_pairs={{0,8},{4,12},{8,0},{12,4},{16,24},{20,28},{24,16},{28,20},{1,9},{5... | collective-permute-start | bytes 2752520 | tf_op jit(solution)/shard_map/ppermute | solution.py:375
  66.7 2.3 %collective-permute-start.14 = (bf16[896,256]{1,0:T(8,128)(2,1)S(1)}, bf16[896,256]{1,0:T(8,128)(2,1)S(1)}, u32[]{:S(2)}, u32[]{:S(2)}) collective-permute-start(bf16[896,256]{1,0:T(8,128)(2,1)S(1)} %collective-permute-done.7.refs_4_.refs_7_), channel_id=1, source_target_pairs={{0,4},{4,0},{8,12},{12,8},{16,20},{20,16},{24,28},{28,24},{1,5},{5... | collective-permute-start | bytes 1376264 | tf_op jit(solution)/shard_map/ppermute | solution.py:375
  67.5 23.0 %collective-permute-start.13 = (bf16[1792,256]{1,0:T(8,128)(2,1)}, bf16[1792,256]{1,0:T(8,128)(2,1)S(1)}, u32[]{:S(2)}, u32[]{:S(2)}) collective-permute-start(bf16[1792,256]{1,0:T(8,128)(2,1)} %constant_dynamic-update-slice_fusion.4), channel_id=1, source_target_pairs={{0,16},{4,20},{8,24},{12,28},{16,0},{20,4},{24,8},{28,12},{1,17},{... | collective-permute-start | bytes 2752520 | tf_op jit(solution)/shard_map/ppermute | solution.py:375
  69.0 0.8 copy-start.4
  69.7 5.1 %collective-permute-start.15 = (bf16[896,256]{1,0:T(8,128)(2,1)}, bf16[896,256]{1,0:T(8,128)(2,1)}, u32[]{:S(2)}, u32[]{:S(2)}) collective-permute-start(bf16[896,256]{1,0:T(8,128)(2,1)} %collective-permute-done.8.refs_2_), channel_id=1, source_target_pairs={{0,4},{4,0},{8,12},{12,8},{16,20},{20,16},{24,28},{28,24},{1,5},{5... | collective-permute-start | bytes 1376264 | tf_op jit(solution)/shard_map/ppermute | solution.py:375
  70.6 4.3 %copy-start.5 = (bf16[896,256]{1,0:T(8,128)(2,1)S(1)}, bf16[896,256]{1,0:T(8,128)(2,1)}, u32[]{:S(2)}) copy-start(bf16[896,256]{1,0:T(8,128)(2,1)} %copy-done.4) | copy-start | bytes 1376260
  74.9 1.2 copy-start.3
  90.4 10.3 %collective-permute-start.19 = (bf16[1792,256]{1,0:T(8,128)(2,1)}, bf16[1792,256]{1,0:T(8,128)(2,1)}, u32[]{:S(2)}, u32[]{:S(2)}) collective-permute-start(bf16[1792,256]{1,0:T(8,128)(2,1)} %collective-permute-done.12.refs_0_), channel_id=1, source_target_pairs={{0,4},{4,0},{8,12},{12,8},{16,20},{20,16},{24,28},{28,24},{1,5},{5... | collective-permute-start | bytes 2752520 | tf_op jit(solution)/shard_map/ppermute | solution.py:375
  90.4 10.3 %collective-permute-start.20 = (bf16[1792,256]{1,0:T(8,128)(2,1)S(1)}, bf16[1792,256]{1,0:T(8,128)(2,1)S(1)}, u32[]{:S(2)}, u32[]{:S(2)}) collective-permute-start(bf16[1792,256]{1,0:T(8,128)(2,1)S(1)} %collective-permute-done.13.refs_2_.refs_9_), channel_id=1, source_target_pairs={{0,4},{4,0},{8,12},{12,8},{16,20},{20,16},{24,28},{28,24},{1,5},{5... | collective-permute-start | bytes 2752520 | tf_op jit(solution)/shard_map/ppermute | solution.py:375
  100.8 4.0 %collective-permute-start.21 = (bf16[4,1024,128]{2,1,0:T(8,128)(2,1)}, bf16[4,1024,128]{2,1,0:T(8,128)(2,1)S(1)}, u32[]{:S(2)}, u32[]{:S(2)}) collective-permute-start(bf16[4,1024,128]{2,1,0:T(8,128)(2,1)} %get-tuple-element.105), channel_id=1, source_target_pairs={{0,4},{4,0},{8,12},{12,8},{16,20},{20,16},{24,28},{28,24},{1,5},{5... | collective-permute-start | bytes 3145736 | tf_op jit(solution)/shard_map/ppermute | solution.py:375
  100.9 15.0 %collective-permute-start.24 = (bf16[4,1024,128]{2,1,0:T(8,128)(2,1)}, bf16[4,1024,128]{2,1,0:T(8,128)(2,1)S(1)}, u32[]{:S(2)}, u32[]{:S(2)}) collective-permute-start(bf16[4,1024,128]{2,1,0:T(8,128)(2,1)} %get-tuple-element.112), channel_id=1, source_target_pairs={{0,4},{4,0},{8,12},{12,8},{16,20},{20,16},{24,28},{28,24},{1,5},{5... | collective-permute-start | bytes 3145736 | tf_op jit(solution)/shard_map/ppermute | solution.py:375
  101.4 0.9 copy-start.6
  102.3 4.8 %copy-start.7 = (bf16[256,256]{1,0:T(8,128)(2,1)S(1)}, bf16[256,256]{1,0:T(8,128)(2,1)}, u32[]{:S(2)}) copy-start(bf16[256,256]{1,0:T(8,128)(2,1)} %get-tuple-element.119.d_projected.refs_0_) | copy-start | bytes 393220
  102.3 14.2 %copy-start.11 = (s32[8]{0:T(128)S(1)}, s32[8]{0:T(128)}, u32[]{:S(2)}) copy-start(s32[8]{0:T(128)} %constant.73.clone) | copy-start | bytes 100
  105.0 20.6 %collective-permute-start.22 = (bf16[2,1024,128]{2,1,0:T(8,128)(2,1)S(1)}, bf16[2,1024,128]{2,1,0:T(8,128)(2,1)S(1)}, u32[]{:S(2)}, u32[]{:S(2)}) collective-permute-start(bf16[2,1024,128]{2,1,0:T(8,128)(2,1)S(1)} %get-tuple-element.106), channel_id=1, source_target_pairs={{0,8},{4,12},{8,0},{12,4},{16,24},{20,28},{24,16},{28,20},{1,9},{5... | collective-permute-start | bytes 1572872 | tf_op jit(solution)/shard_map/ppermute | solution.py:375
  105.7 19.9 %collective-permute-start.23 = (bf16[2,1024,128]{2,1,0:T(8,128)(2,1)S(1)}, bf16[2,1024,128]{2,1,0:T(8,128)(2,1)S(1)}, u32[]{:S(2)}, u32[]{:S(2)}) collective-permute-start(bf16[2,1024,128]{2,1,0:T(8,128)(2,1)S(1)} %get-tuple-element.107), channel_id=1, source_target_pairs={{0,16},{4,20},{8,24},{12,28},{16,0},{20,4},{24,8},{28,12},{1,17},{... | collective-permute-start | bytes 1572872 | tf_op jit(solution)/shard_map/ppermute | solution.py:375
  107.1 14.7 %collective-permute-start.16 = (bf16[256,256]{1,0:T(8,128)(2,1)S(1)}, bf16[256,256]{1,0:T(8,128)(2,1)S(1)}, u32[]{:S(2)}, u32[]{:S(2)}) collective-permute-start(bf16[256,256]{1,0:T(8,128)(2,1)S(1)} %copy-done.7), channel_id=1, source_target_pairs={{0,3},{1,2},{2,1},{3,0},{4,7},{5,6},{6,5},{7,4},{8,11},{9,10},{10,... | collective-permute-start | bytes 393224 | tf_op jit(solution)/shard_map/ppermute | solution.py:555
  113.9 11.6 %collective-permute-start.17 = (bf16[256,256]{1,0:T(8,128)(2,1)S(1)}, bf16[256,256]{1,0:T(8,128)(2,1)S(1)}, u32[]{:S(2)}, u32[]{:S(2)}) collective-permute-start(bf16[256,256]{1,0:T(8,128)(2,1)S(1)} %copy-done.7), channel_id=1, source_target_pairs={{0,2},{1,3},{2,0},{3,1},{4,6},{5,7},{6,4},{7,5},{8,10},{9,11},{10,... | collective-permute-start | bytes 393224 | tf_op jit(solution)/shard_map/ppermute | solution.py:555
  115.9 9.6 %collective-permute-start.18 = (bf16[256,256]{1,0:T(8,128)(2,1)S(1)}, bf16[256,256]{1,0:T(8,128)(2,1)S(1)}, u32[]{:S(2)}, u32[]{:S(2)}) collective-permute-start(bf16[256,256]{1,0:T(8,128)(2,1)S(1)} %copy-done.7), channel_id=1, source_target_pairs={{0,1},{1,0},{2,3},{3,2},{4,5},{5,4},{6,7},{7,6},{8,9},{9,8},{10,11... | collective-permute-start | bytes 393224 | tf_op jit(solution)/shard_map/ppermute | solution.py:555
  119.3 8.4 %copy-start.10 = (s32[8]{0:T(128)S(1)}, s32[8]{0:T(128)}, u32[]{:S(2)}) copy-start(s32[8]{0:T(128)} %constant.74.clone) | copy-start | bytes 100
  119.3 8.4 %copy-start.1 = (bf16[1792,256]{1,0:T(8,128)(2,1)S(1)}, bf16[1792,256]{1,0:T(8,128)(2,1)}, u32[]{:S(2)}) copy-start(bf16[1792,256]{1,0:T(8,128)(2,1)} %copy-done) | copy-start | bytes 2752516
  125.6 8.1 %collective-permute-start.25 = (bf16[1024,128]{1,0:T(8,128)(2,1)S(1)}, bf16[1024,128]{1,0:T(8,128)(2,1)S(1)}, u32[]{:S(2)}, u32[]{:S(2)}) collective-permute-start(bf16[1024,128]{1,0:T(8,128)(2,1)S(1)} %get-tuple-element.117), channel_id=1, source_target_pairs={{0,16},{4,20},{8,24},{12,28},{16,0},{20,4},{24,8},{28,12},{1,17},{... | collective-permute-start | bytes 786440 | tf_op jit(solution)/shard_map/ppermute | solution.py:375
  126.2 7.7 %collective-permute-start.26 = (bf16[1024,128]{1,0:T(8,128)(2,1)S(1)}, bf16[1024,128]{1,0:T(8,128)(2,1)S(1)}, u32[]{:S(2)}, u32[]{:S(2)}) collective-permute-start(bf16[1024,128]{1,0:T(8,128)(2,1)S(1)} %get-tuple-element.118), channel_id=1, source_target_pairs={{0,8},{4,12},{8,0},{12,4},{16,24},{20,28},{24,16},{28,20},{1,9},{5... | collective-permute-start | bytes 786440 | tf_op jit(solution)/shard_map/ppermute | solution.py:375

commit v16 on v13

--- a/solution.py
+++ b/solution.py
@@ -428,18 +428,20 @@
         self.own = own_cache, own_rows
         self.both = jnp.concatenate([own_cache, own_rows], axis=0)
 
-    def first(self):
+    def first(self, held):
         swap = plane()[3]
-        return swap(self.own[1], 2), swap(self.own[0], 4), swap(self.both, 1)
+        rows_x, cache_y = swap(self.own[1], 2), swap(self.own[0], 4)
+        rows_x, cache_y, _ = lax.optimization_barrier((rows_x, cache_y, held))
+        packs = (
+            jnp.concatenate([self.own[0], cache_y], axis=0),
+            jnp.concatenate([self.own[1], rows_x], axis=0),
+        )
+        return rows_x, cache_y, swap(self.both, 1), packs
 
     def second(self):
         swap = plane()[3]
-        rows_x, cache_y, _ = self.got
-        packs = (
-            swap(jnp.concatenate([self.own[0], cache_y], axis=0), 2),
-            swap(jnp.concatenate([self.own[1], rows_x], axis=0), 4),
-        )
-        return packs, (swap(rows_x, 1), swap(cache_y, 1))
+        rows_x, cache_y, _, packs = self.got
+        return (swap(packs[0], 2), swap(packs[1], 4)), (swap(rows_x, 1), swap(cache_y, 1))
 
     def third(self):
         swap = plane()[3]
@@ -572,8 +574,6 @@
         zero = 0 * me_z
         orders = weight_orders() if tuned else [jnp.zeros((5,), jnp.int32)]
         total, held = absorb([tokens], zero, me_z, cached, total, None, n_z)
-        if tuned:
-            gather = PlaneGather(own_cache, jnp.concatenate(blocks, axis=0))
         from_low, from_high = tokens, tokens
         for s in range(1, n_z):
             low, high = me_z - s, me_z + s
@@ -585,9 +585,13 @@
                 from_high, from_low, held, allowed, orders, here = lax.optimization_barrier(
                     (from_high, from_low, held, allowed, orders, here)
                 )
+                blocks, ready, _, _ = lax.optimization_barrier(
+                    (blocks, own_cache, from_high, from_low)
+                )
+                gather = PlaneGather(ready, jnp.concatenate(blocks, axis=0))
             elif tuned and s == 2:
                 from_high, from_low, held, gather.got = lax.optimization_barrier(
-                    (from_high, from_low, held, gather.first())
+                    (from_high, from_low, held, gather.first(held))
                 )
             elif tuned:
                 packs, swapped = gather.second()

time: 133 us -> 134 us (level)
  waiting for transfers between devices: 34.3 us -> 35.9 us
  transfers between devices with their start and end apart: 27 -> 27, of which waited for: 10 -> 11; matrix products, arithmetic and copies ran while one was open for 9% -> 9% of each run, Pallas kernels for 34% -> 34%
where the time goes in v16:
time: 134 us; the launch traced here: 133 us
  Pallas kernels  46.4 us (35%)
  starting transfers between devices  36.5 us (27%)
  waiting for transfers between devices  35.9 us (27%)
  local copies, waits for them, and re-layouts  7.67 us (6%)
  other arithmetic  5.66 us (4%)
    pallas_call x4, Pallas kernels, absorb(): pl.pallas_call(functools.partial(absorb_kernel, len(chunks)), in_specs=[p...  17 us
    ppermute x15, waiting for transfers between devices, swap(): return lax.ppermute(value, 'dp', [(i, i ^ bit) for i in range(8)])  15.4 us
    ppermute x15, starting transfers between devices, swap(): return lax.ppermute(value, 'dp', [(i, i ^ bit) for i in range(8)])  11.4 us
    ppermute x6, starting transfers between devices, pair(): return lax.ppermute(value, 'tensor', [(z, z ^ s) for z in range(n_z)])  11.4 us
    ppermute x6, waiting for transfers between devices, pair(): return lax.ppermute(value, 'tensor', [(z, z ^ s) for z in range(n_z)])  10.1 us
    ppermute x3, starting transfers between devices, body(): lax.ppermute(from_low, 'tensor', [(z, z + 1) for z in range(s - 1, n_z -...  9.86 us
    pallas_call x1, Pallas kernels, attend(): pl.pallas_call(functools.partial(attend_kernel, len(chunks)), in_specs=[p...  9.73 us
    ppermute x3, waiting for transfers between devices, body(): lax.ppermute(from_high, 'tensor', [(z + 1, z) for z in range(n_z - s)])  9.69 us
  transfers between devices with their start and end apart: 27, of which 11 were waited for; matrix products, arithmetic and copies ran while one was open for 9% of the time, Pallas kernels for 34%

profile of v16, /device:TPU:0, one launch (start us, length us, event | category | flops | bytes accessed | tf_op | source)
XLA Modules:
  0.0 133.1 jit_solution(9669078610275941406)
XLA Ops:
  0.6 1.3 collective-permute-start
  1.9 6.6 %collective-permute-start.1 = (bf16[256,2048]{1,0:T(8,128)(2,1)}, bf16[256,2048]{1,0:T(8,128)(2,1)}, u32[]{:S(2)}, u32[]{:S(2)}) collective-permute-start(bf16[256,2048]{1,0:T(8,128)(2,1)} %refs_0_.1), channel_id=1, source_target_pairs={{0,1},{1,2},{2,3},{4,5},{5,6},{6,7},{8,9},{9,10},{10,11},{12,13},{... | collective-permute-start | bytes 3145736 | tf_op jit(solution)/shard_map/ppermute | solution.py:581
  8.5 1.1 constant_dynamic-slice_fusion
  9.6 1.1 collective-permute-start.4
  10.7 2.0 %collective-permute-start.5 = (bf16[256,256]{1,0:T(8,128)(2,1)S(1)}, bf16[256,256]{1,0:T(8,128)(2,1)S(1)}, u32[]{:S(2)}, u32[]{:S(2)}) collective-permute-start(bf16[256,256]{1,0:T(8,128)(2,1)S(1)} %get-tuple-element.140), channel_id=1, source_target_pairs={{0,2},{1,3},{2,0},{3,1},{4,6},{5,7},{6,4},{7,5},{8,10},{9,11},{10,... | collective-permute-start | bytes 393224 | tf_op jit(solution)/shard_map/ppermute | solution.py:548
  12.7 1.4 %collective-permute-start.6 = (bf16[256,256]{1,0:T(8,128)(2,1)S(1)}, bf16[256,256]{1,0:T(8,128)(2,1)S(1)}, u32[]{:S(2)}, u32[]{:S(2)}) collective-permute-start(bf16[256,256]{1,0:T(8,128)(2,1)S(1)} %get-tuple-element.139), channel_id=1, source_target_pairs={{0,3},{1,2},{2,1},{3,0},{4,7},{5,6},{6,5},{7,4},{8,11},{9,10},{10,... | collective-permute-start | bytes 393224 | tf_op jit(solution)/shard_map/ppermute | solution.py:548
  14.9 4.9 %optimizer.1 = (f32[1024,256]{1,0:T(8,128)}, f32[1024,256]{1,0:T(8,128)}, f32[1024,256]{1,0:T(8,128)}, bf16[1024,256]{1,0:T(8,128)(2,1)}) custom-call(s32[1]{0:T(128)} %bitcast.place, bf16[8192,256]{1,0:T(8,128)(2,1)} %refs_3_.3, f32[1024,256]{1,0:T(8,128)} %master.1, f32[1024,256]{1,0:T(8,128)} %moment.1, f32[1024,256]{1,0:T(8,128)} %second.1, f32[1024,256]{1,0:T(8,128)} %grad.1), custom_call_target="tpu_custom_call" | custom-call | flops 10485760 | bytes 8388608 | tf_op jit(solution)/shard_map/optimizer/pallas_call | solution.py:51
  20.4 0.7 broadcast_in_dim.2.refs_1_
  21.1 4.2 %absorb.4 = (f32[256,256]{1,0:T(8,128)}, bf16[32,2048,256]{2,1,0:T(8,128)(2,1)}) custom-call(s32[3]{0:T(128)} %get-tuple-element.144.place, bf16[256,2048]{1,0:T(8,128)(2,1)} %refs_0_.1, f32[256,256]{1,0:T(8,128)} %broadcast_in_dim.2.refs_1_, bf16[8192,256]{1,0:T(8,128)(2,1)} %refs_3_.3), custom_call_target="tpu_custom_call" | custom-call | flops 268435456 | bytes 3145728 | tf_op jit(solution)/shard_map/absorb/pallas_call | solution.py:140
  25.4 1.4 %constant_dynamic-slice_fusion.3.refs_4_ = bf16[2048,256]{1,0:T(8,128)(2,1)S(1)} fusion(bf16[8192,256]{1,0:T(8,128)(2,1)} %refs_3_.3, s32[]{:T(128)S(6)} %select_n.59), kind=kLoop, calls=%fused_computation.12 | loop fusion | bytes 2097156 | tf_op jit(solution)/shard_map/dynamic_slice | solution.py:566
  26.8 0.8 fusion.1.refs_5_
  27.6 3.1 %collective-permute-done.refs_0_ = bf16[256,2048]{1,0:T(8,128)(2,1)} collective-permute-done((bf16[256,2048]{1,0:T(8,128)(2,1)}, bf16[256,2048]{1,0:T(8,128)(2,1)}, u32[]{:S(2)}, u32[]{:S(2)}) %collective-permute-start) | collective-permute-done | bytes 1048608 | tf_op jit(solution)/shard_map/ppermute | solution.py:580
  30.7 0.7 collective-permute-done.1.refs_0_
  31.4 1.3 collective-permute-start.2
  32.7 1.6 %collective-permute-start.3 = (bf16[256,2048]{1,0:T(8,128)(2,1)}, bf16[256,2048]{1,0:T(8,128)(2,1)}, u32[]{:S(2)}, u32[]{:S(2)}) collective-permute-start(bf16[256,2048]{1,0:T(8,128)(2,1)} %collective-permute-done.1.refs_0_), channel_id=1, source_target_pairs={{1,2},{2,3},{5,6},{6,7},{9,10},{10,11},{13,14},{14,15},{17,18},{18... | collective-permute-start | bytes 3145736 | tf_op jit(solution)/shard_map/ppermute | solution.py:581
  34.3 5.5 %collective-permute-done.5 = bf16[256,256]{1,0:T(8,128)(2,1)S(1)} collective-permute-done((bf16[256,256]{1,0:T(8,128)(2,1)S(1)}, bf16[256,256]{1,0:T(8,128)(2,1)S(1)}, u32[]{:S(2)}, u32[]{:S(2)}) %collective-permute-start.5) | collective-permute-done | bytes 131104 | tf_op jit(solution)/shard_map/ppermute | solution.py:548
  39.8 0.7 constant_dynamic-update-slice_fusion.2
  40.5 1.5 %collective-permute-start.8 = (bf16[1024,256]{1,0:T(8,128)(2,1)S(1)}, bf16[1024,256]{1,0:T(8,128)(2,1)S(1)}, u32[]{:S(2)}, u32[]{:S(2)}) collective-permute-start(bf16[1024,256]{1,0:T(8,128)(2,1)S(1)} %copy-done), channel_id=1, source_target_pairs={{0,16},{4,20},{8,24},{12,28},{16,0},{20,4},{24,8},{28,12},{1,17},{... | collective-permute-start | bytes 1572872 | tf_op jit(solution)/shard_map/ppermute | solution.py:376
  42.0 1.0 pad_maximum_fusion.1
  44.3 1.5 %collective-permute-start.7 = (bf16[768,256]{1,0:T(8,128)(2,1)}, bf16[768,256]{1,0:T(8,128)(2,1)S(1)}, u32[]{:S(2)}, u32[]{:S(2)}) collective-permute-start(bf16[768,256]{1,0:T(8,128)(2,1)} %constant_dynamic-update-slice_fusion.refs_5_), channel_id=1, source_target_pairs={{0,8},{4,12},{8,0},{12,4},{16,24},{20,28},{24,16},{28,20},{1,9},{5... | collective-permute-start | bytes 1179656 | tf_op jit(solution)/shard_map/ppermute | solution.py:376
  46.5 4.2 %absorb.5 = (f32[256,256]{1,0:T(8,128)}, bf16[32,2048,256]{2,1,0:T(8,128)(2,1)}) custom-call(s32[3]{0:T(128)} %get-tuple-element.142.place, bf16[256,2048]{1,0:T(8,128)(2,1)} %collective-permute-done.1.refs_0_, f32[256,256]{1,0:T(8,128)} %get-tuple-element.80.refs_1_, bf16[8192,256]{1,0:T(8,128)(2,1)} %refs_3_.3, ...), custom_call_target="tpu_custom_call", output_to_operand_aliasing={{1}: (4, {})} | custom-call | flops 268435456 | bytes 3145728 | tf_op jit(solution)/shard_map/absorb/pallas_call | solution.py:140
  50.7 4.2 %absorb.6 = (f32[256,256]{1,0:T(8,128)}, bf16[32,2048,256]{2,1,0:T(8,128)(2,1)}) custom-call(s32[3]{0:T(128)} %get-tuple-element.143.place, bf16[256,2048]{1,0:T(8,128)(2,1)} %collective-permute-done.refs_0_, f32[256,256]{1,0:T(8,128)} %get-tuple-element.82.refs_1_, bf16[8192,256]{1,0:T(8,128)(2,1)} %refs_3_.3, ...), custom_call_target="tpu_custom_call", output_to_operand_aliasing={{1}: (4, {})} | custom-call | flops 268435456 | bytes 3145728 | tf_op jit(solution)/shard_map/absorb/pallas_call | solution.py:140
  55.0 1.1 collective-permute-done.7.refs_7_
  56.1 1.0 pad_maximum_fusion
  57.1 0.9 pad_maximum_fusion.2
  58.0 2.1 %collective-permute-done.2.refs_1_ = bf16[256,2048]{1,0:T(8,128)(2,1)} collective-permute-done((bf16[256,2048]{1,0:T(8,128)(2,1)}, bf16[256,2048]{1,0:T(8,128)(2,1)}, u32[]{:S(2)}, u32[]{:S(2)}) %collective-permute-start.2) | collective-permute-done | bytes 1048608 | tf_op jit(solution)/shard_map/ppermute | solution.py:580
  60.2 1.3 collective-permute-start.10
  61.5 1.6 %collective-permute-start.11 = (bf16[256,2048]{1,0:T(8,128)(2,1)}, bf16[256,2048]{1,0:T(8,128)(2,1)}, u32[]{:S(2)}, u32[]{:S(2)}) collective-permute-start(bf16[256,2048]{1,0:T(8,128)(2,1)} %collective-permute-done.3.refs_0_), channel_id=1, source_target_pairs={{2,3},{6,7},{10,11},{14,15},{18,19},{22,23},{26,27},{30,31}} | collective-permute-start | bytes 3145736 | tf_op jit(solution)/shard_map/ppermute | solution.py:581
  63.1 1.4 %collective-permute-start.12 = (bf16[2048,256]{1,0:T(8,128)(2,1)}, bf16[2048,256]{1,0:T(8,128)(2,1)}, u32[]{:S(2)}, u32[]{:S(2)}) collective-permute-start(bf16[2048,256]{1,0:T(8,128)(2,1)} %pad_maximum_fusion), channel_id=1, source_target_pairs={{0,8},{4,12},{8,0},{12,4},{16,24},{20,28},{24,16},{28,20},{1,9},{5... | collective-permute-start | bytes 3145736 | tf_op jit(solution)/shard_map/ppermute | solution.py:376
  64.5 1.5 %collective-permute-start.13 = (bf16[1536,256]{1,0:T(8,128)(2,1)}, bf16[1536,256]{1,0:T(8,128)(2,1)}, u32[]{:S(2)}, u32[]{:S(2)}) collective-permute-start(bf16[1536,256]{1,0:T(8,128)(2,1)} %pad_maximum_fusion.2), channel_id=1, source_target_pairs={{0,16},{4,20},{8,24},{12,28},{16,0},{20,4},{24,8},{28,12},{1,17},{... | collective-permute-start | bytes 2359304 | tf_op jit(solution)/shard_map/ppermute | solution.py:376
  66.4 0.8 copy-done.3
  68.0 4.3 %absorb.7 = (f32[256,256]{1,0:T(8,128)}, bf16[32,2048,256]{2,1,0:T(8,128)(2,1)}) custom-call(s32[3]{0:T(128)} %pad_add_fusion.4.place, bf16[256,2048]{1,0:T(8,128)(2,1)} %collective-permute-done.3.refs_0_, bf16[256,2048]{1,0:T(8,128)(2,1)} %collective-permute-done.2.refs_1_, f32[256,256]{1,0:T(8,128)} %get-tuple-element.94.refs_2_, ...), custom_call_target="tpu_custom_call", output_to_operand_aliasing={{1}: (5, {})} | custom-call | flops 268435456 | bytes 3145728 | tf_op jit(solution)/shard_map/absorb/pallas_call | solution.py:140
  72.3 1.9 %place_rows.2.refs_2_ = bf16[8192,256]{1,0:T(8,128)(2,1)} custom-call(s32[4]{0:T(128)S(1)} %broadcast_xor_fusion.2.place, bf16[1024,256]{1,0:T(8,128)(2,1)S(1)} %copy-done, bf16[1792,256]{1,0:T(8,128)(2,1)S(1)} %collective-permute-done.9.refs_1_.refs_6_, bf16[1024,256]{1,0:T(8,128)(2,1)S(1)} %collective-permute-done.8.refs_2_, bf16[1024,256]{1,0:T(8,128)(2,1)S(1)} %copy-done.4), custom_call_target="tpu_custom_call" | custom-call | bytes 4194304 | tf_op jit(solution)/shard_map/place_rows/pallas_call | solution.py:495
  74.2 10.6 %collective-permute-done.13.refs_9_ = bf16[1536,256]{1,0:T(8,128)(2,1)} collective-permute-done((bf16[1536,256]{1,0:T(8,128)(2,1)}, bf16[1536,256]{1,0:T(8,128)(2,1)}, u32[]{:S(2)}, u32[]{:S(2)}) %collective-permute-start.13) | collective-permute-done | bytes 786464 | tf_op jit(solution)/shard_map/ppermute | solution.py:376
  84.8 4.5 %collective-permute-done.10.refs_1_ = bf16[256,2048]{1,0:T(8,128)(2,1)} collective-permute-done((bf16[256,2048]{1,0:T(8,128)(2,1)}, bf16[256,2048]{1,0:T(8,128)(2,1)}, u32[]{:S(2)}, u32[]{:S(2)}) %collective-permute-start.10) | collective-permute-done | bytes 1048608 | tf_op jit(solution)/shard_map/ppermute | solution.py:580
  89.8 9.7 %attend.1 = (bf16[32,2048,256]{2,1,0:T(8,128)(2,1)}, bf16[256,1024]{1,0:T(8,128)(2,1)}, bf16[256,256]{1,0:T(8,128)(2,1)}, bf16[4,1024,128]{2,1,0:T(8,128)(2,1)}, bf16[4,1024,128]{2,1,0:T(8,128)(2,1)}) custom-call(s32[3]{0:T(128)} %get-tuple-element.145.place, s32[5]{0:T(128)} %stack.98.order, ...), custom_call_target="tpu_custom_call", output_to_operand_aliasing={{0}: (6, {})} | custom-call | flops 805306368 | bytes 2097152 | tf_op jit(solution)/shard_map/attend/pallas_call | solution.py:235
  100.1 0.9 copy-done.1
  101.0 2.5 %weight_send.1 = (f32[2,1024,128]{2,1,0:T(8,128)S(1)}, f32[2,1024,128]{2,1,0:T(8,128)S(1)}) custom-call(s32[5]{0:T(128)S(1)} %stack.100.place, bf16[32,2048,256]{2,1,0:T(8,128)(2,1)} %get-tuple-element.109.held, bf16[256,256]{1,0:T(8,128)(2,1)S(1)} %copy-done.1), custom_call_target="tpu_custom_call" | custom-call | flops 268435456 | bytes 2097152 | tf_op jit(solution)/shard_map/weight_send/pallas_call | solution.py:334
  103.7 1.5 %collective-permute-start.22 = (bf16[2,1024,128]{2,1,0:T(8,128)(2,1)S(1)}, bf16[2,1024,128]{2,1,0:T(8,128)(2,1)S(1)}, u32[]{:S(2)}, u32[]{:S(2)}) collective-permute-start(bf16[2,1024,128]{2,1,0:T(8,128)(2,1)S(1)} %get-tuple-element.116), channel_id=1, source_target_pairs={{0,8},{4,12},{8,0},{12,4},{16,24},{20,28},{24,16},{28,20},{1,9},{5... | collective-permute-start | bytes 1572872 | tf_op jit(solution)/shard_map/ppermute | solution.py:376
  105.2 1.5 %collective-permute-start.23 = (bf16[2,1024,128]{2,1,0:T(8,128)(2,1)S(1)}, bf16[2,1024,128]{2,1,0:T(8,128)(2,1)S(1)}, u32[]{:S(2)}, u32[]{:S(2)}) collective-permute-start(bf16[2,1024,128]{2,1,0:T(8,128)(2,1)S(1)} %get-tuple-element.117), channel_id=1, source_target_pairs={{0,16},{4,20},{8,24},{12,28},{16,0},{20,4},{24,8},{28,12},{1,17},{... | collective-permute-start | bytes 1572872 | tf_op jit(solution)/shard_map/ppermute | solution.py:376
  106.7 5.0 %collective-permute-start.16 = (bf16[256,256]{1,0:T(8,128)(2,1)S(1)}, bf16[256,256]{1,0:T(8,128)(2,1)S(1)}, u32[]{:S(2)}, u32[]{:S(2)}) collective-permute-start(bf16[256,256]{1,0:T(8,128)(2,1)S(1)} %copy-done.2), channel_id=1, source_target_pairs={{0,3},{1,2},{2,1},{3,0},{4,7},{5,6},{6,5},{7,4},{8,11},{9,10},{10,... | collective-permute-start | bytes 393224 | tf_op jit(solution)/shard_map/ppermute | solution.py:548
  111.8 1.3 collective-permute-start.17
  113.6 2.6 %place_rows.3 = bf16[8192,256]{1,0:T(8,128)(2,1)} custom-call(s32[4]{0:T(128)S(1)} %broadcast_xor_fusion.1.place, bf16[2048,256]{1,0:T(8,128)(2,1)} %collective-permute-done.12.refs_0_, bf16[2048,256]{1,0:T(8,128)(2,1)S(1)} %collective-permute-done.19.refs_1_, bf16[8192,256]{1,0:T(8,128)(2,1)} %place_rows.2.refs_2_), custom_call_target="tpu_custom_call", output_to_operand_aliasing={{}: (3, {})} | custom-call | bytes 4194304 | tf_op jit(solution)/shard_map/place_rows/pallas_call | solution.py:495
  116.2 2.5 %weight_keep.1 = (f32[2,1024,128]{2,1,0:T(8,128)S(1)}, f32[2,1024,128]{2,1,0:T(8,128)S(1)}) custom-call(s32[5]{0:T(128)S(1)} %stack.100.place, bf16[32,2048,256]{2,1,0:T(8,128)(2,1)} %get-tuple-element.109.held, bf16[256,256]{1,0:T(8,128)(2,1)S(1)} %copy-done.2, bf16[4,1024,128]{2,1,0:T(8,128)(2,1)S(1)} %collective-permute-done.24.refs_0_), custom_call_target="tpu_custom_call" | custom-call | flops 268435456 | bytes 2097152 | tf_op jit(solution)/shard_map/weight_keep/pallas_call | solution.py:334
  118.7 4.6 %collective-permute-done.17.refs_2_ = bf16[256,256]{1,0:T(8,128)(2,1)S(1)} collective-permute-done((bf16[256,256]{1,0:T(8,128)(2,1)S(1)}, bf16[256,256]{1,0:T(8,128)(2,1)S(1)}, u32[]{:S(2)}, u32[]{:S(2)}) %collective-permute-start.17) | collective-permute-done | bytes 131104 | tf_op jit(solution)/shard_map/ppermute | solution.py:548
  124.7 3.9 %input_gradient.1 = bf16[256,2048]{1,0:T(8,128)(2,1)} custom-call(s32[8]{0:T(128)S(1)} %broadcast_xor_fusion.place, bf16[256,256]{1,0:T(8,128)(2,1)S(1)} %copy-done.2, bf16[256,256]{1,0:T(8,128)(2,1)S(1)} %collective-permute-done.18.refs_1_, bf16[256,256]{1,0:T(8,128)(2,1)S(1)} %collective-permute-done.17.refs_2_, ...), custom_call_target="tpu_custom_call" | custom-call | flops 1073741824 | bytes 6291456 | tf_op jit(solution)/shard_map/input_gradient/pallas_call | solution.py:73
  128.7 3.1 %collective-permute-done.25.last_a = bf16[1024,128]{1,0:T(8,128)(2,1)S(1)} collective-permute-done((bf16[1024,128]{1,0:T(8,128)(2,1)S(1)}, bf16[1024,128]{1,0:T(8,128)(2,1)S(1)}, u32[]{:S(2)}, u32[]{:S(2)}) %collective-permute-start.25) | collective-permute-done | bytes 262176 | tf_op jit(solution)/shard_map/ppermute | solution.py:376
  132.0 1.1 weight_finish.1
  (64 shorter events, 8.0 us)
Async XLA Ops:
  0.6 30.0 %collective-permute-start = (bf16[256,2048]{1,0:T(8,128)(2,1)}, bf16[256,2048]{1,0:T(8,128)(2,1)}, u32[]{:S(2)}, u32[]{:S(2)}) collective-permute-start(bf16[256,2048]{1,0:T(8,128)(2,1)} %refs_0_.1), channel_id=1, source_target_pairs={{1,0},{2,1},{3,2},{5,4},{6,5},{7,6},{9,8},{10,9},{11,10},{13,12},{... | collective-permute-start | bytes 3145736 | tf_op jit(solution)/shard_map/ppermute | solution.py:580
  1.9 29.4 %collective-permute-start.1 = (bf16[256,2048]{1,0:T(8,128)(2,1)}, bf16[256,2048]{1,0:T(8,128)(2,1)}, u32[]{:S(2)}, u32[]{:S(2)}) collective-permute-start(bf16[256,2048]{1,0:T(8,128)(2,1)} %refs_0_.1), channel_id=1, source_target_pairs={{0,1},{1,2},{2,3},{4,5},{5,6},{6,7},{8,9},{9,10},{10,11},{12,13},{... | collective-permute-start | bytes 3145736 | tf_op jit(solution)/shard_map/ppermute | solution.py:581
  9.6 24.7 %collective-permute-start.4 = (bf16[256,256]{1,0:T(8,128)(2,1)S(1)}, bf16[256,256]{1,0:T(8,128)(2,1)S(1)}, u32[]{:S(2)}, u32[]{:S(2)}) collective-permute-start(bf16[256,256]{1,0:T(8,128)(2,1)S(1)} %get-tuple-element.141), channel_id=1, source_target_pairs={{0,1},{1,0},{2,3},{3,2},{4,5},{5,4},{6,7},{7,6},{8,9},{9,8},{10,11... | collective-permute-start | bytes 393224 | tf_op jit(solution)/shard_map/ppermute | solution.py:548
  10.7 29.1 %collective-permute-start.5 = (bf16[256,256]{1,0:T(8,128)(2,1)S(1)}, bf16[256,256]{1,0:T(8,128)(2,1)S(1)}, u32[]{:S(2)}, u32[]{:S(2)}) collective-permute-start(bf16[256,256]{1,0:T(8,128)(2,1)S(1)} %get-tuple-element.140), channel_id=1, source_target_pairs={{0,2},{1,3},{2,0},{3,1},{4,6},{5,7},{6,4},{7,5},{8,10},{9,11},{10,... | collective-permute-start | bytes 393224 | tf_op jit(solution)/shard_map/ppermute | solution.py:548
  12.7 27.0 %collective-permute-start.6 = (bf16[256,256]{1,0:T(8,128)(2,1)S(1)}, bf16[256,256]{1,0:T(8,128)(2,1)S(1)}, u32[]{:S(2)}, u32[]{:S(2)}) collective-permute-start(bf16[256,256]{1,0:T(8,128)(2,1)S(1)} %get-tuple-element.139), channel_id=1, source_target_pairs={{0,3},{1,2},{2,1},{3,0},{4,7},{5,6},{6,5},{7,4},{8,11},{9,10},{10,... | collective-permute-start | bytes 393224 | tf_op jit(solution)/shard_map/ppermute | solution.py:548
  25.4 1.4 %copy-start.9 = (s32[1,256]{1,0:T(1,128)S(1)}, s32[1,256]{1,0:T(1,128)}, u32[]{:S(2)}) copy-start(s32[1,256]{1,0:T(1,128)} %param.15) | copy-start | bytes 3076
  25.4 15.1 %copy-start = (bf16[1024,256]{1,0:T(8,128)(2,1)S(1)}, bf16[1024,256]{1,0:T(8,128)(2,1)}, u32[]{:S(2)}) copy-start(bf16[1024,256]{1,0:T(8,128)(2,1)} %get-tuple-element.89.refs_0_) | copy-start | bytes 1572868
  31.4 28.8 %collective-permute-start.2 = (bf16[256,2048]{1,0:T(8,128)(2,1)}, bf16[256,2048]{1,0:T(8,128)(2,1)}, u32[]{:S(2)}, u32[]{:S(2)}) collective-permute-start(bf16[256,2048]{1,0:T(8,128)(2,1)} %collective-permute-done.refs_0_), channel_id=1, source_target_pairs={{1,0},{2,1},{5,4},{6,5},{9,8},{10,9},{13,12},{14,13},{17,16},{18,1... | collective-permute-start | bytes 3145736 | tf_op jit(solution)/shard_map/ppermute | solution.py:580
  32.7 27.5 %collective-permute-start.3 = (bf16[256,2048]{1,0:T(8,128)(2,1)}, bf16[256,2048]{1,0:T(8,128)(2,1)}, u32[]{:S(2)}, u32[]{:S(2)}) collective-permute-start(bf16[256,2048]{1,0:T(8,128)(2,1)} %collective-permute-done.1.refs_0_), channel_id=1, source_target_pairs={{1,2},{2,3},{5,6},{6,7},{9,10},{10,11},{13,14},{14,15},{17,18},{18... | collective-permute-start | bytes 3145736 | tf_op jit(solution)/shard_map/ppermute | solution.py:581
  39.8 3.2 %copy-start.5 = (bf16[256,256]{1,0:T(8,128)(2,1)}, bf16[256,256]{1,0:T(8,128)(2,1)S(1)}, u32[]{:S(2)}) copy-start(bf16[256,256]{1,0:T(8,128)(2,1)S(1)} %collective-permute-done.5) | copy-start | bytes 393220
  39.8 3.9 %copy-start.7 = (bf16[256,256]{1,0:T(8,128)(2,1)}, bf16[256,256]{1,0:T(8,128)(2,1)S(1)}, u32[]{:S(2)}) copy-start(bf16[256,256]{1,0:T(8,128)(2,1)S(1)} %collective-permute-done.6) | copy-start | bytes 393220
  40.5 15.6 %collective-permute-start.8 = (bf16[1024,256]{1,0:T(8,128)(2,1)S(1)}, bf16[1024,256]{1,0:T(8,128)(2,1)S(1)}, u32[]{:S(2)}, u32[]{:S(2)}) collective-permute-start(bf16[1024,256]{1,0:T(8,128)(2,1)S(1)} %copy-done), channel_id=1, source_target_pairs={{0,16},{4,20},{8,24},{12,28},{16,0},{20,4},{24,8},{28,12},{1,17},{... | collective-permute-start | bytes 1572872 | tf_op jit(solution)/shard_map/ppermute | solution.py:376
  43.6 14.4 %collective-permute-start.9 = (bf16[1792,256]{1,0:T(8,128)(2,1)}, bf16[1792,256]{1,0:T(8,128)(2,1)S(1)}, u32[]{:S(2)}, u32[]{:S(2)}) collective-permute-start(bf16[1792,256]{1,0:T(8,128)(2,1)} %pad_maximum_fusion.1), channel_id=1, source_target_pairs={{0,4},{4,0},{8,12},{12,8},{16,20},{20,16},{24,28},{28,24},{1,5},{5... | collective-permute-start | bytes 2752520 | tf_op jit(solution)/shard_map/ppermute | solution.py:376
  44.3 11.7 %collective-permute-start.7 = (bf16[768,256]{1,0:T(8,128)(2,1)}, bf16[768,256]{1,0:T(8,128)(2,1)S(1)}, u32[]{:S(2)}, u32[]{:S(2)}) collective-permute-start(bf16[768,256]{1,0:T(8,128)(2,1)} %constant_dynamic-update-slice_fusion.refs_5_), channel_id=1, source_target_pairs={{0,8},{4,12},{8,0},{12,4},{16,24},{20,28},{24,16},{28,20},{1,9},{5... | collective-permute-start | bytes 1179656 | tf_op jit(solution)/shard_map/ppermute | solution.py:376
  54.9 2.2 %copy-start.6 = (bf16[256,256]{1,0:T(8,128)(2,1)S(1)}, bf16[256,256]{1,0:T(8,128)(2,1)}, u32[]{:S(2)}) copy-start(bf16[256,256]{1,0:T(8,128)(2,1)} %copy-done.5) | copy-start | bytes 393220
  55.0 2.2 %copy-start.8 = (bf16[256,256]{1,0:T(8,128)(2,1)S(1)}, bf16[256,256]{1,0:T(8,128)(2,1)}, u32[]{:S(2)}) copy-start(bf16[256,256]{1,0:T(8,128)(2,1)} %copy-done.7) | copy-start | bytes 393220
  56.1 11.9 %copy-start.12 = (s32[4]{0:T(128)S(1)}, s32[4]{0:T(128)}, u32[]{:S(2)}) copy-start(s32[4]{0:T(128)} %constant.72.clone) | copy-start | bytes 52
  60.2 29.1 %collective-permute-start.10 = (bf16[256,2048]{1,0:T(8,128)(2,1)}, bf16[256,2048]{1,0:T(8,128)(2,1)}, u32[]{:S(2)}, u32[]{:S(2)}) collective-permute-start(bf16[256,2048]{1,0:T(8,128)(2,1)} %collective-permute-done.2.refs_1_), channel_id=1, source_target_pairs={{1,0},{5,4},{9,8},{13,12},{17,16},{21,20},{25,24},{29,28}} | collective-permute-start | bytes 3145736 | tf_op jit(solution)/shard_map/ppermute | solution.py:580
  61.5 27.8 %collective-permute-start.11 = (bf16[256,2048]{1,0:T(8,128)(2,1)}, bf16[256,2048]{1,0:T(8,128)(2,1)}, u32[]{:S(2)}, u32[]{:S(2)}) collective-permute-start(bf16[256,2048]{1,0:T(8,128)(2,1)} %collective-permute-done.3.refs_0_), channel_id=1, source_target_pairs={{2,3},{6,7},{10,11},{14,15},{18,19},{22,23},{26,27},{30,31}} | collective-permute-start | bytes 3145736 | tf_op jit(solution)/shard_map/ppermute | solution.py:581
  63.1 26.1 %collective-permute-start.12 = (bf16[2048,256]{1,0:T(8,128)(2,1)}, bf16[2048,256]{1,0:T(8,128)(2,1)}, u32[]{:S(2)}, u32[]{:S(2)}) collective-permute-start(bf16[2048,256]{1,0:T(8,128)(2,1)} %pad_maximum_fusion), channel_id=1, source_target_pairs={{0,8},{4,12},{8,0},{12,4},{16,24},{20,28},{24,16},{28,20},{1,9},{5... | collective-permute-start | bytes 3145736 | tf_op jit(solution)/shard_map/ppermute | solution.py:376
  64.5 1.9 %collective-permute-start.15 = (bf16[1024,256]{1,0:T(8,128)(2,1)S(1)}, bf16[1024,256]{1,0:T(8,128)(2,1)S(1)}, u32[]{:S(2)}, u32[]{:S(2)}) collective-permute-start(bf16[1024,256]{1,0:T(8,128)(2,1)S(1)} %collective-permute-done.8.refs_2_), channel_id=1, source_target_pairs={{0,4},{4,0},{8,12},{12,8},{16,20},{20,16},{24,28},{28,24},{1,5},{5... | collective-permute-start | bytes 1572872 | tf_op jit(solution)/shard_map/ppermute | solution.py:376
  64.5 20.3 %collective-permute-start.13 = (bf16[1536,256]{1,0:T(8,128)(2,1)}, bf16[1536,256]{1,0:T(8,128)(2,1)}, u32[]{:S(2)}, u32[]{:S(2)}) collective-permute-start(bf16[1536,256]{1,0:T(8,128)(2,1)} %pad_maximum_fusion.2), channel_id=1, source_target_pairs={{0,16},{4,20},{8,24},{12,28},{16,0},{20,4},{24,8},{28,12},{1,17},{... | collective-permute-start | bytes 2359304 | tf_op jit(solution)/shard_map/ppermute | solution.py:376
  66.4 0.8 copy-start.3
  67.2 7.0 %collective-permute-start.14 = (bf16[768,256]{1,0:T(8,128)(2,1)S(1)}, bf16[768,256]{1,0:T(8,128)(2,1)}, u32[]{:S(2)}, u32[]{:S(2)}) collective-permute-start(bf16[768,256]{1,0:T(8,128)(2,1)S(1)} %collective-permute-done.7.refs_7_), channel_id=1, source_target_pairs={{0,4},{4,0},{8,12},{12,8},{16,20},{20,16},{24,28},{28,24},{1,5},{5... | collective-permute-start | bytes 1179656 | tf_op jit(solution)/shard_map/ppermute | solution.py:376
  68.0 4.3 %copy-start.4 = (bf16[1024,256]{1,0:T(8,128)(2,1)S(1)}, bf16[1024,256]{1,0:T(8,128)(2,1)}, u32[]{:S(2)}) copy-start(bf16[1024,256]{1,0:T(8,128)(2,1)} %copy-done.3) | copy-start | bytes 1572868
  89.3 10.3 %collective-permute-start.19 = (bf16[2048,256]{1,0:T(8,128)(2,1)}, bf16[2048,256]{1,0:T(8,128)(2,1)S(1)}, u32[]{:S(2)}, u32[]{:S(2)}) collective-permute-start(bf16[2048,256]{1,0:T(8,128)(2,1)} %collective-permute-done.12.refs_0_), channel_id=1, source_target_pairs={{0,4},{4,0},{8,12},{12,8},{16,20},{20,16},{24,28},{28,24},{1,5},{5... | collective-permute-start | bytes 3145736 | tf_op jit(solution)/shard_map/ppermute | solution.py:376
  89.3 10.2 %collective-permute-start.20 = (bf16[1536,256]{1,0:T(8,128)(2,1)}, bf16[1536,256]{1,0:T(8,128)(2,1)}, u32[]{:S(2)}, u32[]{:S(2)}) collective-permute-start(bf16[1536,256]{1,0:T(8,128)(2,1)} %collective-permute-done.13.refs_9_), channel_id=1, source_target_pairs={{0,4},{4,0},{8,12},{12,8},{16,20},{20,16},{24,28},{28,24},{1,5},{5... | collective-permute-start | bytes 2359304 | tf_op jit(solution)/shard_map/ppermute | solution.py:376
  99.5 4.0 %collective-permute-start.21 = (bf16[4,1024,128]{2,1,0:T(8,128)(2,1)}, bf16[4,1024,128]{2,1,0:T(8,128)(2,1)S(1)}, u32[]{:S(2)}, u32[]{:S(2)}) collective-permute-start(bf16[4,1024,128]{2,1,0:T(8,128)(2,1)} %get-tuple-element.115), channel_id=1, source_target_pairs={{0,4},{4,0},{8,12},{12,8},{16,20},{20,16},{24,28},{28,24},{1,5},{5... | collective-permute-start | bytes 3145736 | tf_op jit(solution)/shard_map/ppermute | solution.py:376
  99.7 13.4 %collective-permute-start.24 = (bf16[4,1024,128]{2,1,0:T(8,128)(2,1)}, bf16[4,1024,128]{2,1,0:T(8,128)(2,1)S(1)}, u32[]{:S(2)}, u32[]{:S(2)}) collective-permute-start(bf16[4,1024,128]{2,1,0:T(8,128)(2,1)} %get-tuple-element.121), channel_id=1, source_target_pairs={{0,4},{4,0},{8,12},{12,8},{16,20},{20,16},{24,28},{28,24},{1,5},{5... | collective-permute-start | bytes 3145736 | tf_op jit(solution)/shard_map/ppermute | solution.py:376
  100.1 0.9 copy-start.1
  103.5 3.2 %copy-start.2 = (bf16[256,256]{1,0:T(8,128)(2,1)S(1)}, bf16[256,256]{1,0:T(8,128)(2,1)}, u32[]{:S(2)}) copy-start(bf16[256,256]{1,0:T(8,128)(2,1)} %get-tuple-element.128.d_projected.refs_0_) | copy-start | bytes 393220
  103.5 10.1 %copy-start.11 = (s32[4]{0:T(128)S(1)}, s32[4]{0:T(128)}, u32[]{:S(2)}) copy-start(s32[4]{0:T(128)} %constant.73.clone) | copy-start | bytes 52
  103.7 19.7 %collective-permute-start.22 = (bf16[2,1024,128]{2,1,0:T(8,128)(2,1)S(1)}, bf16[2,1024,128]{2,1,0:T(8,128)(2,1)S(1)}, u32[]{:S(2)}, u32[]{:S(2)}) collective-permute-start(bf16[2,1024,128]{2,1,0:T(8,128)(2,1)S(1)} %get-tuple-element.116), channel_id=1, source_target_pairs={{0,8},{4,12},{8,0},{12,4},{16,24},{20,28},{24,16},{28,20},{1,9},{5... | collective-permute-start | bytes 1572872 | tf_op jit(solution)/shard_map/ppermute | solution.py:376
  105.2 18.2 %collective-permute-start.23 = (bf16[2,1024,128]{2,1,0:T(8,128)(2,1)S(1)}, bf16[2,1024,128]{2,1,0:T(8,128)(2,1)S(1)}, u32[]{:S(2)}, u32[]{:S(2)}) collective-permute-start(bf16[2,1024,128]{2,1,0:T(8,128)(2,1)S(1)} %get-tuple-element.117), channel_id=1, source_target_pairs={{0,16},{4,20},{8,24},{12,28},{16,0},{20,4},{24,8},{28,12},{1,17},{... | collective-permute-start | bytes 1572872 | tf_op jit(solution)/shard_map/ppermute | solution.py:376
  106.7 12.0 %collective-permute-start.16 = (bf16[256,256]{1,0:T(8,128)(2,1)S(1)}, bf16[256,256]{1,0:T(8,128)(2,1)S(1)}, u32[]{:S(2)}, u32[]{:S(2)}) collective-permute-start(bf16[256,256]{1,0:T(8,128)(2,1)S(1)} %copy-done.2), channel_id=1, source_target_pairs={{0,3},{1,2},{2,1},{3,0},{4,7},{5,6},{6,5},{7,4},{8,11},{9,10},{10,... | collective-permute-start | bytes 393224 | tf_op jit(solution)/shard_map/ppermute | solution.py:548
  111.8 11.6 %collective-permute-start.17 = (bf16[256,256]{1,0:T(8,128)(2,1)S(1)}, bf16[256,256]{1,0:T(8,128)(2,1)S(1)}, u32[]{:S(2)}, u32[]{:S(2)}) collective-permute-start(bf16[256,256]{1,0:T(8,128)(2,1)S(1)} %copy-done.2), channel_id=1, source_target_pairs={{0,2},{1,3},{2,0},{3,1},{4,6},{5,7},{6,4},{7,5},{8,10},{9,11},{10,... | collective-permute-start | bytes 393224 | tf_op jit(solution)/shard_map/ppermute | solution.py:548
  113.0 10.3 %collective-permute-start.18 = (bf16[256,256]{1,0:T(8,128)(2,1)S(1)}, bf16[256,256]{1,0:T(8,128)(2,1)S(1)}, u32[]{:S(2)}, u32[]{:S(2)}) collective-permute-start(bf16[256,256]{1,0:T(8,128)(2,1)S(1)} %copy-done.2), channel_id=1, source_target_pairs={{0,1},{1,0},{2,3},{3,2},{4,5},{5,4},{6,7},{7,6},{8,9},{9,8},{10,11... | collective-permute-start | bytes 393224 | tf_op jit(solution)/shard_map/ppermute | solution.py:548
  118.7 6.0 %copy-start.10 = (s32[8]{0:T(128)S(1)}, s32[8]{0:T(128)}, u32[]{:S(2)}) copy-start(s32[8]{0:T(128)} %constant.74.clone) | copy-start | bytes 100
  123.5 8.3 %collective-permute-start.25 = (bf16[1024,128]{1,0:T(8,128)(2,1)S(1)}, bf16[1024,128]{1,0:T(8,128)(2,1)S(1)}, u32[]{:S(2)}, u32[]{:S(2)}) collective-permute-start(bf16[1024,128]{1,0:T(8,128)(2,1)S(1)} %get-tuple-element.126), channel_id=1, source_target_pairs={{0,16},{4,20},{8,24},{12,28},{16,0},{20,4},{24,8},{28,12},{1,17},{... | collective-permute-start | bytes 786440 | tf_op jit(solution)/shard_map/ppermute | solution.py:376
  124.1 7.9 %collective-permute-start.26 = (bf16[1024,128]{1,0:T(8,128)(2,1)S(1)}, bf16[1024,128]{1,0:T(8,128)(2,1)S(1)}, u32[]{:S(2)}, u32[]{:S(2)}) collective-permute-start(bf16[1024,128]{1,0:T(8,128)(2,1)S(1)} %get-tuple-element.127), channel_id=1, source_target_pairs={{0,8},{4,12},{8,0},{12,4},{16,24},{20,28},{24,16},{28,20},{1,9},{5... | collective-permute-start | bytes 786440 | tf_op jit(solution)/shard_map/ppermute | solution.py:376

commit v17 on v16

--- a/solution.py
+++ b/solution.py
@@ -225,7 +225,17 @@
         out = (sent, kept)[g]
         out[2 * side + position, here, :] = part.astype(out.dtype)
 
+    save = None
+    if held.shape[2] == d_projected.shape[1]:
+        save = pltpu.make_async_copy(
+            d_projected,
+            held.at[held.shape[0] - 1, pl.ds(0, d_projected.shape[0]), :],
+            sems.at[2],
+        )
+        save.start()
     weight_products(copies, (SENT, KEPT), buffer, d_projected, give)
+    if save is not None:
+        save.wait()
 
 
 def attend(chunks, which, index, cached, total, held, queries, d_out, allowed, order, n_chunks):
@@ -277,6 +287,13 @@
 KEPT = ((1, 1, 0), (2, 0, 0), (3, 0, 1), (3, 1, 1))
 
 
+def fetch_columns(held, columns, sem):
+    length = columns.shape[0]
+    return pltpu.make_async_copy(
+        held.at[held.shape[0] - 1, pl.ds(0, length), :], columns, sem
+    )
+
+
 def fetch_parts(place, held, chunks, buffer, sems):
     rows = buffer.shape[1]
     start = pl.multiple_of(place[4] * rows, rows)
@@ -314,9 +331,12 @@
                 give(g, side, position, here, part)
 
 
-def weight_kernel(group, place, held, d_projected, *refs):
-    *added, out_a, out_b, buffer, sems = refs
+def weight_kernel(group, place, held, *refs):
+    *added, out_a, out_b, buffer, columns, sems, sem = refs
+    columns_copy = fetch_columns(held, columns, sem)
+    columns_copy.start()
     copies = fetch_parts(place, held, sorted({part[0] for part in group}), buffer, sems)
+    columns_copy.wait()
 
     def give(_, side, position, here, part):
         if added:
@@ -324,29 +344,31 @@
         out = (out_a, out_b)[side]
         out[position, here, :] = part.astype(out.dtype)
 
-    weight_products(copies, (group,), buffer, d_projected, give)
-
-
-def weight_parts(held, d_projected, place, group, added, dtype, name):
-    length, cols = d_projected.shape
+    weight_products(copies, (group,), buffer, columns, give)
+
+
+def weight_parts(held, place, group, added, dtype, name):
+    length = cols = held.shape[2]
     rows = held.shape[1] // 2
     vmem = pl.BlockSpec(memory_space=pltpu.VMEM)
     return pl.pallas_call(
         functools.partial(weight_kernel, group),
         in_specs=[pl.BlockSpec(memory_space=pltpu.SMEM), pl.BlockSpec(memory_space=pl.ANY)]
-        + [vmem] * (1 + len(added)),
+        + [vmem] * len(added),
         out_specs=[vmem] * 2,
         out_shape=[jax.ShapeDtypeStruct((2, rows, cols // 2), dtype)] * 2,
         scratch_shapes=[
             pltpu.VMEM((4, rows, length), held.dtype),
+            pltpu.VMEM((length, cols), held.dtype),
             pltpu.SemaphoreType.DMA((4,)),
+            pltpu.SemaphoreType.DMA,
         ],
         cost_estimate=pl.CostEstimate(
             flops=4 * length * rows * cols, bytes_accessed=8 * rows * cols, transcendentals=0
         ),
         compiler_params=pltpu.CompilerParams(vmem_limit_bytes=VMEM_WHOLE),
         name=name,
-    )(place, held, d_projected, *added)
+    )(place, held, *added)
 
 
 def add_kernel(place, own_a, own_b, other, out_a, out_b):
@@ -384,22 +406,21 @@
     return [jnp.stack(chunks + [half]) for half in (1 - core, core)]
 
 
-def weight_sum(held, d_projected, order, sent, kept, pieces, beside):
+def weight_sum(held, order, sent, kept, pieces, beside):
     swap = plane()[3]
-    rows, cols = held.shape[1] // 2, d_projected.shape[1]
+    rows, cols = held.shape[1] // 2, held.shape[2]
     none = jnp.zeros((1,), jnp.int32)
     sent, kept = swap(sent, 1), swap(kept, 1)
-    own = weight_parts(held, d_projected, order, SENT, [], jnp.float32, "weight_send")
+    own = weight_parts(held, order, SENT, [], jnp.float32, "weight_send")
     shape = jax.ShapeDtypeStruct(own[0].shape, jnp.bfloat16)
     send_a, send_b = on_chip(
         add_kernel, none, list(own) + [sent], [shape] * 2, 2 * cols * rows, "weight_add"
     )
     got_a, got_b = swap(send_a, 2), swap(send_b, 4)
     keep_a, keep_b = weight_parts(
-        held, d_projected, order, KEPT, [kept], jnp.float32, "weight_keep"
-    )
-    pieces, got_a, got_b, beside = lax.optimization_barrier((pieces[::-1], got_a, got_b, beside))
-    pieces = pieces[::-1]
+        held, order, KEPT, [kept], jnp.float32, "weight_keep"
+    )
+    got_a, got_b, pieces, beside = lax.optimization_barrier((got_a, got_b, pieces, beside))
 
     small = jax.ShapeDtypeStruct((rows, cols // 2), jnp.bfloat16)
     arrays = [keep_a, got_a, keep_b, got_b]
@@ -542,7 +563,7 @@
 
 
 def make_body(n_dp, n_z):
-    tuned = n_dp == 8 and n_z == 4
+    mesh_tuned = n_dp == 8 and n_z == 4
 
     def pair(value, s):
         return lax.ppermute(value, "tensor", [(z, z ^ s) for z in range(n_z)])
@@ -552,6 +573,7 @@
         me_z = lax.axis_index("tensor").astype(jnp.int32)
         length, feats = tokens.shape
         cols = cached.shape[1]
+        tuned = mesh_tuned and length == cols
 
         master_new, moment_new, second_new, own_cache = optimizer(
             cached, master, moment, second, grad
@@ -611,13 +633,12 @@
             chunks, which, index, cached, total, held, queries, d_out, allowed, orders[0], n_z
         )
 
-        pieces = [pair(d_projected, s) for s in range(n_z - 1, 0, -1)]
-        pieces = [d_projected] + pieces[::-1]
+        pieces = [d_projected] + [pair(d_projected, s) for s in range(1, n_z)]
         if tuned:
             sent, gather.packs_other = lax.optimization_barrier((sent, gather.third()))
             new_cache = gather.lay_rest(laid)
             finish, pieces, new_cache = weight_sum(
-                held, d_projected, orders[1], sent, kept, pieces, new_cache
+                held, orders[1], sent, kept, pieces, new_cache
             )
             new_grad, d_tokens = finish(input_gradient(pieces, here, *gather.feature_rows()))
         else:

time: 134 us -> 132 us (0.985)
  waiting for transfers between devices: 35.9 us -> 33.7 us
    ppermute x15, waiting for transfers between devices: 15.4 us -> 14 us  [swap(): return lax.ppermute(value, 'dp', [(i, i ^ bit) for i in range(8)])]
    unnamed x28 -> x26, local copies, waits for them, and re-layouts: 3.11 us -> 2.2 us
  transfers between devices with their start and end apart: 27 -> 27, of which waited for: 11 -> 11; matrix products, arithmetic and copies ran while one was open for 9% -> 9% of each run, Pallas kernels for 34% -> 35%
where the time goes in v17:
time: 132 us; the launch traced here: 131 us
  Pallas kernels  47.1 us (36%)
  starting transfers between devices  37.3 us (28%)
  waiting for transfers between devices  33.7 us (26%)
  local copies, waits for them, and re-layouts  6.68 us (5%)
  other arithmetic  5.69 us (4%)
    pallas_call x4, Pallas kernels, absorb(): pl.pallas_call(functools.partial(absorb_kernel, len(chunks)), in_specs=[p...  17 us
    ppermute x15, waiting for transfers between devices, swap(): return lax.ppermute(value, 'dp', [(i, i ^ bit) for i in range(8)])  14 us
    ppermute x6, starting transfers between devices, pair(): return lax.ppermute(value, 'tensor', [(z, z ^ s) for z in range(n_z)])  12.3 us
    ppermute x15, starting transfers between devices, swap(): return lax.ppermute(value, 'dp', [(i, i ^ bit) for i in range(8)])  11.2 us
    pallas_call x1, Pallas kernels, attend(): pl.pallas_call(functools.partial(attend_kernel, len(chunks)), in_specs=[p...  10 us
    ppermute x3, starting transfers between devices, body(): lax.ppermute(from_low, 'tensor', [(z, z + 1) for z in range(s - 1, n_z -...  9.86 us
    ppermute x3, waiting for transfers between devices, body(): lax.ppermute(from_high, 'tensor', [(z + 1, z) for z in range(n_z - s)])  9.8 us
    ppermute x6, waiting for transfers between devices, pair(): return lax.ppermute(value, 'tensor', [(z, z ^ s) for z in range(n_z)])  9.25 us
  transfers between devices with their start and end apart: 27, of which 11 were waited for; matrix products, arithmetic and copies ran while one was open for 9% of the time, Pallas kernels for 35%

profile of v17, /device:TPU:0, one launch (start us, length us, event | category | flops | bytes accessed | tf_op | source)
XLA Modules:
  0.0 131.3 jit_solution(1376047525688971981)
XLA Ops:
  0.6 1.3 collective-permute-start
  1.9 6.6 %collective-permute-start.1 = (bf16[256,2048]{1,0:T(8,128)(2,1)}, bf16[256,2048]{1,0:T(8,128)(2,1)}, u32[]{:S(2)}, u32[]{:S(2)}) collective-permute-start(bf16[256,2048]{1,0:T(8,128)(2,1)} %refs_0_.1), channel_id=1, source_target_pairs={{0,1},{1,2},{2,3},{4,5},{5,6},{6,7},{8,9},{9,10},{10,11},{12,13},{... | collective-permute-start | bytes 3145736 | tf_op jit(solution)/shard_map/ppermute | solution.py:603
  8.5 1.1 constant_dynamic-slice_fusion
  9.6 1.1 collective-permute-start.4
  10.7 2.0 %collective-permute-start.5 = (bf16[256,256]{1,0:T(8,128)(2,1)S(1)}, bf16[256,256]{1,0:T(8,128)(2,1)S(1)}, u32[]{:S(2)}, u32[]{:S(2)}) collective-permute-start(bf16[256,256]{1,0:T(8,128)(2,1)S(1)} %get-tuple-element.140), channel_id=1, source_target_pairs={{0,2},{1,3},{2,0},{3,1},{4,6},{5,7},{6,4},{7,5},{8,10},{9,11},{10,... | collective-permute-start | bytes 393224 | tf_op jit(solution)/shard_map/ppermute | solution.py:569
  12.7 1.4 %collective-permute-start.6 = (bf16[256,256]{1,0:T(8,128)(2,1)S(1)}, bf16[256,256]{1,0:T(8,128)(2,1)S(1)}, u32[]{:S(2)}, u32[]{:S(2)}) collective-permute-start(bf16[256,256]{1,0:T(8,128)(2,1)S(1)} %get-tuple-element.139), channel_id=1, source_target_pairs={{0,3},{1,2},{2,1},{3,0},{4,7},{5,6},{6,5},{7,4},{8,11},{9,10},{10,... | collective-permute-start | bytes 393224 | tf_op jit(solution)/shard_map/ppermute | solution.py:569
  14.8 4.9 %optimizer.1 = (f32[1024,256]{1,0:T(8,128)}, f32[1024,256]{1,0:T(8,128)}, f32[1024,256]{1,0:T(8,128)}, bf16[1024,256]{1,0:T(8,128)(2,1)}) custom-call(s32[1]{0:T(128)} %bitcast.place, bf16[8192,256]{1,0:T(8,128)(2,1)} %refs_3_.3, f32[1024,256]{1,0:T(8,128)} %master.1, f32[1024,256]{1,0:T(8,128)} %moment.1, f32[1024,256]{1,0:T(8,128)} %second.1, f32[1024,256]{1,0:T(8,128)} %grad.1), custom_call_target="tpu_custom_call" | custom-call | flops 10485760 | bytes 8388608 | tf_op jit(solution)/shard_map/optimizer/pallas_call | solution.py:51
  20.3 0.7 broadcast_in_dim.2.refs_1_
  21.0 4.2 %absorb.4 = (f32[256,256]{1,0:T(8,128)}, bf16[32,2048,256]{2,1,0:T(8,128)(2,1)}) custom-call(s32[3]{0:T(128)} %get-tuple-element.144.place, bf16[256,2048]{1,0:T(8,128)(2,1)} %refs_0_.1, f32[256,256]{1,0:T(8,128)} %broadcast_in_dim.2.refs_1_, bf16[8192,256]{1,0:T(8,128)(2,1)} %refs_3_.3), custom_call_target="tpu_custom_call" | custom-call | flops 268435456 | bytes 3145728 | tf_op jit(solution)/shard_map/absorb/pallas_call | solution.py:140
  25.3 1.4 %constant_dynamic-slice_fusion.3.refs_4_ = bf16[2048,256]{1,0:T(8,128)(2,1)S(1)} fusion(bf16[8192,256]{1,0:T(8,128)(2,1)} %refs_3_.3, s32[]{:T(128)S(6)} %select_n.57), kind=kLoop, calls=%fused_computation.12 | loop fusion | bytes 2097156 | tf_op jit(solution)/shard_map/dynamic_slice | solution.py:588
  26.7 0.8 fusion.1.refs_5_
  27.5 3.2 %collective-permute-done.refs_0_ = bf16[256,2048]{1,0:T(8,128)(2,1)} collective-permute-done((bf16[256,2048]{1,0:T(8,128)(2,1)}, bf16[256,2048]{1,0:T(8,128)(2,1)}, u32[]{:S(2)}, u32[]{:S(2)}) %collective-permute-start) | collective-permute-done | bytes 1048608 | tf_op jit(solution)/shard_map/ppermute | solution.py:602
  30.7 0.7 collective-permute-done.1.refs_0_
  31.4 1.3 collective-permute-start.2
  32.7 1.6 %collective-permute-start.3 = (bf16[256,2048]{1,0:T(8,128)(2,1)}, bf16[256,2048]{1,0:T(8,128)(2,1)}, u32[]{:S(2)}, u32[]{:S(2)}) collective-permute-start(bf16[256,2048]{1,0:T(8,128)(2,1)} %collective-permute-done.1.refs_0_), channel_id=1, source_target_pairs={{1,2},{2,3},{5,6},{6,7},{9,10},{10,11},{13,14},{14,15},{17,18},{18... | collective-permute-start | bytes 3145736 | tf_op jit(solution)/shard_map/ppermute | solution.py:603
  34.3 5.5 %collective-permute-done.5 = bf16[256,256]{1,0:T(8,128)(2,1)S(1)} collective-permute-done((bf16[256,256]{1,0:T(8,128)(2,1)S(1)}, bf16[256,256]{1,0:T(8,128)(2,1)S(1)}, u32[]{:S(2)}, u32[]{:S(2)}) %collective-permute-start.5) | collective-permute-done | bytes 131104 | tf_op jit(solution)/shard_map/ppermute | solution.py:569
  39.8 0.7 constant_dynamic-update-slice_fusion.2
  40.5 1.5 %collective-permute-start.8 = (bf16[1024,256]{1,0:T(8,128)(2,1)S(1)}, bf16[1024,256]{1,0:T(8,128)(2,1)S(1)}, u32[]{:S(2)}, u32[]{:S(2)}) collective-permute-start(bf16[1024,256]{1,0:T(8,128)(2,1)S(1)} %copy-done), channel_id=1, source_target_pairs={{0,16},{4,20},{8,24},{12,28},{16,0},{20,4},{24,8},{28,12},{1,17},{... | collective-permute-start | bytes 1572872 | tf_op jit(solution)/shard_map/ppermute | solution.py:398
  42.0 1.0 pad_maximum_fusion.1
  44.3 1.5 %collective-permute-start.7 = (bf16[768,256]{1,0:T(8,128)(2,1)}, bf16[768,256]{1,0:T(8,128)(2,1)S(1)}, u32[]{:S(2)}, u32[]{:S(2)}) collective-permute-start(bf16[768,256]{1,0:T(8,128)(2,1)} %constant_dynamic-update-slice_fusion.refs_5_), channel_id=1, source_target_pairs={{0,8},{4,12},{8,0},{12,4},{16,24},{20,28},{24,16},{28,20},{1,9},{5... | collective-permute-start | bytes 1179656 | tf_op jit(solution)/shard_map/ppermute | solution.py:398
  46.5 4.2 %absorb.5 = (f32[256,256]{1,0:T(8,128)}, bf16[32,2048,256]{2,1,0:T(8,128)(2,1)}) custom-call(s32[3]{0:T(128)} %get-tuple-element.142.place, bf16[256,2048]{1,0:T(8,128)(2,1)} %collective-permute-done.1.refs_0_, f32[256,256]{1,0:T(8,128)} %get-tuple-element.81.refs_1_, bf16[8192,256]{1,0:T(8,128)(2,1)} %refs_3_.3, ...), custom_call_target="tpu_custom_call", output_to_operand_aliasing={{1}: (4, {})} | custom-call | flops 268435456 | bytes 3145728 | tf_op jit(solution)/shard_map/absorb/pallas_call | solution.py:140
  50.7 4.2 %absorb.6 = (f32[256,256]{1,0:T(8,128)}, bf16[32,2048,256]{2,1,0:T(8,128)(2,1)}) custom-call(s32[3]{0:T(128)} %get-tuple-element.143.place, bf16[256,2048]{1,0:T(8,128)(2,1)} %collective-permute-done.refs_0_, f32[256,256]{1,0:T(8,128)} %get-tuple-element.83.refs_1_, bf16[8192,256]{1,0:T(8,128)(2,1)} %refs_3_.3, ...), custom_call_target="tpu_custom_call", output_to_operand_aliasing={{1}: (4, {})} | custom-call | flops 268435456 | bytes 3145728 | tf_op jit(solution)/shard_map/absorb/pallas_call | solution.py:140
  55.0 1.1 collective-permute-done.7.refs_7_
  56.0 1.0 pad_maximum_fusion
  57.1 0.9 pad_maximum_fusion.2
  58.0 2.2 %collective-permute-done.2.refs_1_ = bf16[256,2048]{1,0:T(8,128)(2,1)} collective-permute-done((bf16[256,2048]{1,0:T(8,128)(2,1)}, bf16[256,2048]{1,0:T(8,128)(2,1)}, u32[]{:S(2)}, u32[]{:S(2)}) %collective-permute-start.2) | collective-permute-done | bytes 1048608 | tf_op jit(solution)/shard_map/ppermute | solution.py:602
  60.2 1.3 collective-permute-start.10
  61.5 1.6 %collective-permute-start.11 = (bf16[256,2048]{1,0:T(8,128)(2,1)}, bf16[256,2048]{1,0:T(8,128)(2,1)}, u32[]{:S(2)}, u32[]{:S(2)}) collective-permute-start(bf16[256,2048]{1,0:T(8,128)(2,1)} %collective-permute-done.3.refs_0_), channel_id=1, source_target_pairs={{2,3},{6,7},{10,11},{14,15},{18,19},{22,23},{26,27},{30,31}} | collective-permute-start | bytes 3145736 | tf_op jit(solution)/shard_map/ppermute | solution.py:603
  63.1 1.4 %collective-permute-start.12 = (bf16[2048,256]{1,0:T(8,128)(2,1)}, bf16[2048,256]{1,0:T(8,128)(2,1)}, u32[]{:S(2)}, u32[]{:S(2)}) collective-permute-start(bf16[2048,256]{1,0:T(8,128)(2,1)} %pad_maximum_fusion), channel_id=1, source_target_pairs={{0,8},{4,12},{8,0},{12,4},{16,24},{20,28},{24,16},{28,20},{1,9},{5... | collective-permute-start | bytes 3145736 | tf_op jit(solution)/shard_map/ppermute | solution.py:398
  64.5 1.5 %collective-permute-start.13 = (bf16[1536,256]{1,0:T(8,128)(2,1)}, bf16[1536,256]{1,0:T(8,128)(2,1)}, u32[]{:S(2)}, u32[]{:S(2)}) collective-permute-start(bf16[1536,256]{1,0:T(8,128)(2,1)} %pad_maximum_fusion.2), channel_id=1, source_target_pairs={{0,16},{4,20},{8,24},{12,28},{16,0},{20,4},{24,8},{28,12},{1,17},{... | collective-permute-start | bytes 2359304 | tf_op jit(solution)/shard_map/ppermute | solution.py:398
  66.4 0.8 copy-done.1
  68.0 4.3 %absorb.7 = (f32[256,256]{1,0:T(8,128)}, bf16[32,2048,256]{2,1,0:T(8,128)(2,1)}) custom-call(s32[3]{0:T(128)} %pad_add_fusion.4.place, bf16[256,2048]{1,0:T(8,128)(2,1)} %collective-permute-done.3.refs_0_, bf16[256,2048]{1,0:T(8,128)(2,1)} %collective-permute-done.2.refs_1_, f32[256,256]{1,0:T(8,128)} %get-tuple-element.95.refs_2_, ...), custom_call_target="tpu_custom_call", output_to_operand_aliasing={{1}: (5, {})} | custom-call | flops 268435456 | bytes 3145728 | tf_op jit(solution)/shard_map/absorb/pallas_call | solution.py:140
  72.3 1.9 %place_rows.2.refs_2_ = bf16[8192,256]{1,0:T(8,128)(2,1)} custom-call(s32[4]{0:T(128)S(1)} %broadcast_xor_fusion.2.place, bf16[1024,256]{1,0:T(8,128)(2,1)S(1)} %copy-done, bf16[1792,256]{1,0:T(8,128)(2,1)S(1)} %collective-permute-done.9.refs_1_.refs_6_, bf16[1024,256]{1,0:T(8,128)(2,1)S(1)} %collective-permute-done.8.refs_2_, bf16[1024,256]{1,0:T(8,128)(2,1)S(1)} %copy-done.2), custom_call_target="tpu_custom_call" | custom-call | bytes 4194304 | tf_op jit(solution)/shard_map/place_rows/pallas_call | solution.py:516
  74.2 10.6 %collective-permute-done.13.refs_9_ = bf16[1536,256]{1,0:T(8,128)(2,1)} collective-permute-done((bf16[1536,256]{1,0:T(8,128)(2,1)}, bf16[1536,256]{1,0:T(8,128)(2,1)}, u32[]{:S(2)}, u32[]{:S(2)}) %collective-permute-start.13) | collective-permute-done | bytes 786464 | tf_op jit(solution)/shard_map/ppermute | solution.py:398
  84.8 4.5 %collective-permute-done.10.refs_1_ = bf16[256,2048]{1,0:T(8,128)(2,1)} collective-permute-done((bf16[256,2048]{1,0:T(8,128)(2,1)}, bf16[256,2048]{1,0:T(8,128)(2,1)}, u32[]{:S(2)}, u32[]{:S(2)}) %collective-permute-start.10) | collective-permute-done | bytes 1048608 | tf_op jit(solution)/shard_map/ppermute | solution.py:602
  89.8 10.0 %attend.1 = (bf16[32,2048,256]{2,1,0:T(8,128)(2,1)}, bf16[256,1024]{1,0:T(8,128)(2,1)}, bf16[256,256]{1,0:T(8,128)(2,1)}, bf16[4,1024,128]{2,1,0:T(8,128)(2,1)}, bf16[4,1024,128]{2,1,0:T(8,128)(2,1)}) custom-call(s32[3]{0:T(128)} %get-tuple-element.145.place, s32[5]{0:T(128)} %stack.93.order, ...), custom_call_target="tpu_custom_call", output_to_operand_aliasing={{0}: (6, {})} | custom-call | flops 805306368 | bytes 2097152 | tf_op jit(solution)/shard_map/attend/pallas_call | solution.py:245
  100.4 2.7 %weight_send.1 = (f32[2,1024,128]{2,1,0:T(8,128)S(1)}, f32[2,1024,128]{2,1,0:T(8,128)S(1)}) custom-call(s32[5]{0:T(128)S(1)} %stack.95.place, bf16[32,2048,256]{2,1,0:T(8,128)(2,1)} %get-tuple-element.108.held), custom_call_target="tpu_custom_call" | custom-call | flops 268435456 | bytes 2097152 | tf_op jit(solution)/shard_map/weight_send/pallas_call | solution.py:354
  103.3 1.5 %collective-permute-start.19 = (bf16[2,1024,128]{2,1,0:T(8,128)(2,1)S(1)}, bf16[2,1024,128]{2,1,0:T(8,128)(2,1)S(1)}, u32[]{:S(2)}, u32[]{:S(2)}) collective-permute-start(bf16[2,1024,128]{2,1,0:T(8,128)(2,1)S(1)} %get-tuple-element.115), channel_id=1, source_target_pairs={{0,8},{4,12},{8,0},{12,4},{16,24},{20,28},{24,16},{28,20},{1,9},{5... | collective-permute-start | bytes 1572872 | tf_op jit(solution)/shard_map/ppermute | solution.py:398
  104.8 1.5 %collective-permute-start.20 = (bf16[2,1024,128]{2,1,0:T(8,128)(2,1)S(1)}, bf16[2,1024,128]{2,1,0:T(8,128)(2,1)S(1)}, u32[]{:S(2)}, u32[]{:S(2)}) collective-permute-start(bf16[2,1024,128]{2,1,0:T(8,128)(2,1)S(1)} %get-tuple-element.116), channel_id=1, source_target_pairs={{0,16},{4,20},{8,24},{12,28},{16,0},{20,4},{24,8},{28,12},{1,17},{... | collective-permute-start | bytes 1572872 | tf_op jit(solution)/shard_map/ppermute | solution.py:398
  106.3 4.4 %collective-permute-start.21 = (bf16[256,256]{1,0:T(8,128)(2,1)S(1)}, bf16[256,256]{1,0:T(8,128)(2,1)S(1)}, u32[]{:S(2)}, u32[]{:S(2)}) collective-permute-start(bf16[256,256]{1,0:T(8,128)(2,1)S(1)} %copy-done.3), channel_id=1, source_target_pairs={{0,1},{1,0},{2,3},{3,2},{4,5},{5,4},{6,7},{7,6},{8,9},{9,8},{10,11... | collective-permute-start | bytes 393224 | tf_op jit(solution)/shard_map/ppermute | solution.py:569
  110.7 1.9 %collective-permute-start.22 = (bf16[256,256]{1,0:T(8,128)(2,1)S(1)}, bf16[256,256]{1,0:T(8,128)(2,1)S(1)}, u32[]{:S(2)}, u32[]{:S(2)}) collective-permute-start(bf16[256,256]{1,0:T(8,128)(2,1)S(1)} %copy-done.3), channel_id=1, source_target_pairs={{0,2},{1,3},{2,0},{3,1},{4,6},{5,7},{6,4},{7,5},{8,10},{9,11},{10,... | collective-permute-start | bytes 393224 | tf_op jit(solution)/shard_map/ppermute | solution.py:569
  112.6 1.5 %collective-permute-start.23 = (bf16[256,256]{1,0:T(8,128)(2,1)S(1)}, bf16[256,256]{1,0:T(8,128)(2,1)S(1)}, u32[]{:S(2)}, u32[]{:S(2)}) collective-permute-start(bf16[256,256]{1,0:T(8,128)(2,1)S(1)} %copy-done.3), channel_id=1, source_target_pairs={{0,3},{1,2},{2,1},{3,0},{4,7},{5,6},{6,5},{7,4},{8,11},{9,10},{10,... | collective-permute-start | bytes 393224 | tf_op jit(solution)/shard_map/ppermute | solution.py:569
  114.1 2.6 %place_rows.3 = bf16[8192,256]{1,0:T(8,128)(2,1)} custom-call(s32[4]{0:T(128)S(1)} %broadcast_xor_fusion.1.place, bf16[2048,256]{1,0:T(8,128)(2,1)} %collective-permute-done.12.refs_0_, bf16[2048,256]{1,0:T(8,128)(2,1)S(1)} %collective-permute-done.16.refs_1_, bf16[8192,256]{1,0:T(8,128)(2,1)} %place_rows.2.refs_2_), custom_call_target="tpu_custom_call", output_to_operand_aliasing={{}: (3, {})} | custom-call | bytes 4194304 | tf_op jit(solution)/shard_map/place_rows/pallas_call | solution.py:516
  116.7 2.7 %weight_keep.1 = (f32[2,1024,128]{2,1,0:T(8,128)S(1)}, f32[2,1024,128]{2,1,0:T(8,128)S(1)}) custom-call(s32[5]{0:T(128)S(1)} %stack.95.place, bf16[32,2048,256]{2,1,0:T(8,128)(2,1)} %get-tuple-element.108.held, bf16[4,1024,128]{2,1,0:T(8,128)(2,1)S(1)} %collective-permute-done.24.refs_0_), custom_call_target="tpu_custom_call" | custom-call | flops 268435456 | bytes 2097152 | tf_op jit(solution)/shard_map/weight_keep/pallas_call | solution.py:354
  119.4 3.8 %collective-permute-done.22.refs_2_ = bf16[256,256]{1,0:T(8,128)(2,1)S(1)} collective-permute-done((bf16[256,256]{1,0:T(8,128)(2,1)S(1)}, bf16[256,256]{1,0:T(8,128)(2,1)S(1)}, u32[]{:S(2)}, u32[]{:S(2)}) %collective-permute-start.22) | collective-permute-done | bytes 131104 | tf_op jit(solution)/shard_map/ppermute | solution.py:569
  124.4 3.9 %input_gradient.1 = bf16[256,2048]{1,0:T(8,128)(2,1)} custom-call(s32[8]{0:T(128)S(1)} %broadcast_xor_fusion.place, bf16[256,256]{1,0:T(8,128)(2,1)S(1)} %copy-done.3, bf16[256,256]{1,0:T(8,128)(2,1)S(1)} %collective-permute-done.21.refs_1_, bf16[256,256]{1,0:T(8,128)(2,1)S(1)} %collective-permute-done.22.refs_2_, ...), custom_call_target="tpu_custom_call" | custom-call | flops 1073741824 | bytes 6291456 | tf_op jit(solution)/shard_map/input_gradient/pallas_call | solution.py:73
  128.3 1.4 %collective-permute-done.25.last_a = bf16[1024,128]{1,0:T(8,128)(2,1)S(1)} collective-permute-done((bf16[1024,128]{1,0:T(8,128)(2,1)S(1)}, bf16[1024,128]{1,0:T(8,128)(2,1)S(1)}, u32[]{:S(2)}, u32[]{:S(2)}) %collective-permute-start.25) | collective-permute-done | bytes 262176 | tf_op jit(solution)/shard_map/ppermute | solution.py:398
  130.2 1.1 weight_finish.1
  (62 shorter events, 7.5 us)
Async XLA Ops:
  0.6 30.0 %collective-permute-start = (bf16[256,2048]{1,0:T(8,128)(2,1)}, bf16[256,2048]{1,0:T(8,128)(2,1)}, u32[]{:S(2)}, u32[]{:S(2)}) collective-permute-start(bf16[256,2048]{1,0:T(8,128)(2,1)} %refs_0_.1), channel_id=1, source_target_pairs={{1,0},{2,1},{3,2},{5,4},{6,5},{7,6},{9,8},{10,9},{11,10},{13,12},{... | collective-permute-start | bytes 3145736 | tf_op jit(solution)/shard_map/ppermute | solution.py:602
  1.9 29.4 %collective-permute-start.1 = (bf16[256,2048]{1,0:T(8,128)(2,1)}, bf16[256,2048]{1,0:T(8,128)(2,1)}, u32[]{:S(2)}, u32[]{:S(2)}) collective-permute-start(bf16[256,2048]{1,0:T(8,128)(2,1)} %refs_0_.1), channel_id=1, source_target_pairs={{0,1},{1,2},{2,3},{4,5},{5,6},{6,7},{8,9},{9,10},{10,11},{12,13},{... | collective-permute-start | bytes 3145736 | tf_op jit(solution)/shard_map/ppermute | solution.py:603
  9.6 24.7 %collective-permute-start.4 = (bf16[256,256]{1,0:T(8,128)(2,1)S(1)}, bf16[256,256]{1,0:T(8,128)(2,1)S(1)}, u32[]{:S(2)}, u32[]{:S(2)}) collective-permute-start(bf16[256,256]{1,0:T(8,128)(2,1)S(1)} %get-tuple-element.141), channel_id=1, source_target_pairs={{0,1},{1,0},{2,3},{3,2},{4,5},{5,4},{6,7},{7,6},{8,9},{9,8},{10,11... | collective-permute-start | bytes 393224 | tf_op jit(solution)/shard_map/ppermute | solution.py:569
  10.7 29.1 %collective-permute-start.5 = (bf16[256,256]{1,0:T(8,128)(2,1)S(1)}, bf16[256,256]{1,0:T(8,128)(2,1)S(1)}, u32[]{:S(2)}, u32[]{:S(2)}) collective-permute-start(bf16[256,256]{1,0:T(8,128)(2,1)S(1)} %get-tuple-element.140), channel_id=1, source_target_pairs={{0,2},{1,3},{2,0},{3,1},{4,6},{5,7},{6,4},{7,5},{8,10},{9,11},{10,... | collective-permute-start | bytes 393224 | tf_op jit(solution)/shard_map/ppermute | solution.py:569
  12.7 27.0 %collective-permute-start.6 = (bf16[256,256]{1,0:T(8,128)(2,1)S(1)}, bf16[256,256]{1,0:T(8,128)(2,1)S(1)}, u32[]{:S(2)}, u32[]{:S(2)}) collective-permute-start(bf16[256,256]{1,0:T(8,128)(2,1)S(1)} %get-tuple-element.139), channel_id=1, source_target_pairs={{0,3},{1,2},{2,1},{3,0},{4,7},{5,6},{6,5},{7,4},{8,11},{9,10},{10,... | collective-permute-start | bytes 393224 | tf_op jit(solution)/shard_map/ppermute | solution.py:569
  25.3 1.4 %copy-start.8 = (s32[1,256]{1,0:T(1,128)S(1)}, s32[1,256]{1,0:T(1,128)}, u32[]{:S(2)}) copy-start(s32[1,256]{1,0:T(1,128)} %param.15) | copy-start | bytes 3076
  25.3 15.2 %copy-start = (bf16[1024,256]{1,0:T(8,128)(2,1)S(1)}, bf16[1024,256]{1,0:T(8,128)(2,1)}, u32[]{:S(2)}) copy-start(bf16[1024,256]{1,0:T(8,128)(2,1)} %get-tuple-element.90.refs_0_) | copy-start | bytes 1572868
  31.4 28.8 %collective-permute-start.2 = (bf16[256,2048]{1,0:T(8,128)(2,1)}, bf16[256,2048]{1,0:T(8,128)(2,1)}, u32[]{:S(2)}, u32[]{:S(2)}) collective-permute-start(bf16[256,2048]{1,0:T(8,128)(2,1)} %collective-permute-done.refs_0_), channel_id=1, source_target_pairs={{1,0},{2,1},{5,4},{6,5},{9,8},{10,9},{13,12},{14,13},{17,16},{18,1... | collective-permute-start | bytes 3145736 | tf_op jit(solution)/shard_map/ppermute | solution.py:602
  32.7 27.5 %collective-permute-start.3 = (bf16[256,2048]{1,0:T(8,128)(2,1)}, bf16[256,2048]{1,0:T(8,128)(2,1)}, u32[]{:S(2)}, u32[]{:S(2)}) collective-permute-start(bf16[256,2048]{1,0:T(8,128)(2,1)} %collective-permute-done.1.refs_0_), channel_id=1, source_target_pairs={{1,2},{2,3},{5,6},{6,7},{9,10},{10,11},{13,14},{14,15},{17,18},{18... | collective-permute-start | bytes 3145736 | tf_op jit(solution)/shard_map/ppermute | solution.py:603
  39.8 3.2 %copy-start.4 = (bf16[256,256]{1,0:T(8,128)(2,1)}, bf16[256,256]{1,0:T(8,128)(2,1)S(1)}, u32[]{:S(2)}) copy-start(bf16[256,256]{1,0:T(8,128)(2,1)S(1)} %collective-permute-done.5) | copy-start | bytes 393220
  39.8 3.9 %copy-start.6 = (bf16[256,256]{1,0:T(8,128)(2,1)}, bf16[256,256]{1,0:T(8,128)(2,1)S(1)}, u32[]{:S(2)}) copy-start(bf16[256,256]{1,0:T(8,128)(2,1)S(1)} %collective-permute-done.6) | copy-start | bytes 393220
  40.5 15.6 %collective-permute-start.8 = (bf16[1024,256]{1,0:T(8,128)(2,1)S(1)}, bf16[1024,256]{1,0:T(8,128)(2,1)S(1)}, u32[]{:S(2)}, u32[]{:S(2)}) collective-permute-start(bf16[1024,256]{1,0:T(8,128)(2,1)S(1)} %copy-done), channel_id=1, source_target_pairs={{0,16},{4,20},{8,24},{12,28},{16,0},{20,4},{24,8},{28,12},{1,17},{... | collective-permute-start | bytes 1572872 | tf_op jit(solution)/shard_map/ppermute | solution.py:398
  43.6 14.4 %collective-permute-start.9 = (bf16[1792,256]{1,0:T(8,128)(2,1)}, bf16[1792,256]{1,0:T(8,128)(2,1)S(1)}, u32[]{:S(2)}, u32[]{:S(2)}) collective-permute-start(bf16[1792,256]{1,0:T(8,128)(2,1)} %pad_maximum_fusion.1), channel_id=1, source_target_pairs={{0,4},{4,0},{8,12},{12,8},{16,20},{20,16},{24,28},{28,24},{1,5},{5... | collective-permute-start | bytes 2752520 | tf_op jit(solution)/shard_map/ppermute | solution.py:398
  44.3 11.7 %collective-permute-start.7 = (bf16[768,256]{1,0:T(8,128)(2,1)}, bf16[768,256]{1,0:T(8,128)(2,1)S(1)}, u32[]{:S(2)}, u32[]{:S(2)}) collective-permute-start(bf16[768,256]{1,0:T(8,128)(2,1)} %constant_dynamic-update-slice_fusion.refs_5_), channel_id=1, source_target_pairs={{0,8},{4,12},{8,0},{12,4},{16,24},{20,28},{24,16},{28,20},{1,9},{5... | collective-permute-start | bytes 1179656 | tf_op jit(solution)/shard_map/ppermute | solution.py:398
  55.0 2.1 %copy-start.5 = (bf16[256,256]{1,0:T(8,128)(2,1)S(1)}, bf16[256,256]{1,0:T(8,128)(2,1)}, u32[]{:S(2)}) copy-start(bf16[256,256]{1,0:T(8,128)(2,1)} %copy-done.4) | copy-start | bytes 393220
  55.0 2.1 %copy-start.7 = (bf16[256,256]{1,0:T(8,128)(2,1)S(1)}, bf16[256,256]{1,0:T(8,128)(2,1)}, u32[]{:S(2)}) copy-start(bf16[256,256]{1,0:T(8,128)(2,1)} %copy-done.6) | copy-start | bytes 393220
  56.0 12.0 %copy-start.11 = (s32[4]{0:T(128)S(1)}, s32[4]{0:T(128)}, u32[]{:S(2)}) copy-start(s32[4]{0:T(128)} %constant.72.clone) | copy-start | bytes 52
  60.2 29.1 %collective-permute-start.10 = (bf16[256,2048]{1,0:T(8,128)(2,1)}, bf16[256,2048]{1,0:T(8,128)(2,1)}, u32[]{:S(2)}, u32[]{:S(2)}) collective-permute-start(bf16[256,2048]{1,0:T(8,128)(2,1)} %collective-permute-done.2.refs_1_), channel_id=1, source_target_pairs={{1,0},{5,4},{9,8},{13,12},{17,16},{21,20},{25,24},{29,28}} | collective-permute-start | bytes 3145736 | tf_op jit(solution)/shard_map/ppermute | solution.py:602
  61.5 27.8 %collective-permute-start.11 = (bf16[256,2048]{1,0:T(8,128)(2,1)}, bf16[256,2048]{1,0:T(8,128)(2,1)}, u32[]{:S(2)}, u32[]{:S(2)}) collective-permute-start(bf16[256,2048]{1,0:T(8,128)(2,1)} %collective-permute-done.3.refs_0_), channel_id=1, source_target_pairs={{2,3},{6,7},{10,11},{14,15},{18,19},{22,23},{26,27},{30,31}} | collective-permute-start | bytes 3145736 | tf_op jit(solution)/shard_map/ppermute | solution.py:603
  63.1 26.1 %collective-permute-start.12 = (bf16[2048,256]{1,0:T(8,128)(2,1)}, bf16[2048,256]{1,0:T(8,128)(2,1)}, u32[]{:S(2)}, u32[]{:S(2)}) collective-permute-start(bf16[2048,256]{1,0:T(8,128)(2,1)} %pad_maximum_fusion), channel_id=1, source_target_pairs={{0,8},{4,12},{8,0},{12,4},{16,24},{20,28},{24,16},{28,20},{1,9},{5... | collective-permute-start | bytes 3145736 | tf_op jit(solution)/shard_map/ppermute | solution.py:398
  64.5 1.9 %collective-permute-start.15 = (bf16[1024,256]{1,0:T(8,128)(2,1)S(1)}, bf16[1024,256]{1,0:T(8,128)(2,1)S(1)}, u32[]{:S(2)}, u32[]{:S(2)}) collective-permute-start(bf16[1024,256]{1,0:T(8,128)(2,1)S(1)} %collective-permute-done.8.refs_2_), channel_id=1, source_target_pairs={{0,4},{4,0},{8,12},{12,8},{16,20},{20,16},{24,28},{28,24},{1,5},{5... | collective-permute-start | bytes 1572872 | tf_op jit(solution)/shard_map/ppermute | solution.py:398
  64.5 20.3 %collective-permute-start.13 = (bf16[1536,256]{1,0:T(8,128)(2,1)}, bf16[1536,256]{1,0:T(8,128)(2,1)}, u32[]{:S(2)}, u32[]{:S(2)}) collective-permute-start(bf16[1536,256]{1,0:T(8,128)(2,1)} %pad_maximum_fusion.2), channel_id=1, source_target_pairs={{0,16},{4,20},{8,24},{12,28},{16,0},{20,4},{24,8},{28,12},{1,17},{... | collective-permute-start | bytes 2359304 | tf_op jit(solution)/shard_map/ppermute | solution.py:398
  66.4 0.8 copy-start.1
  67.2 7.0 %collective-permute-start.14 = (bf16[768,256]{1,0:T(8,128)(2,1)S(1)}, bf16[768,256]{1,0:T(8,128)(2,1)}, u32[]{:S(2)}, u32[]{:S(2)}) collective-permute-start(bf16[768,256]{1,0:T(8,128)(2,1)S(1)} %collective-permute-done.7.refs_7_), channel_id=1, source_target_pairs={{0,4},{4,0},{8,12},{12,8},{16,20},{20,16},{24,28},{28,24},{1,5},{5... | collective-permute-start | bytes 1179656 | tf_op jit(solution)/shard_map/ppermute | solution.py:398
  68.0 4.3 %copy-start.2 = (bf16[1024,256]{1,0:T(8,128)(2,1)S(1)}, bf16[1024,256]{1,0:T(8,128)(2,1)}, u32[]{:S(2)}) copy-start(bf16[1024,256]{1,0:T(8,128)(2,1)} %copy-done.1) | copy-start | bytes 1572868
  89.3 10.6 %collective-permute-start.16 = (bf16[2048,256]{1,0:T(8,128)(2,1)}, bf16[2048,256]{1,0:T(8,128)(2,1)S(1)}, u32[]{:S(2)}, u32[]{:S(2)}) collective-permute-start(bf16[2048,256]{1,0:T(8,128)(2,1)} %collective-permute-done.12.refs_0_), channel_id=1, source_target_pairs={{0,4},{4,0},{8,12},{12,8},{16,20},{20,16},{24,28},{28,24},{1,5},{5... | collective-permute-start | bytes 3145736 | tf_op jit(solution)/shard_map/ppermute | solution.py:398
  89.3 10.5 %collective-permute-start.17 = (bf16[1536,256]{1,0:T(8,128)(2,1)}, bf16[1536,256]{1,0:T(8,128)(2,1)}, u32[]{:S(2)}, u32[]{:S(2)}) collective-permute-start(bf16[1536,256]{1,0:T(8,128)(2,1)} %collective-permute-done.13.refs_9_), channel_id=1, source_target_pairs={{0,4},{4,0},{8,12},{12,8},{16,20},{20,16},{24,28},{28,24},{1,5},{5... | collective-permute-start | bytes 2359304 | tf_op jit(solution)/shard_map/ppermute | solution.py:398
  99.8 3.3 %collective-permute-start.18 = (bf16[4,1024,128]{2,1,0:T(8,128)(2,1)}, bf16[4,1024,128]{2,1,0:T(8,128)(2,1)S(1)}, u32[]{:S(2)}, u32[]{:S(2)}) collective-permute-start(bf16[4,1024,128]{2,1,0:T(8,128)(2,1)} %get-tuple-element.114), channel_id=1, source_target_pairs={{0,4},{4,0},{8,12},{12,8},{16,20},{20,16},{24,28},{28,24},{1,5},{5... | collective-permute-start | bytes 3145736 | tf_op jit(solution)/shard_map/ppermute | solution.py:398
  100.0 12.7 %collective-permute-start.24 = (bf16[4,1024,128]{2,1,0:T(8,128)(2,1)}, bf16[4,1024,128]{2,1,0:T(8,128)(2,1)S(1)}, u32[]{:S(2)}, u32[]{:S(2)}) collective-permute-start(bf16[4,1024,128]{2,1,0:T(8,128)(2,1)} %get-tuple-element.121), channel_id=1, source_target_pairs={{0,4},{4,0},{8,12},{12,8},{16,20},{20,16},{24,28},{28,24},{1,5},{5... | collective-permute-start | bytes 3145736 | tf_op jit(solution)/shard_map/ppermute | solution.py:398
  103.1 3.2 %copy-start.3 = (bf16[256,256]{1,0:T(8,128)(2,1)S(1)}, bf16[256,256]{1,0:T(8,128)(2,1)}, u32[]{:S(2)}) copy-start(bf16[256,256]{1,0:T(8,128)(2,1)} %get-tuple-element.128.refs_0_) | copy-start | bytes 393220
  103.1 11.0 %copy-start.10 = (s32[4]{0:T(128)S(1)}, s32[4]{0:T(128)}, u32[]{:S(2)}) copy-start(s32[4]{0:T(128)} %constant.73.clone) | copy-start | bytes 52
  103.3 19.9 %collective-permute-start.19 = (bf16[2,1024,128]{2,1,0:T(8,128)(2,1)S(1)}, bf16[2,1024,128]{2,1,0:T(8,128)(2,1)S(1)}, u32[]{:S(2)}, u32[]{:S(2)}) collective-permute-start(bf16[2,1024,128]{2,1,0:T(8,128)(2,1)S(1)} %get-tuple-element.115), channel_id=1, source_target_pairs={{0,8},{4,12},{8,0},{12,4},{16,24},{20,28},{24,16},{28,20},{1,9},{5... | collective-permute-start | bytes 1572872 | tf_op jit(solution)/shard_map/ppermute | solution.py:398
  104.8 18.4 %collective-permute-start.20 = (bf16[2,1024,128]{2,1,0:T(8,128)(2,1)S(1)}, bf16[2,1024,128]{2,1,0:T(8,128)(2,1)S(1)}, u32[]{:S(2)}, u32[]{:S(2)}) collective-permute-start(bf16[2,1024,128]{2,1,0:T(8,128)(2,1)S(1)} %get-tuple-element.116), channel_id=1, source_target_pairs={{0,16},{4,20},{8,24},{12,28},{16,0},{20,4},{24,8},{28,12},{1,17},{... | collective-permute-start | bytes 1572872 | tf_op jit(solution)/shard_map/ppermute | solution.py:398
  106.3 13.1 %collective-permute-start.21 = (bf16[256,256]{1,0:T(8,128)(2,1)S(1)}, bf16[256,256]{1,0:T(8,128)(2,1)S(1)}, u32[]{:S(2)}, u32[]{:S(2)}) collective-permute-start(bf16[256,256]{1,0:T(8,128)(2,1)S(1)} %copy-done.3), channel_id=1, source_target_pairs={{0,1},{1,0},{2,3},{3,2},{4,5},{5,4},{6,7},{7,6},{8,9},{9,8},{10,11... | collective-permute-start | bytes 393224 | tf_op jit(solution)/shard_map/ppermute | solution.py:569
  110.7 12.5 %collective-permute-start.22 = (bf16[256,256]{1,0:T(8,128)(2,1)S(1)}, bf16[256,256]{1,0:T(8,128)(2,1)S(1)}, u32[]{:S(2)}, u32[]{:S(2)}) collective-permute-start(bf16[256,256]{1,0:T(8,128)(2,1)S(1)} %copy-done.3), channel_id=1, source_target_pairs={{0,2},{1,3},{2,0},{3,1},{4,6},{5,7},{6,4},{7,5},{8,10},{9,11},{10,... | collective-permute-start | bytes 393224 | tf_op jit(solution)/shard_map/ppermute | solution.py:569
  112.6 10.6 %collective-permute-start.23 = (bf16[256,256]{1,0:T(8,128)(2,1)S(1)}, bf16[256,256]{1,0:T(8,128)(2,1)S(1)}, u32[]{:S(2)}, u32[]{:S(2)}) collective-permute-start(bf16[256,256]{1,0:T(8,128)(2,1)S(1)} %copy-done.3), channel_id=1, source_target_pairs={{0,3},{1,2},{2,1},{3,0},{4,7},{5,6},{6,5},{7,4},{8,11},{9,10},{10,... | collective-permute-start | bytes 393224 | tf_op jit(solution)/shard_map/ppermute | solution.py:569
  119.4 5.0 %copy-start.9 = (s32[8]{0:T(128)S(1)}, s32[8]{0:T(128)}, u32[]{:S(2)}) copy-start(s32[8]{0:T(128)} %constant.74.clone) | copy-start | bytes 100
  123.3 6.4 %collective-permute-start.25 = (bf16[1024,128]{1,0:T(8,128)(2,1)S(1)}, bf16[1024,128]{1,0:T(8,128)(2,1)S(1)}, u32[]{:S(2)}, u32[]{:S(2)}) collective-permute-start(bf16[1024,128]{1,0:T(8,128)(2,1)S(1)} %get-tuple-element.126), channel_id=1, source_target_pairs={{0,16},{4,20},{8,24},{12,28},{16,0},{20,4},{24,8},{28,12},{1,17},{... | collective-permute-start | bytes 786440 | tf_op jit(solution)/shard_map/ppermute | solution.py:398
  123.9 6.4 %collective-permute-start.26 = (bf16[1024,128]{1,0:T(8,128)(2,1)S(1)}, bf16[1024,128]{1,0:T(8,128)(2,1)S(1)}, u32[]{:S(2)}, u32[]{:S(2)}) collective-permute-start(bf16[1024,128]{1,0:T(8,128)(2,1)S(1)} %get-tuple-element.127), channel_id=1, source_target_pairs={{0,8},{4,12},{8,0},{12,4},{16,24},{20,28},{24,16},{28,20},{1,9},{5... | collective-permute-start | bytes 786440 | tf_op jit(solution)/shard_map/ppermute | solution.py:398

commit v18 on v17

--- a/solution.py
+++ b/solution.py
@@ -309,7 +309,7 @@
 def weight_products(copies, groups, buffer, d_projected, give):
     rows = buffer.shape[1]
     half = d_projected.shape[1] // 2
-    block = min(rows, 256)
+    block = min(rows, 128)
     for chunk, copy in copies.items():
         copy.wait()
         wanted = [

time: 132 us -> 133 us (level)
  no operation moved by 1% of the time
where the time goes in v18:
time: 133 us; the launch traced here: 131 us
  Pallas kernels  47.1 us (35%)
  starting transfers between devices  37.2 us (28%)
  waiting for transfers between devices  33.8 us (25%)
  local copies, waits for them, and re-layouts  6.68 us (5%)
  other arithmetic  5.69 us (4%)
    pallas_call x4, Pallas kernels, absorb(): pl.pallas_call(functools.partial(absorb_kernel, len(chunks)), in_specs=[p...  17 us
    ppermute x15, waiting for transfers between devices, swap(): return lax.ppermute(value, 'dp', [(i, i ^ bit) for i in range(8)])  14 us
    ppermute x6, starting transfers between devices, pair(): return lax.ppermute(value, 'tensor', [(z, z ^ s) for z in range(n_z)])  12.3 us
    ppermute x15, starting transfers between devices, swap(): return lax.ppermute(value, 'dp', [(i, i ^ bit) for i in range(8)])  11.2 us
    pallas_call x1, Pallas kernels, attend(): pl.pallas_call(functools.partial(attend_kernel, len(chunks)), in_specs=[p...  10.1 us
    ppermute x3, starting transfers between devices, body(): lax.ppermute(from_low, 'tensor', [(z, z + 1) for z in range(s - 1, n_z -...  9.86 us
    ppermute x3, waiting for transfers between devices, body(): lax.ppermute(from_high, 'tensor', [(z + 1, z) for z in range(n_z - s)])  9.8 us
    ppermute x6, waiting for transfers between devices, pair(): return lax.ppermute(value, 'tensor', [(z, z ^ s) for z in range(n_z)])  9.27 us
  transfers between devices with their start and end apart: 27, of which 11 were waited for; matrix products, arithmetic and copies ran while one was open for 9% of the time, Pallas kernels for 35%

profile of v18, /device:TPU:0, one launch (start us, length us, event | category | flops | bytes accessed | tf_op | source)
XLA Modules:
  0.0 131.4 jit_solution(1913466901775065816)
XLA Ops:
  0.6 1.3 collective-permute-start
  1.9 6.6 %collective-permute-start.1 = (bf16[256,2048]{1,0:T(8,128)(2,1)}, bf16[256,2048]{1,0:T(8,128)(2,1)}, u32[]{:S(2)}, u32[]{:S(2)}) collective-permute-start(bf16[256,2048]{1,0:T(8,128)(2,1)} %refs_0_.1), channel_id=1, source_target_pairs={{0,1},{1,2},{2,3},{4,5},{5,6},{6,7},{8,9},{9,10},{10,11},{12,13},{... | collective-permute-start | bytes 3145736 | tf_op jit(solution)/shard_map/ppermute | solution.py:603
  8.5 1.1 constant_dynamic-slice_fusion
  9.6 1.1 collective-permute-start.4
  10.7 2.0 %collective-permute-start.5 = (bf16[256,256]{1,0:T(8,128)(2,1)S(1)}, bf16[256,256]{1,0:T(8,128)(2,1)S(1)}, u32[]{:S(2)}, u32[]{:S(2)}) collective-permute-start(bf16[256,256]{1,0:T(8,128)(2,1)S(1)} %get-tuple-element.140), channel_id=1, source_target_pairs={{0,2},{1,3},{2,0},{3,1},{4,6},{5,7},{6,4},{7,5},{8,10},{9,11},{10,... | collective-permute-start | bytes 393224 | tf_op jit(solution)/shard_map/ppermute | solution.py:569
  12.7 1.4 %collective-permute-start.6 = (bf16[256,256]{1,0:T(8,128)(2,1)S(1)}, bf16[256,256]{1,0:T(8,128)(2,1)S(1)}, u32[]{:S(2)}, u32[]{:S(2)}) collective-permute-start(bf16[256,256]{1,0:T(8,128)(2,1)S(1)} %get-tuple-element.139), channel_id=1, source_target_pairs={{0,3},{1,2},{2,1},{3,0},{4,7},{5,6},{6,5},{7,4},{8,11},{9,10},{10,... | collective-permute-start | bytes 393224 | tf_op jit(solution)/shard_map/ppermute | solution.py:569
  14.8 4.9 %optimizer.1 = (f32[1024,256]{1,0:T(8,128)}, f32[1024,256]{1,0:T(8,128)}, f32[1024,256]{1,0:T(8,128)}, bf16[1024,256]{1,0:T(8,128)(2,1)}) custom-call(s32[1]{0:T(128)} %bitcast.place, bf16[8192,256]{1,0:T(8,128)(2,1)} %refs_3_.3, f32[1024,256]{1,0:T(8,128)} %master.1, f32[1024,256]{1,0:T(8,128)} %moment.1, f32[1024,256]{1,0:T(8,128)} %second.1, f32[1024,256]{1,0:T(8,128)} %grad.1), custom_call_target="tpu_custom_call" | custom-call | flops 10485760 | bytes 8388608 | tf_op jit(solution)/shard_map/optimizer/pallas_call | solution.py:51
  20.3 0.7 broadcast_in_dim.2.refs_1_
  21.0 4.2 %absorb.4 = (f32[256,256]{1,0:T(8,128)}, bf16[32,2048,256]{2,1,0:T(8,128)(2,1)}) custom-call(s32[3]{0:T(128)} %get-tuple-element.144.place, bf16[256,2048]{1,0:T(8,128)(2,1)} %refs_0_.1, f32[256,256]{1,0:T(8,128)} %broadcast_in_dim.2.refs_1_, bf16[8192,256]{1,0:T(8,128)(2,1)} %refs_3_.3), custom_call_target="tpu_custom_call" | custom-call | flops 268435456 | bytes 3145728 | tf_op jit(solution)/shard_map/absorb/pallas_call | solution.py:140
  25.3 1.4 %constant_dynamic-slice_fusion.3.refs_4_ = bf16[2048,256]{1,0:T(8,128)(2,1)S(1)} fusion(bf16[8192,256]{1,0:T(8,128)(2,1)} %refs_3_.3, s32[]{:T(128)S(6)} %select_n.57), kind=kLoop, calls=%fused_computation.12 | loop fusion | bytes 2097156 | tf_op jit(solution)/shard_map/dynamic_slice | solution.py:588
  26.7 0.8 fusion.1.refs_5_
  27.5 3.2 %collective-permute-done.refs_0_ = bf16[256,2048]{1,0:T(8,128)(2,1)} collective-permute-done((bf16[256,2048]{1,0:T(8,128)(2,1)}, bf16[256,2048]{1,0:T(8,128)(2,1)}, u32[]{:S(2)}, u32[]{:S(2)}) %collective-permute-start) | collective-permute-done | bytes 1048608 | tf_op jit(solution)/shard_map/ppermute | solution.py:602
  30.7 0.7 collective-permute-done.1.refs_0_
  31.4 1.3 collective-permute-start.2
  32.7 1.6 %collective-permute-start.3 = (bf16[256,2048]{1,0:T(8,128)(2,1)}, bf16[256,2048]{1,0:T(8,128)(2,1)}, u32[]{:S(2)}, u32[]{:S(2)}) collective-permute-start(bf16[256,2048]{1,0:T(8,128)(2,1)} %collective-permute-done.1.refs_0_), channel_id=1, source_target_pairs={{1,2},{2,3},{5,6},{6,7},{9,10},{10,11},{13,14},{14,15},{17,18},{18... | collective-permute-start | bytes 3145736 | tf_op jit(solution)/shard_map/ppermute | solution.py:603
  34.3 5.5 %collective-permute-done.5 = bf16[256,256]{1,0:T(8,128)(2,1)S(1)} collective-permute-done((bf16[256,256]{1,0:T(8,128)(2,1)S(1)}, bf16[256,256]{1,0:T(8,128)(2,1)S(1)}, u32[]{:S(2)}, u32[]{:S(2)}) %collective-permute-start.5) | collective-permute-done | bytes 131104 | tf_op jit(solution)/shard_map/ppermute | solution.py:569
  39.8 0.7 constant_dynamic-update-slice_fusion.2
  40.5 1.5 %collective-permute-start.8 = (bf16[1024,256]{1,0:T(8,128)(2,1)S(1)}, bf16[1024,256]{1,0:T(8,128)(2,1)S(1)}, u32[]{:S(2)}, u32[]{:S(2)}) collective-permute-start(bf16[1024,256]{1,0:T(8,128)(2,1)S(1)} %copy-done), channel_id=1, source_target_pairs={{0,16},{4,20},{8,24},{12,28},{16,0},{20,4},{24,8},{28,12},{1,17},{... | collective-permute-start | bytes 1572872 | tf_op jit(solution)/shard_map/ppermute | solution.py:398
  42.0 1.0 pad_maximum_fusion.1
  44.3 1.5 %collective-permute-start.7 = (bf16[768,256]{1,0:T(8,128)(2,1)}, bf16[768,256]{1,0:T(8,128)(2,1)S(1)}, u32[]{:S(2)}, u32[]{:S(2)}) collective-permute-start(bf16[768,256]{1,0:T(8,128)(2,1)} %constant_dynamic-update-slice_fusion.refs_5_), channel_id=1, source_target_pairs={{0,8},{4,12},{8,0},{12,4},{16,24},{20,28},{24,16},{28,20},{1,9},{5... | collective-permute-start | bytes 1179656 | tf_op jit(solution)/shard_map/ppermute | solution.py:398
  46.5 4.2 %absorb.5 = (f32[256,256]{1,0:T(8,128)}, bf16[32,2048,256]{2,1,0:T(8,128)(2,1)}) custom-call(s32[3]{0:T(128)} %get-tuple-element.142.place, bf16[256,2048]{1,0:T(8,128)(2,1)} %collective-permute-done.1.refs_0_, f32[256,256]{1,0:T(8,128)} %get-tuple-element.81.refs_1_, bf16[8192,256]{1,0:T(8,128)(2,1)} %refs_3_.3, ...), custom_call_target="tpu_custom_call", output_to_operand_aliasing={{1}: (4, {})} | custom-call | flops 268435456 | bytes 3145728 | tf_op jit(solution)/shard_map/absorb/pallas_call | solution.py:140
  50.7 4.2 %absorb.6 = (f32[256,256]{1,0:T(8,128)}, bf16[32,2048,256]{2,1,0:T(8,128)(2,1)}) custom-call(s32[3]{0:T(128)} %get-tuple-element.143.place, bf16[256,2048]{1,0:T(8,128)(2,1)} %collective-permute-done.refs_0_, f32[256,256]{1,0:T(8,128)} %get-tuple-element.83.refs_1_, bf16[8192,256]{1,0:T(8,128)(2,1)} %refs_3_.3, ...), custom_call_target="tpu_custom_call", output_to_operand_aliasing={{1}: (4, {})} | custom-call | flops 268435456 | bytes 3145728 | tf_op jit(solution)/shard_map/absorb/pallas_call | solution.py:140
  55.0 1.1 collective-permute-done.7.refs_7_
  56.0 1.0 pad_maximum_fusion
  57.1 0.9 pad_maximum_fusion.2
  58.0 2.2 %collective-permute-done.2.refs_1_ = bf16[256,2048]{1,0:T(8,128)(2,1)} collective-permute-done((bf16[256,2048]{1,0:T(8,128)(2,1)}, bf16[256,2048]{1,0:T(8,128)(2,1)}, u32[]{:S(2)}, u32[]{:S(2)}) %collective-permute-start.2) | collective-permute-done | bytes 1048608 | tf_op jit(solution)/shard_map/ppermute | solution.py:602
  60.2 1.3 collective-permute-start.10
  61.5 1.6 %collective-permute-start.11 = (bf16[256,2048]{1,0:T(8,128)(2,1)}, bf16[256,2048]{1,0:T(8,128)(2,1)}, u32[]{:S(2)}, u32[]{:S(2)}) collective-permute-start(bf16[256,2048]{1,0:T(8,128)(2,1)} %collective-permute-done.3.refs_0_), channel_id=1, source_target_pairs={{2,3},{6,7},{10,11},{14,15},{18,19},{22,23},{26,27},{30,31}} | collective-permute-start | bytes 3145736 | tf_op jit(solution)/shard_map/ppermute | solution.py:603
  63.1 1.4 %collective-permute-start.12 = (bf16[2048,256]{1,0:T(8,128)(2,1)}, bf16[2048,256]{1,0:T(8,128)(2,1)}, u32[]{:S(2)}, u32[]{:S(2)}) collective-permute-start(bf16[2048,256]{1,0:T(8,128)(2,1)} %pad_maximum_fusion), channel_id=1, source_target_pairs={{0,8},{4,12},{8,0},{12,4},{16,24},{20,28},{24,16},{28,20},{1,9},{5... | collective-permute-start | bytes 3145736 | tf_op jit(solution)/shard_map/ppermute | solution.py:398
  64.5 1.5 %collective-permute-start.13 = (bf16[1536,256]{1,0:T(8,128)(2,1)}, bf16[1536,256]{1,0:T(8,128)(2,1)}, u32[]{:S(2)}, u32[]{:S(2)}) collective-permute-start(bf16[1536,256]{1,0:T(8,128)(2,1)} %pad_maximum_fusion.2), channel_id=1, source_target_pairs={{0,16},{4,20},{8,24},{12,28},{16,0},{20,4},{24,8},{28,12},{1,17},{... | collective-permute-start | bytes 2359304 | tf_op jit(solution)/shard_map/ppermute | solution.py:398
  66.4 0.8 copy-done.1
  68.0 4.3 %absorb.7 = (f32[256,256]{1,0:T(8,128)}, bf16[32,2048,256]{2,1,0:T(8,128)(2,1)}) custom-call(s32[3]{0:T(128)} %pad_add_fusion.4.place, bf16[256,2048]{1,0:T(8,128)(2,1)} %collective-permute-done.3.refs_0_, bf16[256,2048]{1,0:T(8,128)(2,1)} %collective-permute-done.2.refs_1_, f32[256,256]{1,0:T(8,128)} %get-tuple-element.95.refs_2_, ...), custom_call_target="tpu_custom_call", output_to_operand_aliasing={{1}: (5, {})} | custom-call | flops 268435456 | bytes 3145728 | tf_op jit(solution)/shard_map/absorb/pallas_call | solution.py:140
  72.3 1.9 %place_rows.2.refs_2_ = bf16[8192,256]{1,0:T(8,128)(2,1)} custom-call(s32[4]{0:T(128)S(1)} %broadcast_xor_fusion.2.place, bf16[1024,256]{1,0:T(8,128)(2,1)S(1)} %copy-done, bf16[1792,256]{1,0:T(8,128)(2,1)S(1)} %collective-permute-done.9.refs_1_.refs_6_, bf16[1024,256]{1,0:T(8,128)(2,1)S(1)} %collective-permute-done.8.refs_2_, bf16[1024,256]{1,0:T(8,128)(2,1)S(1)} %copy-done.2), custom_call_target="tpu_custom_call" | custom-call | bytes 4194304 | tf_op jit(solution)/shard_map/place_rows/pallas_call | solution.py:516
  74.2 10.6 %collective-permute-done.13.refs_9_ = bf16[1536,256]{1,0:T(8,128)(2,1)} collective-permute-done((bf16[1536,256]{1,0:T(8,128)(2,1)}, bf16[1536,256]{1,0:T(8,128)(2,1)}, u32[]{:S(2)}, u32[]{:S(2)}) %collective-permute-start.13) | collective-permute-done | bytes 786464 | tf_op jit(solution)/shard_map/ppermute | solution.py:398
  84.8 4.5 %collective-permute-done.10.refs_1_ = bf16[256,2048]{1,0:T(8,128)(2,1)} collective-permute-done((bf16[256,2048]{1,0:T(8,128)(2,1)}, bf16[256,2048]{1,0:T(8,128)(2,1)}, u32[]{:S(2)}, u32[]{:S(2)}) %collective-permute-start.10) | collective-permute-done | bytes 1048608 | tf_op jit(solution)/shard_map/ppermute | solution.py:602
  89.8 10.1 %attend.1 = (bf16[32,2048,256]{2,1,0:T(8,128)(2,1)}, bf16[256,1024]{1,0:T(8,128)(2,1)}, bf16[256,256]{1,0:T(8,128)(2,1)}, bf16[4,1024,128]{2,1,0:T(8,128)(2,1)}, bf16[4,1024,128]{2,1,0:T(8,128)(2,1)}) custom-call(s32[3]{0:T(128)} %get-tuple-element.145.place, s32[5]{0:T(128)} %stack.93.order, ...), custom_call_target="tpu_custom_call", output_to_operand_aliasing={{0}: (6, {})} | custom-call | flops 805306368 | bytes 2097152 | tf_op jit(solution)/shard_map/attend/pallas_call | solution.py:245
  100.4 2.7 %weight_send.1 = (f32[2,1024,128]{2,1,0:T(8,128)S(1)}, f32[2,1024,128]{2,1,0:T(8,128)S(1)}) custom-call(s32[5]{0:T(128)S(1)} %stack.95.place, bf16[32,2048,256]{2,1,0:T(8,128)(2,1)} %get-tuple-element.108.held), custom_call_target="tpu_custom_call" | custom-call | flops 268435456 | bytes 2097152 | tf_op jit(solution)/shard_map/weight_send/pallas_call | solution.py:354
  103.3 1.5 %collective-permute-start.19 = (bf16[2,1024,128]{2,1,0:T(8,128)(2,1)S(1)}, bf16[2,1024,128]{2,1,0:T(8,128)(2,1)S(1)}, u32[]{:S(2)}, u32[]{:S(2)}) collective-permute-start(bf16[2,1024,128]{2,1,0:T(8,128)(2,1)S(1)} %get-tuple-element.115), channel_id=1, source_target_pairs={{0,8},{4,12},{8,0},{12,4},{16,24},{20,28},{24,16},{28,20},{1,9},{5... | collective-permute-start | bytes 1572872 | tf_op jit(solution)/shard_map/ppermute | solution.py:398
  104.9 1.5 %collective-permute-start.20 = (bf16[2,1024,128]{2,1,0:T(8,128)(2,1)S(1)}, bf16[2,1024,128]{2,1,0:T(8,128)(2,1)S(1)}, u32[]{:S(2)}, u32[]{:S(2)}) collective-permute-start(bf16[2,1024,128]{2,1,0:T(8,128)(2,1)S(1)} %get-tuple-element.116), channel_id=1, source_target_pairs={{0,16},{4,20},{8,24},{12,28},{16,0},{20,4},{24,8},{28,12},{1,17},{... | collective-permute-start | bytes 1572872 | tf_op jit(solution)/shard_map/ppermute | solution.py:398
  106.4 4.4 %collective-permute-start.21 = (bf16[256,256]{1,0:T(8,128)(2,1)S(1)}, bf16[256,256]{1,0:T(8,128)(2,1)S(1)}, u32[]{:S(2)}, u32[]{:S(2)}) collective-permute-start(bf16[256,256]{1,0:T(8,128)(2,1)S(1)} %copy-done.3), channel_id=1, source_target_pairs={{0,1},{1,0},{2,3},{3,2},{4,5},{5,4},{6,7},{7,6},{8,9},{9,8},{10,11... | collective-permute-start | bytes 393224 | tf_op jit(solution)/shard_map/ppermute | solution.py:569
  110.7 1.9 %collective-permute-start.22 = (bf16[256,256]{1,0:T(8,128)(2,1)S(1)}, bf16[256,256]{1,0:T(8,128)(2,1)S(1)}, u32[]{:S(2)}, u32[]{:S(2)}) collective-permute-start(bf16[256,256]{1,0:T(8,128)(2,1)S(1)} %copy-done.3), channel_id=1, source_target_pairs={{0,2},{1,3},{2,0},{3,1},{4,6},{5,7},{6,4},{7,5},{8,10},{9,11},{10,... | collective-permute-start | bytes 393224 | tf_op jit(solution)/shard_map/ppermute | solution.py:569
  112.7 1.5 %collective-permute-start.23 = (bf16[256,256]{1,0:T(8,128)(2,1)S(1)}, bf16[256,256]{1,0:T(8,128)(2,1)S(1)}, u32[]{:S(2)}, u32[]{:S(2)}) collective-permute-start(bf16[256,256]{1,0:T(8,128)(2,1)S(1)} %copy-done.3), channel_id=1, source_target_pairs={{0,3},{1,2},{2,1},{3,0},{4,7},{5,6},{6,5},{7,4},{8,11},{9,10},{10,... | collective-permute-start | bytes 393224 | tf_op jit(solution)/shard_map/ppermute | solution.py:569
  114.1 2.6 %place_rows.3 = bf16[8192,256]{1,0:T(8,128)(2,1)} custom-call(s32[4]{0:T(128)S(1)} %broadcast_xor_fusion.1.place, bf16[2048,256]{1,0:T(8,128)(2,1)} %collective-permute-done.12.refs_0_, bf16[2048,256]{1,0:T(8,128)(2,1)S(1)} %collective-permute-done.16.refs_1_, bf16[8192,256]{1,0:T(8,128)(2,1)} %place_rows.2.refs_2_), custom_call_target="tpu_custom_call", output_to_operand_aliasing={{}: (3, {})} | custom-call | bytes 4194304 | tf_op jit(solution)/shard_map/place_rows/pallas_call | solution.py:516
  116.7 2.7 %weight_keep.1 = (f32[2,1024,128]{2,1,0:T(8,128)S(1)}, f32[2,1024,128]{2,1,0:T(8,128)S(1)}) custom-call(s32[5]{0:T(128)S(1)} %stack.95.place, bf16[32,2048,256]{2,1,0:T(8,128)(2,1)} %get-tuple-element.108.held, bf16[4,1024,128]{2,1,0:T(8,128)(2,1)S(1)} %collective-permute-done.24.refs_0_), custom_call_target="tpu_custom_call" | custom-call | flops 268435456 | bytes 2097152 | tf_op jit(solution)/shard_map/weight_keep/pallas_call | solution.py:354
  119.4 3.8 %collective-permute-done.22.refs_2_ = bf16[256,256]{1,0:T(8,128)(2,1)S(1)} collective-permute-done((bf16[256,256]{1,0:T(8,128)(2,1)S(1)}, bf16[256,256]{1,0:T(8,128)(2,1)S(1)}, u32[]{:S(2)}, u32[]{:S(2)}) %collective-permute-start.22) | collective-permute-done | bytes 131104 | tf_op jit(solution)/shard_map/ppermute | solution.py:569
  124.4 3.9 %input_gradient.1 = bf16[256,2048]{1,0:T(8,128)(2,1)} custom-call(s32[8]{0:T(128)S(1)} %broadcast_xor_fusion.place, bf16[256,256]{1,0:T(8,128)(2,1)S(1)} %copy-done.3, bf16[256,256]{1,0:T(8,128)(2,1)S(1)} %collective-permute-done.21.refs_1_, bf16[256,256]{1,0:T(8,128)(2,1)S(1)} %collective-permute-done.22.refs_2_, ...), custom_call_target="tpu_custom_call" | custom-call | flops 1073741824 | bytes 6291456 | tf_op jit(solution)/shard_map/input_gradient/pallas_call | solution.py:73
  128.3 1.4 %collective-permute-done.25.last_a = bf16[1024,128]{1,0:T(8,128)(2,1)S(1)} collective-permute-done((bf16[1024,128]{1,0:T(8,128)(2,1)S(1)}, bf16[1024,128]{1,0:T(8,128)(2,1)S(1)}, u32[]{:S(2)}, u32[]{:S(2)}) %collective-permute-start.25) | collective-permute-done | bytes 262176 | tf_op jit(solution)/shard_map/ppermute | solution.py:398
  130.3 1.1 weight_finish.1
  (62 shorter events, 7.5 us)
Async XLA Ops:
  0.6 30.0 %collective-permute-start = (bf16[256,2048]{1,0:T(8,128)(2,1)}, bf16[256,2048]{1,0:T(8,128)(2,1)}, u32[]{:S(2)}, u32[]{:S(2)}) collective-permute-start(bf16[256,2048]{1,0:T(8,128)(2,1)} %refs_0_.1), channel_id=1, source_target_pairs={{1,0},{2,1},{3,2},{5,4},{6,5},{7,6},{9,8},{10,9},{11,10},{13,12},{... | collective-permute-start | bytes 3145736 | tf_op jit(solution)/shard_map/ppermute | solution.py:602
  1.9 29.4 %collective-permute-start.1 = (bf16[256,2048]{1,0:T(8,128)(2,1)}, bf16[256,2048]{1,0:T(8,128)(2,1)}, u32[]{:S(2)}, u32[]{:S(2)}) collective-permute-start(bf16[256,2048]{1,0:T(8,128)(2,1)} %refs_0_.1), channel_id=1, source_target_pairs={{0,1},{1,2},{2,3},{4,5},{5,6},{6,7},{8,9},{9,10},{10,11},{12,13},{... | collective-permute-start | bytes 3145736 | tf_op jit(solution)/shard_map/ppermute | solution.py:603
  9.6 24.7 %collective-permute-start.4 = (bf16[256,256]{1,0:T(8,128)(2,1)S(1)}, bf16[256,256]{1,0:T(8,128)(2,1)S(1)}, u32[]{:S(2)}, u32[]{:S(2)}) collective-permute-start(bf16[256,256]{1,0:T(8,128)(2,1)S(1)} %get-tuple-element.141), channel_id=1, source_target_pairs={{0,1},{1,0},{2,3},{3,2},{4,5},{5,4},{6,7},{7,6},{8,9},{9,8},{10,11... | collective-permute-start | bytes 393224 | tf_op jit(solution)/shard_map/ppermute | solution.py:569
  10.7 29.1 %collective-permute-start.5 = (bf16[256,256]{1,0:T(8,128)(2,1)S(1)}, bf16[256,256]{1,0:T(8,128)(2,1)S(1)}, u32[]{:S(2)}, u32[]{:S(2)}) collective-permute-start(bf16[256,256]{1,0:T(8,128)(2,1)S(1)} %get-tuple-element.140), channel_id=1, source_target_pairs={{0,2},{1,3},{2,0},{3,1},{4,6},{5,7},{6,4},{7,5},{8,10},{9,11},{10,... | collective-permute-start | bytes 393224 | tf_op jit(solution)/shard_map/ppermute | solution.py:569
  12.7 27.0 %collective-permute-start.6 = (bf16[256,256]{1,0:T(8,128)(2,1)S(1)}, bf16[256,256]{1,0:T(8,128)(2,1)S(1)}, u32[]{:S(2)}, u32[]{:S(2)}) collective-permute-start(bf16[256,256]{1,0:T(8,128)(2,1)S(1)} %get-tuple-element.139), channel_id=1, source_target_pairs={{0,3},{1,2},{2,1},{3,0},{4,7},{5,6},{6,5},{7,4},{8,11},{9,10},{10,... | collective-permute-start | bytes 393224 | tf_op jit(solution)/shard_map/ppermute | solution.py:569
  25.3 1.4 %copy-start.8 = (s32[1,256]{1,0:T(1,128)S(1)}, s32[1,256]{1,0:T(1,128)}, u32[]{:S(2)}) copy-start(s32[1,256]{1,0:T(1,128)} %param.15) | copy-start | bytes 3076
  25.3 15.2 %copy-start = (bf16[1024,256]{1,0:T(8,128)(2,1)S(1)}, bf16[1024,256]{1,0:T(8,128)(2,1)}, u32[]{:S(2)}) copy-start(bf16[1024,256]{1,0:T(8,128)(2,1)} %get-tuple-element.90.refs_0_) | copy-start | bytes 1572868
  31.4 28.8 %collective-permute-start.2 = (bf16[256,2048]{1,0:T(8,128)(2,1)}, bf16[256,2048]{1,0:T(8,128)(2,1)}, u32[]{:S(2)}, u32[]{:S(2)}) collective-permute-start(bf16[256,2048]{1,0:T(8,128)(2,1)} %collective-permute-done.refs_0_), channel_id=1, source_target_pairs={{1,0},{2,1},{5,4},{6,5},{9,8},{10,9},{13,12},{14,13},{17,16},{18,1... | collective-permute-start | bytes 3145736 | tf_op jit(solution)/shard_map/ppermute | solution.py:602
  32.7 27.5 %collective-permute-start.3 = (bf16[256,2048]{1,0:T(8,128)(2,1)}, bf16[256,2048]{1,0:T(8,128)(2,1)}, u32[]{:S(2)}, u32[]{:S(2)}) collective-permute-start(bf16[256,2048]{1,0:T(8,128)(2,1)} %collective-permute-done.1.refs_0_), channel_id=1, source_target_pairs={{1,2},{2,3},{5,6},{6,7},{9,10},{10,11},{13,14},{14,15},{17,18},{18... | collective-permute-start | bytes 3145736 | tf_op jit(solution)/shard_map/ppermute | solution.py:603
  39.8 3.2 %copy-start.4 = (bf16[256,256]{1,0:T(8,128)(2,1)}, bf16[256,256]{1,0:T(8,128)(2,1)S(1)}, u32[]{:S(2)}) copy-start(bf16[256,256]{1,0:T(8,128)(2,1)S(1)} %collective-permute-done.5) | copy-start | bytes 393220
  39.8 3.9 %copy-start.6 = (bf16[256,256]{1,0:T(8,128)(2,1)}, bf16[256,256]{1,0:T(8,128)(2,1)S(1)}, u32[]{:S(2)}) copy-start(bf16[256,256]{1,0:T(8,128)(2,1)S(1)} %collective-permute-done.6) | copy-start | bytes 393220
  40.5 15.6 %collective-permute-start.8 = (bf16[1024,256]{1,0:T(8,128)(2,1)S(1)}, bf16[1024,256]{1,0:T(8,128)(2,1)S(1)}, u32[]{:S(2)}, u32[]{:S(2)}) collective-permute-start(bf16[1024,256]{1,0:T(8,128)(2,1)S(1)} %copy-done), channel_id=1, source_target_pairs={{0,16},{4,20},{8,24},{12,28},{16,0},{20,4},{24,8},{28,12},{1,17},{... | collective-permute-start | bytes 1572872 | tf_op jit(solution)/shard_map/ppermute | solution.py:398
  43.6 14.4 %collective-permute-start.9 = (bf16[1792,256]{1,0:T(8,128)(2,1)}, bf16[1792,256]{1,0:T(8,128)(2,1)S(1)}, u32[]{:S(2)}, u32[]{:S(2)}) collective-permute-start(bf16[1792,256]{1,0:T(8,128)(2,1)} %pad_maximum_fusion.1), channel_id=1, source_target_pairs={{0,4},{4,0},{8,12},{12,8},{16,20},{20,16},{24,28},{28,24},{1,5},{5... | collective-permute-start | bytes 2752520 | tf_op jit(solution)/shard_map/ppermute | solution.py:398
  44.3 11.7 %collective-permute-start.7 = (bf16[768,256]{1,0:T(8,128)(2,1)}, bf16[768,256]{1,0:T(8,128)(2,1)S(1)}, u32[]{:S(2)}, u32[]{:S(2)}) collective-permute-start(bf16[768,256]{1,0:T(8,128)(2,1)} %constant_dynamic-update-slice_fusion.refs_5_), channel_id=1, source_target_pairs={{0,8},{4,12},{8,0},{12,4},{16,24},{20,28},{24,16},{28,20},{1,9},{5... | collective-permute-start | bytes 1179656 | tf_op jit(solution)/shard_map/ppermute | solution.py:398
  55.0 2.1 %copy-start.5 = (bf16[256,256]{1,0:T(8,128)(2,1)S(1)}, bf16[256,256]{1,0:T(8,128)(2,1)}, u32[]{:S(2)}) copy-start(bf16[256,256]{1,0:T(8,128)(2,1)} %copy-done.4) | copy-start | bytes 393220
  55.0 2.1 %copy-start.7 = (bf16[256,256]{1,0:T(8,128)(2,1)S(1)}, bf16[256,256]{1,0:T(8,128)(2,1)}, u32[]{:S(2)}) copy-start(bf16[256,256]{1,0:T(8,128)(2,1)} %copy-done.6) | copy-start | bytes 393220
  56.0 12.0 %copy-start.11 = (s32[4]{0:T(128)S(1)}, s32[4]{0:T(128)}, u32[]{:S(2)}) copy-start(s32[4]{0:T(128)} %constant.72.clone) | copy-start | bytes 52
  60.2 29.1 %collective-permute-start.10 = (bf16[256,2048]{1,0:T(8,128)(2,1)}, bf16[256,2048]{1,0:T(8,128)(2,1)}, u32[]{:S(2)}, u32[]{:S(2)}) collective-permute-start(bf16[256,2048]{1,0:T(8,128)(2,1)} %collective-permute-done.2.refs_1_), channel_id=1, source_target_pairs={{1,0},{5,4},{9,8},{13,12},{17,16},{21,20},{25,24},{29,28}} | collective-permute-start | bytes 3145736 | tf_op jit(solution)/shard_map/ppermute | solution.py:602
  61.5 27.8 %collective-permute-start.11 = (bf16[256,2048]{1,0:T(8,128)(2,1)}, bf16[256,2048]{1,0:T(8,128)(2,1)}, u32[]{:S(2)}, u32[]{:S(2)}) collective-permute-start(bf16[256,2048]{1,0:T(8,128)(2,1)} %collective-permute-done.3.refs_0_), channel_id=1, source_target_pairs={{2,3},{6,7},{10,11},{14,15},{18,19},{22,23},{26,27},{30,31}} | collective-permute-start | bytes 3145736 | tf_op jit(solution)/shard_map/ppermute | solution.py:603
  63.1 26.1 %collective-permute-start.12 = (bf16[2048,256]{1,0:T(8,128)(2,1)}, bf16[2048,256]{1,0:T(8,128)(2,1)}, u32[]{:S(2)}, u32[]{:S(2)}) collective-permute-start(bf16[2048,256]{1,0:T(8,128)(2,1)} %pad_maximum_fusion), channel_id=1, source_target_pairs={{0,8},{4,12},{8,0},{12,4},{16,24},{20,28},{24,16},{28,20},{1,9},{5... | collective-permute-start | bytes 3145736 | tf_op jit(solution)/shard_map/ppermute | solution.py:398
  64.5 1.9 %collective-permute-start.15 = (bf16[1024,256]{1,0:T(8,128)(2,1)S(1)}, bf16[1024,256]{1,0:T(8,128)(2,1)S(1)}, u32[]{:S(2)}, u32[]{:S(2)}) collective-permute-start(bf16[1024,256]{1,0:T(8,128)(2,1)S(1)} %collective-permute-done.8.refs_2_), channel_id=1, source_target_pairs={{0,4},{4,0},{8,12},{12,8},{16,20},{20,16},{24,28},{28,24},{1,5},{5... | collective-permute-start | bytes 1572872 | tf_op jit(solution)/shard_map/ppermute | solution.py:398
  64.5 20.3 %collective-permute-start.13 = (bf16[1536,256]{1,0:T(8,128)(2,1)}, bf16[1536,256]{1,0:T(8,128)(2,1)}, u32[]{:S(2)}, u32[]{:S(2)}) collective-permute-start(bf16[1536,256]{1,0:T(8,128)(2,1)} %pad_maximum_fusion.2), channel_id=1, source_target_pairs={{0,16},{4,20},{8,24},{12,28},{16,0},{20,4},{24,8},{28,12},{1,17},{... | collective-permute-start | bytes 2359304 | tf_op jit(solution)/shard_map/ppermute | solution.py:398
  66.4 0.8 copy-start.1
  67.2 7.0 %collective-permute-start.14 = (bf16[768,256]{1,0:T(8,128)(2,1)S(1)}, bf16[768,256]{1,0:T(8,128)(2,1)}, u32[]{:S(2)}, u32[]{:S(2)}) collective-permute-start(bf16[768,256]{1,0:T(8,128)(2,1)S(1)} %collective-permute-done.7.refs_7_), channel_id=1, source_target_pairs={{0,4},{4,0},{8,12},{12,8},{16,20},{20,16},{24,28},{28,24},{1,5},{5... | collective-permute-start | bytes 1179656 | tf_op jit(solution)/shard_map/ppermute | solution.py:398
  68.0 4.3 %copy-start.2 = (bf16[1024,256]{1,0:T(8,128)(2,1)S(1)}, bf16[1024,256]{1,0:T(8,128)(2,1)}, u32[]{:S(2)}) copy-start(bf16[1024,256]{1,0:T(8,128)(2,1)} %copy-done.1) | copy-start | bytes 1572868
  89.3 10.6 %collective-permute-start.16 = (bf16[2048,256]{1,0:T(8,128)(2,1)}, bf16[2048,256]{1,0:T(8,128)(2,1)S(1)}, u32[]{:S(2)}, u32[]{:S(2)}) collective-permute-start(bf16[2048,256]{1,0:T(8,128)(2,1)} %collective-permute-done.12.refs_0_), channel_id=1, source_target_pairs={{0,4},{4,0},{8,12},{12,8},{16,20},{20,16},{24,28},{28,24},{1,5},{5... | collective-permute-start | bytes 3145736 | tf_op jit(solution)/shard_map/ppermute | solution.py:398
  89.3 10.6 %collective-permute-start.17 = (bf16[1536,256]{1,0:T(8,128)(2,1)}, bf16[1536,256]{1,0:T(8,128)(2,1)}, u32[]{:S(2)}, u32[]{:S(2)}) collective-permute-start(bf16[1536,256]{1,0:T(8,128)(2,1)} %collective-permute-done.13.refs_9_), channel_id=1, source_target_pairs={{0,4},{4,0},{8,12},{12,8},{16,20},{20,16},{24,28},{28,24},{1,5},{5... | collective-permute-start | bytes 2359304 | tf_op jit(solution)/shard_map/ppermute | solution.py:398
  99.8 3.3 %collective-permute-start.18 = (bf16[4,1024,128]{2,1,0:T(8,128)(2,1)}, bf16[4,1024,128]{2,1,0:T(8,128)(2,1)S(1)}, u32[]{:S(2)}, u32[]{:S(2)}) collective-permute-start(bf16[4,1024,128]{2,1,0:T(8,128)(2,1)} %get-tuple-element.114), channel_id=1, source_target_pairs={{0,4},{4,0},{8,12},{12,8},{16,20},{20,16},{24,28},{28,24},{1,5},{5... | collective-permute-start | bytes 3145736 | tf_op jit(solution)/shard_map/ppermute | solution.py:398
  100.0 12.7 %collective-permute-start.24 = (bf16[4,1024,128]{2,1,0:T(8,128)(2,1)}, bf16[4,1024,128]{2,1,0:T(8,128)(2,1)S(1)}, u32[]{:S(2)}, u32[]{:S(2)}) collective-permute-start(bf16[4,1024,128]{2,1,0:T(8,128)(2,1)} %get-tuple-element.121), channel_id=1, source_target_pairs={{0,4},{4,0},{8,12},{12,8},{16,20},{20,16},{24,28},{28,24},{1,5},{5... | collective-permute-start | bytes 3145736 | tf_op jit(solution)/shard_map/ppermute | solution.py:398
  103.1 3.3 %copy-start.3 = (bf16[256,256]{1,0:T(8,128)(2,1)S(1)}, bf16[256,256]{1,0:T(8,128)(2,1)}, u32[]{:S(2)}) copy-start(bf16[256,256]{1,0:T(8,128)(2,1)} %get-tuple-element.128.refs_0_) | copy-start | bytes 393220
  103.1 11.0 %copy-start.10 = (s32[4]{0:T(128)S(1)}, s32[4]{0:T(128)}, u32[]{:S(2)}) copy-start(s32[4]{0:T(128)} %constant.73.clone) | copy-start | bytes 52
  103.3 19.9 %collective-permute-start.19 = (bf16[2,1024,128]{2,1,0:T(8,128)(2,1)S(1)}, bf16[2,1024,128]{2,1,0:T(8,128)(2,1)S(1)}, u32[]{:S(2)}, u32[]{:S(2)}) collective-permute-start(bf16[2,1024,128]{2,1,0:T(8,128)(2,1)S(1)} %get-tuple-element.115), channel_id=1, source_target_pairs={{0,8},{4,12},{8,0},{12,4},{16,24},{20,28},{24,16},{28,20},{1,9},{5... | collective-permute-start | bytes 1572872 | tf_op jit(solution)/shard_map/ppermute | solution.py:398
  104.9 18.4 %collective-permute-start.20 = (bf16[2,1024,128]{2,1,0:T(8,128)(2,1)S(1)}, bf16[2,1024,128]{2,1,0:T(8,128)(2,1)S(1)}, u32[]{:S(2)}, u32[]{:S(2)}) collective-permute-start(bf16[2,1024,128]{2,1,0:T(8,128)(2,1)S(1)} %get-tuple-element.116), channel_id=1, source_target_pairs={{0,16},{4,20},{8,24},{12,28},{16,0},{20,4},{24,8},{28,12},{1,17},{... | collective-permute-start | bytes 1572872 | tf_op jit(solution)/shard_map/ppermute | solution.py:398
  106.4 13.1 %collective-permute-start.21 = (bf16[256,256]{1,0:T(8,128)(2,1)S(1)}, bf16[256,256]{1,0:T(8,128)(2,1)S(1)}, u32[]{:S(2)}, u32[]{:S(2)}) collective-permute-start(bf16[256,256]{1,0:T(8,128)(2,1)S(1)} %copy-done.3), channel_id=1, source_target_pairs={{0,1},{1,0},{2,3},{3,2},{4,5},{5,4},{6,7},{7,6},{8,9},{9,8},{10,11... | collective-permute-start | bytes 393224 | tf_op jit(solution)/shard_map/ppermute | solution.py:569
  110.7 12.5 %collective-permute-start.22 = (bf16[256,256]{1,0:T(8,128)(2,1)S(1)}, bf16[256,256]{1,0:T(8,128)(2,1)S(1)}, u32[]{:S(2)}, u32[]{:S(2)}) collective-permute-start(bf16[256,256]{1,0:T(8,128)(2,1)S(1)} %copy-done.3), channel_id=1, source_target_pairs={{0,2},{1,3},{2,0},{3,1},{4,6},{5,7},{6,4},{7,5},{8,10},{9,11},{10,... | collective-permute-start | bytes 393224 | tf_op jit(solution)/shard_map/ppermute | solution.py:569
  112.7 10.6 %collective-permute-start.23 = (bf16[256,256]{1,0:T(8,128)(2,1)S(1)}, bf16[256,256]{1,0:T(8,128)(2,1)S(1)}, u32[]{:S(2)}, u32[]{:S(2)}) collective-permute-start(bf16[256,256]{1,0:T(8,128)(2,1)S(1)} %copy-done.3), channel_id=1, source_target_pairs={{0,3},{1,2},{2,1},{3,0},{4,7},{5,6},{6,5},{7,4},{8,11},{9,10},{10,... | collective-permute-start | bytes 393224 | tf_op jit(solution)/shard_map/ppermute | solution.py:569
  119.4 5.0 %copy-start.9 = (s32[8]{0:T(128)S(1)}, s32[8]{0:T(128)}, u32[]{:S(2)}) copy-start(s32[8]{0:T(128)} %constant.74.clone) | copy-start | bytes 100
  123.4 6.4 %collective-permute-start.25 = (bf16[1024,128]{1,0:T(8,128)(2,1)S(1)}, bf16[1024,128]{1,0:T(8,128)(2,1)S(1)}, u32[]{:S(2)}, u32[]{:S(2)}) collective-permute-start(bf16[1024,128]{1,0:T(8,128)(2,1)S(1)} %get-tuple-element.126), channel_id=1, source_target_pairs={{0,16},{4,20},{8,24},{12,28},{16,0},{20,4},{24,8},{28,12},{1,17},{... | collective-permute-start | bytes 786440 | tf_op jit(solution)/shard_map/ppermute | solution.py:398
  123.9 6.4 %collective-permute-start.26 = (bf16[1024,128]{1,0:T(8,128)(2,1)S(1)}, bf16[1024,128]{1,0:T(8,128)(2,1)S(1)}, u32[]{:S(2)}, u32[]{:S(2)}) collective-permute-start(bf16[1024,128]{1,0:T(8,128)(2,1)S(1)} %get-tuple-element.127), channel_id=1, source_target_pairs={{0,8},{4,12},{8,0},{12,4},{16,24},{20,28},{24,16},{28,20},{1,9},{5... | collective-permute-start | bytes 786440 | tf_op jit(solution)/shard_map/ppermute | solution.py:398

commit v19 on v17

--- a/solution.py
+++ b/solution.py
@@ -177,13 +177,13 @@
     for copy in others:
         copy.start()
     chunk_copy.wait()
-    turned[...] = chunk[...].T
-    keep = pltpu.make_async_copy(turned, held.at[place[1]], sems.at[2])
-    keep.start()
     rows_copy.wait()
     projected = (
         total[...] + jnp.dot(chunk[...], rows[...], preferred_element_type=jnp.float32)
     ).astype(jnp.bfloat16)
+    turned[...] = chunk[...].T
+    keep = pltpu.make_async_copy(turned, held.at[place[1]], sems.at[2])
+    keep.start()
     seen = allowed[...] > 0
     for copy in others:
         copy.wait()

time: 132 us -> 132 us (level)
  no operation moved by 1% of the time
where the time goes in v19:
time: 132 us; the launch traced here: 131 us
  Pallas kernels  47 us (36%)
  starting transfers between devices  37.3 us (28%)
  waiting for transfers between devices  33.8 us (26%)
  local copies, waits for them, and re-layouts  6.68 us (5%)
  other arithmetic  5.69 us (4%)
    pallas_call x4, Pallas kernels, absorb(): pl.pallas_call(functools.partial(absorb_kernel, len(chunks)), in_specs=[p...  17 us
    ppermute x15, waiting for transfers between devices, swap(): return lax.ppermute(value, 'dp', [(i, i ^ bit) for i in range(8)])  14 us
    ppermute x6, starting transfers between devices, pair(): return lax.ppermute(value, 'tensor', [(z, z ^ s) for z in range(n_z)])  12.3 us
    ppermute x15, starting transfers between devices, swap(): return lax.ppermute(value, 'dp', [(i, i ^ bit) for i in range(8)])  11.3 us
    pallas_call x1, Pallas kernels, attend(): pl.pallas_call(functools.partial(attend_kernel, len(chunks)), in_specs=[p...  10 us
    ppermute x3, starting transfers between devices, body(): lax.ppermute(from_low, 'tensor', [(z, z + 1) for z in range(s - 1, n_z -...  9.86 us
    ppermute x3, waiting for transfers between devices, body(): lax.ppermute(from_high, 'tensor', [(z + 1, z) for z in range(n_z - s)])  9.8 us
    ppermute x6, waiting for transfers between devices, pair(): return lax.ppermute(value, 'tensor', [(z, z ^ s) for z in range(n_z)])  9.28 us
  transfers between devices with their start and end apart: 27, of which 11 were waited for; matrix products, arithmetic and copies ran while one was open for 9% of the time, Pallas kernels for 35%

profile of v19, /device:TPU:0, one launch (start us, length us, event | category | flops | bytes accessed | tf_op | source)
XLA Modules:
  0.0 131.3 jit_solution(14076698704920308178)
XLA Ops:
  0.6 1.3 collective-permute-start
  1.9 6.6 %collective-permute-start.1 = (bf16[256,2048]{1,0:T(8,128)(2,1)}, bf16[256,2048]{1,0:T(8,128)(2,1)}, u32[]{:S(2)}, u32[]{:S(2)}) collective-permute-start(bf16[256,2048]{1,0:T(8,128)(2,1)} %refs_0_.1), channel_id=1, source_target_pairs={{0,1},{1,2},{2,3},{4,5},{5,6},{6,7},{8,9},{9,10},{10,11},{12,13},{... | collective-permute-start | bytes 3145736 | tf_op jit(solution)/shard_map/ppermute | solution.py:603
  8.5 1.1 constant_dynamic-slice_fusion
  9.6 1.1 collective-permute-start.4
  10.7 2.0 %collective-permute-start.5 = (bf16[256,256]{1,0:T(8,128)(2,1)S(1)}, bf16[256,256]{1,0:T(8,128)(2,1)S(1)}, u32[]{:S(2)}, u32[]{:S(2)}) collective-permute-start(bf16[256,256]{1,0:T(8,128)(2,1)S(1)} %get-tuple-element.140), channel_id=1, source_target_pairs={{0,2},{1,3},{2,0},{3,1},{4,6},{5,7},{6,4},{7,5},{8,10},{9,11},{10,... | collective-permute-start | bytes 393224 | tf_op jit(solution)/shard_map/ppermute | solution.py:569
  12.7 1.4 %collective-permute-start.6 = (bf16[256,256]{1,0:T(8,128)(2,1)S(1)}, bf16[256,256]{1,0:T(8,128)(2,1)S(1)}, u32[]{:S(2)}, u32[]{:S(2)}) collective-permute-start(bf16[256,256]{1,0:T(8,128)(2,1)S(1)} %get-tuple-element.139), channel_id=1, source_target_pairs={{0,3},{1,2},{2,1},{3,0},{4,7},{5,6},{6,5},{7,4},{8,11},{9,10},{10,... | collective-permute-start | bytes 393224 | tf_op jit(solution)/shard_map/ppermute | solution.py:569
  14.8 4.9 %optimizer.1 = (f32[1024,256]{1,0:T(8,128)}, f32[1024,256]{1,0:T(8,128)}, f32[1024,256]{1,0:T(8,128)}, bf16[1024,256]{1,0:T(8,128)(2,1)}) custom-call(s32[1]{0:T(128)} %bitcast.place, bf16[8192,256]{1,0:T(8,128)(2,1)} %refs_3_.3, f32[1024,256]{1,0:T(8,128)} %master.1, f32[1024,256]{1,0:T(8,128)} %moment.1, f32[1024,256]{1,0:T(8,128)} %second.1, f32[1024,256]{1,0:T(8,128)} %grad.1), custom_call_target="tpu_custom_call" | custom-call | flops 10485760 | bytes 8388608 | tf_op jit(solution)/shard_map/optimizer/pallas_call | solution.py:51
  20.3 0.7 broadcast_in_dim.2.refs_1_
  21.0 4.2 %absorb.4 = (f32[256,256]{1,0:T(8,128)}, bf16[32,2048,256]{2,1,0:T(8,128)(2,1)}) custom-call(s32[3]{0:T(128)} %get-tuple-element.144.place, bf16[256,2048]{1,0:T(8,128)(2,1)} %refs_0_.1, f32[256,256]{1,0:T(8,128)} %broadcast_in_dim.2.refs_1_, bf16[8192,256]{1,0:T(8,128)(2,1)} %refs_3_.3), custom_call_target="tpu_custom_call" | custom-call | flops 268435456 | bytes 3145728 | tf_op jit(solution)/shard_map/absorb/pallas_call | solution.py:140
  25.3 1.4 %constant_dynamic-slice_fusion.3.refs_4_ = bf16[2048,256]{1,0:T(8,128)(2,1)S(1)} fusion(bf16[8192,256]{1,0:T(8,128)(2,1)} %refs_3_.3, s32[]{:T(128)S(6)} %select_n.57), kind=kLoop, calls=%fused_computation.12 | loop fusion | bytes 2097156 | tf_op jit(solution)/shard_map/dynamic_slice | solution.py:588
  26.7 0.8 fusion.1.refs_5_
  27.5 3.2 %collective-permute-done.refs_0_ = bf16[256,2048]{1,0:T(8,128)(2,1)} collective-permute-done((bf16[256,2048]{1,0:T(8,128)(2,1)}, bf16[256,2048]{1,0:T(8,128)(2,1)}, u32[]{:S(2)}, u32[]{:S(2)}) %collective-permute-start) | collective-permute-done | bytes 1048608 | tf_op jit(solution)/shard_map/ppermute | solution.py:602
  30.7 0.7 collective-permute-done.1.refs_0_
  31.4 1.3 collective-permute-start.2
  32.7 1.6 %collective-permute-start.3 = (bf16[256,2048]{1,0:T(8,128)(2,1)}, bf16[256,2048]{1,0:T(8,128)(2,1)}, u32[]{:S(2)}, u32[]{:S(2)}) collective-permute-start(bf16[256,2048]{1,0:T(8,128)(2,1)} %collective-permute-done.1.refs_0_), channel_id=1, source_target_pairs={{1,2},{2,3},{5,6},{6,7},{9,10},{10,11},{13,14},{14,15},{17,18},{18... | collective-permute-start | bytes 3145736 | tf_op jit(solution)/shard_map/ppermute | solution.py:603
  34.3 5.5 %collective-permute-done.5 = bf16[256,256]{1,0:T(8,128)(2,1)S(1)} collective-permute-done((bf16[256,256]{1,0:T(8,128)(2,1)S(1)}, bf16[256,256]{1,0:T(8,128)(2,1)S(1)}, u32[]{:S(2)}, u32[]{:S(2)}) %collective-permute-start.5) | collective-permute-done | bytes 131104 | tf_op jit(solution)/shard_map/ppermute | solution.py:569
  39.8 0.7 constant_dynamic-update-slice_fusion.2
  40.5 1.5 %collective-permute-start.8 = (bf16[1024,256]{1,0:T(8,128)(2,1)S(1)}, bf16[1024,256]{1,0:T(8,128)(2,1)S(1)}, u32[]{:S(2)}, u32[]{:S(2)}) collective-permute-start(bf16[1024,256]{1,0:T(8,128)(2,1)S(1)} %copy-done), channel_id=1, source_target_pairs={{0,16},{4,20},{8,24},{12,28},{16,0},{20,4},{24,8},{28,12},{1,17},{... | collective-permute-start | bytes 1572872 | tf_op jit(solution)/shard_map/ppermute | solution.py:398
  42.0 1.0 pad_maximum_fusion.1
  44.3 1.5 %collective-permute-start.7 = (bf16[768,256]{1,0:T(8,128)(2,1)}, bf16[768,256]{1,0:T(8,128)(2,1)S(1)}, u32[]{:S(2)}, u32[]{:S(2)}) collective-permute-start(bf16[768,256]{1,0:T(8,128)(2,1)} %constant_dynamic-update-slice_fusion.refs_5_), channel_id=1, source_target_pairs={{0,8},{4,12},{8,0},{12,4},{16,24},{20,28},{24,16},{28,20},{1,9},{5... | collective-permute-start | bytes 1179656 | tf_op jit(solution)/shard_map/ppermute | solution.py:398
  46.5 4.2 %absorb.5 = (f32[256,256]{1,0:T(8,128)}, bf16[32,2048,256]{2,1,0:T(8,128)(2,1)}) custom-call(s32[3]{0:T(128)} %get-tuple-element.142.place, bf16[256,2048]{1,0:T(8,128)(2,1)} %collective-permute-done.1.refs_0_, f32[256,256]{1,0:T(8,128)} %get-tuple-element.81.refs_1_, bf16[8192,256]{1,0:T(8,128)(2,1)} %refs_3_.3, ...), custom_call_target="tpu_custom_call", output_to_operand_aliasing={{1}: (4, {})} | custom-call | flops 268435456 | bytes 3145728 | tf_op jit(solution)/shard_map/absorb/pallas_call | solution.py:140
  50.7 4.2 %absorb.6 = (f32[256,256]{1,0:T(8,128)}, bf16[32,2048,256]{2,1,0:T(8,128)(2,1)}) custom-call(s32[3]{0:T(128)} %get-tuple-element.143.place, bf16[256,2048]{1,0:T(8,128)(2,1)} %collective-permute-done.refs_0_, f32[256,256]{1,0:T(8,128)} %get-tuple-element.83.refs_1_, bf16[8192,256]{1,0:T(8,128)(2,1)} %refs_3_.3, ...), custom_call_target="tpu_custom_call", output_to_operand_aliasing={{1}: (4, {})} | custom-call | flops 268435456 | bytes 3145728 | tf_op jit(solution)/shard_map/absorb/pallas_call | solution.py:140
  55.0 1.1 collective-permute-done.7.refs_7_
  56.0 1.0 pad_maximum_fusion
  57.1 0.9 pad_maximum_fusion.2
  58.0 2.2 %collective-permute-done.2.refs_1_ = bf16[256,2048]{1,0:T(8,128)(2,1)} collective-permute-done((bf16[256,2048]{1,0:T(8,128)(2,1)}, bf16[256,2048]{1,0:T(8,128)(2,1)}, u32[]{:S(2)}, u32[]{:S(2)}) %collective-permute-start.2) | collective-permute-done | bytes 1048608 | tf_op jit(solution)/shard_map/ppermute | solution.py:602
  60.2 1.3 collective-permute-start.10
  61.5 1.6 %collective-permute-start.11 = (bf16[256,2048]{1,0:T(8,128)(2,1)}, bf16[256,2048]{1,0:T(8,128)(2,1)}, u32[]{:S(2)}, u32[]{:S(2)}) collective-permute-start(bf16[256,2048]{1,0:T(8,128)(2,1)} %collective-permute-done.3.refs_0_), channel_id=1, source_target_pairs={{2,3},{6,7},{10,11},{14,15},{18,19},{22,23},{26,27},{30,31}} | collective-permute-start | bytes 3145736 | tf_op jit(solution)/shard_map/ppermute | solution.py:603
  63.1 1.4 %collective-permute-start.12 = (bf16[2048,256]{1,0:T(8,128)(2,1)}, bf16[2048,256]{1,0:T(8,128)(2,1)}, u32[]{:S(2)}, u32[]{:S(2)}) collective-permute-start(bf16[2048,256]{1,0:T(8,128)(2,1)} %pad_maximum_fusion), channel_id=1, source_target_pairs={{0,8},{4,12},{8,0},{12,4},{16,24},{20,28},{24,16},{28,20},{1,9},{5... | collective-permute-start | bytes 3145736 | tf_op jit(solution)/shard_map/ppermute | solution.py:398
  64.5 1.5 %collective-permute-start.13 = (bf16[1536,256]{1,0:T(8,128)(2,1)}, bf16[1536,256]{1,0:T(8,128)(2,1)}, u32[]{:S(2)}, u32[]{:S(2)}) collective-permute-start(bf16[1536,256]{1,0:T(8,128)(2,1)} %pad_maximum_fusion.2), channel_id=1, source_target_pairs={{0,16},{4,20},{8,24},{12,28},{16,0},{20,4},{24,8},{28,12},{1,17},{... | collective-permute-start | bytes 2359304 | tf_op jit(solution)/shard_map/ppermute | solution.py:398
  66.4 0.8 copy-done.1
  68.0 4.3 %absorb.7 = (f32[256,256]{1,0:T(8,128)}, bf16[32,2048,256]{2,1,0:T(8,128)(2,1)}) custom-call(s32[3]{0:T(128)} %pad_add_fusion.4.place, bf16[256,2048]{1,0:T(8,128)(2,1)} %collective-permute-done.3.refs_0_, bf16[256,2048]{1,0:T(8,128)(2,1)} %collective-permute-done.2.refs_1_, f32[256,256]{1,0:T(8,128)} %get-tuple-element.95.refs_2_, ...), custom_call_target="tpu_custom_call", output_to_operand_aliasing={{1}: (5, {})} | custom-call | flops 268435456 | bytes 3145728 | tf_op jit(solution)/shard_map/absorb/pallas_call | solution.py:140
  72.3 1.9 %place_rows.2.refs_2_ = bf16[8192,256]{1,0:T(8,128)(2,1)} custom-call(s32[4]{0:T(128)S(1)} %broadcast_xor_fusion.2.place, bf16[1024,256]{1,0:T(8,128)(2,1)S(1)} %copy-done, bf16[1792,256]{1,0:T(8,128)(2,1)S(1)} %collective-permute-done.9.refs_1_.refs_6_, bf16[1024,256]{1,0:T(8,128)(2,1)S(1)} %collective-permute-done.8.refs_2_, bf16[1024,256]{1,0:T(8,128)(2,1)S(1)} %copy-done.2), custom_call_target="tpu_custom_call" | custom-call | bytes 4194304 | tf_op jit(solution)/shard_map/place_rows/pallas_call | solution.py:516
  74.2 10.6 %collective-permute-done.13.refs_9_ = bf16[1536,256]{1,0:T(8,128)(2,1)} collective-permute-done((bf16[1536,256]{1,0:T(8,128)(2,1)}, bf16[1536,256]{1,0:T(8,128)(2,1)}, u32[]{:S(2)}, u32[]{:S(2)}) %collective-permute-start.13) | collective-permute-done | bytes 786464 | tf_op jit(solution)/shard_map/ppermute | solution.py:398
  84.8 4.5 %collective-permute-done.10.refs_1_ = bf16[256,2048]{1,0:T(8,128)(2,1)} collective-permute-done((bf16[256,2048]{1,0:T(8,128)(2,1)}, bf16[256,2048]{1,0:T(8,128)(2,1)}, u32[]{:S(2)}, u32[]{:S(2)}) %collective-permute-start.10) | collective-permute-done | bytes 1048608 | tf_op jit(solution)/shard_map/ppermute | solution.py:602
  89.8 10.0 %attend.1 = (bf16[32,2048,256]{2,1,0:T(8,128)(2,1)}, bf16[256,1024]{1,0:T(8,128)(2,1)}, bf16[256,256]{1,0:T(8,128)(2,1)}, bf16[4,1024,128]{2,1,0:T(8,128)(2,1)}, bf16[4,1024,128]{2,1,0:T(8,128)(2,1)}) custom-call(s32[3]{0:T(128)} %get-tuple-element.145.place, s32[5]{0:T(128)} %stack.93.order, ...), custom_call_target="tpu_custom_call", output_to_operand_aliasing={{0}: (6, {})} | custom-call | flops 805306368 | bytes 2097152 | tf_op jit(solution)/shard_map/attend/pallas_call | solution.py:245
  100.4 2.7 %weight_send.1 = (f32[2,1024,128]{2,1,0:T(8,128)S(1)}, f32[2,1024,128]{2,1,0:T(8,128)S(1)}) custom-call(s32[5]{0:T(128)S(1)} %stack.95.place, bf16[32,2048,256]{2,1,0:T(8,128)(2,1)} %get-tuple-element.108.held), custom_call_target="tpu_custom_call" | custom-call | flops 268435456 | bytes 2097152 | tf_op jit(solution)/shard_map/weight_send/pallas_call | solution.py:354
  103.3 1.5 %collective-permute-start.19 = (bf16[2,1024,128]{2,1,0:T(8,128)(2,1)S(1)}, bf16[2,1024,128]{2,1,0:T(8,128)(2,1)S(1)}, u32[]{:S(2)}, u32[]{:S(2)}) collective-permute-start(bf16[2,1024,128]{2,1,0:T(8,128)(2,1)S(1)} %get-tuple-element.115), channel_id=1, source_target_pairs={{0,8},{4,12},{8,0},{12,4},{16,24},{20,28},{24,16},{28,20},{1,9},{5... | collective-permute-start | bytes 1572872 | tf_op jit(solution)/shard_map/ppermute | solution.py:398
  104.8 1.5 %collective-permute-start.20 = (bf16[2,1024,128]{2,1,0:T(8,128)(2,1)S(1)}, bf16[2,1024,128]{2,1,0:T(8,128)(2,1)S(1)}, u32[]{:S(2)}, u32[]{:S(2)}) collective-permute-start(bf16[2,1024,128]{2,1,0:T(8,128)(2,1)S(1)} %get-tuple-element.116), channel_id=1, source_target_pairs={{0,16},{4,20},{8,24},{12,28},{16,0},{20,4},{24,8},{28,12},{1,17},{... | collective-permute-start | bytes 1572872 | tf_op jit(solution)/shard_map/ppermute | solution.py:398
  106.3 4.3 %collective-permute-start.21 = (bf16[256,256]{1,0:T(8,128)(2,1)S(1)}, bf16[256,256]{1,0:T(8,128)(2,1)S(1)}, u32[]{:S(2)}, u32[]{:S(2)}) collective-permute-start(bf16[256,256]{1,0:T(8,128)(2,1)S(1)} %copy-done.3), channel_id=1, source_target_pairs={{0,1},{1,0},{2,3},{3,2},{4,5},{5,4},{6,7},{7,6},{8,9},{9,8},{10,11... | collective-permute-start | bytes 393224 | tf_op jit(solution)/shard_map/ppermute | solution.py:569
  110.7 1.9 %collective-permute-start.22 = (bf16[256,256]{1,0:T(8,128)(2,1)S(1)}, bf16[256,256]{1,0:T(8,128)(2,1)S(1)}, u32[]{:S(2)}, u32[]{:S(2)}) collective-permute-start(bf16[256,256]{1,0:T(8,128)(2,1)S(1)} %copy-done.3), channel_id=1, source_target_pairs={{0,2},{1,3},{2,0},{3,1},{4,6},{5,7},{6,4},{7,5},{8,10},{9,11},{10,... | collective-permute-start | bytes 393224 | tf_op jit(solution)/shard_map/ppermute | solution.py:569
  112.6 1.5 %collective-permute-start.23 = (bf16[256,256]{1,0:T(8,128)(2,1)S(1)}, bf16[256,256]{1,0:T(8,128)(2,1)S(1)}, u32[]{:S(2)}, u32[]{:S(2)}) collective-permute-start(bf16[256,256]{1,0:T(8,128)(2,1)S(1)} %copy-done.3), channel_id=1, source_target_pairs={{0,3},{1,2},{2,1},{3,0},{4,7},{5,6},{6,5},{7,4},{8,11},{9,10},{10,... | collective-permute-start | bytes 393224 | tf_op jit(solution)/shard_map/ppermute | solution.py:569
  114.1 2.6 %place_rows.3 = bf16[8192,256]{1,0:T(8,128)(2,1)} custom-call(s32[4]{0:T(128)S(1)} %broadcast_xor_fusion.1.place, bf16[2048,256]{1,0:T(8,128)(2,1)} %collective-permute-done.12.refs_0_, bf16[2048,256]{1,0:T(8,128)(2,1)S(1)} %collective-permute-done.16.refs_1_, bf16[8192,256]{1,0:T(8,128)(2,1)} %place_rows.2.refs_2_), custom_call_target="tpu_custom_call", output_to_operand_aliasing={{}: (3, {})} | custom-call | bytes 4194304 | tf_op jit(solution)/shard_map/place_rows/pallas_call | solution.py:516
  116.7 2.7 %weight_keep.1 = (f32[2,1024,128]{2,1,0:T(8,128)S(1)}, f32[2,1024,128]{2,1,0:T(8,128)S(1)}) custom-call(s32[5]{0:T(128)S(1)} %stack.95.place, bf16[32,2048,256]{2,1,0:T(8,128)(2,1)} %get-tuple-element.108.held, bf16[4,1024,128]{2,1,0:T(8,128)(2,1)S(1)} %collective-permute-done.24.refs_0_), custom_call_target="tpu_custom_call" | custom-call | flops 268435456 | bytes 2097152 | tf_op jit(solution)/shard_map/weight_keep/pallas_call | solution.py:354
  119.4 3.8 %collective-permute-done.22.refs_2_ = bf16[256,256]{1,0:T(8,128)(2,1)S(1)} collective-permute-done((bf16[256,256]{1,0:T(8,128)(2,1)S(1)}, bf16[256,256]{1,0:T(8,128)(2,1)S(1)}, u32[]{:S(2)}, u32[]{:S(2)}) %collective-permute-start.22) | collective-permute-done | bytes 131104 | tf_op jit(solution)/shard_map/ppermute | solution.py:569
  124.4 3.9 %input_gradient.1 = bf16[256,2048]{1,0:T(8,128)(2,1)} custom-call(s32[8]{0:T(128)S(1)} %broadcast_xor_fusion.place, bf16[256,256]{1,0:T(8,128)(2,1)S(1)} %copy-done.3, bf16[256,256]{1,0:T(8,128)(2,1)S(1)} %collective-permute-done.21.refs_1_, bf16[256,256]{1,0:T(8,128)(2,1)S(1)} %collective-permute-done.22.refs_2_, ...), custom_call_target="tpu_custom_call" | custom-call | flops 1073741824 | bytes 6291456 | tf_op jit(solution)/shard_map/input_gradient/pallas_call | solution.py:73
  128.3 1.4 %collective-permute-done.25.last_a = bf16[1024,128]{1,0:T(8,128)(2,1)S(1)} collective-permute-done((bf16[1024,128]{1,0:T(8,128)(2,1)S(1)}, bf16[1024,128]{1,0:T(8,128)(2,1)S(1)}, u32[]{:S(2)}, u32[]{:S(2)}) %collective-permute-start.25) | collective-permute-done | bytes 262176 | tf_op jit(solution)/shard_map/ppermute | solution.py:398
  130.2 1.1 weight_finish.1
  (62 shorter events, 7.5 us)
Async XLA Ops:
  0.6 30.0 %collective-permute-start = (bf16[256,2048]{1,0:T(8,128)(2,1)}, bf16[256,2048]{1,0:T(8,128)(2,1)}, u32[]{:S(2)}, u32[]{:S(2)}) collective-permute-start(bf16[256,2048]{1,0:T(8,128)(2,1)} %refs_0_.1), channel_id=1, source_target_pairs={{1,0},{2,1},{3,2},{5,4},{6,5},{7,6},{9,8},{10,9},{11,10},{13,12},{... | collective-permute-start | bytes 3145736 | tf_op jit(solution)/shard_map/ppermute | solution.py:602
  1.9 29.4 %collective-permute-start.1 = (bf16[256,2048]{1,0:T(8,128)(2,1)}, bf16[256,2048]{1,0:T(8,128)(2,1)}, u32[]{:S(2)}, u32[]{:S(2)}) collective-permute-start(bf16[256,2048]{1,0:T(8,128)(2,1)} %refs_0_.1), channel_id=1, source_target_pairs={{0,1},{1,2},{2,3},{4,5},{5,6},{6,7},{8,9},{9,10},{10,11},{12,13},{... | collective-permute-start | bytes 3145736 | tf_op jit(solution)/shard_map/ppermute | solution.py:603
  9.6 24.7 %collective-permute-start.4 = (bf16[256,256]{1,0:T(8,128)(2,1)S(1)}, bf16[256,256]{1,0:T(8,128)(2,1)S(1)}, u32[]{:S(2)}, u32[]{:S(2)}) collective-permute-start(bf16[256,256]{1,0:T(8,128)(2,1)S(1)} %get-tuple-element.141), channel_id=1, source_target_pairs={{0,1},{1,0},{2,3},{3,2},{4,5},{5,4},{6,7},{7,6},{8,9},{9,8},{10,11... | collective-permute-start | bytes 393224 | tf_op jit(solution)/shard_map/ppermute | solution.py:569
  10.7 29.1 %collective-permute-start.5 = (bf16[256,256]{1,0:T(8,128)(2,1)S(1)}, bf16[256,256]{1,0:T(8,128)(2,1)S(1)}, u32[]{:S(2)}, u32[]{:S(2)}) collective-permute-start(bf16[256,256]{1,0:T(8,128)(2,1)S(1)} %get-tuple-element.140), channel_id=1, source_target_pairs={{0,2},{1,3},{2,0},{3,1},{4,6},{5,7},{6,4},{7,5},{8,10},{9,11},{10,... | collective-permute-start | bytes 393224 | tf_op jit(solution)/shard_map/ppermute | solution.py:569
  12.7 27.0 %collective-permute-start.6 = (bf16[256,256]{1,0:T(8,128)(2,1)S(1)}, bf16[256,256]{1,0:T(8,128)(2,1)S(1)}, u32[]{:S(2)}, u32[]{:S(2)}) collective-permute-start(bf16[256,256]{1,0:T(8,128)(2,1)S(1)} %get-tuple-element.139), channel_id=1, source_target_pairs={{0,3},{1,2},{2,1},{3,0},{4,7},{5,6},{6,5},{7,4},{8,11},{9,10},{10,... | collective-permute-start | bytes 393224 | tf_op jit(solution)/shard_map/ppermute | solution.py:569
  25.3 1.4 %copy-start.8 = (s32[1,256]{1,0:T(1,128)S(1)}, s32[1,256]{1,0:T(1,128)}, u32[]{:S(2)}) copy-start(s32[1,256]{1,0:T(1,128)} %param.15) | copy-start | bytes 3076
  25.3 15.2 %copy-start = (bf16[1024,256]{1,0:T(8,128)(2,1)S(1)}, bf16[1024,256]{1,0:T(8,128)(2,1)}, u32[]{:S(2)}) copy-start(bf16[1024,256]{1,0:T(8,128)(2,1)} %get-tuple-element.90.refs_0_) | copy-start | bytes 1572868
  31.4 28.8 %collective-permute-start.2 = (bf16[256,2048]{1,0:T(8,128)(2,1)}, bf16[256,2048]{1,0:T(8,128)(2,1)}, u32[]{:S(2)}, u32[]{:S(2)}) collective-permute-start(bf16[256,2048]{1,0:T(8,128)(2,1)} %collective-permute-done.refs_0_), channel_id=1, source_target_pairs={{1,0},{2,1},{5,4},{6,5},{9,8},{10,9},{13,12},{14,13},{17,16},{18,1... | collective-permute-start | bytes 3145736 | tf_op jit(solution)/shard_map/ppermute | solution.py:602
  32.7 27.5 %collective-permute-start.3 = (bf16[256,2048]{1,0:T(8,128)(2,1)}, bf16[256,2048]{1,0:T(8,128)(2,1)}, u32[]{:S(2)}, u32[]{:S(2)}) collective-permute-start(bf16[256,2048]{1,0:T(8,128)(2,1)} %collective-permute-done.1.refs_0_), channel_id=1, source_target_pairs={{1,2},{2,3},{5,6},{6,7},{9,10},{10,11},{13,14},{14,15},{17,18},{18... | collective-permute-start | bytes 3145736 | tf_op jit(solution)/shard_map/ppermute | solution.py:603
  39.8 3.2 %copy-start.4 = (bf16[256,256]{1,0:T(8,128)(2,1)}, bf16[256,256]{1,0:T(8,128)(2,1)S(1)}, u32[]{:S(2)}) copy-start(bf16[256,256]{1,0:T(8,128)(2,1)S(1)} %collective-permute-done.5) | copy-start | bytes 393220
  39.8 3.9 %copy-start.6 = (bf16[256,256]{1,0:T(8,128)(2,1)}, bf16[256,256]{1,0:T(8,128)(2,1)S(1)}, u32[]{:S(2)}) copy-start(bf16[256,256]{1,0:T(8,128)(2,1)S(1)} %collective-permute-done.6) | copy-start | bytes 393220
  40.5 15.6 %collective-permute-start.8 = (bf16[1024,256]{1,0:T(8,128)(2,1)S(1)}, bf16[1024,256]{1,0:T(8,128)(2,1)S(1)}, u32[]{:S(2)}, u32[]{:S(2)}) collective-permute-start(bf16[1024,256]{1,0:T(8,128)(2,1)S(1)} %copy-done), channel_id=1, source_target_pairs={{0,16},{4,20},{8,24},{12,28},{16,0},{20,4},{24,8},{28,12},{1,17},{... | collective-permute-start | bytes 1572872 | tf_op jit(solution)/shard_map/ppermute | solution.py:398
  43.6 14.4 %collective-permute-start.9 = (bf16[1792,256]{1,0:T(8,128)(2,1)}, bf16[1792,256]{1,0:T(8,128)(2,1)S(1)}, u32[]{:S(2)}, u32[]{:S(2)}) collective-permute-start(bf16[1792,256]{1,0:T(8,128)(2,1)} %pad_maximum_fusion.1), channel_id=1, source_target_pairs={{0,4},{4,0},{8,12},{12,8},{16,20},{20,16},{24,28},{28,24},{1,5},{5... | collective-permute-start | bytes 2752520 | tf_op jit(solution)/shard_map/ppermute | solution.py:398
  44.3 11.7 %collective-permute-start.7 = (bf16[768,256]{1,0:T(8,128)(2,1)}, bf16[768,256]{1,0:T(8,128)(2,1)S(1)}, u32[]{:S(2)}, u32[]{:S(2)}) collective-permute-start(bf16[768,256]{1,0:T(8,128)(2,1)} %constant_dynamic-update-slice_fusion.refs_5_), channel_id=1, source_target_pairs={{0,8},{4,12},{8,0},{12,4},{16,24},{20,28},{24,16},{28,20},{1,9},{5... | collective-permute-start | bytes 1179656 | tf_op jit(solution)/shard_map/ppermute | solution.py:398
  55.0 2.1 %copy-start.5 = (bf16[256,256]{1,0:T(8,128)(2,1)S(1)}, bf16[256,256]{1,0:T(8,128)(2,1)}, u32[]{:S(2)}) copy-start(bf16[256,256]{1,0:T(8,128)(2,1)} %copy-done.4) | copy-start | bytes 393220
  55.0 2.1 %copy-start.7 = (bf16[256,256]{1,0:T(8,128)(2,1)S(1)}, bf16[256,256]{1,0:T(8,128)(2,1)}, u32[]{:S(2)}) copy-start(bf16[256,256]{1,0:T(8,128)(2,1)} %copy-done.6) | copy-start | bytes 393220
  56.0 12.0 %copy-start.11 = (s32[4]{0:T(128)S(1)}, s32[4]{0:T(128)}, u32[]{:S(2)}) copy-start(s32[4]{0:T(128)} %constant.72.clone) | copy-start | bytes 52
  60.2 29.1 %collective-permute-start.10 = (bf16[256,2048]{1,0:T(8,128)(2,1)}, bf16[256,2048]{1,0:T(8,128)(2,1)}, u32[]{:S(2)}, u32[]{:S(2)}) collective-permute-start(bf16[256,2048]{1,0:T(8,128)(2,1)} %collective-permute-done.2.refs_1_), channel_id=1, source_target_pairs={{1,0},{5,4},{9,8},{13,12},{17,16},{21,20},{25,24},{29,28}} | collective-permute-start | bytes 3145736 | tf_op jit(solution)/shard_map/ppermute | solution.py:602
  61.5 27.8 %collective-permute-start.11 = (bf16[256,2048]{1,0:T(8,128)(2,1)}, bf16[256,2048]{1,0:T(8,128)(2,1)}, u32[]{:S(2)}, u32[]{:S(2)}) collective-permute-start(bf16[256,2048]{1,0:T(8,128)(2,1)} %collective-permute-done.3.refs_0_), channel_id=1, source_target_pairs={{2,3},{6,7},{10,11},{14,15},{18,19},{22,23},{26,27},{30,31}} | collective-permute-start | bytes 3145736 | tf_op jit(solution)/shard_map/ppermute | solution.py:603
  63.1 26.1 %collective-permute-start.12 = (bf16[2048,256]{1,0:T(8,128)(2,1)}, bf16[2048,256]{1,0:T(8,128)(2,1)}, u32[]{:S(2)}, u32[]{:S(2)}) collective-permute-start(bf16[2048,256]{1,0:T(8,128)(2,1)} %pad_maximum_fusion), channel_id=1, source_target_pairs={{0,8},{4,12},{8,0},{12,4},{16,24},{20,28},{24,16},{28,20},{1,9},{5... | collective-permute-start | bytes 3145736 | tf_op jit(solution)/shard_map/ppermute | solution.py:398
  64.5 1.9 %collective-permute-start.15 = (bf16[1024,256]{1,0:T(8,128)(2,1)S(1)}, bf16[1024,256]{1,0:T(8,128)(2,1)S(1)}, u32[]{:S(2)}, u32[]{:S(2)}) collective-permute-start(bf16[1024,256]{1,0:T(8,128)(2,1)S(1)} %collective-permute-done.8.refs_2_), channel_id=1, source_target_pairs={{0,4},{4,0},{8,12},{12,8},{16,20},{20,16},{24,28},{28,24},{1,5},{5... | collective-permute-start | bytes 1572872 | tf_op jit(solution)/shard_map/ppermute | solution.py:398
  64.5 20.3 %collective-permute-start.13 = (bf16[1536,256]{1,0:T(8,128)(2,1)}, bf16[1536,256]{1,0:T(8,128)(2,1)}, u32[]{:S(2)}, u32[]{:S(2)}) collective-permute-start(bf16[1536,256]{1,0:T(8,128)(2,1)} %pad_maximum_fusion.2), channel_id=1, source_target_pairs={{0,16},{4,20},{8,24},{12,28},{16,0},{20,4},{24,8},{28,12},{1,17},{... | collective-permute-start | bytes 2359304 | tf_op jit(solution)/shard_map/ppermute | solution.py:398
  66.4 0.8 copy-start.1
  67.2 7.0 %collective-permute-start.14 = (bf16[768,256]{1,0:T(8,128)(2,1)S(1)}, bf16[768,256]{1,0:T(8,128)(2,1)}, u32[]{:S(2)}, u32[]{:S(2)}) collective-permute-start(bf16[768,256]{1,0:T(8,128)(2,1)S(1)} %collective-permute-done.7.refs_7_), channel_id=1, source_target_pairs={{0,4},{4,0},{8,12},{12,8},{16,20},{20,16},{24,28},{28,24},{1,5},{5... | collective-permute-start | bytes 1179656 | tf_op jit(solution)/shard_map/ppermute | solution.py:398
  68.0 4.3 %copy-start.2 = (bf16[1024,256]{1,0:T(8,128)(2,1)S(1)}, bf16[1024,256]{1,0:T(8,128)(2,1)}, u32[]{:S(2)}) copy-start(bf16[1024,256]{1,0:T(8,128)(2,1)} %copy-done.1) | copy-start | bytes 1572868
  89.3 10.5 %collective-permute-start.16 = (bf16[2048,256]{1,0:T(8,128)(2,1)}, bf16[2048,256]{1,0:T(8,128)(2,1)S(1)}, u32[]{:S(2)}, u32[]{:S(2)}) collective-permute-start(bf16[2048,256]{1,0:T(8,128)(2,1)} %collective-permute-done.12.refs_0_), channel_id=1, source_target_pairs={{0,4},{4,0},{8,12},{12,8},{16,20},{20,16},{24,28},{28,24},{1,5},{5... | collective-permute-start | bytes 3145736 | tf_op jit(solution)/shard_map/ppermute | solution.py:398
  89.3 10.5 %collective-permute-start.17 = (bf16[1536,256]{1,0:T(8,128)(2,1)}, bf16[1536,256]{1,0:T(8,128)(2,1)}, u32[]{:S(2)}, u32[]{:S(2)}) collective-permute-start(bf16[1536,256]{1,0:T(8,128)(2,1)} %collective-permute-done.13.refs_9_), channel_id=1, source_target_pairs={{0,4},{4,0},{8,12},{12,8},{16,20},{20,16},{24,28},{28,24},{1,5},{5... | collective-permute-start | bytes 2359304 | tf_op jit(solution)/shard_map/ppermute | solution.py:398
  99.8 3.3 %collective-permute-start.18 = (bf16[4,1024,128]{2,1,0:T(8,128)(2,1)}, bf16[4,1024,128]{2,1,0:T(8,128)(2,1)S(1)}, u32[]{:S(2)}, u32[]{:S(2)}) collective-permute-start(bf16[4,1024,128]{2,1,0:T(8,128)(2,1)} %get-tuple-element.114), channel_id=1, source_target_pairs={{0,4},{4,0},{8,12},{12,8},{16,20},{20,16},{24,28},{28,24},{1,5},{5... | collective-permute-start | bytes 3145736 | tf_op jit(solution)/shard_map/ppermute | solution.py:398
  99.9 12.7 %collective-permute-start.24 = (bf16[4,1024,128]{2,1,0:T(8,128)(2,1)}, bf16[4,1024,128]{2,1,0:T(8,128)(2,1)S(1)}, u32[]{:S(2)}, u32[]{:S(2)}) collective-permute-start(bf16[4,1024,128]{2,1,0:T(8,128)(2,1)} %get-tuple-element.121), channel_id=1, source_target_pairs={{0,4},{4,0},{8,12},{12,8},{16,20},{20,16},{24,28},{28,24},{1,5},{5... | collective-permute-start | bytes 3145736 | tf_op jit(solution)/shard_map/ppermute | solution.py:398
  103.1 3.3 %copy-start.3 = (bf16[256,256]{1,0:T(8,128)(2,1)S(1)}, bf16[256,256]{1,0:T(8,128)(2,1)}, u32[]{:S(2)}) copy-start(bf16[256,256]{1,0:T(8,128)(2,1)} %get-tuple-element.128.refs_0_) | copy-start | bytes 393220
  103.1 11.0 %copy-start.10 = (s32[4]{0:T(128)S(1)}, s32[4]{0:T(128)}, u32[]{:S(2)}) copy-start(s32[4]{0:T(128)} %constant.73.clone) | copy-start | bytes 52
  103.3 19.9 %collective-permute-start.19 = (bf16[2,1024,128]{2,1,0:T(8,128)(2,1)S(1)}, bf16[2,1024,128]{2,1,0:T(8,128)(2,1)S(1)}, u32[]{:S(2)}, u32[]{:S(2)}) collective-permute-start(bf16[2,1024,128]{2,1,0:T(8,128)(2,1)S(1)} %get-tuple-element.115), channel_id=1, source_target_pairs={{0,8},{4,12},{8,0},{12,4},{16,24},{20,28},{24,16},{28,20},{1,9},{5... | collective-permute-start | bytes 1572872 | tf_op jit(solution)/shard_map/ppermute | solution.py:398
  104.8 18.4 %collective-permute-start.20 = (bf16[2,1024,128]{2,1,0:T(8,128)(2,1)S(1)}, bf16[2,1024,128]{2,1,0:T(8,128)(2,1)S(1)}, u32[]{:S(2)}, u32[]{:S(2)}) collective-permute-start(bf16[2,1024,128]{2,1,0:T(8,128)(2,1)S(1)} %get-tuple-element.116), channel_id=1, source_target_pairs={{0,16},{4,20},{8,24},{12,28},{16,0},{20,4},{24,8},{28,12},{1,17},{... | collective-permute-start | bytes 1572872 | tf_op jit(solution)/shard_map/ppermute | solution.py:398
  106.3 13.0 %collective-permute-start.21 = (bf16[256,256]{1,0:T(8,128)(2,1)S(1)}, bf16[256,256]{1,0:T(8,128)(2,1)S(1)}, u32[]{:S(2)}, u32[]{:S(2)}) collective-permute-start(bf16[256,256]{1,0:T(8,128)(2,1)S(1)} %copy-done.3), channel_id=1, source_target_pairs={{0,1},{1,0},{2,3},{3,2},{4,5},{5,4},{6,7},{7,6},{8,9},{9,8},{10,11... | collective-permute-start | bytes 393224 | tf_op jit(solution)/shard_map/ppermute | solution.py:569
  110.7 12.5 %collective-permute-start.22 = (bf16[256,256]{1,0:T(8,128)(2,1)S(1)}, bf16[256,256]{1,0:T(8,128)(2,1)S(1)}, u32[]{:S(2)}, u32[]{:S(2)}) collective-permute-start(bf16[256,256]{1,0:T(8,128)(2,1)S(1)} %copy-done.3), channel_id=1, source_target_pairs={{0,2},{1,3},{2,0},{3,1},{4,6},{5,7},{6,4},{7,5},{8,10},{9,11},{10,... | collective-permute-start | bytes 393224 | tf_op jit(solution)/shard_map/ppermute | solution.py:569
  112.6 10.6 %collective-permute-start.23 = (bf16[256,256]{1,0:T(8,128)(2,1)S(1)}, bf16[256,256]{1,0:T(8,128)(2,1)S(1)}, u32[]{:S(2)}, u32[]{:S(2)}) collective-permute-start(bf16[256,256]{1,0:T(8,128)(2,1)S(1)} %copy-done.3), channel_id=1, source_target_pairs={{0,3},{1,2},{2,1},{3,0},{4,7},{5,6},{6,5},{7,4},{8,11},{9,10},{10,... | collective-permute-start | bytes 393224 | tf_op jit(solution)/shard_map/ppermute | solution.py:569
  119.3 5.0 %copy-start.9 = (s32[8]{0:T(128)S(1)}, s32[8]{0:T(128)}, u32[]{:S(2)}) copy-start(s32[8]{0:T(128)} %constant.74.clone) | copy-start | bytes 100
  123.3 6.4 %collective-permute-start.25 = (bf16[1024,128]{1,0:T(8,128)(2,1)S(1)}, bf16[1024,128]{1,0:T(8,128)(2,1)S(1)}, u32[]{:S(2)}, u32[]{:S(2)}) collective-permute-start(bf16[1024,128]{1,0:T(8,128)(2,1)S(1)} %get-tuple-element.126), channel_id=1, source_target_pairs={{0,16},{4,20},{8,24},{12,28},{16,0},{20,4},{24,8},{28,12},{1,17},{... | collective-permute-start | bytes 786440 | tf_op jit(solution)/shard_map/ppermute | solution.py:398
  123.9 6.4 %collective-permute-start.26 = (bf16[1024,128]{1,0:T(8,128)(2,1)S(1)}, bf16[1024,128]{1,0:T(8,128)(2,1)S(1)}, u32[]{:S(2)}, u32[]{:S(2)}) collective-permute-start(bf16[1024,128]{1,0:T(8,128)(2,1)S(1)} %get-tuple-element.127), channel_id=1, source_target_pairs={{0,8},{4,12},{8,0},{12,4},{16,24},{20,28},{24,16},{28,20},{1,9},{5... | collective-permute-start | bytes 786440 | tf_op jit(solution)/shard_map/ppermute | solution.py:398
